TPU v7x, 32 devices: a whole 2x2x4 slice. The times are simulated.
32 devices in a mesh: groups: 2 (over x), tensor: 16 (over z, y, core).
Axes of the slice: x: 2, y: 2, z: 4, core: 2. Of those that a mesh axis runs over, the one named last changes fastest.
Arguments:
- queries: bfloat16 [2, 128, 8192], P(None, ('groups', 'tensor')), parts along dimension 1, may hold values from -8 to 8
- new_keys: bfloat16 [2, 128, 1024], P(None, ('groups', 'tensor')), parts along dimension 1, may hold values from -6 to 6
- new_values: bfloat16 [2, 128, 1024], P(None, ('groups', 'tensor')), parts along dimension 1, may hold values from -24 to 24
- cache_keys: bfloat16 [128, 512, 1024], P(('groups', 'tensor')), parts along dimension 0, may hold values from -8 to 8
- cache_values: bfloat16 [128, 512, 1024], P(('groups', 'tensor')), parts along dimension 0, may hold values from -24 to 24
- kv_len: int32 [128], P(('groups', 'tensor')), parts along dimension 0, may hold values from 2 to 512, as said below
- adapter_rows: int32 [24], P('groups'), parts along dimension 0, may hold values from 1 to 8, 64 in all
- adapter_rank: int32 [12], replicated, may hold values from 1 to 2, as said below
- adapter_owner: int32 [12], replicated, may hold values from 0 to 15, as said below
- out_weight: bfloat16 [8192, 8192], P(None, 'tensor'), may hold values from -0.0625 to 0.0625
- store_down: bfloat16 [16, 8192, 128], P('tensor'), may hold values from -0.0625 to 0.0625
- store_up: bfloat16 [16, 8192, 128], P('tensor'), may hold values from -0.5 to 0.5
Outputs:
- projected: bfloat16 [2, 128, 8192], P(None, 'groups', 'tensor'), parts along dimension 1
There are 2 independent parts, one for each index of `groups`. A program takes and returns all parts, laid end to end along the dimension named above; an argument that names none is the same for every part. Nothing has to cross between parts.
Inputs may be any that keep to these rules, and one draw needn't show every extreme that they name: `kv_len`: 512 is reached by some request of every part. `adapter_rows`: sums to 64; some adapter has exactly 8 requests. `adapter_rank`: exactly 4 adapters have 2 blocks, the others 1. `adapter_owner`: the blocks of all adapters tile the store: every store index holds exactly one block.
All inputs are finite; a program needn't handle non-finite values.
Results may differ from a plain program's by a relative error of at most 0.0062.
Values may be sent and summed in bfloat16 or wider, within the bound.
No kernel may reach another device: no remote copies, remote signals or barrier semaphores. Data moves between devices by JAX's collectives and lax.ppermute only.
A program may use at most 128 MiB of HBM per device.

v0:
```python
import jax
import jax.numpy as jnp
from jax import lax
from jax.sharding import PartitionSpec as P

HQ = 64
KVH = 8
HD = 128
CACHE = 512


def attend(queries, new_keys, new_values, cache_keys, cache_values, kv_len):
    steps, rows, width = queries.shape
    group = HQ // KVH
    scale = HD ** (-0.5)
    query = queries.reshape(steps, rows, KVH, group, HD)
    ckeys = cache_keys.reshape(rows, CACHE, KVH, HD)
    cvals = cache_values.reshape(rows, CACHE, KVH, HD)
    nkeys = new_keys.reshape(steps, rows, KVH, HD)
    nvals = new_values.reshape(steps, rows, KVH, HD)
    older = (
        jnp.einsum("trkgd,rlkd->trkgl", query, ckeys, preferred_element_type=jnp.float32) * scale
    )
    fresh = (
        jnp.einsum("trkgd,srkd->trkgs", query, nkeys, preferred_element_type=jnp.float32) * scale
    )
    live = jnp.arange(CACHE)[None, :] < kv_len[:, None]
    older = jnp.where(live[None, :, None, None, :], older, -jnp.inf)
    causal = jnp.arange(steps)[:, None] >= jnp.arange(steps)[None, :]
    fresh = jnp.where(causal[:, None, None, None, :], fresh, -jnp.inf)
    top = jnp.maximum(jnp.max(older, axis=-1), jnp.max(fresh, axis=-1))[..., None]
    e_older = jnp.exp(older - top)
    e_fresh = jnp.exp(fresh - top)
    total = jnp.sum(e_older, axis=-1, keepdims=True) + jnp.sum(e_fresh, axis=-1, keepdims=True)
    p_older = (e_older / total).astype(jnp.bfloat16)
    p_fresh = (e_fresh / total).astype(jnp.bfloat16)
    mixed = jnp.einsum("trkgl,rlkd->trkgd", p_older, cvals, preferred_element_type=jnp.float32)
    mixed = mixed + jnp.einsum(
        "trkgs,srkd->trkgd", p_fresh, nvals, preferred_element_type=jnp.float32
    )
    return mixed.reshape(steps, rows, width).astype(jnp.bfloat16)


def row_tables(adapter_rows, adapter_rank, adapter_owner, total_rows, blocks):
    ends = jnp.cumsum(adapter_rows)
    starts = ends - adapter_rows
    row_ids = jnp.arange(total_rows, dtype=jnp.int32)
    row_adapter = jnp.sum((row_ids[:, None] >= ends[None, :]).astype(jnp.int32), axis=1)
    adapter_ids = jnp.arange(adapter_rows.shape[0], dtype=jnp.int32)
    match = row_adapter[:, None] == adapter_ids[None, :]
    row_owner = jnp.sum(jnp.where(match, adapter_owner[None, :], 0), axis=1)
    rank_per_row = jnp.sum(jnp.where(match, adapter_rank[None, :], 0), axis=1)
    slots = jnp.arange(2, dtype=jnp.int32)
    slot_block = row_owner[:, None] + slots[None, :]
    slot_live = slots[None, :] < rank_per_row[:, None]
    block_numbers = jnp.arange(blocks, dtype=jnp.int32)
    picks = (slot_block[:, :, None] == block_numbers[None, None, :]) & slot_live[:, :, None]
    owned = (block_numbers[None, :] >= adapter_owner[:, None]) & (
        block_numbers[None, :] < adapter_owner[:, None] + adapter_rank[:, None]
    )
    block_adapter = jnp.sum(jnp.where(owned, adapter_ids[:, None], 0), axis=0)
    return (starts, block_adapter, jnp.minimum(slot_block, blocks - 1), slot_live, picks)


def apply_up(low, picks, up_parts):
    positioned_rows = jnp.einsum(
        "trjk,rjb->trbk", low, picks.astype(jnp.bfloat16), preferred_element_type=jnp.float32
    ).astype(jnp.bfloat16)
    return jnp.einsum(
        "trbk,bck->trc", positioned_rows, up_parts, preferred_element_type=jnp.float32
    )


def per_device(
    queries,
    new_keys,
    new_values,
    cache_keys,
    cache_values,
    kv_len,
    adapter_rows,
    adapter_rank,
    adapter_owner,
    out_weight,
    store_down,
    store_up,
):
    parts = lax.axis_size("tensor")
    index = lax.axis_index("tensor")
    steps, rows_dev, width = queries.shape
    rank_w = store_down.shape[2]
    slice_w = width // parts
    cols = out_weight.shape[1]
    total_rows = rows_dev * parts
    attended = attend(queries, new_keys, new_values, cache_keys, cache_values, kv_len)
    starts, block_adapter, slot_block, slot_live, picks = row_tables(
        adapter_rows, adapter_rank, adapter_owner, total_rows, parts
    )
    down_portions, up_parts = (
        lax.all_to_all(
            store_down.reshape(parts, slice_w, rank_w),
            "tensor",
            split_axis=0,
            concat_axis=0,
            tiled=True,
        ),
        lax.all_to_all(
            store_up.reshape(parts, slice_w, rank_w),
            "tensor",
            split_axis=0,
            concat_axis=0,
            tiled=True,
        ),
    )
    pick_values = picks.astype(jnp.float32)
    piece = lax.all_gather(attended, "tensor", axis=1, tiled=True)
    count = piece.shape[1]
    base_portion = jnp.einsum("trd,dc->trc", piece, out_weight, preferred_element_type=jnp.float32)
    cut_section = lax.dynamic_slice_in_dim(piece, index * slice_w, slice_w, 2)
    scattered_rows = jnp.einsum(
        "zwx,exy->zwey", cut_section, down_portions, preferred_element_type=jnp.float32
    )
    partial_value = jnp.einsum(
        "trbk,rjb->trjk", scattered_rows, pick_values, precision=lax.Precision.HIGHEST
    )
    joined = jnp.concatenate(
        [base_portion, partial_value.reshape(steps, count, 2 * rank_w)], axis=2
    )
    base = joined[:, :, :cols]
    summed = lax.psum(joined[:, :, cols:], "tensor")
    low = summed.astype(jnp.bfloat16).reshape(steps, total_rows, 2, rank_w)
    delta = apply_up(low, picks, up_parts)
    return (base + delta).astype(jnp.bfloat16)


def solution(mesh):
    in_specs = (
        P(None, ("groups", "tensor"), None),
        P(None, ("groups", "tensor"), None),
        P(None, ("groups", "tensor"), None),
        P(("groups", "tensor"), None, None),
        P(("groups", "tensor"), None, None),
        P(("groups", "tensor")),
        P("groups"),
        P(),
        P(),
        P(None, "tensor"),
        P("tensor", None, None),
        P("tensor", None, None),
    )
    out_specs = P(None, "groups", "tensor")
    return jax.shard_map(
        per_device, mesh=mesh, in_specs=in_specs, out_specs=out_specs, check_vma=False
    )
```

profile of v0, /device:TPU:0, one launch (start us, length us, event | category | flops | bytes accessed | tf_op | source)
XLA Modules:
  0.0 181.3 jit_solution(17110300085338460843)
XLA Ops:
  6.5 7.5 %all-to-all-start = ((bf16[16,512,128]{2,1,0:T(8,128)(2,1)}), bf16[16,512,128]{2,1,0:T(8,128)(2,1)S(1)}, u32[]{:S(2)}, u32[]{:S(2)}) async-start(bf16[16,512,128]{2,1,0:T(8,128)(2,1)} %bitcast.81), calls=%async_computation | async-start | bytes 4194304 | tf_op jit(solution)/shard_map/all_to_all | solution.py:100
  14.1 0.0 all-gather.2.cloned.1.call-start
  14.1 0.2 reshape.139
  14.3 5.2 %copy.67 = bf16[256,8,8,128]{3,2,1,0:T(8,128)(2,1)} copy(bf16[256,8,8,128]{3,1,2,0:T(8,128)(2,1)} %bitcast.79) | data formatting | bytes 8388608
  19.6 3.5 %copy.68 = bf16[256,8,8,128]{3,2,1,0:T(8,128)(2,1)S(1)} copy(bf16[256,8,8,128]{3,1,2,0:T(8,128)(2,1)} %bitcast.80) | data formatting | bytes 8388608
  23.1 0.7 fusion.64
  23.8 0.1 iota_compare_fusion.3
  23.9 0.3 bitcast_bitcast_fusion.1
  24.1 1.4 fusion.63
  25.5 0.1 fusion.53
  25.7 0.4 fusion.41
  26.1 0.3 fusion.54
  26.3 0.3 bitcast_bitcast_fusion
  26.6 1.1 fusion.35
  27.8 0.7 reshape.159
  28.5 30.8 %all-to-all-done = bf16[16,512,128]{2,1,0:T(8,128)(2,1)S(1)} async-done(((bf16[16,512,128]{2,1,0:T(8,128)(2,1)}), bf16[16,512,128]{2,1,0:T(8,128)(2,1)S(1)}, u32[]{:S(2)}, u32[]{:S(2)}) %all-to-all-start) | async-done | bytes 2097184 | tf_op jit(solution)/shard_map/all_to_all | solution.py:100
  59.3 11.4 %all-to-all-start.1 = ((bf16[16,512,128]{2,1,0:T(8,128)(2,1)}), bf16[16,512,128]{2,1,0:T(8,128)(2,1)}, u32[]{:S(2)}, u32[]{:S(2)}) async-start(bf16[16,512,128]{2,1,0:T(8,128)(2,1)} %bitcast.82), calls=%async_computation.1 | async-start | bytes 4194304 | tf_op jit(solution)/shard_map/all_to_all | solution.py:107
  70.7 0.2 reduce-window.8
  70.9 0.1 convert_reduce_fusion
  71.0 0.1 select_reduce_fusion.1
  71.1 0.1 iota_compare_fusion
  71.1 0.1 iota_add_fusion
  71.2 22.4 %all-gather.2.cloned.1.call-done = bf16[2,64,8192]{2,0,1:T(2,128)(2,1)} async-done(((bf16[2,4,8192]{2,0,1:T(2,128)(2,1)}), bf16[2,64,8192]{2,0,1:T(2,128)(2,1)}) %all-gather.2.cloned.1.call-update) | async-done | bytes 2097168 | tf_op jit(solution)/shard_map/all_gather | solution.py:116
  93.6 2.9 %copy.46 = bf16[2,64,8192]{2,1,0:T(8,128)(2,1)S(1)} copy(bf16[2,64,8192]{2,0,1:T(2,128)(2,1)} %all-gather.2.cloned.1.call-done) | data formatting | bytes 4194304 | tf_op jit(solution)/shard_map/all_gather | solution.py:116
  96.5 0.4 fusion.8
  97.0 1.2 convolution_bitcast_fusion
  98.1 0.2 reshape.146
  98.3 67.1 %all-reduce.1 = bf16[2,64,256]{2,0,1:T(2,128)(2,1)S(1)} all-reduce(f32[2,64,256]{2,0,1:T(2,128)S(1)} %reshape.146), channel_id=1, replica_groups=mesh['groups'=2,'tensor'=16] {'tensor'}, use_global_device_ids=true, to_apply=%region_8.9 | all-reduce | flops 32768 | bytes 196608 | tf_op jit(solution)/shard_map/psum | solution.py:130
  165.4 0.1 reshape.147
  165.4 0.7 fusion.19
  166.1 5.3 %fusion = f32[2,64,512]{2,1,0:T(8,128)S(1)} fusion(bf16[8192,512]{1,0:T(8,128)(2,1)} %param.21, bf16[2,64,8192]{2,0,1:T(2,128)(2,1)S(1)} %copy-done.1), kind=kOutput, calls=%fused_computation | convolution fusion | flops 1073741824 | bytes 10747904 | tf_op jit(solution)/shard_map/trd,dc->trc/dot_general | solution.py:118
  171.4 3.1 %fusion.29 = bf16[2,64,512]{2,1,0:T(8,128)(2,1)} fusion(f32[2,64,512]{2,1,0:T(8,128)S(1)} %fusion, bf16[16,512,128]{2,1,0:T(8,128)(2,1)} %all-to-all-done.1, bf16[2,64,16,128]{3,2,0,1:T(8,128)(2,1)S(1)} %fusion.19), kind=kOutput, calls=%fused_computation.20 | convolution fusion | flops 268566528 | bytes 3014656 | tf_op jit(solution)/shard_map/trbk,bck->trc/dot_general | solution.py:69
  (30 shorter events, 0.2 us)
Async XLA Ops:
  6.5 7.6 %copy-start.4 = (bf16[2,4,8192]{2,1,0:T(4,128)(2,1)S(1)}, bf16[2,4,8192]{2,1,0:T(4,128)(2,1)}, u32[]{:S(2)}) copy-start(bf16[2,4,8192]{2,1,0:T(4,128)(2,1)} %param.12) | copy-start | bytes 393220
  6.5 52.8 %all-to-all-start = ((bf16[16,512,128]{2,1,0:T(8,128)(2,1)}), bf16[16,512,128]{2,1,0:T(8,128)(2,1)S(1)}, u32[]{:S(2)}, u32[]{:S(2)}) async-start(bf16[16,512,128]{2,1,0:T(8,128)(2,1)} %bitcast.81), calls=%async_computation | async-start | bytes 4194304 | tf_op jit(solution)/shard_map/all_to_all | solution.py:100
  14.1 79.5 %all-gather.2.cloned.1.call-start = ((), (), s32[]{:S(2)}) async-start(), calls=%async_computation.2 | async-start | bytes 2228224 | tf_op jit(solution)/shard_map/all_gather | solution.py:116
  14.3 5.2 %copy-start.5 = (bf16[2,4,1024]{2,1,0:T(4,128)(2,1)S(1)}, bf16[2,4,1024]{2,1,0:T(4,128)(2,1)}, u32[]{:S(2)}) copy-start(bf16[2,4,1024]{2,1,0:T(4,128)(2,1)} %param.13) | copy-start | bytes 49156
  14.3 5.2 %copy-start.6 = (bf16[2,4,1024]{2,1,0:T(4,128)(2,1)S(1)}, bf16[2,4,1024]{2,1,0:T(4,128)(2,1)}, u32[]{:S(2)}) copy-start(bf16[2,4,1024]{2,1,0:T(4,128)(2,1)} %param.14) | copy-start | bytes 49156
  19.6 4.2 %copy-start.7 = (s32[4]{0:T(128)S(1)}, s32[4]{0:T(128)}, u32[]{:S(2)}) copy-start(s32[4]{0:T(128)} %param.17) | copy-start | bytes 52
  19.6 4.3 %copy-start = (bf16[256,8,8,128]{3,2,1,0:T(8,128)(2,1)S(1)}, bf16[256,8,8,128]{3,2,1,0:T(8,128)(2,1)}, u32[]{:S(2)}) copy-start(bf16[256,8,8,128]{3,2,1,0:T(8,128)(2,1)} %copy.67) | copy-start | bytes 12582916
  27.7 42.9 %copy-start.10 = (s32[12]{0:T(128)S(1)}, s32[12]{0:T(128)}, u32[]{:S(2)}) copy-start(s32[12]{0:T(128)} %param.18) | copy-start | bytes 148
  27.7 43.2 %copy-start.8 = (s32[12]{0:T(128)S(1)}, s32[12]{0:T(128)}, u32[]{:S(2)}) copy-start(s32[12]{0:T(128)} %param.20) | copy-start | bytes 148
  27.7 43.2 %copy-start.9 = (s32[12]{0:T(128)S(1)}, s32[12]{0:T(128)}, u32[]{:S(2)}) copy-start(s32[12]{0:T(128)} %param.19) | copy-start | bytes 148
  59.3 11.9 %copy-start.2 = (bf16[16,512,128]{2,1,0:T(8,128)(2,1)}, bf16[16,512,128]{2,1,0:T(8,128)(2,1)S(1)}, u32[]{:S(2)}) copy-start(bf16[16,512,128]{2,1,0:T(8,128)(2,1)S(1)} %all-to-all-done) | copy-start | bytes 6291460
  59.3 112.1 %all-to-all-start.1 = ((bf16[16,512,128]{2,1,0:T(8,128)(2,1)}), bf16[16,512,128]{2,1,0:T(8,128)(2,1)}, u32[]{:S(2)}, u32[]{:S(2)}) async-start(bf16[16,512,128]{2,1,0:T(8,128)(2,1)} %bitcast.82), calls=%async_computation.1 | async-start | bytes 4194304 | tf_op jit(solution)/shard_map/all_to_all | solution.py:107
  93.6 2.9 %copy-start.3 = (bf16[16,512,128]{2,1,0:T(8,128)(2,1)S(1)}, bf16[16,512,128]{2,1,0:T(8,128)(2,1)}, u32[]{:S(2)}) copy-start(bf16[16,512,128]{2,1,0:T(8,128)(2,1)} %copy-done.2) | copy-start | bytes 6291460
  93.6 72.5 %copy-start.1 = (bf16[2,64,8192]{2,0,1:T(2,128)(2,1)S(1)}, bf16[2,64,8192]{2,0,1:T(2,128)(2,1)}, u32[]{:S(2)}) copy-start(bf16[2,64,8192]{2,0,1:T(2,128)(2,1)} %all-gather.2.cloned.1.call-done) | copy-start | bytes 6291460
Sparse Core Ops, SparseCore 0:
  28.6 64.9 all-gather.1
where the time goes:
time: 182 us; the launch traced here: 181 us
  blocking collectives  67.1 us (37%)
  waiting for transfers between devices  53.2 us (29%)
  starting transfers between devices  18.9 us (10%)
  matrix products  14.1 us (8%)
  between operations  13.7 us (8%)
  local copies, waits for them, and re-layouts  13.3 us (7%)
    psum x1, blocking collectives, per_device(): summed = lax.psum(joined[:, :, cols:], 'tensor')  67.1 us
    all_to_all x1, waiting for transfers between devices, per_device(): lax.all_to_all(store_down.reshape(parts, slice_w, rank_w), 'tensor', spli...  30.8 us
    all_gather x1, waiting for transfers between devices, per_device(): piece = lax.all_gather(attended, 'tensor', axis=1, tiled=True)  22.4 us
    all_to_all x1, starting transfers between devices, per_device(): lax.all_to_all(store_up.reshape(parts, slice_w, rank_w), 'tensor', split_...  11.4 us
    unnamed x24, local copies, waits for them, and re-layouts  8.73 us
    all_to_all x1, starting transfers between devices, per_device(): lax.all_to_all(store_down.reshape(parts, slice_w, rank_w), 'tensor', spli...  7.52 us
    dot_general x1, matrix products, per_device(): jnp.einsum('trd,dc->trc', piece, out_weight, preferred_element_type=jnp.f...  5.29 us
  transfers between devices with their start and end apart: 3, of which 2 were waited for; matrix products, arithmetic and copies ran while one was open for 14% of the time, Pallas kernels for 0%

commit v1 on v0

v1 whole, which is shorter than its diff:
```python
import functools

import jax
import jax.numpy as jnp
from jax import lax
from jax.experimental import pallas as pl
from jax.experimental.pallas import tpu as pltpu
from jax.sharding import PartitionSpec as P

HQ = 64
KVH = 8
HD = 128
GROUP = HQ // KVH
MOST = 8
F32 = jnp.float32
BF16 = jnp.bfloat16
NT = (((1,), (1,)), ((), ()))


def dot(a, b):
    return jnp.dot(a, b, preferred_element_type=F32)


def dot_nt(a, b):
    return lax.dot_general(a, b, NT, preferred_element_type=F32)


def attend_kernel(
    len_ref, q_ref, nk_ref, nv_ref, k_ref, v_ref, out_ref, qs, nks, nvs, mixed
):
    steps, rows, width = q_ref.shape
    cache = k_ref.shape[1]
    both = steps * rows
    pack = steps * GROUP
    r = pl.program_id(0)

    @pl.when(r == 0)
    def _():
        flat = jnp.concatenate([q_ref[t].astype(F32) for t in range(steps)], axis=0)
        for k in range(KVH):
            heads = jnp.stack(
                [flat[:, (k * GROUP + g) * HD : (k * GROUP + g + 1) * HD] for g in range(GROUP)]
            )
            turned = jnp.swapaxes(heads, 0, 1)
            for i in range(rows):
                qs[i, k] = jnp.concatenate(
                    [turned[t * rows + i] for t in range(steps)], axis=0
                ).astype(BF16)
        for src, dst in ((nk_ref, nks), (nv_ref, nvs)):
            fresh = [src[t].astype(F32) for t in range(steps)]
            fresh.append(jnp.zeros((16 - both, src.shape[2]), F32))
            dst[...] = jnp.concatenate(fresh, axis=0).astype(BF16)

    scale = HD ** (-0.5)
    older = jnp.concatenate(
        [dot_nt(qs[r, k], k_ref[0, :, k * HD : (k + 1) * HD]) for k in range(KVH)], axis=0
    )
    fresh = jnp.concatenate(
        [dot_nt(qs[r, k], nks[:, k * HD : (k + 1) * HD]) for k in range(KVH)], axis=0
    )
    place = lax.broadcasted_iota(jnp.int32, older.shape, 1)
    older = jnp.where(place < len_ref[r], older * scale, -jnp.inf)
    slot = lax.broadcasted_iota(jnp.int32, fresh.shape, 1)
    step = (lax.broadcasted_iota(jnp.int32, fresh.shape, 0) // GROUP) % steps
    seen = (slot < both) & (slot % rows == r) & (slot // rows <= step)
    fresh = jnp.where(seen, fresh * scale, -jnp.inf)
    top = jnp.maximum(
        jnp.max(older, axis=1, keepdims=True), jnp.max(fresh, axis=1, keepdims=True)
    )
    e_older = jnp.exp(older - top)
    e_fresh = jnp.exp(fresh - top)
    total = jnp.sum(e_older, axis=1, keepdims=True) + jnp.sum(e_fresh, axis=1, keepdims=True)
    inverse = 1.0 / total
    p_older = (e_older * inverse).astype(BF16)
    p_fresh = (e_fresh * inverse).astype(BF16)
    for k in range(KVH):
        own = slice(k * pack, (k + 1) * pack)
        cols = slice(k * HD, (k + 1) * HD)
        mixed[r, k] = dot(p_older[own], v_ref[0, :, cols]) + dot(p_fresh[own], nvs[:, cols])

    @pl.when(r == rows - 1)
    def _():
        for k in range(KVH):
            turned = jnp.stack(
                [
                    mixed[i, k, t * GROUP : (t + 1) * GROUP, :]
                    for t in range(steps)
                    for i in range(rows)
                ]
            )
            heads = jnp.swapaxes(turned, 0, 1)
            for g in range(GROUP):
                at = (k * GROUP + g) * HD
                out_ref[:, at : at + HD] = heads[g].astype(BF16)


def attend(queries, new_keys, new_values, cache_keys, cache_values, kv_len):
    steps, rows, width = queries.shape
    cache, kv_width = cache_keys.shape[1:]
    pack = steps * GROUP
    whole = lambda r, lens: (0, 0, 0)
    mine = lambda r, lens: (r, 0, 0)
    flops = 4 * rows * steps * HQ * cache * HD
    return pl.pallas_call(
        attend_kernel,
        out_shape=jax.ShapeDtypeStruct((steps * rows, width), BF16),
        grid_spec=pltpu.PrefetchScalarGridSpec(
            num_scalar_prefetch=1,
            grid=(rows,),
            in_specs=[
                pl.BlockSpec((steps, rows, width), whole),
                pl.BlockSpec((steps, rows, kv_width), whole),
                pl.BlockSpec((steps, rows, kv_width), whole),
                pl.BlockSpec((1, cache, kv_width), mine),
                pl.BlockSpec((1, cache, kv_width), mine),
            ],
            out_specs=pl.BlockSpec((steps * rows, width), lambda r, lens: (0, 0)),
            scratch_shapes=[
                pltpu.VMEM((rows, KVH, pack, HD), BF16),
                pltpu.VMEM((16, kv_width), BF16),
                pltpu.VMEM((16, kv_width), BF16),
                pltpu.VMEM((rows, KVH, pack, HD), F32),
            ],
        ),
        compiler_params=pltpu.CompilerParams(vmem_limit_bytes=24 * 2**20),
        cost_estimate=pl.CostEstimate(
            flops=flops,
            bytes_accessed=4 * rows * cache * kv_width,
            transcendentals=rows * steps * HQ * cache,
        ),
        name="attend",
    )(kv_len, queries, new_keys, new_values, cache_keys, cache_values)


def row_place(index, steps, rows):
    both = steps * rows
    return (index // both) * rows + index % rows, (index % both) // rows


def delta_kernel(steps, rows, count_ref, rank_ref, owner_ref, a_ref, d_ref, u_ref, out_ref):
    block = lax.axis_index("tensor")
    total = a_ref.shape[0]
    parts, slots, cols = out_ref.shape
    start = jnp.int32(0)
    first = jnp.int32(0)
    amount = jnp.int32(0)
    for a in range(count_ref.shape[0]):
        owned = (owner_ref[a] <= block) & (block < owner_ref[a] + rank_ref[a])
        first = jnp.where(owned, start, first)
        amount = jnp.where(owned, count_ref[a], amount)
        start = start + count_ref[a]
    low = dot(a_ref[...], d_ref[0]).astype(BF16)
    slot = lax.broadcasted_iota(jnp.int32, (slots, total), 0)
    request, step = row_place(lax.broadcasted_iota(jnp.int32, (slots, total), 1), steps, rows)
    nth = slot % MOST
    pick = (step == slot // MOST) & (request == first + nth) & (nth < amount)
    chosen = dot(pick.astype(F32).astype(BF16), low).astype(BF16)
    for p in range(parts):
        out_ref[p] = dot_nt(chosen, u_ref[0, p * cols : (p + 1) * cols, :]).astype(BF16)


def delta_parts(gathered, store_down, store_up, tables, steps, rows, parts):
    total, width = gathered.shape
    slots = steps * MOST
    cols = width // parts
    rank_w = store_down.shape[2]
    vmem = pl.BlockSpec(memory_space=pltpu.VMEM)
    smem = pl.BlockSpec(memory_space=pltpu.SMEM)
    return pl.pallas_call(
        functools.partial(delta_kernel, steps, rows),
        out_shape=jax.ShapeDtypeStruct((parts, slots, cols), BF16),
        in_specs=[smem] * 3 + [vmem] * 3,
        out_specs=vmem,
        compiler_params=pltpu.CompilerParams(vmem_limit_bytes=40 * 2**20),
        cost_estimate=pl.CostEstimate(
            flops=2 * (total + slots) * width * rank_w,
            bytes_accessed=2 * width * (total + 2 * rank_w + slots),
            transcendentals=0,
        ),
        name="delta",
    )(*tables, gathered, store_down, store_up)


def base_kernel(a_ref, w_ref, out_ref):
    @pl.when(pl.program_id(0) == 0)
    def _():
        out_ref[...] = jnp.zeros_like(out_ref)

    out_ref[...] += dot(a_ref[...], w_ref[...])


def base_part(gathered, out_weight):
    total, width = gathered.shape
    cols = out_weight.shape[1]
    deep = 1024
    return pl.pallas_call(
        base_kernel,
        out_shape=jax.ShapeDtypeStruct((total, cols), F32),
        grid=(width // deep,),
        in_specs=[
            pl.BlockSpec((total, deep), lambda k: (0, k)),
            pl.BlockSpec((deep, cols), lambda k: (k, 0)),
        ],
        out_specs=pl.BlockSpec((total, cols), lambda k: (0, 0)),
        compiler_params=pltpu.CompilerParams(vmem_limit_bytes=24 * 2**20),
        cost_estimate=pl.CostEstimate(
            flops=2 * total * width * cols,
            bytes_accessed=2 * width * (total + cols) + 4 * total * cols,
            transcendentals=0,
        ),
        name="base",
    )(gathered, out_weight)


def join_kernel(rows, count_ref, rank_ref, owner_ref, base_ref, delta_ref, out_ref):
    steps, requests, cols = out_ref.shape
    parts, slots, _ = delta_ref.shape
    total = base_ref.shape[0]
    wide = parts * slots
    entry = lax.broadcasted_iota(jnp.int32, (1, wide), 1)
    block = entry // slots
    first = jnp.zeros((1, wide), jnp.int32)
    amount = jnp.zeros((1, wide), jnp.int32)
    start = jnp.int32(0)
    for a in range(count_ref.shape[0]):
        owned = (owner_ref[a] <= block) & (block < owner_ref[a] + rank_ref[a])
        first = jnp.where(owned, start, first)
        amount = jnp.where(owned, count_ref[a], amount)
        start = start + count_ref[a]
    nth = entry % MOST
    goal = jnp.where(nth < amount, first + nth, -1)
    goal_step = (entry % slots) // MOST
    request, step = row_place(lax.broadcasted_iota(jnp.int32, (total, 1), 0), steps, rows)
    place = (request == goal) & (step == goal_step)
    delta = dot(place.astype(F32).astype(BF16), delta_ref[...].reshape(wide, cols))
    result = (base_ref[...] + delta).astype(BF16)
    request, step = row_place(lax.broadcasted_iota(jnp.int32, (total, total), 1), steps, rows)
    goal = lax.broadcasted_iota(jnp.int32, (total, total), 0)
    order = (goal == step * requests + request).astype(F32).astype(BF16)
    turned = dot(order, result).astype(BF16)
    for t in range(steps):
        out_ref[t] = turned[t * requests : (t + 1) * requests]


def join(base, delta, tables, steps, rows):
    total, cols = base.shape
    vmem = pl.BlockSpec(memory_space=pltpu.VMEM)
    smem = pl.BlockSpec(memory_space=pltpu.SMEM)
    return pl.pallas_call(
        functools.partial(join_kernel, rows),
        out_shape=jax.ShapeDtypeStruct((steps, total // steps, cols), BF16),
        in_specs=[smem] * 3 + [vmem] * 2,
        out_specs=vmem,
        compiler_params=pltpu.CompilerParams(vmem_limit_bytes=24 * 2**20),
        name="join",
    )(*tables, base, delta)


def per_device(
    queries,
    new_keys,
    new_values,
    cache_keys,
    cache_values,
    kv_len,
    adapter_rows,
    adapter_rank,
    adapter_owner,
    out_weight,
    store_down,
    store_up,
):
    parts = lax.axis_size("tensor")
    steps, rows, width = queries.shape
    tables = (adapter_rows, adapter_rank, adapter_owner)
    attended = attend(queries, new_keys, new_values, cache_keys, cache_values, kv_len)
    gathered = lax.all_gather(attended, "tensor", axis=0, tiled=True)
    send = delta_parts(gathered, store_down, store_up, tables, steps, rows, parts)
    delta = lax.all_to_all(send, "tensor", split_axis=0, concat_axis=0, tiled=True)
    base = base_part(gathered, out_weight)
    return join(base, delta, tables, steps, rows)


def solution(mesh):
    in_specs = (
        P(None, ("groups", "tensor"), None),
        P(None, ("groups", "tensor"), None),
        P(None, ("groups", "tensor"), None),
        P(("groups", "tensor"), None, None),
        P(("groups", "tensor"), None, None),
        P(("groups", "tensor")),
        P("groups"),
        P(),
        P(),
        P(None, "tensor"),
        P("tensor", None, None),
        P("tensor", None, None),
    )
    out_specs = P(None, "groups", "tensor")
    return jax.shard_map(
        per_device, mesh=mesh, in_specs=in_specs, out_specs=out_specs, check_vma=False
    )
```

time: 182 us -> 93.3 us (0.51)
  blocking collectives: 67.1 us -> 0 us
  starting transfers between devices: 18.9 us -> 3.53 us
  matrix products: 14.1 us -> 0 us
  Pallas kernels: 0 us -> 12.2 us
  waiting for transfers between devices: 53.2 us -> 48.1 us
  local copies, waits for them, and re-layouts: 13.3 us -> 15.5 us
    psum x1 -> x0, blocking collectives: 67.1 us -> none  [per_device(): summed = lax.psum(joined[:, :, cols:], 'tensor')]
    all_to_all x2 -> x1, waiting for transfers between devices: 30.8 us -> 3.8 us  [per_device(): lax.all_to_all(send, 'tensor', split_axis=0, concat_axis=0, tiled=True)]
    all_gather x1, waiting for transfers between devices: 22.4 us -> 44.3 us  [per_device(): gathered = lax.all_gather(attended, 'tensor', axis=0, tiled=True)]
    all_to_all x2 -> x1, starting transfers between devices: 18.9 us -> 3.53 us  [per_device(): lax.all_to_all(send, 'tensor', split_axis=0, concat_axis=0, tiled=True)]
    dot_general x9 -> x0, matrix products: 14.1 us -> none  [the longest x1 5.29 us: per_device(): jnp.einsum('trd,dc->trc', piece, out_weight, preferred_element_type=jnp.f...]
    pallas_call x0 -> x4, Pallas kernels: none -> 12.2 us  [the longest x1 5.12 us: attend(): pl.pallas_call(attend_kernel, out_shape=jax.ShapeDtypeStruct((steps * row...]
    unnamed x24 -> x28, local copies, waits for them, and re-layouts: 8.73 us -> 15.5 us
    all_gather x1 -> x0, local copies, waits for them, and re-layouts: 2.9 us -> none  [per_device(): piece = lax.all_gather(attended, 'tensor', axis=1, tiled=True)]
  transfers between devices with their start and end apart: 3 -> 2, of which waited for: 2 -> 2; matrix products, arithmetic and copies ran while one was open for 14% -> 0% of each run, Pallas kernels for 0% -> 3%
where the time goes in v1:
time: 93.3 us; the launch traced here: 92.8 us
  waiting for transfers between devices  48.1 us (52%)
  local copies, waits for them, and re-layouts  15.5 us (17%)
  between operations  13.4 us (14%)
  Pallas kernels  12.2 us (13%)
  starting transfers between devices  3.53 us (4%)
    all_gather x1, waiting for transfers between devices, per_device(): gathered = lax.all_gather(attended, 'tensor', axis=0, tiled=True)  44.3 us
    unnamed x28, local copies, waits for them, and re-layouts  15.5 us
    pallas_call x1, Pallas kernels, attend(): pl.pallas_call(attend_kernel, out_shape=jax.ShapeDtypeStruct((steps * row...  5.12 us
    all_to_all x1, waiting for transfers between devices, per_device(): lax.all_to_all(send, 'tensor', split_axis=0, concat_axis=0, tiled=True)  3.8 us
    all_to_all x1, starting transfers between devices, per_device(): lax.all_to_all(send, 'tensor', split_axis=0, concat_axis=0, tiled=True)  3.53 us
    pallas_call x1, Pallas kernels, base_part(): pl.pallas_call(base_kernel, out_shape=jax.ShapeDtypeStruct((total, cols),...  2.8 us
    pallas_call x1, Pallas kernels, delta_parts(): pl.pallas_call(functools.partial(delta_kernel, steps, rows), out_shape=ja...  2.74 us
  transfers between devices with their start and end apart: 2, of which 2 were waited for; matrix products, arithmetic and copies ran while one was open for 0% of the time, Pallas kernels for 3%

profile of v1, /device:TPU:0, one launch (start us, length us, event | category | flops | bytes accessed | tf_op | source)
XLA Modules:
  0.0 92.8 jit_solution(4315808363793414103)
XLA Ops:
  6.5 0.0 all-gather.2.cloned.1.call-start
  6.5 0.0 copy-start.3
  6.5 2.2 %copy-done.3 = bf16[4,512,1024]{2,1,0:T(8,128)(2,1)S(1)} copy-done((bf16[4,512,1024]{2,1,0:T(8,128)(2,1)S(1)}, bf16[4,512,1024]{2,1,0:T(8,128)(2,1)}, u32[]{:S(2)}) %copy-start.3) | copy-done | bytes 4194328
  8.7 0.0 copy-start.4
  8.7 2.2 %copy-done.4 = bf16[4,512,1024]{2,1,0:T(8,128)(2,1)S(1)} copy-done((bf16[4,512,1024]{2,1,0:T(8,128)(2,1)S(1)}, bf16[4,512,1024]{2,1,0:T(8,128)(2,1)}, u32[]{:S(2)}) %copy-start.4) | copy-done | bytes 4194328
  10.9 0.0 copy-start.7
  10.9 0.9 copy-done.7
  11.8 0.0 copy-start.8
  11.8 0.7 copy-done.8
  12.5 0.0 copy-start.9
  12.5 0.7 copy-done.9
  13.3 0.0 copy-start.13
  13.3 0.7 copy-done.13
  13.9 0.0 copy-start.10
  13.9 0.0 copy-start.12
  13.9 5.1 %attend.1 = bf16[8,8192]{1,0:T(8,128)(2,1)} custom-call(s32[4]{0:T(128)S(1)} %copy-done.13, bf16[2,4,8192]{2,1,0:T(4,128)(2,1)S(1)} %copy-done.7, bf16[2,4,1024]{2,1,0:T(4,128)(2,1)S(1)} %copy-done.8, bf16[2,4,1024]{2,1,0:T(4,128)(2,1)S(1)} %copy-done.9, bf16[4,512,1024]{2,1,0:T(8,128)(2,1)S(1)} %copy-done.3, bf16[4,512,1024]{2,1,0:T(8,128)(2,1)S(1)} %copy-done.4), custom_call_target="tpu_custom_call" | custom-call | flops 134217728 | bytes 8388608 | tf_op jit(solution)/shard_map/attend/pallas_call | solution.py:104
  19.0 0.0 all-gather.2.cloned.1.call-update
  19.1 44.3 %all-gather.2.cloned.1.call-done.a_ref = bf16[128,8192]{1,0:T(8,128)(2,1)} async-done(((bf16[8,8192]{1,0:T(8,128)(2,1)}), bf16[128,8192]{1,0:T(8,128)(2,1)}) %all-gather.2.cloned.1.call-update) | async-done | bytes 2097168 | tf_op jit(solution)/shard_map/all_gather | solution.py:277
  63.3 0.0 copy-done.10
  63.3 0.0 copy-done.11
  63.3 0.0 copy-done.12
  63.3 1.6 %copy-done.1 = bf16[128,8192]{1,0:T(8,128)(2,1)S(1)} copy-done((bf16[128,8192]{1,0:T(8,128)(2,1)S(1)}, bf16[128,8192]{1,0:T(8,128)(2,1)}, u32[]{:S(2)}) %copy-start.1) | copy-done | bytes 2097176
  64.9 1.6 %copy-done.5 = bf16[1,8192,128]{2,1,0:T(8,128)(2,1)S(1)} copy-done((bf16[1,8192,128]{2,1,0:T(8,128)(2,1)S(1)}, bf16[1,8192,128]{2,1,0:T(8,128)(2,1)}, u32[]{:S(2)}) %copy-start.5) | copy-done | bytes 2097176
  66.5 1.6 %copy-done.6 = bf16[1,8192,128]{2,1,0:T(8,128)(2,1)S(1)} copy-done((bf16[1,8192,128]{2,1,0:T(8,128)(2,1)S(1)}, bf16[1,8192,128]{2,1,0:T(8,128)(2,1)}, u32[]{:S(2)}) %copy-start.6) | copy-done | bytes 2097176
  68.1 2.7 %delta.1 = bf16[16,16,512]{2,1,0:T(8,128)(2,1)} custom-call(s32[12]{0:T(128)S(1)} %copy-done.10, s32[12]{0:T(128)S(1)} %copy-done.11, s32[12]{0:T(128)S(1)} %copy-done.12, bf16[128,8192]{1,0:T(8,128)(2,1)S(1)} %copy-done.1, bf16[1,8192,128]{2,1,0:T(8,128)(2,1)S(1)} %copy-done.5, bf16[1,8192,128]{2,1,0:T(8,128)(2,1)S(1)} %copy-done.6), custom_call_target="tpu_custom_call" | custom-call | flops 301989888 | bytes 6553600 | tf_op jit(solution)/shard_map/delta/pallas_call | solution.py:169
  70.8 3.5 %all-to-all-start = ((bf16[16,16,512]{2,1,0:T(8,128)(2,1)}), bf16[16,16,512]{2,1,0:T(8,128)(2,1)S(1)}, u32[]{:S(2)}, u32[]{:S(2)}) async-start(bf16[16,16,512]{2,1,0:T(8,128)(2,1)} %delta.1), calls=%async_computation | async-start | bytes 524288 | tf_op jit(solution)/shard_map/all_to_all | solution.py:279
  74.4 0.0 copy-done.2
  74.4 0.0 copy-start
  74.4 3.4 %copy-done = bf16[8192,512]{1,0:T(8,128)(2,1)S(1)} copy-done((bf16[8192,512]{1,0:T(8,128)(2,1)S(1)}, bf16[8192,512]{1,0:T(8,128)(2,1)}, u32[]{:S(2)}) %copy-start) | copy-done | bytes 8388632
  77.8 2.8 %base.1.base_ref = f32[128,512]{1,0:T(8,128)S(1)} custom-call(bf16[128,8192]{1,0:T(8,128)(2,1)S(1)} %copy-done.2, bf16[8192,512]{1,0:T(8,128)(2,1)S(1)} %copy-done), custom_call_target="tpu_custom_call" | custom-call | flops 1073741824 | bytes 10747904 | tf_op jit(solution)/shard_map/base/pallas_call | solution.py:196
  80.6 3.8 %all-to-all-done.delta_ref = bf16[16,16,512]{2,1,0:T(8,128)(2,1)S(1)} async-done(((bf16[16,16,512]{2,1,0:T(8,128)(2,1)}), bf16[16,16,512]{2,1,0:T(8,128)(2,1)S(1)}, u32[]{:S(2)}, u32[]{:S(2)}) %all-to-all-start) | async-done | bytes 262176 | tf_op jit(solution)/shard_map/all_to_all | solution.py:279
  84.4 1.6 %join.1 = bf16[2,64,512]{2,1,0:T(8,128)(2,1)} custom-call(s32[12]{0:T(128)S(1)} %copy-done.10, s32[12]{0:T(128)S(1)} %copy-done.11, s32[12]{0:T(128)S(1)} %copy-done.12, f32[128,512]{1,0:T(8,128)S(1)} %base.1.base_ref, bf16[16,16,512]{2,1,0:T(8,128)(2,1)S(1)} %all-to-all-done.delta_ref), custom_call_target="tpu_custom_call" | custom-call | tf_op jit(solution)/shard_map/join/pallas_call | solution.py:249
  (5 shorter events, 0.0 us)
Async XLA Ops:
  6.5 56.8 %all-gather.2.cloned.1.call-start = ((), (), s32[]{:S(2)}) async-start(), calls=%async_computation.1 | async-start | bytes 2228224 | tf_op jit(solution)/shard_map/all_gather | solution.py:277
  6.5 2.2 %copy-start.3 = (bf16[4,512,1024]{2,1,0:T(8,128)(2,1)S(1)}, bf16[4,512,1024]{2,1,0:T(8,128)(2,1)}, u32[]{:S(2)}) copy-start(bf16[4,512,1024]{2,1,0:T(8,128)(2,1)} %k_ref.1) | copy-start | bytes 12582916
  8.7 2.2 %copy-start.4 = (bf16[4,512,1024]{2,1,0:T(8,128)(2,1)S(1)}, bf16[4,512,1024]{2,1,0:T(8,128)(2,1)}, u32[]{:S(2)}) copy-start(bf16[4,512,1024]{2,1,0:T(8,128)(2,1)} %v_ref.1) | copy-start | bytes 12582916
  10.9 0.9 copy-start.7
  11.8 0.7 copy-start.8
  12.5 0.7 copy-start.9
  13.3 0.7 copy-start.13
  13.9 49.4 %copy-start.10 = (s32[12]{0:T(128)S(1)}, s32[12]{0:T(128)}, u32[]{:S(2)}) copy-start(s32[12]{0:T(128)} %count_ref.3) | copy-start | bytes 148
  13.9 49.4 %copy-start.11 = (s32[12]{0:T(128)S(1)}, s32[12]{0:T(128)}, u32[]{:S(2)}) copy-start(s32[12]{0:T(128)} %rank_ref.3) | copy-start | bytes 148
  13.9 49.4 %copy-start.12 = (s32[12]{0:T(128)S(1)}, s32[12]{0:T(128)}, u32[]{:S(2)}) copy-start(s32[12]{0:T(128)} %owner_ref.3) | copy-start | bytes 148
  63.3 1.6 %copy-start.1 = (bf16[128,8192]{1,0:T(8,128)(2,1)S(1)}, bf16[128,8192]{1,0:T(8,128)(2,1)}, u32[]{:S(2)}) copy-start(bf16[128,8192]{1,0:T(8,128)(2,1)} %all-gather.2.cloned.1.call-done.a_ref) | copy-start | bytes 6291460
  64.9 1.6 %copy-start.5 = (bf16[1,8192,128]{2,1,0:T(8,128)(2,1)S(1)}, bf16[1,8192,128]{2,1,0:T(8,128)(2,1)}, u32[]{:S(2)}) copy-start(bf16[1,8192,128]{2,1,0:T(8,128)(2,1)} %d_ref.1) | copy-start | bytes 6291460
  66.5 1.6 %copy-start.6 = (bf16[1,8192,128]{2,1,0:T(8,128)(2,1)S(1)}, bf16[1,8192,128]{2,1,0:T(8,128)(2,1)}, u32[]{:S(2)}) copy-start(bf16[1,8192,128]{2,1,0:T(8,128)(2,1)} %u_ref.1) | copy-start | bytes 6291460
  68.1 6.3 %copy-start.2 = (bf16[128,8192]{1,0:T(8,128)(2,1)S(1)}, bf16[128,8192]{1,0:T(8,128)(2,1)}, u32[]{:S(2)}) copy-start(bf16[128,8192]{1,0:T(8,128)(2,1)} %all-gather.2.cloned.1.call-done.a_ref) | copy-start | bytes 6291460
  70.8 13.5 %all-to-all-start = ((bf16[16,16,512]{2,1,0:T(8,128)(2,1)}), bf16[16,16,512]{2,1,0:T(8,128)(2,1)S(1)}, u32[]{:S(2)}, u32[]{:S(2)}) async-start(bf16[16,16,512]{2,1,0:T(8,128)(2,1)} %delta.1), calls=%async_computation | async-start | bytes 524288 | tf_op jit(solution)/shard_map/all_to_all | solution.py:279
  74.4 3.4 %copy-start = (bf16[8192,512]{1,0:T(8,128)(2,1)S(1)}, bf16[8192,512]{1,0:T(8,128)(2,1)}, u32[]{:S(2)}) copy-start(bf16[8192,512]{1,0:T(8,128)(2,1)} %w_ref.1) | copy-start | bytes 25165828
Sparse Core Ops, SparseCore 0:
  19.2 44.0 all-gather.1

commit v2 on v1

--- a/solution.py
+++ b/solution.py
@@ -12,6 +12,7 @@
 HD = 128
 GROUP = HQ // KVH
 MOST = 8
+RING = 16
 F32 = jnp.float32
 BF16 = jnp.bfloat16
 NT = (((1,), (1,)), ((), ()))
@@ -129,18 +130,66 @@
             transcendentals=rows * steps * HQ * cache,
         ),
         name="attend",
-    )(kv_len, queries, new_keys, new_values, cache_keys, cache_values)
-
-
-def row_place(index, steps, rows):
+    )(
+        kv_len,
+        queries,
+        new_keys,
+        new_values,
+        pltpu.with_memory_space_constraint(cache_keys, pltpu.HBM),
+        pltpu.with_memory_space_constraint(cache_values, pltpu.HBM),
+    )
+
+
+def sender(slot, me, parts):
+    if parts != RING:
+        return slot
+    ahead = (me // 4 + RING // 4 - slot // 4) % (RING // 4)
+    return ahead * 4 + ((me % 4) ^ (slot % 4))
+
+
+def row_place(index, me, parts, steps, rows):
     both = steps * rows
-    return (index // both) * rows + index % rows, (index % both) // rows
-
-
-def delta_kernel(steps, rows, count_ref, rank_ref, owner_ref, a_ref, d_ref, u_ref, out_ref):
+    return sender(index // both, me, parts) * rows + index % rows, (index % both) // rows
+
+
+def gather(block, parts):
+    if parts != RING:
+        whole = lax.all_gather(block, "tensor", axis=0, tiled=False)
+        return [whole[i] for i in range(parts)]
+    devices = range(RING)
+
+    def forward(x, back):
+        pairs = [(i, (i + 4 * back) % RING) for i in devices]
+        return lax.ppermute(x, "tensor", pairs)
+
+    def flip(x, bit):
+        return lax.ppermute(x, "tensor", [(i, i ^ bit) for i in devices])
+
+    column = [block] + [forward(block, back) for back in range(1, RING // 4)]
+    other = [flip(x, 2) for x in column]
+    held = []
+    for x, y in zip(column, other):
+        held += [x, flip(x, 1), y, flip(y, 1)]
+    return held
+
+
+def delta_kernel(steps, rows, parts, count_ref, rank_ref, owner_ref, d_hbm, u_hbm, *rest):
+    blocks, (out_ref, down, up, sems) = rest[:parts], rest[parts:]
     block = lax.axis_index("tensor")
-    total = a_ref.shape[0]
-    parts, slots, cols = out_ref.shape
+    each, width = blocks[0].shape
+    total = parts * each
+    _, slots, cols = out_ref.shape
+    cuts = 4
+    deep = width // cuts
+    copies = [
+        pltpu.make_async_copy(
+            src.at[0, pl.ds(i * deep, deep)], dst.at[pl.ds(i * deep, deep)], sems.at[j, i]
+        )
+        for j, (src, dst) in enumerate(((d_hbm, down), (u_hbm, up)))
+        for i in range(cuts)
+    ]
+    for copy in copies:
+        copy.start()
     start = jnp.int32(0)
     first = jnp.int32(0)
     amount = jnp.int32(0)
@@ -149,58 +198,78 @@
         first = jnp.where(owned, start, first)
         amount = jnp.where(owned, count_ref[a], amount)
         start = start + count_ref[a]
-    low = dot(a_ref[...], d_ref[0]).astype(BF16)
     slot = lax.broadcasted_iota(jnp.int32, (slots, total), 0)
-    request, step = row_place(lax.broadcasted_iota(jnp.int32, (slots, total), 1), steps, rows)
+    place = lax.broadcasted_iota(jnp.int32, (slots, total), 1)
+    request, step = row_place(place, block, parts, steps, rows)
     nth = slot % MOST
     pick = (step == slot // MOST) & (request == first + nth) & (nth < amount)
-    chosen = dot(pick.astype(F32).astype(BF16), low).astype(BF16)
+    low = jnp.zeros((total, down.shape[1]), F32)
+    for i in range(cuts):
+        at = slice(i * deep, (i + 1) * deep)
+        copies[i].wait()
+        low = low + dot(jnp.concatenate([b[:, at] for b in blocks], axis=0), down[at, :])
+    chosen = dot(pick.astype(F32).astype(BF16), low.astype(BF16)).astype(BF16)
     for p in range(parts):
-        out_ref[p] = dot_nt(chosen, u_ref[0, p * cols : (p + 1) * cols, :]).astype(BF16)
-
-
-def delta_parts(gathered, store_down, store_up, tables, steps, rows, parts):
-    total, width = gathered.shape
+        if p % (parts // cuts) == 0:
+            copies[cuts + p // (parts // cuts)].wait()
+        out_ref[p] = dot_nt(chosen, up[p * cols : (p + 1) * cols, :]).astype(BF16)
+
+
+def delta_parts(blocks, store_down, store_up, tables, steps, rows):
+    parts = len(blocks)
+    each, width = blocks[0].shape
     slots = steps * MOST
     cols = width // parts
     rank_w = store_down.shape[2]
     vmem = pl.BlockSpec(memory_space=pltpu.VMEM)
     smem = pl.BlockSpec(memory_space=pltpu.SMEM)
+    hbm = pl.BlockSpec(memory_space=pl.ANY)
     return pl.pallas_call(
-        functools.partial(delta_kernel, steps, rows),
+        functools.partial(delta_kernel, steps, rows, parts),
         out_shape=jax.ShapeDtypeStruct((parts, slots, cols), BF16),
-        in_specs=[smem] * 3 + [vmem] * 3,
+        in_specs=[smem] * 3 + [hbm] * 2 + [vmem] * parts,
         out_specs=vmem,
+        scratch_shapes=[
+            pltpu.VMEM((width, rank_w), BF16),
+            pltpu.VMEM((width, rank_w), BF16),
+            pltpu.SemaphoreType.DMA((2, 4)),
+        ],
         compiler_params=pltpu.CompilerParams(vmem_limit_bytes=40 * 2**20),
         cost_estimate=pl.CostEstimate(
-            flops=2 * (total + slots) * width * rank_w,
-            bytes_accessed=2 * width * (total + 2 * rank_w + slots),
+            flops=2 * (parts * each + slots) * width * rank_w,
+            bytes_accessed=2 * width * (parts * each + 2 * rank_w + slots),
             transcendentals=0,
         ),
         name="delta",
-    )(*tables, gathered, store_down, store_up)
-
-
-def base_kernel(a_ref, w_ref, out_ref):
+    )(
+        *tables,
+        pltpu.with_memory_space_constraint(store_down, pltpu.HBM),
+        pltpu.with_memory_space_constraint(store_up, pltpu.HBM),
+        *blocks,
+    )
+
+
+def base_kernel(*refs):
+    blocks, (w_ref, out_ref) = refs[:-2], refs[-2:]
+
     @pl.when(pl.program_id(0) == 0)
     def _():
         out_ref[...] = jnp.zeros_like(out_ref)
 
-    out_ref[...] += dot(a_ref[...], w_ref[...])
-
-
-def base_part(gathered, out_weight):
-    total, width = gathered.shape
+    out_ref[...] += dot(jnp.concatenate([b[...] for b in blocks], axis=0), w_ref[...])
+
+
+def base_part(blocks, out_weight):
+    each, width = blocks[0].shape
+    total = len(blocks) * each
     cols = out_weight.shape[1]
     deep = 1024
     return pl.pallas_call(
         base_kernel,
         out_shape=jax.ShapeDtypeStruct((total, cols), F32),
         grid=(width // deep,),
-        in_specs=[
-            pl.BlockSpec((total, deep), lambda k: (0, k)),
-            pl.BlockSpec((deep, cols), lambda k: (k, 0)),
-        ],
+        in_specs=[pl.BlockSpec((each, deep), lambda k: (0, k))] * len(blocks)
+        + [pl.BlockSpec((deep, cols), lambda k: (k, 0))],
         out_specs=pl.BlockSpec((total, cols), lambda k: (0, 0)),
         compiler_params=pltpu.CompilerParams(vmem_limit_bytes=24 * 2**20),
         cost_estimate=pl.CostEstimate(
@@ -209,13 +278,14 @@
             transcendentals=0,
         ),
         name="base",
-    )(gathered, out_weight)
+    )(*blocks, out_weight)
 
 
 def join_kernel(rows, count_ref, rank_ref, owner_ref, base_ref, delta_ref, out_ref):
     steps, requests, cols = out_ref.shape
     parts, slots, _ = delta_ref.shape
     total = base_ref.shape[0]
+    me = lax.axis_index("tensor")
     wide = parts * slots
     entry = lax.broadcasted_iota(jnp.int32, (1, wide), 1)
     block = entry // slots
@@ -230,11 +300,15 @@
     nth = entry % MOST
     goal = jnp.where(nth < amount, first + nth, -1)
     goal_step = (entry % slots) // MOST
-    request, step = row_place(lax.broadcasted_iota(jnp.int32, (total, 1), 0), steps, rows)
+    request, step = row_place(
+        lax.broadcasted_iota(jnp.int32, (total, 1), 0), me, parts, steps, rows
+    )
     place = (request == goal) & (step == goal_step)
     delta = dot(place.astype(F32).astype(BF16), delta_ref[...].reshape(wide, cols))
     result = (base_ref[...] + delta).astype(BF16)
-    request, step = row_place(lax.broadcasted_iota(jnp.int32, (total, total), 1), steps, rows)
+    request, step = row_place(
+        lax.broadcasted_iota(jnp.int32, (total, total), 1), me, parts, steps, rows
+    )
     goal = lax.broadcasted_iota(jnp.int32, (total, total), 0)
     order = (goal == step * requests + request).astype(F32).astype(BF16)
     turned = dot(order, result).astype(BF16)
@@ -274,10 +348,10 @@
     steps, rows, width = queries.shape
     tables = (adapter_rows, adapter_rank, adapter_owner)
     attended = attend(queries, new_keys, new_values, cache_keys, cache_values, kv_len)
-    gathered = lax.all_gather(attended, "tensor", axis=0, tiled=True)
-    send = delta_parts(gathered, store_down, store_up, tables, steps, rows, parts)
+    blocks = gather(attended, parts)
+    send = delta_parts(blocks, store_down, store_up, tables, steps, rows)
     delta = lax.all_to_all(send, "tensor", split_axis=0, concat_axis=0, tiled=True)
-    base = base_part(gathered, out_weight)
+    base = base_part(blocks, out_weight)
     return join(base, delta, tables, steps, rows)
 
 

time: 93.3 us -> 57 us (0.61)
  waiting for transfers between devices: 48.1 us -> 17.9 us
  between operations: 13.4 us -> 0.09 us
  starting transfers between devices: 3.53 us -> 16.5 us
  local copies, waits for them, and re-layouts: 15.5 us -> 6.38 us
  Pallas kernels: 12.2 us -> 15.7 us
    all_gather x1 -> x0, waiting for transfers between devices: 44.3 us -> none  [per_device(): gathered = lax.all_gather(attended, 'tensor', axis=0, tiled=True)]
    ppermute x0 -> x15, waiting for transfers between devices: none -> 13.9 us  [the longest x3 7.15 us: forward(): return lax.ppermute(x, 'tensor', pairs)]
    ppermute x0 -> x15, starting transfers between devices: none -> 12.4 us  [the longest x12 6.32 us: flip(): return lax.ppermute(x, 'tensor', [(i, i ^ bit) for i in devices])]
    unnamed x28 -> x16, local copies, waits for them, and re-layouts: 15.5 us -> 6.38 us
    pallas_call x1, Pallas kernels: 2.74 us -> 4.71 us  [delta_parts(): pl.pallas_call(functools.partial(delta_kernel, steps, rows, parts), out_s...]
    pallas_call x1, Pallas kernels: 5.12 us -> 6.74 us  [attend(): pl.pallas_call(attend_kernel, out_shape=jax.ShapeDtypeStruct((steps * row...]
  transfers between devices with their start and end apart: 2 -> 16, of which waited for: 2 -> 6; matrix products, arithmetic and copies ran while one was open for 0% -> 0% of each run, Pallas kernels for 3% -> 5%
where the time goes in v2:
time: 57 us; the launch traced here: 56.6 us
  waiting for transfers between devices  17.9 us (31%)
  starting transfers between devices  16.5 us (29%)
  Pallas kernels  15.7 us (28%)
  local copies, waits for them, and re-layouts  6.38 us (11%)
    ppermute x3, waiting for transfers between devices, forward(): return lax.ppermute(x, 'tensor', pairs)  7.15 us
    ppermute x12, waiting for transfers between devices, flip(): return lax.ppermute(x, 'tensor', [(i, i ^ bit) for i in devices])  6.76 us
    pallas_call x1, Pallas kernels, attend(): pl.pallas_call(attend_kernel, out_shape=jax.ShapeDtypeStruct((steps * row...  6.74 us
    unnamed x16, local copies, waits for them, and re-layouts  6.38 us
    ppermute x12, starting transfers between devices, flip(): return lax.ppermute(x, 'tensor', [(i, i ^ bit) for i in devices])  6.32 us
    ppermute x3, starting transfers between devices, forward(): return lax.ppermute(x, 'tensor', pairs)  6.12 us
    pallas_call x1, Pallas kernels, delta_parts(): pl.pallas_call(functools.partial(delta_kernel, steps, rows, parts), out_s...  4.71 us
    all_to_all x1, starting transfers between devices, per_device(): lax.all_to_all(send, 'tensor', split_axis=0, concat_axis=0, tiled=True)  4.04 us
  transfers between devices with their start and end apart: 16, of which 6 were waited for; matrix products, arithmetic and copies ran while one was open for 0% of the time, Pallas kernels for 5%

profile of v2, /device:TPU:0, one launch (start us, length us, event | category | flops | bytes accessed | tf_op | source)
XLA Modules:
  0.0 56.6 jit_solution(11851673231113387419)
XLA Ops:
  0.0 0.9 %copy-done.1 = bf16[2,4,8192]{2,1,0:T(4,128)(2,1)S(1)} copy-done((bf16[2,4,8192]{2,1,0:T(4,128)(2,1)S(1)}, bf16[2,4,8192]{2,1,0:T(4,128)(2,1)}, u32[]{:S(2)}) %copy-start.1) | copy-done | bytes 131096
  0.9 0.7 %copy-done.2 = bf16[2,4,1024]{2,1,0:T(4,128)(2,1)S(1)} copy-done((bf16[2,4,1024]{2,1,0:T(4,128)(2,1)S(1)}, bf16[2,4,1024]{2,1,0:T(4,128)(2,1)}, u32[]{:S(2)}) %copy-start.2) | copy-done | bytes 16408
  1.6 0.7 %copy-done.3 = bf16[2,4,1024]{2,1,0:T(4,128)(2,1)S(1)} copy-done((bf16[2,4,1024]{2,1,0:T(4,128)(2,1)S(1)}, bf16[2,4,1024]{2,1,0:T(4,128)(2,1)}, u32[]{:S(2)}) %copy-start.3) | copy-done | bytes 16408
  2.3 0.7 %copy-done.7 = s32[4]{0:T(128)S(1)} copy-done((s32[4]{0:T(128)S(1)}, s32[4]{0:T(128)}, u32[]{:S(2)}) %copy-start.7) | copy-done | bytes 40
  3.0 6.7 %attend.1.refs_0_.rest_0_ = bf16[8,8192]{1,0:T(8,128)(2,1)S(1)} custom-call(s32[4]{0:T(128)S(1)} %copy-done.7, bf16[2,4,8192]{2,1,0:T(4,128)(2,1)S(1)} %copy-done.1, bf16[2,4,1024]{2,1,0:T(4,128)(2,1)S(1)} %copy-done.2, bf16[2,4,1024]{2,1,0:T(4,128)(2,1)S(1)} %copy-done.3, bf16[4,512,1024]{2,1,0:T(8,128)(2,1)} %k_ref.1, bf16[4,512,1024]{2,1,0:T(8,128)(2,1)} %v_ref.1), custom_call_target="tpu_custom_call" | custom-call | flops 134217728 | bytes 8388608 | tf_op jit(solution)/shard_map/attend/pallas_call | solution.py:105
  9.8 5.1 %collective-permute-start.11 = (bf16[8,8192]{1,0:T(8,128)(2,1)S(1)}, bf16[8,8192]{1,0:T(8,128)(2,1)S(1)}, u32[]{:S(2)}, u32[]{:S(2)}) collective-permute-start(bf16[8,8192]{1,0:T(8,128)(2,1)S(1)} %attend.1.refs_0_.rest_0_), channel_id=1, source_target_pairs={{0,12},{1,13},{2,14},{3,15},{4,0},{5,1},{6,2},{7,3},{8,4},{9,5},{1... | collective-permute-start | bytes 393224 | tf_op jit(solution)/shard_map/ppermute | solution.py:163
  14.9 0.0 collective-permute-start.7
  14.9 1.0 %collective-permute-start.3 = (bf16[8,8192]{1,0:T(8,128)(2,1)S(1)}, bf16[8,8192]{1,0:T(8,128)(2,1)S(1)}, u32[]{:S(2)}, u32[]{:S(2)}) collective-permute-start(bf16[8,8192]{1,0:T(8,128)(2,1)S(1)} %attend.1.refs_0_.rest_0_), channel_id=1, source_target_pairs={{0,4},{1,5},{2,6},{3,7},{4,8},{5,9},{6,10},{7,11},{8,12},{9,13},{1... | collective-permute-start | bytes 393224 | tf_op jit(solution)/shard_map/ppermute | solution.py:163
  15.9 1.5 %collective-permute-start.1 = (bf16[8,8192]{1,0:T(8,128)(2,1)S(1)}, bf16[8,8192]{1,0:T(8,128)(2,1)S(1)}, u32[]{:S(2)}, u32[]{:S(2)}) collective-permute-start(bf16[8,8192]{1,0:T(8,128)(2,1)S(1)} %attend.1.refs_0_.rest_0_), channel_id=1, source_target_pairs={{0,2},{1,3},{2,0},{3,1},{4,6},{5,7},{6,4},{7,5},{8,10},{9,11},{10,... | collective-permute-start | bytes 393224 | tf_op jit(solution)/shard_map/ppermute | solution.py:166
  17.4 0.0 collective-permute-start
  17.4 1.4 %collective-permute-done.11.refs_12_.rest_12_ = bf16[8,8192]{1,0:T(8,128)(2,1)S(1)} collective-permute-done((bf16[8,8192]{1,0:T(8,128)(2,1)S(1)}, bf16[8,8192]{1,0:T(8,128)(2,1)S(1)}, u32[]{:S(2)}, u32[]{:S(2)}) %collective-permute-start.11) | collective-permute-done | bytes 131104 | tf_op jit(solution)/shard_map/ppermute | solution.py:163
  18.8 1.5 %collective-permute-start.13 = (bf16[8,8192]{1,0:T(8,128)(2,1)S(1)}, bf16[8,8192]{1,0:T(8,128)(2,1)S(1)}, u32[]{:S(2)}, u32[]{:S(2)}) collective-permute-start(bf16[8,8192]{1,0:T(8,128)(2,1)S(1)} %collective-permute-done.11.refs_12_.rest_12_), channel_id=1, source_target_pairs={{0,2},{1,3},{2,0},{3,1},{4,6},{5,7},{6,4},{7,5},{8,10},{9,11},{10,... | collective-permute-start | bytes 393224 | tf_op jit(solution)/shard_map/ppermute | solution.py:166
  20.3 5.8 %collective-permute-done.7.refs_8_.rest_8_ = bf16[8,8192]{1,0:T(8,128)(2,1)S(1)} collective-permute-done((bf16[8,8192]{1,0:T(8,128)(2,1)S(1)}, bf16[8,8192]{1,0:T(8,128)(2,1)S(1)}, u32[]{:S(2)}, u32[]{:S(2)}) %collective-permute-start.7) | collective-permute-done | bytes 131104 | tf_op jit(solution)/shard_map/ppermute | solution.py:163
  26.1 0.0 collective-permute-start.12
  26.1 0.0 collective-permute-done.3.refs_4_.rest_4_
  26.1 1.5 %collective-permute-start.9 = (bf16[8,8192]{1,0:T(8,128)(2,1)S(1)}, bf16[8,8192]{1,0:T(8,128)(2,1)S(1)}, u32[]{:S(2)}, u32[]{:S(2)}) collective-permute-start(bf16[8,8192]{1,0:T(8,128)(2,1)S(1)} %collective-permute-done.7.refs_8_.rest_8_), channel_id=1, source_target_pairs={{0,2},{1,3},{2,0},{3,1},{4,6},{5,7},{6,4},{7,5},{8,10},{9,11},{10,... | collective-permute-start | bytes 393224 | tf_op jit(solution)/shard_map/ppermute | solution.py:166
  27.6 0.0 collective-permute-done.1.refs_2_.rest_2_
  27.6 0.2 collective-permute-start.8
  27.8 0.5 collective-permute-start.5
  28.3 0.0 collective-permute-start.4
  28.3 0.5 collective-permute-start.2
  28.8 3.5 %collective-permute-done.9.refs_10_.rest_10_ = bf16[8,8192]{1,0:T(8,128)(2,1)S(1)} collective-permute-done((bf16[8,8192]{1,0:T(8,128)(2,1)S(1)}, bf16[8,8192]{1,0:T(8,128)(2,1)S(1)}, u32[]{:S(2)}, u32[]{:S(2)}) %collective-permute-start.9) | collective-permute-done | bytes 131104 | tf_op jit(solution)/shard_map/ppermute | solution.py:166
  32.4 0.5 collective-permute-start.10
  32.9 1.9 %collective-permute-done.5.refs_6_.rest_6_ = bf16[8,8192]{1,0:T(8,128)(2,1)S(1)} collective-permute-done((bf16[8,8192]{1,0:T(8,128)(2,1)S(1)}, bf16[8,8192]{1,0:T(8,128)(2,1)S(1)}, u32[]{:S(2)}, u32[]{:S(2)}) %collective-permute-start.5) | collective-permute-done | bytes 131104 | tf_op jit(solution)/shard_map/ppermute | solution.py:166
  34.8 1.3 %collective-permute-done.6.refs_7_.rest_7_ = bf16[8,8192]{1,0:T(8,128)(2,1)S(1)} collective-permute-done((bf16[8,8192]{1,0:T(8,128)(2,1)S(1)}, bf16[8,8192]{1,0:T(8,128)(2,1)S(1)}, u32[]{:S(2)}, u32[]{:S(2)}) %collective-permute-start.6) | collective-permute-done | bytes 131104 | tf_op jit(solution)/shard_map/ppermute | solution.py:166
  36.1 4.7 %delta.1 = bf16[16,16,512]{2,1,0:T(8,128)(2,1)} custom-call(s32[12]{0:T(128)S(1)} %copy-done.4, s32[12]{0:T(128)S(1)} %copy-done.5, s32[12]{0:T(128)S(1)} %copy-done.6, bf16[1,8192,128]{2,1,0:T(8,128)(2,1)} %d_hbm.1, bf16[1,8192,128]{2,1,0:T(8,128)(2,1)} %u_hbm.1, bf16[8,8192]{1,0:T(8,128)(2,1)S(1)} %attend.1.refs_0_.rest_0_, ...), custom_call_target="tpu_custom_call" | custom-call | flops 301989888 | bytes 6553600 | tf_op jit(solution)/shard_map/delta/pallas_call | solution.py:227
  40.9 4.0 %all-to-all-start = ((bf16[16,16,512]{2,1,0:T(8,128)(2,1)}), bf16[16,16,512]{2,1,0:T(8,128)(2,1)S(1)}, u32[]{:S(2)}, u32[]{:S(2)}) async-start(bf16[16,16,512]{2,1,0:T(8,128)(2,1)} %delta.1), calls=%async_computation | async-start | bytes 524288 | tf_op jit(solution)/shard_map/all_to_all | solution.py:353
  44.9 0.0 copy-start
  44.9 3.4 %copy-done = bf16[8192,512]{1,0:T(8,128)(2,1)S(1)} copy-done((bf16[8192,512]{1,0:T(8,128)(2,1)S(1)}, bf16[8192,512]{1,0:T(8,128)(2,1)}, u32[]{:S(2)}) %copy-start) | copy-done | bytes 8388632
  48.3 2.7 %base.1.base_ref = f32[128,512]{1,0:T(8,128)S(1)} custom-call(bf16[8,8192]{1,0:T(8,128)(2,1)S(1)} %attend.1.refs_0_.rest_0_, bf16[8,8192]{1,0:T(8,128)(2,1)S(1)} %collective-permute-done.refs_1_.rest_1_, bf16[8,8192]{1,0:T(8,128)(2,1)S(1)} %collective-permute-done.1.refs_2_.rest_2_, bf16[8,8192]{1,0:T(8,128)(2,1)S(1)} %collective-permute-done.2.refs_3_.rest_3_, ...), custom_call_target="tpu_custom_call" | custom-call | flops 1073741824 | bytes 10747904 | tf_op jit(solution)/shard_map/base/pallas_call | solution.py:267
  51.0 4.0 %all-to-all-done.delta_ref = bf16[16,16,512]{2,1,0:T(8,128)(2,1)S(1)} async-done(((bf16[16,16,512]{2,1,0:T(8,128)(2,1)}), bf16[16,16,512]{2,1,0:T(8,128)(2,1)S(1)}, u32[]{:S(2)}, u32[]{:S(2)}) %all-to-all-start) | async-done | bytes 262176 | tf_op jit(solution)/shard_map/all_to_all | solution.py:353
  55.0 1.6 %join.1 = bf16[2,64,512]{2,1,0:T(8,128)(2,1)} custom-call(s32[12]{0:T(128)S(1)} %copy-done.4, s32[12]{0:T(128)S(1)} %copy-done.5, s32[12]{0:T(128)S(1)} %copy-done.6, f32[128,512]{1,0:T(8,128)S(1)} %base.1.base_ref, bf16[16,16,512]{2,1,0:T(8,128)(2,1)S(1)} %all-to-all-done.delta_ref), custom_call_target="tpu_custom_call" | custom-call | tf_op jit(solution)/shard_map/join/pallas_call | solution.py:323
  (20 shorter events, 0.0 us)
Async XLA Ops:
  0.0 0.9 %copy-start.1 = (bf16[2,4,8192]{2,1,0:T(4,128)(2,1)S(1)}, bf16[2,4,8192]{2,1,0:T(4,128)(2,1)}, u32[]{:S(2)}) copy-start(bf16[2,4,8192]{2,1,0:T(4,128)(2,1)} %q_ref.1) | copy-start | bytes 393220
  0.9 0.7 %copy-start.2 = (bf16[2,4,1024]{2,1,0:T(4,128)(2,1)S(1)}, bf16[2,4,1024]{2,1,0:T(4,128)(2,1)}, u32[]{:S(2)}) copy-start(bf16[2,4,1024]{2,1,0:T(4,128)(2,1)} %nk_ref.1) | copy-start | bytes 49156
  1.6 0.7 %copy-start.3 = (bf16[2,4,1024]{2,1,0:T(4,128)(2,1)S(1)}, bf16[2,4,1024]{2,1,0:T(4,128)(2,1)}, u32[]{:S(2)}) copy-start(bf16[2,4,1024]{2,1,0:T(4,128)(2,1)} %nv_ref.1) | copy-start | bytes 49156
  2.3 0.7 %copy-start.7 = (s32[4]{0:T(128)S(1)}, s32[4]{0:T(128)}, u32[]{:S(2)}) copy-start(s32[4]{0:T(128)} %len_ref.1) | copy-start | bytes 52
  3.0 33.1 %copy-start.4 = (s32[12]{0:T(128)S(1)}, s32[12]{0:T(128)}, u32[]{:S(2)}) copy-start(s32[12]{0:T(128)} %count_ref.3) | copy-start | bytes 148
  3.0 33.1 %copy-start.5 = (s32[12]{0:T(128)S(1)}, s32[12]{0:T(128)}, u32[]{:S(2)}) copy-start(s32[12]{0:T(128)} %rank_ref.3) | copy-start | bytes 148
  3.0 33.1 %copy-start.6 = (s32[12]{0:T(128)S(1)}, s32[12]{0:T(128)}, u32[]{:S(2)}) copy-start(s32[12]{0:T(128)} %owner_ref.3) | copy-start | bytes 148
  9.8 9.0 %collective-permute-start.11 = (bf16[8,8192]{1,0:T(8,128)(2,1)S(1)}, bf16[8,8192]{1,0:T(8,128)(2,1)S(1)}, u32[]{:S(2)}, u32[]{:S(2)}) collective-permute-start(bf16[8,8192]{1,0:T(8,128)(2,1)S(1)} %attend.1.refs_0_.rest_0_), channel_id=1, source_target_pairs={{0,12},{1,13},{2,14},{3,15},{4,0},{5,1},{6,2},{7,3},{8,4},{9,5},{1... | collective-permute-start | bytes 393224 | tf_op jit(solution)/shard_map/ppermute | solution.py:163
  14.9 11.2 %collective-permute-start.7 = (bf16[8,8192]{1,0:T(8,128)(2,1)S(1)}, bf16[8,8192]{1,0:T(8,128)(2,1)S(1)}, u32[]{:S(2)}, u32[]{:S(2)}) collective-permute-start(bf16[8,8192]{1,0:T(8,128)(2,1)S(1)} %attend.1.refs_0_.rest_0_), channel_id=1, source_target_pairs={{0,8},{1,9},{2,10},{3,11},{4,12},{5,13},{6,14},{7,15},{8,0},{9,1},... | collective-permute-start | bytes 393224 | tf_op jit(solution)/shard_map/ppermute | solution.py:163
  14.9 11.2 %collective-permute-start.3 = (bf16[8,8192]{1,0:T(8,128)(2,1)S(1)}, bf16[8,8192]{1,0:T(8,128)(2,1)S(1)}, u32[]{:S(2)}, u32[]{:S(2)}) collective-permute-start(bf16[8,8192]{1,0:T(8,128)(2,1)S(1)} %attend.1.refs_0_.rest_0_), channel_id=1, source_target_pairs={{0,4},{1,5},{2,6},{3,7},{4,8},{5,9},{6,10},{7,11},{8,12},{9,13},{1... | collective-permute-start | bytes 393224 | tf_op jit(solution)/shard_map/ppermute | solution.py:163
  15.9 11.7 %collective-permute-start.1 = (bf16[8,8192]{1,0:T(8,128)(2,1)S(1)}, bf16[8,8192]{1,0:T(8,128)(2,1)S(1)}, u32[]{:S(2)}, u32[]{:S(2)}) collective-permute-start(bf16[8,8192]{1,0:T(8,128)(2,1)S(1)} %attend.1.refs_0_.rest_0_), channel_id=1, source_target_pairs={{0,2},{1,3},{2,0},{3,1},{4,6},{5,7},{6,4},{7,5},{8,10},{9,11},{10,... | collective-permute-start | bytes 393224 | tf_op jit(solution)/shard_map/ppermute | solution.py:166
  17.4 10.4 %collective-permute-start = (bf16[8,8192]{1,0:T(8,128)(2,1)S(1)}, bf16[8,8192]{1,0:T(8,128)(2,1)S(1)}, u32[]{:S(2)}, u32[]{:S(2)}) collective-permute-start(bf16[8,8192]{1,0:T(8,128)(2,1)S(1)} %attend.1.refs_0_.rest_0_), channel_id=1, source_target_pairs={{0,1},{1,0},{2,3},{3,2},{4,5},{5,4},{6,7},{7,6},{8,9},{9,8},{10,11... | collective-permute-start | bytes 393224 | tf_op jit(solution)/shard_map/ppermute | solution.py:166
  18.8 9.6 %collective-permute-start.13 = (bf16[8,8192]{1,0:T(8,128)(2,1)S(1)}, bf16[8,8192]{1,0:T(8,128)(2,1)S(1)}, u32[]{:S(2)}, u32[]{:S(2)}) collective-permute-start(bf16[8,8192]{1,0:T(8,128)(2,1)S(1)} %collective-permute-done.11.refs_12_.rest_12_), channel_id=1, source_target_pairs={{0,2},{1,3},{2,0},{3,1},{4,6},{5,7},{6,4},{7,5},{8,10},{9,11},{10,... | collective-permute-start | bytes 393224 | tf_op jit(solution)/shard_map/ppermute | solution.py:166
  26.1 2.3 %collective-permute-start.12 = (bf16[8,8192]{1,0:T(8,128)(2,1)S(1)}, bf16[8,8192]{1,0:T(8,128)(2,1)S(1)}, u32[]{:S(2)}, u32[]{:S(2)}) collective-permute-start(bf16[8,8192]{1,0:T(8,128)(2,1)S(1)} %collective-permute-done.11.refs_12_.rest_12_), channel_id=1, source_target_pairs={{0,1},{1,0},{2,3},{3,2},{4,5},{5,4},{6,7},{7,6},{8,9},{9,8},{10,11... | collective-permute-start | bytes 393224 | tf_op jit(solution)/shard_map/ppermute | solution.py:166
  26.1 6.3 %collective-permute-start.9 = (bf16[8,8192]{1,0:T(8,128)(2,1)S(1)}, bf16[8,8192]{1,0:T(8,128)(2,1)S(1)}, u32[]{:S(2)}, u32[]{:S(2)}) collective-permute-start(bf16[8,8192]{1,0:T(8,128)(2,1)S(1)} %collective-permute-done.7.refs_8_.rest_8_), channel_id=1, source_target_pairs={{0,2},{1,3},{2,0},{3,1},{4,6},{5,7},{6,4},{7,5},{8,10},{9,11},{10,... | collective-permute-start | bytes 393224 | tf_op jit(solution)/shard_map/ppermute | solution.py:166
  27.6 4.8 %collective-permute-start.8 = (bf16[8,8192]{1,0:T(8,128)(2,1)S(1)}, bf16[8,8192]{1,0:T(8,128)(2,1)S(1)}, u32[]{:S(2)}, u32[]{:S(2)}) collective-permute-start(bf16[8,8192]{1,0:T(8,128)(2,1)S(1)} %collective-permute-done.7.refs_8_.rest_8_), channel_id=1, source_target_pairs={{0,1},{1,0},{2,3},{3,2},{4,5},{5,4},{6,7},{7,6},{8,9},{9,8},{10,11... | collective-permute-start | bytes 393224 | tf_op jit(solution)/shard_map/ppermute | solution.py:166
  27.8 7.0 %collective-permute-start.5 = (bf16[8,8192]{1,0:T(8,128)(2,1)S(1)}, bf16[8,8192]{1,0:T(8,128)(2,1)S(1)}, u32[]{:S(2)}, u32[]{:S(2)}) collective-permute-start(bf16[8,8192]{1,0:T(8,128)(2,1)S(1)} %collective-permute-done.3.refs_4_.rest_4_), channel_id=1, source_target_pairs={{0,2},{1,3},{2,0},{3,1},{4,6},{5,7},{6,4},{7,5},{8,10},{9,11},{10,... | collective-permute-start | bytes 393224 | tf_op jit(solution)/shard_map/ppermute | solution.py:166
  28.3 6.5 %collective-permute-start.4 = (bf16[8,8192]{1,0:T(8,128)(2,1)S(1)}, bf16[8,8192]{1,0:T(8,128)(2,1)S(1)}, u32[]{:S(2)}, u32[]{:S(2)}) collective-permute-start(bf16[8,8192]{1,0:T(8,128)(2,1)S(1)} %collective-permute-done.3.refs_4_.rest_4_), channel_id=1, source_target_pairs={{0,1},{1,0},{2,3},{3,2},{4,5},{5,4},{6,7},{7,6},{8,9},{9,8},{10,11... | collective-permute-start | bytes 393224 | tf_op jit(solution)/shard_map/ppermute | solution.py:166
  28.3 6.5 %collective-permute-start.2 = (bf16[8,8192]{1,0:T(8,128)(2,1)S(1)}, bf16[8,8192]{1,0:T(8,128)(2,1)S(1)}, u32[]{:S(2)}, u32[]{:S(2)}) collective-permute-start(bf16[8,8192]{1,0:T(8,128)(2,1)S(1)} %collective-permute-done.1.refs_2_.rest_2_), channel_id=1, source_target_pairs={{0,1},{1,0},{2,3},{3,2},{4,5},{5,4},{6,7},{7,6},{8,9},{9,8},{10,11... | collective-permute-start | bytes 393224 | tf_op jit(solution)/shard_map/ppermute | solution.py:166
  32.4 2.4 %collective-permute-start.14 = (bf16[8,8192]{1,0:T(8,128)(2,1)S(1)}, bf16[8,8192]{1,0:T(8,128)(2,1)S(1)}, u32[]{:S(2)}, u32[]{:S(2)}) collective-permute-start(bf16[8,8192]{1,0:T(8,128)(2,1)S(1)} %collective-permute-done.13.refs_14_.rest_14_), channel_id=1, source_target_pairs={{0,1},{1,0},{2,3},{3,2},{4,5},{5,4},{6,7},{7,6},{8,9},{9,8},{10,11... | collective-permute-start | bytes 393224 | tf_op jit(solution)/shard_map/ppermute | solution.py:166
  32.4 2.4 %collective-permute-start.10 = (bf16[8,8192]{1,0:T(8,128)(2,1)S(1)}, bf16[8,8192]{1,0:T(8,128)(2,1)S(1)}, u32[]{:S(2)}, u32[]{:S(2)}) collective-permute-start(bf16[8,8192]{1,0:T(8,128)(2,1)S(1)} %collective-permute-done.9.refs_10_.rest_10_), channel_id=1, source_target_pairs={{0,1},{1,0},{2,3},{3,2},{4,5},{5,4},{6,7},{7,6},{8,9},{9,8},{10,11... | collective-permute-start | bytes 393224 | tf_op jit(solution)/shard_map/ppermute | solution.py:166
  34.8 1.3 %collective-permute-start.6 = (bf16[8,8192]{1,0:T(8,128)(2,1)S(1)}, bf16[8,8192]{1,0:T(8,128)(2,1)S(1)}, u32[]{:S(2)}, u32[]{:S(2)}) collective-permute-start(bf16[8,8192]{1,0:T(8,128)(2,1)S(1)} %collective-permute-done.5.refs_6_.rest_6_), channel_id=1, source_target_pairs={{0,1},{1,0},{2,3},{3,2},{4,5},{5,4},{6,7},{7,6},{8,9},{9,8},{10,11... | collective-permute-start | bytes 393224 | tf_op jit(solution)/shard_map/ppermute | solution.py:166
  40.9 14.1 %all-to-all-start = ((bf16[16,16,512]{2,1,0:T(8,128)(2,1)}), bf16[16,16,512]{2,1,0:T(8,128)(2,1)S(1)}, u32[]{:S(2)}, u32[]{:S(2)}) async-start(bf16[16,16,512]{2,1,0:T(8,128)(2,1)} %delta.1), calls=%async_computation | async-start | bytes 524288 | tf_op jit(solution)/shard_map/all_to_all | solution.py:353
  44.9 3.4 %copy-start = (bf16[8192,512]{1,0:T(8,128)(2,1)S(1)}, bf16[8192,512]{1,0:T(8,128)(2,1)}, u32[]{:S(2)}) copy-start(bf16[8192,512]{1,0:T(8,128)(2,1)} %refs_16_.1) | copy-start | bytes 25165828

commit v3 on v2

--- a/solution.py
+++ b/solution.py
@@ -18,6 +18,10 @@
 NT = (((1,), (1,)), ((), ()))
 
 
+def in_hbm(*arrays):
+    return [pltpu.with_memory_space_constraint(a, pltpu.HBM) for a in arrays]
+
+
 def dot(a, b):
     return jnp.dot(a, b, preferred_element_type=F32)
 
@@ -27,7 +31,7 @@
 
 
 def attend_kernel(
-    len_ref, q_ref, nk_ref, nv_ref, k_ref, v_ref, out_ref, qs, nks, nvs, mixed
+    len_ref, q_ref, nk_ref, nv_ref, k_ref, v_ref, out_ref, turned_q, nks, nvs, mixed
 ):
     steps, rows, width = q_ref.shape
     cache = k_ref.shape[1]
@@ -38,14 +42,21 @@
     @pl.when(r == 0)
     def _():
         flat = jnp.concatenate([q_ref[t].astype(F32) for t in range(steps)], axis=0)
+        heads = []
         for k in range(KVH):
-            heads = jnp.stack(
+            group = jnp.stack(
                 [flat[:, (k * GROUP + g) * HD : (k * GROUP + g + 1) * HD] for g in range(GROUP)]
             )
-            turned = jnp.swapaxes(heads, 0, 1)
-            for i in range(rows):
-                qs[i, k] = jnp.concatenate(
-                    [turned[t * rows + i] for t in range(steps)], axis=0
+            heads.append(jnp.swapaxes(group, 0, 1))
+        column = lax.broadcasted_iota(jnp.int32, (HD, KVH * pack), 1)
+        for i in range(rows):
+            mine = jnp.concatenate(
+                [heads[k][t * rows + i] for k in range(KVH) for t in range(steps)], axis=0
+            )
+            mine = jnp.transpose(mine)
+            for k in range(KVH):
+                turned_q[i, k * HD : (k + 1) * HD, :] = jnp.where(
+                    column // pack == k, mine, 0.0
                 ).astype(BF16)
         for src, dst in ((nk_ref, nks), (nv_ref, nvs)):
             fresh = [src[t].astype(F32) for t in range(steps)]
@@ -53,31 +64,29 @@
             dst[...] = jnp.concatenate(fresh, axis=0).astype(BF16)
 
     scale = HD ** (-0.5)
-    older = jnp.concatenate(
-        [dot_nt(qs[r, k], k_ref[0, :, k * HD : (k + 1) * HD]) for k in range(KVH)], axis=0
-    )
-    fresh = jnp.concatenate(
-        [dot_nt(qs[r, k], nks[:, k * HD : (k + 1) * HD]) for k in range(KVH)], axis=0
-    )
-    place = lax.broadcasted_iota(jnp.int32, older.shape, 1)
-    older = jnp.where(place < len_ref[r], older * scale, -jnp.inf)
-    slot = lax.broadcasted_iota(jnp.int32, fresh.shape, 1)
-    step = (lax.broadcasted_iota(jnp.int32, fresh.shape, 0) // GROUP) % steps
+    older = dot(k_ref[0], turned_q[r]) * scale
+    fresh = dot(nks[...], turned_q[r]) * scale
+    place = lax.broadcasted_iota(jnp.int32, older.shape, 0)
+    older = jnp.where(place < len_ref[r], older, -jnp.inf)
+    slot = lax.broadcasted_iota(jnp.int32, fresh.shape, 0)
+    step = (lax.broadcasted_iota(jnp.int32, fresh.shape, 1) // GROUP) % steps
     seen = (slot < both) & (slot % rows == r) & (slot // rows <= step)
-    fresh = jnp.where(seen, fresh * scale, -jnp.inf)
+    fresh = jnp.where(seen, fresh, -jnp.inf)
     top = jnp.maximum(
-        jnp.max(older, axis=1, keepdims=True), jnp.max(fresh, axis=1, keepdims=True)
+        jnp.max(older, axis=0, keepdims=True), jnp.max(fresh, axis=0, keepdims=True)
     )
     e_older = jnp.exp(older - top)
     e_fresh = jnp.exp(fresh - top)
-    total = jnp.sum(e_older, axis=1, keepdims=True) + jnp.sum(e_fresh, axis=1, keepdims=True)
+    total = jnp.sum(e_older, axis=0, keepdims=True) + jnp.sum(e_fresh, axis=0, keepdims=True)
     inverse = 1.0 / total
-    p_older = (e_older * inverse).astype(BF16)
-    p_fresh = (e_fresh * inverse).astype(BF16)
-    for k in range(KVH):
-        own = slice(k * pack, (k + 1) * pack)
-        cols = slice(k * HD, (k + 1) * HD)
-        mixed[r, k] = dot(p_older[own], v_ref[0, :, cols]) + dot(p_fresh[own], nvs[:, cols])
+    p_older = jnp.transpose(e_older * inverse).astype(BF16)
+    p_fresh = jnp.transpose(e_fresh * inverse).astype(BF16)
+    for k in range(0, KVH, 2):
+        own = slice(k * pack, (k + 2) * pack)
+        cols = slice(k * HD, (k + 2) * HD)
+        pair = dot(p_older[own], v_ref[0, :, cols]) + dot(p_fresh[own], nvs[:, cols])
+        mixed[r, k] = pair[:pack, :HD]
+        mixed[r, k + 1] = pair[pack:, HD:]
 
     @pl.when(r == rows - 1)
     def _():
@@ -117,7 +126,7 @@
             ],
             out_specs=pl.BlockSpec((steps * rows, width), lambda r, lens: (0, 0)),
             scratch_shapes=[
-                pltpu.VMEM((rows, KVH, pack, HD), BF16),
+                pltpu.VMEM((rows, kv_width, KVH * pack), BF16),
                 pltpu.VMEM((16, kv_width), BF16),
                 pltpu.VMEM((16, kv_width), BF16),
                 pltpu.VMEM((rows, KVH, pack, HD), F32),
@@ -130,21 +139,11 @@
             transcendentals=rows * steps * HQ * cache,
         ),
         name="attend",
-    )(
-        kv_len,
-        queries,
-        new_keys,
-        new_values,
-        pltpu.with_memory_space_constraint(cache_keys, pltpu.HBM),
-        pltpu.with_memory_space_constraint(cache_values, pltpu.HBM),
-    )
+    )(*in_hbm(kv_len, queries, new_keys, new_values, cache_keys, cache_values))
 
 
 def sender(slot, me, parts):
-    if parts != RING:
-        return slot
-    ahead = (me // 4 + RING // 4 - slot // 4) % (RING // 4)
-    return ahead * 4 + ((me % 4) ^ (slot % 4))
+    return me ^ slot if parts == RING else slot
 
 
 def row_place(index, me, parts, steps, rows):
@@ -156,21 +155,22 @@
     if parts != RING:
         whole = lax.all_gather(block, "tensor", axis=0, tiled=False)
         return [whole[i] for i in range(parts)]
-    devices = range(RING)
-
-    def forward(x, back):
-        pairs = [(i, (i + 4 * back) % RING) for i in devices]
-        return lax.ppermute(x, "tensor", pairs)
-
-    def flip(x, bit):
-        return lax.ppermute(x, "tensor", [(i, i ^ bit) for i in devices])
-
-    column = [block] + [forward(block, back) for back in range(1, RING // 4)]
-    other = [flip(x, 2) for x in column]
-    held = []
-    for x, y in zip(column, other):
-        held += [x, flip(x, 1), y, flip(y, 1)]
-    return held
+
+    def flip(x, bits):
+        return lax.ppermute(x, "tensor", [(i, i ^ bits) for i in range(RING)])
+
+    core, y, z_near, z_far = 1, 2, 4, 8
+    held = {0: block}
+    held[z_far] = flip(block, z_far)
+    held[z_near] = flip(block, z_near)
+    held[y] = flip(block, y)
+    held[y | z_near] = flip(held[z_near], y)
+    held[y | z_far] = flip(held[z_far], y)
+    held[y | z_far | z_near] = flip(held[z_far], y | z_near)
+    held[z_far | z_near] = flip(held[z_far], z_near)
+    for slot in list(held):
+        held[slot | core] = flip(held[slot], core)
+    return [held[slot] for slot in range(RING)]
 
 
 def delta_kernel(steps, rows, parts, count_ref, rank_ref, owner_ref, d_hbm, u_hbm, *rest):
@@ -242,9 +242,7 @@
         ),
         name="delta",
     )(
-        *tables,
-        pltpu.with_memory_space_constraint(store_down, pltpu.HBM),
-        pltpu.with_memory_space_constraint(store_up, pltpu.HBM),
+        *in_hbm(*tables, store_down, store_up),
         *blocks,
     )
 
@@ -278,7 +276,7 @@
             transcendentals=0,
         ),
         name="base",
-    )(*blocks, out_weight)
+    )(*blocks, *in_hbm(out_weight))
 
 
 def join_kernel(rows, count_ref, rank_ref, owner_ref, base_ref, delta_ref, out_ref):
@@ -327,7 +325,7 @@
         out_specs=vmem,
         compiler_params=pltpu.CompilerParams(vmem_limit_bytes=24 * 2**20),
         name="join",
-    )(*tables, base, delta)
+    )(*in_hbm(*tables), base, delta)
 
 
 def per_device(

time: 57 us -> 54.6 us (0.958)
  local copies, waits for them, and re-layouts: 6.38 us -> 0 us
  Pallas kernels: 15.7 us -> 21.1 us
  waiting for transfers between devices: 17.9 us -> 12.8 us
  starting transfers between devices: 16.5 us -> 20.1 us
    unnamed x16 -> x0, local copies, waits for them, and re-layouts: 6.38 us -> none
    ppermute x15, waiting for transfers between devices: 13.9 us -> 9.61 us  [flip(): return lax.ppermute(x, 'tensor', [(i, i ^ bits) for i in range(RING)])]
    pallas_call x1, Pallas kernels: 2.68 us -> 6.81 us  [base_part(): pl.pallas_call(base_kernel, out_shape=jax.ShapeDtypeStruct((total, cols),...]
    all_to_all x1, starting transfers between devices: 4.04 us -> 6.78 us  [per_device(): lax.all_to_all(send, 'tensor', split_axis=0, concat_axis=0, tiled=True)]
    pallas_call x1, Pallas kernels: 6.74 us -> 7.81 us  [attend(): pl.pallas_call(attend_kernel, out_shape=jax.ShapeDtypeStruct((steps * row...]
    ppermute x15, starting transfers between devices: 12.4 us -> 13.4 us  [flip(): return lax.ppermute(x, 'tensor', [(i, i ^ bits) for i in range(RING)])]
    all_to_all x1, waiting for transfers between devices: 3.97 us -> 3.23 us  [per_device(): lax.all_to_all(send, 'tensor', split_axis=0, concat_axis=0, tiled=True)]
  transfers between devices with their start and end apart: 16 -> 16, of which waited for: 6 -> 8; matrix products, arithmetic and copies ran while one was open for 0% -> 0% of each run, Pallas kernels for 5% -> 13%
where the time goes in v3:
time: 54.6 us; the launch traced here: 54.2 us
  Pallas kernels  21.1 us (39%)
  starting transfers between devices  20.1 us (37%)
  waiting for transfers between devices  12.8 us (23%)
    ppermute x15, starting transfers between devices, flip(): return lax.ppermute(x, 'tensor', [(i, i ^ bits) for i in range(RING)])  13.4 us
    ppermute x15, waiting for transfers between devices, flip(): return lax.ppermute(x, 'tensor', [(i, i ^ bits) for i in range(RING)])  9.61 us
    pallas_call x1, Pallas kernels, attend(): pl.pallas_call(attend_kernel, out_shape=jax.ShapeDtypeStruct((steps * row...  7.81 us
    pallas_call x1, Pallas kernels, base_part(): pl.pallas_call(base_kernel, out_shape=jax.ShapeDtypeStruct((total, cols),...  6.81 us
    all_to_all x1, starting transfers between devices, per_device(): lax.all_to_all(send, 'tensor', split_axis=0, concat_axis=0, tiled=True)  6.78 us
    pallas_call x1, Pallas kernels, delta_parts(): pl.pallas_call(functools.partial(delta_kernel, steps, rows, parts), out_s...  4.81 us
    all_to_all x1, waiting for transfers between devices, per_device(): lax.all_to_all(send, 'tensor', split_axis=0, concat_axis=0, tiled=True)  3.23 us
    pallas_call x1, Pallas kernels, join(): pl.pallas_call(functools.partial(join_kernel, rows), out_shape=jax.ShapeD...  1.71 us
  transfers between devices with their start and end apart: 16, of which 8 were waited for; matrix products, arithmetic and copies ran while one was open for 0% of the time, Pallas kernels for 13%

profile of v3, /device:TPU:0, one launch (start us, length us, event | category | flops | bytes accessed | tf_op | source)
XLA Modules:
  0.0 54.2 jit_solution(4663240362858889362)
XLA Ops:
  0.0 7.8 %attend.1.refs_0_.rest_0_ = bf16[8,8192]{1,0:T(8,128)(2,1)S(1)} custom-call(s32[4]{0:T(128)} %len_ref.1, bf16[2,4,8192]{2,1,0:T(4,128)(2,1)} %q_ref.1, bf16[2,4,1024]{2,1,0:T(4,128)(2,1)} %nk_ref.1, bf16[2,4,1024]{2,1,0:T(4,128)(2,1)} %nv_ref.1, bf16[4,512,1024]{2,1,0:T(8,128)(2,1)} %k_ref.1, bf16[4,512,1024]{2,1,0:T(8,128)(2,1)} %v_ref.1), custom_call_target="tpu_custom_call" | custom-call | flops 134217728 | bytes 8388608 | tf_op jit(solution)/shard_map/attend/pallas_call | solution.py:114
  7.8 4.1 %collective-permute-start.7 = (bf16[8,8192]{1,0:T(8,128)(2,1)S(1)}, bf16[8,8192]{1,0:T(8,128)(2,1)S(1)}, u32[]{:S(2)}, u32[]{:S(2)}) collective-permute-start(bf16[8,8192]{1,0:T(8,128)(2,1)S(1)} %attend.1.refs_0_.rest_0_), channel_id=1, source_target_pairs={{0,8},{1,9},{2,10},{3,11},{4,12},{5,13},{6,14},{7,15},{8,0},{9,1},... | collective-permute-start | bytes 393224 | tf_op jit(solution)/shard_map/ppermute | solution.py:160
  11.9 1.6 %collective-permute-start.3 = (bf16[8,8192]{1,0:T(8,128)(2,1)S(1)}, bf16[8,8192]{1,0:T(8,128)(2,1)S(1)}, u32[]{:S(2)}, u32[]{:S(2)}) collective-permute-start(bf16[8,8192]{1,0:T(8,128)(2,1)S(1)} %attend.1.refs_0_.rest_0_), channel_id=1, source_target_pairs={{0,4},{1,5},{2,6},{3,7},{4,0},{5,1},{6,2},{7,3},{8,12},{9,13},{10,... | collective-permute-start | bytes 393224 | tf_op jit(solution)/shard_map/ppermute | solution.py:160
  13.5 1.5 %collective-permute-start.1 = (bf16[8,8192]{1,0:T(8,128)(2,1)S(1)}, bf16[8,8192]{1,0:T(8,128)(2,1)S(1)}, u32[]{:S(2)}, u32[]{:S(2)}) collective-permute-start(bf16[8,8192]{1,0:T(8,128)(2,1)S(1)} %attend.1.refs_0_.rest_0_), channel_id=1, source_target_pairs={{0,2},{1,3},{2,0},{3,1},{4,6},{5,7},{6,4},{7,5},{8,10},{9,11},{10,... | collective-permute-start | bytes 393224 | tf_op jit(solution)/shard_map/ppermute | solution.py:160
  15.0 0.0 collective-permute-start
  15.0 3.3 %collective-permute-done.7.refs_8_.rest_8_ = bf16[8,8192]{1,0:T(8,128)(2,1)S(1)} collective-permute-done((bf16[8,8192]{1,0:T(8,128)(2,1)S(1)}, bf16[8,8192]{1,0:T(8,128)(2,1)S(1)}, u32[]{:S(2)}, u32[]{:S(2)}) %collective-permute-start.7) | collective-permute-done | bytes 131104 | tf_op jit(solution)/shard_map/ppermute | solution.py:160
  18.3 1.6 %collective-permute-start.13 = (bf16[8,8192]{1,0:T(8,128)(2,1)S(1)}, bf16[8,8192]{1,0:T(8,128)(2,1)S(1)}, u32[]{:S(2)}, u32[]{:S(2)}) collective-permute-start(bf16[8,8192]{1,0:T(8,128)(2,1)S(1)} %collective-permute-done.7.refs_8_.rest_8_), channel_id=1, source_target_pairs={{0,6},{1,7},{2,4},{3,5},{4,2},{5,3},{6,0},{7,1},{8,14},{9,15},{10,... | collective-permute-start | bytes 393224 | tf_op jit(solution)/shard_map/ppermute | solution.py:160
  19.9 1.5 %collective-permute-start.11 = (bf16[8,8192]{1,0:T(8,128)(2,1)S(1)}, bf16[8,8192]{1,0:T(8,128)(2,1)S(1)}, u32[]{:S(2)}, u32[]{:S(2)}) collective-permute-start(bf16[8,8192]{1,0:T(8,128)(2,1)S(1)} %collective-permute-done.7.refs_8_.rest_8_), channel_id=1, source_target_pairs={{0,4},{1,5},{2,6},{3,7},{4,0},{5,1},{6,2},{7,3},{8,12},{9,13},{10,... | collective-permute-start | bytes 393224 | tf_op jit(solution)/shard_map/ppermute | solution.py:160
  21.4 0.0 collective-permute-done.3.refs_4_.rest_4_
  21.4 0.5 collective-permute-start.9
  21.8 0.0 collective-permute-done.1.refs_2_.rest_2_
  21.8 0.0 collective-permute-start.8
  21.8 0.0 collective-permute-done.refs_1_.rest_1_
  21.8 1.6 %collective-permute-start.5 = (bf16[8,8192]{1,0:T(8,128)(2,1)S(1)}, bf16[8,8192]{1,0:T(8,128)(2,1)S(1)}, u32[]{:S(2)}, u32[]{:S(2)}) collective-permute-start(bf16[8,8192]{1,0:T(8,128)(2,1)S(1)} %collective-permute-done.3.refs_4_.rest_4_), channel_id=1, source_target_pairs={{0,2},{1,3},{2,0},{3,1},{4,6},{5,7},{6,4},{7,5},{8,10},{9,11},{10,... | collective-permute-start | bytes 393224 | tf_op jit(solution)/shard_map/ppermute | solution.py:160
  23.5 1.6 %collective-permute-done.13.refs_14_.rest_14_ = bf16[8,8192]{1,0:T(8,128)(2,1)S(1)} collective-permute-done((bf16[8,8192]{1,0:T(8,128)(2,1)S(1)}, bf16[8,8192]{1,0:T(8,128)(2,1)S(1)}, u32[]{:S(2)}, u32[]{:S(2)}) %collective-permute-start.13) | collective-permute-done | bytes 131104 | tf_op jit(solution)/shard_map/ppermute | solution.py:160
  25.1 0.0 collective-permute-start.4
  25.1 1.4 %collective-permute-done.11.refs_12_.rest_12_ = bf16[8,8192]{1,0:T(8,128)(2,1)S(1)} collective-permute-done((bf16[8,8192]{1,0:T(8,128)(2,1)S(1)}, bf16[8,8192]{1,0:T(8,128)(2,1)S(1)}, u32[]{:S(2)}, u32[]{:S(2)}) %collective-permute-start.11) | collective-permute-done | bytes 131104 | tf_op jit(solution)/shard_map/ppermute | solution.py:160
  26.5 0.0 collective-permute-start.2
  26.5 1.4 %collective-permute-done.9.refs_10_.rest_10_ = bf16[8,8192]{1,0:T(8,128)(2,1)S(1)} collective-permute-done((bf16[8,8192]{1,0:T(8,128)(2,1)S(1)}, bf16[8,8192]{1,0:T(8,128)(2,1)S(1)}, u32[]{:S(2)}, u32[]{:S(2)}) %collective-permute-start.9) | collective-permute-done | bytes 131104 | tf_op jit(solution)/shard_map/ppermute | solution.py:160
  27.9 0.0 collective-permute-start.14
  27.9 0.0 collective-permute-done.8.refs_9_.rest_9_
  27.9 0.5 collective-permute-start.12
  28.4 0.9 %collective-permute-done.5.refs_6_.rest_6_ = bf16[8,8192]{1,0:T(8,128)(2,1)S(1)} collective-permute-done((bf16[8,8192]{1,0:T(8,128)(2,1)S(1)}, bf16[8,8192]{1,0:T(8,128)(2,1)S(1)}, u32[]{:S(2)}, u32[]{:S(2)}) %collective-permute-start.5) | collective-permute-done | bytes 131104 | tf_op jit(solution)/shard_map/ppermute | solution.py:160
  29.3 0.0 collective-permute-start.10
  29.3 0.5 collective-permute-start.6
  29.8 0.8 %collective-permute-done.10.refs_11_.rest_11_ = bf16[8,8192]{1,0:T(8,128)(2,1)S(1)} collective-permute-done((bf16[8,8192]{1,0:T(8,128)(2,1)S(1)}, bf16[8,8192]{1,0:T(8,128)(2,1)S(1)}, u32[]{:S(2)}, u32[]{:S(2)}) %collective-permute-start.10) | collective-permute-done | bytes 131104 | tf_op jit(solution)/shard_map/ppermute | solution.py:160
  30.6 0.2 collective-permute-done.6.refs_7_.rest_7_
  30.8 4.8 %delta.1 = bf16[16,16,512]{2,1,0:T(8,128)(2,1)} custom-call(s32[12]{0:T(128)} %count_ref.3, s32[12]{0:T(128)} %rank_ref.3, s32[12]{0:T(128)} %owner_ref.3, bf16[1,8192,128]{2,1,0:T(8,128)(2,1)} %d_hbm.1, bf16[1,8192,128]{2,1,0:T(8,128)(2,1)} %u_hbm.1, bf16[8,8192]{1,0:T(8,128)(2,1)S(1)} %attend.1.refs_0_.rest_0_, ...), custom_call_target="tpu_custom_call" | custom-call | flops 301989888 | bytes 6553600 | tf_op jit(solution)/shard_map/delta/pallas_call | solution.py:227
  35.6 6.8 %all-to-all-start = ((bf16[16,16,512]{2,1,0:T(8,128)(2,1)}), bf16[16,16,512]{2,1,0:T(8,128)(2,1)S(1)}, u32[]{:S(2)}, u32[]{:S(2)}) async-start(bf16[16,16,512]{2,1,0:T(8,128)(2,1)} %delta.1), calls=%async_computation | async-start | bytes 524288 | tf_op jit(solution)/shard_map/all_to_all | solution.py:351
  42.4 6.8 %base.1.base_ref = f32[128,512]{1,0:T(8,128)S(1)} custom-call(bf16[8,8192]{1,0:T(8,128)(2,1)S(1)} %attend.1.refs_0_.rest_0_, bf16[8,8192]{1,0:T(8,128)(2,1)S(1)} %collective-permute-done.refs_1_.rest_1_, bf16[8,8192]{1,0:T(8,128)(2,1)S(1)} %collective-permute-done.1.refs_2_.rest_2_, bf16[8,8192]{1,0:T(8,128)(2,1)S(1)} %collective-permute-done.2.refs_3_.rest_3_, ...), custom_call_target="tpu_custom_call" | custom-call | flops 1073741824 | bytes 10747904 | tf_op jit(solution)/shard_map/base/pallas_call | solution.py:265
  49.2 3.2 %all-to-all-done.delta_ref = bf16[16,16,512]{2,1,0:T(8,128)(2,1)S(1)} async-done(((bf16[16,16,512]{2,1,0:T(8,128)(2,1)}), bf16[16,16,512]{2,1,0:T(8,128)(2,1)S(1)}, u32[]{:S(2)}, u32[]{:S(2)}) %all-to-all-start) | async-done | bytes 262176 | tf_op jit(solution)/shard_map/all_to_all | solution.py:351
  52.5 1.7 %join.1 = bf16[2,64,512]{2,1,0:T(8,128)(2,1)} custom-call(s32[12]{0:T(128)} %count_ref.3, s32[12]{0:T(128)} %rank_ref.3, s32[12]{0:T(128)} %owner_ref.3, f32[128,512]{1,0:T(8,128)S(1)} %base.1.base_ref, bf16[16,16,512]{2,1,0:T(8,128)(2,1)S(1)} %all-to-all-done.delta_ref), custom_call_target="tpu_custom_call" | custom-call | tf_op jit(solution)/shard_map/join/pallas_call | solution.py:321
  (4 shorter events, 0.0 us)
Async XLA Ops:
  7.8 10.5 %collective-permute-start.7 = (bf16[8,8192]{1,0:T(8,128)(2,1)S(1)}, bf16[8,8192]{1,0:T(8,128)(2,1)S(1)}, u32[]{:S(2)}, u32[]{:S(2)}) collective-permute-start(bf16[8,8192]{1,0:T(8,128)(2,1)S(1)} %attend.1.refs_0_.rest_0_), channel_id=1, source_target_pairs={{0,8},{1,9},{2,10},{3,11},{4,12},{5,13},{6,14},{7,15},{8,0},{9,1},... | collective-permute-start | bytes 393224 | tf_op jit(solution)/shard_map/ppermute | solution.py:160
  11.9 9.4 %collective-permute-start.3 = (bf16[8,8192]{1,0:T(8,128)(2,1)S(1)}, bf16[8,8192]{1,0:T(8,128)(2,1)S(1)}, u32[]{:S(2)}, u32[]{:S(2)}) collective-permute-start(bf16[8,8192]{1,0:T(8,128)(2,1)S(1)} %attend.1.refs_0_.rest_0_), channel_id=1, source_target_pairs={{0,4},{1,5},{2,6},{3,7},{4,0},{5,1},{6,2},{7,3},{8,12},{9,13},{10,... | collective-permute-start | bytes 393224 | tf_op jit(solution)/shard_map/ppermute | solution.py:160
  13.5 8.3 %collective-permute-start.1 = (bf16[8,8192]{1,0:T(8,128)(2,1)S(1)}, bf16[8,8192]{1,0:T(8,128)(2,1)S(1)}, u32[]{:S(2)}, u32[]{:S(2)}) collective-permute-start(bf16[8,8192]{1,0:T(8,128)(2,1)S(1)} %attend.1.refs_0_.rest_0_), channel_id=1, source_target_pairs={{0,2},{1,3},{2,0},{3,1},{4,6},{5,7},{6,4},{7,5},{8,10},{9,11},{10,... | collective-permute-start | bytes 393224 | tf_op jit(solution)/shard_map/ppermute | solution.py:160
  15.0 6.8 %collective-permute-start = (bf16[8,8192]{1,0:T(8,128)(2,1)S(1)}, bf16[8,8192]{1,0:T(8,128)(2,1)S(1)}, u32[]{:S(2)}, u32[]{:S(2)}) collective-permute-start(bf16[8,8192]{1,0:T(8,128)(2,1)S(1)} %attend.1.refs_0_.rest_0_), channel_id=1, source_target_pairs={{0,1},{1,0},{2,3},{3,2},{4,5},{5,4},{6,7},{7,6},{8,9},{9,8},{10,11... | collective-permute-start | bytes 393224 | tf_op jit(solution)/shard_map/ppermute | solution.py:160
  18.3 6.7 %collective-permute-start.13 = (bf16[8,8192]{1,0:T(8,128)(2,1)S(1)}, bf16[8,8192]{1,0:T(8,128)(2,1)S(1)}, u32[]{:S(2)}, u32[]{:S(2)}) collective-permute-start(bf16[8,8192]{1,0:T(8,128)(2,1)S(1)} %collective-permute-done.7.refs_8_.rest_8_), channel_id=1, source_target_pairs={{0,6},{1,7},{2,4},{3,5},{4,2},{5,3},{6,0},{7,1},{8,14},{9,15},{10,... | collective-permute-start | bytes 393224 | tf_op jit(solution)/shard_map/ppermute | solution.py:160
  19.9 6.5 %collective-permute-start.11 = (bf16[8,8192]{1,0:T(8,128)(2,1)S(1)}, bf16[8,8192]{1,0:T(8,128)(2,1)S(1)}, u32[]{:S(2)}, u32[]{:S(2)}) collective-permute-start(bf16[8,8192]{1,0:T(8,128)(2,1)S(1)} %collective-permute-done.7.refs_8_.rest_8_), channel_id=1, source_target_pairs={{0,4},{1,5},{2,6},{3,7},{4,0},{5,1},{6,2},{7,3},{8,12},{9,13},{10,... | collective-permute-start | bytes 393224 | tf_op jit(solution)/shard_map/ppermute | solution.py:160
  21.4 6.5 %collective-permute-start.9 = (bf16[8,8192]{1,0:T(8,128)(2,1)S(1)}, bf16[8,8192]{1,0:T(8,128)(2,1)S(1)}, u32[]{:S(2)}, u32[]{:S(2)}) collective-permute-start(bf16[8,8192]{1,0:T(8,128)(2,1)S(1)} %collective-permute-done.7.refs_8_.rest_8_), channel_id=1, source_target_pairs={{0,2},{1,3},{2,0},{3,1},{4,6},{5,7},{6,4},{7,5},{8,10},{9,11},{10,... | collective-permute-start | bytes 393224 | tf_op jit(solution)/shard_map/ppermute | solution.py:160
  21.8 6.0 %collective-permute-start.8 = (bf16[8,8192]{1,0:T(8,128)(2,1)S(1)}, bf16[8,8192]{1,0:T(8,128)(2,1)S(1)}, u32[]{:S(2)}, u32[]{:S(2)}) collective-permute-start(bf16[8,8192]{1,0:T(8,128)(2,1)S(1)} %collective-permute-done.7.refs_8_.rest_8_), channel_id=1, source_target_pairs={{0,1},{1,0},{2,3},{3,2},{4,5},{5,4},{6,7},{7,6},{8,9},{9,8},{10,11... | collective-permute-start | bytes 393224 | tf_op jit(solution)/shard_map/ppermute | solution.py:160
  21.8 7.4 %collective-permute-start.5 = (bf16[8,8192]{1,0:T(8,128)(2,1)S(1)}, bf16[8,8192]{1,0:T(8,128)(2,1)S(1)}, u32[]{:S(2)}, u32[]{:S(2)}) collective-permute-start(bf16[8,8192]{1,0:T(8,128)(2,1)S(1)} %collective-permute-done.3.refs_4_.rest_4_), channel_id=1, source_target_pairs={{0,2},{1,3},{2,0},{3,1},{4,6},{5,7},{6,4},{7,5},{8,10},{9,11},{10,... | collective-permute-start | bytes 393224 | tf_op jit(solution)/shard_map/ppermute | solution.py:160
  25.1 4.2 %collective-permute-start.4 = (bf16[8,8192]{1,0:T(8,128)(2,1)S(1)}, bf16[8,8192]{1,0:T(8,128)(2,1)S(1)}, u32[]{:S(2)}, u32[]{:S(2)}) collective-permute-start(bf16[8,8192]{1,0:T(8,128)(2,1)S(1)} %collective-permute-done.3.refs_4_.rest_4_), channel_id=1, source_target_pairs={{0,1},{1,0},{2,3},{3,2},{4,5},{5,4},{6,7},{7,6},{8,9},{9,8},{10,11... | collective-permute-start | bytes 393224 | tf_op jit(solution)/shard_map/ppermute | solution.py:160
  26.5 3.3 %collective-permute-start.2 = (bf16[8,8192]{1,0:T(8,128)(2,1)S(1)}, bf16[8,8192]{1,0:T(8,128)(2,1)S(1)}, u32[]{:S(2)}, u32[]{:S(2)}) collective-permute-start(bf16[8,8192]{1,0:T(8,128)(2,1)S(1)} %collective-permute-done.1.refs_2_.rest_2_), channel_id=1, source_target_pairs={{0,1},{1,0},{2,3},{3,2},{4,5},{5,4},{6,7},{7,6},{8,9},{9,8},{10,11... | collective-permute-start | bytes 393224 | tf_op jit(solution)/shard_map/ppermute | solution.py:160
  27.9 1.9 %collective-permute-start.14 = (bf16[8,8192]{1,0:T(8,128)(2,1)S(1)}, bf16[8,8192]{1,0:T(8,128)(2,1)S(1)}, u32[]{:S(2)}, u32[]{:S(2)}) collective-permute-start(bf16[8,8192]{1,0:T(8,128)(2,1)S(1)} %collective-permute-done.13.refs_14_.rest_14_), channel_id=1, source_target_pairs={{0,1},{1,0},{2,3},{3,2},{4,5},{5,4},{6,7},{7,6},{8,9},{9,8},{10,11... | collective-permute-start | bytes 393224 | tf_op jit(solution)/shard_map/ppermute | solution.py:160
  27.9 1.9 %collective-permute-start.12 = (bf16[8,8192]{1,0:T(8,128)(2,1)S(1)}, bf16[8,8192]{1,0:T(8,128)(2,1)S(1)}, u32[]{:S(2)}, u32[]{:S(2)}) collective-permute-start(bf16[8,8192]{1,0:T(8,128)(2,1)S(1)} %collective-permute-done.11.refs_12_.rest_12_), channel_id=1, source_target_pairs={{0,1},{1,0},{2,3},{3,2},{4,5},{5,4},{6,7},{7,6},{8,9},{9,8},{10,11... | collective-permute-start | bytes 393224 | tf_op jit(solution)/shard_map/ppermute | solution.py:160
  29.3 1.3 %collective-permute-start.10 = (bf16[8,8192]{1,0:T(8,128)(2,1)S(1)}, bf16[8,8192]{1,0:T(8,128)(2,1)S(1)}, u32[]{:S(2)}, u32[]{:S(2)}) collective-permute-start(bf16[8,8192]{1,0:T(8,128)(2,1)S(1)} %collective-permute-done.9.refs_10_.rest_10_), channel_id=1, source_target_pairs={{0,1},{1,0},{2,3},{3,2},{4,5},{5,4},{6,7},{7,6},{8,9},{9,8},{10,11... | collective-permute-start | bytes 393224 | tf_op jit(solution)/shard_map/ppermute | solution.py:160
  29.3 1.5 %collective-permute-start.6 = (bf16[8,8192]{1,0:T(8,128)(2,1)S(1)}, bf16[8,8192]{1,0:T(8,128)(2,1)S(1)}, u32[]{:S(2)}, u32[]{:S(2)}) collective-permute-start(bf16[8,8192]{1,0:T(8,128)(2,1)S(1)} %collective-permute-done.5.refs_6_.rest_6_), channel_id=1, source_target_pairs={{0,1},{1,0},{2,3},{3,2},{4,5},{5,4},{6,7},{7,6},{8,9},{9,8},{10,11... | collective-permute-start | bytes 393224 | tf_op jit(solution)/shard_map/ppermute | solution.py:160
  35.6 16.8 %all-to-all-start = ((bf16[16,16,512]{2,1,0:T(8,128)(2,1)}), bf16[16,16,512]{2,1,0:T(8,128)(2,1)S(1)}, u32[]{:S(2)}, u32[]{:S(2)}) async-start(bf16[16,16,512]{2,1,0:T(8,128)(2,1)} %delta.1), calls=%async_computation | async-start | bytes 524288 | tf_op jit(solution)/shard_map/all_to_all | solution.py:351

commit v4 on v1

v4 whole, which is shorter than its diff:
```python
import functools

import jax
import jax.numpy as jnp
from jax import lax
from jax.experimental import pallas as pl
from jax.experimental.pallas import tpu as pltpu
from jax.sharding import PartitionSpec as P

HQ = 64
KVH = 8
HD = 128
GROUP = HQ // KVH
MOST = 8
RING = 8
F32 = jnp.float32
BF16 = jnp.bfloat16
NT = (((1,), (1,)), ((), ()))


def in_hbm(*arrays):
    return [pltpu.with_memory_space_constraint(a, pltpu.HBM) for a in arrays]


def dot(a, b):
    return jnp.dot(a, b, preferred_element_type=F32)


def dot_nt(a, b):
    return lax.dot_general(a, b, NT, preferred_element_type=F32)


def attend_kernel(
    len_ref, q_hbm, nk_hbm, nv_hbm, k_hbm, v_hbm, d_hbm, u_hbm, out_ref, store_ref,
    q_ref, nk_ref, nv_ref, k_ref, v_ref, turned_q, nks, nvs, mixed, small_sems, sems, store_sems,
):
    steps, rows, width = q_ref.shape
    cache = k_ref.shape[1]
    both = steps * rows
    pack = steps * GROUP
    cuts = sems.shape[2]
    small = [
        pltpu.make_async_copy(src, dst, small_sems.at[i])
        for i, (src, dst) in enumerate(((q_hbm, q_ref), (nk_hbm, nk_ref), (nv_hbm, nv_ref)))
    ]
    large = []
    for r in range(rows):
        for j, (src, dst) in enumerate(((k_hbm, k_ref), (v_hbm, v_ref))):
            pieces = [pl.ds(i * (cache // cuts), cache // cuts) for i in range(cuts)]
            large.append(
                [
                    pltpu.make_async_copy(src.at[r, at], dst.at[r, at], sems.at[r, j, i])
                    for i, at in enumerate(pieces)
                ]
            )
    for copy in small:
        copy.start()
    for copies in large:
        for copy in copies:
            copy.start()
    deep = d_hbm.shape[1]
    stores = [
        pltpu.make_async_copy(src.at[0], store_ref.at[pl.ds(j * deep, deep)], store_sems.at[j])
        for j, src in enumerate((d_hbm, u_hbm))
    ]
    for copy in stores:
        copy.start()
    for copy in small:
        copy.wait()

    flat = jnp.concatenate([q_ref[t].astype(F32) for t in range(steps)], axis=0)
    heads = []
    for k in range(KVH):
        group = jnp.stack(
            [flat[:, (k * GROUP + g) * HD : (k * GROUP + g + 1) * HD] for g in range(GROUP)]
        )
        heads.append(jnp.swapaxes(group, 0, 1))
    column = lax.broadcasted_iota(jnp.int32, (HD, KVH * pack), 1)
    for r in range(rows):
        mine = jnp.concatenate(
            [heads[k][t * rows + r] for k in range(KVH) for t in range(steps)], axis=0
        )
        mine = jnp.transpose(mine)
        for k in range(KVH):
            turned_q[r, k * HD : (k + 1) * HD, :] = jnp.where(
                column // pack == k, mine, 0.0
            ).astype(BF16)
    for src, dst in ((nk_ref, nks), (nv_ref, nvs)):
        fresh = [src[t].astype(F32) for t in range(steps)]
        fresh.append(jnp.zeros((16 - both, src.shape[2]), F32))
        dst[...] = jnp.concatenate(fresh, axis=0).astype(BF16)

    scale = HD ** (-0.5)
    for r in range(rows):
        fresh = dot(nks[...], turned_q[r]) * scale
        slot = lax.broadcasted_iota(jnp.int32, fresh.shape, 0)
        step = (lax.broadcasted_iota(jnp.int32, fresh.shape, 1) // GROUP) % steps
        seen = (slot < both) & (slot % rows == r) & (slot // rows <= step)
        fresh = jnp.where(seen, fresh, -jnp.inf)
        for copy in large[2 * r]:
            copy.wait()
        older = dot(k_ref[r], turned_q[r]) * scale
        place = lax.broadcasted_iota(jnp.int32, older.shape, 0)
        older = jnp.where(place < len_ref[r], older, -jnp.inf)
        top = jnp.maximum(
            jnp.max(older, axis=0, keepdims=True), jnp.max(fresh, axis=0, keepdims=True)
        )
        e_older = jnp.exp(older - top)
        e_fresh = jnp.exp(fresh - top)
        total = jnp.sum(e_older, axis=0, keepdims=True) + jnp.sum(e_fresh, axis=0, keepdims=True)
        inverse = 1.0 / total
        p_older = jnp.transpose(e_older * inverse).astype(BF16)
        p_fresh = jnp.transpose(e_fresh * inverse).astype(BF16)
        for copy in large[2 * r + 1]:
            copy.wait()
        for k in range(0, KVH, 2):
            own = slice(k * pack, (k + 2) * pack)
            cols = slice(k * HD, (k + 2) * HD)
            pair = dot(p_older[own], v_ref[r, :, cols]) + dot(p_fresh[own], nvs[:, cols])
            mixed[r, k] = pair[:pack, :HD]
            mixed[r, k + 1] = pair[pack:, HD:]

    for k in range(KVH):
        turned = jnp.stack(
            [
                mixed[r, k, t * GROUP : (t + 1) * GROUP, :]
                for t in range(steps)
                for r in range(rows)
            ]
        )
        heads = jnp.swapaxes(turned, 0, 1)
        for g in range(GROUP):
            at = (k * GROUP + g) * HD
            out_ref[:, at : at + HD] = heads[g].astype(BF16)
    for copy in stores:
        copy.wait()


def attend(
    queries, new_keys, new_values, cache_keys, cache_values, kv_len, store_down, store_up
):
    steps, rows, width = queries.shape
    cache, kv_width = cache_keys.shape[1:]
    pack = steps * GROUP
    return pl.pallas_call(
        attend_kernel,
        out_shape=(
            jax.ShapeDtypeStruct((steps * rows, width), BF16),
            jax.ShapeDtypeStruct((2 * store_down.shape[1], store_down.shape[2]), BF16),
        ),
        in_specs=[pl.BlockSpec(memory_space=pltpu.SMEM)]
        + [pl.BlockSpec(memory_space=pl.ANY)] * 7,
        out_specs=(pl.BlockSpec(memory_space=pltpu.VMEM),) * 2,
        scratch_shapes=[
            pltpu.VMEM(queries.shape, BF16),
            pltpu.VMEM(new_keys.shape, BF16),
            pltpu.VMEM(new_values.shape, BF16),
            pltpu.VMEM(cache_keys.shape, BF16),
            pltpu.VMEM(cache_values.shape, BF16),
            pltpu.VMEM((rows, kv_width, KVH * pack), BF16),
            pltpu.VMEM((16, kv_width), BF16),
            pltpu.VMEM((16, kv_width), BF16),
            pltpu.VMEM((rows, KVH, pack, HD), F32),
            pltpu.SemaphoreType.DMA((3,)),
            pltpu.SemaphoreType.DMA((rows, 2, 2)),
            pltpu.SemaphoreType.DMA((2,)),
        ],
        compiler_params=pltpu.CompilerParams(vmem_limit_bytes=32 * 2**20),
        cost_estimate=pl.CostEstimate(
            flops=4 * rows * steps * HQ * cache * HD,
            bytes_accessed=4 * rows * cache * kv_width,
            transcendentals=rows * steps * HQ * cache,
        ),
        name="attend",
    )(
        *in_hbm(
            kv_len,
            queries,
            new_keys,
            new_values,
            cache_keys,
            cache_values,
            store_down,
            store_up,
        )
    )


def sender(slot, chip, chips):
    return chip ^ slot if chips == RING else slot


def swap(x, bits, parts):
    return lax.ppermute(x, "tensor", [(i, i ^ bits) for i in range(parts)])


def gather(block, parts):
    if parts // 2 != RING:
        groups = [list(range(core, parts, 2)) for core in range(2)]
        whole = lax.all_gather(block, "tensor", axis_index_groups=groups)
        return [whole[i] for i in range(parts // 2)]
    y, near, far = 1, 2, 4

    def flip(x, bits):
        return swap(x, 2 * bits, parts)

    held = {0: block}
    held[far] = flip(block, far)
    held[near] = flip(block, near)
    held[y] = flip(block, y)
    held[y | near] = flip(held[near], y)
    held[y | far] = flip(held[far], y)
    held[y | far | near] = flip(held[far], y | near)
    held[far | near] = flip(held[far], near)
    return [held[slot] for slot in range(RING)]


def turn_kernel(store_ref, out_ref):
    width = out_ref.shape[1]
    cuts = 4
    deep = width // cuts
    for i in range(cuts):
        at = slice(width + i * deep, width + (i + 1) * deep)
        out_ref[:, i * deep : (i + 1) * deep] = jnp.transpose(store_ref[at, :])


def turn(store):
    width, rank_w = store.shape[0] // 2, store.shape[1]
    vmem = pl.BlockSpec(memory_space=pltpu.VMEM)
    return pl.pallas_call(
        turn_kernel,
        out_shape=jax.ShapeDtypeStruct((rank_w, width), BF16),
        in_specs=[vmem],
        out_specs=vmem,
        compiler_params=pltpu.CompilerParams(vmem_limit_bytes=16 * 2**20),
        cost_estimate=pl.CostEstimate(
            flops=0, bytes_accessed=4 * width * rank_w, transcendentals=0
        ),
        name="turn",
    )(store)


def stage_weight_kernel(after, w_hbm, w_ref, sems):
    deep = w_hbm.shape[0] // sems.shape[0]
    copies = []
    for i in range(sems.shape[0]):
        at = pl.ds(i * deep, deep)
        copies.append(pltpu.make_async_copy(w_hbm.at[at], w_ref.at[at], sems.at[i]))
        copies[-1].start()
    for copy in copies:
        copy.wait()


def stage_weight(after, out_weight):
    return pl.pallas_call(
        stage_weight_kernel,
        out_shape=jax.ShapeDtypeStruct(out_weight.shape, BF16),
        in_specs=[pl.BlockSpec(memory_space=pl.ANY)] * 2,
        out_specs=pl.BlockSpec(memory_space=pltpu.VMEM),
        scratch_shapes=[pltpu.SemaphoreType.DMA((8,))],
        compiler_params=pltpu.CompilerParams(vmem_limit_bytes=16 * 2**20),
        cost_estimate=pl.CostEstimate(
            flops=4 * 10**10, bytes_accessed=4 * out_weight.size, transcendentals=0
        ),
        name="stage_weight",
    )(after, *in_hbm(out_weight))


def slot_request(first, amount, core, slot, rows):
    ahead = (core * rows + slot + 2 * MOST - first % MOST) % MOST
    return jnp.where(ahead < amount, first + ahead, -1)


def adapter_of(block, count_ref, rank_ref, owner_ref):
    start = jnp.int32(0)
    first = jnp.zeros_like(block)
    amount = jnp.zeros_like(block)
    for a in range(count_ref.shape[0]):
        owned = (owner_ref[a] <= block) & (block < owner_ref[a] + rank_ref[a])
        first = jnp.where(owned, start, first)
        amount = jnp.where(owned, count_ref[a], amount)
        start = start + count_ref[a]
    return first, amount


def iota(shape, dim):
    return lax.broadcasted_iota(jnp.int32, shape, dim)


def one_hot(mask):
    return mask.astype(F32).astype(BF16)


def delta_kernel(steps, rows, count_ref, rank_ref, owner_ref, *rest):
    (d0, d1, u0, u1), blocks, (_, out_ref, rows_ref) = rest[:4], rest[4:-3], rest[-3:]
    me = lax.axis_index("tensor")
    chip, core = me // 2, me % 2
    chips = len(blocks)
    each, width = blocks[0].shape
    total = chips * each
    parts, slots, cols = out_ref.shape
    rank_w = d0.shape[1]
    cuts = 8
    deep = width // cuts
    low = jnp.zeros((total, 2 * rank_w), F32)
    for i in range(cuts):
        at = slice(i * deep, (i + 1) * deep)
        piece = jnp.concatenate([b[:, at] for b in blocks], axis=0)
        rows_ref[:, at] = piece
        low = low + dot(piece, jnp.concatenate([d0[at, :], d1[at, :]], axis=1))
    low = low.astype(BF16)
    shape = (slots, total)
    slot, place = iota(shape, 0), iota(shape, 1)
    device = sender(place // each, chip, chips) * 2 + core
    request = device * rows + place % rows
    step = (place % each) // rows
    half = slots // 2
    first, amount = adapter_of(
        chip * 2 + (core + slot // half) % 2, count_ref, rank_ref, owner_ref
    )
    wanted = slot_request(first, amount, core, slot % rows, rows)
    chosen = dot(one_hot((request == wanted) & (step == (slot % half) // rows)), low)
    shape = chosen.shape
    own = iota(shape, 0) // half == iota(shape, 1) // rank_w
    chosen = jnp.where(own, chosen, 0.0).astype(BF16)
    for p in range(parts):
        at = slice(p * cols, (p + 1) * cols)
        turned = jnp.concatenate([u0[:, at], u1[:, at]], axis=0)
        out_ref[p] = dot(chosen, turned).astype(BF16)


def delta_parts(blocks, downs, ups, before, tables, steps, rows):
    each, width = blocks[0].shape
    parts = 2 * len(blocks)
    slots = 2 * steps * rows
    rank_w = downs[0].shape[1]
    vmem = pl.BlockSpec(memory_space=pltpu.VMEM)
    smem = pl.BlockSpec(memory_space=pltpu.SMEM)
    return pl.pallas_call(
        functools.partial(delta_kernel, steps, rows),
        out_shape=(
            jax.ShapeDtypeStruct((parts, slots, width // parts), BF16),
            jax.ShapeDtypeStruct((len(blocks) * each, width), BF16),
        ),
        in_specs=[smem] * 3
        + [vmem] * (4 + len(blocks))
        + [pl.BlockSpec(memory_space=pl.ANY)],
        out_specs=(vmem, vmem),
        compiler_params=pltpu.CompilerParams(vmem_limit_bytes=24 * 2**20),
        cost_estimate=pl.CostEstimate(
            flops=4 * (len(blocks) * each + slots) * width * rank_w,
            bytes_accessed=2 * width * (len(blocks) * each + 4 * rank_w + slots),
            transcendentals=0,
        ),
        name="delta",
    )(*in_hbm(*tables), *downs, *ups, *blocks, before)


def base_kernel(own_ref, other_ref, w_ref, out_ref):
    total, width = own_ref.shape
    cuts = 8
    deep = width // cuts
    for i in range(cuts):
        at = slice(i * deep, (i + 1) * deep)
        part = dot(jnp.concatenate([own_ref[:, at], other_ref[:, at]], axis=0), w_ref[at, :])
        out_ref[...] = part if i == 0 else out_ref[...] + part


def base_part(own, other, out_weight):
    total, width = own.shape
    cols = out_weight.shape[1]
    vmem = pl.BlockSpec(memory_space=pltpu.VMEM)
    return pl.pallas_call(
        base_kernel,
        out_shape=jax.ShapeDtypeStruct((2 * total, cols), F32),
        in_specs=[vmem] * 3,
        out_specs=vmem,
        compiler_params=pltpu.CompilerParams(vmem_limit_bytes=24 * 2**20),
        cost_estimate=pl.CostEstimate(
            flops=4 * total * width * cols,
            bytes_accessed=2 * width * (2 * total + cols) + 8 * total * cols,
            transcendentals=0,
        ),
        name="base",
    )(own, other, out_weight)


def join_kernel(rows, count_ref, rank_ref, owner_ref, base_ref, delta_ref, out_ref):
    me = lax.axis_index("tensor")
    chip, core = me // 2, me % 2
    steps, requests, cols = out_ref.shape
    parts, slots, _ = delta_ref.shape
    total = base_ref.shape[0]
    wide = parts * slots
    half = slots // 2
    each = steps * rows
    entry = iota((1, wide), 1)
    source, slot = entry // slots, entry % slots
    first, amount = adapter_of(
        source // 2 * 2 + (source + slot // half) % 2, count_ref, rank_ref, owner_ref
    )
    wanted = slot_request(first, amount, source % 2, slot % rows, rows)

    def row_place(index):
        turn = index // (total // 2)
        rest = index % (total // 2)
        device = sender(rest // each, chip, parts // 2) * 2 + (core + turn) % 2
        return device * rows + index % rows, (index % each) // rows

    request, step = row_place(iota((total, 1), 0))
    place = (request == wanted) & (step == (slot % half) // rows)
    delta = dot(one_hot(place), delta_ref[...].reshape(wide, cols))
    result = (base_ref[...] + delta).astype(BF16)
    request, step = row_place(iota((total, total), 1))
    order = one_hot(iota((total, total), 0) == step * requests + request)
    turned = dot(order, result).astype(BF16)
    for t in range(steps):
        out_ref[t] = turned[t * requests : (t + 1) * requests]


def join(base, delta, tables, steps, rows):
    total, cols = base.shape
    vmem = pl.BlockSpec(memory_space=pltpu.VMEM)
    smem = pl.BlockSpec(memory_space=pltpu.SMEM)
    return pl.pallas_call(
        functools.partial(join_kernel, rows),
        out_shape=jax.ShapeDtypeStruct((steps, total // steps, cols), BF16),
        in_specs=[smem] * 3 + [vmem] * 2,
        out_specs=vmem,
        compiler_params=pltpu.CompilerParams(vmem_limit_bytes=24 * 2**20),
        name="join",
    )(*in_hbm(*tables), base, delta)


def per_device(
    queries,
    new_keys,
    new_values,
    cache_keys,
    cache_values,
    kv_len,
    adapter_rows,
    adapter_rank,
    adapter_owner,
    out_weight,
    store_down,
    store_up,
):
    parts = lax.axis_size("tensor")
    steps, rows, width = queries.shape
    tables = (adapter_rows, adapter_rank, adapter_owner)
    attended, store = attend(
        queries, new_keys, new_values, cache_keys, cache_values, kv_len, store_down, store_up
    )
    blocks = gather(attended, parts)
    other = swap(store, 1, parts)
    weight = stage_weight(attended, out_weight)
    send, own_rows = delta_parts(
        blocks, (store, other), (turn(store), turn(other)), weight, tables, steps, rows
    )
    other_rows = swap(own_rows, 1, parts)
    delta = lax.all_to_all(send, "tensor", split_axis=0, concat_axis=0, tiled=True)
    base = base_part(own_rows, other_rows, weight)
    return join(base, delta, tables, steps, rows)


def solution(mesh):
    in_specs = (
        P(None, ("groups", "tensor"), None),
        P(None, ("groups", "tensor"), None),
        P(None, ("groups", "tensor"), None),
        P(("groups", "tensor"), None, None),
        P(("groups", "tensor"), None, None),
        P(("groups", "tensor")),
        P("groups"),
        P(),
        P(),
        P(None, "tensor"),
        P("tensor", None, None),
        P("tensor", None, None),
    )
    out_specs = P(None, "groups", "tensor")
    return jax.shard_map(
        per_device, mesh=mesh, in_specs=in_specs, out_specs=out_specs, check_vma=False
    )
```

time: 93.3 us -> 55.7 us (0.60)
  waiting for transfers between devices: 48.1 us -> 11.2 us
  starting transfers between devices: 3.53 us -> 18.4 us
  between operations: 13.4 us -> 0.1 us
  local copies, waits for them, and re-layouts: 15.5 us -> 3.46 us
  Pallas kernels: 12.2 us -> 22.1 us
    all_gather x1 -> x0, waiting for transfers between devices: 44.3 us -> none  [per_device(): gathered = lax.all_gather(attended, 'tensor', axis=0, tiled=True)]
    ppermute x0 -> x9, starting transfers between devices: none -> 12.4 us  [swap(): return lax.ppermute(x, 'tensor', [(i, i ^ bits) for i in range(parts)])]
    unnamed x28 -> x4, local copies, waits for them, and re-layouts: 15.5 us -> 3.46 us
    pallas_call x3 -> x6, Pallas kernels: 10.7 us -> 20.4 us  [the longest x1 10.4 us: attend(): pl.pallas_call(attend_kernel, out_shape=(jax.ShapeDtypeStruct((steps * ro...]
    ppermute x0 -> x9, waiting for transfers between devices: none -> 5.83 us  [swap(): return lax.ppermute(x, 'tensor', [(i, i ^ bits) for i in range(parts)])]
    all_to_all x1, starting transfers between devices: 3.53 us -> 6.09 us  [per_device(): lax.all_to_all(send, 'tensor', split_axis=0, concat_axis=0, tiled=True)]
    all_to_all x1, waiting for transfers between devices: 3.8 us -> 5.4 us  [per_device(): lax.all_to_all(send, 'tensor', split_axis=0, concat_axis=0, tiled=True)]
  transfers between devices with their start and end apart: 2 -> 10, of which waited for: 2 -> 3; matrix products, arithmetic and copies ran while one was open for 0% -> 0% of each run, Pallas kernels for 3% -> 11%
where the time goes in v4:
time: 55.7 us; the launch traced here: 55.3 us
  Pallas kernels  22.1 us (40%)
  starting transfers between devices  18.4 us (33%)
  waiting for transfers between devices  11.2 us (20%)
  local copies, waits for them, and re-layouts  3.46 us (6%)
    ppermute x9, starting transfers between devices, swap(): return lax.ppermute(x, 'tensor', [(i, i ^ bits) for i in range(parts)])  12.4 us
    pallas_call x1, Pallas kernels, attend(): pl.pallas_call(attend_kernel, out_shape=(jax.ShapeDtypeStruct((steps * ro...  10.4 us
    all_to_all x1, starting transfers between devices, per_device(): lax.all_to_all(send, 'tensor', split_axis=0, concat_axis=0, tiled=True)  6.09 us
    ppermute x9, waiting for transfers between devices, swap(): return lax.ppermute(x, 'tensor', [(i, i ^ bits) for i in range(parts)])  5.83 us
    all_to_all x1, waiting for transfers between devices, per_device(): lax.all_to_all(send, 'tensor', split_axis=0, concat_axis=0, tiled=True)  5.4 us
    pallas_call x1, Pallas kernels, delta_parts(): pl.pallas_call(functools.partial(delta_kernel, steps, rows), out_shape=(j...  4.01 us
    pallas_call x1, Pallas kernels, stage_weight(): pl.pallas_call(stage_weight_kernel, out_shape=jax.ShapeDtypeStruct(out_we...  3.47 us
    unnamed x4, local copies, waits for them, and re-layouts  3.46 us
  transfers between devices with their start and end apart: 10, of which 3 were waited for; matrix products, arithmetic and copies ran while one was open for 0% of the time, Pallas kernels for 11%

profile of v4, /device:TPU:0, one launch (start us, length us, event | category | flops | bytes accessed | tf_op | source)
XLA Modules:
  0.0 55.3 jit_solution(13598682051723003290)
XLA Ops:
  0.0 10.4 %attend.1 = (bf16[8,8192]{1,0:T(8,128)(2,1)S(1)}, bf16[16384,128]{1,0:T(8,128)(2,1)S(1)}) custom-call(s32[4]{0:T(128)} %len_ref.1, bf16[2,4,8192]{2,1,0:T(4,128)(2,1)} %q_hbm.1, bf16[2,4,1024]{2,1,0:T(4,128)(2,1)} %nk_hbm.1, bf16[2,4,1024]{2,1,0:T(4,128)(2,1)} %nv_hbm.1, bf16[4,512,1024]{2,1,0:T(8,128)(2,1)} %k_hbm.1, bf16[4,512,1024]{2,1,0:T(8,128)(2,1)} %v_hbm.1, ...), custom_call_target="tpu_custom_call" | custom-call | flops 134217728 | bytes 8388608 | tf_op jit(solution)/shard_map/attend/pallas_call | solution.py:145
  10.4 0.5 collective-permute-start
  11.0 3.7 %collective-permute-start.4 = (bf16[8,8192]{1,0:T(8,128)(2,1)S(1)}, bf16[8,8192]{1,0:T(8,128)(2,1)S(1)}, u32[]{:S(2)}, u32[]{:S(2)}) collective-permute-start(bf16[8,8192]{1,0:T(8,128)(2,1)S(1)} %get-tuple-element.10.after.rest_4_), channel_id=1, source_target_pairs={{0,8},{1,9},{2,10},{3,11},{4,12},{5,13},{6,14},{7,15},{8,0},{9,1},... | collective-permute-start | bytes 393224 | tf_op jit(solution)/shard_map/ppermute | solution.py:194
  14.6 1.6 %collective-permute-start.2 = (bf16[8,8192]{1,0:T(8,128)(2,1)S(1)}, bf16[8,8192]{1,0:T(8,128)(2,1)S(1)}, u32[]{:S(2)}, u32[]{:S(2)}) collective-permute-start(bf16[8,8192]{1,0:T(8,128)(2,1)S(1)} %get-tuple-element.10.after.rest_4_), channel_id=1, source_target_pairs={{0,4},{1,5},{2,6},{3,7},{4,0},{5,1},{6,2},{7,3},{8,12},{9,13},{10,... | collective-permute-start | bytes 393224 | tf_op jit(solution)/shard_map/ppermute | solution.py:194
  16.2 1.5 %collective-permute-start.1 = (bf16[8,8192]{1,0:T(8,128)(2,1)S(1)}, bf16[8,8192]{1,0:T(8,128)(2,1)S(1)}, u32[]{:S(2)}, u32[]{:S(2)}) collective-permute-start(bf16[8,8192]{1,0:T(8,128)(2,1)S(1)} %get-tuple-element.10.after.rest_4_), channel_id=1, source_target_pairs={{0,2},{1,3},{2,0},{3,1},{4,6},{5,7},{6,4},{7,5},{8,10},{9,11},{10,... | collective-permute-start | bytes 393224 | tf_op jit(solution)/shard_map/ppermute | solution.py:194
  17.7 3.9 %collective-permute-done.4.rest_8_ = bf16[8,8192]{1,0:T(8,128)(2,1)S(1)} collective-permute-done((bf16[8,8192]{1,0:T(8,128)(2,1)S(1)}, bf16[8,8192]{1,0:T(8,128)(2,1)S(1)}, u32[]{:S(2)}, u32[]{:S(2)}) %collective-permute-start.4) | collective-permute-done | bytes 131104 | tf_op jit(solution)/shard_map/ppermute | solution.py:194
  21.6 1.6 %collective-permute-start.7 = (bf16[8,8192]{1,0:T(8,128)(2,1)S(1)}, bf16[8,8192]{1,0:T(8,128)(2,1)S(1)}, u32[]{:S(2)}, u32[]{:S(2)}) collective-permute-start(bf16[8,8192]{1,0:T(8,128)(2,1)S(1)} %collective-permute-done.4.rest_8_), channel_id=1, source_target_pairs={{0,6},{1,7},{2,4},{3,5},{4,2},{5,3},{6,0},{7,1},{8,14},{9,15},{10,... | collective-permute-start | bytes 393224 | tf_op jit(solution)/shard_map/ppermute | solution.py:194
  23.2 1.4 %collective-permute-start.6 = (bf16[8,8192]{1,0:T(8,128)(2,1)S(1)}, bf16[8,8192]{1,0:T(8,128)(2,1)S(1)}, u32[]{:S(2)}, u32[]{:S(2)}) collective-permute-start(bf16[8,8192]{1,0:T(8,128)(2,1)S(1)} %collective-permute-done.4.rest_8_), channel_id=1, source_target_pairs={{0,4},{1,5},{2,6},{3,7},{4,0},{5,1},{6,2},{7,3},{8,12},{9,13},{10,... | collective-permute-start | bytes 393224 | tf_op jit(solution)/shard_map/ppermute | solution.py:194
  24.7 0.0 collective-permute-done.2.rest_6_
  24.7 0.4 collective-permute-start.5
  25.1 0.0 collective-permute-done.store_ref.rest_1_
  25.1 1.6 %collective-permute-start.3 = (bf16[8,8192]{1,0:T(8,128)(2,1)S(1)}, bf16[8,8192]{1,0:T(8,128)(2,1)S(1)}, u32[]{:S(2)}, u32[]{:S(2)}) collective-permute-start(bf16[8,8192]{1,0:T(8,128)(2,1)S(1)} %collective-permute-done.2.rest_6_), channel_id=1, source_target_pairs={{0,2},{1,3},{2,0},{3,1},{4,6},{5,7},{6,4},{7,5},{8,10},{9,11},{10,... | collective-permute-start | bytes 393224 | tf_op jit(solution)/shard_map/ppermute | solution.py:194
  26.7 3.5 %stage_weight.1.rest_12_.w_ref = bf16[8192,512]{1,0:T(8,128)(2,1)S(1)} custom-call(bf16[8,8192]{1,0:T(8,128)(2,1)S(1)} %get-tuple-element.10.after.rest_4_, bf16[8192,512]{1,0:T(8,128)(2,1)} %w_hbm.1), custom_call_target="tpu_custom_call" | custom-call | flops 40000000000 | bytes 16777216 | tf_op jit(solution)/shard_map/stage_weight/pallas_call | solution.py:255
  30.2 0.0 copy-start
  30.2 0.6 %turn.2.rest_2_ = bf16[128,8192]{1,0:T(8,128)(2,1)S(1)} custom-call(bf16[16384,128]{1,0:T(8,128)(2,1)S(1)} %get-tuple-element.9.store_ref.rest_0_), custom_call_target="tpu_custom_call" | custom-call | bytes 4194304 | tf_op jit(solution)/shard_map/turn/pallas_call | solution.py:230
  30.8 0.6 %turn.3.rest_3_ = bf16[128,8192]{1,0:T(8,128)(2,1)S(1)} custom-call(bf16[16384,128]{1,0:T(8,128)(2,1)S(1)} %collective-permute-done.store_ref.rest_1_), custom_call_target="tpu_custom_call" | custom-call | bytes 4194304 | tf_op jit(solution)/shard_map/turn/pallas_call | solution.py:230
  31.4 0.0 collective-permute-done.1.rest_5_
  31.4 0.0 collective-permute-done.7.rest_11_
  31.4 0.0 collective-permute-done.6.rest_10_
  31.4 0.0 collective-permute-done.5.rest_9_
  31.5 1.9 %collective-permute-done.3.rest_7_ = bf16[8,8192]{1,0:T(8,128)(2,1)S(1)} collective-permute-done((bf16[8,8192]{1,0:T(8,128)(2,1)S(1)}, bf16[8,8192]{1,0:T(8,128)(2,1)S(1)}, u32[]{:S(2)}, u32[]{:S(2)}) %collective-permute-start.3) | collective-permute-done | bytes 131104 | tf_op jit(solution)/shard_map/ppermute | solution.py:194
  33.3 0.1 copy-done
  33.4 4.0 %delta.1 = (bf16[16,16,512]{2,1,0:T(8,128)(2,1)}, bf16[64,8192]{1,0:T(8,128)(2,1)S(1)}) custom-call(s32[12]{0:T(128)} %count_ref.3, s32[12]{0:T(128)} %rank_ref.3, s32[12]{0:T(128)} %owner_ref.3, bf16[16384,128]{1,0:T(8,128)(2,1)S(1)} %get-tuple-element.9.store_ref.rest_0_, bf16[16384,128]{1,0:T(8,128)(2,1)S(1)} %collective-permute-done.store_ref.rest_1_, ...), custom_call_target="tpu_custom_call" | custom-call | flops 335544320 | bytes 9699328 | tf_op jit(solution)/shard_map/delta/pallas_call | solution.py:339
  37.4 0.0 collective-permute-start.8
  37.4 6.1 %all-to-all-start = ((bf16[16,16,512]{2,1,0:T(8,128)(2,1)}), bf16[16,16,512]{2,1,0:T(8,128)(2,1)S(1)}, u32[]{:S(2)}, u32[]{:S(2)}) async-start(bf16[16,16,512]{2,1,0:T(8,128)(2,1)} %get-tuple-element.12), calls=%async_computation | async-start | bytes 524288 | tf_op jit(solution)/shard_map/all_to_all | solution.py:462
  43.5 0.0 collective-permute-done.8.other_ref
  43.6 0.0 copy-start.1
  43.6 3.4 %copy-done.1 = bf16[8192,512]{1,0:T(8,128)(2,1)S(1)} copy-done((bf16[8192,512]{1,0:T(8,128)(2,1)S(1)}, bf16[8192,512]{1,0:T(8,128)(2,1)}, u32[]{:S(2)}) %copy-start.1) | copy-done | bytes 8388632
  46.9 1.2 %base.1.base_ref = f32[128,512]{1,0:T(8,128)S(1)} custom-call(bf16[64,8192]{1,0:T(8,128)(2,1)S(1)} %get-tuple-element.11.own_ref, bf16[64,8192]{1,0:T(8,128)(2,1)S(1)} %collective-permute-done.8.other_ref, bf16[8192,512]{1,0:T(8,128)(2,1)S(1)} %copy-done.1), custom_call_target="tpu_custom_call" | custom-call | flops 1073741824 | bytes 10747904 | tf_op jit(solution)/shard_map/base/pallas_call | solution.py:373
  48.2 5.4 %all-to-all-done.delta_ref = bf16[16,16,512]{2,1,0:T(8,128)(2,1)S(1)} async-done(((bf16[16,16,512]{2,1,0:T(8,128)(2,1)}), bf16[16,16,512]{2,1,0:T(8,128)(2,1)S(1)}, u32[]{:S(2)}, u32[]{:S(2)}) %all-to-all-start) | async-done | bytes 262176 | tf_op jit(solution)/shard_map/all_to_all | solution.py:462
  53.6 1.8 %join.1 = bf16[2,64,512]{2,1,0:T(8,128)(2,1)} custom-call(s32[12]{0:T(128)} %count_ref.3, s32[12]{0:T(128)} %rank_ref.3, s32[12]{0:T(128)} %owner_ref.3, f32[128,512]{1,0:T(8,128)S(1)} %base.1.base_ref, bf16[16,16,512]{2,1,0:T(8,128)(2,1)S(1)} %all-to-all-done.delta_ref), custom_call_target="tpu_custom_call" | custom-call | tf_op jit(solution)/shard_map/join/pallas_call | solution.py:425
Async XLA Ops:
  10.4 14.7 %collective-permute-start = (bf16[16384,128]{1,0:T(8,128)(2,1)S(1)}, bf16[16384,128]{1,0:T(8,128)(2,1)S(1)}, u32[]{:S(2)}, u32[]{:S(2)}) collective-permute-start(bf16[16384,128]{1,0:T(8,128)(2,1)S(1)} %get-tuple-element.9.store_ref.rest_0_), channel_id=1, source_target_pairs={{0,1},{1,0},{2,3},{3,2},{4,5},{5,4},{6,7},{7,6},{8,9},{9,8},{10,11... | collective-permute-start | bytes 12582920 | tf_op jit(solution)/shard_map/ppermute | solution.py:194
  11.0 10.7 %collective-permute-start.4 = (bf16[8,8192]{1,0:T(8,128)(2,1)S(1)}, bf16[8,8192]{1,0:T(8,128)(2,1)S(1)}, u32[]{:S(2)}, u32[]{:S(2)}) collective-permute-start(bf16[8,8192]{1,0:T(8,128)(2,1)S(1)} %get-tuple-element.10.after.rest_4_), channel_id=1, source_target_pairs={{0,8},{1,9},{2,10},{3,11},{4,12},{5,13},{6,14},{7,15},{8,0},{9,1},... | collective-permute-start | bytes 393224 | tf_op jit(solution)/shard_map/ppermute | solution.py:194
  14.6 10.1 %collective-permute-start.2 = (bf16[8,8192]{1,0:T(8,128)(2,1)S(1)}, bf16[8,8192]{1,0:T(8,128)(2,1)S(1)}, u32[]{:S(2)}, u32[]{:S(2)}) collective-permute-start(bf16[8,8192]{1,0:T(8,128)(2,1)S(1)} %get-tuple-element.10.after.rest_4_), channel_id=1, source_target_pairs={{0,4},{1,5},{2,6},{3,7},{4,0},{5,1},{6,2},{7,3},{8,12},{9,13},{10,... | collective-permute-start | bytes 393224 | tf_op jit(solution)/shard_map/ppermute | solution.py:194
  16.2 15.2 %collective-permute-start.1 = (bf16[8,8192]{1,0:T(8,128)(2,1)S(1)}, bf16[8,8192]{1,0:T(8,128)(2,1)S(1)}, u32[]{:S(2)}, u32[]{:S(2)}) collective-permute-start(bf16[8,8192]{1,0:T(8,128)(2,1)S(1)} %get-tuple-element.10.after.rest_4_), channel_id=1, source_target_pairs={{0,2},{1,3},{2,0},{3,1},{4,6},{5,7},{6,4},{7,5},{8,10},{9,11},{10,... | collective-permute-start | bytes 393224 | tf_op jit(solution)/shard_map/ppermute | solution.py:194
  21.6 9.8 %collective-permute-start.7 = (bf16[8,8192]{1,0:T(8,128)(2,1)S(1)}, bf16[8,8192]{1,0:T(8,128)(2,1)S(1)}, u32[]{:S(2)}, u32[]{:S(2)}) collective-permute-start(bf16[8,8192]{1,0:T(8,128)(2,1)S(1)} %collective-permute-done.4.rest_8_), channel_id=1, source_target_pairs={{0,6},{1,7},{2,4},{3,5},{4,2},{5,3},{6,0},{7,1},{8,14},{9,15},{10,... | collective-permute-start | bytes 393224 | tf_op jit(solution)/shard_map/ppermute | solution.py:194
  23.2 8.2 %collective-permute-start.6 = (bf16[8,8192]{1,0:T(8,128)(2,1)S(1)}, bf16[8,8192]{1,0:T(8,128)(2,1)S(1)}, u32[]{:S(2)}, u32[]{:S(2)}) collective-permute-start(bf16[8,8192]{1,0:T(8,128)(2,1)S(1)} %collective-permute-done.4.rest_8_), channel_id=1, source_target_pairs={{0,4},{1,5},{2,6},{3,7},{4,0},{5,1},{6,2},{7,3},{8,12},{9,13},{10,... | collective-permute-start | bytes 393224 | tf_op jit(solution)/shard_map/ppermute | solution.py:194
  24.7 6.8 %collective-permute-start.5 = (bf16[8,8192]{1,0:T(8,128)(2,1)S(1)}, bf16[8,8192]{1,0:T(8,128)(2,1)S(1)}, u32[]{:S(2)}, u32[]{:S(2)}) collective-permute-start(bf16[8,8192]{1,0:T(8,128)(2,1)S(1)} %collective-permute-done.4.rest_8_), channel_id=1, source_target_pairs={{0,2},{1,3},{2,0},{3,1},{4,6},{5,7},{6,4},{7,5},{8,10},{9,11},{10,... | collective-permute-start | bytes 393224 | tf_op jit(solution)/shard_map/ppermute | solution.py:194
  25.1 8.2 %collective-permute-start.3 = (bf16[8,8192]{1,0:T(8,128)(2,1)S(1)}, bf16[8,8192]{1,0:T(8,128)(2,1)S(1)}, u32[]{:S(2)}, u32[]{:S(2)}) collective-permute-start(bf16[8,8192]{1,0:T(8,128)(2,1)S(1)} %collective-permute-done.2.rest_6_), channel_id=1, source_target_pairs={{0,2},{1,3},{2,0},{3,1},{4,6},{5,7},{6,4},{7,5},{8,10},{9,11},{10,... | collective-permute-start | bytes 393224 | tf_op jit(solution)/shard_map/ppermute | solution.py:194
  30.2 3.2 %copy-start = (bf16[8192,512]{1,0:T(8,128)(2,1)}, bf16[8192,512]{1,0:T(8,128)(2,1)S(1)}, u32[]{:S(2)}) copy-start(bf16[8192,512]{1,0:T(8,128)(2,1)S(1)} %stage_weight.1.rest_12_.w_ref) | copy-start | bytes 25165828
  37.4 6.1 %collective-permute-start.8 = (bf16[64,8192]{1,0:T(8,128)(2,1)S(1)}, bf16[64,8192]{1,0:T(8,128)(2,1)S(1)}, u32[]{:S(2)}, u32[]{:S(2)}) collective-permute-start(bf16[64,8192]{1,0:T(8,128)(2,1)S(1)} %get-tuple-element.11.own_ref), channel_id=1, source_target_pairs={{0,1},{1,0},{2,3},{3,2},{4,5},{5,4},{6,7},{7,6},{8,9},{9,8},{10,11... | collective-permute-start | bytes 3145736 | tf_op jit(solution)/shard_map/ppermute | solution.py:194
  37.4 16.1 %all-to-all-start = ((bf16[16,16,512]{2,1,0:T(8,128)(2,1)}), bf16[16,16,512]{2,1,0:T(8,128)(2,1)S(1)}, u32[]{:S(2)}, u32[]{:S(2)}) async-start(bf16[16,16,512]{2,1,0:T(8,128)(2,1)} %get-tuple-element.12), calls=%async_computation | async-start | bytes 524288 | tf_op jit(solution)/shard_map/all_to_all | solution.py:462
  43.6 3.4 %copy-start.1 = (bf16[8192,512]{1,0:T(8,128)(2,1)S(1)}, bf16[8192,512]{1,0:T(8,128)(2,1)}, u32[]{:S(2)}) copy-start(bf16[8192,512]{1,0:T(8,128)(2,1)} %copy-done) | copy-start | bytes 25165828

commit v5 on v3

v5 whole, which is shorter than its diff:
```python
import functools

import jax
import jax.numpy as jnp
from jax import lax
from jax.experimental import pallas as pl
from jax.experimental.pallas import tpu as pltpu
from jax.sharding import PartitionSpec as P

HQ = 64
KVH = 8
HD = 128
GROUP = HQ // KVH
MOST = 8
RING = 16
F32 = jnp.float32
BF16 = jnp.bfloat16
NT = (((1,), (1,)), ((), ()))


def in_hbm(*arrays):
    return [pltpu.with_memory_space_constraint(a, pltpu.HBM) for a in arrays]


def iota(shape, dim):
    return lax.broadcasted_iota(jnp.int32, shape, dim)


def one_hot(mask):
    return mask.astype(F32).astype(BF16)


def dot(a, b):
    return jnp.dot(a, b, preferred_element_type=F32)


def dot_nt(a, b):
    return lax.dot_general(a, b, NT, preferred_element_type=F32)


def attend_kernel(
    len_ref, q_hbm, nk_hbm, nv_hbm, k_hbm, v_hbm, out_ref,
    q_ref, nk_ref, nv_ref, k_ref, v_ref, qs, nks, nvs, mixed, small_sems, sems,
):
    steps, rows, width = q_ref.shape
    cache = k_ref.shape[1]
    both = steps * rows
    pack = steps * GROUP
    cuts = sems.shape[2]
    small = [
        pltpu.make_async_copy(src, dst, small_sems.at[i])
        for i, (src, dst) in enumerate(((q_hbm, q_ref), (nk_hbm, nk_ref), (nv_hbm, nv_ref)))
    ]
    pieces = [pl.ds(i * (cache // cuts), cache // cuts) for i in range(cuts)]
    keys, values = [
        [
            [
                pltpu.make_async_copy(src.at[r, at], dst.at[r, at], sems.at[r, j, i])
                for i, at in enumerate(pieces)
            ]
            for r in range(rows)
        ]
        for j, (src, dst) in enumerate(((k_hbm, k_ref), (v_hbm, v_ref)))
    ]
    for copy in small + keys[0] + values[0] + keys[1] + values[1]:
        copy.start()
    for copy in small:
        copy.wait()

    flat = jnp.concatenate([q_ref[t].astype(F32) for t in range(steps)], axis=0)
    blank = jnp.zeros((pack, HD), F32)
    for k in range(KVH):
        group = jnp.stack(
            [flat[:, (k * GROUP + g) * HD : (k * GROUP + g + 1) * HD] for g in range(GROUP)]
        )
        turned = jnp.swapaxes(group, 0, 1)
        for r in range(rows):
            mine = jnp.concatenate([turned[t * rows + r] for t in range(steps)], axis=0)
            sides = [mine, blank] if k % 2 == 0 else [blank, mine]
            qs[r, k * pack : (k + 1) * pack, :] = jnp.concatenate(sides, axis=1).astype(BF16)
    for src, dst in ((nk_ref, nks), (nv_ref, nvs)):
        fresh = [src[t].astype(F32) for t in range(steps)]
        fresh.append(jnp.zeros((16 - both, src.shape[2]), F32))
        dst[...] = jnp.concatenate(fresh, axis=0).astype(BF16)

    scale = HD ** (-0.5)
    pairs = [
        (slice(k * pack, (k + 2) * pack), slice(k * HD, (k + 2) * HD)) for k in range(0, KVH, 2)
    ]
    for r in range(rows):
        if r + 2 < rows:
            for copy in keys[r + 2] + values[r + 2]:
                copy.start()
        fresh = jnp.concatenate(
            [dot_nt(qs[r, own, :], nks[:, cols]) for own, cols in pairs], axis=0
        )
        slot = iota(fresh.shape, 1)
        step = (iota(fresh.shape, 0) // GROUP) % steps
        seen = (slot < both) & (slot % rows == r) & (slot // rows <= step)
        fresh = jnp.where(seen, fresh * scale, -jnp.inf)
        for copy in keys[r]:
            copy.wait()
        older = jnp.concatenate(
            [dot_nt(qs[r, own, :], k_ref[r, :, cols]) for own, cols in pairs], axis=0
        )
        older = jnp.where(iota(older.shape, 1) < len_ref[r], older * scale, -jnp.inf)
        top = jnp.maximum(
            jnp.max(older, axis=1, keepdims=True), jnp.max(fresh, axis=1, keepdims=True)
        )
        e_older = jnp.exp(older - top)
        e_fresh = jnp.exp(fresh - top)
        total = jnp.sum(e_older, axis=1, keepdims=True) + jnp.sum(e_fresh, axis=1, keepdims=True)
        inverse = 1.0 / total
        p_older = (e_older * inverse).astype(BF16)
        p_fresh = (e_fresh * inverse).astype(BF16)
        for copy in values[r]:
            copy.wait()
        for k, (own, cols) in zip(range(0, KVH, 2), pairs):
            pair = dot(p_older[own], v_ref[r, :, cols]) + dot(p_fresh[own], nvs[:, cols])
            mixed[r, k] = pair[:pack, :HD]
            mixed[r, k + 1] = pair[pack:, HD:]

    for k in range(KVH):
        turned = jnp.stack(
            [
                mixed[r, k, t * GROUP : (t + 1) * GROUP, :]
                for t in range(steps)
                for r in range(rows)
            ]
        )
        heads = jnp.swapaxes(turned, 0, 1)
        for g in range(GROUP):
            at = (k * GROUP + g) * HD
            out_ref[:, at : at + HD] = heads[g].astype(BF16)


def attend(queries, new_keys, new_values, cache_keys, cache_values, kv_len):
    steps, rows, width = queries.shape
    cache, kv_width = cache_keys.shape[1:]
    pack = steps * GROUP
    return pl.pallas_call(
        attend_kernel,
        out_shape=jax.ShapeDtypeStruct((steps * rows, width), BF16),
        in_specs=[pl.BlockSpec(memory_space=pltpu.SMEM)]
        + [pl.BlockSpec(memory_space=pl.ANY)] * 5,
        out_specs=pl.BlockSpec(memory_space=pltpu.VMEM),
        scratch_shapes=[
            pltpu.VMEM(queries.shape, BF16),
            pltpu.VMEM(new_keys.shape, BF16),
            pltpu.VMEM(new_values.shape, BF16),
            pltpu.VMEM(cache_keys.shape, BF16),
            pltpu.VMEM(cache_values.shape, BF16),
            pltpu.VMEM((rows, KVH * pack, 2 * HD), BF16),
            pltpu.VMEM((16, kv_width), BF16),
            pltpu.VMEM((16, kv_width), BF16),
            pltpu.VMEM((rows, KVH, pack, HD), F32),
            pltpu.SemaphoreType.DMA((3,)),
            pltpu.SemaphoreType.DMA((rows, 2, 2)),
        ],
        compiler_params=pltpu.CompilerParams(vmem_limit_bytes=32 * 2**20),
        cost_estimate=pl.CostEstimate(
            flops=4 * rows * steps * HQ * cache * HD,
            bytes_accessed=4 * rows * cache * kv_width,
            transcendentals=rows * steps * HQ * cache,
        ),
        name="attend",
    )(*in_hbm(kv_len, queries, new_keys, new_values, cache_keys, cache_values))


def sender(slot, me, parts):
    return me ^ slot if parts == RING else slot


def row_place(index, me, parts, steps, rows):
    both = steps * rows
    return sender(index // both, me, parts) * rows + index % rows, (index % both) // rows


def gather(block, parts):
    if parts != RING:
        whole = lax.all_gather(block, "tensor", axis=0, tiled=False)
        return [whole[i] for i in range(parts)]

    def flip(x, bits):
        return lax.ppermute(x, "tensor", [(i, i ^ bits) for i in range(RING)])

    core, y, z_near, z_far = 1, 2, 4, 8
    held = {0: block}
    held[z_far] = flip(block, z_far)
    held[z_near] = flip(block, z_near)
    held[y] = flip(block, y)
    held[y | z_near] = flip(block, y | z_near)
    held[y | z_far] = flip(held[z_far], y)
    held[y | z_far | z_near] = flip(held[z_far], y | z_near)
    held[z_far | z_near] = flip(held[z_far], z_near)
    for slot in list(held):
        held[slot | core] = flip(held[slot], core)
    return [held[slot] for slot in range(RING)]


def stage_kernel(after, d_hbm, u_hbm, d_ref, ut_ref, up, sems):
    width = u_hbm.shape[1]
    cuts = sems.shape[1]
    deep = width // cuts
    copies = []
    for j, (src, dst) in enumerate(((u_hbm, up), (d_hbm, d_ref))):
        for i in range(cuts):
            at = pl.ds(i * deep, deep)
            copies.append(pltpu.make_async_copy(src.at[0, at], dst.at[at], sems.at[j, i]))
            copies[-1].start()
    for i in range(cuts):
        copies[i].wait()
        at = slice(i * deep, (i + 1) * deep)
        ut_ref[:, at] = jnp.transpose(up[at, :])
    for copy in copies[cuts:]:
        copy.wait()


def stage(after, store_down, store_up):
    width, rank_w = store_down.shape[1:]
    vmem = pl.BlockSpec(memory_space=pltpu.VMEM)
    return pl.pallas_call(
        stage_kernel,
        out_shape=(
            jax.ShapeDtypeStruct((width, rank_w), BF16),
            jax.ShapeDtypeStruct((rank_w, width), BF16),
        ),
        in_specs=[pl.BlockSpec(memory_space=pl.ANY)] * 3,
        out_specs=(vmem, vmem),
        scratch_shapes=[
            pltpu.VMEM((width, rank_w), BF16),
            pltpu.SemaphoreType.DMA((2, 4)),
        ],
        compiler_params=pltpu.CompilerParams(vmem_limit_bytes=16 * 2**20),
        cost_estimate=pl.CostEstimate(
            flops=4 * 10**10, bytes_accessed=8 * width * rank_w, transcendentals=0
        ),
        name="stage",
    )(after, *in_hbm(store_down, store_up))


def delta_kernel(steps, rows, count_ref, rank_ref, owner_ref, d_ref, ut_ref, *rest):
    blocks, (out_ref, rows_ref) = rest[:-2], rest[-2:]
    block = lax.axis_index("tensor")
    parts, slots, cols = out_ref.shape
    each, width = blocks[0].shape
    total = parts * each
    cuts = 8
    deep = width // cuts
    low = jnp.zeros((total, d_ref.shape[1]), F32)
    for i in range(cuts):
        at = slice(i * deep, (i + 1) * deep)
        piece = jnp.concatenate([b[:, at] for b in blocks], axis=0)
        rows_ref[:, at] = piece
        low = low + dot(piece, d_ref[at, :])
    start = jnp.int32(0)
    first = jnp.int32(0)
    amount = jnp.int32(0)
    for a in range(count_ref.shape[0]):
        owned = (owner_ref[a] <= block) & (block < owner_ref[a] + rank_ref[a])
        first = jnp.where(owned, start, first)
        amount = jnp.where(owned, count_ref[a], amount)
        start = start + count_ref[a]
    slot = iota((slots, total), 0)
    request, step = row_place(iota((slots, total), 1), block, parts, steps, rows)
    nth = slot % MOST
    pick = (step == slot // MOST) & (request == first + nth) & (nth < amount)
    chosen = dot(one_hot(pick), low.astype(BF16)).astype(BF16)
    for p in range(parts):
        out_ref[p] = dot(chosen, ut_ref[:, p * cols : (p + 1) * cols]).astype(BF16)


def delta_parts(blocks, down, up, tables, steps, rows):
    parts = len(blocks)
    each, width = blocks[0].shape
    slots = steps * MOST
    rank_w = down.shape[1]
    vmem = pl.BlockSpec(memory_space=pltpu.VMEM)
    smem = pl.BlockSpec(memory_space=pltpu.SMEM)
    return pl.pallas_call(
        functools.partial(delta_kernel, steps, rows),
        out_shape=(
            jax.ShapeDtypeStruct((parts, slots, width // parts), BF16),
            jax.ShapeDtypeStruct((parts * each, width), BF16),
        ),
        in_specs=[smem] * 3 + [vmem] * (2 + parts),
        out_specs=(vmem, vmem),
        compiler_params=pltpu.CompilerParams(vmem_limit_bytes=24 * 2**20),
        cost_estimate=pl.CostEstimate(
            flops=2 * (parts * each + slots) * width * rank_w,
            bytes_accessed=2 * width * (2 * parts * each + 2 * rank_w + slots),
            transcendentals=0,
        ),
        name="delta",
    )(*in_hbm(*tables), down, up, *blocks)


def base_kernel(a_ref, w_ref, out_ref):
    width = a_ref.shape[1]
    cuts = 8
    deep = width // cuts
    for i in range(cuts):
        at = slice(i * deep, (i + 1) * deep)
        part = dot(a_ref[:, at], w_ref[at, :])
        out_ref[...] = part if i == 0 else out_ref[...] + part


def base_part(gathered, out_weight):
    total, width = gathered.shape
    cols = out_weight.shape[1]
    vmem = pl.BlockSpec(memory_space=pltpu.VMEM)
    return pl.pallas_call(
        base_kernel,
        out_shape=jax.ShapeDtypeStruct((total, cols), F32),
        in_specs=[vmem] * 2,
        out_specs=vmem,
        compiler_params=pltpu.CompilerParams(vmem_limit_bytes=24 * 2**20),
        cost_estimate=pl.CostEstimate(
            flops=2 * total * width * cols,
            bytes_accessed=2 * width * (total + cols) + 4 * total * cols,
            transcendentals=0,
        ),
        name="base",
    )(gathered, out_weight)


def join_kernel(rows, count_ref, rank_ref, owner_ref, base_ref, delta_ref, out_ref):
    steps, requests, cols = out_ref.shape
    parts, slots, _ = delta_ref.shape
    total = base_ref.shape[0]
    me = lax.axis_index("tensor")
    wide = parts * slots
    entry = lax.broadcasted_iota(jnp.int32, (1, wide), 1)
    block = entry // slots
    first = jnp.zeros((1, wide), jnp.int32)
    amount = jnp.zeros((1, wide), jnp.int32)
    start = jnp.int32(0)
    for a in range(count_ref.shape[0]):
        owned = (owner_ref[a] <= block) & (block < owner_ref[a] + rank_ref[a])
        first = jnp.where(owned, start, first)
        amount = jnp.where(owned, count_ref[a], amount)
        start = start + count_ref[a]
    nth = entry % MOST
    goal = jnp.where(nth < amount, first + nth, -1)
    goal_step = (entry % slots) // MOST
    request, step = row_place(
        lax.broadcasted_iota(jnp.int32, (total, 1), 0), me, parts, steps, rows
    )
    place = (request == goal) & (step == goal_step)
    delta = dot(place.astype(F32).astype(BF16), delta_ref[...].reshape(wide, cols))
    result = (base_ref[...] + delta).astype(BF16)
    request, step = row_place(
        lax.broadcasted_iota(jnp.int32, (total, total), 1), me, parts, steps, rows
    )
    goal = lax.broadcasted_iota(jnp.int32, (total, total), 0)
    order = (goal == step * requests + request).astype(F32).astype(BF16)
    turned = dot(order, result).astype(BF16)
    for t in range(steps):
        out_ref[t] = turned[t * requests : (t + 1) * requests]


def join(base, delta, tables, steps, rows):
    total, cols = base.shape
    vmem = pl.BlockSpec(memory_space=pltpu.VMEM)
    smem = pl.BlockSpec(memory_space=pltpu.SMEM)
    return pl.pallas_call(
        functools.partial(join_kernel, rows),
        out_shape=jax.ShapeDtypeStruct((steps, total // steps, cols), BF16),
        in_specs=[smem] * 3 + [vmem] * 2,
        out_specs=vmem,
        compiler_params=pltpu.CompilerParams(vmem_limit_bytes=24 * 2**20),
        name="join",
    )(*in_hbm(*tables), base, delta)


def per_device(
    queries,
    new_keys,
    new_values,
    cache_keys,
    cache_values,
    kv_len,
    adapter_rows,
    adapter_rank,
    adapter_owner,
    out_weight,
    store_down,
    store_up,
):
    parts = lax.axis_size("tensor")
    steps, rows, width = queries.shape
    tables = (adapter_rows, adapter_rank, adapter_owner)
    attended = attend(queries, new_keys, new_values, cache_keys, cache_values, kv_len)
    blocks = gather(attended, parts)
    down, up = stage(blocks[2], store_down, store_up)
    send, gathered = delta_parts(blocks, down, up, tables, steps, rows)
    delta = lax.all_to_all(send, "tensor", split_axis=0, concat_axis=0, tiled=True)
    base = base_part(gathered, out_weight)
    return join(base, delta, tables, steps, rows)


def solution(mesh):
    in_specs = (
        P(None, ("groups", "tensor"), None),
        P(None, ("groups", "tensor"), None),
        P(None, ("groups", "tensor"), None),
        P(("groups", "tensor"), None, None),
        P(("groups", "tensor"), None, None),
        P(("groups", "tensor")),
        P("groups"),
        P(),
        P(),
        P(None, "tensor"),
        P("tensor", None, None),
        P("tensor", None, None),
    )
    out_specs = P(None, "groups", "tensor")
    return jax.shard_map(
        per_device, mesh=mesh, in_specs=in_specs, out_specs=out_specs, check_vma=False
    )
```

time: 54.6 us -> 49.7 us (0.910)
  Pallas kernels: 21.1 us -> 14.4 us
  local copies, waits for them, and re-layouts: 0 us -> 3.38 us
  starting transfers between devices: 20.1 us -> 17.4 us
  waiting for transfers between devices: 12.8 us -> 14.1 us
    pallas_call x1, Pallas kernels: 6.81 us -> 1.25 us  [base_part(): pl.pallas_call(base_kernel, out_shape=jax.ShapeDtypeStruct((total, cols),...]
    unnamed x0 -> x2, local copies, waits for them, and re-layouts: none -> 3.38 us
    all_to_all x1, waiting for transfers between devices: 3.23 us -> 5.41 us  [per_device(): lax.all_to_all(send, 'tensor', split_axis=0, concat_axis=0, tiled=True)]
    all_to_all x1, starting transfers between devices: 6.78 us -> 4.97 us  [per_device(): lax.all_to_all(send, 'tensor', split_axis=0, concat_axis=0, tiled=True)]
    pallas_call x1, Pallas kernels: 7.81 us -> 6.69 us  [attend(): pl.pallas_call(attend_kernel, out_shape=jax.ShapeDtypeStruct((steps * row...]
    ppermute x15, waiting for transfers between devices: 9.61 us -> 8.68 us  [flip(): return lax.ppermute(x, 'tensor', [(i, i ^ bits) for i in range(RING)])]
    ppermute x15, starting transfers between devices: 13.4 us -> 12.4 us  [flip(): return lax.ppermute(x, 'tensor', [(i, i ^ bits) for i in range(RING)])]
    pallas_call x1 -> x2, Pallas kernels: 4.81 us -> 4.81 us  [the longest x1 2.59 us: delta_parts(): pl.pallas_call(functools.partial(delta_kernel, steps, rows), out_shape=(j...]
  transfers between devices with their start and end apart: 16 -> 16, of which waited for: 8 -> 7; matrix products, arithmetic and copies ran while one was open for 0% -> 0% of each run, Pallas kernels for 13% -> 7%
where the time goes in v5:
time: 49.7 us; the launch traced here: 49.4 us
  starting transfers between devices  17.4 us (35%)
  Pallas kernels  14.4 us (29%)
  waiting for transfers between devices  14.1 us (28%)
  local copies, waits for them, and re-layouts  3.38 us (7%)
    ppermute x15, starting transfers between devices, flip(): return lax.ppermute(x, 'tensor', [(i, i ^ bits) for i in range(RING)])  12.4 us
    ppermute x15, waiting for transfers between devices, flip(): return lax.ppermute(x, 'tensor', [(i, i ^ bits) for i in range(RING)])  8.68 us
    pallas_call x1, Pallas kernels, attend(): pl.pallas_call(attend_kernel, out_shape=jax.ShapeDtypeStruct((steps * row...  6.69 us
    all_to_all x1, waiting for transfers between devices, per_device(): lax.all_to_all(send, 'tensor', split_axis=0, concat_axis=0, tiled=True)  5.41 us
    all_to_all x1, starting transfers between devices, per_device(): lax.all_to_all(send, 'tensor', split_axis=0, concat_axis=0, tiled=True)  4.97 us
    unnamed x2, local copies, waits for them, and re-layouts  3.38 us
    pallas_call x1, Pallas kernels, delta_parts(): pl.pallas_call(functools.partial(delta_kernel, steps, rows), out_shape=(j...  2.59 us
    pallas_call x1, Pallas kernels, stage(): pl.pallas_call(stage_kernel, out_shape=(jax.ShapeDtypeStruct((width, rank...  2.21 us
  transfers between devices with their start and end apart: 16, of which 7 were waited for; matrix products, arithmetic and copies ran while one was open for 0% of the time, Pallas kernels for 7%

profile of v5, /device:TPU:0, one launch (start us, length us, event | category | flops | bytes accessed | tf_op | source)
XLA Modules:
  0.0 49.4 jit_solution(17350909016987777135)
XLA Ops:
  0.0 6.7 %attend.1.rest_0_ = bf16[8,8192]{1,0:T(8,128)(2,1)S(1)} custom-call(s32[4]{0:T(128)} %len_ref.1, bf16[2,4,8192]{2,1,0:T(4,128)(2,1)} %q_hbm.1, bf16[2,4,1024]{2,1,0:T(4,128)(2,1)} %nk_hbm.1, bf16[2,4,1024]{2,1,0:T(4,128)(2,1)} %nv_hbm.1, bf16[4,512,1024]{2,1,0:T(8,128)(2,1)} %k_hbm.1, bf16[4,512,1024]{2,1,0:T(8,128)(2,1)} %v_hbm.1), custom_call_target="tpu_custom_call" | custom-call | flops 134217728 | bytes 8388608 | tf_op jit(solution)/shard_map/attend/pallas_call | solution.py:141
  6.7 4.1 %collective-permute-start.7 = (bf16[8,8192]{1,0:T(8,128)(2,1)S(1)}, bf16[8,8192]{1,0:T(8,128)(2,1)S(1)}, u32[]{:S(2)}, u32[]{:S(2)}) collective-permute-start(bf16[8,8192]{1,0:T(8,128)(2,1)S(1)} %attend.1.rest_0_), channel_id=1, source_target_pairs={{0,8},{1,9},{2,10},{3,11},{4,12},{5,13},{6,14},{7,15},{8,0},{9,1},... | collective-permute-start | bytes 393224 | tf_op jit(solution)/shard_map/ppermute | solution.py:185
  10.8 2.5 %collective-permute-start.5 = (bf16[8,8192]{1,0:T(8,128)(2,1)S(1)}, bf16[8,8192]{1,0:T(8,128)(2,1)S(1)}, u32[]{:S(2)}, u32[]{:S(2)}) collective-permute-start(bf16[8,8192]{1,0:T(8,128)(2,1)S(1)} %attend.1.rest_0_), channel_id=1, source_target_pairs={{0,6},{1,7},{2,4},{3,5},{4,2},{5,3},{6,0},{7,1},{8,14},{9,15},{10,... | collective-permute-start | bytes 393224 | tf_op jit(solution)/shard_map/ppermute | solution.py:185
  13.3 0.5 collective-permute-start.3
  13.8 0.0 collective-permute-start.1
  13.8 0.5 %collective-permute-start = (bf16[8,8192]{1,0:T(8,128)(2,1)S(1)}, bf16[8,8192]{1,0:T(8,128)(2,1)S(1)}, u32[]{:S(2)}, u32[]{:S(2)}) collective-permute-start(bf16[8,8192]{1,0:T(8,128)(2,1)S(1)} %attend.1.rest_0_), channel_id=1, source_target_pairs={{0,2},{1,3},{2,0},{3,1},{4,6},{5,7},{6,4},{7,5},{8,10},{9,11},{10,... | collective-permute-start | bytes 393224 | tf_op jit(solution)/shard_map/ppermute | solution.py:185
  14.3 2.9 %collective-permute-done.7.rest_8_ = bf16[8,8192]{1,0:T(8,128)(2,1)S(1)} collective-permute-done((bf16[8,8192]{1,0:T(8,128)(2,1)S(1)}, bf16[8,8192]{1,0:T(8,128)(2,1)S(1)}, u32[]{:S(2)}, u32[]{:S(2)}) %collective-permute-start.7) | collective-permute-done | bytes 131104 | tf_op jit(solution)/shard_map/ppermute | solution.py:185
  17.2 1.6 %collective-permute-start.13 = (bf16[8,8192]{1,0:T(8,128)(2,1)S(1)}, bf16[8,8192]{1,0:T(8,128)(2,1)S(1)}, u32[]{:S(2)}, u32[]{:S(2)}) collective-permute-start(bf16[8,8192]{1,0:T(8,128)(2,1)S(1)} %collective-permute-done.7.rest_8_), channel_id=1, source_target_pairs={{0,6},{1,7},{2,4},{3,5},{4,2},{5,3},{6,0},{7,1},{8,14},{9,15},{10,... | collective-permute-start | bytes 393224 | tf_op jit(solution)/shard_map/ppermute | solution.py:185
  18.8 1.0 %collective-permute-done.5.rest_6_ = bf16[8,8192]{1,0:T(8,128)(2,1)S(1)} collective-permute-done((bf16[8,8192]{1,0:T(8,128)(2,1)S(1)}, bf16[8,8192]{1,0:T(8,128)(2,1)S(1)}, u32[]{:S(2)}, u32[]{:S(2)}) %collective-permute-start.5) | collective-permute-done | bytes 131104 | tf_op jit(solution)/shard_map/ppermute | solution.py:185
  19.9 1.1 %collective-permute-start.11 = (bf16[8,8192]{1,0:T(8,128)(2,1)S(1)}, bf16[8,8192]{1,0:T(8,128)(2,1)S(1)}, u32[]{:S(2)}, u32[]{:S(2)}) collective-permute-start(bf16[8,8192]{1,0:T(8,128)(2,1)S(1)} %collective-permute-done.7.rest_8_), channel_id=1, source_target_pairs={{0,4},{1,5},{2,6},{3,7},{4,0},{5,1},{6,2},{7,3},{8,12},{9,13},{10,... | collective-permute-start | bytes 393224 | tf_op jit(solution)/shard_map/ppermute | solution.py:185
  21.0 1.2 %collective-permute-done.3.rest_4_ = bf16[8,8192]{1,0:T(8,128)(2,1)S(1)} collective-permute-done((bf16[8,8192]{1,0:T(8,128)(2,1)S(1)}, bf16[8,8192]{1,0:T(8,128)(2,1)S(1)}, u32[]{:S(2)}, u32[]{:S(2)}) %collective-permute-start.3) | collective-permute-done | bytes 131104 | tf_op jit(solution)/shard_map/ppermute | solution.py:185
  22.2 0.9 %collective-permute-start.9 = (bf16[8,8192]{1,0:T(8,128)(2,1)S(1)}, bf16[8,8192]{1,0:T(8,128)(2,1)S(1)}, u32[]{:S(2)}, u32[]{:S(2)}) collective-permute-start(bf16[8,8192]{1,0:T(8,128)(2,1)S(1)} %collective-permute-done.7.rest_8_), channel_id=1, source_target_pairs={{0,2},{1,3},{2,0},{3,1},{4,6},{5,7},{6,4},{7,5},{8,10},{9,11},{10,... | collective-permute-start | bytes 393224 | tf_op jit(solution)/shard_map/ppermute | solution.py:185
  23.1 0.0 collective-permute-done.1.rest_1_
  23.1 0.0 collective-permute-start.8
  23.1 0.0 collective-permute-done.after.rest_2_
  23.1 0.5 %collective-permute-start.6 = (bf16[8,8192]{1,0:T(8,128)(2,1)S(1)}, bf16[8,8192]{1,0:T(8,128)(2,1)S(1)}, u32[]{:S(2)}, u32[]{:S(2)}) collective-permute-start(bf16[8,8192]{1,0:T(8,128)(2,1)S(1)} %collective-permute-done.5.rest_6_), channel_id=1, source_target_pairs={{0,1},{1,0},{2,3},{3,2},{4,5},{5,4},{6,7},{7,6},{8,9},{9,8},{10,11... | collective-permute-start | bytes 393224 | tf_op jit(solution)/shard_map/ppermute | solution.py:185
  23.6 1.7 %collective-permute-done.13.rest_14_ = bf16[8,8192]{1,0:T(8,128)(2,1)S(1)} collective-permute-done((bf16[8,8192]{1,0:T(8,128)(2,1)S(1)}, bf16[8,8192]{1,0:T(8,128)(2,1)S(1)}, u32[]{:S(2)}, u32[]{:S(2)}) %collective-permute-start.13) | collective-permute-done | bytes 131104 | tf_op jit(solution)/shard_map/ppermute | solution.py:185
  25.4 0.0 collective-permute-start.4
  25.4 1.4 %collective-permute-done.11.rest_12_ = bf16[8,8192]{1,0:T(8,128)(2,1)S(1)} collective-permute-done((bf16[8,8192]{1,0:T(8,128)(2,1)S(1)}, bf16[8,8192]{1,0:T(8,128)(2,1)S(1)}, u32[]{:S(2)}, u32[]{:S(2)}) %collective-permute-start.11) | collective-permute-done | bytes 131104 | tf_op jit(solution)/shard_map/ppermute | solution.py:185
  26.8 0.4 collective-permute-done.9.rest_10_
  27.1 0.2 collective-permute-start.14
  27.3 0.4 collective-permute-start.12
  27.7 0.2 collective-permute-start.10
  27.8 2.2 %stage.1 = (bf16[8192,128]{1,0:T(8,128)(2,1)S(1)}, bf16[128,8192]{1,0:T(8,128)(2,1)S(1)}) custom-call(bf16[8,8192]{1,0:T(8,128)(2,1)S(1)} %collective-permute-done.after.rest_2_, bf16[1,8192,128]{2,1,0:T(8,128)(2,1)} %d_hbm.1, bf16[1,8192,128]{2,1,0:T(8,128)(2,1)} %u_hbm.1), custom_call_target="tpu_custom_call" | custom-call | flops 40000000000 | bytes 8388608 | tf_op jit(solution)/shard_map/stage/pallas_call | solution.py:222
  30.0 0.0 collective-permute-done.2.rest_3_
  30.1 2.6 %delta.1 = (bf16[16,16,512]{2,1,0:T(8,128)(2,1)}, bf16[128,8192]{1,0:T(8,128)(2,1)S(1)}) custom-call(s32[12]{0:T(128)} %count_ref.3, s32[12]{0:T(128)} %rank_ref.3, s32[12]{0:T(128)} %owner_ref.3, bf16[8192,128]{1,0:T(8,128)(2,1)S(1)} %get-tuple-element.9.d_ref, bf16[128,8192]{1,0:T(8,128)(2,1)S(1)} %get-tuple-element.10.ut_ref, ...), custom_call_target="tpu_custom_call" | custom-call | flops 301989888 | bytes 8650752 | tf_op jit(solution)/shard_map/delta/pallas_call | solution.py:280
  32.7 5.0 %all-to-all-start = ((bf16[16,16,512]{2,1,0:T(8,128)(2,1)}), bf16[16,16,512]{2,1,0:T(8,128)(2,1)S(1)}, u32[]{:S(2)}, u32[]{:S(2)}) async-start(bf16[16,16,512]{2,1,0:T(8,128)(2,1)} %get-tuple-element.12), calls=%async_computation | async-start | bytes 524288 | tf_op jit(solution)/shard_map/all_to_all | solution.py:397
  37.7 0.0 copy-start
  37.7 3.4 %copy-done = bf16[8192,512]{1,0:T(8,128)(2,1)S(1)} copy-done((bf16[8192,512]{1,0:T(8,128)(2,1)S(1)}, bf16[8192,512]{1,0:T(8,128)(2,1)}, u32[]{:S(2)}) %copy-start) | copy-done | bytes 8388632
  41.0 1.2 %base.1.base_ref = f32[128,512]{1,0:T(8,128)S(1)} custom-call(bf16[128,8192]{1,0:T(8,128)(2,1)S(1)} %get-tuple-element.11.a_ref, bf16[8192,512]{1,0:T(8,128)(2,1)S(1)} %copy-done), custom_call_target="tpu_custom_call" | custom-call | flops 1073741824 | bytes 10747904 | tf_op jit(solution)/shard_map/base/pallas_call | solution.py:312
  42.3 5.4 %all-to-all-done.delta_ref = bf16[16,16,512]{2,1,0:T(8,128)(2,1)S(1)} async-done(((bf16[16,16,512]{2,1,0:T(8,128)(2,1)}), bf16[16,16,512]{2,1,0:T(8,128)(2,1)S(1)}, u32[]{:S(2)}, u32[]{:S(2)}) %all-to-all-start) | async-done | bytes 262176 | tf_op jit(solution)/shard_map/all_to_all | solution.py:397
  47.7 1.7 %join.1 = bf16[2,64,512]{2,1,0:T(8,128)(2,1)} custom-call(s32[12]{0:T(128)} %count_ref.3, s32[12]{0:T(128)} %rank_ref.3, s32[12]{0:T(128)} %owner_ref.3, f32[128,512]{1,0:T(8,128)S(1)} %base.1.base_ref, bf16[16,16,512]{2,1,0:T(8,128)(2,1)S(1)} %all-to-all-done.delta_ref), custom_call_target="tpu_custom_call" | custom-call | tf_op jit(solution)/shard_map/join/pallas_call | solution.py:366
  (7 shorter events, 0.0 us)
Async XLA Ops:
  6.7 10.5 %collective-permute-start.7 = (bf16[8,8192]{1,0:T(8,128)(2,1)S(1)}, bf16[8,8192]{1,0:T(8,128)(2,1)S(1)}, u32[]{:S(2)}, u32[]{:S(2)}) collective-permute-start(bf16[8,8192]{1,0:T(8,128)(2,1)S(1)} %attend.1.rest_0_), channel_id=1, source_target_pairs={{0,8},{1,9},{2,10},{3,11},{4,12},{5,13},{6,14},{7,15},{8,0},{9,1},... | collective-permute-start | bytes 393224 | tf_op jit(solution)/shard_map/ppermute | solution.py:185
  10.8 9.1 %collective-permute-start.5 = (bf16[8,8192]{1,0:T(8,128)(2,1)S(1)}, bf16[8,8192]{1,0:T(8,128)(2,1)S(1)}, u32[]{:S(2)}, u32[]{:S(2)}) collective-permute-start(bf16[8,8192]{1,0:T(8,128)(2,1)S(1)} %attend.1.rest_0_), channel_id=1, source_target_pairs={{0,6},{1,7},{2,4},{3,5},{4,2},{5,3},{6,0},{7,1},{8,14},{9,15},{10,... | collective-permute-start | bytes 393224 | tf_op jit(solution)/shard_map/ppermute | solution.py:185
  13.3 8.8 %collective-permute-start.3 = (bf16[8,8192]{1,0:T(8,128)(2,1)S(1)}, bf16[8,8192]{1,0:T(8,128)(2,1)S(1)}, u32[]{:S(2)}, u32[]{:S(2)}) collective-permute-start(bf16[8,8192]{1,0:T(8,128)(2,1)S(1)} %attend.1.rest_0_), channel_id=1, source_target_pairs={{0,4},{1,5},{2,6},{3,7},{4,0},{5,1},{6,2},{7,3},{8,12},{9,13},{10,... | collective-permute-start | bytes 393224 | tf_op jit(solution)/shard_map/ppermute | solution.py:185
  13.8 9.3 %collective-permute-start.1 = (bf16[8,8192]{1,0:T(8,128)(2,1)S(1)}, bf16[8,8192]{1,0:T(8,128)(2,1)S(1)}, u32[]{:S(2)}, u32[]{:S(2)}) collective-permute-start(bf16[8,8192]{1,0:T(8,128)(2,1)S(1)} %attend.1.rest_0_), channel_id=1, source_target_pairs={{0,1},{1,0},{2,3},{3,2},{4,5},{5,4},{6,7},{7,6},{8,9},{9,8},{10,11... | collective-permute-start | bytes 393224 | tf_op jit(solution)/shard_map/ppermute | solution.py:185
  13.8 9.3 %collective-permute-start = (bf16[8,8192]{1,0:T(8,128)(2,1)S(1)}, bf16[8,8192]{1,0:T(8,128)(2,1)S(1)}, u32[]{:S(2)}, u32[]{:S(2)}) collective-permute-start(bf16[8,8192]{1,0:T(8,128)(2,1)S(1)} %attend.1.rest_0_), channel_id=1, source_target_pairs={{0,2},{1,3},{2,0},{3,1},{4,6},{5,7},{6,4},{7,5},{8,10},{9,11},{10,... | collective-permute-start | bytes 393224 | tf_op jit(solution)/shard_map/ppermute | solution.py:185
  17.2 8.2 %collective-permute-start.13 = (bf16[8,8192]{1,0:T(8,128)(2,1)S(1)}, bf16[8,8192]{1,0:T(8,128)(2,1)S(1)}, u32[]{:S(2)}, u32[]{:S(2)}) collective-permute-start(bf16[8,8192]{1,0:T(8,128)(2,1)S(1)} %collective-permute-done.7.rest_8_), channel_id=1, source_target_pairs={{0,6},{1,7},{2,4},{3,5},{4,2},{5,3},{6,0},{7,1},{8,14},{9,15},{10,... | collective-permute-start | bytes 393224 | tf_op jit(solution)/shard_map/ppermute | solution.py:185
  19.9 6.9 %collective-permute-start.11 = (bf16[8,8192]{1,0:T(8,128)(2,1)S(1)}, bf16[8,8192]{1,0:T(8,128)(2,1)S(1)}, u32[]{:S(2)}, u32[]{:S(2)}) collective-permute-start(bf16[8,8192]{1,0:T(8,128)(2,1)S(1)} %collective-permute-done.7.rest_8_), channel_id=1, source_target_pairs={{0,4},{1,5},{2,6},{3,7},{4,0},{5,1},{6,2},{7,3},{8,12},{9,13},{10,... | collective-permute-start | bytes 393224 | tf_op jit(solution)/shard_map/ppermute | solution.py:185
  22.2 5.0 %collective-permute-start.9 = (bf16[8,8192]{1,0:T(8,128)(2,1)S(1)}, bf16[8,8192]{1,0:T(8,128)(2,1)S(1)}, u32[]{:S(2)}, u32[]{:S(2)}) collective-permute-start(bf16[8,8192]{1,0:T(8,128)(2,1)S(1)} %collective-permute-done.7.rest_8_), channel_id=1, source_target_pairs={{0,2},{1,3},{2,0},{3,1},{4,6},{5,7},{6,4},{7,5},{8,10},{9,11},{10,... | collective-permute-start | bytes 393224 | tf_op jit(solution)/shard_map/ppermute | solution.py:185
  23.1 4.2 %collective-permute-start.8 = (bf16[8,8192]{1,0:T(8,128)(2,1)S(1)}, bf16[8,8192]{1,0:T(8,128)(2,1)S(1)}, u32[]{:S(2)}, u32[]{:S(2)}) collective-permute-start(bf16[8,8192]{1,0:T(8,128)(2,1)S(1)} %collective-permute-done.7.rest_8_), channel_id=1, source_target_pairs={{0,1},{1,0},{2,3},{3,2},{4,5},{5,4},{6,7},{7,6},{8,9},{9,8},{10,11... | collective-permute-start | bytes 393224 | tf_op jit(solution)/shard_map/ppermute | solution.py:185
  23.1 4.5 %collective-permute-start.6 = (bf16[8,8192]{1,0:T(8,128)(2,1)S(1)}, bf16[8,8192]{1,0:T(8,128)(2,1)S(1)}, u32[]{:S(2)}, u32[]{:S(2)}) collective-permute-start(bf16[8,8192]{1,0:T(8,128)(2,1)S(1)} %collective-permute-done.5.rest_6_), channel_id=1, source_target_pairs={{0,1},{1,0},{2,3},{3,2},{4,5},{5,4},{6,7},{7,6},{8,9},{9,8},{10,11... | collective-permute-start | bytes 393224 | tf_op jit(solution)/shard_map/ppermute | solution.py:185
  25.4 4.7 %collective-permute-start.4 = (bf16[8,8192]{1,0:T(8,128)(2,1)S(1)}, bf16[8,8192]{1,0:T(8,128)(2,1)S(1)}, u32[]{:S(2)}, u32[]{:S(2)}) collective-permute-start(bf16[8,8192]{1,0:T(8,128)(2,1)S(1)} %collective-permute-done.3.rest_4_), channel_id=1, source_target_pairs={{0,1},{1,0},{2,3},{3,2},{4,5},{5,4},{6,7},{7,6},{8,9},{9,8},{10,11... | collective-permute-start | bytes 393224 | tf_op jit(solution)/shard_map/ppermute | solution.py:185
  26.8 3.3 %collective-permute-start.2 = (bf16[8,8192]{1,0:T(8,128)(2,1)S(1)}, bf16[8,8192]{1,0:T(8,128)(2,1)S(1)}, u32[]{:S(2)}, u32[]{:S(2)}) collective-permute-start(bf16[8,8192]{1,0:T(8,128)(2,1)S(1)} %collective-permute-done.after.rest_2_), channel_id=1, source_target_pairs={{0,1},{1,0},{2,3},{3,2},{4,5},{5,4},{6,7},{7,6},{8,9},{9,8},{10,11... | collective-permute-start | bytes 393224 | tf_op jit(solution)/shard_map/ppermute | solution.py:185
  27.1 2.9 %collective-permute-start.14 = (bf16[8,8192]{1,0:T(8,128)(2,1)S(1)}, bf16[8,8192]{1,0:T(8,128)(2,1)S(1)}, u32[]{:S(2)}, u32[]{:S(2)}) collective-permute-start(bf16[8,8192]{1,0:T(8,128)(2,1)S(1)} %collective-permute-done.13.rest_14_), channel_id=1, source_target_pairs={{0,1},{1,0},{2,3},{3,2},{4,5},{5,4},{6,7},{7,6},{8,9},{9,8},{10,11... | collective-permute-start | bytes 393224 | tf_op jit(solution)/shard_map/ppermute | solution.py:185
  27.3 2.8 %collective-permute-start.12 = (bf16[8,8192]{1,0:T(8,128)(2,1)S(1)}, bf16[8,8192]{1,0:T(8,128)(2,1)S(1)}, u32[]{:S(2)}, u32[]{:S(2)}) collective-permute-start(bf16[8,8192]{1,0:T(8,128)(2,1)S(1)} %collective-permute-done.11.rest_12_), channel_id=1, source_target_pairs={{0,1},{1,0},{2,3},{3,2},{4,5},{5,4},{6,7},{7,6},{8,9},{9,8},{10,11... | collective-permute-start | bytes 393224 | tf_op jit(solution)/shard_map/ppermute | solution.py:185
  27.7 2.4 %collective-permute-start.10 = (bf16[8,8192]{1,0:T(8,128)(2,1)S(1)}, bf16[8,8192]{1,0:T(8,128)(2,1)S(1)}, u32[]{:S(2)}, u32[]{:S(2)}) collective-permute-start(bf16[8,8192]{1,0:T(8,128)(2,1)S(1)} %collective-permute-done.9.rest_10_), channel_id=1, source_target_pairs={{0,1},{1,0},{2,3},{3,2},{4,5},{5,4},{6,7},{7,6},{8,9},{9,8},{10,11... | collective-permute-start | bytes 393224 | tf_op jit(solution)/shard_map/ppermute | solution.py:185
  32.7 15.0 %all-to-all-start = ((bf16[16,16,512]{2,1,0:T(8,128)(2,1)}), bf16[16,16,512]{2,1,0:T(8,128)(2,1)S(1)}, u32[]{:S(2)}, u32[]{:S(2)}) async-start(bf16[16,16,512]{2,1,0:T(8,128)(2,1)} %get-tuple-element.12), calls=%async_computation | async-start | bytes 524288 | tf_op jit(solution)/shard_map/all_to_all | solution.py:397
  37.7 3.4 %copy-start = (bf16[8192,512]{1,0:T(8,128)(2,1)S(1)}, bf16[8192,512]{1,0:T(8,128)(2,1)}, u32[]{:S(2)}) copy-start(bf16[8192,512]{1,0:T(8,128)(2,1)} %w_ref.1) | copy-start | bytes 25165828

commit v6 on v5

v6 whole, which is shorter than its diff:
```python
import functools

import jax
import jax.numpy as jnp
from jax import lax
from jax.experimental import pallas as pl
from jax.experimental.pallas import tpu as pltpu
from jax.sharding import PartitionSpec as P

HQ = 64
KVH = 8
HD = 128
GROUP = HQ // KVH
MOST = 8
RING = 8
F32 = jnp.float32
BF16 = jnp.bfloat16
NT = (((1,), (1,)), ((), ()))


def in_hbm(*arrays):
    return [pltpu.with_memory_space_constraint(a, pltpu.HBM) for a in arrays]


def iota(shape, dim):
    return lax.broadcasted_iota(jnp.int32, shape, dim)


def one_hot(mask):
    return mask.astype(F32).astype(BF16)


def dot(a, b):
    return jnp.dot(a, b, preferred_element_type=F32)


def dot_nt(a, b):
    return lax.dot_general(a, b, NT, preferred_element_type=F32)


def attend_kernel(
    len_hbm, q_hbm, nk_hbm, nv_hbm, k_hbm, v_hbm, d_hbm, u_hbm,
    out_ref, d_ref, keep_ref, give_ref,
    len_ref, q_ref, nk_ref, nv_ref, k_ref, v_ref, qs, nks, nvs, raw, mixed,
    small_sems, sems, store_sems,
):
    steps, rows, width = q_ref.shape
    cache = k_ref.shape[1]
    both = steps * rows
    pack = steps * GROUP
    cuts = sems.shape[2]
    core = lax.axis_index("tensor") % 2
    chips = store_sems.shape[1]
    cols = keep_ref.shape[0] // chips

    small = [
        pltpu.make_async_copy(src, dst, small_sems.at[i])
        for i, (src, dst) in enumerate(
            ((q_hbm, q_ref), (len_hbm, len_ref), (nk_hbm, nk_ref), (nv_hbm, nv_ref))
        )
    ]
    pieces = [pl.ds(i * (cache // cuts), cache // cuts) for i in range(cuts)]
    keys, values = [
        [
            [
                pltpu.make_async_copy(src.at[r, at], dst.at[r, at], sems.at[r, j, i])
                for i, at in enumerate(pieces)
            ]
            for r in range(rows)
        ]
        for j, (src, dst) in enumerate(((k_hbm, k_ref), (v_hbm, v_ref)))
    ]
    deep = d_ref.shape[0] // chips
    store = [
        pltpu.make_async_copy(
            d_hbm.at[0, pl.ds(i * deep, deep)], d_ref.at[pl.ds(i * deep, deep)], store_sems.at[0, i]
        )
        for i in range(chips)
    ]
    for j, (side, dst) in enumerate(((core, keep_ref), (1 - core, give_ref))):
        for i in range(chips):
            at = pl.multiple_of((2 * i + side) * cols, cols)
            store.append(
                pltpu.make_async_copy(
                    u_hbm.at[0, pl.ds(at, cols)],
                    dst.at[pl.ds(i * cols, cols)],
                    store_sems.at[1 + j, i],
                )
            )
    queue = [keys[0], values[0], keys[1]]
    for r in range(rows):
        queue += [values[r + 1]] if r + 1 < rows else [store]
        queue += [keys[r + 2]] if r + 2 < rows else []
    for copy in small + queue[0] + queue[1] + queue[2]:
        copy.start()
    queue = queue[3:]
    for copy in small:
        copy.wait()

    flat = jnp.concatenate([q_ref[t].astype(F32) for t in range(steps)], axis=0)
    blank = jnp.zeros((pack, HD), F32)
    for k in range(KVH):
        group = jnp.stack(
            [flat[:, (k * GROUP + g) * HD : (k * GROUP + g + 1) * HD] for g in range(GROUP)]
        )
        turned = jnp.swapaxes(group, 0, 1)
        for r in range(rows):
            mine = jnp.concatenate([turned[t * rows + r] for t in range(steps)], axis=0)
            sides = [mine, blank] if k % 2 == 0 else [blank, mine]
            qs[r, k * pack : (k + 1) * pack, :] = jnp.concatenate(sides, axis=1).astype(BF16)
    for src, dst in ((nk_ref, nks), (nv_ref, nvs)):
        fresh = [src[t].astype(F32) for t in range(steps)]
        fresh.append(jnp.zeros((16 - both, src.shape[2]), F32))
        dst[...] = jnp.concatenate(fresh, axis=0).astype(BF16)

    scale = HD ** (-0.5)
    pairs = [
        (slice(k * pack, (k + 2) * pack), slice(k * HD, (k + 2) * HD)) for k in range(0, KVH, 2)
    ]
    for turn in range(rows + 1):
        if turn < rows:
            for copy in keys[turn]:
                copy.wait()
        if turn > 0:
            for copy in values[turn - 1]:
                copy.wait()
        for copies in queue[2 * turn : 2 * turn + 2]:
            for copy in copies:
                copy.start()
        if turn < rows:
            for own, cols_k in pairs:
                raw[turn % 2, own, :cache] = dot_nt(qs[turn, own, :], k_ref[turn, :, cols_k])
        if turn == 0:
            continue
        r = turn - 1
        fresh = jnp.concatenate(
            [dot_nt(qs[r, own, :], nks[:, cols_k]) for own, cols_k in pairs], axis=0
        )
        slot = iota(fresh.shape, 1)
        step = (iota(fresh.shape, 0) // GROUP) % steps
        seen = (slot < both) & (slot % rows == r) & (slot // rows <= step)
        fresh = jnp.where(seen, fresh * scale, -jnp.inf)
        older = raw[r % 2]
        older = jnp.where(iota(older.shape, 1) < len_ref[r], older * scale, -jnp.inf)
        top = jnp.maximum(
            jnp.max(older, axis=1, keepdims=True), jnp.max(fresh, axis=1, keepdims=True)
        )
        e_older = jnp.exp(older - top)
        e_fresh = jnp.exp(fresh - top)
        total = jnp.sum(e_older, axis=1, keepdims=True) + jnp.sum(e_fresh, axis=1, keepdims=True)
        inverse = 1.0 / total
        p_older = (e_older * inverse).astype(BF16)
        p_fresh = (e_fresh * inverse).astype(BF16)
        for k, (own, cols_k) in zip(range(0, KVH, 2), pairs):
            pair = dot(p_older[own], v_ref[r, :, cols_k]) + dot(p_fresh[own], nvs[:, cols_k])
            mixed[r, k] = pair[:pack, :HD]
            mixed[r, k + 1] = pair[pack:, HD:]

    for k in range(KVH):
        turned = jnp.stack(
            [
                mixed[r, k, t * GROUP : (t + 1) * GROUP, :]
                for t in range(steps)
                for r in range(rows)
            ]
        )
        heads = jnp.swapaxes(turned, 0, 1)
        for g in range(GROUP):
            at = (k * GROUP + g) * HD
            out_ref[:, at : at + HD] = heads[g].astype(BF16)
    for copy in store:
        copy.wait()


def attend(
    queries, new_keys, new_values, cache_keys, cache_values, kv_len, store_down, store_up, parts
):
    steps, rows, width = queries.shape
    cache, kv_width = cache_keys.shape[1:]
    pack = steps * GROUP
    rank_w = store_down.shape[2]
    vmem = pl.BlockSpec(memory_space=pltpu.VMEM)
    return pl.pallas_call(
        attend_kernel,
        out_shape=(
            jax.ShapeDtypeStruct((steps * rows, width), BF16),
            jax.ShapeDtypeStruct((width, rank_w), BF16),
            jax.ShapeDtypeStruct((width // 2, rank_w), BF16),
            jax.ShapeDtypeStruct((width // 2, rank_w), BF16),
        ),
        in_specs=[pl.BlockSpec(memory_space=pl.ANY)] * 8,
        out_specs=(vmem,) * 4,
        scratch_shapes=[
            pltpu.SMEM(kv_len.shape, jnp.int32),
            pltpu.VMEM(queries.shape, BF16),
            pltpu.VMEM(new_keys.shape, BF16),
            pltpu.VMEM(new_values.shape, BF16),
            pltpu.VMEM(cache_keys.shape, BF16),
            pltpu.VMEM(cache_values.shape, BF16),
            pltpu.VMEM((rows, KVH * pack, 2 * HD), BF16),
            pltpu.VMEM((16, kv_width), BF16),
            pltpu.VMEM((16, kv_width), BF16),
            pltpu.VMEM((2, KVH * pack, cache), F32),
            pltpu.VMEM((rows, KVH, pack, HD), F32),
            pltpu.SemaphoreType.DMA((4,)),
            pltpu.SemaphoreType.DMA((rows, 2, 2)),
            pltpu.SemaphoreType.DMA((3, parts // 2)),
        ],
        compiler_params=pltpu.CompilerParams(vmem_limit_bytes=32 * 2**20),
        cost_estimate=pl.CostEstimate(
            flops=4 * rows * steps * HQ * cache * HD,
            bytes_accessed=4 * rows * cache * kv_width,
            transcendentals=rows * steps * HQ * cache,
        ),
        name="attend",
    )(
        *in_hbm(
            kv_len,
            queries,
            new_keys,
            new_values,
            cache_keys,
            cache_values,
            store_down,
            store_up,
        )
    )


def sender(slot, chip, chips):
    return chip ^ slot if chips == RING else slot


def row_place(index, me, chips, steps, rows):
    both = steps * rows
    block = index // both
    device = sender(block // 2, me // 2, chips) * 2 + (me + block) % 2
    return device * rows + index % rows, (index % both) // rows


def swap(x, bits, parts):
    return lax.ppermute(x, "tensor", [(i, i ^ bits) for i in range(parts)])


def stage_kernel(half, after, w_hbm, w_ref, sems):
    deep = w_ref.shape[0] // sems.shape[0]
    copies = []
    for i in range(sems.shape[0]):
        at = pl.ds(half * w_ref.shape[0] + i * deep, deep)
        copies.append(pltpu.make_async_copy(w_hbm.at[at], w_ref.at[pl.ds(i * deep, deep)], sems.at[i]))
        copies[-1].start()
    for copy in copies:
        copy.wait()


def stage(after, out_weight, half):
    width, cols = out_weight.shape
    return pl.pallas_call(
        functools.partial(stage_kernel, half),
        out_shape=jax.ShapeDtypeStruct((width // 2, cols), BF16),
        in_specs=[pl.BlockSpec(memory_space=pl.ANY)] * 2,
        out_specs=pl.BlockSpec(memory_space=pltpu.VMEM),
        scratch_shapes=[pltpu.SemaphoreType.DMA((8,))],
        compiler_params=pltpu.CompilerParams(vmem_limit_bytes=8 * 2**20),
        cost_estimate=pl.CostEstimate(
            flops=2 * 10**10, bytes_accessed=2 * out_weight.size, transcendentals=0
        ),
        name="stage",
    )(after, *in_hbm(out_weight))


def gather(block, give, out_weight, parts):
    if parts // 2 != RING:
        whole = lax.all_gather(block, "tensor")
        core = lax.axis_index("tensor") % 2
        pairs = whole.reshape(parts // 2, 2, *block.shape)
        pairs = jnp.where(core == 0, pairs, pairs[:, ::-1])
        held = [pairs[i // 2, i % 2] for i in range(parts)]
        weights = [stage(block, out_weight, half) for half in range(2)]
        return held, weights, swap(give, 1, parts)
    core, y, near, far = 1, 2, 4, 8
    held = {0: block}
    held[far] = swap(block, far, parts)
    held[near] = swap(block, near, parts)
    held[y] = swap(block, y, parts)
    first = stage(block, out_weight, 0)
    held[near], held[y], first, give = lax.optimization_barrier(
        (held[near], held[y], first, give)
    )
    held[near | y] = swap(held[near], y, parts)
    other = swap(give, core, parts)
    second = stage(held[near], out_weight, 1)
    held[far], second = lax.optimization_barrier((held[far], second))
    held[far | y] = swap(held[far], y, parts)
    held[far | near | y] = swap(held[far], near | y, parts)
    held[far | near] = swap(held[far], near, parts)
    for slot in list(held):
        held[slot | core] = swap(held[slot], core, parts)
    return [held[slot] for slot in range(parts)], [first, second], other


def low_kernel(order, steps, rows, count_ref, rank_ref, owner_ref, d_ref, *rest):
    (*blocks, out_ref, rows_ref) = rest
    blocks = [blocks[order.index(i)] for i in range(len(blocks))]
    block = lax.axis_index("tensor")
    slots = out_ref.shape[0]
    parts = len(blocks)
    each, width = blocks[0].shape
    total = parts * each
    cuts = 8
    deep = width // cuts
    low = jnp.zeros((total, d_ref.shape[1]), F32)
    for i in range(cuts):
        at = slice(i * deep, (i + 1) * deep)
        piece = jnp.concatenate([b[:, at] for b in blocks], axis=0)
        rows_ref[:, at] = piece
        low = low + dot(piece, d_ref[at, :])
    start = jnp.int32(0)
    first = jnp.int32(0)
    amount = jnp.int32(0)
    for a in range(count_ref.shape[0]):
        owned = (owner_ref[a] <= block) & (block < owner_ref[a] + rank_ref[a])
        first = jnp.where(owned, start, first)
        amount = jnp.where(owned, count_ref[a], amount)
        start = start + count_ref[a]
    slot = iota((slots, total), 0)
    request, step = row_place(iota((slots, total), 1), block, parts // 2, steps, rows)
    nth = slot % MOST
    pick = (step == slot // MOST) & (request == first + nth) & (nth < amount)
    out_ref[...] = dot(one_hot(pick), low.astype(BF16)).astype(BF16)


def low_rows(blocks, down, tables, steps, rows):
    parts = len(blocks)
    each, width = blocks[0].shape
    slots = steps * MOST
    rank_w = down.shape[1]
    order = [i for i in range(parts) if i // 2 != 5] + [i for i in range(parts) if i // 2 == 5]
    vmem = pl.BlockSpec(memory_space=pltpu.VMEM)
    smem = pl.BlockSpec(memory_space=pltpu.SMEM)
    return pl.pallas_call(
        functools.partial(low_kernel, order, steps, rows),
        out_shape=(
            jax.ShapeDtypeStruct((slots, rank_w), BF16),
            jax.ShapeDtypeStruct((parts * each, width), BF16),
        ),
        in_specs=[smem] * 3 + [vmem] * (1 + parts),
        out_specs=(vmem, vmem),
        compiler_params=pltpu.CompilerParams(vmem_limit_bytes=24 * 2**20),
        cost_estimate=pl.CostEstimate(
            flops=2 * parts * each * width * rank_w,
            bytes_accessed=2 * width * (2 * parts * each + rank_w),
            transcendentals=0,
        ),
        name="low",
    )(*in_hbm(*tables), down, *[blocks[i] for i in order])


def delta_kernel(own_ref, other_ref, keep_ref, taken_ref, *outs):
    chips = len(outs)
    chip = lax.axis_index("tensor") // 2
    slots = own_ref.shape[0]
    cols = outs[0].shape[1]
    for k in range(chips):
        at = pl.ds(pl.multiple_of(sender(k, chip, chips) * cols, cols), cols)
        outs[k][:slots, :] = dot_nt(own_ref[...], keep_ref[at, :]).astype(BF16)
        outs[k][slots:, :] = dot_nt(other_ref[...], taken_ref[at, :]).astype(BF16)


def deltas(own, other, keep, taken, chips):
    slots, rank_w = own.shape
    cols = keep.shape[0] // chips
    vmem = pl.BlockSpec(memory_space=pltpu.VMEM)
    return pl.pallas_call(
        delta_kernel,
        out_shape=[jax.ShapeDtypeStruct((2 * slots, cols), BF16)] * chips,
        in_specs=[vmem] * 4,
        out_specs=[vmem] * chips,
        compiler_params=pltpu.CompilerParams(vmem_limit_bytes=16 * 2**20),
        cost_estimate=pl.CostEstimate(
            flops=4 * slots * rank_w * keep.shape[0],
            bytes_accessed=4 * keep.shape[0] * (rank_w + slots),
            transcendentals=0,
        ),
        name="delta",
    )(own, other, keep, taken)


def send(pieces, parts):
    chips = len(pieces)
    if chips != RING:
        groups = [list(range(core, parts, 2)) for core in range(2)]
        all_pieces = lax.all_to_all(
            jnp.stack(pieces), "tensor", 0, 0, axis_index_groups=groups, tiled=True
        )
        return [all_pieces[i] for i in range(chips)]
    got = {0: pieces[0]}
    for k in range(1, chips):
        got[k] = swap(pieces[k], 2 * k, parts)
    return [got[k] for k in range(chips)]


def base_kernel(a_ref, first_ref, second_ref, out_ref):
    half = first_ref.shape[0]
    cuts = 4
    deep = half // cuts
    for j, w_ref in enumerate((first_ref, second_ref)):
        for i in range(cuts):
            part = dot(
                a_ref[:, j * half + i * deep : j * half + (i + 1) * deep],
                w_ref[i * deep : (i + 1) * deep, :],
            )
            out_ref[...] = part if i + j == 0 else out_ref[...] + part


def base_part(gathered, weights):
    total, width = gathered.shape
    cols = weights[0].shape[1]
    vmem = pl.BlockSpec(memory_space=pltpu.VMEM)
    return pl.pallas_call(
        base_kernel,
        out_shape=jax.ShapeDtypeStruct((total, cols), F32),
        in_specs=[vmem] * 3,
        out_specs=vmem,
        compiler_params=pltpu.CompilerParams(vmem_limit_bytes=24 * 2**20),
        cost_estimate=pl.CostEstimate(
            flops=2 * total * width * cols,
            bytes_accessed=2 * width * (total + cols) + 4 * total * cols,
            transcendentals=0,
        ),
        name="base",
    )(gathered, *weights)


def join_kernel(order, rows, count_ref, rank_ref, owner_ref, base_ref, *rest):
    (*pieces, out_ref) = rest
    pieces = [pieces[order.index(i)] for i in range(len(pieces))]
    me = lax.axis_index("tensor")
    steps, requests, cols = out_ref.shape
    chips = len(pieces)
    slots = pieces[0].shape[0] // 2
    total = base_ref.shape[0]
    wide = chips * 2 * slots
    entry = iota((1, wide), 1)
    source = entry // slots
    block = sender(source // 2, me // 2, chips) * 2 + (me + source) % 2
    first = jnp.zeros((1, wide), jnp.int32)
    amount = jnp.zeros((1, wide), jnp.int32)
    start = jnp.int32(0)
    for a in range(count_ref.shape[0]):
        owned = (owner_ref[a] <= block) & (block < owner_ref[a] + rank_ref[a])
        first = jnp.where(owned, start, first)
        amount = jnp.where(owned, count_ref[a], amount)
        start = start + count_ref[a]
    nth = entry % MOST
    goal = jnp.where(nth < amount, first + nth, -1)
    goal_step = (entry % slots) // MOST
    request, step = row_place(iota((total, 1), 0), me, chips, steps, rows)
    place = one_hot((request == goal) & (step == goal_step))
    delta = dot(place, jnp.concatenate([piece[...] for piece in pieces], axis=0))
    result = (base_ref[...] + delta).astype(BF16)
    request, step = row_place(iota((total, total), 1), me, chips, steps, rows)
    order = one_hot(iota((total, total), 0) == step * requests + request)
    turned = dot(order, result).astype(BF16)
    for t in range(steps):
        out_ref[t] = turned[t * requests : (t + 1) * requests]


def join(base, pieces, tables, steps, rows):
    total, cols = base.shape
    chips = len(pieces)
    order = [0] + [*range(chips // 2, chips)] + [*range(1, chips // 2)]
    vmem = pl.BlockSpec(memory_space=pltpu.VMEM)
    smem = pl.BlockSpec(memory_space=pltpu.SMEM)
    return pl.pallas_call(
        functools.partial(join_kernel, order, rows),
        out_shape=jax.ShapeDtypeStruct((steps, total // steps, cols), BF16),
        in_specs=[smem] * 3 + [vmem] * (1 + len(pieces)),
        out_specs=vmem,
        compiler_params=pltpu.CompilerParams(vmem_limit_bytes=24 * 2**20),
        name="join",
    )(*in_hbm(*tables), base, *[pieces[i] for i in order])


def per_device(
    queries,
    new_keys,
    new_values,
    cache_keys,
    cache_values,
    kv_len,
    adapter_rows,
    adapter_rank,
    adapter_owner,
    out_weight,
    store_down,
    store_up,
):
    parts = lax.axis_size("tensor")
    steps, rows, width = queries.shape
    tables = (adapter_rows, adapter_rank, adapter_owner)
    attended, down, keep, give = attend(
        queries,
        new_keys,
        new_values,
        cache_keys,
        cache_values,
        kv_len,
        store_down,
        store_up,
        parts,
    )
    blocks, weights, taken = gather(attended, give, out_weight, parts)
    own, gathered = low_rows(blocks, down, tables, steps, rows)
    other = swap(own, 1, parts)
    base = base_part(gathered, weights)
    other, base = lax.optimization_barrier((other, base))
    pieces = send(deltas(own, other, keep, taken, parts // 2), parts)
    return join(base, pieces, tables, steps, rows)


def solution(mesh):
    in_specs = (
        P(None, ("groups", "tensor"), None),
        P(None, ("groups", "tensor"), None),
        P(None, ("groups", "tensor"), None),
        P(("groups", "tensor"), None, None),
        P(("groups", "tensor"), None, None),
        P(("groups", "tensor")),
        P("groups"),
        P(),
        P(),
        P(None, "tensor"),
        P("tensor", None, None),
        P("tensor", None, None),
    )
    out_specs = P(None, "groups", "tensor")
    return jax.shard_map(
        per_device, mesh=mesh, in_specs=in_specs, out_specs=out_specs, check_vma=False
    )
```

time: 49.7 us -> 52.7 us (1.060)
  starting transfers between devices: 17.4 us -> 24.4 us
  local copies, waits for them, and re-layouts: 3.38 us -> 0 us
  waiting for transfers between devices: 14.1 us -> 12.3 us
  Pallas kernels: 14.4 us -> 15.7 us
    ppermute x15 -> x24, starting transfers between devices: 12.4 us -> 24.4 us  [swap(): return lax.ppermute(x, 'tensor', [(i, i ^ bits) for i in range(parts)])]
    all_to_all x1 -> x0, waiting for transfers between devices: 5.41 us -> none  [per_device(): lax.all_to_all(send, 'tensor', split_axis=0, concat_axis=0, tiled=True)]
    all_to_all x1 -> x0, starting transfers between devices: 4.97 us -> none  [per_device(): lax.all_to_all(send, 'tensor', split_axis=0, concat_axis=0, tiled=True)]
    ppermute x15 -> x24, waiting for transfers between devices: 8.68 us -> 12.3 us  [swap(): return lax.ppermute(x, 'tensor', [(i, i ^ bits) for i in range(parts)])]
    unnamed x2 -> x0, local copies, waits for them, and re-layouts: 3.38 us -> none
    pallas_call x4 -> x6, Pallas kernels: 13.2 us -> 14.5 us  [the longest x1 6.15 us: attend(): pl.pallas_call(attend_kernel, out_shape=(jax.ShapeDtypeStruct((steps * ro...]
  transfers between devices with their start and end apart: 16 -> 24, of which waited for: 7 -> 7; matrix products, arithmetic and copies ran while one was open for 0% -> 0% of each run, Pallas kernels for 7% -> 14%
where the time goes in v6:
time: 52.7 us; the launch traced here: 52.5 us
  starting transfers between devices  24.4 us (46%)
  Pallas kernels  15.7 us (30%)
  waiting for transfers between devices  12.3 us (23%)
    ppermute x24, starting transfers between devices, swap(): return lax.ppermute(x, 'tensor', [(i, i ^ bits) for i in range(parts)])  24.4 us
    ppermute x24, waiting for transfers between devices, swap(): return lax.ppermute(x, 'tensor', [(i, i ^ bits) for i in range(parts)])  12.3 us
    pallas_call x1, Pallas kernels, attend(): pl.pallas_call(attend_kernel, out_shape=(jax.ShapeDtypeStruct((steps * ro...  6.15 us
    pallas_call x2, Pallas kernels, stage(): pl.pallas_call(functools.partial(stage_kernel, half), out_shape=jax.Shape...  4.43 us
    pallas_call x1, Pallas kernels, join(): pl.pallas_call(functools.partial(join_kernel, order, rows), out_shape=jax...  1.73 us
    pallas_call x1, Pallas kernels, low_rows(): pl.pallas_call(functools.partial(low_kernel, order, steps, rows), out_sha...  1.5 us
    pallas_call x1, Pallas kernels, base_part(): pl.pallas_call(base_kernel, out_shape=jax.ShapeDtypeStruct((total, cols),...  1.25 us
  transfers between devices with their start and end apart: 24, of which 7 were waited for; matrix products, arithmetic and copies ran while one was open for 0% of the time, Pallas kernels for 14%

profile of v6, /device:TPU:0, one launch (start us, length us, event | category | flops | bytes accessed | tf_op | source)
XLA Modules:
  0.0 52.5 jit_solution(17807652735321977507)
XLA Ops:
  0.0 6.2 %attend.1 = (bf16[8,8192]{1,0:T(8,128)(2,1)S(1)}, bf16[8192,128]{1,0:T(8,128)(2,1)S(1)}, bf16[4096,128]{1,0:T(8,128)(2,1)S(1)}, bf16[4096,128]{1,0:T(8,128)(2,1)S(1)}) custom-call(s32[4]{0:T(128)} %len_hbm.1, bf16[2,4,8192]{2,1,0:T(4,128)(2,1)} %q_hbm.1, bf16[2,4,1024]{2,1,0:T(4,128)(2,1)} %nk_hbm.1, bf16[2,4,1024]{2,1,0:T(4,128)(2,1)} %nv_hbm.1, ...), custom_call_target="tpu_custom_call" | custom-call | flops 134217728 | bytes 8388608 | tf_op jit(solution)/shard_map/attend/pallas_call | solution.py:183
  6.2 4.1 %collective-permute-start.7 = (bf16[8,8192]{1,0:T(8,128)(2,1)S(1)}, bf16[8,8192]{1,0:T(8,128)(2,1)S(1)}, u32[]{:S(2)}, u32[]{:S(2)}) collective-permute-start(bf16[8,8192]{1,0:T(8,128)(2,1)S(1)} %get-tuple-element.28.after.rest_0_), channel_id=1, source_target_pairs={{0,8},{1,9},{2,10},{3,11},{4,12},{5,13},{6,14},{7,15},{8,0},{9,1},... | collective-permute-start | bytes 393224 | tf_op jit(solution)/shard_map/ppermute | solution.py:242
  10.3 1.5 %collective-permute-start.2 = (bf16[8,8192]{1,0:T(8,128)(2,1)S(1)}, bf16[8,8192]{1,0:T(8,128)(2,1)S(1)}, u32[]{:S(2)}, u32[]{:S(2)}) collective-permute-start(bf16[8,8192]{1,0:T(8,128)(2,1)S(1)} %get-tuple-element.28.after.rest_0_), channel_id=1, source_target_pairs={{0,2},{1,3},{2,0},{3,1},{4,6},{5,7},{6,4},{7,5},{8,10},{9,11},{10,... | collective-permute-start | bytes 393224 | tf_op jit(solution)/shard_map/ppermute | solution.py:242
  11.8 1.6 %collective-permute-start.1 = (bf16[8,8192]{1,0:T(8,128)(2,1)S(1)}, bf16[8,8192]{1,0:T(8,128)(2,1)S(1)}, u32[]{:S(2)}, u32[]{:S(2)}) collective-permute-start(bf16[8,8192]{1,0:T(8,128)(2,1)S(1)} %get-tuple-element.28.after.rest_0_), channel_id=1, source_target_pairs={{0,4},{1,5},{2,6},{3,7},{4,0},{5,1},{6,2},{7,3},{8,12},{9,13},{10,... | collective-permute-start | bytes 393224 | tf_op jit(solution)/shard_map/ppermute | solution.py:242
  13.4 2.2 %stage.2.first_ref = bf16[4096,512]{1,0:T(8,128)(2,1)S(1)} custom-call(bf16[8,8192]{1,0:T(8,128)(2,1)S(1)} %get-tuple-element.28.after.rest_0_, bf16[8192,512]{1,0:T(8,128)(2,1)} %w_hbm.3), custom_call_target="tpu_custom_call" | custom-call | flops 20000000000 | bytes 8388608 | tf_op jit(solution)/shard_map/stage/pallas_call | solution.py:258
  15.6 2.5 %collective-permute-done.1.after.rest_4_ = bf16[8,8192]{1,0:T(8,128)(2,1)S(1)} collective-permute-done((bf16[8,8192]{1,0:T(8,128)(2,1)S(1)}, bf16[8,8192]{1,0:T(8,128)(2,1)S(1)}, u32[]{:S(2)}, u32[]{:S(2)}) %collective-permute-start.1) | collective-permute-done | bytes 131104 | tf_op jit(solution)/shard_map/ppermute | solution.py:242
  18.1 0.6 %collective-permute-start.5 = (bf16[8,8192]{1,0:T(8,128)(2,1)S(1)}, bf16[8,8192]{1,0:T(8,128)(2,1)S(1)}, u32[]{:S(2)}, u32[]{:S(2)}) collective-permute-start(bf16[8,8192]{1,0:T(8,128)(2,1)S(1)} %collective-permute-done.1.after.rest_4_), channel_id=1, source_target_pairs={{0,2},{1,3},{2,0},{3,1},{4,6},{5,7},{6,4},{7,5},{8,10},{9,11},{10,... | collective-permute-start | bytes 393224 | tf_op jit(solution)/shard_map/ppermute | solution.py:242
  18.7 0.5 collective-permute-start.3
  19.2 0.0 collective-permute-start.16
  19.2 2.2 %stage.3.second_ref = bf16[4096,512]{1,0:T(8,128)(2,1)S(1)} custom-call(bf16[8,8192]{1,0:T(8,128)(2,1)S(1)} %collective-permute-done.1.after.rest_4_, bf16[8192,512]{1,0:T(8,128)(2,1)} %w_hbm.3), custom_call_target="tpu_custom_call" | custom-call | flops 20000000000 | bytes 8388608 | tf_op jit(solution)/shard_map/stage/pallas_call | solution.py:258
  21.5 1.5 %collective-permute-start.13 = (bf16[8,8192]{1,0:T(8,128)(2,1)S(1)}, bf16[8,8192]{1,0:T(8,128)(2,1)S(1)}, u32[]{:S(2)}, u32[]{:S(2)}) collective-permute-start(bf16[8,8192]{1,0:T(8,128)(2,1)S(1)} %collective-permute-done.7.rest_8_), channel_id=1, source_target_pairs={{0,2},{1,3},{2,0},{3,1},{4,6},{5,7},{6,4},{7,5},{8,10},{9,11},{10,... | collective-permute-start | bytes 393224 | tf_op jit(solution)/shard_map/ppermute | solution.py:242
  23.0 1.2 %collective-permute-start.11 = (bf16[8,8192]{1,0:T(8,128)(2,1)S(1)}, bf16[8,8192]{1,0:T(8,128)(2,1)S(1)}, u32[]{:S(2)}, u32[]{:S(2)}) collective-permute-start(bf16[8,8192]{1,0:T(8,128)(2,1)S(1)} %collective-permute-done.7.rest_8_), channel_id=1, source_target_pairs={{0,6},{1,7},{2,4},{3,5},{4,2},{5,3},{6,0},{7,1},{8,14},{9,15},{10,... | collective-permute-start | bytes 393224 | tf_op jit(solution)/shard_map/ppermute | solution.py:242
  24.1 0.9 %collective-permute-start.9 = (bf16[8,8192]{1,0:T(8,128)(2,1)S(1)}, bf16[8,8192]{1,0:T(8,128)(2,1)S(1)}, u32[]{:S(2)}, u32[]{:S(2)}) collective-permute-start(bf16[8,8192]{1,0:T(8,128)(2,1)S(1)} %collective-permute-done.7.rest_8_), channel_id=1, source_target_pairs={{0,4},{1,5},{2,6},{3,7},{4,0},{5,1},{6,2},{7,3},{8,12},{9,13},{10,... | collective-permute-start | bytes 393224 | tf_op jit(solution)/shard_map/ppermute | solution.py:242
  25.0 5.2 %collective-permute-done.13.rest_14_ = bf16[8,8192]{1,0:T(8,128)(2,1)S(1)} collective-permute-done((bf16[8,8192]{1,0:T(8,128)(2,1)S(1)}, bf16[8,8192]{1,0:T(8,128)(2,1)S(1)}, u32[]{:S(2)}, u32[]{:S(2)}) %collective-permute-start.13) | collective-permute-done | bytes 131104 | tf_op jit(solution)/shard_map/ppermute | solution.py:242
  30.3 0.5 collective-permute-start.14
  30.8 0.7 %collective-permute-done.9.rest_10_ = bf16[8,8192]{1,0:T(8,128)(2,1)S(1)} collective-permute-done((bf16[8,8192]{1,0:T(8,128)(2,1)S(1)}, bf16[8,8192]{1,0:T(8,128)(2,1)S(1)}, u32[]{:S(2)}, u32[]{:S(2)}) %collective-permute-start.9) | collective-permute-done | bytes 131104 | tf_op jit(solution)/shard_map/ppermute | solution.py:242
  31.5 0.5 collective-permute-start.10
  32.0 0.8 %collective-permute-done.12.rest_13_ = bf16[8,8192]{1,0:T(8,128)(2,1)S(1)} collective-permute-done((bf16[8,8192]{1,0:T(8,128)(2,1)S(1)}, bf16[8,8192]{1,0:T(8,128)(2,1)S(1)}, u32[]{:S(2)}, u32[]{:S(2)}) %collective-permute-start.12) | collective-permute-done | bytes 131104 | tf_op jit(solution)/shard_map/ppermute | solution.py:242
  32.8 0.2 collective-permute-done.10.rest_11_
  33.0 1.5 %low.1 = (bf16[16,128]{1,0:T(8,128)(2,1)S(1)}, bf16[128,8192]{1,0:T(8,128)(2,1)S(1)}) custom-call(s32[12]{0:T(128)} %count_ref.3, s32[12]{0:T(128)} %rank_ref.3, s32[12]{0:T(128)} %owner_ref.3, bf16[8192,128]{1,0:T(8,128)(2,1)S(1)} %get-tuple-element.27.d_ref, bf16[8,8192]{1,0:T(8,128)(2,1)S(1)} %get-tuple-element.28.after.rest_0_, ...), custom_call_target="tpu_custom_call" | custom-call | flops 268435456 | bytes 6291456 | tf_op jit(solution)/shard_map/low/pallas_call | solution.py:341
  34.5 0.3 collective-permute-start.15
  34.9 1.2 %base.1.base_ref = f32[128,512]{1,0:T(8,128)S(1)} custom-call(bf16[128,8192]{1,0:T(8,128)(2,1)S(1)} %get-tuple-element.34.a_ref, bf16[4096,512]{1,0:T(8,128)(2,1)S(1)} %stage.2.first_ref, bf16[4096,512]{1,0:T(8,128)(2,1)S(1)} %stage.3.second_ref), custom_call_target="tpu_custom_call" | custom-call | flops 1073741824 | bytes 10747904 | tf_op jit(solution)/shard_map/base/pallas_call | solution.py:420
  36.1 0.7 %delta.1 = (bf16[32,512]{1,0:T(8,128)(2,1)S(1)}, bf16[32,512]{1,0:T(8,128)(2,1)S(1)}, bf16[32,512]{1,0:T(8,128)(2,1)S(1)}, bf16[32,512]{1,0:T(8,128)(2,1)S(1)}, ...) custom-call(bf16[16,128]{1,0:T(8,128)(2,1)S(1)} %get-tuple-element.3, ...), custom_call_target="tpu_custom_call" | custom-call | flops 33554432 | bytes 2359296 | tf_op jit(solution)/shard_map/delta/pallas_call | solution.py:374
  36.8 1.5 %collective-permute-start.17 = (bf16[32,512]{1,0:T(8,128)(2,1)S(1)}, bf16[32,512]{1,0:T(8,128)(2,1)S(1)}, u32[]{:S(2)}, u32[]{:S(2)}) collective-permute-start(bf16[32,512]{1,0:T(8,128)(2,1)S(1)} %get-tuple-element.42), channel_id=1, source_target_pairs={{0,8},{1,9},{2,10},{3,11},{4,12},{5,13},{6,14},{7,15},{8,0},{9,1},... | collective-permute-start | bytes 98312 | tf_op jit(solution)/shard_map/ppermute | solution.py:242
  38.3 2.3 %collective-permute-start.18 = (bf16[32,512]{1,0:T(8,128)(2,1)S(1)}, bf16[32,512]{1,0:T(8,128)(2,1)S(1)}, u32[]{:S(2)}, u32[]{:S(2)}) collective-permute-start(bf16[32,512]{1,0:T(8,128)(2,1)S(1)} %get-tuple-element.43), channel_id=1, source_target_pairs={{0,10},{1,11},{2,8},{3,9},{4,14},{5,15},{6,12},{7,13},{8,2},{9,3},... | collective-permute-start | bytes 98312 | tf_op jit(solution)/shard_map/ppermute | solution.py:242
  40.6 2.7 %collective-permute-start.19 = (bf16[32,512]{1,0:T(8,128)(2,1)S(1)}, bf16[32,512]{1,0:T(8,128)(2,1)S(1)}, u32[]{:S(2)}, u32[]{:S(2)}) collective-permute-start(bf16[32,512]{1,0:T(8,128)(2,1)S(1)} %get-tuple-element.44), channel_id=1, source_target_pairs={{0,12},{1,13},{2,14},{3,15},{4,8},{5,9},{6,10},{7,11},{8,4},{9,5},... | collective-permute-start | bytes 98312 | tf_op jit(solution)/shard_map/ppermute | solution.py:242
  43.3 1.2 %collective-permute-start.20 = (bf16[32,512]{1,0:T(8,128)(2,1)S(1)}, bf16[32,512]{1,0:T(8,128)(2,1)S(1)}, u32[]{:S(2)}, u32[]{:S(2)}) collective-permute-start(bf16[32,512]{1,0:T(8,128)(2,1)S(1)} %get-tuple-element.45), channel_id=1, source_target_pairs={{0,14},{1,15},{2,12},{3,13},{4,10},{5,11},{6,8},{7,9},{8,6},{9,7},... | collective-permute-start | bytes 98312 | tf_op jit(solution)/shard_map/ppermute | solution.py:242
  44.5 1.4 %collective-permute-start.21 = (bf16[32,512]{1,0:T(8,128)(2,1)S(1)}, bf16[32,512]{1,0:T(8,128)(2,1)S(1)}, u32[]{:S(2)}, u32[]{:S(2)}) collective-permute-start(bf16[32,512]{1,0:T(8,128)(2,1)S(1)} %get-tuple-element.46), channel_id=1, source_target_pairs={{0,2},{1,3},{2,0},{3,1},{4,6},{5,7},{6,4},{7,5},{8,10},{9,11},{10,... | collective-permute-start | bytes 98312 | tf_op jit(solution)/shard_map/ppermute | solution.py:242
  45.9 2.1 %collective-permute-start.23 = (bf16[32,512]{1,0:T(8,128)(2,1)S(1)}, bf16[32,512]{1,0:T(8,128)(2,1)S(1)}, u32[]{:S(2)}, u32[]{:S(2)}) collective-permute-start(bf16[32,512]{1,0:T(8,128)(2,1)S(1)} %get-tuple-element.48), channel_id=1, source_target_pairs={{0,6},{1,7},{2,4},{3,5},{4,2},{5,3},{6,0},{7,1},{8,14},{9,15},{10,... | collective-permute-start | bytes 98312 | tf_op jit(solution)/shard_map/ppermute | solution.py:242
  48.0 2.0 %collective-permute-done.20.rest_4_ = bf16[32,512]{1,0:T(8,128)(2,1)S(1)} collective-permute-done((bf16[32,512]{1,0:T(8,128)(2,1)S(1)}, bf16[32,512]{1,0:T(8,128)(2,1)S(1)}, u32[]{:S(2)}, u32[]{:S(2)}) %collective-permute-start.20) | collective-permute-done | bytes 32800 | tf_op jit(solution)/shard_map/ppermute | solution.py:242
  50.0 0.8 %collective-permute-done.23.rest_7_ = bf16[32,512]{1,0:T(8,128)(2,1)S(1)} collective-permute-done((bf16[32,512]{1,0:T(8,128)(2,1)S(1)}, bf16[32,512]{1,0:T(8,128)(2,1)S(1)}, u32[]{:S(2)}, u32[]{:S(2)}) %collective-permute-start.23) | collective-permute-done | bytes 32800 | tf_op jit(solution)/shard_map/ppermute | solution.py:242
  50.8 1.7 %join.1 = bf16[2,64,512]{2,1,0:T(8,128)(2,1)} custom-call(s32[12]{0:T(128)} %count_ref.3, s32[12]{0:T(128)} %rank_ref.3, s32[12]{0:T(128)} %owner_ref.3, f32[128,512]{1,0:T(8,128)S(1)} %base.1.base_ref, bf16[32,512]{1,0:T(8,128)(2,1)S(1)} %get-tuple-element.41.rest_0_, bf16[32,512]{1,0:T(8,128)(2,1)S(1)} %collective-permute-done.17.rest_1_, ...), custom_call_target="tpu_custom_call" | custom-call | tf_op jit(solution)/shard_map/join/pallas_call | solution.py:475
  (23 shorter events, 0.1 us)
Async XLA Ops:
  6.2 13.1 %collective-permute-start.7 = (bf16[8,8192]{1,0:T(8,128)(2,1)S(1)}, bf16[8,8192]{1,0:T(8,128)(2,1)S(1)}, u32[]{:S(2)}, u32[]{:S(2)}) collective-permute-start(bf16[8,8192]{1,0:T(8,128)(2,1)S(1)} %get-tuple-element.28.after.rest_0_), channel_id=1, source_target_pairs={{0,8},{1,9},{2,10},{3,11},{4,12},{5,13},{6,14},{7,15},{8,0},{9,1},... | collective-permute-start | bytes 393224 | tf_op jit(solution)/shard_map/ppermute | solution.py:242
  10.3 5.3 %collective-permute-start.2 = (bf16[8,8192]{1,0:T(8,128)(2,1)S(1)}, bf16[8,8192]{1,0:T(8,128)(2,1)S(1)}, u32[]{:S(2)}, u32[]{:S(2)}) collective-permute-start(bf16[8,8192]{1,0:T(8,128)(2,1)S(1)} %get-tuple-element.28.after.rest_0_), channel_id=1, source_target_pairs={{0,2},{1,3},{2,0},{3,1},{4,6},{5,7},{6,4},{7,5},{8,10},{9,11},{10,... | collective-permute-start | bytes 393224 | tf_op jit(solution)/shard_map/ppermute | solution.py:242
  11.8 6.3 %collective-permute-start.1 = (bf16[8,8192]{1,0:T(8,128)(2,1)S(1)}, bf16[8,8192]{1,0:T(8,128)(2,1)S(1)}, u32[]{:S(2)}, u32[]{:S(2)}) collective-permute-start(bf16[8,8192]{1,0:T(8,128)(2,1)S(1)} %get-tuple-element.28.after.rest_0_), channel_id=1, source_target_pairs={{0,4},{1,5},{2,6},{3,7},{4,0},{5,1},{6,2},{7,3},{8,12},{9,13},{10,... | collective-permute-start | bytes 393224 | tf_op jit(solution)/shard_map/ppermute | solution.py:242
  13.4 8.1 %collective-permute-start = (bf16[8,8192]{1,0:T(8,128)(2,1)S(1)}, bf16[8,8192]{1,0:T(8,128)(2,1)S(1)}, u32[]{:S(2)}, u32[]{:S(2)}) collective-permute-start(bf16[8,8192]{1,0:T(8,128)(2,1)S(1)} %get-tuple-element.28.after.rest_0_), channel_id=1, source_target_pairs={{0,1},{1,0},{2,3},{3,2},{4,5},{5,4},{6,7},{7,6},{8,9},{9,8},{10,11... | collective-permute-start | bytes 393224 | tf_op jit(solution)/shard_map/ppermute | solution.py:242
  18.1 6.0 %collective-permute-start.5 = (bf16[8,8192]{1,0:T(8,128)(2,1)S(1)}, bf16[8,8192]{1,0:T(8,128)(2,1)S(1)}, u32[]{:S(2)}, u32[]{:S(2)}) collective-permute-start(bf16[8,8192]{1,0:T(8,128)(2,1)S(1)} %collective-permute-done.1.after.rest_4_), channel_id=1, source_target_pairs={{0,2},{1,3},{2,0},{3,1},{4,6},{5,7},{6,4},{7,5},{8,10},{9,11},{10,... | collective-permute-start | bytes 393224 | tf_op jit(solution)/shard_map/ppermute | solution.py:242
  18.7 6.3 %collective-permute-start.4 = (bf16[8,8192]{1,0:T(8,128)(2,1)S(1)}, bf16[8,8192]{1,0:T(8,128)(2,1)S(1)}, u32[]{:S(2)}, u32[]{:S(2)}) collective-permute-start(bf16[8,8192]{1,0:T(8,128)(2,1)S(1)} %collective-permute-done.1.after.rest_4_), channel_id=1, source_target_pairs={{0,1},{1,0},{2,3},{3,2},{4,5},{5,4},{6,7},{7,6},{8,9},{9,8},{10,11... | collective-permute-start | bytes 393224 | tf_op jit(solution)/shard_map/ppermute | solution.py:242
  18.7 4.2 %collective-permute-start.3 = (bf16[8,8192]{1,0:T(8,128)(2,1)S(1)}, bf16[8,8192]{1,0:T(8,128)(2,1)S(1)}, u32[]{:S(2)}, u32[]{:S(2)}) collective-permute-start(bf16[8,8192]{1,0:T(8,128)(2,1)S(1)} %collective-permute-done.2.rest_2_), channel_id=1, source_target_pairs={{0,1},{1,0},{2,3},{3,2},{4,5},{5,4},{6,7},{7,6},{8,9},{9,8},{10,11... | collective-permute-start | bytes 393224 | tf_op jit(solution)/shard_map/ppermute | solution.py:242
  19.2 16.9 %collective-permute-start.16 = (bf16[4096,128]{1,0:T(8,128)(2,1)S(1)}, bf16[4096,128]{1,0:T(8,128)(2,1)S(1)}, u32[]{:S(2)}, u32[]{:S(2)}) collective-permute-start(bf16[4096,128]{1,0:T(8,128)(2,1)S(1)} %get-tuple-element.40), channel_id=1, source_target_pairs={{0,1},{1,0},{2,3},{3,2},{4,5},{5,4},{6,7},{7,6},{8,9},{9,8},{10,11... | collective-permute-start | bytes 3145736 | tf_op jit(solution)/shard_map/ppermute | solution.py:242
  21.5 8.8 %collective-permute-start.13 = (bf16[8,8192]{1,0:T(8,128)(2,1)S(1)}, bf16[8,8192]{1,0:T(8,128)(2,1)S(1)}, u32[]{:S(2)}, u32[]{:S(2)}) collective-permute-start(bf16[8,8192]{1,0:T(8,128)(2,1)S(1)} %collective-permute-done.7.rest_8_), channel_id=1, source_target_pairs={{0,2},{1,3},{2,0},{3,1},{4,6},{5,7},{6,4},{7,5},{8,10},{9,11},{10,... | collective-permute-start | bytes 393224 | tf_op jit(solution)/shard_map/ppermute | solution.py:242
  23.0 7.3 %collective-permute-start.11 = (bf16[8,8192]{1,0:T(8,128)(2,1)S(1)}, bf16[8,8192]{1,0:T(8,128)(2,1)S(1)}, u32[]{:S(2)}, u32[]{:S(2)}) collective-permute-start(bf16[8,8192]{1,0:T(8,128)(2,1)S(1)} %collective-permute-done.7.rest_8_), channel_id=1, source_target_pairs={{0,6},{1,7},{2,4},{3,5},{4,2},{5,3},{6,0},{7,1},{8,14},{9,15},{10,... | collective-permute-start | bytes 393224 | tf_op jit(solution)/shard_map/ppermute | solution.py:242
  24.1 7.4 %collective-permute-start.9 = (bf16[8,8192]{1,0:T(8,128)(2,1)S(1)}, bf16[8,8192]{1,0:T(8,128)(2,1)S(1)}, u32[]{:S(2)}, u32[]{:S(2)}) collective-permute-start(bf16[8,8192]{1,0:T(8,128)(2,1)S(1)} %collective-permute-done.7.rest_8_), channel_id=1, source_target_pairs={{0,4},{1,5},{2,6},{3,7},{4,0},{5,1},{6,2},{7,3},{8,12},{9,13},{10,... | collective-permute-start | bytes 393224 | tf_op jit(solution)/shard_map/ppermute | solution.py:242
  25.0 6.5 %collective-permute-start.8 = (bf16[8,8192]{1,0:T(8,128)(2,1)S(1)}, bf16[8,8192]{1,0:T(8,128)(2,1)S(1)}, u32[]{:S(2)}, u32[]{:S(2)}) collective-permute-start(bf16[8,8192]{1,0:T(8,128)(2,1)S(1)} %collective-permute-done.7.rest_8_), channel_id=1, source_target_pairs={{0,1},{1,0},{2,3},{3,2},{4,5},{5,4},{6,7},{7,6},{8,9},{9,8},{10,11... | collective-permute-start | bytes 393224 | tf_op jit(solution)/shard_map/ppermute | solution.py:242
  30.3 1.7 %collective-permute-start.6 = (bf16[8,8192]{1,0:T(8,128)(2,1)S(1)}, bf16[8,8192]{1,0:T(8,128)(2,1)S(1)}, u32[]{:S(2)}, u32[]{:S(2)}) collective-permute-start(bf16[8,8192]{1,0:T(8,128)(2,1)S(1)} %collective-permute-done.5.rest_6_), channel_id=1, source_target_pairs={{0,1},{1,0},{2,3},{3,2},{4,5},{5,4},{6,7},{7,6},{8,9},{9,8},{10,11... | collective-permute-start | bytes 393224 | tf_op jit(solution)/shard_map/ppermute | solution.py:242
  30.3 1.7 %collective-permute-start.14 = (bf16[8,8192]{1,0:T(8,128)(2,1)S(1)}, bf16[8,8192]{1,0:T(8,128)(2,1)S(1)}, u32[]{:S(2)}, u32[]{:S(2)}) collective-permute-start(bf16[8,8192]{1,0:T(8,128)(2,1)S(1)} %collective-permute-done.13.rest_14_), channel_id=1, source_target_pairs={{0,1},{1,0},{2,3},{3,2},{4,5},{5,4},{6,7},{7,6},{8,9},{9,8},{10,11... | collective-permute-start | bytes 393224 | tf_op jit(solution)/shard_map/ppermute | solution.py:242
  31.5 1.3 %collective-permute-start.12 = (bf16[8,8192]{1,0:T(8,128)(2,1)S(1)}, bf16[8,8192]{1,0:T(8,128)(2,1)S(1)}, u32[]{:S(2)}, u32[]{:S(2)}) collective-permute-start(bf16[8,8192]{1,0:T(8,128)(2,1)S(1)} %collective-permute-done.11.rest_12_), channel_id=1, source_target_pairs={{0,1},{1,0},{2,3},{3,2},{4,5},{5,4},{6,7},{7,6},{8,9},{9,8},{10,11... | collective-permute-start | bytes 393224 | tf_op jit(solution)/shard_map/ppermute | solution.py:242
  31.5 1.5 %collective-permute-start.10 = (bf16[8,8192]{1,0:T(8,128)(2,1)S(1)}, bf16[8,8192]{1,0:T(8,128)(2,1)S(1)}, u32[]{:S(2)}, u32[]{:S(2)}) collective-permute-start(bf16[8,8192]{1,0:T(8,128)(2,1)S(1)} %collective-permute-done.9.rest_10_), channel_id=1, source_target_pairs={{0,1},{1,0},{2,3},{3,2},{4,5},{5,4},{6,7},{7,6},{8,9},{9,8},{10,11... | collective-permute-start | bytes 393224 | tf_op jit(solution)/shard_map/ppermute | solution.py:242
  34.5 1.6 %collective-permute-start.15 = (bf16[16,128]{1,0:T(8,128)(2,1)S(1)}, bf16[16,128]{1,0:T(8,128)(2,1)S(1)}, u32[]{:S(2)}, u32[]{:S(2)}) collective-permute-start(bf16[16,128]{1,0:T(8,128)(2,1)S(1)} %get-tuple-element.33.own_ref), channel_id=1, source_target_pairs={{0,1},{1,0},{2,3},{3,2},{4,5},{5,4},{6,7},{7,6},{8,9},{9,8},{10,11... | collective-permute-start | bytes 12296 | tf_op jit(solution)/shard_map/ppermute | solution.py:242
  36.8 9.1 %collective-permute-start.17 = (bf16[32,512]{1,0:T(8,128)(2,1)S(1)}, bf16[32,512]{1,0:T(8,128)(2,1)S(1)}, u32[]{:S(2)}, u32[]{:S(2)}) collective-permute-start(bf16[32,512]{1,0:T(8,128)(2,1)S(1)} %get-tuple-element.42), channel_id=1, source_target_pairs={{0,8},{1,9},{2,10},{3,11},{4,12},{5,13},{6,14},{7,15},{8,0},{9,1},... | collective-permute-start | bytes 98312 | tf_op jit(solution)/shard_map/ppermute | solution.py:242
  38.3 7.6 %collective-permute-start.18 = (bf16[32,512]{1,0:T(8,128)(2,1)S(1)}, bf16[32,512]{1,0:T(8,128)(2,1)S(1)}, u32[]{:S(2)}, u32[]{:S(2)}) collective-permute-start(bf16[32,512]{1,0:T(8,128)(2,1)S(1)} %get-tuple-element.43), channel_id=1, source_target_pairs={{0,10},{1,11},{2,8},{3,9},{4,14},{5,15},{6,12},{7,13},{8,2},{9,3},... | collective-permute-start | bytes 98312 | tf_op jit(solution)/shard_map/ppermute | solution.py:242
  40.6 7.4 %collective-permute-start.19 = (bf16[32,512]{1,0:T(8,128)(2,1)S(1)}, bf16[32,512]{1,0:T(8,128)(2,1)S(1)}, u32[]{:S(2)}, u32[]{:S(2)}) collective-permute-start(bf16[32,512]{1,0:T(8,128)(2,1)S(1)} %get-tuple-element.44), channel_id=1, source_target_pairs={{0,12},{1,13},{2,14},{3,15},{4,8},{5,9},{6,10},{7,11},{8,4},{9,5},... | collective-permute-start | bytes 98312 | tf_op jit(solution)/shard_map/ppermute | solution.py:242
  43.3 6.7 %collective-permute-start.20 = (bf16[32,512]{1,0:T(8,128)(2,1)S(1)}, bf16[32,512]{1,0:T(8,128)(2,1)S(1)}, u32[]{:S(2)}, u32[]{:S(2)}) collective-permute-start(bf16[32,512]{1,0:T(8,128)(2,1)S(1)} %get-tuple-element.45), channel_id=1, source_target_pairs={{0,14},{1,15},{2,12},{3,13},{4,10},{5,11},{6,8},{7,9},{8,6},{9,7},... | collective-permute-start | bytes 98312 | tf_op jit(solution)/shard_map/ppermute | solution.py:242
  44.5 5.5 %collective-permute-start.21 = (bf16[32,512]{1,0:T(8,128)(2,1)S(1)}, bf16[32,512]{1,0:T(8,128)(2,1)S(1)}, u32[]{:S(2)}, u32[]{:S(2)}) collective-permute-start(bf16[32,512]{1,0:T(8,128)(2,1)S(1)} %get-tuple-element.46), channel_id=1, source_target_pairs={{0,2},{1,3},{2,0},{3,1},{4,6},{5,7},{6,4},{7,5},{8,10},{9,11},{10,... | collective-permute-start | bytes 98312 | tf_op jit(solution)/shard_map/ppermute | solution.py:242
  45.9 4.1 %collective-permute-start.22 = (bf16[32,512]{1,0:T(8,128)(2,1)S(1)}, bf16[32,512]{1,0:T(8,128)(2,1)S(1)}, u32[]{:S(2)}, u32[]{:S(2)}) collective-permute-start(bf16[32,512]{1,0:T(8,128)(2,1)S(1)} %get-tuple-element.47), channel_id=1, source_target_pairs={{0,4},{1,5},{2,6},{3,7},{4,0},{5,1},{6,2},{7,3},{8,12},{9,13},{10,... | collective-permute-start | bytes 98312 | tf_op jit(solution)/shard_map/ppermute | solution.py:242
  45.9 4.9 %collective-permute-start.23 = (bf16[32,512]{1,0:T(8,128)(2,1)S(1)}, bf16[32,512]{1,0:T(8,128)(2,1)S(1)}, u32[]{:S(2)}, u32[]{:S(2)}) collective-permute-start(bf16[32,512]{1,0:T(8,128)(2,1)S(1)} %get-tuple-element.48), channel_id=1, source_target_pairs={{0,6},{1,7},{2,4},{3,5},{4,2},{5,3},{6,0},{7,1},{8,14},{9,15},{10,... | collective-permute-start | bytes 98312 | tf_op jit(solution)/shard_map/ppermute | solution.py:242

commit v7 on v5

v7 whole, which is shorter than its diff:
```python
import functools

import jax
import jax.numpy as jnp
from jax import lax
from jax.experimental import pallas as pl
from jax.experimental.pallas import tpu as pltpu
from jax.sharding import PartitionSpec as P

HQ = 64
KVH = 8
HD = 128
GROUP = HQ // KVH
MOST = 8
RING = 16
ORDER = [0,1,6,7,2,3,4,5,8,9,12,13,14,15,10,11]
F32 = jnp.float32
BF16 = jnp.bfloat16
NT = (((1,), (1,)), ((), ()))


def in_hbm(*arrays):
    return [pltpu.with_memory_space_constraint(a, pltpu.HBM) for a in arrays]


def iota(shape, dim):
    return lax.broadcasted_iota(jnp.int32, shape, dim)


def one_hot(mask):
    return mask.astype(F32).astype(BF16)


def dot(a, b):
    return jnp.dot(a, b, preferred_element_type=F32)


def dot_nt(a, b):
    return lax.dot_general(a, b, NT, preferred_element_type=F32)


def attend_kernel(
    len_hbm, q_hbm, nk_hbm, nv_hbm, k_hbm, v_hbm, out_ref,
    len_ref, q_ref, nk_ref, nv_ref, k_ref, v_ref, turned_q, nks, nvs, raw, mixed,
    small_sems, sems,
):
    steps, rows, width = q_ref.shape
    cache = k_ref.shape[1]
    both = steps * rows
    pack = steps * GROUP
    cuts = sems.shape[2]

    small = [
        pltpu.make_async_copy(src, dst, small_sems.at[i])
        for i, (src, dst) in enumerate(
            ((q_hbm, q_ref), (len_hbm, len_ref), (nk_hbm, nk_ref), (nv_hbm, nv_ref))
        )
    ]
    pieces = [pl.ds(i * (cache // cuts), cache // cuts) for i in range(cuts)]
    keys, values = [
        [
            [
                pltpu.make_async_copy(src.at[r, at], dst.at[r, at], sems.at[r, j, i])
                for i, at in enumerate(pieces)
            ]
            for r in range(rows)
        ]
        for j, (src, dst) in enumerate(((k_hbm, k_ref), (v_hbm, v_ref)))
    ]
    queue = [keys[0], values[0], keys[1]]
    for r in range(rows):
        queue += [values[r + 1]] if r + 1 < rows else [[]]
        queue += [keys[r + 2]] if r + 2 < rows else []
    for copy in small + queue[0] + queue[1] + queue[2]:
        copy.start()
    queue = queue[3:]
    for copy in small:
        copy.wait()

    flat = jnp.concatenate([q_ref[t].astype(F32) for t in range(steps)], axis=0)
    heads = []
    for k in range(KVH):
        group = jnp.stack(
            [flat[:, (k * GROUP + g) * HD : (k * GROUP + g + 1) * HD] for g in range(GROUP)]
        )
        heads.append(jnp.swapaxes(group, 0, 1))
    column = iota((HD, KVH * pack), 1)
    for r in range(rows):
        mine = jnp.concatenate(
            [heads[k][t * rows + r] for k in range(KVH) for t in range(steps)], axis=0
        )
        mine = jnp.transpose(mine)
        for k in range(KVH):
            turned_q[r, k * HD : (k + 1) * HD, :] = jnp.where(
                column // pack == k, mine, 0.0
            ).astype(BF16)
    for src, dst in ((nk_ref, nks), (nv_ref, nvs)):
        fresh = [src[t].astype(F32) for t in range(steps)]
        fresh.append(jnp.zeros((16 - both, src.shape[2]), F32))
        dst[...] = jnp.concatenate(fresh, axis=0).astype(BF16)

    scale = HD ** (-0.5)
    pairs = [
        (slice(k * pack, (k + 2) * pack), slice(k * HD, (k + 2) * HD)) for k in range(0, KVH, 2)
    ]
    for turn in range(rows + 1):
        if turn < rows:
            for copy in keys[turn]:
                copy.wait()
        if turn > 0:
            for copy in values[turn - 1]:
                copy.wait()
        for copies in queue[2 * turn : 2 * turn + 2]:
            for copy in copies:
                copy.start()
        if turn < rows:
            raw[turn % 2] = dot(k_ref[turn], turned_q[turn])
        if turn == 0:
            continue
        r = turn - 1
        fresh = dot(nks[...], turned_q[r])
        slot = iota(fresh.shape, 0)
        step = (iota(fresh.shape, 1) // GROUP) % steps
        seen = (slot < both) & (slot % rows == r) & (slot // rows <= step)
        fresh = jnp.where(seen, fresh * scale, -jnp.inf)
        older = raw[r % 2]
        older = jnp.where(iota(older.shape, 0) < len_ref[r], older * scale, -jnp.inf)
        top = jnp.maximum(
            jnp.max(older, axis=0, keepdims=True), jnp.max(fresh, axis=0, keepdims=True)
        )
        e_older = jnp.exp(older - top)
        e_fresh = jnp.exp(fresh - top)
        total = jnp.sum(e_older, axis=0, keepdims=True) + jnp.sum(e_fresh, axis=0, keepdims=True)
        inverse = 1.0 / total
        p_older = jnp.transpose((e_older * inverse).astype(BF16))
        p_fresh = jnp.transpose((e_fresh * inverse).astype(BF16))
        for k, (own, cols_k) in zip(range(0, KVH, 2), pairs):
            pair = dot(p_older[own], v_ref[r, :, cols_k]) + dot(p_fresh[own], nvs[:, cols_k])
            mixed[r, k] = pair[:pack, :HD]
            mixed[r, k + 1] = pair[pack:, HD:]

    for k in range(KVH):
        turned = jnp.stack(
            [
                mixed[r, k, t * GROUP : (t + 1) * GROUP, :]
                for t in range(steps)
                for r in range(rows)
            ]
        )
        heads = jnp.swapaxes(turned, 0, 1)
        for g in range(GROUP):
            at = (k * GROUP + g) * HD
            out_ref[:, at : at + HD] = heads[g].astype(BF16)


def attend(queries, new_keys, new_values, cache_keys, cache_values, kv_len):
    steps, rows, width = queries.shape
    cache, kv_width = cache_keys.shape[1:]
    pack = steps * GROUP
    return pl.pallas_call(
        attend_kernel,
        out_shape=jax.ShapeDtypeStruct((steps * rows, width), BF16),
        in_specs=[pl.BlockSpec(memory_space=pl.ANY)] * 6,
        out_specs=pl.BlockSpec(memory_space=pltpu.VMEM),
        scratch_shapes=[
            pltpu.SMEM(kv_len.shape, jnp.int32),
            pltpu.VMEM(queries.shape, BF16),
            pltpu.VMEM(new_keys.shape, BF16),
            pltpu.VMEM(new_values.shape, BF16),
            pltpu.VMEM(cache_keys.shape, BF16),
            pltpu.VMEM(cache_values.shape, BF16),
            pltpu.VMEM((rows, kv_width, KVH * pack), BF16),
            pltpu.VMEM((16, kv_width), BF16),
            pltpu.VMEM((16, kv_width), BF16),
            pltpu.VMEM((2, cache, KVH * pack), F32),
            pltpu.VMEM((rows, KVH, pack, HD), F32),
            pltpu.SemaphoreType.DMA((4,)),
            pltpu.SemaphoreType.DMA((rows, 2, 2)),
        ],
        compiler_params=pltpu.CompilerParams(vmem_limit_bytes=32 * 2**20),
        cost_estimate=pl.CostEstimate(
            flops=4 * rows * steps * HQ * cache * HD,
            bytes_accessed=4 * rows * cache * kv_width,
            transcendentals=rows * steps * HQ * cache,
        ),
        name="attend",
    )(*in_hbm(kv_len, queries, new_keys, new_values, cache_keys, cache_values))


def sender(slot, me, parts):
    return me ^ slot if parts == RING else slot


def swap(x, bits, parts):
    return lax.ppermute(x, "tensor", [(i, i ^ bits) for i in range(parts)])


def prepare_kernel(
    rows, count_ref, rank_ref, owner_ref, after, d_hbm, u_hbm,
    d_ref, u_ref, pick_ref, place_ref, order_ref, sems,
):
    me = lax.axis_index("tensor")
    cuts = sems.shape[1]
    deep = d_ref.shape[0] // cuts
    copies = []
    for j, (src, dst) in enumerate(((d_hbm, d_ref), (u_hbm, u_ref))):
        for i in range(cuts):
            at = pl.ds(i * deep, deep)
            copies.append(pltpu.make_async_copy(src.at[0, at], dst.at[at], sems.at[j, i]))
            copies[-1].start()
    slots, total = pick_ref.shape
    steps = slots // MOST
    each = steps * rows
    parts = total // each
    requests = parts * rows

    def adapter_of(block):
        first = jnp.zeros(block.shape, jnp.int32)
        amount = jnp.zeros(block.shape, jnp.int32)
        start = jnp.int32(0)
        for a in range(count_ref.shape[0]):
            owned = (owner_ref[a] <= block) & (block < owner_ref[a] + rank_ref[a])
            first = jnp.where(owned, start, first)
            amount = jnp.where(owned, count_ref[a], amount)
            start = start + count_ref[a]
        return first, amount

    def row_place(index):
        device = sender(index // each, me, parts)
        return device * rows + index % rows, (index % each) // rows

    row = iota((slots, 1), 0)
    nth = row % MOST
    first, amount = adapter_of(jnp.zeros_like(row) + me)
    request, step = row_place(iota((1, total), 1))
    pick = (request == first + nth) & (nth < amount) & (step == row // MOST)
    pick_ref[...] = one_hot(pick)

    request, step = row_place(iota((total, total), 1))
    order_ref[...] = one_hot(iota((total, total), 0) == step * requests + request)

    entry = iota((1, parts * slots), 1)
    nth = entry % MOST
    first, amount = adapter_of(entry // slots)
    goal = jnp.where(nth < amount, (entry % slots) // MOST * requests + first + nth, -1)
    place_ref[...] = one_hot(iota((total, parts * slots), 0) == goal)
    for copy in copies:
        copy.wait()


def prepare(after, store_down, store_up, tables, steps, rows, parts):
    width, rank_w = store_down.shape[1:]
    total = parts * steps * rows
    slots = steps * MOST
    vmem = pl.BlockSpec(memory_space=pltpu.VMEM)
    shapes = [(width, rank_w)] * 2 + [(slots, total), (total, parts * slots), (total, total)]
    return pl.pallas_call(
        functools.partial(prepare_kernel, rows),
        out_shape=[jax.ShapeDtypeStruct(shape, BF16) for shape in shapes],
        in_specs=[pl.BlockSpec(memory_space=pltpu.SMEM)] * 3
        + [pl.BlockSpec(memory_space=pl.ANY)] * 3,
        out_specs=[vmem] * len(shapes),
        scratch_shapes=[pltpu.SemaphoreType.DMA((2, 4))],
        compiler_params=pltpu.CompilerParams(vmem_limit_bytes=16 * 2**20),
        cost_estimate=pl.CostEstimate(
            flops=2 * 10**10, bytes_accessed=8 * width * rank_w, transcendentals=0
        ),
        name="prepare",
    )(*in_hbm(*tables), after, *in_hbm(store_down, store_up))


def gather(block, prepared, parts):
    if parts != RING:
        whole = lax.all_gather(block, "tensor")
        return [whole[i] for i in range(parts)], prepared
    core, y, near, far = 1, 2, 4, 8
    held = {0: block}
    held[far] = swap(block, far, parts)
    held[near] = swap(block, near, parts)
    held[y] = swap(block, y, parts)
    held[near | y] = swap(block, near | y, parts)
    held[far], *prepared = lax.optimization_barrier((held[far], *prepared))
    held[far | y] = swap(held[far], y, parts)
    held[far | near | y] = swap(held[far], near | y, parts)
    held[far | near] = swap(held[far], near, parts)
    names = (near, y, near | y, far | near)
    held.update(zip(names, lax.optimization_barrier(tuple(held[n] for n in names))))
    for slot in list(held):
        held[slot | core] = swap(held[slot], core, parts)
    return [held[slot] for slot in range(parts)], prepared


def delta_kernel(at_slot, *refs):
    (*blocks, pick_ref, d_ref, u_ref, out_ref, rows_ref) = refs
    blocks = [blocks[at_slot.index(i)] for i in range(len(blocks))]
    parts, slots, cols = out_ref.shape
    each, width = blocks[0].shape
    cuts = 8
    deep = width // cuts
    low = jnp.zeros((parts * each, d_ref.shape[1]), F32)
    for i in range(cuts):
        at = slice(i * deep, (i + 1) * deep)
        piece = jnp.concatenate([b[:, at] for b in blocks], axis=0)
        rows_ref[:, at] = piece
        low = low + dot(piece, d_ref[at, :])
    chosen = dot(pick_ref[...], low.astype(BF16)).astype(BF16)
    for p in range(parts):
        out_ref[p] = dot_nt(chosen, u_ref[p * cols : (p + 1) * cols, :]).astype(BF16)


def deltas(blocks, pick, down, up):
    parts = len(blocks)
    each, width = blocks[0].shape
    slots = pick.shape[0]
    rank_w = down.shape[1]
    vmem = pl.BlockSpec(memory_space=pltpu.VMEM)
    at_slot = ORDER if parts == RING else [*range(parts)]
    return pl.pallas_call(
        functools.partial(delta_kernel, at_slot),
        out_shape=(
            jax.ShapeDtypeStruct((parts, slots, width // parts), BF16),
            jax.ShapeDtypeStruct((parts * each, width), BF16),
        ),
        in_specs=[vmem] * (3 + parts),
        out_specs=(vmem, vmem),
        compiler_params=pltpu.CompilerParams(vmem_limit_bytes=24 * 2**20),
        cost_estimate=pl.CostEstimate(
            flops=2 * (parts * each + slots) * width * rank_w,
            bytes_accessed=2 * width * (2 * parts * each + 2 * rank_w + slots),
            transcendentals=0,
        ),
        name="delta",
    )(*[blocks[i] for i in at_slot], pick, down, up)


def base_kernel(a_ref, w_ref, order_ref, out_ref):
    width = a_ref.shape[1]
    cuts = 8
    deep = width // cuts
    for i in range(cuts):
        at = slice(i * deep, (i + 1) * deep)
        part = dot(dot(order_ref[...], a_ref[:, at]).astype(BF16), w_ref[at, :])
        out_ref[...] = part if i == 0 else out_ref[...] + part


def base_part(gathered, out_weight, order):
    total, width = gathered.shape
    cols = out_weight.shape[1]
    vmem = pl.BlockSpec(memory_space=pltpu.VMEM)
    return pl.pallas_call(
        base_kernel,
        out_shape=jax.ShapeDtypeStruct((total, cols), F32),
        in_specs=[vmem] * 3,
        out_specs=vmem,
        compiler_params=pltpu.CompilerParams(vmem_limit_bytes=24 * 2**20),
        cost_estimate=pl.CostEstimate(
            flops=2 * total * width * (cols + total),
            bytes_accessed=2 * width * (total + cols) + 4 * total * cols,
            transcendentals=0,
        ),
        name="base",
    )(gathered, out_weight, order)


def join_kernel(base_ref, place_ref, delta_ref, out_ref):
    steps, requests, cols = out_ref.shape
    parts, slots, _ = delta_ref.shape
    delta = dot(place_ref[...], delta_ref[...].reshape(parts * slots, cols))
    result = (base_ref[...] + delta).astype(BF16)
    for t in range(steps):
        out_ref[t] = result[t * requests : (t + 1) * requests]


def join(base, place, delta, steps):
    total, cols = base.shape
    vmem = pl.BlockSpec(memory_space=pltpu.VMEM)
    return pl.pallas_call(
        join_kernel,
        out_shape=jax.ShapeDtypeStruct((steps, total // steps, cols), BF16),
        in_specs=[vmem] * 3,
        out_specs=vmem,
        compiler_params=pltpu.CompilerParams(vmem_limit_bytes=24 * 2**20),
        name="join",
    )(base, place, delta)


def per_device(
    queries,
    new_keys,
    new_values,
    cache_keys,
    cache_values,
    kv_len,
    adapter_rows,
    adapter_rank,
    adapter_owner,
    out_weight,
    store_down,
    store_up,
):
    parts = lax.axis_size("tensor")
    steps, rows, width = queries.shape
    tables = (adapter_rows, adapter_rank, adapter_owner)
    attended = attend(queries, new_keys, new_values, cache_keys, cache_values, kv_len)
    prepared = prepare(attended, store_down, store_up, tables, steps, rows, parts)
    blocks, (down, up, pick, place, order) = gather(attended, prepared, parts)
    send, gathered = deltas(blocks, pick, down, up)
    delta = lax.all_to_all(send, "tensor", split_axis=0, concat_axis=0, tiled=True)
    base = base_part(gathered, out_weight, order)
    return join(base, place, delta, steps)


def solution(mesh):
    in_specs = (
        P(None, ("groups", "tensor"), None),
        P(None, ("groups", "tensor"), None),
        P(None, ("groups", "tensor"), None),
        P(("groups", "tensor"), None, None),
        P(("groups", "tensor"), None, None),
        P(("groups", "tensor")),
        P("groups"),
        P(),
        P(),
        P(None, "tensor"),
        P("tensor", None, None),
        P("tensor", None, None),
    )
    out_specs = P(None, "groups", "tensor")
    return jax.shard_map(
        per_device, mesh=mesh, in_specs=in_specs, out_specs=out_specs, check_vma=False
    )
```

time: 49.7 us -> 47.1 us (0.948)
  waiting for transfers between devices: 14.1 us -> 10.6 us
  starting transfers between devices: 17.4 us -> 18.4 us
    ppermute x15, waiting for transfers between devices: 8.68 us -> 6.33 us  [swap(): return lax.ppermute(x, 'tensor', [(i, i ^ bits) for i in range(parts)])]
    all_to_all x1, waiting for transfers between devices: 5.41 us -> 4.26 us  [per_device(): lax.all_to_all(send, 'tensor', split_axis=0, concat_axis=0, tiled=True)]
    pallas_call x1, Pallas kernels: 1.25 us -> 2.4 us  [base_part(): pl.pallas_call(base_kernel, out_shape=jax.ShapeDtypeStruct((total, cols),...]
    ppermute x15, starting transfers between devices: 12.4 us -> 13.1 us  [swap(): return lax.ppermute(x, 'tensor', [(i, i ^ bits) for i in range(parts)])]
    pallas_call x1, Pallas kernels: 6.69 us -> 6.08 us  [attend(): pl.pallas_call(attend_kernel, out_shape=jax.ShapeDtypeStruct((steps * row...]
    pallas_call x3, Pallas kernels: 6.51 us -> 5.93 us  [the longest x1 2.9 us: prepare(): pl.pallas_call(functools.partial(prepare_kernel, rows), out_shape=[jax.Sh...]
  transfers between devices with their start and end apart: 16 -> 16, of which waited for: 7 -> 8; matrix products, arithmetic and copies ran while one was open for 0% -> 0% of each run, Pallas kernels for 7% -> 11%
where the time goes in v7:
time: 47.1 us; the launch traced here: 46.8 us
  starting transfers between devices  18.4 us (39%)
  Pallas kernels  14.4 us (31%)
  waiting for transfers between devices  10.6 us (23%)
  local copies, waits for them, and re-layouts  3.38 us (7%)
    ppermute x15, starting transfers between devices, swap(): return lax.ppermute(x, 'tensor', [(i, i ^ bits) for i in range(parts)])  13.1 us
    ppermute x15, waiting for transfers between devices, swap(): return lax.ppermute(x, 'tensor', [(i, i ^ bits) for i in range(parts)])  6.33 us
    pallas_call x1, Pallas kernels, attend(): pl.pallas_call(attend_kernel, out_shape=jax.ShapeDtypeStruct((steps * row...  6.08 us
    all_to_all x1, starting transfers between devices, per_device(): lax.all_to_all(send, 'tensor', split_axis=0, concat_axis=0, tiled=True)  5.25 us
    all_to_all x1, waiting for transfers between devices, per_device(): lax.all_to_all(send, 'tensor', split_axis=0, concat_axis=0, tiled=True)  4.26 us
    unnamed x2, local copies, waits for them, and re-layouts  3.38 us
    pallas_call x1, Pallas kernels, prepare(): pl.pallas_call(functools.partial(prepare_kernel, rows), out_shape=[jax.Sh...  2.9 us
    pallas_call x1, Pallas kernels, base_part(): pl.pallas_call(base_kernel, out_shape=jax.ShapeDtypeStruct((total, cols),...  2.4 us
  transfers between devices with their start and end apart: 16, of which 8 were waited for; matrix products, arithmetic and copies ran while one was open for 0% of the time, Pallas kernels for 11%

profile of v7, /device:TPU:0, one launch (start us, length us, event | category | flops | bytes accessed | tf_op | source)
XLA Modules:
  0.0 46.8 jit_solution(7199247609076286218)
XLA Ops:
  0.0 6.1 %attend.1.after.refs_0_ = bf16[8,8192]{1,0:T(8,128)(2,1)S(1)} custom-call(s32[4]{0:T(128)} %len_hbm.1, bf16[2,4,8192]{2,1,0:T(4,128)(2,1)} %q_hbm.1, bf16[2,4,1024]{2,1,0:T(4,128)(2,1)} %nk_hbm.1, bf16[2,4,1024]{2,1,0:T(4,128)(2,1)} %nv_hbm.1, bf16[4,512,1024]{2,1,0:T(8,128)(2,1)} %k_hbm.1, bf16[4,512,1024]{2,1,0:T(8,128)(2,1)} %v_hbm.1), custom_call_target="tpu_custom_call" | custom-call | flops 134217728 | bytes 8388608 | tf_op jit(solution)/shard_map/attend/pallas_call | solution.py:160
  6.1 4.1 %collective-permute-start.4 = (bf16[8,8192]{1,0:T(8,128)(2,1)S(1)}, bf16[8,8192]{1,0:T(8,128)(2,1)S(1)}, u32[]{:S(2)}, u32[]{:S(2)}) collective-permute-start(bf16[8,8192]{1,0:T(8,128)(2,1)S(1)} %attend.1.after.refs_0_), channel_id=1, source_target_pairs={{0,8},{1,9},{2,10},{3,11},{4,12},{5,13},{6,14},{7,15},{8,0},{9,1},... | collective-permute-start | bytes 393224 | tf_op jit(solution)/shard_map/ppermute | solution.py:195
  10.2 2.5 %collective-permute-start.3 = (bf16[8,8192]{1,0:T(8,128)(2,1)S(1)}, bf16[8,8192]{1,0:T(8,128)(2,1)S(1)}, u32[]{:S(2)}, u32[]{:S(2)}) collective-permute-start(bf16[8,8192]{1,0:T(8,128)(2,1)S(1)} %attend.1.after.refs_0_), channel_id=1, source_target_pairs={{0,6},{1,7},{2,4},{3,5},{4,2},{5,3},{6,0},{7,1},{8,14},{9,15},{10,... | collective-permute-start | bytes 393224 | tf_op jit(solution)/shard_map/ppermute | solution.py:195
  12.7 0.5 %collective-permute-start.2 = (bf16[8,8192]{1,0:T(8,128)(2,1)S(1)}, bf16[8,8192]{1,0:T(8,128)(2,1)S(1)}, u32[]{:S(2)}, u32[]{:S(2)}) collective-permute-start(bf16[8,8192]{1,0:T(8,128)(2,1)S(1)} %attend.1.after.refs_0_), channel_id=1, source_target_pairs={{0,2},{1,3},{2,0},{3,1},{4,6},{5,7},{6,4},{7,5},{8,10},{9,11},{10,... | collective-permute-start | bytes 393224 | tf_op jit(solution)/shard_map/ppermute | solution.py:195
  13.2 0.5 collective-permute-start.1
  13.7 2.9 %prepare.1 = (bf16[8192,128]{1,0:T(8,128)(2,1)S(1)}, bf16[8192,128]{1,0:T(8,128)(2,1)S(1)}, bf16[16,128]{1,0:T(8,128)(2,1)S(1)}, bf16[128,256]{1,0:T(8,128)(2,1)S(1)}, bf16[128,128]{1,0:T(8,128)(2,1)S(1)}) custom-call(s32[12]{0:T(128)} %count_ref.1, s32[12]{0:T(128)} %rank_ref.1, s32[12]{0:T(128)} %owner_ref.1, bf16[8,8192]{1,0:T(8,128)(2,1)S(1)} %attend.1.after.refs_0_, ...), custom_call_target="tpu_custom_call" | custom-call | flops 20000000000 | bytes 8388608 | tf_op jit(solution)/shard_map/prepare/pallas_call | solution.py:257
  16.6 0.0 collective-permute-done.4.refs_8_
  16.6 1.6 %collective-permute-start.13 = (bf16[8,8192]{1,0:T(8,128)(2,1)S(1)}, bf16[8,8192]{1,0:T(8,128)(2,1)S(1)}, u32[]{:S(2)}, u32[]{:S(2)}) collective-permute-start(bf16[8,8192]{1,0:T(8,128)(2,1)S(1)} %collective-permute-done.4.refs_8_), channel_id=1, source_target_pairs={{0,2},{1,3},{2,0},{3,1},{4,6},{5,7},{6,4},{7,5},{8,10},{9,11},{10,... | collective-permute-start | bytes 393224 | tf_op jit(solution)/shard_map/ppermute | solution.py:195
  18.2 1.6 %collective-permute-start.5 = (bf16[8,8192]{1,0:T(8,128)(2,1)S(1)}, bf16[8,8192]{1,0:T(8,128)(2,1)S(1)}, u32[]{:S(2)}, u32[]{:S(2)}) collective-permute-start(bf16[8,8192]{1,0:T(8,128)(2,1)S(1)} %collective-permute-done.4.refs_8_), channel_id=1, source_target_pairs={{0,4},{1,5},{2,6},{3,7},{4,0},{5,1},{6,2},{7,3},{8,12},{9,13},{10,... | collective-permute-start | bytes 393224 | tf_op jit(solution)/shard_map/ppermute | solution.py:195
  19.8 0.8 %collective-permute-start.11 = (bf16[8,8192]{1,0:T(8,128)(2,1)S(1)}, bf16[8,8192]{1,0:T(8,128)(2,1)S(1)}, u32[]{:S(2)}, u32[]{:S(2)}) collective-permute-start(bf16[8,8192]{1,0:T(8,128)(2,1)S(1)} %collective-permute-done.4.refs_8_), channel_id=1, source_target_pairs={{0,6},{1,7},{2,4},{3,5},{4,2},{5,3},{6,0},{7,1},{8,14},{9,15},{10,... | collective-permute-start | bytes 393224 | tf_op jit(solution)/shard_map/ppermute | solution.py:195
  20.6 1.0 %collective-permute-done.1.refs_6_ = bf16[8,8192]{1,0:T(8,128)(2,1)S(1)} collective-permute-done((bf16[8,8192]{1,0:T(8,128)(2,1)S(1)}, bf16[8,8192]{1,0:T(8,128)(2,1)S(1)}, u32[]{:S(2)}, u32[]{:S(2)}) %collective-permute-start.1) | collective-permute-done | bytes 131104 | tf_op jit(solution)/shard_map/ppermute | solution.py:195
  21.6 0.0 collective-permute-start.9
  21.6 0.1 collective-permute-done.13.refs_14_
  21.7 0.4 collective-permute-start.14
  22.1 1.8 %collective-permute-done.5.refs_10_ = bf16[8,8192]{1,0:T(8,128)(2,1)S(1)} collective-permute-done((bf16[8,8192]{1,0:T(8,128)(2,1)S(1)}, bf16[8,8192]{1,0:T(8,128)(2,1)S(1)}, u32[]{:S(2)}, u32[]{:S(2)}) %collective-permute-start.5) | collective-permute-done | bytes 131104 | tf_op jit(solution)/shard_map/ppermute | solution.py:195
  23.9 0.5 %collective-permute-start.7 = (bf16[8,8192]{1,0:T(8,128)(2,1)S(1)}, bf16[8,8192]{1,0:T(8,128)(2,1)S(1)}, u32[]{:S(2)}, u32[]{:S(2)}) collective-permute-start(bf16[8,8192]{1,0:T(8,128)(2,1)S(1)} %collective-permute-done.2.refs_4_), channel_id=1, source_target_pairs={{0,1},{1,0},{2,3},{3,2},{4,5},{5,4},{6,7},{7,6},{8,9},{9,8},{10,11... | collective-permute-start | bytes 393224 | tf_op jit(solution)/shard_map/ppermute | solution.py:195
  24.4 2.1 %collective-permute-done.11.refs_12_ = bf16[8,8192]{1,0:T(8,128)(2,1)S(1)} collective-permute-done((bf16[8,8192]{1,0:T(8,128)(2,1)S(1)}, bf16[8,8192]{1,0:T(8,128)(2,1)S(1)}, u32[]{:S(2)}, u32[]{:S(2)}) %collective-permute-start.11) | collective-permute-done | bytes 131104 | tf_op jit(solution)/shard_map/ppermute | solution.py:195
  26.6 0.0 collective-permute-start.12
  26.6 0.0 collective-permute-done.9.refs_9_
  26.6 0.5 %collective-permute-start.8 = (bf16[8,8192]{1,0:T(8,128)(2,1)S(1)}, bf16[8,8192]{1,0:T(8,128)(2,1)S(1)}, u32[]{:S(2)}, u32[]{:S(2)}) collective-permute-start(bf16[8,8192]{1,0:T(8,128)(2,1)S(1)} %collective-permute-done.1.refs_6_), channel_id=1, source_target_pairs={{0,1},{1,0},{2,3},{3,2},{4,5},{5,4},{6,7},{7,6},{8,9},{9,8},{10,11... | collective-permute-start | bytes 393224 | tf_op jit(solution)/shard_map/ppermute | solution.py:195
  27.1 0.0 collective-permute-done.14.refs_15_
  27.1 0.1 collective-permute-start.10
  27.2 0.8 %collective-permute-done.12.refs_13_ = bf16[8,8192]{1,0:T(8,128)(2,1)S(1)} collective-permute-done((bf16[8,8192]{1,0:T(8,128)(2,1)S(1)}, bf16[8,8192]{1,0:T(8,128)(2,1)S(1)}, u32[]{:S(2)}, u32[]{:S(2)}) %collective-permute-start.12) | collective-permute-done | bytes 131104 | tf_op jit(solution)/shard_map/ppermute | solution.py:195
  27.9 0.2 collective-permute-done.8.refs_7_
  28.1 0.3 collective-permute-done.10.refs_11_
  28.4 2.2 %delta.1 = (bf16[16,16,512]{2,1,0:T(8,128)(2,1)}, bf16[128,8192]{1,0:T(8,128)(2,1)S(1)}) custom-call(bf16[8,8192]{1,0:T(8,128)(2,1)S(1)} %attend.1.after.refs_0_, bf16[8,8192]{1,0:T(8,128)(2,1)S(1)} %collective-permute-done.refs_1_, bf16[8,8192]{1,0:T(8,128)(2,1)S(1)} %collective-permute-done.3.refs_2_, bf16[8,8192]{1,0:T(8,128)(2,1)S(1)} %collective-permute-done.6.refs_3_, ...), custom_call_target="tpu_custom_call" | custom-call | flops 301989888 | bytes 8650752 | tf_op jit(solution)/shard_map/delta/pallas_call | solution.py:318
  30.6 5.3 %all-to-all-start = ((bf16[16,16,512]{2,1,0:T(8,128)(2,1)}), bf16[16,16,512]{2,1,0:T(8,128)(2,1)S(1)}, u32[]{:S(2)}, u32[]{:S(2)}) async-start(bf16[16,16,512]{2,1,0:T(8,128)(2,1)} %get-tuple-element.38), calls=%async_computation | async-start | bytes 524288 | tf_op jit(solution)/shard_map/all_to_all | solution.py:408
  35.9 0.0 copy-start
  35.9 3.4 %copy-done = bf16[8192,512]{1,0:T(8,128)(2,1)S(1)} copy-done((bf16[8192,512]{1,0:T(8,128)(2,1)S(1)}, bf16[8192,512]{1,0:T(8,128)(2,1)}, u32[]{:S(2)}) %copy-start) | copy-done | bytes 8388632
  39.3 2.4 %base.1.base_ref = f32[128,512]{1,0:T(8,128)S(1)} custom-call(bf16[128,8192]{1,0:T(8,128)(2,1)S(1)} %get-tuple-element.35.a_ref, bf16[8192,512]{1,0:T(8,128)(2,1)S(1)} %copy-done, bf16[128,128]{1,0:T(8,128)(2,1)S(1)} %get-tuple-element.36.order_ref), custom_call_target="tpu_custom_call" | custom-call | flops 1342177280 | bytes 10747904 | tf_op jit(solution)/shard_map/base/pallas_call | solution.py:350
  41.7 4.3 %all-to-all-done.delta_ref = bf16[16,16,512]{2,1,0:T(8,128)(2,1)S(1)} async-done(((bf16[16,16,512]{2,1,0:T(8,128)(2,1)}), bf16[16,16,512]{2,1,0:T(8,128)(2,1)S(1)}, u32[]{:S(2)}, u32[]{:S(2)}) %all-to-all-start) | async-done | bytes 262176 | tf_op jit(solution)/shard_map/all_to_all | solution.py:408
  45.9 0.8 %join.1 = bf16[2,64,512]{2,1,0:T(8,128)(2,1)} custom-call(f32[128,512]{1,0:T(8,128)S(1)} %base.1.base_ref, bf16[128,256]{1,0:T(8,128)(2,1)S(1)} %get-tuple-element.37.place_ref, bf16[16,16,512]{2,1,0:T(8,128)(2,1)S(1)} %all-to-all-done.delta_ref), custom_call_target="tpu_custom_call" | custom-call | tf_op jit(solution)/shard_map/join/pallas_call | solution.py:377
  (7 shorter events, 0.0 us)
Async XLA Ops:
  6.1 10.5 %collective-permute-start.4 = (bf16[8,8192]{1,0:T(8,128)(2,1)S(1)}, bf16[8,8192]{1,0:T(8,128)(2,1)S(1)}, u32[]{:S(2)}, u32[]{:S(2)}) collective-permute-start(bf16[8,8192]{1,0:T(8,128)(2,1)S(1)} %attend.1.after.refs_0_), channel_id=1, source_target_pairs={{0,8},{1,9},{2,10},{3,11},{4,12},{5,13},{6,14},{7,15},{8,0},{9,1},... | collective-permute-start | bytes 393224 | tf_op jit(solution)/shard_map/ppermute | solution.py:195
  10.2 9.6 %collective-permute-start.3 = (bf16[8,8192]{1,0:T(8,128)(2,1)S(1)}, bf16[8,8192]{1,0:T(8,128)(2,1)S(1)}, u32[]{:S(2)}, u32[]{:S(2)}) collective-permute-start(bf16[8,8192]{1,0:T(8,128)(2,1)S(1)} %attend.1.after.refs_0_), channel_id=1, source_target_pairs={{0,6},{1,7},{2,4},{3,5},{4,2},{5,3},{6,0},{7,1},{8,14},{9,15},{10,... | collective-permute-start | bytes 393224 | tf_op jit(solution)/shard_map/ppermute | solution.py:195
  12.7 7.0 %collective-permute-start.2 = (bf16[8,8192]{1,0:T(8,128)(2,1)S(1)}, bf16[8,8192]{1,0:T(8,128)(2,1)S(1)}, u32[]{:S(2)}, u32[]{:S(2)}) collective-permute-start(bf16[8,8192]{1,0:T(8,128)(2,1)S(1)} %attend.1.after.refs_0_), channel_id=1, source_target_pairs={{0,2},{1,3},{2,0},{3,1},{4,6},{5,7},{6,4},{7,5},{8,10},{9,11},{10,... | collective-permute-start | bytes 393224 | tf_op jit(solution)/shard_map/ppermute | solution.py:195
  13.2 8.3 %collective-permute-start.1 = (bf16[8,8192]{1,0:T(8,128)(2,1)S(1)}, bf16[8,8192]{1,0:T(8,128)(2,1)S(1)}, u32[]{:S(2)}, u32[]{:S(2)}) collective-permute-start(bf16[8,8192]{1,0:T(8,128)(2,1)S(1)} %attend.1.after.refs_0_), channel_id=1, source_target_pairs={{0,4},{1,5},{2,6},{3,7},{4,0},{5,1},{6,2},{7,3},{8,12},{9,13},{10,... | collective-permute-start | bytes 393224 | tf_op jit(solution)/shard_map/ppermute | solution.py:195
  16.6 5.1 %collective-permute-start.13 = (bf16[8,8192]{1,0:T(8,128)(2,1)S(1)}, bf16[8,8192]{1,0:T(8,128)(2,1)S(1)}, u32[]{:S(2)}, u32[]{:S(2)}) collective-permute-start(bf16[8,8192]{1,0:T(8,128)(2,1)S(1)} %collective-permute-done.4.refs_8_), channel_id=1, source_target_pairs={{0,2},{1,3},{2,0},{3,1},{4,6},{5,7},{6,4},{7,5},{8,10},{9,11},{10,... | collective-permute-start | bytes 393224 | tf_op jit(solution)/shard_map/ppermute | solution.py:195
  18.2 5.7 %collective-permute-start.5 = (bf16[8,8192]{1,0:T(8,128)(2,1)S(1)}, bf16[8,8192]{1,0:T(8,128)(2,1)S(1)}, u32[]{:S(2)}, u32[]{:S(2)}) collective-permute-start(bf16[8,8192]{1,0:T(8,128)(2,1)S(1)} %collective-permute-done.4.refs_8_), channel_id=1, source_target_pairs={{0,4},{1,5},{2,6},{3,7},{4,0},{5,1},{6,2},{7,3},{8,12},{9,13},{10,... | collective-permute-start | bytes 393224 | tf_op jit(solution)/shard_map/ppermute | solution.py:195
  19.8 4.2 %collective-permute-start = (bf16[8,8192]{1,0:T(8,128)(2,1)S(1)}, bf16[8,8192]{1,0:T(8,128)(2,1)S(1)}, u32[]{:S(2)}, u32[]{:S(2)}) collective-permute-start(bf16[8,8192]{1,0:T(8,128)(2,1)S(1)} %attend.1.after.refs_0_), channel_id=1, source_target_pairs={{0,1},{1,0},{2,3},{3,2},{4,5},{5,4},{6,7},{7,6},{8,9},{9,8},{10,11... | collective-permute-start | bytes 393224 | tf_op jit(solution)/shard_map/ppermute | solution.py:195
  19.8 6.8 %collective-permute-start.11 = (bf16[8,8192]{1,0:T(8,128)(2,1)S(1)}, bf16[8,8192]{1,0:T(8,128)(2,1)S(1)}, u32[]{:S(2)}, u32[]{:S(2)}) collective-permute-start(bf16[8,8192]{1,0:T(8,128)(2,1)S(1)} %collective-permute-done.4.refs_8_), channel_id=1, source_target_pairs={{0,6},{1,7},{2,4},{3,5},{4,2},{5,3},{6,0},{7,1},{8,14},{9,15},{10,... | collective-permute-start | bytes 393224 | tf_op jit(solution)/shard_map/ppermute | solution.py:195
  21.6 5.0 %collective-permute-start.9 = (bf16[8,8192]{1,0:T(8,128)(2,1)S(1)}, bf16[8,8192]{1,0:T(8,128)(2,1)S(1)}, u32[]{:S(2)}, u32[]{:S(2)}) collective-permute-start(bf16[8,8192]{1,0:T(8,128)(2,1)S(1)} %collective-permute-done.4.refs_8_), channel_id=1, source_target_pairs={{0,1},{1,0},{2,3},{3,2},{4,5},{5,4},{6,7},{7,6},{8,9},{9,8},{10,11... | collective-permute-start | bytes 393224 | tf_op jit(solution)/shard_map/ppermute | solution.py:195
  21.7 5.4 %collective-permute-start.14 = (bf16[8,8192]{1,0:T(8,128)(2,1)S(1)}, bf16[8,8192]{1,0:T(8,128)(2,1)S(1)}, u32[]{:S(2)}, u32[]{:S(2)}) collective-permute-start(bf16[8,8192]{1,0:T(8,128)(2,1)S(1)} %collective-permute-done.13.refs_14_), channel_id=1, source_target_pairs={{0,1},{1,0},{2,3},{3,2},{4,5},{5,4},{6,7},{7,6},{8,9},{9,8},{10,11... | collective-permute-start | bytes 393224 | tf_op jit(solution)/shard_map/ppermute | solution.py:195
  23.9 4.0 %collective-permute-start.6 = (bf16[8,8192]{1,0:T(8,128)(2,1)S(1)}, bf16[8,8192]{1,0:T(8,128)(2,1)S(1)}, u32[]{:S(2)}, u32[]{:S(2)}) collective-permute-start(bf16[8,8192]{1,0:T(8,128)(2,1)S(1)} %collective-permute-done.3.refs_2_), channel_id=1, source_target_pairs={{0,1},{1,0},{2,3},{3,2},{4,5},{5,4},{6,7},{7,6},{8,9},{9,8},{10,11... | collective-permute-start | bytes 393224 | tf_op jit(solution)/shard_map/ppermute | solution.py:195
  23.9 4.0 %collective-permute-start.7 = (bf16[8,8192]{1,0:T(8,128)(2,1)S(1)}, bf16[8,8192]{1,0:T(8,128)(2,1)S(1)}, u32[]{:S(2)}, u32[]{:S(2)}) collective-permute-start(bf16[8,8192]{1,0:T(8,128)(2,1)S(1)} %collective-permute-done.2.refs_4_), channel_id=1, source_target_pairs={{0,1},{1,0},{2,3},{3,2},{4,5},{5,4},{6,7},{7,6},{8,9},{9,8},{10,11... | collective-permute-start | bytes 393224 | tf_op jit(solution)/shard_map/ppermute | solution.py:195
  26.6 1.3 %collective-permute-start.12 = (bf16[8,8192]{1,0:T(8,128)(2,1)S(1)}, bf16[8,8192]{1,0:T(8,128)(2,1)S(1)}, u32[]{:S(2)}, u32[]{:S(2)}) collective-permute-start(bf16[8,8192]{1,0:T(8,128)(2,1)S(1)} %collective-permute-done.11.refs_12_), channel_id=1, source_target_pairs={{0,1},{1,0},{2,3},{3,2},{4,5},{5,4},{6,7},{7,6},{8,9},{9,8},{10,11... | collective-permute-start | bytes 393224 | tf_op jit(solution)/shard_map/ppermute | solution.py:195
  26.6 1.5 %collective-permute-start.8 = (bf16[8,8192]{1,0:T(8,128)(2,1)S(1)}, bf16[8,8192]{1,0:T(8,128)(2,1)S(1)}, u32[]{:S(2)}, u32[]{:S(2)}) collective-permute-start(bf16[8,8192]{1,0:T(8,128)(2,1)S(1)} %collective-permute-done.1.refs_6_), channel_id=1, source_target_pairs={{0,1},{1,0},{2,3},{3,2},{4,5},{5,4},{6,7},{7,6},{8,9},{9,8},{10,11... | collective-permute-start | bytes 393224 | tf_op jit(solution)/shard_map/ppermute | solution.py:195
  27.1 1.3 %collective-permute-start.10 = (bf16[8,8192]{1,0:T(8,128)(2,1)S(1)}, bf16[8,8192]{1,0:T(8,128)(2,1)S(1)}, u32[]{:S(2)}, u32[]{:S(2)}) collective-permute-start(bf16[8,8192]{1,0:T(8,128)(2,1)S(1)} %collective-permute-done.5.refs_10_), channel_id=1, source_target_pairs={{0,1},{1,0},{2,3},{3,2},{4,5},{5,4},{6,7},{7,6},{8,9},{9,8},{10,11... | collective-permute-start | bytes 393224 | tf_op jit(solution)/shard_map/ppermute | solution.py:195
  30.6 15.3 %all-to-all-start = ((bf16[16,16,512]{2,1,0:T(8,128)(2,1)}), bf16[16,16,512]{2,1,0:T(8,128)(2,1)S(1)}, u32[]{:S(2)}, u32[]{:S(2)}) async-start(bf16[16,16,512]{2,1,0:T(8,128)(2,1)} %get-tuple-element.38), calls=%async_computation | async-start | bytes 524288 | tf_op jit(solution)/shard_map/all_to_all | solution.py:408
  35.9 3.4 %copy-start = (bf16[8192,512]{1,0:T(8,128)(2,1)S(1)}, bf16[8192,512]{1,0:T(8,128)(2,1)}, u32[]{:S(2)}) copy-start(bf16[8192,512]{1,0:T(8,128)(2,1)} %w_ref.1) | copy-start | bytes 25165828

commit v8 on v7

--- a/solution.py
+++ b/solution.py
@@ -13,7 +13,7 @@
 GROUP = HQ // KVH
 MOST = 8
 RING = 16
-ORDER = [0,1,6,7,2,3,4,5,8,9,12,13,14,15,10,11]
+ORDER = [0, 1, 8, 9, 12, 13, 14, 15, 10, 11, 4, 5, 2, 3, 6, 7]
 F32 = jnp.float32
 BF16 = jnp.bfloat16
 NT = (((1,), (1,)), ((), ()))
@@ -39,10 +39,55 @@
     return lax.dot_general(a, b, NT, preferred_element_type=F32)
 
 
+def sender(slot, me, parts):
+    return me ^ slot if parts == RING else slot
+
+
+def write_plan(rows, count_ref, rank_ref, owner_ref, pick_ref, place_ref, order_ref):
+    me = lax.axis_index("tensor")
+    slots, total = pick_ref.shape
+    steps = slots // MOST
+    each = steps * rows
+    parts = total // each
+    requests = parts * rows
+
+    def adapter_of(block):
+        first = jnp.zeros(block.shape, jnp.int32)
+        amount = jnp.zeros(block.shape, jnp.int32)
+        start = jnp.int32(0)
+        for a in range(count_ref.shape[0]):
+            owned = (owner_ref[a] <= block) & (block < owner_ref[a] + rank_ref[a])
+            first = jnp.where(owned, start, first)
+            amount = jnp.where(owned, count_ref[a], amount)
+            start = start + count_ref[a]
+        return first, amount
+
+    def row_place(index):
+        device = sender(index // each, me, parts)
+        return device * rows + index % rows, (index % each) // rows
+
+    row = iota((slots, 1), 0)
+    nth = row % MOST
+    first, amount = adapter_of(jnp.zeros_like(row) + me)
+    request, step = row_place(iota((1, total), 1))
+    pick = (request == first + nth) & (nth < amount) & (step == row // MOST)
+    pick_ref[...] = one_hot(pick)
+
+    request, step = row_place(iota((1, total), 1))
+    order_ref[...] = one_hot(iota((total, total), 0) == step * requests + request)
+
+    entry = iota((1, parts * slots), 1)
+    nth = entry % MOST
+    first, amount = adapter_of(entry // slots)
+    goal = jnp.where(nth < amount, (entry % slots) // MOST * requests + first + nth, -1)
+    place_ref[...] = one_hot(iota((total, parts * slots), 0) == goal)
+
+
 def attend_kernel(
-    len_hbm, q_hbm, nk_hbm, nv_hbm, k_hbm, v_hbm, out_ref,
-    len_ref, q_ref, nk_ref, nv_ref, k_ref, v_ref, turned_q, nks, nvs, raw, mixed,
-    small_sems, sems,
+    len_hbm, q_hbm, nk_hbm, nv_hbm, k_hbm, v_hbm, d_hbm, u_hbm, count_hbm, rank_hbm, owner_hbm,
+    out_ref, d_ref, u_ref, pick_ref, place_ref, order_ref,
+    len_ref, count_ref, rank_ref, owner_ref, q_ref, nk_ref, nv_ref, k_ref, v_ref, turned_q, nks, nvs, raw, mixed,
+    small_sems, sems, store_sems,
 ):
     steps, rows, width = q_ref.shape
     cache = k_ref.shape[1]
@@ -53,7 +98,15 @@
     small = [
         pltpu.make_async_copy(src, dst, small_sems.at[i])
         for i, (src, dst) in enumerate(
-            ((q_hbm, q_ref), (len_hbm, len_ref), (nk_hbm, nk_ref), (nv_hbm, nv_ref))
+            (
+                (q_hbm, q_ref),
+                (nk_hbm, nk_ref),
+                (nv_hbm, nv_ref),
+                (len_hbm, len_ref),
+                (count_hbm, count_ref),
+                (rank_hbm, rank_ref),
+                (owner_hbm, owner_ref),
+            )
         )
     ]
     pieces = [pl.ds(i * (cache // cuts), cache // cuts) for i in range(cuts)]
@@ -67,9 +120,17 @@
         ]
         for j, (src, dst) in enumerate(((k_hbm, k_ref), (v_hbm, v_ref)))
     ]
+    deep = d_ref.shape[0] // store_sems.shape[1]
+    store = [
+        pltpu.make_async_copy(
+            src.at[0, pl.ds(i * deep, deep)], dst.at[pl.ds(i * deep, deep)], store_sems.at[j, i]
+        )
+        for j, (src, dst) in enumerate(((d_hbm, d_ref), (u_hbm, u_ref)))
+        for i in range(store_sems.shape[1])
+    ]
     queue = [keys[0], values[0], keys[1]]
     for r in range(rows):
-        queue += [values[r + 1]] if r + 1 < rows else [[]]
+        queue += [values[r + 1]] if r + 1 < rows else [store]
         queue += [keys[r + 2]] if r + 2 < rows else []
     for copy in small + queue[0] + queue[1] + queue[2]:
         copy.start()
@@ -98,6 +159,8 @@
         fresh = [src[t].astype(F32) for t in range(steps)]
         fresh.append(jnp.zeros((16 - both, src.shape[2]), F32))
         dst[...] = jnp.concatenate(fresh, axis=0).astype(BF16)
+
+    write_plan(rows, count_ref, rank_ref, owner_ref, pick_ref, place_ref, order_ref)
 
     scale = HD ** (-0.5)
     pairs = [
@@ -151,19 +214,38 @@
         for g in range(GROUP):
             at = (k * GROUP + g) * HD
             out_ref[:, at : at + HD] = heads[g].astype(BF16)
-
-
-def attend(queries, new_keys, new_values, cache_keys, cache_values, kv_len):
+    for copy in store:
+        copy.wait()
+
+
+def attend(
+    queries,
+    new_keys,
+    new_values,
+    cache_keys,
+    cache_values,
+    kv_len,
+    store_down,
+    store_up,
+    tables,
+    parts,
+):
     steps, rows, width = queries.shape
     cache, kv_width = cache_keys.shape[1:]
     pack = steps * GROUP
+    rank_w = store_down.shape[2]
+    total = parts * steps * rows
+    slots = steps * MOST
+    shapes = [(steps * rows, width), (width, rank_w), (width, rank_w)]
+    shapes += [(slots, total), (total, parts * slots), (total, total)]
     return pl.pallas_call(
         attend_kernel,
-        out_shape=jax.ShapeDtypeStruct((steps * rows, width), BF16),
-        in_specs=[pl.BlockSpec(memory_space=pl.ANY)] * 6,
-        out_specs=pl.BlockSpec(memory_space=pltpu.VMEM),
+        out_shape=[jax.ShapeDtypeStruct(shape, BF16) for shape in shapes],
+        in_specs=[pl.BlockSpec(memory_space=pl.ANY)] * 11,
+        out_specs=[pl.BlockSpec(memory_space=pltpu.VMEM)] * len(shapes),
         scratch_shapes=[
             pltpu.SMEM(kv_len.shape, jnp.int32),
+            *[pltpu.SMEM(table.shape, jnp.int32) for table in tables],
             pltpu.VMEM(queries.shape, BF16),
             pltpu.VMEM(new_keys.shape, BF16),
             pltpu.VMEM(new_values.shape, BF16),
@@ -174,8 +256,9 @@
             pltpu.VMEM((16, kv_width), BF16),
             pltpu.VMEM((2, cache, KVH * pack), F32),
             pltpu.VMEM((rows, KVH, pack, HD), F32),
-            pltpu.SemaphoreType.DMA((4,)),
+            pltpu.SemaphoreType.DMA((7,)),
             pltpu.SemaphoreType.DMA((rows, 2, 2)),
+            pltpu.SemaphoreType.DMA((2, 4)),
         ],
         compiler_params=pltpu.CompilerParams(vmem_limit_bytes=32 * 2**20),
         cost_estimate=pl.CostEstimate(
@@ -184,110 +267,41 @@
             transcendentals=rows * steps * HQ * cache,
         ),
         name="attend",
-    )(*in_hbm(kv_len, queries, new_keys, new_values, cache_keys, cache_values))
-
-
-def sender(slot, me, parts):
-    return me ^ slot if parts == RING else slot
+    )(
+        *in_hbm(
+            kv_len,
+            queries,
+            new_keys,
+            new_values,
+            cache_keys,
+            cache_values,
+            store_down,
+            store_up,
+            *tables,
+        )
+    )
 
 
 def swap(x, bits, parts):
     return lax.ppermute(x, "tensor", [(i, i ^ bits) for i in range(parts)])
 
 
-def prepare_kernel(
-    rows, count_ref, rank_ref, owner_ref, after, d_hbm, u_hbm,
-    d_ref, u_ref, pick_ref, place_ref, order_ref, sems,
-):
-    me = lax.axis_index("tensor")
-    cuts = sems.shape[1]
-    deep = d_ref.shape[0] // cuts
-    copies = []
-    for j, (src, dst) in enumerate(((d_hbm, d_ref), (u_hbm, u_ref))):
-        for i in range(cuts):
-            at = pl.ds(i * deep, deep)
-            copies.append(pltpu.make_async_copy(src.at[0, at], dst.at[at], sems.at[j, i]))
-            copies[-1].start()
-    slots, total = pick_ref.shape
-    steps = slots // MOST
-    each = steps * rows
-    parts = total // each
-    requests = parts * rows
-
-    def adapter_of(block):
-        first = jnp.zeros(block.shape, jnp.int32)
-        amount = jnp.zeros(block.shape, jnp.int32)
-        start = jnp.int32(0)
-        for a in range(count_ref.shape[0]):
-            owned = (owner_ref[a] <= block) & (block < owner_ref[a] + rank_ref[a])
-            first = jnp.where(owned, start, first)
-            amount = jnp.where(owned, count_ref[a], amount)
-            start = start + count_ref[a]
-        return first, amount
-
-    def row_place(index):
-        device = sender(index // each, me, parts)
-        return device * rows + index % rows, (index % each) // rows
-
-    row = iota((slots, 1), 0)
-    nth = row % MOST
-    first, amount = adapter_of(jnp.zeros_like(row) + me)
-    request, step = row_place(iota((1, total), 1))
-    pick = (request == first + nth) & (nth < amount) & (step == row // MOST)
-    pick_ref[...] = one_hot(pick)
-
-    request, step = row_place(iota((total, total), 1))
-    order_ref[...] = one_hot(iota((total, total), 0) == step * requests + request)
-
-    entry = iota((1, parts * slots), 1)
-    nth = entry % MOST
-    first, amount = adapter_of(entry // slots)
-    goal = jnp.where(nth < amount, (entry % slots) // MOST * requests + first + nth, -1)
-    place_ref[...] = one_hot(iota((total, parts * slots), 0) == goal)
-    for copy in copies:
-        copy.wait()
-
-
-def prepare(after, store_down, store_up, tables, steps, rows, parts):
-    width, rank_w = store_down.shape[1:]
-    total = parts * steps * rows
-    slots = steps * MOST
-    vmem = pl.BlockSpec(memory_space=pltpu.VMEM)
-    shapes = [(width, rank_w)] * 2 + [(slots, total), (total, parts * slots), (total, total)]
-    return pl.pallas_call(
-        functools.partial(prepare_kernel, rows),
-        out_shape=[jax.ShapeDtypeStruct(shape, BF16) for shape in shapes],
-        in_specs=[pl.BlockSpec(memory_space=pltpu.SMEM)] * 3
-        + [pl.BlockSpec(memory_space=pl.ANY)] * 3,
-        out_specs=[vmem] * len(shapes),
-        scratch_shapes=[pltpu.SemaphoreType.DMA((2, 4))],
-        compiler_params=pltpu.CompilerParams(vmem_limit_bytes=16 * 2**20),
-        cost_estimate=pl.CostEstimate(
-            flops=2 * 10**10, bytes_accessed=8 * width * rank_w, transcendentals=0
-        ),
-        name="prepare",
-    )(*in_hbm(*tables), after, *in_hbm(store_down, store_up))
-
-
-def gather(block, prepared, parts):
+def gather(block, parts):
     if parts != RING:
         whole = lax.all_gather(block, "tensor")
-        return [whole[i] for i in range(parts)], prepared
+        return [whole[i] for i in range(parts)]
     core, y, near, far = 1, 2, 4, 8
     held = {0: block}
     held[far] = swap(block, far, parts)
     held[near] = swap(block, near, parts)
     held[y] = swap(block, y, parts)
-    held[near | y] = swap(block, near | y, parts)
-    held[far], *prepared = lax.optimization_barrier((held[far], *prepared))
+    held[near | y] = swap(held[y], near, parts)
     held[far | y] = swap(held[far], y, parts)
     held[far | near | y] = swap(held[far], near | y, parts)
     held[far | near] = swap(held[far], near, parts)
-    names = (near, y, near | y, far | near)
-    held.update(zip(names, lax.optimization_barrier(tuple(held[n] for n in names))))
     for slot in list(held):
         held[slot | core] = swap(held[slot], core, parts)
-    return [held[slot] for slot in range(parts)], prepared
+    return [held[slot] for slot in range(parts)]
 
 
 def delta_kernel(at_slot, *refs):
@@ -401,9 +415,19 @@
     parts = lax.axis_size("tensor")
     steps, rows, width = queries.shape
     tables = (adapter_rows, adapter_rank, adapter_owner)
-    attended = attend(queries, new_keys, new_values, cache_keys, cache_values, kv_len)
-    prepared = prepare(attended, store_down, store_up, tables, steps, rows, parts)
-    blocks, (down, up, pick, place, order) = gather(attended, prepared, parts)
+    attended, down, up, pick, place, order = attend(
+        queries,
+        new_keys,
+        new_values,
+        cache_keys,
+        cache_values,
+        kv_len,
+        store_down,
+        store_up,
+        tables,
+        parts,
+    )
+    blocks = gather(attended, parts)
     send, gathered = deltas(blocks, pick, down, up)
     delta = lax.all_to_all(send, "tensor", split_axis=0, concat_axis=0, tiled=True)
     base = base_part(gathered, out_weight, order)

time: 47.1 us -> 47.7 us (1.013)
  Pallas kernels: 14.4 us -> 11.6 us
  waiting for transfers between devices: 10.6 us -> 13.4 us
  starting transfers between devices: 18.4 us -> 19 us
    ppermute x15, waiting for transfers between devices: 6.33 us -> 9.16 us  [swap(): return lax.ppermute(x, 'tensor', [(i, i ^ bits) for i in range(parts)])]
    pallas_call x2 -> x1, Pallas kernels: 8.97 us -> 6.14 us  [attend(): pl.pallas_call(attend_kernel, out_shape=[jax.ShapeDtypeStruct(shape, BF16...]
  transfers between devices with their start and end apart: 16 -> 16, of which waited for: 8 -> 7; matrix products, arithmetic and copies ran while one was open for 0% -> 0% of each run, Pallas kernels for 11% -> 5%
where the time goes in v8:
time: 47.7 us; the launch traced here: 47.4 us
  starting transfers between devices  19 us (40%)
  waiting for transfers between devices  13.4 us (28%)
  Pallas kernels  11.6 us (24%)
  local copies, waits for them, and re-layouts  3.38 us (7%)
    ppermute x15, starting transfers between devices, swap(): return lax.ppermute(x, 'tensor', [(i, i ^ bits) for i in range(parts)])  13.4 us
    ppermute x15, waiting for transfers between devices, swap(): return lax.ppermute(x, 'tensor', [(i, i ^ bits) for i in range(parts)])  9.16 us
    pallas_call x1, Pallas kernels, attend(): pl.pallas_call(attend_kernel, out_shape=[jax.ShapeDtypeStruct(shape, BF16...  6.14 us
    all_to_all x1, starting transfers between devices, per_device(): lax.all_to_all(send, 'tensor', split_axis=0, concat_axis=0, tiled=True)  5.59 us
    all_to_all x1, waiting for transfers between devices, per_device(): lax.all_to_all(send, 'tensor', split_axis=0, concat_axis=0, tiled=True)  4.25 us
    unnamed x2, local copies, waits for them, and re-layouts  3.38 us
    pallas_call x1, Pallas kernels, base_part(): pl.pallas_call(base_kernel, out_shape=jax.ShapeDtypeStruct((total, cols),...  2.4 us
    pallas_call x1, Pallas kernels, deltas(): pl.pallas_call(functools.partial(delta_kernel, at_slot), out_shape=(jax.S...  2.2 us
  transfers between devices with their start and end apart: 16, of which 7 were waited for; matrix products, arithmetic and copies ran while one was open for 0% of the time, Pallas kernels for 5%

profile of v8, /device:TPU:0, one launch (start us, length us, event | category | flops | bytes accessed | tf_op | source)
XLA Modules:
  0.0 47.4 jit_solution(16817417188000989196)
XLA Ops:
  0.0 6.1 %attend.1 = (bf16[8,8192]{1,0:T(8,128)(2,1)S(1)}, bf16[8192,128]{1,0:T(8,128)(2,1)S(1)}, bf16[8192,128]{1,0:T(8,128)(2,1)S(1)}, bf16[16,128]{1,0:T(8,128)(2,1)S(...) custom-call(s32[4]{0:T(128)} %len_hbm.1, bf16[2,4,8192]{2,1,0:T(4,128)(2,1)} %q_hbm.1, ...), custom_call_target="tpu_custom_call" | custom-call | flops 134217728 | bytes 8388608 | tf_op jit(solution)/shard_map/attend/pallas_call | solution.py:241
  6.2 3.0 %collective-permute-start.11 = (bf16[8,8192]{1,0:T(8,128)(2,1)S(1)}, bf16[8,8192]{1,0:T(8,128)(2,1)S(1)}, u32[]{:S(2)}, u32[]{:S(2)}) collective-permute-start(bf16[8,8192]{1,0:T(8,128)(2,1)S(1)} %get-tuple-element.13.refs_0_), channel_id=1, source_target_pairs={{0,2},{1,3},{2,0},{3,1},{4,6},{5,7},{6,4},{7,5},{8,10},{9,11},{10,... | collective-permute-start | bytes 393224 | tf_op jit(solution)/shard_map/ppermute | solution.py:286
  9.2 1.6 %collective-permute-start.9 = (bf16[8,8192]{1,0:T(8,128)(2,1)S(1)}, bf16[8,8192]{1,0:T(8,128)(2,1)S(1)}, u32[]{:S(2)}, u32[]{:S(2)}) collective-permute-start(bf16[8,8192]{1,0:T(8,128)(2,1)S(1)} %get-tuple-element.13.refs_0_), channel_id=1, source_target_pairs={{0,4},{1,5},{2,6},{3,7},{4,0},{5,1},{6,2},{7,3},{8,12},{9,13},{10,... | collective-permute-start | bytes 393224 | tf_op jit(solution)/shard_map/ppermute | solution.py:286
  10.8 2.6 %collective-permute-start.1 = (bf16[8,8192]{1,0:T(8,128)(2,1)S(1)}, bf16[8,8192]{1,0:T(8,128)(2,1)S(1)}, u32[]{:S(2)}, u32[]{:S(2)}) collective-permute-start(bf16[8,8192]{1,0:T(8,128)(2,1)S(1)} %get-tuple-element.13.refs_0_), channel_id=1, source_target_pairs={{0,8},{1,9},{2,10},{3,11},{4,12},{5,13},{6,14},{7,15},{8,0},{9,1},... | collective-permute-start | bytes 393224 | tf_op jit(solution)/shard_map/ppermute | solution.py:286
  13.4 1.1 %collective-permute-start.13 = (bf16[8,8192]{1,0:T(8,128)(2,1)S(1)}, bf16[8,8192]{1,0:T(8,128)(2,1)S(1)}, u32[]{:S(2)}, u32[]{:S(2)}) collective-permute-start(bf16[8,8192]{1,0:T(8,128)(2,1)S(1)} %collective-permute-done.11.refs_12_), channel_id=1, source_target_pairs={{0,4},{1,5},{2,6},{3,7},{4,0},{5,1},{6,2},{7,3},{8,12},{9,13},{10,... | collective-permute-start | bytes 393224 | tf_op jit(solution)/shard_map/ppermute | solution.py:286
  14.5 1.4 %collective-permute-done.9.refs_10_ = bf16[8,8192]{1,0:T(8,128)(2,1)S(1)} collective-permute-done((bf16[8,8192]{1,0:T(8,128)(2,1)S(1)}, bf16[8,8192]{1,0:T(8,128)(2,1)S(1)}, u32[]{:S(2)}, u32[]{:S(2)}) %collective-permute-start.9) | collective-permute-done | bytes 131104 | tf_op jit(solution)/shard_map/ppermute | solution.py:286
  15.9 2.1 %collective-permute-done.1.refs_2_ = bf16[8,8192]{1,0:T(8,128)(2,1)S(1)} collective-permute-done((bf16[8,8192]{1,0:T(8,128)(2,1)S(1)}, bf16[8,8192]{1,0:T(8,128)(2,1)S(1)}, u32[]{:S(2)}, u32[]{:S(2)}) %collective-permute-start.1) | collective-permute-done | bytes 131104 | tf_op jit(solution)/shard_map/ppermute | solution.py:286
  17.9 0.5 %collective-permute-start.7 = (bf16[8,8192]{1,0:T(8,128)(2,1)S(1)}, bf16[8,8192]{1,0:T(8,128)(2,1)S(1)}, u32[]{:S(2)}, u32[]{:S(2)}) collective-permute-start(bf16[8,8192]{1,0:T(8,128)(2,1)S(1)} %collective-permute-done.1.refs_2_), channel_id=1, source_target_pairs={{0,2},{1,3},{2,0},{3,1},{4,6},{5,7},{6,4},{7,5},{8,10},{9,11},{10,... | collective-permute-start | bytes 393224 | tf_op jit(solution)/shard_map/ppermute | solution.py:286
  18.4 0.0 collective-permute-done.refs_1_
  18.4 4.0 %collective-permute-start.5 = (bf16[8,8192]{1,0:T(8,128)(2,1)S(1)}, bf16[8,8192]{1,0:T(8,128)(2,1)S(1)}, u32[]{:S(2)}, u32[]{:S(2)}) collective-permute-start(bf16[8,8192]{1,0:T(8,128)(2,1)S(1)} %collective-permute-done.1.refs_2_), channel_id=1, source_target_pairs={{0,6},{1,7},{2,4},{3,5},{4,2},{5,3},{6,0},{7,1},{8,14},{9,15},{10,... | collective-permute-start | bytes 393224 | tf_op jit(solution)/shard_map/ppermute | solution.py:286
  22.4 0.0 collective-permute-done.13.refs_14_
  22.4 0.0 collective-permute-start.3
  22.4 0.0 collective-permute-done.12.refs_13_
  22.4 0.1 collective-permute-start.2
  22.5 0.5 %collective-permute-start.14 = (bf16[8,8192]{1,0:T(8,128)(2,1)S(1)}, bf16[8,8192]{1,0:T(8,128)(2,1)S(1)}, u32[]{:S(2)}, u32[]{:S(2)}) collective-permute-start(bf16[8,8192]{1,0:T(8,128)(2,1)S(1)} %collective-permute-done.13.refs_14_), channel_id=1, source_target_pairs={{0,1},{1,0},{2,3},{3,2},{4,5},{5,4},{6,7},{7,6},{8,9},{9,8},{10,11... | collective-permute-start | bytes 393224 | tf_op jit(solution)/shard_map/ppermute | solution.py:286
  23.0 0.2 collective-permute-done.7.refs_8_
  23.2 2.2 %collective-permute-done.5.refs_6_ = bf16[8,8192]{1,0:T(8,128)(2,1)S(1)} collective-permute-done((bf16[8,8192]{1,0:T(8,128)(2,1)S(1)}, bf16[8,8192]{1,0:T(8,128)(2,1)S(1)}, u32[]{:S(2)}, u32[]{:S(2)}) %collective-permute-start.5) | collective-permute-done | bytes 131104 | tf_op jit(solution)/shard_map/ppermute | solution.py:286
  25.4 0.0 collective-permute-start.6
  25.4 2.0 %collective-permute-done.3.refs_4_ = bf16[8,8192]{1,0:T(8,128)(2,1)S(1)} collective-permute-done((bf16[8,8192]{1,0:T(8,128)(2,1)S(1)}, bf16[8,8192]{1,0:T(8,128)(2,1)S(1)}, u32[]{:S(2)}, u32[]{:S(2)}) %collective-permute-start.3) | collective-permute-done | bytes 131104 | tf_op jit(solution)/shard_map/ppermute | solution.py:286
  27.4 0.0 collective-permute-start.4
  27.4 0.0 collective-permute-done.2.refs_3_
  27.4 0.0 collective-permute-done.14.refs_15_
  27.4 0.0 collective-permute-done.8.refs_9_
  27.4 0.0 collective-permute-done.6.refs_7_
  27.4 1.3 %collective-permute-done.4.refs_5_ = bf16[8,8192]{1,0:T(8,128)(2,1)S(1)} collective-permute-done((bf16[8,8192]{1,0:T(8,128)(2,1)S(1)}, bf16[8,8192]{1,0:T(8,128)(2,1)S(1)}, u32[]{:S(2)}, u32[]{:S(2)}) %collective-permute-start.4) | collective-permute-done | bytes 131104 | tf_op jit(solution)/shard_map/ppermute | solution.py:286
  28.7 2.2 %delta.1 = (bf16[16,16,512]{2,1,0:T(8,128)(2,1)}, bf16[128,8192]{1,0:T(8,128)(2,1)S(1)}) custom-call(bf16[8,8192]{1,0:T(8,128)(2,1)S(1)} %get-tuple-element.13.refs_0_, bf16[8,8192]{1,0:T(8,128)(2,1)S(1)} %collective-permute-done.refs_1_, bf16[8,8192]{1,0:T(8,128)(2,1)S(1)} %collective-permute-done.1.refs_2_, ...), custom_call_target="tpu_custom_call" | custom-call | flops 301989888 | bytes 8650752 | tf_op jit(solution)/shard_map/delta/pallas_call | solution.py:332
  30.9 5.6 %all-to-all-start = ((bf16[16,16,512]{2,1,0:T(8,128)(2,1)}), bf16[16,16,512]{2,1,0:T(8,128)(2,1)S(1)}, u32[]{:S(2)}, u32[]{:S(2)}) async-start(bf16[16,16,512]{2,1,0:T(8,128)(2,1)} %get-tuple-element.20), calls=%async_computation | async-start | bytes 524288 | tf_op jit(solution)/shard_map/all_to_all | solution.py:432
  36.5 0.0 copy-start
  36.5 3.4 %copy-done = bf16[8192,512]{1,0:T(8,128)(2,1)S(1)} copy-done((bf16[8192,512]{1,0:T(8,128)(2,1)S(1)}, bf16[8192,512]{1,0:T(8,128)(2,1)}, u32[]{:S(2)}) %copy-start) | copy-done | bytes 8388632
  39.9 2.4 %base.1.base_ref = f32[128,512]{1,0:T(8,128)S(1)} custom-call(bf16[128,8192]{1,0:T(8,128)(2,1)S(1)} %get-tuple-element.17.a_ref, bf16[8192,512]{1,0:T(8,128)(2,1)S(1)} %copy-done, bf16[128,128]{1,0:T(8,128)(2,1)S(1)} %get-tuple-element.18.order_ref), custom_call_target="tpu_custom_call" | custom-call | flops 1342177280 | bytes 10747904 | tf_op jit(solution)/shard_map/base/pallas_call | solution.py:364
  42.3 4.3 %all-to-all-done.delta_ref = bf16[16,16,512]{2,1,0:T(8,128)(2,1)S(1)} async-done(((bf16[16,16,512]{2,1,0:T(8,128)(2,1)}), bf16[16,16,512]{2,1,0:T(8,128)(2,1)S(1)}, u32[]{:S(2)}, u32[]{:S(2)}) %all-to-all-start) | async-done | bytes 262176 | tf_op jit(solution)/shard_map/all_to_all | solution.py:432
  46.6 0.8 %join.1 = bf16[2,64,512]{2,1,0:T(8,128)(2,1)} custom-call(f32[128,512]{1,0:T(8,128)S(1)} %base.1.base_ref, bf16[128,256]{1,0:T(8,128)(2,1)S(1)} %get-tuple-element.19.place_ref, bf16[16,16,512]{2,1,0:T(8,128)(2,1)S(1)} %all-to-all-done.delta_ref), custom_call_target="tpu_custom_call" | custom-call | tf_op jit(solution)/shard_map/join/pallas_call | solution.py:391
  (6 shorter events, 0.0 us)
Async XLA Ops:
  6.2 7.2 %collective-permute-start.11 = (bf16[8,8192]{1,0:T(8,128)(2,1)S(1)}, bf16[8,8192]{1,0:T(8,128)(2,1)S(1)}, u32[]{:S(2)}, u32[]{:S(2)}) collective-permute-start(bf16[8,8192]{1,0:T(8,128)(2,1)S(1)} %get-tuple-element.13.refs_0_), channel_id=1, source_target_pairs={{0,2},{1,3},{2,0},{3,1},{4,6},{5,7},{6,4},{7,5},{8,10},{9,11},{10,... | collective-permute-start | bytes 393224 | tf_op jit(solution)/shard_map/ppermute | solution.py:286
  9.2 6.7 %collective-permute-start.9 = (bf16[8,8192]{1,0:T(8,128)(2,1)S(1)}, bf16[8,8192]{1,0:T(8,128)(2,1)S(1)}, u32[]{:S(2)}, u32[]{:S(2)}) collective-permute-start(bf16[8,8192]{1,0:T(8,128)(2,1)S(1)} %get-tuple-element.13.refs_0_), channel_id=1, source_target_pairs={{0,4},{1,5},{2,6},{3,7},{4,0},{5,1},{6,2},{7,3},{8,12},{9,13},{10,... | collective-permute-start | bytes 393224 | tf_op jit(solution)/shard_map/ppermute | solution.py:286
  10.8 7.2 %collective-permute-start.1 = (bf16[8,8192]{1,0:T(8,128)(2,1)S(1)}, bf16[8,8192]{1,0:T(8,128)(2,1)S(1)}, u32[]{:S(2)}, u32[]{:S(2)}) collective-permute-start(bf16[8,8192]{1,0:T(8,128)(2,1)S(1)} %get-tuple-element.13.refs_0_), channel_id=1, source_target_pairs={{0,8},{1,9},{2,10},{3,11},{4,12},{5,13},{6,14},{7,15},{8,0},{9,1},... | collective-permute-start | bytes 393224 | tf_op jit(solution)/shard_map/ppermute | solution.py:286
  13.4 5.1 %collective-permute-start = (bf16[8,8192]{1,0:T(8,128)(2,1)S(1)}, bf16[8,8192]{1,0:T(8,128)(2,1)S(1)}, u32[]{:S(2)}, u32[]{:S(2)}) collective-permute-start(bf16[8,8192]{1,0:T(8,128)(2,1)S(1)} %get-tuple-element.13.refs_0_), channel_id=1, source_target_pairs={{0,1},{1,0},{2,3},{3,2},{4,5},{5,4},{6,7},{7,6},{8,9},{9,8},{10,11... | collective-permute-start | bytes 393224 | tf_op jit(solution)/shard_map/ppermute | solution.py:286
  13.4 9.1 %collective-permute-start.13 = (bf16[8,8192]{1,0:T(8,128)(2,1)S(1)}, bf16[8,8192]{1,0:T(8,128)(2,1)S(1)}, u32[]{:S(2)}, u32[]{:S(2)}) collective-permute-start(bf16[8,8192]{1,0:T(8,128)(2,1)S(1)} %collective-permute-done.11.refs_12_), channel_id=1, source_target_pairs={{0,4},{1,5},{2,6},{3,7},{4,0},{5,1},{6,2},{7,3},{8,12},{9,13},{10,... | collective-permute-start | bytes 393224 | tf_op jit(solution)/shard_map/ppermute | solution.py:286
  14.5 7.9 %collective-permute-start.12 = (bf16[8,8192]{1,0:T(8,128)(2,1)S(1)}, bf16[8,8192]{1,0:T(8,128)(2,1)S(1)}, u32[]{:S(2)}, u32[]{:S(2)}) collective-permute-start(bf16[8,8192]{1,0:T(8,128)(2,1)S(1)} %collective-permute-done.11.refs_12_), channel_id=1, source_target_pairs={{0,1},{1,0},{2,3},{3,2},{4,5},{5,4},{6,7},{7,6},{8,9},{9,8},{10,11... | collective-permute-start | bytes 393224 | tf_op jit(solution)/shard_map/ppermute | solution.py:286
  15.9 6.7 %collective-permute-start.10 = (bf16[8,8192]{1,0:T(8,128)(2,1)S(1)}, bf16[8,8192]{1,0:T(8,128)(2,1)S(1)}, u32[]{:S(2)}, u32[]{:S(2)}) collective-permute-start(bf16[8,8192]{1,0:T(8,128)(2,1)S(1)} %collective-permute-done.9.refs_10_), channel_id=1, source_target_pairs={{0,1},{1,0},{2,3},{3,2},{4,5},{5,4},{6,7},{7,6},{8,9},{9,8},{10,11... | collective-permute-start | bytes 393224 | tf_op jit(solution)/shard_map/ppermute | solution.py:286
  17.9 5.2 %collective-permute-start.7 = (bf16[8,8192]{1,0:T(8,128)(2,1)S(1)}, bf16[8,8192]{1,0:T(8,128)(2,1)S(1)}, u32[]{:S(2)}, u32[]{:S(2)}) collective-permute-start(bf16[8,8192]{1,0:T(8,128)(2,1)S(1)} %collective-permute-done.1.refs_2_), channel_id=1, source_target_pairs={{0,2},{1,3},{2,0},{3,1},{4,6},{5,7},{6,4},{7,5},{8,10},{9,11},{10,... | collective-permute-start | bytes 393224 | tf_op jit(solution)/shard_map/ppermute | solution.py:286
  18.4 6.9 %collective-permute-start.5 = (bf16[8,8192]{1,0:T(8,128)(2,1)S(1)}, bf16[8,8192]{1,0:T(8,128)(2,1)S(1)}, u32[]{:S(2)}, u32[]{:S(2)}) collective-permute-start(bf16[8,8192]{1,0:T(8,128)(2,1)S(1)} %collective-permute-done.1.refs_2_), channel_id=1, source_target_pairs={{0,6},{1,7},{2,4},{3,5},{4,2},{5,3},{6,0},{7,1},{8,14},{9,15},{10,... | collective-permute-start | bytes 393224 | tf_op jit(solution)/shard_map/ppermute | solution.py:286
  22.4 5.0 %collective-permute-start.3 = (bf16[8,8192]{1,0:T(8,128)(2,1)S(1)}, bf16[8,8192]{1,0:T(8,128)(2,1)S(1)}, u32[]{:S(2)}, u32[]{:S(2)}) collective-permute-start(bf16[8,8192]{1,0:T(8,128)(2,1)S(1)} %collective-permute-done.1.refs_2_), channel_id=1, source_target_pairs={{0,4},{1,5},{2,6},{3,7},{4,0},{5,1},{6,2},{7,3},{8,12},{9,13},{10,... | collective-permute-start | bytes 393224 | tf_op jit(solution)/shard_map/ppermute | solution.py:286
  22.4 5.0 %collective-permute-start.2 = (bf16[8,8192]{1,0:T(8,128)(2,1)S(1)}, bf16[8,8192]{1,0:T(8,128)(2,1)S(1)}, u32[]{:S(2)}, u32[]{:S(2)}) collective-permute-start(bf16[8,8192]{1,0:T(8,128)(2,1)S(1)} %collective-permute-done.1.refs_2_), channel_id=1, source_target_pairs={{0,1},{1,0},{2,3},{3,2},{4,5},{5,4},{6,7},{7,6},{8,9},{9,8},{10,11... | collective-permute-start | bytes 393224 | tf_op jit(solution)/shard_map/ppermute | solution.py:286
  22.5 4.9 %collective-permute-start.14 = (bf16[8,8192]{1,0:T(8,128)(2,1)S(1)}, bf16[8,8192]{1,0:T(8,128)(2,1)S(1)}, u32[]{:S(2)}, u32[]{:S(2)}) collective-permute-start(bf16[8,8192]{1,0:T(8,128)(2,1)S(1)} %collective-permute-done.13.refs_14_), channel_id=1, source_target_pairs={{0,1},{1,0},{2,3},{3,2},{4,5},{5,4},{6,7},{7,6},{8,9},{9,8},{10,11... | collective-permute-start | bytes 393224 | tf_op jit(solution)/shard_map/ppermute | solution.py:286
  23.2 4.2 %collective-permute-start.8 = (bf16[8,8192]{1,0:T(8,128)(2,1)S(1)}, bf16[8,8192]{1,0:T(8,128)(2,1)S(1)}, u32[]{:S(2)}, u32[]{:S(2)}) collective-permute-start(bf16[8,8192]{1,0:T(8,128)(2,1)S(1)} %collective-permute-done.7.refs_8_), channel_id=1, source_target_pairs={{0,1},{1,0},{2,3},{3,2},{4,5},{5,4},{6,7},{7,6},{8,9},{9,8},{10,11... | collective-permute-start | bytes 393224 | tf_op jit(solution)/shard_map/ppermute | solution.py:286
  25.4 2.1 %collective-permute-start.6 = (bf16[8,8192]{1,0:T(8,128)(2,1)S(1)}, bf16[8,8192]{1,0:T(8,128)(2,1)S(1)}, u32[]{:S(2)}, u32[]{:S(2)}) collective-permute-start(bf16[8,8192]{1,0:T(8,128)(2,1)S(1)} %collective-permute-done.5.refs_6_), channel_id=1, source_target_pairs={{0,1},{1,0},{2,3},{3,2},{4,5},{5,4},{6,7},{7,6},{8,9},{9,8},{10,11... | collective-permute-start | bytes 393224 | tf_op jit(solution)/shard_map/ppermute | solution.py:286
  27.4 1.3 %collective-permute-start.4 = (bf16[8,8192]{1,0:T(8,128)(2,1)S(1)}, bf16[8,8192]{1,0:T(8,128)(2,1)S(1)}, u32[]{:S(2)}, u32[]{:S(2)}) collective-permute-start(bf16[8,8192]{1,0:T(8,128)(2,1)S(1)} %collective-permute-done.3.refs_4_), channel_id=1, source_target_pairs={{0,1},{1,0},{2,3},{3,2},{4,5},{5,4},{6,7},{7,6},{8,9},{9,8},{10,11... | collective-permute-start | bytes 393224 | tf_op jit(solution)/shard_map/ppermute | solution.py:286
  30.9 15.6 %all-to-all-start = ((bf16[16,16,512]{2,1,0:T(8,128)(2,1)}), bf16[16,16,512]{2,1,0:T(8,128)(2,1)S(1)}, u32[]{:S(2)}, u32[]{:S(2)}) async-start(bf16[16,16,512]{2,1,0:T(8,128)(2,1)} %get-tuple-element.20), calls=%async_computation | async-start | bytes 524288 | tf_op jit(solution)/shard_map/all_to_all | solution.py:432
  36.5 3.4 %copy-start = (bf16[8192,512]{1,0:T(8,128)(2,1)S(1)}, bf16[8192,512]{1,0:T(8,128)(2,1)}, u32[]{:S(2)}) copy-start(bf16[8192,512]{1,0:T(8,128)(2,1)} %w_ref.1) | copy-start | bytes 25165828

commit v9 on v8

--- a/solution.py
+++ b/solution.py
@@ -13,7 +13,7 @@
 GROUP = HQ // KVH
 MOST = 8
 RING = 16
-ORDER = [0, 1, 8, 9, 12, 13, 14, 15, 10, 11, 4, 5, 2, 3, 6, 7]
+ORDER = [0, 1, 2, 3, 4, 5, 6, 7, 8, 9, 12, 13, 14, 15, 10, 11]
 F32 = jnp.float32
 BF16 = jnp.bfloat16
 NT = (((1,), (1,)), ((), ()))
@@ -295,10 +295,12 @@
     held[far] = swap(block, far, parts)
     held[near] = swap(block, near, parts)
     held[y] = swap(block, y, parts)
-    held[near | y] = swap(held[y], near, parts)
     held[far | y] = swap(held[far], y, parts)
     held[far | near | y] = swap(held[far], near | y, parts)
     held[far | near] = swap(held[far], near, parts)
+    mixed = jnp.where(lax.axis_index("tensor") % 2 == 0, held[near], held[y])
+    pairs = [(i, i ^ (y if i % 2 == 0 else near)) for i in range(parts)]
+    held[near | y] = lax.ppermute(mixed, "tensor", pairs)
     for slot in list(held):
         held[slot | core] = swap(held[slot], core, parts)
     return [held[slot] for slot in range(parts)]

time: 47.7 us -> 54.6 us (1.14)
  local copies, waits for them, and re-layouts: 3.38 us -> 9.2 us
  starting transfers between devices: 19 us -> 21.3 us
  waiting for transfers between devices: 13.4 us -> 12 us
    unnamed x2 -> x10, local copies, waits for them, and re-layouts: 3.38 us -> 9.2 us
    all_to_all x1, starting transfers between devices: 5.59 us -> 8.03 us  [per_device(): lax.all_to_all(send, 'tensor', split_axis=0, concat_axis=0, tiled=True)]
    all_to_all x1, waiting for transfers between devices: 4.25 us -> 2.65 us  [per_device(): lax.all_to_all(send, 'tensor', split_axis=0, concat_axis=0, tiled=True)]
    ppermute x15 -> x14, starting transfers between devices: 13.4 us -> 11.8 us  [swap(): return lax.ppermute(x, 'tensor', [(i, i ^ bits) for i in range(parts)])]
    ppermute x0 -> x1, starting transfers between devices: none -> 1.53 us  [gather(): held[near | y] = lax.ppermute(mixed, 'tensor', pairs)]
    ppermute x0 -> x1, waiting for transfers between devices: none -> 0.62 us  [gather(): held[near | y] = lax.ppermute(mixed, 'tensor', pairs)]
    ppermute x15 -> x14, waiting for transfers between devices: 9.16 us -> 8.78 us  [swap(): return lax.ppermute(x, 'tensor', [(i, i ^ bits) for i in range(parts)])]
  transfers between devices with their start and end apart: 16 -> 16, of which waited for: 7 -> 10; matrix products, arithmetic and copies ran while one was open for 0% -> 0% of each run, Pallas kernels for 5% -> 4%
where the time goes in v9:
time: 54.6 us; the launch traced here: 54.3 us
  starting transfers between devices  21.3 us (39%)
  waiting for transfers between devices  12 us (22%)
  Pallas kernels  11.6 us (21%)
  local copies, waits for them, and re-layouts  9.2 us (17%)
    ppermute x14, starting transfers between devices, swap(): return lax.ppermute(x, 'tensor', [(i, i ^ bits) for i in range(parts)])  11.8 us
    unnamed x10, local copies, waits for them, and re-layouts  9.2 us
    ppermute x14, waiting for transfers between devices, swap(): return lax.ppermute(x, 'tensor', [(i, i ^ bits) for i in range(parts)])  8.78 us
    all_to_all x1, starting transfers between devices, per_device(): lax.all_to_all(send, 'tensor', split_axis=0, concat_axis=0, tiled=True)  8.03 us
    pallas_call x1, Pallas kernels, attend(): pl.pallas_call(attend_kernel, out_shape=[jax.ShapeDtypeStruct(shape, BF16...  6.14 us
    all_to_all x1, waiting for transfers between devices, per_device(): lax.all_to_all(send, 'tensor', split_axis=0, concat_axis=0, tiled=True)  2.65 us
    pallas_call x1, Pallas kernels, base_part(): pl.pallas_call(base_kernel, out_shape=jax.ShapeDtypeStruct((total, cols),...  2.41 us
    pallas_call x1, Pallas kernels, deltas(): pl.pallas_call(functools.partial(delta_kernel, at_slot), out_shape=(jax.S...  2.2 us
  transfers between devices with their start and end apart: 16, of which 10 were waited for; matrix products, arithmetic and copies ran while one was open for 0% of the time, Pallas kernels for 4%

profile of v9, /device:TPU:0, one launch (start us, length us, event | category | flops | bytes accessed | tf_op | source)
XLA Modules:
  0.0 54.3 jit_solution(3552631267548389014)
XLA Ops:
  0.0 6.1 %attend.1 = (bf16[8,8192]{1,0:T(8,128)(2,1)S(1)}, bf16[8192,128]{1,0:T(8,128)(2,1)S(1)}, bf16[8192,128]{1,0:T(8,128)(2,1)S(1)}, bf16[16,128]{1,0:T(8,128)(2,1)S(...) custom-call(s32[4]{0:T(128)} %len_hbm.1, bf16[2,4,8192]{2,1,0:T(4,128)(2,1)} %q_hbm.1, ...), custom_call_target="tpu_custom_call" | custom-call | flops 134217728 | bytes 8388608 | tf_op jit(solution)/shard_map/attend/pallas_call | solution.py:241
  6.2 1.3 %copy-done.1 = bf16[8192,128]{1,0:T(8,128)(2,1)} copy-done((bf16[8192,128]{1,0:T(8,128)(2,1)}, bf16[8192,128]{1,0:T(8,128)(2,1)S(1)}, u32[]{:S(2)}) %copy-start.1) | copy-done | bytes 2097176
  7.5 4.0 %collective-permute-start.7 = (bf16[8,8192]{1,0:T(8,128)(2,1)S(1)}, bf16[8,8192]{1,0:T(8,128)(2,1)S(1)}, u32[]{:S(2)}, u32[]{:S(2)}) collective-permute-start(bf16[8,8192]{1,0:T(8,128)(2,1)S(1)} %get-tuple-element.13.refs_0_), channel_id=1, source_target_pairs={{0,8},{1,9},{2,10},{3,11},{4,12},{5,13},{6,14},{7,15},{8,0},{9,1},... | collective-permute-start | bytes 393224 | tf_op jit(solution)/shard_map/ppermute | solution.py:286
  11.5 1.6 %collective-permute-start.3 = (bf16[8,8192]{1,0:T(8,128)(2,1)S(1)}, bf16[8,8192]{1,0:T(8,128)(2,1)S(1)}, u32[]{:S(2)}, u32[]{:S(2)}) collective-permute-start(bf16[8,8192]{1,0:T(8,128)(2,1)S(1)} %get-tuple-element.13.refs_0_), channel_id=1, source_target_pairs={{0,4},{1,5},{2,6},{3,7},{4,0},{5,1},{6,2},{7,3},{8,12},{9,13},{10,... | collective-permute-start | bytes 393224 | tf_op jit(solution)/shard_map/ppermute | solution.py:286
  13.1 1.5 %collective-permute-start.1 = (bf16[8,8192]{1,0:T(8,128)(2,1)S(1)}, bf16[8,8192]{1,0:T(8,128)(2,1)S(1)}, u32[]{:S(2)}, u32[]{:S(2)}) collective-permute-start(bf16[8,8192]{1,0:T(8,128)(2,1)S(1)} %get-tuple-element.13.refs_0_), channel_id=1, source_target_pairs={{0,2},{1,3},{2,0},{3,1},{4,6},{5,7},{6,4},{7,5},{8,10},{9,11},{10,... | collective-permute-start | bytes 393224 | tf_op jit(solution)/shard_map/ppermute | solution.py:286
  14.6 0.0 collective-permute-start
  14.6 3.3 %collective-permute-done.7.refs_8_ = bf16[8,8192]{1,0:T(8,128)(2,1)S(1)} collective-permute-done((bf16[8,8192]{1,0:T(8,128)(2,1)S(1)}, bf16[8,8192]{1,0:T(8,128)(2,1)S(1)}, u32[]{:S(2)}, u32[]{:S(2)}) %collective-permute-start.7) | collective-permute-done | bytes 131104 | tf_op jit(solution)/shard_map/ppermute | solution.py:286
  17.9 1.6 %collective-permute-start.13 = (bf16[8,8192]{1,0:T(8,128)(2,1)S(1)}, bf16[8,8192]{1,0:T(8,128)(2,1)S(1)}, u32[]{:S(2)}, u32[]{:S(2)}) collective-permute-start(bf16[8,8192]{1,0:T(8,128)(2,1)S(1)} %collective-permute-done.7.refs_8_), channel_id=1, source_target_pairs={{0,2},{1,3},{2,0},{3,1},{4,6},{5,7},{6,4},{7,5},{8,10},{9,11},{10,... | collective-permute-start | bytes 393224 | tf_op jit(solution)/shard_map/ppermute | solution.py:286
  19.5 0.5 collective-permute-start.11
  20.0 1.4 %collective-permute-start.9 = (bf16[8,8192]{1,0:T(8,128)(2,1)S(1)}, bf16[8,8192]{1,0:T(8,128)(2,1)S(1)}, u32[]{:S(2)}, u32[]{:S(2)}) collective-permute-start(bf16[8,8192]{1,0:T(8,128)(2,1)S(1)} %collective-permute-done.7.refs_8_), channel_id=1, source_target_pairs={{0,4},{1,5},{2,6},{3,7},{4,0},{5,1},{6,2},{7,3},{8,12},{9,13},{10,... | collective-permute-start | bytes 393224 | tf_op jit(solution)/shard_map/ppermute | solution.py:286
  21.5 0.6 %collective-permute-start.4 = (bf16[8,8192]{1,0:T(8,128)(2,1)S(1)}, bf16[8,8192]{1,0:T(8,128)(2,1)S(1)}, u32[]{:S(2)}, u32[]{:S(2)}) collective-permute-start(bf16[8,8192]{1,0:T(8,128)(2,1)S(1)} %collective-permute-done.3.refs_4_), channel_id=1, source_target_pairs={{0,1},{1,0},{2,3},{3,2},{4,5},{5,4},{6,7},{7,6},{8,9},{9,8},{10,11... | collective-permute-start | bytes 393224 | tf_op jit(solution)/shard_map/ppermute | solution.py:286
  22.0 1.9 %collective-permute-done.13.refs_14_ = bf16[8,8192]{1,0:T(8,128)(2,1)S(1)} collective-permute-done((bf16[8,8192]{1,0:T(8,128)(2,1)S(1)}, bf16[8,8192]{1,0:T(8,128)(2,1)S(1)}, u32[]{:S(2)}, u32[]{:S(2)}) %collective-permute-start.13) | collective-permute-done | bytes 131104 | tf_op jit(solution)/shard_map/ppermute | solution.py:286
  23.9 1.5 %collective-permute-start.5 = (bf16[8,8192]{1,0:T(8,128)(2,1)S(1)}, bf16[8,8192]{1,0:T(8,128)(2,1)S(1)}, u32[]{:S(2)}, u32[]{:S(2)}) collective-permute-start(bf16[8,8192]{1,0:T(8,128)(2,1)S(1)} %broadcast_select_fusion), channel_id=1, source_target_pairs={{0,2},{1,5},{2,0},{3,7},{4,6},{5,1},{6,4},{7,3},{8,10},{9,13},{10,... | collective-permute-start | bytes 393224 | tf_op jit(solution)/shard_map/ppermute | solution.py:303
  25.4 0.4 collective-permute-done.11.refs_12_
  25.8 1.8 %collective-permute-done.9.refs_10_ = bf16[8,8192]{1,0:T(8,128)(2,1)S(1)} collective-permute-done((bf16[8,8192]{1,0:T(8,128)(2,1)S(1)}, bf16[8,8192]{1,0:T(8,128)(2,1)S(1)}, u32[]{:S(2)}, u32[]{:S(2)}) %collective-permute-start.9) | collective-permute-done | bytes 131104 | tf_op jit(solution)/shard_map/ppermute | solution.py:286
  27.7 0.5 collective-permute-start.12
  28.2 0.1 collective-permute-start.10
  28.3 0.6 %collective-permute-done.5.refs_6_ = bf16[8,8192]{1,0:T(8,128)(2,1)S(1)} collective-permute-done((bf16[8,8192]{1,0:T(8,128)(2,1)S(1)}, bf16[8,8192]{1,0:T(8,128)(2,1)S(1)}, u32[]{:S(2)}, u32[]{:S(2)}) %collective-permute-start.5) | collective-permute-done | bytes 131104 | tf_op jit(solution)/shard_map/ppermute | solution.py:303
  28.9 0.1 collective-permute-done.14.refs_15_
  29.0 0.2 collective-permute-done.12.refs_13_
  29.2 0.3 collective-permute-done.10.refs_11_
  29.5 0.7 %collective-permute-done.6.refs_7_ = bf16[8,8192]{1,0:T(8,128)(2,1)S(1)} collective-permute-done((bf16[8,8192]{1,0:T(8,128)(2,1)S(1)}, bf16[8,8192]{1,0:T(8,128)(2,1)S(1)}, u32[]{:S(2)}, u32[]{:S(2)}) %collective-permute-start.6) | collective-permute-done | bytes 131104 | tf_op jit(solution)/shard_map/ppermute | solution.py:286
  30.2 1.6 %copy-done.2 = bf16[8192,128]{1,0:T(8,128)(2,1)S(1)} copy-done((bf16[8192,128]{1,0:T(8,128)(2,1)S(1)}, bf16[8192,128]{1,0:T(8,128)(2,1)}, u32[]{:S(2)}) %copy-start.2) | copy-done | bytes 2097176
  31.8 2.2 %delta.1 = (bf16[16,16,512]{2,1,0:T(8,128)(2,1)}, bf16[128,8192]{1,0:T(8,128)(2,1)S(1)}) custom-call(bf16[8,8192]{1,0:T(8,128)(2,1)S(1)} %get-tuple-element.13.refs_0_, bf16[8,8192]{1,0:T(8,128)(2,1)S(1)} %collective-permute-done.refs_1_, bf16[8,8192]{1,0:T(8,128)(2,1)S(1)} %collective-permute-done.1.refs_2_, ...), custom_call_target="tpu_custom_call" | custom-call | flops 301989888 | bytes 8650752 | tf_op jit(solution)/shard_map/delta/pallas_call | solution.py:334
  34.0 1.3 %copy-done.3 = bf16[128,8192]{1,0:T(8,128)(2,1)} copy-done((bf16[128,8192]{1,0:T(8,128)(2,1)}, bf16[128,8192]{1,0:T(8,128)(2,1)S(1)}, u32[]{:S(2)}) %copy-start.3) | copy-done | bytes 2097176
  35.3 8.0 %all-to-all-start = ((bf16[16,16,512]{2,1,0:T(8,128)(2,1)}), bf16[16,16,512]{2,1,0:T(8,128)(2,1)S(1)}, u32[]{:S(2)}, u32[]{:S(2)}) async-start(bf16[16,16,512]{2,1,0:T(8,128)(2,1)} %get-tuple-element.20), calls=%async_computation | async-start | bytes 524288 | tf_op jit(solution)/shard_map/all_to_all | solution.py:434
  43.4 0.0 copy-start
  43.4 3.4 %copy-done = bf16[8192,512]{1,0:T(8,128)(2,1)S(1)} copy-done((bf16[8192,512]{1,0:T(8,128)(2,1)S(1)}, bf16[8192,512]{1,0:T(8,128)(2,1)}, u32[]{:S(2)}) %copy-start) | copy-done | bytes 8388632
  46.8 1.6 %copy-done.4 = bf16[128,8192]{1,0:T(8,128)(2,1)S(1)} copy-done((bf16[128,8192]{1,0:T(8,128)(2,1)S(1)}, bf16[128,8192]{1,0:T(8,128)(2,1)}, u32[]{:S(2)}) %copy-start.4) | copy-done | bytes 2097176
  48.4 2.4 %base.1.base_ref = f32[128,512]{1,0:T(8,128)S(1)} custom-call(bf16[128,8192]{1,0:T(8,128)(2,1)S(1)} %copy-done.4, bf16[8192,512]{1,0:T(8,128)(2,1)S(1)} %copy-done, bf16[128,128]{1,0:T(8,128)(2,1)S(1)} %get-tuple-element.18.order_ref), custom_call_target="tpu_custom_call" | custom-call | flops 1342177280 | bytes 10747904 | tf_op jit(solution)/shard_map/base/pallas_call | solution.py:366
  50.8 2.6 %all-to-all-done.delta_ref = bf16[16,16,512]{2,1,0:T(8,128)(2,1)S(1)} async-done(((bf16[16,16,512]{2,1,0:T(8,128)(2,1)}), bf16[16,16,512]{2,1,0:T(8,128)(2,1)S(1)}, u32[]{:S(2)}, u32[]{:S(2)}) %all-to-all-start) | async-done | bytes 262176 | tf_op jit(solution)/shard_map/all_to_all | solution.py:434
  53.4 0.8 %join.1 = bf16[2,64,512]{2,1,0:T(8,128)(2,1)} custom-call(f32[128,512]{1,0:T(8,128)S(1)} %base.1.base_ref, bf16[128,256]{1,0:T(8,128)(2,1)S(1)} %get-tuple-element.19.place_ref, bf16[16,16,512]{2,1,0:T(8,128)(2,1)S(1)} %all-to-all-done.delta_ref), custom_call_target="tpu_custom_call" | custom-call | tf_op jit(solution)/shard_map/join/pallas_call | solution.py:393
  (15 shorter events, 0.0 us)
Async XLA Ops:
  6.2 1.3 %copy-start.1 = (bf16[8192,128]{1,0:T(8,128)(2,1)}, bf16[8192,128]{1,0:T(8,128)(2,1)S(1)}, u32[]{:S(2)}) copy-start(bf16[8192,128]{1,0:T(8,128)(2,1)S(1)} %get-tuple-element.16.refs_18_) | copy-start | bytes 6291460
  7.5 10.4 %collective-permute-start.7 = (bf16[8,8192]{1,0:T(8,128)(2,1)S(1)}, bf16[8,8192]{1,0:T(8,128)(2,1)S(1)}, u32[]{:S(2)}, u32[]{:S(2)}) collective-permute-start(bf16[8,8192]{1,0:T(8,128)(2,1)S(1)} %get-tuple-element.13.refs_0_), channel_id=1, source_target_pairs={{0,8},{1,9},{2,10},{3,11},{4,12},{5,13},{6,14},{7,15},{8,0},{9,1},... | collective-permute-start | bytes 393224 | tf_op jit(solution)/shard_map/ppermute | solution.py:286
  11.5 8.5 %collective-permute-start.3 = (bf16[8,8192]{1,0:T(8,128)(2,1)S(1)}, bf16[8,8192]{1,0:T(8,128)(2,1)S(1)}, u32[]{:S(2)}, u32[]{:S(2)}) collective-permute-start(bf16[8,8192]{1,0:T(8,128)(2,1)S(1)} %get-tuple-element.13.refs_0_), channel_id=1, source_target_pairs={{0,4},{1,5},{2,6},{3,7},{4,0},{5,1},{6,2},{7,3},{8,12},{9,13},{10,... | collective-permute-start | bytes 393224 | tf_op jit(solution)/shard_map/ppermute | solution.py:286
  13.1 8.3 %collective-permute-start.1 = (bf16[8,8192]{1,0:T(8,128)(2,1)S(1)}, bf16[8,8192]{1,0:T(8,128)(2,1)S(1)}, u32[]{:S(2)}, u32[]{:S(2)}) collective-permute-start(bf16[8,8192]{1,0:T(8,128)(2,1)S(1)} %get-tuple-element.13.refs_0_), channel_id=1, source_target_pairs={{0,2},{1,3},{2,0},{3,1},{4,6},{5,7},{6,4},{7,5},{8,10},{9,11},{10,... | collective-permute-start | bytes 393224 | tf_op jit(solution)/shard_map/ppermute | solution.py:286
  14.6 6.8 %collective-permute-start = (bf16[8,8192]{1,0:T(8,128)(2,1)S(1)}, bf16[8,8192]{1,0:T(8,128)(2,1)S(1)}, u32[]{:S(2)}, u32[]{:S(2)}) collective-permute-start(bf16[8,8192]{1,0:T(8,128)(2,1)S(1)} %get-tuple-element.13.refs_0_), channel_id=1, source_target_pairs={{0,1},{1,0},{2,3},{3,2},{4,5},{5,4},{6,7},{7,6},{8,9},{9,8},{10,11... | collective-permute-start | bytes 393224 | tf_op jit(solution)/shard_map/ppermute | solution.py:286
  17.9 6.0 %collective-permute-start.13 = (bf16[8,8192]{1,0:T(8,128)(2,1)S(1)}, bf16[8,8192]{1,0:T(8,128)(2,1)S(1)}, u32[]{:S(2)}, u32[]{:S(2)}) collective-permute-start(bf16[8,8192]{1,0:T(8,128)(2,1)S(1)} %collective-permute-done.7.refs_8_), channel_id=1, source_target_pairs={{0,2},{1,3},{2,0},{3,1},{4,6},{5,7},{6,4},{7,5},{8,10},{9,11},{10,... | collective-permute-start | bytes 393224 | tf_op jit(solution)/shard_map/ppermute | solution.py:286
  19.5 6.3 %collective-permute-start.11 = (bf16[8,8192]{1,0:T(8,128)(2,1)S(1)}, bf16[8,8192]{1,0:T(8,128)(2,1)S(1)}, u32[]{:S(2)}, u32[]{:S(2)}) collective-permute-start(bf16[8,8192]{1,0:T(8,128)(2,1)S(1)} %collective-permute-done.7.refs_8_), channel_id=1, source_target_pairs={{0,6},{1,7},{2,4},{3,5},{4,2},{5,3},{6,0},{7,1},{8,14},{9,15},{10,... | collective-permute-start | bytes 393224 | tf_op jit(solution)/shard_map/ppermute | solution.py:286
  20.0 7.7 %collective-permute-start.9 = (bf16[8,8192]{1,0:T(8,128)(2,1)S(1)}, bf16[8,8192]{1,0:T(8,128)(2,1)S(1)}, u32[]{:S(2)}, u32[]{:S(2)}) collective-permute-start(bf16[8,8192]{1,0:T(8,128)(2,1)S(1)} %collective-permute-done.7.refs_8_), channel_id=1, source_target_pairs={{0,4},{1,5},{2,6},{3,7},{4,0},{5,1},{6,2},{7,3},{8,12},{9,13},{10,... | collective-permute-start | bytes 393224 | tf_op jit(solution)/shard_map/ppermute | solution.py:286
  21.4 6.3 %collective-permute-start.8 = (bf16[8,8192]{1,0:T(8,128)(2,1)S(1)}, bf16[8,8192]{1,0:T(8,128)(2,1)S(1)}, u32[]{:S(2)}, u32[]{:S(2)}) collective-permute-start(bf16[8,8192]{1,0:T(8,128)(2,1)S(1)} %collective-permute-done.7.refs_8_), channel_id=1, source_target_pairs={{0,1},{1,0},{2,3},{3,2},{4,5},{5,4},{6,7},{7,6},{8,9},{9,8},{10,11... | collective-permute-start | bytes 393224 | tf_op jit(solution)/shard_map/ppermute | solution.py:286
  21.5 6.7 %collective-permute-start.4 = (bf16[8,8192]{1,0:T(8,128)(2,1)S(1)}, bf16[8,8192]{1,0:T(8,128)(2,1)S(1)}, u32[]{:S(2)}, u32[]{:S(2)}) collective-permute-start(bf16[8,8192]{1,0:T(8,128)(2,1)S(1)} %collective-permute-done.3.refs_4_), channel_id=1, source_target_pairs={{0,1},{1,0},{2,3},{3,2},{4,5},{5,4},{6,7},{7,6},{8,9},{9,8},{10,11... | collective-permute-start | bytes 393224 | tf_op jit(solution)/shard_map/ppermute | solution.py:286
  23.9 5.0 %collective-permute-start.5 = (bf16[8,8192]{1,0:T(8,128)(2,1)S(1)}, bf16[8,8192]{1,0:T(8,128)(2,1)S(1)}, u32[]{:S(2)}, u32[]{:S(2)}) collective-permute-start(bf16[8,8192]{1,0:T(8,128)(2,1)S(1)} %broadcast_select_fusion), channel_id=1, source_target_pairs={{0,2},{1,5},{2,0},{3,7},{4,6},{5,1},{6,4},{7,3},{8,10},{9,13},{10,... | collective-permute-start | bytes 393224 | tf_op jit(solution)/shard_map/ppermute | solution.py:303
  25.8 3.1 %collective-permute-start.2 = (bf16[8,8192]{1,0:T(8,128)(2,1)S(1)}, bf16[8,8192]{1,0:T(8,128)(2,1)S(1)}, u32[]{:S(2)}, u32[]{:S(2)}) collective-permute-start(bf16[8,8192]{1,0:T(8,128)(2,1)S(1)} %collective-permute-done.1.refs_2_), channel_id=1, source_target_pairs={{0,1},{1,0},{2,3},{3,2},{4,5},{5,4},{6,7},{7,6},{8,9},{9,8},{10,11... | collective-permute-start | bytes 393224 | tf_op jit(solution)/shard_map/ppermute | solution.py:286
  27.7 1.3 %collective-permute-start.14 = (bf16[8,8192]{1,0:T(8,128)(2,1)S(1)}, bf16[8,8192]{1,0:T(8,128)(2,1)S(1)}, u32[]{:S(2)}, u32[]{:S(2)}) collective-permute-start(bf16[8,8192]{1,0:T(8,128)(2,1)S(1)} %collective-permute-done.13.refs_14_), channel_id=1, source_target_pairs={{0,1},{1,0},{2,3},{3,2},{4,5},{5,4},{6,7},{7,6},{8,9},{9,8},{10,11... | collective-permute-start | bytes 393224 | tf_op jit(solution)/shard_map/ppermute | solution.py:286
  27.7 1.5 %collective-permute-start.12 = (bf16[8,8192]{1,0:T(8,128)(2,1)S(1)}, bf16[8,8192]{1,0:T(8,128)(2,1)S(1)}, u32[]{:S(2)}, u32[]{:S(2)}) collective-permute-start(bf16[8,8192]{1,0:T(8,128)(2,1)S(1)} %collective-permute-done.11.refs_12_), channel_id=1, source_target_pairs={{0,1},{1,0},{2,3},{3,2},{4,5},{5,4},{6,7},{7,6},{8,9},{9,8},{10,11... | collective-permute-start | bytes 393224 | tf_op jit(solution)/shard_map/ppermute | solution.py:286
  28.2 1.3 %collective-permute-start.10 = (bf16[8,8192]{1,0:T(8,128)(2,1)S(1)}, bf16[8,8192]{1,0:T(8,128)(2,1)S(1)}, u32[]{:S(2)}, u32[]{:S(2)}) collective-permute-start(bf16[8,8192]{1,0:T(8,128)(2,1)S(1)} %collective-permute-done.9.refs_10_), channel_id=1, source_target_pairs={{0,1},{1,0},{2,3},{3,2},{4,5},{5,4},{6,7},{7,6},{8,9},{9,8},{10,11... | collective-permute-start | bytes 393224 | tf_op jit(solution)/shard_map/ppermute | solution.py:286
  28.9 1.3 %collective-permute-start.6 = (bf16[8,8192]{1,0:T(8,128)(2,1)S(1)}, bf16[8,8192]{1,0:T(8,128)(2,1)S(1)}, u32[]{:S(2)}, u32[]{:S(2)}) collective-permute-start(bf16[8,8192]{1,0:T(8,128)(2,1)S(1)} %collective-permute-done.5.refs_6_), channel_id=1, source_target_pairs={{0,1},{1,0},{2,3},{3,2},{4,5},{5,4},{6,7},{7,6},{8,9},{9,8},{10,11... | collective-permute-start | bytes 393224 | tf_op jit(solution)/shard_map/ppermute | solution.py:286
  30.2 1.6 %copy-start.2 = (bf16[8192,128]{1,0:T(8,128)(2,1)S(1)}, bf16[8192,128]{1,0:T(8,128)(2,1)}, u32[]{:S(2)}) copy-start(bf16[8192,128]{1,0:T(8,128)(2,1)} %copy-done.1) | copy-start | bytes 6291460
  34.0 1.3 %copy-start.3 = (bf16[128,8192]{1,0:T(8,128)(2,1)}, bf16[128,8192]{1,0:T(8,128)(2,1)S(1)}, u32[]{:S(2)}) copy-start(bf16[128,8192]{1,0:T(8,128)(2,1)S(1)} %get-tuple-element.17.a_ref) | copy-start | bytes 6291460
  35.3 18.1 %all-to-all-start = ((bf16[16,16,512]{2,1,0:T(8,128)(2,1)}), bf16[16,16,512]{2,1,0:T(8,128)(2,1)S(1)}, u32[]{:S(2)}, u32[]{:S(2)}) async-start(bf16[16,16,512]{2,1,0:T(8,128)(2,1)} %get-tuple-element.20), calls=%async_computation | async-start | bytes 524288 | tf_op jit(solution)/shard_map/all_to_all | solution.py:434
  43.4 3.4 %copy-start = (bf16[8192,512]{1,0:T(8,128)(2,1)S(1)}, bf16[8192,512]{1,0:T(8,128)(2,1)}, u32[]{:S(2)}) copy-start(bf16[8192,512]{1,0:T(8,128)(2,1)} %w_ref.1) | copy-start | bytes 25165828
  46.8 1.6 %copy-start.4 = (bf16[128,8192]{1,0:T(8,128)(2,1)S(1)}, bf16[128,8192]{1,0:T(8,128)(2,1)}, u32[]{:S(2)}) copy-start(bf16[128,8192]{1,0:T(8,128)(2,1)} %copy-done.3) | copy-start | bytes 6291460

commit v10 on v8

--- a/solution.py
+++ b/solution.py
@@ -13,7 +13,7 @@
 GROUP = HQ // KVH
 MOST = 8
 RING = 16
-ORDER = [0, 1, 8, 9, 12, 13, 14, 15, 10, 11, 4, 5, 2, 3, 6, 7]
+QUAD = 4
 F32 = jnp.float32
 BF16 = jnp.bfloat16
 NT = (((1,), (1,)), ((), ()))
@@ -40,7 +40,11 @@
 
 
 def sender(slot, me, parts):
-    return me ^ slot if parts == RING else slot
+    if parts != RING:
+        return slot
+    four, member = slot // QUAD, slot % QUAD
+    half = (me // 8 + four // 2) % 2
+    return half * 8 + member * 2 + (me + four) % 2
 
 
 def write_plan(rows, count_ref, rank_ref, owner_ref, pick_ref, place_ref, order_ref):
@@ -85,7 +89,7 @@
 
 def attend_kernel(
     len_hbm, q_hbm, nk_hbm, nv_hbm, k_hbm, v_hbm, d_hbm, u_hbm, count_hbm, rank_hbm, owner_hbm,
-    out_ref, d_ref, u_ref, pick_ref, place_ref, order_ref,
+    out_ref, spread_ref, d_ref, u_ref, pick_ref, place_ref, order_ref,
     len_ref, count_ref, rank_ref, owner_ref, q_ref, nk_ref, nv_ref, k_ref, v_ref, turned_q, nks, nvs, raw, mixed,
     small_sems, sems, store_sems,
 ):
@@ -214,6 +218,8 @@
         for g in range(GROUP):
             at = (k * GROUP + g) * HD
             out_ref[:, at : at + HD] = heads[g].astype(BF16)
+            for i in range(spread_ref.shape[0]):
+                spread_ref[i, :, at : at + HD] = heads[g].astype(BF16)
     for copy in store:
         copy.wait()
 
@@ -236,7 +242,7 @@
     rank_w = store_down.shape[2]
     total = parts * steps * rows
     slots = steps * MOST
-    shapes = [(steps * rows, width), (width, rank_w), (width, rank_w)]
+    shapes = [(steps * rows, width), (QUAD, steps * rows, width), (width, rank_w), (width, rank_w)]
     shapes += [(slots, total), (total, parts * slots), (total, total)]
     return pl.pallas_call(
         attend_kernel,
@@ -286,35 +292,50 @@
     return lax.ppermute(x, "tensor", [(i, i ^ bits) for i in range(parts)])
 
 
-def gather(block, parts):
+def spread_kernel(block_ref, out_ref):
+    for i in range(out_ref.shape[0]):
+        out_ref[i] = block_ref[...]
+
+
+def spread_out(block):
+    vmem = pl.BlockSpec(memory_space=pltpu.VMEM)
+    return pl.pallas_call(
+        spread_kernel,
+        out_shape=jax.ShapeDtypeStruct((QUAD, *block.shape), block.dtype),
+        in_specs=[vmem],
+        out_specs=vmem,
+        compiler_params=pltpu.CompilerParams(vmem_limit_bytes=8 * 2**20),
+        cost_estimate=pl.CostEstimate(
+            flops=0, bytes_accessed=2 * (QUAD + 1) * block.size, transcendentals=0
+        ),
+        name="spread",
+    )(block)
+
+
+def gather(block, spread, parts):
     if parts != RING:
-        whole = lax.all_gather(block, "tensor")
-        return [whole[i] for i in range(parts)]
-    core, y, near, far = 1, 2, 4, 8
-    held = {0: block}
-    held[far] = swap(block, far, parts)
-    held[near] = swap(block, near, parts)
-    held[y] = swap(block, y, parts)
-    held[near | y] = swap(held[y], near, parts)
-    held[far | y] = swap(held[far], y, parts)
-    held[far | near | y] = swap(held[far], near | y, parts)
-    held[far | near] = swap(held[far], near, parts)
-    for slot in list(held):
-        held[slot | core] = swap(held[slot], core, parts)
-    return [held[slot] for slot in range(parts)]
-
-
-def delta_kernel(at_slot, *refs):
+        return [lax.all_gather(block, "tensor")]
+    quads = [[8 * half + 2 * i + core for i in range(QUAD)] for half in range(2) for core in range(2)]
+
+    def exchange(x):
+        return lax.all_to_all(x, "tensor", 0, 0, axis_index_groups=quads, tiled=True)
+
+    far = swap(block, 8, parts)
+    near_half = exchange(spread)
+    far_half = exchange(spread_out(far))
+    return [near_half, swap(near_half, 1, parts), far_half, swap(far_half, 1, parts)]
+
+
+def delta_kernel(*refs):
     (*blocks, pick_ref, d_ref, u_ref, out_ref, rows_ref) = refs
-    blocks = [blocks[at_slot.index(i)] for i in range(len(blocks))]
     parts, slots, cols = out_ref.shape
-    each, width = blocks[0].shape
+    count, each, width = blocks[0].shape
     cuts = 8
     deep = width // cuts
     low = jnp.zeros((parts * each, d_ref.shape[1]), F32)
     for i in range(cuts):
         at = slice(i * deep, (i + 1) * deep)
-        piece = jnp.concatenate([b[:, at] for b in blocks], axis=0)
+        piece = jnp.concatenate([b[j, :, at] for b in blocks for j in range(count)], axis=0)
         rows_ref[:, at] = piece
         low = low + dot(piece, d_ref[at, :])
     chosen = dot(pick_ref[...], low.astype(BF16)).astype(BF16)
@@ -322,20 +343,18 @@
         out_ref[p] = dot_nt(chosen, u_ref[p * cols : (p + 1) * cols, :]).astype(BF16)
 
 
-def deltas(blocks, pick, down, up):
-    parts = len(blocks)
-    each, width = blocks[0].shape
+def deltas(blocks, pick, down, up, parts):
+    _, each, width = blocks[0].shape
     slots = pick.shape[0]
     rank_w = down.shape[1]
     vmem = pl.BlockSpec(memory_space=pltpu.VMEM)
-    at_slot = ORDER if parts == RING else [*range(parts)]
     return pl.pallas_call(
-        functools.partial(delta_kernel, at_slot),
+        delta_kernel,
         out_shape=(
             jax.ShapeDtypeStruct((parts, slots, width // parts), BF16),
             jax.ShapeDtypeStruct((parts * each, width), BF16),
         ),
-        in_specs=[vmem] * (3 + parts),
+        in_specs=[vmem] * (3 + len(blocks)),
         out_specs=(vmem, vmem),
         compiler_params=pltpu.CompilerParams(vmem_limit_bytes=24 * 2**20),
         cost_estimate=pl.CostEstimate(
@@ -344,7 +363,7 @@
             transcendentals=0,
         ),
         name="delta",
-    )(*[blocks[i] for i in at_slot], pick, down, up)
+    )(*blocks, pick, down, up)
 
 
 def base_kernel(a_ref, w_ref, order_ref, out_ref):
@@ -415,7 +434,7 @@
     parts = lax.axis_size("tensor")
     steps, rows, width = queries.shape
     tables = (adapter_rows, adapter_rank, adapter_owner)
-    attended, down, up, pick, place, order = attend(
+    attended, spread, down, up, pick, place, order = attend(
         queries,
         new_keys,
         new_values,
@@ -427,8 +446,8 @@
         tables,
         parts,
     )
-    blocks = gather(attended, parts)
-    send, gathered = deltas(blocks, pick, down, up)
+    blocks = gather(attended, spread, parts)
+    send, gathered = deltas(blocks, pick, down, up, parts)
     delta = lax.all_to_all(send, "tensor", split_axis=0, concat_axis=0, tiled=True)
     base = base_part(gathered, out_weight, order)
     return join(base, place, delta, steps)

time: 47.7 us -> 59.5 us (1.25)
  local copies, waits for them, and re-layouts: 3.38 us -> 9.22 us
  waiting for transfers between devices: 13.4 us -> 18.5 us
  Pallas kernels: 11.6 us -> 14.3 us
  starting transfers between devices: 19 us -> 17 us
    all_to_all x0 -> x2, starting transfers between devices: none -> 10.9 us  [exchange(): lax.all_to_all(x, 'tensor', 0, 0, axis_index_groups=quads, tiled=True)]
    ppermute x15 -> x3, starting transfers between devices: 13.4 us -> 2.59 us  [swap(): return lax.ppermute(x, 'tensor', [(i, i ^ bits) for i in range(parts)])]
    all_to_all x0 -> x2, waiting for transfers between devices: none -> 7.97 us  [exchange(): lax.all_to_all(x, 'tensor', 0, 0, axis_index_groups=quads, tiled=True)]
    unnamed x2 -> x10, local copies, waits for them, and re-layouts: 3.38 us -> 9.22 us
    all_to_all x1, starting transfers between devices: 5.59 us -> 3.53 us  [per_device(): lax.all_to_all(send, 'tensor', split_axis=0, concat_axis=0, tiled=True)]
    pallas_call x1 -> x2, Pallas kernels: 2.2 us -> 4.1 us  [the longest x1 3.25 us: deltas(): pl.pallas_call(delta_kernel, out_shape=(jax.ShapeDtypeStruct((parts, slot...]
    all_to_all x1, waiting for transfers between devices: 4.25 us -> 2.6 us  [per_device(): lax.all_to_all(send, 'tensor', split_axis=0, concat_axis=0, tiled=True)]
    ppermute x15 -> x3, waiting for transfers between devices: 9.16 us -> 7.9 us  [swap(): return lax.ppermute(x, 'tensor', [(i, i ^ bits) for i in range(parts)])]
  transfers between devices with their start and end apart: 16 -> 6, of which waited for: 7 -> 5; matrix products, arithmetic and copies ran while one was open for 0% -> 0% of each run, Pallas kernels for 5% -> 6%
where the time goes in v10:
time: 59.5 us; the launch traced here: 59.1 us
  waiting for transfers between devices  18.5 us (31%)
  starting transfers between devices  17 us (29%)
  Pallas kernels  14.3 us (24%)
  local copies, waits for them, and re-layouts  9.22 us (15%)
    all_to_all x2, starting transfers between devices, exchange(): lax.all_to_all(x, 'tensor', 0, 0, axis_index_groups=quads, tiled=True)  10.9 us
    unnamed x10, local copies, waits for them, and re-layouts  9.22 us
    all_to_all x2, waiting for transfers between devices, exchange(): lax.all_to_all(x, 'tensor', 0, 0, axis_index_groups=quads, tiled=True)  7.97 us
    ppermute x3, waiting for transfers between devices, swap(): return lax.ppermute(x, 'tensor', [(i, i ^ bits) for i in range(parts)])  7.9 us
    pallas_call x1, Pallas kernels, attend(): pl.pallas_call(attend_kernel, out_shape=[jax.ShapeDtypeStruct(shape, BF16...  6.95 us
    all_to_all x1, starting transfers between devices, per_device(): lax.all_to_all(send, 'tensor', split_axis=0, concat_axis=0, tiled=True)  3.53 us
    pallas_call x1, Pallas kernels, deltas(): pl.pallas_call(delta_kernel, out_shape=(jax.ShapeDtypeStruct((parts, slot...  3.25 us
    all_to_all x1, waiting for transfers between devices, per_device(): lax.all_to_all(send, 'tensor', split_axis=0, concat_axis=0, tiled=True)  2.6 us
  transfers between devices with their start and end apart: 6, of which 5 were waited for; matrix products, arithmetic and copies ran while one was open for 0% of the time, Pallas kernels for 6%

profile of v10, /device:TPU:0, one launch (start us, length us, event | category | flops | bytes accessed | tf_op | source)
XLA Modules:
  0.0 59.1 jit_solution(9156373313907767142)
XLA Ops:
  0.0 6.9 %attend.1 = (bf16[8,8192]{1,0:T(8,128)(2,1)S(1)}, bf16[4,8,8192]{2,1,0:T(8,128)(2,1)}, bf16[8192,128]{1,0:T(8,128)(2,1)S(1)}, bf16[8192,128]{1,0:T(8,128)(2,1)S(...) custom-call(s32[4]{0:T(128)} %len_hbm.1, bf16[2,4,8192]{2,1,0:T(4,128)(2,1)} %q_hbm.1, ...), custom_call_target="tpu_custom_call" | custom-call | flops 134217728 | bytes 8388608 | tf_op jit(solution)/shard_map/attend/pallas_call | solution.py:247
  7.0 0.0 copy-start.1
  7.0 1.3 %copy-done.1 = bf16[8192,128]{1,0:T(8,128)(2,1)} copy-done((bf16[8192,128]{1,0:T(8,128)(2,1)}, bf16[8192,128]{1,0:T(8,128)(2,1)S(1)}, u32[]{:S(2)}) %copy-start.1) | copy-done | bytes 2097176
  8.3 5.2 %all-to-all-start = ((bf16[4,8,8192]{2,1,0:T(8,128)(2,1)}), bf16[4,8,8192]{2,1,0:T(8,128)(2,1)S(1)}, u32[]{:S(2)}, u32[]{:S(2)}) async-start(bf16[4,8,8192]{2,1,0:T(8,128)(2,1)} %get-tuple-element.14), calls=%async_computation | async-start | bytes 1048576 | tf_op jit(solution)/shard_map/all_to_all | solution.py:321
  13.5 2.6 %collective-permute-start.1 = (bf16[8,8192]{1,0:T(8,128)(2,1)S(1)}, bf16[8,8192]{1,0:T(8,128)(2,1)S(1)}, u32[]{:S(2)}, u32[]{:S(2)}) collective-permute-start(bf16[8,8192]{1,0:T(8,128)(2,1)S(1)} %get-tuple-element.15), channel_id=1, source_target_pairs={{0,8},{1,9},{2,10},{3,11},{4,12},{5,13},{6,14},{7,15},{8,0},{9,1},... | collective-permute-start | bytes 393224 | tf_op jit(solution)/shard_map/ppermute | solution.py:292
  16.1 6.0 %collective-permute-done.1.block_ref = bf16[8,8192]{1,0:T(8,128)(2,1)S(1)} collective-permute-done((bf16[8,8192]{1,0:T(8,128)(2,1)S(1)}, bf16[8,8192]{1,0:T(8,128)(2,1)S(1)}, u32[]{:S(2)}, u32[]{:S(2)}) %collective-permute-start.1) | collective-permute-done | bytes 131104 | tf_op jit(solution)/shard_map/ppermute | solution.py:292
  22.1 0.8 %spread.1 = bf16[4,8,8192]{2,1,0:T(8,128)(2,1)} custom-call(bf16[8,8192]{1,0:T(8,128)(2,1)S(1)} %collective-permute-done.1.block_ref), custom_call_target="tpu_custom_call" | custom-call | bytes 655360 | tf_op jit(solution)/shard_map/spread/pallas_call | solution.py:302
  23.0 1.4 %all-to-all-done.refs_0_ = bf16[4,8,8192]{2,1,0:T(8,128)(2,1)S(1)} async-done(((bf16[4,8,8192]{2,1,0:T(8,128)(2,1)}), bf16[4,8,8192]{2,1,0:T(8,128)(2,1)S(1)}, u32[]{:S(2)}, u32[]{:S(2)}) %all-to-all-start) | async-done | bytes 524320 | tf_op jit(solution)/shard_map/all_to_all | solution.py:321
  24.3 5.7 %all-to-all-start.1 = ((bf16[4,8,8192]{2,1,0:T(8,128)(2,1)}), bf16[4,8,8192]{2,1,0:T(8,128)(2,1)S(1)}, u32[]{:S(2)}, u32[]{:S(2)}) async-start(bf16[4,8,8192]{2,1,0:T(8,128)(2,1)} %spread.1), calls=%async_computation.1 | async-start | bytes 1048576 | tf_op jit(solution)/shard_map/all_to_all | solution.py:321
  30.0 0.0 collective-permute-start
  30.0 6.6 %all-to-all-done.1.refs_2_ = bf16[4,8,8192]{2,1,0:T(8,128)(2,1)S(1)} async-done(((bf16[4,8,8192]{2,1,0:T(8,128)(2,1)}), bf16[4,8,8192]{2,1,0:T(8,128)(2,1)S(1)}, u32[]{:S(2)}, u32[]{:S(2)}) %all-to-all-start.1) | async-done | bytes 524320 | tf_op jit(solution)/shard_map/all_to_all | solution.py:321
  36.6 0.0 collective-permute-start.2
  36.6 0.0 collective-permute-done.refs_1_
  36.6 1.9 %collective-permute-done.2.refs_3_ = bf16[4,8,8192]{2,1,0:T(8,128)(2,1)S(1)} collective-permute-done((bf16[4,8,8192]{2,1,0:T(8,128)(2,1)S(1)}, bf16[4,8,8192]{2,1,0:T(8,128)(2,1)S(1)}, u32[]{:S(2)}, u32[]{:S(2)}) %collective-permute-start.2) | collective-permute-done | bytes 524320 | tf_op jit(solution)/shard_map/ppermute | solution.py:292
  38.5 0.0 copy-start.2
  38.5 1.6 %copy-done.2 = bf16[8192,128]{1,0:T(8,128)(2,1)S(1)} copy-done((bf16[8192,128]{1,0:T(8,128)(2,1)S(1)}, bf16[8192,128]{1,0:T(8,128)(2,1)}, u32[]{:S(2)}) %copy-start.2) | copy-done | bytes 2097176
  40.1 3.2 %delta.1 = (bf16[16,16,512]{2,1,0:T(8,128)(2,1)}, bf16[128,8192]{1,0:T(8,128)(2,1)S(1)}) custom-call(bf16[4,8,8192]{2,1,0:T(8,128)(2,1)S(1)} %all-to-all-done.refs_0_, bf16[4,8,8192]{2,1,0:T(8,128)(2,1)} %collective-permute-done.refs_1_, bf16[4,8,8192]{2,1,0:T(8,128)(2,1)S(1)} %all-to-all-done.1.refs_2_, ...), custom_call_target="tpu_custom_call" | custom-call | flops 301989888 | bytes 8650752 | tf_op jit(solution)/shard_map/delta/pallas_call | solution.py:351
  43.4 0.0 copy-start.3
  43.4 1.3 %copy-done.3 = bf16[128,8192]{1,0:T(8,128)(2,1)} copy-done((bf16[128,8192]{1,0:T(8,128)(2,1)}, bf16[128,8192]{1,0:T(8,128)(2,1)S(1)}, u32[]{:S(2)}) %copy-start.3) | copy-done | bytes 2097176
  44.7 3.5 %all-to-all-start.2 = ((bf16[16,16,512]{2,1,0:T(8,128)(2,1)}), bf16[16,16,512]{2,1,0:T(8,128)(2,1)S(1)}, u32[]{:S(2)}, u32[]{:S(2)}) async-start(bf16[16,16,512]{2,1,0:T(8,128)(2,1)} %get-tuple-element.22), calls=%async_computation.2 | async-start | bytes 524288 | tf_op jit(solution)/shard_map/all_to_all | solution.py:451
  48.2 0.0 copy-start
  48.2 3.4 %copy-done = bf16[8192,512]{1,0:T(8,128)(2,1)S(1)} copy-done((bf16[8192,512]{1,0:T(8,128)(2,1)S(1)}, bf16[8192,512]{1,0:T(8,128)(2,1)}, u32[]{:S(2)}) %copy-start) | copy-done | bytes 8388632
  51.6 0.0 copy-start.4
  51.6 1.6 %copy-done.4 = bf16[128,8192]{1,0:T(8,128)(2,1)S(1)} copy-done((bf16[128,8192]{1,0:T(8,128)(2,1)S(1)}, bf16[128,8192]{1,0:T(8,128)(2,1)}, u32[]{:S(2)}) %copy-start.4) | copy-done | bytes 2097176
  53.2 2.4 %base.1.base_ref = f32[128,512]{1,0:T(8,128)S(1)} custom-call(bf16[128,8192]{1,0:T(8,128)(2,1)S(1)} %copy-done.4, bf16[8192,512]{1,0:T(8,128)(2,1)S(1)} %copy-done, bf16[128,128]{1,0:T(8,128)(2,1)S(1)} %get-tuple-element.20.order_ref), custom_call_target="tpu_custom_call" | custom-call | flops 1342177280 | bytes 10747904 | tf_op jit(solution)/shard_map/base/pallas_call | solution.py:383
  55.6 2.6 %all-to-all-done.2.delta_ref = bf16[16,16,512]{2,1,0:T(8,128)(2,1)S(1)} async-done(((bf16[16,16,512]{2,1,0:T(8,128)(2,1)}), bf16[16,16,512]{2,1,0:T(8,128)(2,1)S(1)}, u32[]{:S(2)}, u32[]{:S(2)}) %all-to-all-start.2) | async-done | bytes 262176 | tf_op jit(solution)/shard_map/all_to_all | solution.py:451
  58.2 0.8 %join.1 = bf16[2,64,512]{2,1,0:T(8,128)(2,1)} custom-call(f32[128,512]{1,0:T(8,128)S(1)} %base.1.base_ref, bf16[128,256]{1,0:T(8,128)(2,1)S(1)} %get-tuple-element.21.place_ref, bf16[16,16,512]{2,1,0:T(8,128)(2,1)S(1)} %all-to-all-done.2.delta_ref), custom_call_target="tpu_custom_call" | custom-call | tf_op jit(solution)/shard_map/join/pallas_call | solution.py:410
Async XLA Ops:
  7.0 1.3 %copy-start.1 = (bf16[8192,128]{1,0:T(8,128)(2,1)}, bf16[8192,128]{1,0:T(8,128)(2,1)S(1)}, u32[]{:S(2)}) copy-start(bf16[8192,128]{1,0:T(8,128)(2,1)S(1)} %get-tuple-element.18.refs_6_) | copy-start | bytes 6291460
  8.3 16.0 %all-to-all-start = ((bf16[4,8,8192]{2,1,0:T(8,128)(2,1)}), bf16[4,8,8192]{2,1,0:T(8,128)(2,1)S(1)}, u32[]{:S(2)}, u32[]{:S(2)}) async-start(bf16[4,8,8192]{2,1,0:T(8,128)(2,1)} %get-tuple-element.14), calls=%async_computation | async-start | bytes 1048576 | tf_op jit(solution)/shard_map/all_to_all | solution.py:321
  13.5 8.6 %collective-permute-start.1 = (bf16[8,8192]{1,0:T(8,128)(2,1)S(1)}, bf16[8,8192]{1,0:T(8,128)(2,1)S(1)}, u32[]{:S(2)}, u32[]{:S(2)}) collective-permute-start(bf16[8,8192]{1,0:T(8,128)(2,1)S(1)} %get-tuple-element.15), channel_id=1, source_target_pairs={{0,8},{1,9},{2,10},{3,11},{4,12},{5,13},{6,14},{7,15},{8,0},{9,1},... | collective-permute-start | bytes 393224 | tf_op jit(solution)/shard_map/ppermute | solution.py:292
  24.3 12.3 %all-to-all-start.1 = ((bf16[4,8,8192]{2,1,0:T(8,128)(2,1)}), bf16[4,8,8192]{2,1,0:T(8,128)(2,1)S(1)}, u32[]{:S(2)}, u32[]{:S(2)}) async-start(bf16[4,8,8192]{2,1,0:T(8,128)(2,1)} %spread.1), calls=%async_computation.1 | async-start | bytes 1048576 | tf_op jit(solution)/shard_map/all_to_all | solution.py:321
  30.0 6.6 %collective-permute-start = (bf16[4,8,8192]{2,1,0:T(8,128)(2,1)S(1)}, bf16[4,8,8192]{2,1,0:T(8,128)(2,1)}, u32[]{:S(2)}, u32[]{:S(2)}) collective-permute-start(bf16[4,8,8192]{2,1,0:T(8,128)(2,1)S(1)} %all-to-all-done.refs_0_), channel_id=1, source_target_pairs={{0,1},{1,0},{2,3},{3,2},{4,5},{5,4},{6,7},{7,6},{8,9},{9,8},{10,11... | collective-permute-start | bytes 1572872 | tf_op jit(solution)/shard_map/ppermute | solution.py:292
  36.6 1.9 %collective-permute-start.2 = (bf16[4,8,8192]{2,1,0:T(8,128)(2,1)S(1)}, bf16[4,8,8192]{2,1,0:T(8,128)(2,1)S(1)}, u32[]{:S(2)}, u32[]{:S(2)}) collective-permute-start(bf16[4,8,8192]{2,1,0:T(8,128)(2,1)S(1)} %all-to-all-done.1.refs_2_), channel_id=1, source_target_pairs={{0,1},{1,0},{2,3},{3,2},{4,5},{5,4},{6,7},{7,6},{8,9},{9,8},{10,11... | collective-permute-start | bytes 1572872 | tf_op jit(solution)/shard_map/ppermute | solution.py:292
  38.5 1.6 %copy-start.2 = (bf16[8192,128]{1,0:T(8,128)(2,1)S(1)}, bf16[8192,128]{1,0:T(8,128)(2,1)}, u32[]{:S(2)}) copy-start(bf16[8192,128]{1,0:T(8,128)(2,1)} %copy-done.1) | copy-start | bytes 6291460
  43.4 1.3 %copy-start.3 = (bf16[128,8192]{1,0:T(8,128)(2,1)}, bf16[128,8192]{1,0:T(8,128)(2,1)S(1)}, u32[]{:S(2)}) copy-start(bf16[128,8192]{1,0:T(8,128)(2,1)S(1)} %get-tuple-element.19.a_ref) | copy-start | bytes 6291460
  44.7 13.5 %all-to-all-start.2 = ((bf16[16,16,512]{2,1,0:T(8,128)(2,1)}), bf16[16,16,512]{2,1,0:T(8,128)(2,1)S(1)}, u32[]{:S(2)}, u32[]{:S(2)}) async-start(bf16[16,16,512]{2,1,0:T(8,128)(2,1)} %get-tuple-element.22), calls=%async_computation.2 | async-start | bytes 524288 | tf_op jit(solution)/shard_map/all_to_all | solution.py:451
  48.2 3.4 %copy-start = (bf16[8192,512]{1,0:T(8,128)(2,1)S(1)}, bf16[8192,512]{1,0:T(8,128)(2,1)}, u32[]{:S(2)}) copy-start(bf16[8192,512]{1,0:T(8,128)(2,1)} %w_ref.1) | copy-start | bytes 25165828
  51.6 1.6 %copy-start.4 = (bf16[128,8192]{1,0:T(8,128)(2,1)S(1)}, bf16[128,8192]{1,0:T(8,128)(2,1)}, u32[]{:S(2)}) copy-start(bf16[128,8192]{1,0:T(8,128)(2,1)} %copy-done.3) | copy-start | bytes 6291460

commit v11 on v8

--- a/solution.py
+++ b/solution.py
@@ -1,4 +1,5 @@
 import functools
+import math
 
 import jax
 import jax.numpy as jnp
@@ -13,7 +14,7 @@
 GROUP = HQ // KVH
 MOST = 8
 RING = 16
-ORDER = [0, 1, 8, 9, 12, 13, 14, 15, 10, 11, 4, 5, 2, 3, 6, 7]
+ORDER = [0, 1, 6, 7, 4, 5, 2, 3, 8, 9, 12, 13, 14, 15, 10, 11]
 F32 = jnp.float32
 BF16 = jnp.bfloat16
 NT = (((1,), (1,)), ((), ()))
@@ -132,11 +133,13 @@
     for r in range(rows):
         queue += [values[r + 1]] if r + 1 < rows else [store]
         queue += [keys[r + 2]] if r + 2 < rows else []
-    for copy in small + queue[0] + queue[1] + queue[2]:
+    for copy in small + queue[0]:
+        copy.start()
+    for copy in small:
+        copy.wait()
+    for copy in queue[1] + queue[2]:
         copy.start()
     queue = queue[3:]
-    for copy in small:
-        copy.wait()
 
     flat = jnp.concatenate([q_ref[t].astype(F32) for t in range(steps)], axis=0)
     heads = []
@@ -162,7 +165,7 @@
 
     write_plan(rows, count_ref, rank_ref, owner_ref, pick_ref, place_ref, order_ref)
 
-    scale = HD ** (-0.5)
+    rate = HD ** (-0.5) * math.log2(math.e)
     pairs = [
         (slice(k * pack, (k + 2) * pack), slice(k * HD, (k + 2) * HD)) for k in range(0, KVH, 2)
     ]
@@ -185,14 +188,14 @@
         slot = iota(fresh.shape, 0)
         step = (iota(fresh.shape, 1) // GROUP) % steps
         seen = (slot < both) & (slot % rows == r) & (slot // rows <= step)
-        fresh = jnp.where(seen, fresh * scale, -jnp.inf)
+        fresh = jnp.where(seen, fresh, -jnp.inf)
         older = raw[r % 2]
-        older = jnp.where(iota(older.shape, 0) < len_ref[r], older * scale, -jnp.inf)
+        older = jnp.where(iota(older.shape, 0) < len_ref[r], older, -jnp.inf)
         top = jnp.maximum(
             jnp.max(older, axis=0, keepdims=True), jnp.max(fresh, axis=0, keepdims=True)
         )
-        e_older = jnp.exp(older - top)
-        e_fresh = jnp.exp(fresh - top)
+        e_older = jnp.exp2((older - top) * rate)
+        e_fresh = jnp.exp2((fresh - top) * rate)
         total = jnp.sum(e_older, axis=0, keepdims=True) + jnp.sum(e_fresh, axis=0, keepdims=True)
         inverse = 1.0 / total
         p_older = jnp.transpose((e_older * inverse).astype(BF16))
@@ -295,7 +298,7 @@
     held[far] = swap(block, far, parts)
     held[near] = swap(block, near, parts)
     held[y] = swap(block, y, parts)
-    held[near | y] = swap(held[y], near, parts)
+    held[near | y] = swap(block, near | y, parts)
     held[far | y] = swap(held[far], y, parts)
     held[far | near | y] = swap(held[far], near | y, parts)
     held[far | near] = swap(held[far], near, parts)

time: 47.7 us -> 47.7 us (level)
  starting transfers between devices: 19 us -> 17.7 us
  waiting for transfers between devices: 13.4 us -> 14.1 us
  Pallas kernels: 11.6 us -> 12.1 us
    ppermute x15, starting transfers between devices: 13.4 us -> 12.4 us  [swap(): return lax.ppermute(x, 'tensor', [(i, i ^ bits) for i in range(parts)])]
    ppermute x15, waiting for transfers between devices: 9.16 us -> 9.91 us  [swap(): return lax.ppermute(x, 'tensor', [(i, i ^ bits) for i in range(parts)])]
    pallas_call x1, Pallas kernels: 6.14 us -> 6.66 us  [attend(): pl.pallas_call(attend_kernel, out_shape=[jax.ShapeDtypeStruct(shape, BF16...]
  transfers between devices with their start and end apart: 16 -> 16, of which waited for: 7 -> 10; matrix products, arithmetic and copies ran while one was open for 0% -> 0% of each run, Pallas kernels for 5% -> 5%
where the time goes in v11:
time: 47.7 us; the launch traced here: 47.4 us
  starting transfers between devices  17.7 us (37%)
  waiting for transfers between devices  14.1 us (30%)
  Pallas kernels  12.1 us (25%)
  local copies, waits for them, and re-layouts  3.38 us (7%)
    ppermute x15, starting transfers between devices, swap(): return lax.ppermute(x, 'tensor', [(i, i ^ bits) for i in range(parts)])  12.4 us
    ppermute x15, waiting for transfers between devices, swap(): return lax.ppermute(x, 'tensor', [(i, i ^ bits) for i in range(parts)])  9.91 us
    pallas_call x1, Pallas kernels, attend(): pl.pallas_call(attend_kernel, out_shape=[jax.ShapeDtypeStruct(shape, BF16...  6.66 us
    all_to_all x1, starting transfers between devices, per_device(): lax.all_to_all(send, 'tensor', split_axis=0, concat_axis=0, tiled=True)  5.37 us
    all_to_all x1, waiting for transfers between devices, per_device(): lax.all_to_all(send, 'tensor', split_axis=0, concat_axis=0, tiled=True)  4.24 us
    unnamed x2, local copies, waits for them, and re-layouts  3.38 us
    pallas_call x1, Pallas kernels, base_part(): pl.pallas_call(base_kernel, out_shape=jax.ShapeDtypeStruct((total, cols),...  2.42 us
    pallas_call x1, Pallas kernels, deltas(): pl.pallas_call(functools.partial(delta_kernel, at_slot), out_shape=(jax.S...  2.2 us
  transfers between devices with their start and end apart: 16, of which 10 were waited for; matrix products, arithmetic and copies ran while one was open for 0% of the time, Pallas kernels for 5%

profile of v11, /device:TPU:0, one launch (start us, length us, event | category | flops | bytes accessed | tf_op | source)
XLA Modules:
  0.0 47.4 jit_solution(10746157894436678286)
XLA Ops:
  0.0 6.7 %attend.1 = (bf16[8,8192]{1,0:T(8,128)(2,1)S(1)}, bf16[8192,128]{1,0:T(8,128)(2,1)S(1)}, bf16[8192,128]{1,0:T(8,128)(2,1)S(1)}, bf16[16,128]{1,0:T(8,128)(2,1)S(...) custom-call(s32[4]{0:T(128)} %len_hbm.1, bf16[2,4,8192]{2,1,0:T(4,128)(2,1)} %q_hbm.1, ...), custom_call_target="tpu_custom_call" | custom-call | flops 134217728 | bytes 8388608 | tf_op jit(solution)/shard_map/attend/pallas_call | solution.py:244
  6.7 4.1 %collective-permute-start.7 = (bf16[8,8192]{1,0:T(8,128)(2,1)S(1)}, bf16[8,8192]{1,0:T(8,128)(2,1)S(1)}, u32[]{:S(2)}, u32[]{:S(2)}) collective-permute-start(bf16[8,8192]{1,0:T(8,128)(2,1)S(1)} %get-tuple-element.13.refs_0_), channel_id=1, source_target_pairs={{0,8},{1,9},{2,10},{3,11},{4,12},{5,13},{6,14},{7,15},{8,0},{9,1},... | collective-permute-start | bytes 393224 | tf_op jit(solution)/shard_map/ppermute | solution.py:289
  10.8 1.5 %collective-permute-start.5 = (bf16[8,8192]{1,0:T(8,128)(2,1)S(1)}, bf16[8,8192]{1,0:T(8,128)(2,1)S(1)}, u32[]{:S(2)}, u32[]{:S(2)}) collective-permute-start(bf16[8,8192]{1,0:T(8,128)(2,1)S(1)} %get-tuple-element.13.refs_0_), channel_id=1, source_target_pairs={{0,2},{1,3},{2,0},{3,1},{4,6},{5,7},{6,4},{7,5},{8,10},{9,11},{10,... | collective-permute-start | bytes 393224 | tf_op jit(solution)/shard_map/ppermute | solution.py:289
  12.3 1.6 %collective-permute-start.3 = (bf16[8,8192]{1,0:T(8,128)(2,1)S(1)}, bf16[8,8192]{1,0:T(8,128)(2,1)S(1)}, u32[]{:S(2)}, u32[]{:S(2)}) collective-permute-start(bf16[8,8192]{1,0:T(8,128)(2,1)S(1)} %get-tuple-element.13.refs_0_), channel_id=1, source_target_pairs={{0,4},{1,5},{2,6},{3,7},{4,0},{5,1},{6,2},{7,3},{8,12},{9,13},{10,... | collective-permute-start | bytes 393224 | tf_op jit(solution)/shard_map/ppermute | solution.py:289
  13.9 0.4 collective-permute-start.1
  14.3 0.0 collective-permute-start
  14.3 2.9 %collective-permute-done.7.refs_8_ = bf16[8,8192]{1,0:T(8,128)(2,1)S(1)} collective-permute-done((bf16[8,8192]{1,0:T(8,128)(2,1)S(1)}, bf16[8,8192]{1,0:T(8,128)(2,1)S(1)}, u32[]{:S(2)}, u32[]{:S(2)}) %collective-permute-start.7) | collective-permute-done | bytes 131104 | tf_op jit(solution)/shard_map/ppermute | solution.py:289
  17.2 1.6 %collective-permute-start.13 = (bf16[8,8192]{1,0:T(8,128)(2,1)S(1)}, bf16[8,8192]{1,0:T(8,128)(2,1)S(1)}, u32[]{:S(2)}, u32[]{:S(2)}) collective-permute-start(bf16[8,8192]{1,0:T(8,128)(2,1)S(1)} %collective-permute-done.7.refs_8_), channel_id=1, source_target_pairs={{0,2},{1,3},{2,0},{3,1},{4,6},{5,7},{6,4},{7,5},{8,10},{9,11},{10,... | collective-permute-start | bytes 393224 | tf_op jit(solution)/shard_map/ppermute | solution.py:289
  18.7 0.0 collective-permute-done.5.refs_6_
  18.8 0.6 %collective-permute-start.11 = (bf16[8,8192]{1,0:T(8,128)(2,1)S(1)}, bf16[8,8192]{1,0:T(8,128)(2,1)S(1)}, u32[]{:S(2)}, u32[]{:S(2)}) collective-permute-start(bf16[8,8192]{1,0:T(8,128)(2,1)S(1)} %collective-permute-done.7.refs_8_), channel_id=1, source_target_pairs={{0,6},{1,7},{2,4},{3,5},{4,2},{5,3},{6,0},{7,1},{8,14},{9,15},{10,... | collective-permute-start | bytes 393224 | tf_op jit(solution)/shard_map/ppermute | solution.py:289
  19.3 0.3 collective-permute-done.3.refs_4_
  19.6 1.0 %collective-permute-start.9 = (bf16[8,8192]{1,0:T(8,128)(2,1)S(1)}, bf16[8,8192]{1,0:T(8,128)(2,1)S(1)}, u32[]{:S(2)}, u32[]{:S(2)}) collective-permute-start(bf16[8,8192]{1,0:T(8,128)(2,1)S(1)} %collective-permute-done.7.refs_8_), channel_id=1, source_target_pairs={{0,4},{1,5},{2,6},{3,7},{4,0},{5,1},{6,2},{7,3},{8,12},{9,13},{10,... | collective-permute-start | bytes 393224 | tf_op jit(solution)/shard_map/ppermute | solution.py:289
  20.7 1.9 %collective-permute-done.1.refs_2_ = bf16[8,8192]{1,0:T(8,128)(2,1)S(1)} collective-permute-done((bf16[8,8192]{1,0:T(8,128)(2,1)S(1)}, bf16[8,8192]{1,0:T(8,128)(2,1)S(1)}, u32[]{:S(2)}, u32[]{:S(2)}) %collective-permute-start.1) | collective-permute-done | bytes 131104 | tf_op jit(solution)/shard_map/ppermute | solution.py:289
  22.6 0.5 %collective-permute-start.6 = (bf16[8,8192]{1,0:T(8,128)(2,1)S(1)}, bf16[8,8192]{1,0:T(8,128)(2,1)S(1)}, u32[]{:S(2)}, u32[]{:S(2)}) collective-permute-start(bf16[8,8192]{1,0:T(8,128)(2,1)S(1)} %collective-permute-done.5.refs_6_), channel_id=1, source_target_pairs={{0,1},{1,0},{2,3},{3,2},{4,5},{5,4},{6,7},{7,6},{8,9},{9,8},{10,11... | collective-permute-start | bytes 393224 | tf_op jit(solution)/shard_map/ppermute | solution.py:289
  23.1 3.4 %collective-permute-done.13.refs_14_ = bf16[8,8192]{1,0:T(8,128)(2,1)S(1)} collective-permute-done((bf16[8,8192]{1,0:T(8,128)(2,1)S(1)}, bf16[8,8192]{1,0:T(8,128)(2,1)S(1)}, u32[]{:S(2)}, u32[]{:S(2)}) %collective-permute-start.13) | collective-permute-done | bytes 131104 | tf_op jit(solution)/shard_map/ppermute | solution.py:289
  26.6 0.5 %collective-permute-start.2 = (bf16[8,8192]{1,0:T(8,128)(2,1)S(1)}, bf16[8,8192]{1,0:T(8,128)(2,1)S(1)}, u32[]{:S(2)}, u32[]{:S(2)}) collective-permute-start(bf16[8,8192]{1,0:T(8,128)(2,1)S(1)} %collective-permute-done.1.refs_2_), channel_id=1, source_target_pairs={{0,1},{1,0},{2,3},{3,2},{4,5},{5,4},{6,7},{7,6},{8,9},{9,8},{10,11... | collective-permute-start | bytes 393224 | tf_op jit(solution)/shard_map/ppermute | solution.py:289
  27.1 0.0 collective-permute-done.9.refs_10_
  27.1 0.1 collective-permute-start.14
  27.1 0.5 collective-permute-start.12
  27.6 0.1 collective-permute-start.10
  27.7 0.2 collective-permute-done.4.refs_5_
  27.9 0.2 collective-permute-done.2.refs_3_
  28.1 0.3 collective-permute-done.14.refs_15_
  28.4 0.2 collective-permute-done.12.refs_13_
  28.6 0.3 collective-permute-done.10.refs_11_
  29.0 2.2 %delta.1 = (bf16[16,16,512]{2,1,0:T(8,128)(2,1)}, bf16[128,8192]{1,0:T(8,128)(2,1)S(1)}) custom-call(bf16[8,8192]{1,0:T(8,128)(2,1)S(1)} %get-tuple-element.13.refs_0_, bf16[8,8192]{1,0:T(8,128)(2,1)S(1)} %collective-permute-done.refs_1_, bf16[8,8192]{1,0:T(8,128)(2,1)S(1)} %collective-permute-done.1.refs_2_, ...), custom_call_target="tpu_custom_call" | custom-call | flops 301989888 | bytes 8650752 | tf_op jit(solution)/shard_map/delta/pallas_call | solution.py:335
  31.2 5.4 %all-to-all-start = ((bf16[16,16,512]{2,1,0:T(8,128)(2,1)}), bf16[16,16,512]{2,1,0:T(8,128)(2,1)S(1)}, u32[]{:S(2)}, u32[]{:S(2)}) async-start(bf16[16,16,512]{2,1,0:T(8,128)(2,1)} %get-tuple-element.20), calls=%async_computation | async-start | bytes 524288 | tf_op jit(solution)/shard_map/all_to_all | solution.py:435
  36.5 0.0 copy-start
  36.5 3.4 %copy-done = bf16[8192,512]{1,0:T(8,128)(2,1)S(1)} copy-done((bf16[8192,512]{1,0:T(8,128)(2,1)S(1)}, bf16[8192,512]{1,0:T(8,128)(2,1)}, u32[]{:S(2)}) %copy-start) | copy-done | bytes 8388632
  39.9 2.4 %base.1.base_ref = f32[128,512]{1,0:T(8,128)S(1)} custom-call(bf16[128,8192]{1,0:T(8,128)(2,1)S(1)} %get-tuple-element.17.a_ref, bf16[8192,512]{1,0:T(8,128)(2,1)S(1)} %copy-done, bf16[128,128]{1,0:T(8,128)(2,1)S(1)} %get-tuple-element.18.order_ref), custom_call_target="tpu_custom_call" | custom-call | flops 1342177280 | bytes 10747904 | tf_op jit(solution)/shard_map/base/pallas_call | solution.py:367
  42.3 4.2 %all-to-all-done.delta_ref = bf16[16,16,512]{2,1,0:T(8,128)(2,1)S(1)} async-done(((bf16[16,16,512]{2,1,0:T(8,128)(2,1)}), bf16[16,16,512]{2,1,0:T(8,128)(2,1)S(1)}, u32[]{:S(2)}, u32[]{:S(2)}) %all-to-all-start) | async-done | bytes 262176 | tf_op jit(solution)/shard_map/all_to_all | solution.py:435
  46.6 0.8 %join.1 = bf16[2,64,512]{2,1,0:T(8,128)(2,1)} custom-call(f32[128,512]{1,0:T(8,128)S(1)} %base.1.base_ref, bf16[128,256]{1,0:T(8,128)(2,1)S(1)} %get-tuple-element.19.place_ref, bf16[16,16,512]{2,1,0:T(8,128)(2,1)S(1)} %all-to-all-done.delta_ref), custom_call_target="tpu_custom_call" | custom-call | tf_op jit(solution)/shard_map/join/pallas_call | solution.py:394
  (6 shorter events, 0.0 us)
Async XLA Ops:
  6.7 10.5 %collective-permute-start.7 = (bf16[8,8192]{1,0:T(8,128)(2,1)S(1)}, bf16[8,8192]{1,0:T(8,128)(2,1)S(1)}, u32[]{:S(2)}, u32[]{:S(2)}) collective-permute-start(bf16[8,8192]{1,0:T(8,128)(2,1)S(1)} %get-tuple-element.13.refs_0_), channel_id=1, source_target_pairs={{0,8},{1,9},{2,10},{3,11},{4,12},{5,13},{6,14},{7,15},{8,0},{9,1},... | collective-permute-start | bytes 393224 | tf_op jit(solution)/shard_map/ppermute | solution.py:289
  10.8 8.0 %collective-permute-start.5 = (bf16[8,8192]{1,0:T(8,128)(2,1)S(1)}, bf16[8,8192]{1,0:T(8,128)(2,1)S(1)}, u32[]{:S(2)}, u32[]{:S(2)}) collective-permute-start(bf16[8,8192]{1,0:T(8,128)(2,1)S(1)} %get-tuple-element.13.refs_0_), channel_id=1, source_target_pairs={{0,2},{1,3},{2,0},{3,1},{4,6},{5,7},{6,4},{7,5},{8,10},{9,11},{10,... | collective-permute-start | bytes 393224 | tf_op jit(solution)/shard_map/ppermute | solution.py:289
  12.3 7.3 %collective-permute-start.3 = (bf16[8,8192]{1,0:T(8,128)(2,1)S(1)}, bf16[8,8192]{1,0:T(8,128)(2,1)S(1)}, u32[]{:S(2)}, u32[]{:S(2)}) collective-permute-start(bf16[8,8192]{1,0:T(8,128)(2,1)S(1)} %get-tuple-element.13.refs_0_), channel_id=1, source_target_pairs={{0,4},{1,5},{2,6},{3,7},{4,0},{5,1},{6,2},{7,3},{8,12},{9,13},{10,... | collective-permute-start | bytes 393224 | tf_op jit(solution)/shard_map/ppermute | solution.py:289
  13.9 8.8 %collective-permute-start.1 = (bf16[8,8192]{1,0:T(8,128)(2,1)S(1)}, bf16[8,8192]{1,0:T(8,128)(2,1)S(1)}, u32[]{:S(2)}, u32[]{:S(2)}) collective-permute-start(bf16[8,8192]{1,0:T(8,128)(2,1)S(1)} %get-tuple-element.13.refs_0_), channel_id=1, source_target_pairs={{0,6},{1,7},{2,4},{3,5},{4,2},{5,3},{6,0},{7,1},{8,14},{9,15},{10,... | collective-permute-start | bytes 393224 | tf_op jit(solution)/shard_map/ppermute | solution.py:289
  14.3 8.4 %collective-permute-start = (bf16[8,8192]{1,0:T(8,128)(2,1)S(1)}, bf16[8,8192]{1,0:T(8,128)(2,1)S(1)}, u32[]{:S(2)}, u32[]{:S(2)}) collective-permute-start(bf16[8,8192]{1,0:T(8,128)(2,1)S(1)} %get-tuple-element.13.refs_0_), channel_id=1, source_target_pairs={{0,1},{1,0},{2,3},{3,2},{4,5},{5,4},{6,7},{7,6},{8,9},{9,8},{10,11... | collective-permute-start | bytes 393224 | tf_op jit(solution)/shard_map/ppermute | solution.py:289
  17.2 9.4 %collective-permute-start.13 = (bf16[8,8192]{1,0:T(8,128)(2,1)S(1)}, bf16[8,8192]{1,0:T(8,128)(2,1)S(1)}, u32[]{:S(2)}, u32[]{:S(2)}) collective-permute-start(bf16[8,8192]{1,0:T(8,128)(2,1)S(1)} %collective-permute-done.7.refs_8_), channel_id=1, source_target_pairs={{0,2},{1,3},{2,0},{3,1},{4,6},{5,7},{6,4},{7,5},{8,10},{9,11},{10,... | collective-permute-start | bytes 393224 | tf_op jit(solution)/shard_map/ppermute | solution.py:289
  18.8 7.8 %collective-permute-start.11 = (bf16[8,8192]{1,0:T(8,128)(2,1)S(1)}, bf16[8,8192]{1,0:T(8,128)(2,1)S(1)}, u32[]{:S(2)}, u32[]{:S(2)}) collective-permute-start(bf16[8,8192]{1,0:T(8,128)(2,1)S(1)} %collective-permute-done.7.refs_8_), channel_id=1, source_target_pairs={{0,6},{1,7},{2,4},{3,5},{4,2},{5,3},{6,0},{7,1},{8,14},{9,15},{10,... | collective-permute-start | bytes 393224 | tf_op jit(solution)/shard_map/ppermute | solution.py:289
  19.6 7.4 %collective-permute-start.9 = (bf16[8,8192]{1,0:T(8,128)(2,1)S(1)}, bf16[8,8192]{1,0:T(8,128)(2,1)S(1)}, u32[]{:S(2)}, u32[]{:S(2)}) collective-permute-start(bf16[8,8192]{1,0:T(8,128)(2,1)S(1)} %collective-permute-done.7.refs_8_), channel_id=1, source_target_pairs={{0,4},{1,5},{2,6},{3,7},{4,0},{5,1},{6,2},{7,3},{8,12},{9,13},{10,... | collective-permute-start | bytes 393224 | tf_op jit(solution)/shard_map/ppermute | solution.py:289
  22.6 4.5 %collective-permute-start.8 = (bf16[8,8192]{1,0:T(8,128)(2,1)S(1)}, bf16[8,8192]{1,0:T(8,128)(2,1)S(1)}, u32[]{:S(2)}, u32[]{:S(2)}) collective-permute-start(bf16[8,8192]{1,0:T(8,128)(2,1)S(1)} %collective-permute-done.7.refs_8_), channel_id=1, source_target_pairs={{0,1},{1,0},{2,3},{3,2},{4,5},{5,4},{6,7},{7,6},{8,9},{9,8},{10,11... | collective-permute-start | bytes 393224 | tf_op jit(solution)/shard_map/ppermute | solution.py:289
  22.6 5.0 %collective-permute-start.6 = (bf16[8,8192]{1,0:T(8,128)(2,1)S(1)}, bf16[8,8192]{1,0:T(8,128)(2,1)S(1)}, u32[]{:S(2)}, u32[]{:S(2)}) collective-permute-start(bf16[8,8192]{1,0:T(8,128)(2,1)S(1)} %collective-permute-done.5.refs_6_), channel_id=1, source_target_pairs={{0,1},{1,0},{2,3},{3,2},{4,5},{5,4},{6,7},{7,6},{8,9},{9,8},{10,11... | collective-permute-start | bytes 393224 | tf_op jit(solution)/shard_map/ppermute | solution.py:289
  26.6 1.3 %collective-permute-start.4 = (bf16[8,8192]{1,0:T(8,128)(2,1)S(1)}, bf16[8,8192]{1,0:T(8,128)(2,1)S(1)}, u32[]{:S(2)}, u32[]{:S(2)}) collective-permute-start(bf16[8,8192]{1,0:T(8,128)(2,1)S(1)} %collective-permute-done.3.refs_4_), channel_id=1, source_target_pairs={{0,1},{1,0},{2,3},{3,2},{4,5},{5,4},{6,7},{7,6},{8,9},{9,8},{10,11... | collective-permute-start | bytes 393224 | tf_op jit(solution)/shard_map/ppermute | solution.py:289
  26.6 1.5 %collective-permute-start.2 = (bf16[8,8192]{1,0:T(8,128)(2,1)S(1)}, bf16[8,8192]{1,0:T(8,128)(2,1)S(1)}, u32[]{:S(2)}, u32[]{:S(2)}) collective-permute-start(bf16[8,8192]{1,0:T(8,128)(2,1)S(1)} %collective-permute-done.1.refs_2_), channel_id=1, source_target_pairs={{0,1},{1,0},{2,3},{3,2},{4,5},{5,4},{6,7},{7,6},{8,9},{9,8},{10,11... | collective-permute-start | bytes 393224 | tf_op jit(solution)/shard_map/ppermute | solution.py:289
  27.1 1.3 %collective-permute-start.14 = (bf16[8,8192]{1,0:T(8,128)(2,1)S(1)}, bf16[8,8192]{1,0:T(8,128)(2,1)S(1)}, u32[]{:S(2)}, u32[]{:S(2)}) collective-permute-start(bf16[8,8192]{1,0:T(8,128)(2,1)S(1)} %collective-permute-done.13.refs_14_), channel_id=1, source_target_pairs={{0,1},{1,0},{2,3},{3,2},{4,5},{5,4},{6,7},{7,6},{8,9},{9,8},{10,11... | collective-permute-start | bytes 393224 | tf_op jit(solution)/shard_map/ppermute | solution.py:289
  27.1 1.5 %collective-permute-start.12 = (bf16[8,8192]{1,0:T(8,128)(2,1)S(1)}, bf16[8,8192]{1,0:T(8,128)(2,1)S(1)}, u32[]{:S(2)}, u32[]{:S(2)}) collective-permute-start(bf16[8,8192]{1,0:T(8,128)(2,1)S(1)} %collective-permute-done.11.refs_12_), channel_id=1, source_target_pairs={{0,1},{1,0},{2,3},{3,2},{4,5},{5,4},{6,7},{7,6},{8,9},{9,8},{10,11... | collective-permute-start | bytes 393224 | tf_op jit(solution)/shard_map/ppermute | solution.py:289
  27.6 1.3 %collective-permute-start.10 = (bf16[8,8192]{1,0:T(8,128)(2,1)S(1)}, bf16[8,8192]{1,0:T(8,128)(2,1)S(1)}, u32[]{:S(2)}, u32[]{:S(2)}) collective-permute-start(bf16[8,8192]{1,0:T(8,128)(2,1)S(1)} %collective-permute-done.9.refs_10_), channel_id=1, source_target_pairs={{0,1},{1,0},{2,3},{3,2},{4,5},{5,4},{6,7},{7,6},{8,9},{9,8},{10,11... | collective-permute-start | bytes 393224 | tf_op jit(solution)/shard_map/ppermute | solution.py:289
  31.2 15.4 %all-to-all-start = ((bf16[16,16,512]{2,1,0:T(8,128)(2,1)}), bf16[16,16,512]{2,1,0:T(8,128)(2,1)S(1)}, u32[]{:S(2)}, u32[]{:S(2)}) async-start(bf16[16,16,512]{2,1,0:T(8,128)(2,1)} %get-tuple-element.20), calls=%async_computation | async-start | bytes 524288 | tf_op jit(solution)/shard_map/all_to_all | solution.py:435
  36.5 3.4 %copy-start = (bf16[8192,512]{1,0:T(8,128)(2,1)S(1)}, bf16[8192,512]{1,0:T(8,128)(2,1)}, u32[]{:S(2)}) copy-start(bf16[8192,512]{1,0:T(8,128)(2,1)} %w_ref.1) | copy-start | bytes 25165828

commit v12 on v11

--- a/solution.py
+++ b/solution.py
@@ -14,7 +14,10 @@
 GROUP = HQ // KVH
 MOST = 8
 RING = 16
-ORDER = [0, 1, 6, 7, 4, 5, 2, 3, 8, 9, 12, 13, 14, 15, 10, 11]
+CORE, Y, NEAR, FAR = 1, 2, 4, 8
+FLIPS = [0, Y, NEAR, FAR, FAR | Y, FAR | NEAR | Y, FAR | NEAR, NEAR | Y]
+FLIPS += [CORE | flip for flip in FLIPS]
+HAND = [0, 6, 5, 11, 1, 7, 4, 10, 3, 9, 2, 8]
 F32 = jnp.float32
 BF16 = jnp.bfloat16
 NT = (((1,), (1,)), ((), ()))
@@ -41,7 +44,12 @@
 
 
 def sender(slot, me, parts):
-    return me ^ slot if parts == RING else slot
+    if parts != RING:
+        return slot
+    flips = jnp.zeros_like(slot)
+    for i, flip in enumerate(FLIPS):
+        flips = jnp.where(slot == i, flip, flips)
+    return me ^ flips
 
 
 def write_plan(rows, count_ref, rank_ref, owner_ref, pick_ref, place_ref, order_ref):
@@ -133,13 +141,13 @@
     for r in range(rows):
         queue += [values[r + 1]] if r + 1 < rows else [store]
         queue += [keys[r + 2]] if r + 2 < rows else []
-    for copy in small + queue[0]:
+    for copy in small + queue[0] + queue[1] + queue[2]:
         copy.start()
     for copy in small:
         copy.wait()
-    for copy in queue[1] + queue[2]:
+    for copy in queue[3] + queue[4]:
         copy.start()
-    queue = queue[3:]
+    queue = queue[5:]
 
     flat = jnp.concatenate([q_ref[t].astype(F32) for t in range(steps)], axis=0)
     heads = []
@@ -289,35 +297,73 @@
     return lax.ppermute(x, "tensor", [(i, i ^ bits) for i in range(parts)])
 
 
+def pack_kernel(own_ref, y_ref, near_ref, out_ref, mixed_ref):
+    for i, src in enumerate((own_ref, y_ref, near_ref)):
+        out_ref[i] = src[...]
+    core = lax.axis_index("tensor") % 2
+
+    @pl.when(core == 0)
+    def _():
+        mixed_ref[...] = near_ref[...]
+
+    @pl.when(core == 1)
+    def _():
+        mixed_ref[...] = y_ref[...]
+
+
+def pack(own, y, near):
+    vmem = pl.BlockSpec(memory_space=pltpu.VMEM)
+    return pl.pallas_call(
+        pack_kernel,
+        out_shape=(
+            jax.ShapeDtypeStruct((3, *own.shape), own.dtype),
+            jax.ShapeDtypeStruct(own.shape, own.dtype),
+        ),
+        in_specs=[vmem] * 3,
+        out_specs=(vmem, vmem),
+        compiler_params=pltpu.CompilerParams(vmem_limit_bytes=4 * 2**20),
+        cost_estimate=pl.CostEstimate(flops=0, bytes_accessed=14 * own.size, transcendentals=0),
+        name="pack",
+    )(own, y, near)
+
+
 def gather(block, parts):
     if parts != RING:
-        whole = lax.all_gather(block, "tensor")
-        return [whole[i] for i in range(parts)]
-    core, y, near, far = 1, 2, 4, 8
-    held = {0: block}
-    held[far] = swap(block, far, parts)
-    held[near] = swap(block, near, parts)
-    held[y] = swap(block, y, parts)
-    held[near | y] = swap(block, near | y, parts)
-    held[far | y] = swap(held[far], y, parts)
-    held[far | near | y] = swap(held[far], near | y, parts)
-    held[far | near] = swap(held[far], near, parts)
-    for slot in list(held):
-        held[slot | core] = swap(held[slot], core, parts)
-    return [held[slot] for slot in range(parts)]
-
-
-def delta_kernel(at_slot, *refs):
+        return [lax.all_gather(block, "tensor")]
+    far = swap(block, FAR, parts)
+    near = swap(block, NEAR, parts)
+    y = swap(block, Y, parts)
+    packed, mixed = pack(block, y, near)
+    far, packed = lax.optimization_barrier((far, packed))
+    across = swap(far, CORE, parts)
+    mixed, across = lax.optimization_barrier((mixed, across))
+    pairs = [(i, i ^ (Y if i % 2 == 0 else NEAR)) for i in range(parts)]
+    blocks = [
+        packed,
+        far,
+        swap(far, Y, parts),
+        swap(far, NEAR | Y, parts),
+        swap(far, NEAR, parts),
+        lax.ppermute(mixed, "tensor", pairs),
+    ]
+    swapped = [across if x is far else swap(x, CORE, parts) for x in blocks]
+    return blocks + swapped
+
+
+def delta_kernel(hand, *refs):
     (*blocks, pick_ref, d_ref, u_ref, out_ref, rows_ref) = refs
-    blocks = [blocks[at_slot.index(i)] for i in range(len(blocks))]
+    blocks = [blocks[hand.index(i)] for i in range(len(blocks))]
     parts, slots, cols = out_ref.shape
-    each, width = blocks[0].shape
+    each, width = blocks[0].shape[-2:]
+    views = []
+    for b in blocks:
+        views += [b.at[i] for i in range(b.shape[0])] if len(b.shape) == 3 else [b]
     cuts = 8
     deep = width // cuts
     low = jnp.zeros((parts * each, d_ref.shape[1]), F32)
     for i in range(cuts):
         at = slice(i * deep, (i + 1) * deep)
-        piece = jnp.concatenate([b[:, at] for b in blocks], axis=0)
+        piece = jnp.concatenate([view[:, at] for view in views], axis=0)
         rows_ref[:, at] = piece
         low = low + dot(piece, d_ref[at, :])
     chosen = dot(pick_ref[...], low.astype(BF16)).astype(BF16)
@@ -325,20 +371,19 @@
         out_ref[p] = dot_nt(chosen, u_ref[p * cols : (p + 1) * cols, :]).astype(BF16)
 
 
-def deltas(blocks, pick, down, up):
-    parts = len(blocks)
-    each, width = blocks[0].shape
+def deltas(blocks, pick, down, up, parts):
+    each, width = blocks[0].shape[-2:]
     slots = pick.shape[0]
     rank_w = down.shape[1]
     vmem = pl.BlockSpec(memory_space=pltpu.VMEM)
-    at_slot = ORDER if parts == RING else [*range(parts)]
+    hand = HAND if len(blocks) > 1 else [0]
     return pl.pallas_call(
-        functools.partial(delta_kernel, at_slot),
+        functools.partial(delta_kernel, hand),
         out_shape=(
             jax.ShapeDtypeStruct((parts, slots, width // parts), BF16),
             jax.ShapeDtypeStruct((parts * each, width), BF16),
         ),
-        in_specs=[vmem] * (3 + parts),
+        in_specs=[vmem] * (3 + len(blocks)),
         out_specs=(vmem, vmem),
         compiler_params=pltpu.CompilerParams(vmem_limit_bytes=24 * 2**20),
         cost_estimate=pl.CostEstimate(
@@ -347,7 +392,7 @@
             transcendentals=0,
         ),
         name="delta",
-    )(*[blocks[i] for i in at_slot], pick, down, up)
+    )(*[blocks[i] for i in hand], pick, down, up)
 
 
 def base_kernel(a_ref, w_ref, order_ref, out_ref):
@@ -431,7 +476,7 @@
         parts,
     )
     blocks = gather(attended, parts)
-    send, gathered = deltas(blocks, pick, down, up)
+    send, gathered = deltas(blocks, pick, down, up, parts)
     delta = lax.all_to_all(send, "tensor", split_axis=0, concat_axis=0, tiled=True)
     base = base_part(gathered, out_weight, order)
     return join(base, place, delta, steps)

time: 47.7 us -> 48.8 us (1.023)
  waiting for transfers between devices: 14.1 us -> 17.1 us
  starting transfers between devices: 17.7 us -> 16.7 us
  Pallas kernels: 12.1 us -> 11.3 us
    ppermute x15 -> x12, waiting for transfers between devices: 9.91 us -> 12.9 us  [swap(): return lax.ppermute(x, 'tensor', [(i, i ^ bits) for i in range(parts)])]
    all_to_all x1, starting transfers between devices: 5.37 us -> 3.9 us  [per_device(): lax.all_to_all(send, 'tensor', split_axis=0, concat_axis=0, tiled=True)]
    pallas_call x1, Pallas kernels: 6.66 us -> 5.79 us  [attend(): pl.pallas_call(attend_kernel, out_shape=[jax.ShapeDtypeStruct(shape, BF16...]
    ppermute x0 -> x1, starting transfers between devices: none -> 0.58 us  [gather(): lax.ppermute(mixed, 'tensor', pairs)]
    ppermute x15 -> x12, starting transfers between devices: 12.4 us -> 12.2 us  [swap(): return lax.ppermute(x, 'tensor', [(i, i ^ bits) for i in range(parts)])]
    pallas_call x1 -> x2, Pallas kernels: 2.2 us -> 2.24 us  [the longest x1 2.21 us: deltas(): pl.pallas_call(functools.partial(delta_kernel, hand), out_shape=(jax.Shap...]
  transfers between devices with their start and end apart: 16 -> 14, of which waited for: 10 -> 7; matrix products, arithmetic and copies ran while one was open for 0% -> 0% of each run, Pallas kernels for 5% -> 5%
where the time goes in v12:
time: 48.8 us; the launch traced here: 48.5 us
  waiting for transfers between devices  17.1 us (35%)
  starting transfers between devices  16.7 us (34%)
  Pallas kernels  11.3 us (23%)
  local copies, waits for them, and re-layouts  3.38 us (7%)
    ppermute x12, waiting for transfers between devices, swap(): return lax.ppermute(x, 'tensor', [(i, i ^ bits) for i in range(parts)])  12.9 us
    ppermute x12, starting transfers between devices, swap(): return lax.ppermute(x, 'tensor', [(i, i ^ bits) for i in range(parts)])  12.2 us
    pallas_call x1, Pallas kernels, attend(): pl.pallas_call(attend_kernel, out_shape=[jax.ShapeDtypeStruct(shape, BF16...  5.79 us
    all_to_all x1, waiting for transfers between devices, per_device(): lax.all_to_all(send, 'tensor', split_axis=0, concat_axis=0, tiled=True)  4.26 us
    all_to_all x1, starting transfers between devices, per_device(): lax.all_to_all(send, 'tensor', split_axis=0, concat_axis=0, tiled=True)  3.9 us
    unnamed x2, local copies, waits for them, and re-layouts  3.38 us
    pallas_call x1, Pallas kernels, base_part(): pl.pallas_call(base_kernel, out_shape=jax.ShapeDtypeStruct((total, cols),...  2.39 us
    pallas_call x1, Pallas kernels, deltas(): pl.pallas_call(functools.partial(delta_kernel, hand), out_shape=(jax.Shap...  2.21 us
  transfers between devices with their start and end apart: 14, of which 7 were waited for; matrix products, arithmetic and copies ran while one was open for 0% of the time, Pallas kernels for 5%

profile of v12, /device:TPU:0, one launch (start us, length us, event | category | flops | bytes accessed | tf_op | source)
XLA Modules:
  0.0 48.5 jit_solution(15707381833364322382)
XLA Ops:
  0.0 5.8 %attend.1 = (bf16[8,8192]{1,0:T(8,128)(2,1)S(1)}, bf16[8192,128]{1,0:T(8,128)(2,1)S(1)}, bf16[8192,128]{1,0:T(8,128)(2,1)S(1)}, bf16[16,128]{1,0:T(8,128)(2,1)S(...) custom-call(s32[4]{0:T(128)} %len_hbm.1, bf16[2,4,8192]{2,1,0:T(4,128)(2,1)} %q_hbm.1, ...), custom_call_target="tpu_custom_call" | custom-call | flops 134217728 | bytes 8388608 | tf_op jit(solution)/shard_map/attend/pallas_call | solution.py:252
  5.8 3.1 %collective-permute-start.2 = (bf16[8,8192]{1,0:T(8,128)(2,1)S(1)}, bf16[8,8192]{1,0:T(8,128)(2,1)S(1)}, u32[]{:S(2)}, u32[]{:S(2)}) collective-permute-start(bf16[8,8192]{1,0:T(8,128)(2,1)S(1)} %get-tuple-element.19.own_ref), channel_id=1, source_target_pairs={{0,4},{1,5},{2,6},{3,7},{4,0},{5,1},{6,2},{7,3},{8,12},{9,13},{10,... | collective-permute-start | bytes 393224 | tf_op jit(solution)/shard_map/ppermute | solution.py:297
  8.9 1.5 %collective-permute-start.1 = (bf16[8,8192]{1,0:T(8,128)(2,1)S(1)}, bf16[8,8192]{1,0:T(8,128)(2,1)S(1)}, u32[]{:S(2)}, u32[]{:S(2)}) collective-permute-start(bf16[8,8192]{1,0:T(8,128)(2,1)S(1)} %get-tuple-element.19.own_ref), channel_id=1, source_target_pairs={{0,2},{1,3},{2,0},{3,1},{4,6},{5,7},{6,4},{7,5},{8,10},{9,11},{10,... | collective-permute-start | bytes 393224 | tf_op jit(solution)/shard_map/ppermute | solution.py:297
  10.4 2.6 %collective-permute-start = (bf16[8,8192]{1,0:T(8,128)(2,1)S(1)}, bf16[8,8192]{1,0:T(8,128)(2,1)S(1)}, u32[]{:S(2)}, u32[]{:S(2)}) collective-permute-start(bf16[8,8192]{1,0:T(8,128)(2,1)S(1)} %get-tuple-element.19.own_ref), channel_id=1, source_target_pairs={{0,8},{1,9},{2,10},{3,11},{4,12},{5,13},{6,14},{7,15},{8,0},{9,1},... | collective-permute-start | bytes 393224 | tf_op jit(solution)/shard_map/ppermute | solution.py:297
  13.0 0.0 collective-permute-done.2.near_ref
  13.0 0.9 %collective-permute-done.1.y_ref = bf16[8,8192]{1,0:T(8,128)(2,1)S(1)} collective-permute-done((bf16[8,8192]{1,0:T(8,128)(2,1)S(1)}, bf16[8,8192]{1,0:T(8,128)(2,1)S(1)}, u32[]{:S(2)}, u32[]{:S(2)}) %collective-permute-start.1) | collective-permute-done | bytes 131104 | tf_op jit(solution)/shard_map/ppermute | solution.py:297
  13.9 4.9 %collective-permute-done.refs_4_ = bf16[8,8192]{1,0:T(8,128)(2,1)S(1)} collective-permute-done((bf16[8,8192]{1,0:T(8,128)(2,1)S(1)}, bf16[8,8192]{1,0:T(8,128)(2,1)S(1)}, u32[]{:S(2)}, u32[]{:S(2)}) %collective-permute-start) | collective-permute-done | bytes 131104 | tf_op jit(solution)/shard_map/ppermute | solution.py:297
  18.8 0.0 collective-permute-start.4
  18.8 0.5 %collective-permute-start.3 = (bf16[3,8,8192]{2,1,0:T(8,128)(2,1)S(1)}, bf16[3,8,8192]{2,1,0:T(8,128)(2,1)S(1)}, u32[]{:S(2)}, u32[]{:S(2)}) collective-permute-start(bf16[3,8,8192]{2,1,0:T(8,128)(2,1)S(1)} %get-tuple-element.21.refs_0_), channel_id=1, source_target_pairs={{0,1},{1,0},{2,3},{3,2},{4,5},{5,4},{6,7},{7,6},{8,9},{9,8},{10,11... | collective-permute-start | bytes 1179656 | tf_op jit(solution)/shard_map/ppermute | solution.py:297
  19.3 0.6 %collective-permute-start.11 = (bf16[8,8192]{1,0:T(8,128)(2,1)S(1)}, bf16[8,8192]{1,0:T(8,128)(2,1)S(1)}, u32[]{:S(2)}, u32[]{:S(2)}) collective-permute-start(bf16[8,8192]{1,0:T(8,128)(2,1)S(1)} %collective-permute-done.refs_4_), channel_id=1, source_target_pairs={{0,2},{1,3},{2,0},{3,1},{4,6},{5,7},{6,4},{7,5},{8,10},{9,11},{10,... | collective-permute-start | bytes 393224 | tf_op jit(solution)/shard_map/ppermute | solution.py:297
  19.9 0.6 %collective-permute-start.9 = (bf16[8,8192]{1,0:T(8,128)(2,1)S(1)}, bf16[8,8192]{1,0:T(8,128)(2,1)S(1)}, u32[]{:S(2)}, u32[]{:S(2)}) collective-permute-start(bf16[8,8192]{1,0:T(8,128)(2,1)S(1)} %collective-permute-done.refs_4_), channel_id=1, source_target_pairs={{0,6},{1,7},{2,4},{3,5},{4,2},{5,3},{6,0},{7,1},{8,14},{9,15},{10,... | collective-permute-start | bytes 393224 | tf_op jit(solution)/shard_map/ppermute | solution.py:297
  20.5 2.3 %collective-permute-start.7 = (bf16[8,8192]{1,0:T(8,128)(2,1)S(1)}, bf16[8,8192]{1,0:T(8,128)(2,1)S(1)}, u32[]{:S(2)}, u32[]{:S(2)}) collective-permute-start(bf16[8,8192]{1,0:T(8,128)(2,1)S(1)} %collective-permute-done.refs_4_), channel_id=1, source_target_pairs={{0,4},{1,5},{2,6},{3,7},{4,0},{5,1},{6,2},{7,3},{8,12},{9,13},{10,... | collective-permute-start | bytes 393224 | tf_op jit(solution)/shard_map/ppermute | solution.py:297
  22.8 0.0 collective-permute-done.4.refs_5_
  22.8 0.6 %collective-permute-start.5 = (bf16[8,8192]{1,0:T(8,128)(2,1)S(1)}, bf16[8,8192]{1,0:T(8,128)(2,1)S(1)}, u32[]{:S(2)}, u32[]{:S(2)}) collective-permute-start(bf16[8,8192]{1,0:T(8,128)(2,1)S(1)} %get-tuple-element.24), channel_id=1, source_target_pairs={{0,2},{1,5},{2,0},{3,7},{4,6},{5,1},{6,4},{7,3},{8,10},{9,13},{10,... | collective-permute-start | bytes 393224 | tf_op jit(solution)/shard_map/ppermute | solution.py:347
  23.4 4.1 %collective-permute-done.11.refs_10_ = bf16[8,8192]{1,0:T(8,128)(2,1)S(1)} collective-permute-done((bf16[8,8192]{1,0:T(8,128)(2,1)S(1)}, bf16[8,8192]{1,0:T(8,128)(2,1)S(1)}, u32[]{:S(2)}, u32[]{:S(2)}) %collective-permute-start.11) | collective-permute-done | bytes 131104 | tf_op jit(solution)/shard_map/ppermute | solution.py:297
  27.5 0.0 collective-permute-start.12
  27.5 0.0 collective-permute-done.9.refs_8_
  27.5 0.5 %collective-permute-start.10 = (bf16[8,8192]{1,0:T(8,128)(2,1)S(1)}, bf16[8,8192]{1,0:T(8,128)(2,1)S(1)}, u32[]{:S(2)}, u32[]{:S(2)}) collective-permute-start(bf16[8,8192]{1,0:T(8,128)(2,1)S(1)} %collective-permute-done.9.refs_8_), channel_id=1, source_target_pairs={{0,1},{1,0},{2,3},{3,2},{4,5},{5,4},{6,7},{7,6},{8,9},{9,8},{10,11... | collective-permute-start | bytes 393224 | tf_op jit(solution)/shard_map/ppermute | solution.py:297
  28.0 1.9 %collective-permute-done.7.refs_6_ = bf16[8,8192]{1,0:T(8,128)(2,1)S(1)} collective-permute-done((bf16[8,8192]{1,0:T(8,128)(2,1)S(1)}, bf16[8,8192]{1,0:T(8,128)(2,1)S(1)}, u32[]{:S(2)}, u32[]{:S(2)}) %collective-permute-start.7) | collective-permute-done | bytes 131104 | tf_op jit(solution)/shard_map/ppermute | solution.py:297
  30.0 0.0 collective-permute-start.8
  30.0 0.0 collective-permute-done.5.refs_2_
  30.0 0.5 %collective-permute-start.6 = (bf16[8,8192]{1,0:T(8,128)(2,1)S(1)}, bf16[8,8192]{1,0:T(8,128)(2,1)S(1)}, u32[]{:S(2)}, u32[]{:S(2)}) collective-permute-start(bf16[8,8192]{1,0:T(8,128)(2,1)S(1)} %collective-permute-done.5.refs_2_), channel_id=1, source_target_pairs={{0,1},{1,0},{2,3},{3,2},{4,5},{5,4},{6,7},{7,6},{8,9},{9,8},{10,11... | collective-permute-start | bytes 393224 | tf_op jit(solution)/shard_map/ppermute | solution.py:297
  30.5 0.0 collective-permute-done.12.refs_11_
  30.5 0.8 %collective-permute-done.8.refs_7_ = bf16[8,8192]{1,0:T(8,128)(2,1)S(1)} collective-permute-done((bf16[8,8192]{1,0:T(8,128)(2,1)S(1)}, bf16[8,8192]{1,0:T(8,128)(2,1)S(1)}, u32[]{:S(2)}, u32[]{:S(2)}) %collective-permute-start.8) | collective-permute-done | bytes 131104 | tf_op jit(solution)/shard_map/ppermute | solution.py:297
  31.3 0.2 collective-permute-done.6.refs_3_
  31.5 2.2 %delta.1 = (bf16[16,16,512]{2,1,0:T(8,128)(2,1)}, bf16[128,8192]{1,0:T(8,128)(2,1)S(1)}) custom-call(bf16[3,8,8192]{2,1,0:T(8,128)(2,1)S(1)} %get-tuple-element.21.refs_0_, bf16[3,8,8192]{2,1,0:T(8,128)(2,1)S(1)} %collective-permute-done.3.refs_1_, bf16[8,8192]{1,0:T(8,128)(2,1)S(1)} %collective-permute-done.5.refs_2_, ...), custom_call_target="tpu_custom_call" | custom-call | flops 301989888 | bytes 8650752 | tf_op jit(solution)/shard_map/delta/pallas_call | solution.py:380
  33.7 3.9 %all-to-all-start = ((bf16[16,16,512]{2,1,0:T(8,128)(2,1)}), bf16[16,16,512]{2,1,0:T(8,128)(2,1)S(1)}, u32[]{:S(2)}, u32[]{:S(2)}) async-start(bf16[16,16,512]{2,1,0:T(8,128)(2,1)} %get-tuple-element.32), calls=%async_computation | async-start | bytes 524288 | tf_op jit(solution)/shard_map/all_to_all | solution.py:480
  37.6 0.0 copy-start
  37.6 3.4 %copy-done = bf16[8192,512]{1,0:T(8,128)(2,1)S(1)} copy-done((bf16[8192,512]{1,0:T(8,128)(2,1)S(1)}, bf16[8192,512]{1,0:T(8,128)(2,1)}, u32[]{:S(2)}) %copy-start) | copy-done | bytes 8388632
  41.0 2.4 %base.1.base_ref = f32[128,512]{1,0:T(8,128)S(1)} custom-call(bf16[128,8192]{1,0:T(8,128)(2,1)S(1)} %get-tuple-element.29.a_ref, bf16[8192,512]{1,0:T(8,128)(2,1)S(1)} %copy-done, bf16[128,128]{1,0:T(8,128)(2,1)S(1)} %get-tuple-element.30.order_ref), custom_call_target="tpu_custom_call" | custom-call | flops 1342177280 | bytes 10747904 | tf_op jit(solution)/shard_map/base/pallas_call | solution.py:412
  43.4 4.3 %all-to-all-done.delta_ref = bf16[16,16,512]{2,1,0:T(8,128)(2,1)S(1)} async-done(((bf16[16,16,512]{2,1,0:T(8,128)(2,1)}), bf16[16,16,512]{2,1,0:T(8,128)(2,1)S(1)}, u32[]{:S(2)}, u32[]{:S(2)}) %all-to-all-start) | async-done | bytes 262176 | tf_op jit(solution)/shard_map/all_to_all | solution.py:480
  47.7 0.8 %join.1 = bf16[2,64,512]{2,1,0:T(8,128)(2,1)} custom-call(f32[128,512]{1,0:T(8,128)S(1)} %base.1.base_ref, bf16[128,256]{1,0:T(8,128)(2,1)S(1)} %get-tuple-element.31.place_ref, bf16[16,16,512]{2,1,0:T(8,128)(2,1)S(1)} %all-to-all-done.delta_ref), custom_call_target="tpu_custom_call" | custom-call | tf_op jit(solution)/shard_map/join/pallas_call | solution.py:439
  (3 shorter events, 0.0 us)
Async XLA Ops:
  5.8 7.2 %collective-permute-start.2 = (bf16[8,8192]{1,0:T(8,128)(2,1)S(1)}, bf16[8,8192]{1,0:T(8,128)(2,1)S(1)}, u32[]{:S(2)}, u32[]{:S(2)}) collective-permute-start(bf16[8,8192]{1,0:T(8,128)(2,1)S(1)} %get-tuple-element.19.own_ref), channel_id=1, source_target_pairs={{0,4},{1,5},{2,6},{3,7},{4,0},{5,1},{6,2},{7,3},{8,12},{9,13},{10,... | collective-permute-start | bytes 393224 | tf_op jit(solution)/shard_map/ppermute | solution.py:297
  8.9 5.0 %collective-permute-start.1 = (bf16[8,8192]{1,0:T(8,128)(2,1)S(1)}, bf16[8,8192]{1,0:T(8,128)(2,1)S(1)}, u32[]{:S(2)}, u32[]{:S(2)}) collective-permute-start(bf16[8,8192]{1,0:T(8,128)(2,1)S(1)} %get-tuple-element.19.own_ref), channel_id=1, source_target_pairs={{0,2},{1,3},{2,0},{3,1},{4,6},{5,7},{6,4},{7,5},{8,10},{9,11},{10,... | collective-permute-start | bytes 393224 | tf_op jit(solution)/shard_map/ppermute | solution.py:297
  10.4 8.4 %collective-permute-start = (bf16[8,8192]{1,0:T(8,128)(2,1)S(1)}, bf16[8,8192]{1,0:T(8,128)(2,1)S(1)}, u32[]{:S(2)}, u32[]{:S(2)}) collective-permute-start(bf16[8,8192]{1,0:T(8,128)(2,1)S(1)} %get-tuple-element.19.own_ref), channel_id=1, source_target_pairs={{0,8},{1,9},{2,10},{3,11},{4,12},{5,13},{6,14},{7,15},{8,0},{9,1},... | collective-permute-start | bytes 393224 | tf_op jit(solution)/shard_map/ppermute | solution.py:297
  18.8 4.0 %collective-permute-start.4 = (bf16[8,8192]{1,0:T(8,128)(2,1)S(1)}, bf16[8,8192]{1,0:T(8,128)(2,1)S(1)}, u32[]{:S(2)}, u32[]{:S(2)}) collective-permute-start(bf16[8,8192]{1,0:T(8,128)(2,1)S(1)} %collective-permute-done.refs_4_), channel_id=1, source_target_pairs={{0,1},{1,0},{2,3},{3,2},{4,5},{5,4},{6,7},{7,6},{8,9},{9,8},{10,11... | collective-permute-start | bytes 393224 | tf_op jit(solution)/shard_map/ppermute | solution.py:297
  18.8 12.7 %collective-permute-start.3 = (bf16[3,8,8192]{2,1,0:T(8,128)(2,1)S(1)}, bf16[3,8,8192]{2,1,0:T(8,128)(2,1)S(1)}, u32[]{:S(2)}, u32[]{:S(2)}) collective-permute-start(bf16[3,8,8192]{2,1,0:T(8,128)(2,1)S(1)} %get-tuple-element.21.refs_0_), channel_id=1, source_target_pairs={{0,1},{1,0},{2,3},{3,2},{4,5},{5,4},{6,7},{7,6},{8,9},{9,8},{10,11... | collective-permute-start | bytes 1179656 | tf_op jit(solution)/shard_map/ppermute | solution.py:297
  19.3 8.2 %collective-permute-start.11 = (bf16[8,8192]{1,0:T(8,128)(2,1)S(1)}, bf16[8,8192]{1,0:T(8,128)(2,1)S(1)}, u32[]{:S(2)}, u32[]{:S(2)}) collective-permute-start(bf16[8,8192]{1,0:T(8,128)(2,1)S(1)} %collective-permute-done.refs_4_), channel_id=1, source_target_pairs={{0,2},{1,3},{2,0},{3,1},{4,6},{5,7},{6,4},{7,5},{8,10},{9,11},{10,... | collective-permute-start | bytes 393224 | tf_op jit(solution)/shard_map/ppermute | solution.py:297
  19.9 7.6 %collective-permute-start.9 = (bf16[8,8192]{1,0:T(8,128)(2,1)S(1)}, bf16[8,8192]{1,0:T(8,128)(2,1)S(1)}, u32[]{:S(2)}, u32[]{:S(2)}) collective-permute-start(bf16[8,8192]{1,0:T(8,128)(2,1)S(1)} %collective-permute-done.refs_4_), channel_id=1, source_target_pairs={{0,6},{1,7},{2,4},{3,5},{4,2},{5,3},{6,0},{7,1},{8,14},{9,15},{10,... | collective-permute-start | bytes 393224 | tf_op jit(solution)/shard_map/ppermute | solution.py:297
  20.5 9.5 %collective-permute-start.7 = (bf16[8,8192]{1,0:T(8,128)(2,1)S(1)}, bf16[8,8192]{1,0:T(8,128)(2,1)S(1)}, u32[]{:S(2)}, u32[]{:S(2)}) collective-permute-start(bf16[8,8192]{1,0:T(8,128)(2,1)S(1)} %collective-permute-done.refs_4_), channel_id=1, source_target_pairs={{0,4},{1,5},{2,6},{3,7},{4,0},{5,1},{6,2},{7,3},{8,12},{9,13},{10,... | collective-permute-start | bytes 393224 | tf_op jit(solution)/shard_map/ppermute | solution.py:297
  22.8 7.2 %collective-permute-start.5 = (bf16[8,8192]{1,0:T(8,128)(2,1)S(1)}, bf16[8,8192]{1,0:T(8,128)(2,1)S(1)}, u32[]{:S(2)}, u32[]{:S(2)}) collective-permute-start(bf16[8,8192]{1,0:T(8,128)(2,1)S(1)} %get-tuple-element.24), channel_id=1, source_target_pairs={{0,2},{1,5},{2,0},{3,7},{4,6},{5,1},{6,4},{7,3},{8,10},{9,13},{10,... | collective-permute-start | bytes 393224 | tf_op jit(solution)/shard_map/ppermute | solution.py:347
  27.5 3.0 %collective-permute-start.12 = (bf16[8,8192]{1,0:T(8,128)(2,1)S(1)}, bf16[8,8192]{1,0:T(8,128)(2,1)S(1)}, u32[]{:S(2)}, u32[]{:S(2)}) collective-permute-start(bf16[8,8192]{1,0:T(8,128)(2,1)S(1)} %collective-permute-done.11.refs_10_), channel_id=1, source_target_pairs={{0,1},{1,0},{2,3},{3,2},{4,5},{5,4},{6,7},{7,6},{8,9},{9,8},{10,11... | collective-permute-start | bytes 393224 | tf_op jit(solution)/shard_map/ppermute | solution.py:297
  27.5 3.0 %collective-permute-start.10 = (bf16[8,8192]{1,0:T(8,128)(2,1)S(1)}, bf16[8,8192]{1,0:T(8,128)(2,1)S(1)}, u32[]{:S(2)}, u32[]{:S(2)}) collective-permute-start(bf16[8,8192]{1,0:T(8,128)(2,1)S(1)} %collective-permute-done.9.refs_8_), channel_id=1, source_target_pairs={{0,1},{1,0},{2,3},{3,2},{4,5},{5,4},{6,7},{7,6},{8,9},{9,8},{10,11... | collective-permute-start | bytes 393224 | tf_op jit(solution)/shard_map/ppermute | solution.py:297
  30.0 1.3 %collective-permute-start.8 = (bf16[8,8192]{1,0:T(8,128)(2,1)S(1)}, bf16[8,8192]{1,0:T(8,128)(2,1)S(1)}, u32[]{:S(2)}, u32[]{:S(2)}) collective-permute-start(bf16[8,8192]{1,0:T(8,128)(2,1)S(1)} %collective-permute-done.7.refs_6_), channel_id=1, source_target_pairs={{0,1},{1,0},{2,3},{3,2},{4,5},{5,4},{6,7},{7,6},{8,9},{9,8},{10,11... | collective-permute-start | bytes 393224 | tf_op jit(solution)/shard_map/ppermute | solution.py:297
  30.0 1.5 %collective-permute-start.6 = (bf16[8,8192]{1,0:T(8,128)(2,1)S(1)}, bf16[8,8192]{1,0:T(8,128)(2,1)S(1)}, u32[]{:S(2)}, u32[]{:S(2)}) collective-permute-start(bf16[8,8192]{1,0:T(8,128)(2,1)S(1)} %collective-permute-done.5.refs_2_), channel_id=1, source_target_pairs={{0,1},{1,0},{2,3},{3,2},{4,5},{5,4},{6,7},{7,6},{8,9},{9,8},{10,11... | collective-permute-start | bytes 393224 | tf_op jit(solution)/shard_map/ppermute | solution.py:297
  33.7 14.0 %all-to-all-start = ((bf16[16,16,512]{2,1,0:T(8,128)(2,1)}), bf16[16,16,512]{2,1,0:T(8,128)(2,1)S(1)}, u32[]{:S(2)}, u32[]{:S(2)}) async-start(bf16[16,16,512]{2,1,0:T(8,128)(2,1)} %get-tuple-element.32), calls=%async_computation | async-start | bytes 524288 | tf_op jit(solution)/shard_map/all_to_all | solution.py:480
  37.6 3.4 %copy-start = (bf16[8192,512]{1,0:T(8,128)(2,1)S(1)}, bf16[8192,512]{1,0:T(8,128)(2,1)}, u32[]{:S(2)}) copy-start(bf16[8192,512]{1,0:T(8,128)(2,1)} %w_ref.1) | copy-start | bytes 25165828

commit v13 on v11

--- a/solution.py
+++ b/solution.py
@@ -14,7 +14,7 @@
 GROUP = HQ // KVH
 MOST = 8
 RING = 16
-ORDER = [0, 1, 6, 7, 4, 5, 2, 3, 8, 9, 12, 13, 14, 15, 10, 11]
+ORDER = [0, 1, 2, 3, 4, 5, 6, 7, 8, 9, 10, 11, 12, 13, 14, 15]
 F32 = jnp.float32
 BF16 = jnp.bfloat16
 NT = (((1,), (1,)), ((), ()))
@@ -133,13 +133,13 @@
     for r in range(rows):
         queue += [values[r + 1]] if r + 1 < rows else [store]
         queue += [keys[r + 2]] if r + 2 < rows else []
-    for copy in small + queue[0]:
+    for copy in small + queue[0] + queue[1] + queue[2]:
         copy.start()
     for copy in small:
         copy.wait()
-    for copy in queue[1] + queue[2]:
+    for copy in queue[3] + queue[4]:
         copy.start()
-    queue = queue[3:]
+    queue = queue[5:]
 
     flat = jnp.concatenate([q_ref[t].astype(F32) for t in range(steps)], axis=0)
     heads = []

time: 47.7 us -> 46.5 us (0.975)
  Pallas kernels: 12.1 us -> 11.2 us
    pallas_call x1, Pallas kernels: 6.66 us -> 5.78 us  [attend(): pl.pallas_call(attend_kernel, out_shape=[jax.ShapeDtypeStruct(shape, BF16...]
  transfers between devices with their start and end apart: 16 -> 16, of which waited for: 10 -> 11; matrix products, arithmetic and copies ran while one was open for 0% -> 0% of each run, Pallas kernels for 5% -> 5%
where the time goes in v13:
time: 46.5 us; the launch traced here: 46.2 us
  starting transfers between devices  17.6 us (38%)
  waiting for transfers between devices  14 us (30%)
  Pallas kernels  11.2 us (24%)
  local copies, waits for them, and re-layouts  3.38 us (7%)
    ppermute x15, starting transfers between devices, swap(): return lax.ppermute(x, 'tensor', [(i, i ^ bits) for i in range(parts)])  12.5 us
    ppermute x15, waiting for transfers between devices, swap(): return lax.ppermute(x, 'tensor', [(i, i ^ bits) for i in range(parts)])  9.76 us
    pallas_call x1, Pallas kernels, attend(): pl.pallas_call(attend_kernel, out_shape=[jax.ShapeDtypeStruct(shape, BF16...  5.78 us
    all_to_all x1, starting transfers between devices, per_device(): lax.all_to_all(send, 'tensor', split_axis=0, concat_axis=0, tiled=True)  5.01 us
    all_to_all x1, waiting for transfers between devices, per_device(): lax.all_to_all(send, 'tensor', split_axis=0, concat_axis=0, tiled=True)  4.26 us
    unnamed x2, local copies, waits for them, and re-layouts  3.38 us
    pallas_call x1, Pallas kernels, base_part(): pl.pallas_call(base_kernel, out_shape=jax.ShapeDtypeStruct((total, cols),...  2.4 us
    pallas_call x1, Pallas kernels, deltas(): pl.pallas_call(functools.partial(delta_kernel, at_slot), out_shape=(jax.S...  2.2 us
  transfers between devices with their start and end apart: 16, of which 11 were waited for; matrix products, arithmetic and copies ran while one was open for 0% of the time, Pallas kernels for 5%

profile of v13, /device:TPU:0, one launch (start us, length us, event | category | flops | bytes accessed | tf_op | source)
XLA Modules:
  0.0 46.2 jit_solution(7050634629200952530)
XLA Ops:
  0.0 5.8 %attend.1 = (bf16[8,8192]{1,0:T(8,128)(2,1)S(1)}, bf16[8192,128]{1,0:T(8,128)(2,1)S(1)}, bf16[8192,128]{1,0:T(8,128)(2,1)S(1)}, bf16[16,128]{1,0:T(8,128)(2,1)S(...) custom-call(s32[4]{0:T(128)} %len_hbm.1, bf16[2,4,8192]{2,1,0:T(4,128)(2,1)} %q_hbm.1, ...), custom_call_target="tpu_custom_call" | custom-call | flops 134217728 | bytes 8388608 | tf_op jit(solution)/shard_map/attend/pallas_call | solution.py:244
  5.8 4.1 %collective-permute-start.7 = (bf16[8,8192]{1,0:T(8,128)(2,1)S(1)}, bf16[8,8192]{1,0:T(8,128)(2,1)S(1)}, u32[]{:S(2)}, u32[]{:S(2)}) collective-permute-start(bf16[8,8192]{1,0:T(8,128)(2,1)S(1)} %get-tuple-element.13.refs_0_), channel_id=1, source_target_pairs={{0,8},{1,9},{2,10},{3,11},{4,12},{5,13},{6,14},{7,15},{8,0},{9,1},... | collective-permute-start | bytes 393224 | tf_op jit(solution)/shard_map/ppermute | solution.py:289
  9.9 2.5 %collective-permute-start.5 = (bf16[8,8192]{1,0:T(8,128)(2,1)S(1)}, bf16[8,8192]{1,0:T(8,128)(2,1)S(1)}, u32[]{:S(2)}, u32[]{:S(2)}) collective-permute-start(bf16[8,8192]{1,0:T(8,128)(2,1)S(1)} %get-tuple-element.13.refs_0_), channel_id=1, source_target_pairs={{0,6},{1,7},{2,4},{3,5},{4,2},{5,3},{6,0},{7,1},{8,14},{9,15},{10,... | collective-permute-start | bytes 393224 | tf_op jit(solution)/shard_map/ppermute | solution.py:289
  12.4 0.5 collective-permute-start.3
  12.9 0.5 %collective-permute-start.1 = (bf16[8,8192]{1,0:T(8,128)(2,1)S(1)}, bf16[8,8192]{1,0:T(8,128)(2,1)S(1)}, u32[]{:S(2)}, u32[]{:S(2)}) collective-permute-start(bf16[8,8192]{1,0:T(8,128)(2,1)S(1)} %get-tuple-element.13.refs_0_), channel_id=1, source_target_pairs={{0,2},{1,3},{2,0},{3,1},{4,6},{5,7},{6,4},{7,5},{8,10},{9,11},{10,... | collective-permute-start | bytes 393224 | tf_op jit(solution)/shard_map/ppermute | solution.py:289
  13.4 2.9 %collective-permute-done.7.refs_8_ = bf16[8,8192]{1,0:T(8,128)(2,1)S(1)} collective-permute-done((bf16[8,8192]{1,0:T(8,128)(2,1)S(1)}, bf16[8,8192]{1,0:T(8,128)(2,1)S(1)}, u32[]{:S(2)}, u32[]{:S(2)}) %collective-permute-start.7) | collective-permute-done | bytes 131104 | tf_op jit(solution)/shard_map/ppermute | solution.py:289
  16.3 1.6 %collective-permute-start.13 = (bf16[8,8192]{1,0:T(8,128)(2,1)S(1)}, bf16[8,8192]{1,0:T(8,128)(2,1)S(1)}, u32[]{:S(2)}, u32[]{:S(2)}) collective-permute-start(bf16[8,8192]{1,0:T(8,128)(2,1)S(1)} %collective-permute-done.7.refs_8_), channel_id=1, source_target_pairs={{0,6},{1,7},{2,4},{3,5},{4,2},{5,3},{6,0},{7,1},{8,14},{9,15},{10,... | collective-permute-start | bytes 393224 | tf_op jit(solution)/shard_map/ppermute | solution.py:289
  17.9 0.9 %collective-permute-done.5.refs_6_ = bf16[8,8192]{1,0:T(8,128)(2,1)S(1)} collective-permute-done((bf16[8,8192]{1,0:T(8,128)(2,1)S(1)}, bf16[8,8192]{1,0:T(8,128)(2,1)S(1)}, u32[]{:S(2)}, u32[]{:S(2)}) %collective-permute-start.5) | collective-permute-done | bytes 131104 | tf_op jit(solution)/shard_map/ppermute | solution.py:289
  18.8 1.2 %collective-permute-start.11 = (bf16[8,8192]{1,0:T(8,128)(2,1)S(1)}, bf16[8,8192]{1,0:T(8,128)(2,1)S(1)}, u32[]{:S(2)}, u32[]{:S(2)}) collective-permute-start(bf16[8,8192]{1,0:T(8,128)(2,1)S(1)} %collective-permute-done.7.refs_8_), channel_id=1, source_target_pairs={{0,4},{1,5},{2,6},{3,7},{4,0},{5,1},{6,2},{7,3},{8,12},{9,13},{10,... | collective-permute-start | bytes 393224 | tf_op jit(solution)/shard_map/ppermute | solution.py:289
  20.1 1.2 %collective-permute-done.3.refs_4_ = bf16[8,8192]{1,0:T(8,128)(2,1)S(1)} collective-permute-done((bf16[8,8192]{1,0:T(8,128)(2,1)S(1)}, bf16[8,8192]{1,0:T(8,128)(2,1)S(1)}, u32[]{:S(2)}, u32[]{:S(2)}) %collective-permute-start.3) | collective-permute-done | bytes 131104 | tf_op jit(solution)/shard_map/ppermute | solution.py:289
  21.3 0.9 %collective-permute-start.9 = (bf16[8,8192]{1,0:T(8,128)(2,1)S(1)}, bf16[8,8192]{1,0:T(8,128)(2,1)S(1)}, u32[]{:S(2)}, u32[]{:S(2)}) collective-permute-start(bf16[8,8192]{1,0:T(8,128)(2,1)S(1)} %collective-permute-done.7.refs_8_), channel_id=1, source_target_pairs={{0,2},{1,3},{2,0},{3,1},{4,6},{5,7},{6,4},{7,5},{8,10},{9,11},{10,... | collective-permute-start | bytes 393224 | tf_op jit(solution)/shard_map/ppermute | solution.py:289
  22.2 0.5 %collective-permute-start.6 = (bf16[8,8192]{1,0:T(8,128)(2,1)S(1)}, bf16[8,8192]{1,0:T(8,128)(2,1)S(1)}, u32[]{:S(2)}, u32[]{:S(2)}) collective-permute-start(bf16[8,8192]{1,0:T(8,128)(2,1)S(1)} %collective-permute-done.5.refs_6_), channel_id=1, source_target_pairs={{0,1},{1,0},{2,3},{3,2},{4,5},{5,4},{6,7},{7,6},{8,9},{9,8},{10,11... | collective-permute-start | bytes 393224 | tf_op jit(solution)/shard_map/ppermute | solution.py:289
  22.7 1.7 %collective-permute-done.13.refs_14_ = bf16[8,8192]{1,0:T(8,128)(2,1)S(1)} collective-permute-done((bf16[8,8192]{1,0:T(8,128)(2,1)S(1)}, bf16[8,8192]{1,0:T(8,128)(2,1)S(1)}, u32[]{:S(2)}, u32[]{:S(2)}) %collective-permute-start.13) | collective-permute-done | bytes 131104 | tf_op jit(solution)/shard_map/ppermute | solution.py:289
  24.5 1.4 %collective-permute-done.11.refs_12_ = bf16[8,8192]{1,0:T(8,128)(2,1)S(1)} collective-permute-done((bf16[8,8192]{1,0:T(8,128)(2,1)S(1)}, bf16[8,8192]{1,0:T(8,128)(2,1)S(1)}, u32[]{:S(2)}, u32[]{:S(2)}) %collective-permute-start.11) | collective-permute-done | bytes 131104 | tf_op jit(solution)/shard_map/ppermute | solution.py:289
  25.9 0.0 collective-permute-start.2
  25.9 0.4 collective-permute-done.9.refs_10_
  26.2 0.2 collective-permute-start.14
  26.4 0.0 collective-permute-done.8.refs_9_
  26.4 0.4 collective-permute-start.12
  26.8 0.0 collective-permute-done.6.refs_7_
  26.8 0.2 collective-permute-start.10
  26.9 0.3 collective-permute-done.2.refs_3_
  27.2 0.4 collective-permute-done.14.refs_15_
  27.6 0.2 collective-permute-done.12.refs_13_
  27.8 0.3 collective-permute-done.10.refs_11_
  28.1 2.2 %delta.1 = (bf16[16,16,512]{2,1,0:T(8,128)(2,1)}, bf16[128,8192]{1,0:T(8,128)(2,1)S(1)}) custom-call(bf16[8,8192]{1,0:T(8,128)(2,1)S(1)} %get-tuple-element.13.refs_0_, bf16[8,8192]{1,0:T(8,128)(2,1)S(1)} %collective-permute-done.refs_1_, bf16[8,8192]{1,0:T(8,128)(2,1)S(1)} %collective-permute-done.1.refs_2_, ...), custom_call_target="tpu_custom_call" | custom-call | flops 301989888 | bytes 8650752 | tf_op jit(solution)/shard_map/delta/pallas_call | solution.py:335
  30.3 5.0 %all-to-all-start = ((bf16[16,16,512]{2,1,0:T(8,128)(2,1)}), bf16[16,16,512]{2,1,0:T(8,128)(2,1)S(1)}, u32[]{:S(2)}, u32[]{:S(2)}) async-start(bf16[16,16,512]{2,1,0:T(8,128)(2,1)} %get-tuple-element.20), calls=%async_computation | async-start | bytes 524288 | tf_op jit(solution)/shard_map/all_to_all | solution.py:435
  35.3 0.0 copy-start
  35.3 3.4 %copy-done = bf16[8192,512]{1,0:T(8,128)(2,1)S(1)} copy-done((bf16[8192,512]{1,0:T(8,128)(2,1)S(1)}, bf16[8192,512]{1,0:T(8,128)(2,1)}, u32[]{:S(2)}) %copy-start) | copy-done | bytes 8388632
  38.7 2.4 %base.1.base_ref = f32[128,512]{1,0:T(8,128)S(1)} custom-call(bf16[128,8192]{1,0:T(8,128)(2,1)S(1)} %get-tuple-element.17.a_ref, bf16[8192,512]{1,0:T(8,128)(2,1)S(1)} %copy-done, bf16[128,128]{1,0:T(8,128)(2,1)S(1)} %get-tuple-element.18.order_ref), custom_call_target="tpu_custom_call" | custom-call | flops 1342177280 | bytes 10747904 | tf_op jit(solution)/shard_map/base/pallas_call | solution.py:367
  41.1 4.3 %all-to-all-done.delta_ref = bf16[16,16,512]{2,1,0:T(8,128)(2,1)S(1)} async-done(((bf16[16,16,512]{2,1,0:T(8,128)(2,1)}), bf16[16,16,512]{2,1,0:T(8,128)(2,1)S(1)}, u32[]{:S(2)}, u32[]{:S(2)}) %all-to-all-start) | async-done | bytes 262176 | tf_op jit(solution)/shard_map/all_to_all | solution.py:435
  45.4 0.8 %join.1 = bf16[2,64,512]{2,1,0:T(8,128)(2,1)} custom-call(f32[128,512]{1,0:T(8,128)S(1)} %base.1.base_ref, bf16[128,256]{1,0:T(8,128)(2,1)S(1)} %get-tuple-element.19.place_ref, bf16[16,16,512]{2,1,0:T(8,128)(2,1)S(1)} %all-to-all-done.delta_ref), custom_call_target="tpu_custom_call" | custom-call | tf_op jit(solution)/shard_map/join/pallas_call | solution.py:394
  (6 shorter events, 0.0 us)
Async XLA Ops:
  5.8 10.5 %collective-permute-start.7 = (bf16[8,8192]{1,0:T(8,128)(2,1)S(1)}, bf16[8,8192]{1,0:T(8,128)(2,1)S(1)}, u32[]{:S(2)}, u32[]{:S(2)}) collective-permute-start(bf16[8,8192]{1,0:T(8,128)(2,1)S(1)} %get-tuple-element.13.refs_0_), channel_id=1, source_target_pairs={{0,8},{1,9},{2,10},{3,11},{4,12},{5,13},{6,14},{7,15},{8,0},{9,1},... | collective-permute-start | bytes 393224 | tf_op jit(solution)/shard_map/ppermute | solution.py:289
  9.9 9.0 %collective-permute-start.5 = (bf16[8,8192]{1,0:T(8,128)(2,1)S(1)}, bf16[8,8192]{1,0:T(8,128)(2,1)S(1)}, u32[]{:S(2)}, u32[]{:S(2)}) collective-permute-start(bf16[8,8192]{1,0:T(8,128)(2,1)S(1)} %get-tuple-element.13.refs_0_), channel_id=1, source_target_pairs={{0,6},{1,7},{2,4},{3,5},{4,2},{5,3},{6,0},{7,1},{8,14},{9,15},{10,... | collective-permute-start | bytes 393224 | tf_op jit(solution)/shard_map/ppermute | solution.py:289
  12.4 8.8 %collective-permute-start.3 = (bf16[8,8192]{1,0:T(8,128)(2,1)S(1)}, bf16[8,8192]{1,0:T(8,128)(2,1)S(1)}, u32[]{:S(2)}, u32[]{:S(2)}) collective-permute-start(bf16[8,8192]{1,0:T(8,128)(2,1)S(1)} %get-tuple-element.13.refs_0_), channel_id=1, source_target_pairs={{0,4},{1,5},{2,6},{3,7},{4,0},{5,1},{6,2},{7,3},{8,12},{9,13},{10,... | collective-permute-start | bytes 393224 | tf_op jit(solution)/shard_map/ppermute | solution.py:289
  12.9 9.3 %collective-permute-start.1 = (bf16[8,8192]{1,0:T(8,128)(2,1)S(1)}, bf16[8,8192]{1,0:T(8,128)(2,1)S(1)}, u32[]{:S(2)}, u32[]{:S(2)}) collective-permute-start(bf16[8,8192]{1,0:T(8,128)(2,1)S(1)} %get-tuple-element.13.refs_0_), channel_id=1, source_target_pairs={{0,2},{1,3},{2,0},{3,1},{4,6},{5,7},{6,4},{7,5},{8,10},{9,11},{10,... | collective-permute-start | bytes 393224 | tf_op jit(solution)/shard_map/ppermute | solution.py:289
  13.4 8.8 %collective-permute-start = (bf16[8,8192]{1,0:T(8,128)(2,1)S(1)}, bf16[8,8192]{1,0:T(8,128)(2,1)S(1)}, u32[]{:S(2)}, u32[]{:S(2)}) collective-permute-start(bf16[8,8192]{1,0:T(8,128)(2,1)S(1)} %get-tuple-element.13.refs_0_), channel_id=1, source_target_pairs={{0,1},{1,0},{2,3},{3,2},{4,5},{5,4},{6,7},{7,6},{8,9},{9,8},{10,11... | collective-permute-start | bytes 393224 | tf_op jit(solution)/shard_map/ppermute | solution.py:289
  16.3 8.2 %collective-permute-start.13 = (bf16[8,8192]{1,0:T(8,128)(2,1)S(1)}, bf16[8,8192]{1,0:T(8,128)(2,1)S(1)}, u32[]{:S(2)}, u32[]{:S(2)}) collective-permute-start(bf16[8,8192]{1,0:T(8,128)(2,1)S(1)} %collective-permute-done.7.refs_8_), channel_id=1, source_target_pairs={{0,6},{1,7},{2,4},{3,5},{4,2},{5,3},{6,0},{7,1},{8,14},{9,15},{10,... | collective-permute-start | bytes 393224 | tf_op jit(solution)/shard_map/ppermute | solution.py:289
  18.8 7.0 %collective-permute-start.11 = (bf16[8,8192]{1,0:T(8,128)(2,1)S(1)}, bf16[8,8192]{1,0:T(8,128)(2,1)S(1)}, u32[]{:S(2)}, u32[]{:S(2)}) collective-permute-start(bf16[8,8192]{1,0:T(8,128)(2,1)S(1)} %collective-permute-done.7.refs_8_), channel_id=1, source_target_pairs={{0,4},{1,5},{2,6},{3,7},{4,0},{5,1},{6,2},{7,3},{8,12},{9,13},{10,... | collective-permute-start | bytes 393224 | tf_op jit(solution)/shard_map/ppermute | solution.py:289
  21.3 5.0 %collective-permute-start.9 = (bf16[8,8192]{1,0:T(8,128)(2,1)S(1)}, bf16[8,8192]{1,0:T(8,128)(2,1)S(1)}, u32[]{:S(2)}, u32[]{:S(2)}) collective-permute-start(bf16[8,8192]{1,0:T(8,128)(2,1)S(1)} %collective-permute-done.7.refs_8_), channel_id=1, source_target_pairs={{0,2},{1,3},{2,0},{3,1},{4,6},{5,7},{6,4},{7,5},{8,10},{9,11},{10,... | collective-permute-start | bytes 393224 | tf_op jit(solution)/shard_map/ppermute | solution.py:289
  22.2 4.2 %collective-permute-start.8 = (bf16[8,8192]{1,0:T(8,128)(2,1)S(1)}, bf16[8,8192]{1,0:T(8,128)(2,1)S(1)}, u32[]{:S(2)}, u32[]{:S(2)}) collective-permute-start(bf16[8,8192]{1,0:T(8,128)(2,1)S(1)} %collective-permute-done.7.refs_8_), channel_id=1, source_target_pairs={{0,1},{1,0},{2,3},{3,2},{4,5},{5,4},{6,7},{7,6},{8,9},{9,8},{10,11... | collective-permute-start | bytes 393224 | tf_op jit(solution)/shard_map/ppermute | solution.py:289
  22.2 4.5 %collective-permute-start.6 = (bf16[8,8192]{1,0:T(8,128)(2,1)S(1)}, bf16[8,8192]{1,0:T(8,128)(2,1)S(1)}, u32[]{:S(2)}, u32[]{:S(2)}) collective-permute-start(bf16[8,8192]{1,0:T(8,128)(2,1)S(1)} %collective-permute-done.5.refs_6_), channel_id=1, source_target_pairs={{0,1},{1,0},{2,3},{3,2},{4,5},{5,4},{6,7},{7,6},{8,9},{9,8},{10,11... | collective-permute-start | bytes 393224 | tf_op jit(solution)/shard_map/ppermute | solution.py:289
  24.5 2.5 %collective-permute-start.4 = (bf16[8,8192]{1,0:T(8,128)(2,1)S(1)}, bf16[8,8192]{1,0:T(8,128)(2,1)S(1)}, u32[]{:S(2)}, u32[]{:S(2)}) collective-permute-start(bf16[8,8192]{1,0:T(8,128)(2,1)S(1)} %collective-permute-done.3.refs_4_), channel_id=1, source_target_pairs={{0,1},{1,0},{2,3},{3,2},{4,5},{5,4},{6,7},{7,6},{8,9},{9,8},{10,11... | collective-permute-start | bytes 393224 | tf_op jit(solution)/shard_map/ppermute | solution.py:289
  25.9 1.3 %collective-permute-start.2 = (bf16[8,8192]{1,0:T(8,128)(2,1)S(1)}, bf16[8,8192]{1,0:T(8,128)(2,1)S(1)}, u32[]{:S(2)}, u32[]{:S(2)}) collective-permute-start(bf16[8,8192]{1,0:T(8,128)(2,1)S(1)} %collective-permute-done.1.refs_2_), channel_id=1, source_target_pairs={{0,1},{1,0},{2,3},{3,2},{4,5},{5,4},{6,7},{7,6},{8,9},{9,8},{10,11... | collective-permute-start | bytes 393224 | tf_op jit(solution)/shard_map/ppermute | solution.py:289
  26.2 1.3 %collective-permute-start.14 = (bf16[8,8192]{1,0:T(8,128)(2,1)S(1)}, bf16[8,8192]{1,0:T(8,128)(2,1)S(1)}, u32[]{:S(2)}, u32[]{:S(2)}) collective-permute-start(bf16[8,8192]{1,0:T(8,128)(2,1)S(1)} %collective-permute-done.13.refs_14_), channel_id=1, source_target_pairs={{0,1},{1,0},{2,3},{3,2},{4,5},{5,4},{6,7},{7,6},{8,9},{9,8},{10,11... | collective-permute-start | bytes 393224 | tf_op jit(solution)/shard_map/ppermute | solution.py:289
  26.4 1.4 %collective-permute-start.12 = (bf16[8,8192]{1,0:T(8,128)(2,1)S(1)}, bf16[8,8192]{1,0:T(8,128)(2,1)S(1)}, u32[]{:S(2)}, u32[]{:S(2)}) collective-permute-start(bf16[8,8192]{1,0:T(8,128)(2,1)S(1)} %collective-permute-done.11.refs_12_), channel_id=1, source_target_pairs={{0,1},{1,0},{2,3},{3,2},{4,5},{5,4},{6,7},{7,6},{8,9},{9,8},{10,11... | collective-permute-start | bytes 393224 | tf_op jit(solution)/shard_map/ppermute | solution.py:289
  26.8 1.3 %collective-permute-start.10 = (bf16[8,8192]{1,0:T(8,128)(2,1)S(1)}, bf16[8,8192]{1,0:T(8,128)(2,1)S(1)}, u32[]{:S(2)}, u32[]{:S(2)}) collective-permute-start(bf16[8,8192]{1,0:T(8,128)(2,1)S(1)} %collective-permute-done.9.refs_10_), channel_id=1, source_target_pairs={{0,1},{1,0},{2,3},{3,2},{4,5},{5,4},{6,7},{7,6},{8,9},{9,8},{10,11... | collective-permute-start | bytes 393224 | tf_op jit(solution)/shard_map/ppermute | solution.py:289
  30.3 15.1 %all-to-all-start = ((bf16[16,16,512]{2,1,0:T(8,128)(2,1)}), bf16[16,16,512]{2,1,0:T(8,128)(2,1)S(1)}, u32[]{:S(2)}, u32[]{:S(2)}) async-start(bf16[16,16,512]{2,1,0:T(8,128)(2,1)} %get-tuple-element.20), calls=%async_computation | async-start | bytes 524288 | tf_op jit(solution)/shard_map/all_to_all | solution.py:435
  35.3 3.4 %copy-start = (bf16[8192,512]{1,0:T(8,128)(2,1)S(1)}, bf16[8192,512]{1,0:T(8,128)(2,1)}, u32[]{:S(2)}) copy-start(bf16[8192,512]{1,0:T(8,128)(2,1)} %w_ref.1) | copy-start | bytes 25165828

commit v14 on v13

--- a/solution.py
+++ b/solution.py
@@ -335,7 +335,7 @@
     return pl.pallas_call(
         functools.partial(delta_kernel, at_slot),
         out_shape=(
-            jax.ShapeDtypeStruct((parts, slots, width // parts), BF16),
+            pltpu.VMEM((parts, slots, width // parts), BF16),
             jax.ShapeDtypeStruct((parts * each, width), BF16),
         ),
         in_specs=[vmem] * (3 + parts),

time: 46.5 us -> 46.5 us (level)
  no operation moved by 1% of the time
where the time goes in v14:
time: 46.5 us; the launch traced here: 46.2 us
  starting transfers between devices  17.6 us (38%)
  waiting for transfers between devices  14 us (30%)
  Pallas kernels  11.2 us (24%)
  local copies, waits for them, and re-layouts  3.38 us (7%)
    ppermute x15, starting transfers between devices, swap(): return lax.ppermute(x, 'tensor', [(i, i ^ bits) for i in range(parts)])  12.5 us
    ppermute x15, waiting for transfers between devices, swap(): return lax.ppermute(x, 'tensor', [(i, i ^ bits) for i in range(parts)])  9.76 us
    pallas_call x1, Pallas kernels, attend(): pl.pallas_call(attend_kernel, out_shape=[jax.ShapeDtypeStruct(shape, BF16...  5.78 us
    all_to_all x1, starting transfers between devices, per_device(): lax.all_to_all(send, 'tensor', split_axis=0, concat_axis=0, tiled=True)  5.01 us
    all_to_all x1, waiting for transfers between devices, per_device(): lax.all_to_all(send, 'tensor', split_axis=0, concat_axis=0, tiled=True)  4.26 us
    unnamed x2, local copies, waits for them, and re-layouts  3.38 us
    pallas_call x1, Pallas kernels, base_part(): pl.pallas_call(base_kernel, out_shape=jax.ShapeDtypeStruct((total, cols),...  2.4 us
    pallas_call x1, Pallas kernels, deltas(): pl.pallas_call(functools.partial(delta_kernel, at_slot), out_shape=(pltpu...  2.2 us
  transfers between devices with their start and end apart: 16, of which 11 were waited for; matrix products, arithmetic and copies ran while one was open for 0% of the time, Pallas kernels for 5%

profile of v14, /device:TPU:0, one launch (start us, length us, event | category | flops | bytes accessed | tf_op | source)
XLA Modules:
  0.0 46.2 jit_solution(7050634629200952530)
XLA Ops:
  0.0 5.8 %attend.1 = (bf16[8,8192]{1,0:T(8,128)(2,1)S(1)}, bf16[8192,128]{1,0:T(8,128)(2,1)S(1)}, bf16[8192,128]{1,0:T(8,128)(2,1)S(1)}, bf16[16,128]{1,0:T(8,128)(2,1)S(...) custom-call(s32[4]{0:T(128)} %len_hbm.1, bf16[2,4,8192]{2,1,0:T(4,128)(2,1)} %q_hbm.1, ...), custom_call_target="tpu_custom_call" | custom-call | flops 134217728 | bytes 8388608 | tf_op jit(solution)/shard_map/attend/pallas_call | solution.py:244
  5.8 4.1 %collective-permute-start.7 = (bf16[8,8192]{1,0:T(8,128)(2,1)S(1)}, bf16[8,8192]{1,0:T(8,128)(2,1)S(1)}, u32[]{:S(2)}, u32[]{:S(2)}) collective-permute-start(bf16[8,8192]{1,0:T(8,128)(2,1)S(1)} %get-tuple-element.13.refs_0_), channel_id=1, source_target_pairs={{0,8},{1,9},{2,10},{3,11},{4,12},{5,13},{6,14},{7,15},{8,0},{9,1},... | collective-permute-start | bytes 393224 | tf_op jit(solution)/shard_map/ppermute | solution.py:289
  9.9 2.5 %collective-permute-start.5 = (bf16[8,8192]{1,0:T(8,128)(2,1)S(1)}, bf16[8,8192]{1,0:T(8,128)(2,1)S(1)}, u32[]{:S(2)}, u32[]{:S(2)}) collective-permute-start(bf16[8,8192]{1,0:T(8,128)(2,1)S(1)} %get-tuple-element.13.refs_0_), channel_id=1, source_target_pairs={{0,6},{1,7},{2,4},{3,5},{4,2},{5,3},{6,0},{7,1},{8,14},{9,15},{10,... | collective-permute-start | bytes 393224 | tf_op jit(solution)/shard_map/ppermute | solution.py:289
  12.4 0.5 collective-permute-start.3
  12.9 0.5 %collective-permute-start.1 = (bf16[8,8192]{1,0:T(8,128)(2,1)S(1)}, bf16[8,8192]{1,0:T(8,128)(2,1)S(1)}, u32[]{:S(2)}, u32[]{:S(2)}) collective-permute-start(bf16[8,8192]{1,0:T(8,128)(2,1)S(1)} %get-tuple-element.13.refs_0_), channel_id=1, source_target_pairs={{0,2},{1,3},{2,0},{3,1},{4,6},{5,7},{6,4},{7,5},{8,10},{9,11},{10,... | collective-permute-start | bytes 393224 | tf_op jit(solution)/shard_map/ppermute | solution.py:289
  13.4 2.9 %collective-permute-done.7.refs_8_ = bf16[8,8192]{1,0:T(8,128)(2,1)S(1)} collective-permute-done((bf16[8,8192]{1,0:T(8,128)(2,1)S(1)}, bf16[8,8192]{1,0:T(8,128)(2,1)S(1)}, u32[]{:S(2)}, u32[]{:S(2)}) %collective-permute-start.7) | collective-permute-done | bytes 131104 | tf_op jit(solution)/shard_map/ppermute | solution.py:289
  16.3 1.6 %collective-permute-start.13 = (bf16[8,8192]{1,0:T(8,128)(2,1)S(1)}, bf16[8,8192]{1,0:T(8,128)(2,1)S(1)}, u32[]{:S(2)}, u32[]{:S(2)}) collective-permute-start(bf16[8,8192]{1,0:T(8,128)(2,1)S(1)} %collective-permute-done.7.refs_8_), channel_id=1, source_target_pairs={{0,6},{1,7},{2,4},{3,5},{4,2},{5,3},{6,0},{7,1},{8,14},{9,15},{10,... | collective-permute-start | bytes 393224 | tf_op jit(solution)/shard_map/ppermute | solution.py:289
  17.9 0.9 %collective-permute-done.5.refs_6_ = bf16[8,8192]{1,0:T(8,128)(2,1)S(1)} collective-permute-done((bf16[8,8192]{1,0:T(8,128)(2,1)S(1)}, bf16[8,8192]{1,0:T(8,128)(2,1)S(1)}, u32[]{:S(2)}, u32[]{:S(2)}) %collective-permute-start.5) | collective-permute-done | bytes 131104 | tf_op jit(solution)/shard_map/ppermute | solution.py:289
  18.8 1.2 %collective-permute-start.11 = (bf16[8,8192]{1,0:T(8,128)(2,1)S(1)}, bf16[8,8192]{1,0:T(8,128)(2,1)S(1)}, u32[]{:S(2)}, u32[]{:S(2)}) collective-permute-start(bf16[8,8192]{1,0:T(8,128)(2,1)S(1)} %collective-permute-done.7.refs_8_), channel_id=1, source_target_pairs={{0,4},{1,5},{2,6},{3,7},{4,0},{5,1},{6,2},{7,3},{8,12},{9,13},{10,... | collective-permute-start | bytes 393224 | tf_op jit(solution)/shard_map/ppermute | solution.py:289
  20.1 1.2 %collective-permute-done.3.refs_4_ = bf16[8,8192]{1,0:T(8,128)(2,1)S(1)} collective-permute-done((bf16[8,8192]{1,0:T(8,128)(2,1)S(1)}, bf16[8,8192]{1,0:T(8,128)(2,1)S(1)}, u32[]{:S(2)}, u32[]{:S(2)}) %collective-permute-start.3) | collective-permute-done | bytes 131104 | tf_op jit(solution)/shard_map/ppermute | solution.py:289
  21.3 0.9 %collective-permute-start.9 = (bf16[8,8192]{1,0:T(8,128)(2,1)S(1)}, bf16[8,8192]{1,0:T(8,128)(2,1)S(1)}, u32[]{:S(2)}, u32[]{:S(2)}) collective-permute-start(bf16[8,8192]{1,0:T(8,128)(2,1)S(1)} %collective-permute-done.7.refs_8_), channel_id=1, source_target_pairs={{0,2},{1,3},{2,0},{3,1},{4,6},{5,7},{6,4},{7,5},{8,10},{9,11},{10,... | collective-permute-start | bytes 393224 | tf_op jit(solution)/shard_map/ppermute | solution.py:289
  22.2 0.5 %collective-permute-start.6 = (bf16[8,8192]{1,0:T(8,128)(2,1)S(1)}, bf16[8,8192]{1,0:T(8,128)(2,1)S(1)}, u32[]{:S(2)}, u32[]{:S(2)}) collective-permute-start(bf16[8,8192]{1,0:T(8,128)(2,1)S(1)} %collective-permute-done.5.refs_6_), channel_id=1, source_target_pairs={{0,1},{1,0},{2,3},{3,2},{4,5},{5,4},{6,7},{7,6},{8,9},{9,8},{10,11... | collective-permute-start | bytes 393224 | tf_op jit(solution)/shard_map/ppermute | solution.py:289
  22.7 1.7 %collective-permute-done.13.refs_14_ = bf16[8,8192]{1,0:T(8,128)(2,1)S(1)} collective-permute-done((bf16[8,8192]{1,0:T(8,128)(2,1)S(1)}, bf16[8,8192]{1,0:T(8,128)(2,1)S(1)}, u32[]{:S(2)}, u32[]{:S(2)}) %collective-permute-start.13) | collective-permute-done | bytes 131104 | tf_op jit(solution)/shard_map/ppermute | solution.py:289
  24.5 1.4 %collective-permute-done.11.refs_12_ = bf16[8,8192]{1,0:T(8,128)(2,1)S(1)} collective-permute-done((bf16[8,8192]{1,0:T(8,128)(2,1)S(1)}, bf16[8,8192]{1,0:T(8,128)(2,1)S(1)}, u32[]{:S(2)}, u32[]{:S(2)}) %collective-permute-start.11) | collective-permute-done | bytes 131104 | tf_op jit(solution)/shard_map/ppermute | solution.py:289
  25.9 0.0 collective-permute-start.2
  25.9 0.4 collective-permute-done.9.refs_10_
  26.2 0.2 collective-permute-start.14
  26.4 0.0 collective-permute-done.8.refs_9_
  26.4 0.4 collective-permute-start.12
  26.8 0.0 collective-permute-done.6.refs_7_
  26.8 0.2 collective-permute-start.10
  26.9 0.3 collective-permute-done.2.refs_3_
  27.2 0.4 collective-permute-done.14.refs_15_
  27.6 0.2 collective-permute-done.12.refs_13_
  27.8 0.3 collective-permute-done.10.refs_11_
  28.1 2.2 %delta.1 = (bf16[16,16,512]{2,1,0:T(8,128)(2,1)}, bf16[128,8192]{1,0:T(8,128)(2,1)S(1)}) custom-call(bf16[8,8192]{1,0:T(8,128)(2,1)S(1)} %get-tuple-element.13.refs_0_, bf16[8,8192]{1,0:T(8,128)(2,1)S(1)} %collective-permute-done.refs_1_, bf16[8,8192]{1,0:T(8,128)(2,1)S(1)} %collective-permute-done.1.refs_2_, ...), custom_call_target="tpu_custom_call" | custom-call | flops 301989888 | bytes 8650752 | tf_op jit(solution)/shard_map/delta/pallas_call | solution.py:335
  30.3 5.0 %all-to-all-start = ((bf16[16,16,512]{2,1,0:T(8,128)(2,1)}), bf16[16,16,512]{2,1,0:T(8,128)(2,1)S(1)}, u32[]{:S(2)}, u32[]{:S(2)}) async-start(bf16[16,16,512]{2,1,0:T(8,128)(2,1)} %get-tuple-element.20), calls=%async_computation | async-start | bytes 524288 | tf_op jit(solution)/shard_map/all_to_all | solution.py:435
  35.3 0.0 copy-start
  35.3 3.4 %copy-done = bf16[8192,512]{1,0:T(8,128)(2,1)S(1)} copy-done((bf16[8192,512]{1,0:T(8,128)(2,1)S(1)}, bf16[8192,512]{1,0:T(8,128)(2,1)}, u32[]{:S(2)}) %copy-start) | copy-done | bytes 8388632
  38.7 2.4 %base.1.base_ref = f32[128,512]{1,0:T(8,128)S(1)} custom-call(bf16[128,8192]{1,0:T(8,128)(2,1)S(1)} %get-tuple-element.17.a_ref, bf16[8192,512]{1,0:T(8,128)(2,1)S(1)} %copy-done, bf16[128,128]{1,0:T(8,128)(2,1)S(1)} %get-tuple-element.18.order_ref), custom_call_target="tpu_custom_call" | custom-call | flops 1342177280 | bytes 10747904 | tf_op jit(solution)/shard_map/base/pallas_call | solution.py:367
  41.1 4.3 %all-to-all-done.delta_ref = bf16[16,16,512]{2,1,0:T(8,128)(2,1)S(1)} async-done(((bf16[16,16,512]{2,1,0:T(8,128)(2,1)}), bf16[16,16,512]{2,1,0:T(8,128)(2,1)S(1)}, u32[]{:S(2)}, u32[]{:S(2)}) %all-to-all-start) | async-done | bytes 262176 | tf_op jit(solution)/shard_map/all_to_all | solution.py:435
  45.4 0.8 %join.1 = bf16[2,64,512]{2,1,0:T(8,128)(2,1)} custom-call(f32[128,512]{1,0:T(8,128)S(1)} %base.1.base_ref, bf16[128,256]{1,0:T(8,128)(2,1)S(1)} %get-tuple-element.19.place_ref, bf16[16,16,512]{2,1,0:T(8,128)(2,1)S(1)} %all-to-all-done.delta_ref), custom_call_target="tpu_custom_call" | custom-call | tf_op jit(solution)/shard_map/join/pallas_call | solution.py:394
  (6 shorter events, 0.0 us)
Async XLA Ops:
  5.8 10.5 %collective-permute-start.7 = (bf16[8,8192]{1,0:T(8,128)(2,1)S(1)}, bf16[8,8192]{1,0:T(8,128)(2,1)S(1)}, u32[]{:S(2)}, u32[]{:S(2)}) collective-permute-start(bf16[8,8192]{1,0:T(8,128)(2,1)S(1)} %get-tuple-element.13.refs_0_), channel_id=1, source_target_pairs={{0,8},{1,9},{2,10},{3,11},{4,12},{5,13},{6,14},{7,15},{8,0},{9,1},... | collective-permute-start | bytes 393224 | tf_op jit(solution)/shard_map/ppermute | solution.py:289
  9.9 9.0 %collective-permute-start.5 = (bf16[8,8192]{1,0:T(8,128)(2,1)S(1)}, bf16[8,8192]{1,0:T(8,128)(2,1)S(1)}, u32[]{:S(2)}, u32[]{:S(2)}) collective-permute-start(bf16[8,8192]{1,0:T(8,128)(2,1)S(1)} %get-tuple-element.13.refs_0_), channel_id=1, source_target_pairs={{0,6},{1,7},{2,4},{3,5},{4,2},{5,3},{6,0},{7,1},{8,14},{9,15},{10,... | collective-permute-start | bytes 393224 | tf_op jit(solution)/shard_map/ppermute | solution.py:289
  12.4 8.8 %collective-permute-start.3 = (bf16[8,8192]{1,0:T(8,128)(2,1)S(1)}, bf16[8,8192]{1,0:T(8,128)(2,1)S(1)}, u32[]{:S(2)}, u32[]{:S(2)}) collective-permute-start(bf16[8,8192]{1,0:T(8,128)(2,1)S(1)} %get-tuple-element.13.refs_0_), channel_id=1, source_target_pairs={{0,4},{1,5},{2,6},{3,7},{4,0},{5,1},{6,2},{7,3},{8,12},{9,13},{10,... | collective-permute-start | bytes 393224 | tf_op jit(solution)/shard_map/ppermute | solution.py:289
  12.9 9.3 %collective-permute-start.1 = (bf16[8,8192]{1,0:T(8,128)(2,1)S(1)}, bf16[8,8192]{1,0:T(8,128)(2,1)S(1)}, u32[]{:S(2)}, u32[]{:S(2)}) collective-permute-start(bf16[8,8192]{1,0:T(8,128)(2,1)S(1)} %get-tuple-element.13.refs_0_), channel_id=1, source_target_pairs={{0,2},{1,3},{2,0},{3,1},{4,6},{5,7},{6,4},{7,5},{8,10},{9,11},{10,... | collective-permute-start | bytes 393224 | tf_op jit(solution)/shard_map/ppermute | solution.py:289
  13.4 8.8 %collective-permute-start = (bf16[8,8192]{1,0:T(8,128)(2,1)S(1)}, bf16[8,8192]{1,0:T(8,128)(2,1)S(1)}, u32[]{:S(2)}, u32[]{:S(2)}) collective-permute-start(bf16[8,8192]{1,0:T(8,128)(2,1)S(1)} %get-tuple-element.13.refs_0_), channel_id=1, source_target_pairs={{0,1},{1,0},{2,3},{3,2},{4,5},{5,4},{6,7},{7,6},{8,9},{9,8},{10,11... | collective-permute-start | bytes 393224 | tf_op jit(solution)/shard_map/ppermute | solution.py:289
  16.3 8.2 %collective-permute-start.13 = (bf16[8,8192]{1,0:T(8,128)(2,1)S(1)}, bf16[8,8192]{1,0:T(8,128)(2,1)S(1)}, u32[]{:S(2)}, u32[]{:S(2)}) collective-permute-start(bf16[8,8192]{1,0:T(8,128)(2,1)S(1)} %collective-permute-done.7.refs_8_), channel_id=1, source_target_pairs={{0,6},{1,7},{2,4},{3,5},{4,2},{5,3},{6,0},{7,1},{8,14},{9,15},{10,... | collective-permute-start | bytes 393224 | tf_op jit(solution)/shard_map/ppermute | solution.py:289
  18.8 7.0 %collective-permute-start.11 = (bf16[8,8192]{1,0:T(8,128)(2,1)S(1)}, bf16[8,8192]{1,0:T(8,128)(2,1)S(1)}, u32[]{:S(2)}, u32[]{:S(2)}) collective-permute-start(bf16[8,8192]{1,0:T(8,128)(2,1)S(1)} %collective-permute-done.7.refs_8_), channel_id=1, source_target_pairs={{0,4},{1,5},{2,6},{3,7},{4,0},{5,1},{6,2},{7,3},{8,12},{9,13},{10,... | collective-permute-start | bytes 393224 | tf_op jit(solution)/shard_map/ppermute | solution.py:289
  21.3 5.0 %collective-permute-start.9 = (bf16[8,8192]{1,0:T(8,128)(2,1)S(1)}, bf16[8,8192]{1,0:T(8,128)(2,1)S(1)}, u32[]{:S(2)}, u32[]{:S(2)}) collective-permute-start(bf16[8,8192]{1,0:T(8,128)(2,1)S(1)} %collective-permute-done.7.refs_8_), channel_id=1, source_target_pairs={{0,2},{1,3},{2,0},{3,1},{4,6},{5,7},{6,4},{7,5},{8,10},{9,11},{10,... | collective-permute-start | bytes 393224 | tf_op jit(solution)/shard_map/ppermute | solution.py:289
  22.2 4.2 %collective-permute-start.8 = (bf16[8,8192]{1,0:T(8,128)(2,1)S(1)}, bf16[8,8192]{1,0:T(8,128)(2,1)S(1)}, u32[]{:S(2)}, u32[]{:S(2)}) collective-permute-start(bf16[8,8192]{1,0:T(8,128)(2,1)S(1)} %collective-permute-done.7.refs_8_), channel_id=1, source_target_pairs={{0,1},{1,0},{2,3},{3,2},{4,5},{5,4},{6,7},{7,6},{8,9},{9,8},{10,11... | collective-permute-start | bytes 393224 | tf_op jit(solution)/shard_map/ppermute | solution.py:289
  22.2 4.5 %collective-permute-start.6 = (bf16[8,8192]{1,0:T(8,128)(2,1)S(1)}, bf16[8,8192]{1,0:T(8,128)(2,1)S(1)}, u32[]{:S(2)}, u32[]{:S(2)}) collective-permute-start(bf16[8,8192]{1,0:T(8,128)(2,1)S(1)} %collective-permute-done.5.refs_6_), channel_id=1, source_target_pairs={{0,1},{1,0},{2,3},{3,2},{4,5},{5,4},{6,7},{7,6},{8,9},{9,8},{10,11... | collective-permute-start | bytes 393224 | tf_op jit(solution)/shard_map/ppermute | solution.py:289
  24.5 2.5 %collective-permute-start.4 = (bf16[8,8192]{1,0:T(8,128)(2,1)S(1)}, bf16[8,8192]{1,0:T(8,128)(2,1)S(1)}, u32[]{:S(2)}, u32[]{:S(2)}) collective-permute-start(bf16[8,8192]{1,0:T(8,128)(2,1)S(1)} %collective-permute-done.3.refs_4_), channel_id=1, source_target_pairs={{0,1},{1,0},{2,3},{3,2},{4,5},{5,4},{6,7},{7,6},{8,9},{9,8},{10,11... | collective-permute-start | bytes 393224 | tf_op jit(solution)/shard_map/ppermute | solution.py:289
  25.9 1.3 %collective-permute-start.2 = (bf16[8,8192]{1,0:T(8,128)(2,1)S(1)}, bf16[8,8192]{1,0:T(8,128)(2,1)S(1)}, u32[]{:S(2)}, u32[]{:S(2)}) collective-permute-start(bf16[8,8192]{1,0:T(8,128)(2,1)S(1)} %collective-permute-done.1.refs_2_), channel_id=1, source_target_pairs={{0,1},{1,0},{2,3},{3,2},{4,5},{5,4},{6,7},{7,6},{8,9},{9,8},{10,11... | collective-permute-start | bytes 393224 | tf_op jit(solution)/shard_map/ppermute | solution.py:289
  26.2 1.3 %collective-permute-start.14 = (bf16[8,8192]{1,0:T(8,128)(2,1)S(1)}, bf16[8,8192]{1,0:T(8,128)(2,1)S(1)}, u32[]{:S(2)}, u32[]{:S(2)}) collective-permute-start(bf16[8,8192]{1,0:T(8,128)(2,1)S(1)} %collective-permute-done.13.refs_14_), channel_id=1, source_target_pairs={{0,1},{1,0},{2,3},{3,2},{4,5},{5,4},{6,7},{7,6},{8,9},{9,8},{10,11... | collective-permute-start | bytes 393224 | tf_op jit(solution)/shard_map/ppermute | solution.py:289
  26.4 1.4 %collective-permute-start.12 = (bf16[8,8192]{1,0:T(8,128)(2,1)S(1)}, bf16[8,8192]{1,0:T(8,128)(2,1)S(1)}, u32[]{:S(2)}, u32[]{:S(2)}) collective-permute-start(bf16[8,8192]{1,0:T(8,128)(2,1)S(1)} %collective-permute-done.11.refs_12_), channel_id=1, source_target_pairs={{0,1},{1,0},{2,3},{3,2},{4,5},{5,4},{6,7},{7,6},{8,9},{9,8},{10,11... | collective-permute-start | bytes 393224 | tf_op jit(solution)/shard_map/ppermute | solution.py:289
  26.8 1.3 %collective-permute-start.10 = (bf16[8,8192]{1,0:T(8,128)(2,1)S(1)}, bf16[8,8192]{1,0:T(8,128)(2,1)S(1)}, u32[]{:S(2)}, u32[]{:S(2)}) collective-permute-start(bf16[8,8192]{1,0:T(8,128)(2,1)S(1)} %collective-permute-done.9.refs_10_), channel_id=1, source_target_pairs={{0,1},{1,0},{2,3},{3,2},{4,5},{5,4},{6,7},{7,6},{8,9},{9,8},{10,11... | collective-permute-start | bytes 393224 | tf_op jit(solution)/shard_map/ppermute | solution.py:289
  30.3 15.1 %all-to-all-start = ((bf16[16,16,512]{2,1,0:T(8,128)(2,1)}), bf16[16,16,512]{2,1,0:T(8,128)(2,1)S(1)}, u32[]{:S(2)}, u32[]{:S(2)}) async-start(bf16[16,16,512]{2,1,0:T(8,128)(2,1)} %get-tuple-element.20), calls=%async_computation | async-start | bytes 524288 | tf_op jit(solution)/shard_map/all_to_all | solution.py:435
  35.3 3.4 %copy-start = (bf16[8192,512]{1,0:T(8,128)(2,1)S(1)}, bf16[8192,512]{1,0:T(8,128)(2,1)}, u32[]{:S(2)}) copy-start(bf16[8192,512]{1,0:T(8,128)(2,1)} %w_ref.1) | copy-start | bytes 25165828

commit v15 on v13

--- a/solution.py
+++ b/solution.py
@@ -166,9 +166,6 @@
     write_plan(rows, count_ref, rank_ref, owner_ref, pick_ref, place_ref, order_ref)
 
     rate = HD ** (-0.5) * math.log2(math.e)
-    pairs = [
-        (slice(k * pack, (k + 2) * pack), slice(k * HD, (k + 2) * HD)) for k in range(0, KVH, 2)
-    ]
     for turn in range(rows + 1):
         if turn < rows:
             for copy in keys[turn]:
@@ -200,10 +197,11 @@
         inverse = 1.0 / total
         p_older = jnp.transpose((e_older * inverse).astype(BF16))
         p_fresh = jnp.transpose((e_fresh * inverse).astype(BF16))
-        for k, (own, cols_k) in zip(range(0, KVH, 2), pairs):
-            pair = dot(p_older[own], v_ref[r, :, cols_k]) + dot(p_fresh[own], nvs[:, cols_k])
-            mixed[r, k] = pair[:pack, :HD]
-            mixed[r, k + 1] = pair[pack:, HD:]
+        older_mix = dot(p_older, v_ref[r])
+        fresh_mix = dot(p_fresh, nvs[...])
+        for k in range(KVH):
+            own, cols_k = slice(k * pack, (k + 1) * pack), slice(k * HD, (k + 1) * HD)
+            mixed[r, k] = older_mix[own, cols_k] + fresh_mix[own, cols_k]
 
     for k in range(KVH):
         turned = jnp.stack(
@@ -312,17 +310,14 @@
     blocks = [blocks[at_slot.index(i)] for i in range(len(blocks))]
     parts, slots, cols = out_ref.shape
     each, width = blocks[0].shape
-    cuts = 8
-    deep = width // cuts
-    low = jnp.zeros((parts * each, d_ref.shape[1]), F32)
-    for i in range(cuts):
-        at = slice(i * deep, (i + 1) * deep)
-        piece = jnp.concatenate([b[:, at] for b in blocks], axis=0)
-        rows_ref[:, at] = piece
-        low = low + dot(piece, d_ref[at, :])
-    chosen = dot(pick_ref[...], low.astype(BF16)).astype(BF16)
+    for i in range(0, len(blocks), 2):
+        pair = jnp.concatenate([blocks[i][...], blocks[i + 1][...]], axis=0)
+        rows_ref[i * each : (i + 2) * each, :] = pair
+    low = dot(rows_ref[...], d_ref[...]).astype(BF16)
+    chosen = dot(pick_ref[...], low).astype(BF16)
+    raised = dot_nt(chosen, u_ref[...]).astype(BF16)
     for p in range(parts):
-        out_ref[p] = dot_nt(chosen, u_ref[p * cols : (p + 1) * cols, :]).astype(BF16)
+        out_ref[p] = raised[:, p * cols : (p + 1) * cols]
 
 
 def deltas(blocks, pick, down, up):

time: 46.5 us -> 46.8 us (level)
  no operation moved by 1% of the time
where the time goes in v15:
time: 46.8 us; the launch traced here: 46.5 us
  starting transfers between devices  17.5 us (37%)
  waiting for transfers between devices  14 us (30%)
  Pallas kernels  11.5 us (25%)
  local copies, waits for them, and re-layouts  3.38 us (7%)
    ppermute x15, starting transfers between devices, swap(): return lax.ppermute(x, 'tensor', [(i, i ^ bits) for i in range(parts)])  12.5 us
    ppermute x15, waiting for transfers between devices, swap(): return lax.ppermute(x, 'tensor', [(i, i ^ bits) for i in range(parts)])  9.76 us
    pallas_call x1, Pallas kernels, attend(): pl.pallas_call(attend_kernel, out_shape=[jax.ShapeDtypeStruct(shape, BF16...  6.07 us
    all_to_all x1, starting transfers between devices, per_device(): lax.all_to_all(send, 'tensor', split_axis=0, concat_axis=0, tiled=True)  5.01 us
    all_to_all x1, waiting for transfers between devices, per_device(): lax.all_to_all(send, 'tensor', split_axis=0, concat_axis=0, tiled=True)  4.26 us
    unnamed x2, local copies, waits for them, and re-layouts  3.38 us
    pallas_call x1, Pallas kernels, base_part(): pl.pallas_call(base_kernel, out_shape=jax.ShapeDtypeStruct((total, cols),...  2.4 us
    pallas_call x1, Pallas kernels, deltas(): pl.pallas_call(functools.partial(delta_kernel, at_slot), out_shape=(jax.S...  2.19 us
  transfers between devices with their start and end apart: 16, of which 11 were waited for; matrix products, arithmetic and copies ran while one was open for 0% of the time, Pallas kernels for 5%

profile of v15, /device:TPU:0, one launch (start us, length us, event | category | flops | bytes accessed | tf_op | source)
XLA Modules:
  0.0 46.5 jit_solution(10982396602014812544)
XLA Ops:
  0.0 6.1 %attend.1 = (bf16[8,8192]{1,0:T(8,128)(2,1)S(1)}, bf16[8192,128]{1,0:T(8,128)(2,1)S(1)}, bf16[8192,128]{1,0:T(8,128)(2,1)S(1)}, bf16[16,128]{1,0:T(8,128)(2,1)S(...) custom-call(s32[4]{0:T(128)} %len_hbm.1, bf16[2,4,8192]{2,1,0:T(4,128)(2,1)} %q_hbm.1, ...), custom_call_target="tpu_custom_call" | custom-call | flops 134217728 | bytes 8388608 | tf_op jit(solution)/shard_map/attend/pallas_call | solution.py:242
  6.1 4.1 %collective-permute-start.7 = (bf16[8,8192]{1,0:T(8,128)(2,1)S(1)}, bf16[8,8192]{1,0:T(8,128)(2,1)S(1)}, u32[]{:S(2)}, u32[]{:S(2)}) collective-permute-start(bf16[8,8192]{1,0:T(8,128)(2,1)S(1)} %get-tuple-element.13.refs_0_), channel_id=1, source_target_pairs={{0,8},{1,9},{2,10},{3,11},{4,12},{5,13},{6,14},{7,15},{8,0},{9,1},... | collective-permute-start | bytes 393224 | tf_op jit(solution)/shard_map/ppermute | solution.py:287
  10.2 2.5 %collective-permute-start.5 = (bf16[8,8192]{1,0:T(8,128)(2,1)S(1)}, bf16[8,8192]{1,0:T(8,128)(2,1)S(1)}, u32[]{:S(2)}, u32[]{:S(2)}) collective-permute-start(bf16[8,8192]{1,0:T(8,128)(2,1)S(1)} %get-tuple-element.13.refs_0_), channel_id=1, source_target_pairs={{0,6},{1,7},{2,4},{3,5},{4,2},{5,3},{6,0},{7,1},{8,14},{9,15},{10,... | collective-permute-start | bytes 393224 | tf_op jit(solution)/shard_map/ppermute | solution.py:287
  12.7 0.4 collective-permute-start.3
  13.2 0.5 %collective-permute-start.1 = (bf16[8,8192]{1,0:T(8,128)(2,1)S(1)}, bf16[8,8192]{1,0:T(8,128)(2,1)S(1)}, u32[]{:S(2)}, u32[]{:S(2)}) collective-permute-start(bf16[8,8192]{1,0:T(8,128)(2,1)S(1)} %get-tuple-element.13.refs_0_), channel_id=1, source_target_pairs={{0,2},{1,3},{2,0},{3,1},{4,6},{5,7},{6,4},{7,5},{8,10},{9,11},{10,... | collective-permute-start | bytes 393224 | tf_op jit(solution)/shard_map/ppermute | solution.py:287
  13.7 0.0 collective-permute-start
  13.7 2.9 %collective-permute-done.7.refs_8_ = bf16[8,8192]{1,0:T(8,128)(2,1)S(1)} collective-permute-done((bf16[8,8192]{1,0:T(8,128)(2,1)S(1)}, bf16[8,8192]{1,0:T(8,128)(2,1)S(1)}, u32[]{:S(2)}, u32[]{:S(2)}) %collective-permute-start.7) | collective-permute-done | bytes 131104 | tf_op jit(solution)/shard_map/ppermute | solution.py:287
  16.6 1.6 %collective-permute-start.13 = (bf16[8,8192]{1,0:T(8,128)(2,1)S(1)}, bf16[8,8192]{1,0:T(8,128)(2,1)S(1)}, u32[]{:S(2)}, u32[]{:S(2)}) collective-permute-start(bf16[8,8192]{1,0:T(8,128)(2,1)S(1)} %collective-permute-done.7.refs_8_), channel_id=1, source_target_pairs={{0,6},{1,7},{2,4},{3,5},{4,2},{5,3},{6,0},{7,1},{8,14},{9,15},{10,... | collective-permute-start | bytes 393224 | tf_op jit(solution)/shard_map/ppermute | solution.py:287
  18.2 0.9 %collective-permute-done.5.refs_6_ = bf16[8,8192]{1,0:T(8,128)(2,1)S(1)} collective-permute-done((bf16[8,8192]{1,0:T(8,128)(2,1)S(1)}, bf16[8,8192]{1,0:T(8,128)(2,1)S(1)}, u32[]{:S(2)}, u32[]{:S(2)}) %collective-permute-start.5) | collective-permute-done | bytes 131104 | tf_op jit(solution)/shard_map/ppermute | solution.py:287
  19.1 1.2 %collective-permute-start.11 = (bf16[8,8192]{1,0:T(8,128)(2,1)S(1)}, bf16[8,8192]{1,0:T(8,128)(2,1)S(1)}, u32[]{:S(2)}, u32[]{:S(2)}) collective-permute-start(bf16[8,8192]{1,0:T(8,128)(2,1)S(1)} %collective-permute-done.7.refs_8_), channel_id=1, source_target_pairs={{0,4},{1,5},{2,6},{3,7},{4,0},{5,1},{6,2},{7,3},{8,12},{9,13},{10,... | collective-permute-start | bytes 393224 | tf_op jit(solution)/shard_map/ppermute | solution.py:287
  20.3 1.2 %collective-permute-done.3.refs_4_ = bf16[8,8192]{1,0:T(8,128)(2,1)S(1)} collective-permute-done((bf16[8,8192]{1,0:T(8,128)(2,1)S(1)}, bf16[8,8192]{1,0:T(8,128)(2,1)S(1)}, u32[]{:S(2)}, u32[]{:S(2)}) %collective-permute-start.3) | collective-permute-done | bytes 131104 | tf_op jit(solution)/shard_map/ppermute | solution.py:287
  21.6 0.9 %collective-permute-start.9 = (bf16[8,8192]{1,0:T(8,128)(2,1)S(1)}, bf16[8,8192]{1,0:T(8,128)(2,1)S(1)}, u32[]{:S(2)}, u32[]{:S(2)}) collective-permute-start(bf16[8,8192]{1,0:T(8,128)(2,1)S(1)} %collective-permute-done.7.refs_8_), channel_id=1, source_target_pairs={{0,2},{1,3},{2,0},{3,1},{4,6},{5,7},{6,4},{7,5},{8,10},{9,11},{10,... | collective-permute-start | bytes 393224 | tf_op jit(solution)/shard_map/ppermute | solution.py:287
  22.5 0.0 collective-permute-done.1.refs_2_
  22.5 0.0 collective-permute-start.8
  22.5 0.5 %collective-permute-start.6 = (bf16[8,8192]{1,0:T(8,128)(2,1)S(1)}, bf16[8,8192]{1,0:T(8,128)(2,1)S(1)}, u32[]{:S(2)}, u32[]{:S(2)}) collective-permute-start(bf16[8,8192]{1,0:T(8,128)(2,1)S(1)} %collective-permute-done.5.refs_6_), channel_id=1, source_target_pairs={{0,1},{1,0},{2,3},{3,2},{4,5},{5,4},{6,7},{7,6},{8,9},{9,8},{10,11... | collective-permute-start | bytes 393224 | tf_op jit(solution)/shard_map/ppermute | solution.py:287
  23.0 1.7 %collective-permute-done.13.refs_14_ = bf16[8,8192]{1,0:T(8,128)(2,1)S(1)} collective-permute-done((bf16[8,8192]{1,0:T(8,128)(2,1)S(1)}, bf16[8,8192]{1,0:T(8,128)(2,1)S(1)}, u32[]{:S(2)}, u32[]{:S(2)}) %collective-permute-start.13) | collective-permute-done | bytes 131104 | tf_op jit(solution)/shard_map/ppermute | solution.py:287
  24.8 1.4 %collective-permute-done.11.refs_12_ = bf16[8,8192]{1,0:T(8,128)(2,1)S(1)} collective-permute-done((bf16[8,8192]{1,0:T(8,128)(2,1)S(1)}, bf16[8,8192]{1,0:T(8,128)(2,1)S(1)}, u32[]{:S(2)}, u32[]{:S(2)}) %collective-permute-start.11) | collective-permute-done | bytes 131104 | tf_op jit(solution)/shard_map/ppermute | solution.py:287
  26.2 0.4 collective-permute-done.9.refs_10_
  26.5 0.2 collective-permute-start.14
  26.7 0.4 collective-permute-start.12
  27.1 0.2 collective-permute-start.10
  27.2 0.3 collective-permute-done.2.refs_3_
  27.5 0.4 collective-permute-done.14.refs_15_
  27.9 0.2 collective-permute-done.12.refs_13_
  28.1 0.3 collective-permute-done.10.refs_11_
  28.4 2.2 %delta.1 = (bf16[16,16,512]{2,1,0:T(8,128)(2,1)}, bf16[128,8192]{1,0:T(8,128)(2,1)S(1)}) custom-call(bf16[8,8192]{1,0:T(8,128)(2,1)S(1)} %get-tuple-element.13.refs_0_, bf16[8,8192]{1,0:T(8,128)(2,1)S(1)} %collective-permute-done.refs_1_, bf16[8,8192]{1,0:T(8,128)(2,1)S(1)} %collective-permute-done.1.refs_2_, ...), custom_call_target="tpu_custom_call" | custom-call | flops 301989888 | bytes 8650752 | tf_op jit(solution)/shard_map/delta/pallas_call | solution.py:330
  30.6 5.0 %all-to-all-start = ((bf16[16,16,512]{2,1,0:T(8,128)(2,1)}), bf16[16,16,512]{2,1,0:T(8,128)(2,1)S(1)}, u32[]{:S(2)}, u32[]{:S(2)}) async-start(bf16[16,16,512]{2,1,0:T(8,128)(2,1)} %get-tuple-element.20), calls=%async_computation | async-start | bytes 524288 | tf_op jit(solution)/shard_map/all_to_all | solution.py:430
  35.6 0.0 copy-start
  35.6 3.4 %copy-done = bf16[8192,512]{1,0:T(8,128)(2,1)S(1)} copy-done((bf16[8192,512]{1,0:T(8,128)(2,1)S(1)}, bf16[8192,512]{1,0:T(8,128)(2,1)}, u32[]{:S(2)}) %copy-start) | copy-done | bytes 8388632
  39.0 2.4 %base.1.base_ref = f32[128,512]{1,0:T(8,128)S(1)} custom-call(bf16[128,8192]{1,0:T(8,128)(2,1)S(1)} %get-tuple-element.17.a_ref, bf16[8192,512]{1,0:T(8,128)(2,1)S(1)} %copy-done, bf16[128,128]{1,0:T(8,128)(2,1)S(1)} %get-tuple-element.18.order_ref), custom_call_target="tpu_custom_call" | custom-call | flops 1342177280 | bytes 10747904 | tf_op jit(solution)/shard_map/base/pallas_call | solution.py:362
  41.4 4.3 %all-to-all-done.delta_ref = bf16[16,16,512]{2,1,0:T(8,128)(2,1)S(1)} async-done(((bf16[16,16,512]{2,1,0:T(8,128)(2,1)}), bf16[16,16,512]{2,1,0:T(8,128)(2,1)S(1)}, u32[]{:S(2)}, u32[]{:S(2)}) %all-to-all-start) | async-done | bytes 262176 | tf_op jit(solution)/shard_map/all_to_all | solution.py:430
  45.7 0.8 %join.1 = bf16[2,64,512]{2,1,0:T(8,128)(2,1)} custom-call(f32[128,512]{1,0:T(8,128)S(1)} %base.1.base_ref, bf16[128,256]{1,0:T(8,128)(2,1)S(1)} %get-tuple-element.19.place_ref, bf16[16,16,512]{2,1,0:T(8,128)(2,1)S(1)} %all-to-all-done.delta_ref), custom_call_target="tpu_custom_call" | custom-call | tf_op jit(solution)/shard_map/join/pallas_call | solution.py:389
  (6 shorter events, 0.0 us)
Async XLA Ops:
  6.1 10.5 %collective-permute-start.7 = (bf16[8,8192]{1,0:T(8,128)(2,1)S(1)}, bf16[8,8192]{1,0:T(8,128)(2,1)S(1)}, u32[]{:S(2)}, u32[]{:S(2)}) collective-permute-start(bf16[8,8192]{1,0:T(8,128)(2,1)S(1)} %get-tuple-element.13.refs_0_), channel_id=1, source_target_pairs={{0,8},{1,9},{2,10},{3,11},{4,12},{5,13},{6,14},{7,15},{8,0},{9,1},... | collective-permute-start | bytes 393224 | tf_op jit(solution)/shard_map/ppermute | solution.py:287
  10.2 9.0 %collective-permute-start.5 = (bf16[8,8192]{1,0:T(8,128)(2,1)S(1)}, bf16[8,8192]{1,0:T(8,128)(2,1)S(1)}, u32[]{:S(2)}, u32[]{:S(2)}) collective-permute-start(bf16[8,8192]{1,0:T(8,128)(2,1)S(1)} %get-tuple-element.13.refs_0_), channel_id=1, source_target_pairs={{0,6},{1,7},{2,4},{3,5},{4,2},{5,3},{6,0},{7,1},{8,14},{9,15},{10,... | collective-permute-start | bytes 393224 | tf_op jit(solution)/shard_map/ppermute | solution.py:287
  12.7 8.8 %collective-permute-start.3 = (bf16[8,8192]{1,0:T(8,128)(2,1)S(1)}, bf16[8,8192]{1,0:T(8,128)(2,1)S(1)}, u32[]{:S(2)}, u32[]{:S(2)}) collective-permute-start(bf16[8,8192]{1,0:T(8,128)(2,1)S(1)} %get-tuple-element.13.refs_0_), channel_id=1, source_target_pairs={{0,4},{1,5},{2,6},{3,7},{4,0},{5,1},{6,2},{7,3},{8,12},{9,13},{10,... | collective-permute-start | bytes 393224 | tf_op jit(solution)/shard_map/ppermute | solution.py:287
  13.2 9.3 %collective-permute-start.1 = (bf16[8,8192]{1,0:T(8,128)(2,1)S(1)}, bf16[8,8192]{1,0:T(8,128)(2,1)S(1)}, u32[]{:S(2)}, u32[]{:S(2)}) collective-permute-start(bf16[8,8192]{1,0:T(8,128)(2,1)S(1)} %get-tuple-element.13.refs_0_), channel_id=1, source_target_pairs={{0,2},{1,3},{2,0},{3,1},{4,6},{5,7},{6,4},{7,5},{8,10},{9,11},{10,... | collective-permute-start | bytes 393224 | tf_op jit(solution)/shard_map/ppermute | solution.py:287
  13.7 8.8 %collective-permute-start = (bf16[8,8192]{1,0:T(8,128)(2,1)S(1)}, bf16[8,8192]{1,0:T(8,128)(2,1)S(1)}, u32[]{:S(2)}, u32[]{:S(2)}) collective-permute-start(bf16[8,8192]{1,0:T(8,128)(2,1)S(1)} %get-tuple-element.13.refs_0_), channel_id=1, source_target_pairs={{0,1},{1,0},{2,3},{3,2},{4,5},{5,4},{6,7},{7,6},{8,9},{9,8},{10,11... | collective-permute-start | bytes 393224 | tf_op jit(solution)/shard_map/ppermute | solution.py:287
  16.6 8.2 %collective-permute-start.13 = (bf16[8,8192]{1,0:T(8,128)(2,1)S(1)}, bf16[8,8192]{1,0:T(8,128)(2,1)S(1)}, u32[]{:S(2)}, u32[]{:S(2)}) collective-permute-start(bf16[8,8192]{1,0:T(8,128)(2,1)S(1)} %collective-permute-done.7.refs_8_), channel_id=1, source_target_pairs={{0,6},{1,7},{2,4},{3,5},{4,2},{5,3},{6,0},{7,1},{8,14},{9,15},{10,... | collective-permute-start | bytes 393224 | tf_op jit(solution)/shard_map/ppermute | solution.py:287
  19.1 7.0 %collective-permute-start.11 = (bf16[8,8192]{1,0:T(8,128)(2,1)S(1)}, bf16[8,8192]{1,0:T(8,128)(2,1)S(1)}, u32[]{:S(2)}, u32[]{:S(2)}) collective-permute-start(bf16[8,8192]{1,0:T(8,128)(2,1)S(1)} %collective-permute-done.7.refs_8_), channel_id=1, source_target_pairs={{0,4},{1,5},{2,6},{3,7},{4,0},{5,1},{6,2},{7,3},{8,12},{9,13},{10,... | collective-permute-start | bytes 393224 | tf_op jit(solution)/shard_map/ppermute | solution.py:287
  21.6 5.0 %collective-permute-start.9 = (bf16[8,8192]{1,0:T(8,128)(2,1)S(1)}, bf16[8,8192]{1,0:T(8,128)(2,1)S(1)}, u32[]{:S(2)}, u32[]{:S(2)}) collective-permute-start(bf16[8,8192]{1,0:T(8,128)(2,1)S(1)} %collective-permute-done.7.refs_8_), channel_id=1, source_target_pairs={{0,2},{1,3},{2,0},{3,1},{4,6},{5,7},{6,4},{7,5},{8,10},{9,11},{10,... | collective-permute-start | bytes 393224 | tf_op jit(solution)/shard_map/ppermute | solution.py:287
  22.5 4.2 %collective-permute-start.8 = (bf16[8,8192]{1,0:T(8,128)(2,1)S(1)}, bf16[8,8192]{1,0:T(8,128)(2,1)S(1)}, u32[]{:S(2)}, u32[]{:S(2)}) collective-permute-start(bf16[8,8192]{1,0:T(8,128)(2,1)S(1)} %collective-permute-done.7.refs_8_), channel_id=1, source_target_pairs={{0,1},{1,0},{2,3},{3,2},{4,5},{5,4},{6,7},{7,6},{8,9},{9,8},{10,11... | collective-permute-start | bytes 393224 | tf_op jit(solution)/shard_map/ppermute | solution.py:287
  22.5 4.5 %collective-permute-start.6 = (bf16[8,8192]{1,0:T(8,128)(2,1)S(1)}, bf16[8,8192]{1,0:T(8,128)(2,1)S(1)}, u32[]{:S(2)}, u32[]{:S(2)}) collective-permute-start(bf16[8,8192]{1,0:T(8,128)(2,1)S(1)} %collective-permute-done.5.refs_6_), channel_id=1, source_target_pairs={{0,1},{1,0},{2,3},{3,2},{4,5},{5,4},{6,7},{7,6},{8,9},{9,8},{10,11... | collective-permute-start | bytes 393224 | tf_op jit(solution)/shard_map/ppermute | solution.py:287
  24.8 2.5 %collective-permute-start.4 = (bf16[8,8192]{1,0:T(8,128)(2,1)S(1)}, bf16[8,8192]{1,0:T(8,128)(2,1)S(1)}, u32[]{:S(2)}, u32[]{:S(2)}) collective-permute-start(bf16[8,8192]{1,0:T(8,128)(2,1)S(1)} %collective-permute-done.3.refs_4_), channel_id=1, source_target_pairs={{0,1},{1,0},{2,3},{3,2},{4,5},{5,4},{6,7},{7,6},{8,9},{9,8},{10,11... | collective-permute-start | bytes 393224 | tf_op jit(solution)/shard_map/ppermute | solution.py:287
  26.2 1.3 %collective-permute-start.2 = (bf16[8,8192]{1,0:T(8,128)(2,1)S(1)}, bf16[8,8192]{1,0:T(8,128)(2,1)S(1)}, u32[]{:S(2)}, u32[]{:S(2)}) collective-permute-start(bf16[8,8192]{1,0:T(8,128)(2,1)S(1)} %collective-permute-done.1.refs_2_), channel_id=1, source_target_pairs={{0,1},{1,0},{2,3},{3,2},{4,5},{5,4},{6,7},{7,6},{8,9},{9,8},{10,11... | collective-permute-start | bytes 393224 | tf_op jit(solution)/shard_map/ppermute | solution.py:287
  26.5 1.3 %collective-permute-start.14 = (bf16[8,8192]{1,0:T(8,128)(2,1)S(1)}, bf16[8,8192]{1,0:T(8,128)(2,1)S(1)}, u32[]{:S(2)}, u32[]{:S(2)}) collective-permute-start(bf16[8,8192]{1,0:T(8,128)(2,1)S(1)} %collective-permute-done.13.refs_14_), channel_id=1, source_target_pairs={{0,1},{1,0},{2,3},{3,2},{4,5},{5,4},{6,7},{7,6},{8,9},{9,8},{10,11... | collective-permute-start | bytes 393224 | tf_op jit(solution)/shard_map/ppermute | solution.py:287
  26.7 1.4 %collective-permute-start.12 = (bf16[8,8192]{1,0:T(8,128)(2,1)S(1)}, bf16[8,8192]{1,0:T(8,128)(2,1)S(1)}, u32[]{:S(2)}, u32[]{:S(2)}) collective-permute-start(bf16[8,8192]{1,0:T(8,128)(2,1)S(1)} %collective-permute-done.11.refs_12_), channel_id=1, source_target_pairs={{0,1},{1,0},{2,3},{3,2},{4,5},{5,4},{6,7},{7,6},{8,9},{9,8},{10,11... | collective-permute-start | bytes 393224 | tf_op jit(solution)/shard_map/ppermute | solution.py:287
  27.1 1.3 %collective-permute-start.10 = (bf16[8,8192]{1,0:T(8,128)(2,1)S(1)}, bf16[8,8192]{1,0:T(8,128)(2,1)S(1)}, u32[]{:S(2)}, u32[]{:S(2)}) collective-permute-start(bf16[8,8192]{1,0:T(8,128)(2,1)S(1)} %collective-permute-done.9.refs_10_), channel_id=1, source_target_pairs={{0,1},{1,0},{2,3},{3,2},{4,5},{5,4},{6,7},{7,6},{8,9},{9,8},{10,11... | collective-permute-start | bytes 393224 | tf_op jit(solution)/shard_map/ppermute | solution.py:287
  30.6 15.1 %all-to-all-start = ((bf16[16,16,512]{2,1,0:T(8,128)(2,1)}), bf16[16,16,512]{2,1,0:T(8,128)(2,1)S(1)}, u32[]{:S(2)}, u32[]{:S(2)}) async-start(bf16[16,16,512]{2,1,0:T(8,128)(2,1)} %get-tuple-element.20), calls=%async_computation | async-start | bytes 524288 | tf_op jit(solution)/shard_map/all_to_all | solution.py:430
  35.6 3.4 %copy-start = (bf16[8192,512]{1,0:T(8,128)(2,1)S(1)}, bf16[8192,512]{1,0:T(8,128)(2,1)}, u32[]{:S(2)}) copy-start(bf16[8192,512]{1,0:T(8,128)(2,1)} %w_ref.1) | copy-start | bytes 25165828

commit v16 on v13

--- a/solution.py
+++ b/solution.py
@@ -298,10 +298,10 @@
     held[far] = swap(block, far, parts)
     held[near] = swap(block, near, parts)
     held[y] = swap(block, y, parts)
-    held[near | y] = swap(block, near | y, parts)
+    held[far | near] = swap(held[far], near, parts)
     held[far | y] = swap(held[far], y, parts)
-    held[far | near | y] = swap(held[far], near | y, parts)
-    held[far | near] = swap(held[far], near, parts)
+    held[near | y] = swap(held[y], near, parts)
+    held[far | near | y] = swap(held[far | near], y, parts)
     for slot in list(held):
         held[slot | core] = swap(held[slot], core, parts)
     return [held[slot] for slot in range(parts)]

time: 46.5 us -> 48.1 us (1.034)
  starting transfers between devices: 17.6 us -> 21.3 us
  waiting for transfers between devices: 14 us -> 11.9 us
    ppermute x15, waiting for transfers between devices: 9.76 us -> 7.65 us  [swap(): return lax.ppermute(x, 'tensor', [(i, i ^ bits) for i in range(parts)])]
    ppermute x15, starting transfers between devices: 12.5 us -> 14.4 us  [swap(): return lax.ppermute(x, 'tensor', [(i, i ^ bits) for i in range(parts)])]
    all_to_all x1, starting transfers between devices: 5.01 us -> 6.85 us  [per_device(): lax.all_to_all(send, 'tensor', split_axis=0, concat_axis=0, tiled=True)]
  transfers between devices with their start and end apart: 16 -> 16, of which waited for: 11 -> 6; matrix products, arithmetic and copies ran while one was open for 0% -> 0% of each run, Pallas kernels for 5% -> 5%
where the time goes in v16:
time: 48.1 us; the launch traced here: 47.8 us
  starting transfers between devices  21.3 us (44%)
  waiting for transfers between devices  11.9 us (25%)
  Pallas kernels  11.2 us (23%)
  local copies, waits for them, and re-layouts  3.38 us (7%)
    ppermute x15, starting transfers between devices, swap(): return lax.ppermute(x, 'tensor', [(i, i ^ bits) for i in range(parts)])  14.4 us
    ppermute x15, waiting for transfers between devices, swap(): return lax.ppermute(x, 'tensor', [(i, i ^ bits) for i in range(parts)])  7.65 us
    all_to_all x1, starting transfers between devices, per_device(): lax.all_to_all(send, 'tensor', split_axis=0, concat_axis=0, tiled=True)  6.85 us
    pallas_call x1, Pallas kernels, attend(): pl.pallas_call(attend_kernel, out_shape=[jax.ShapeDtypeStruct(shape, BF16...  5.78 us
    all_to_all x1, waiting for transfers between devices, per_device(): lax.all_to_all(send, 'tensor', split_axis=0, concat_axis=0, tiled=True)  4.26 us
    unnamed x2, local copies, waits for them, and re-layouts  3.38 us
    pallas_call x1, Pallas kernels, base_part(): pl.pallas_call(base_kernel, out_shape=jax.ShapeDtypeStruct((total, cols),...  2.39 us
    pallas_call x1, Pallas kernels, deltas(): pl.pallas_call(functools.partial(delta_kernel, at_slot), out_shape=(jax.S...  2.2 us
  transfers between devices with their start and end apart: 16, of which 6 were waited for; matrix products, arithmetic and copies ran while one was open for 0% of the time, Pallas kernels for 5%

profile of v16, /device:TPU:0, one launch (start us, length us, event | category | flops | bytes accessed | tf_op | source)
XLA Modules:
  0.0 47.8 jit_solution(7397107582036771001)
XLA Ops:
  0.0 5.8 %attend.1 = (bf16[8,8192]{1,0:T(8,128)(2,1)S(1)}, bf16[8192,128]{1,0:T(8,128)(2,1)S(1)}, bf16[8192,128]{1,0:T(8,128)(2,1)S(1)}, bf16[16,128]{1,0:T(8,128)(2,1)S(...) custom-call(s32[4]{0:T(128)} %len_hbm.1, bf16[2,4,8192]{2,1,0:T(4,128)(2,1)} %q_hbm.1, ...), custom_call_target="tpu_custom_call" | custom-call | flops 134217728 | bytes 8388608 | tf_op jit(solution)/shard_map/attend/pallas_call | solution.py:244
  5.8 4.1 %collective-permute-start.7 = (bf16[8,8192]{1,0:T(8,128)(2,1)S(1)}, bf16[8,8192]{1,0:T(8,128)(2,1)S(1)}, u32[]{:S(2)}, u32[]{:S(2)}) collective-permute-start(bf16[8,8192]{1,0:T(8,128)(2,1)S(1)} %get-tuple-element.13.refs_0_), channel_id=1, source_target_pairs={{0,8},{1,9},{2,10},{3,11},{4,12},{5,13},{6,14},{7,15},{8,0},{9,1},... | collective-permute-start | bytes 393224 | tf_op jit(solution)/shard_map/ppermute | solution.py:289
  9.9 1.6 %collective-permute-start.3 = (bf16[8,8192]{1,0:T(8,128)(2,1)S(1)}, bf16[8,8192]{1,0:T(8,128)(2,1)S(1)}, u32[]{:S(2)}, u32[]{:S(2)}) collective-permute-start(bf16[8,8192]{1,0:T(8,128)(2,1)S(1)} %get-tuple-element.13.refs_0_), channel_id=1, source_target_pairs={{0,4},{1,5},{2,6},{3,7},{4,0},{5,1},{6,2},{7,3},{8,12},{9,13},{10,... | collective-permute-start | bytes 393224 | tf_op jit(solution)/shard_map/ppermute | solution.py:289
  11.5 1.5 %collective-permute-start.1 = (bf16[8,8192]{1,0:T(8,128)(2,1)S(1)}, bf16[8,8192]{1,0:T(8,128)(2,1)S(1)}, u32[]{:S(2)}, u32[]{:S(2)}) collective-permute-start(bf16[8,8192]{1,0:T(8,128)(2,1)S(1)} %get-tuple-element.13.refs_0_), channel_id=1, source_target_pairs={{0,2},{1,3},{2,0},{3,1},{4,6},{5,7},{6,4},{7,5},{8,10},{9,11},{10,... | collective-permute-start | bytes 393224 | tf_op jit(solution)/shard_map/ppermute | solution.py:289
  13.0 3.3 %collective-permute-done.7.refs_8_ = bf16[8,8192]{1,0:T(8,128)(2,1)S(1)} collective-permute-done((bf16[8,8192]{1,0:T(8,128)(2,1)S(1)}, bf16[8,8192]{1,0:T(8,128)(2,1)S(1)}, u32[]{:S(2)}, u32[]{:S(2)}) %collective-permute-start.7) | collective-permute-done | bytes 131104 | tf_op jit(solution)/shard_map/ppermute | solution.py:289
  16.3 0.6 %collective-permute-start.11 = (bf16[8,8192]{1,0:T(8,128)(2,1)S(1)}, bf16[8,8192]{1,0:T(8,128)(2,1)S(1)}, u32[]{:S(2)}, u32[]{:S(2)}) collective-permute-start(bf16[8,8192]{1,0:T(8,128)(2,1)S(1)} %collective-permute-done.7.refs_8_), channel_id=1, source_target_pairs={{0,4},{1,5},{2,6},{3,7},{4,0},{5,1},{6,2},{7,3},{8,12},{9,13},{10,... | collective-permute-start | bytes 393224 | tf_op jit(solution)/shard_map/ppermute | solution.py:289
  16.9 1.5 %collective-permute-start.9 = (bf16[8,8192]{1,0:T(8,128)(2,1)S(1)}, bf16[8,8192]{1,0:T(8,128)(2,1)S(1)}, u32[]{:S(2)}, u32[]{:S(2)}) collective-permute-start(bf16[8,8192]{1,0:T(8,128)(2,1)S(1)} %collective-permute-done.7.refs_8_), channel_id=1, source_target_pairs={{0,2},{1,3},{2,0},{3,1},{4,6},{5,7},{6,4},{7,5},{8,10},{9,11},{10,... | collective-permute-start | bytes 393224 | tf_op jit(solution)/shard_map/ppermute | solution.py:289
  18.4 0.0 collective-permute-done.3.refs_4_
  18.4 0.0 collective-permute-start.8
  18.5 0.5 %collective-permute-start.4 = (bf16[8,8192]{1,0:T(8,128)(2,1)S(1)}, bf16[8,8192]{1,0:T(8,128)(2,1)S(1)}, u32[]{:S(2)}, u32[]{:S(2)}) collective-permute-start(bf16[8,8192]{1,0:T(8,128)(2,1)S(1)} %collective-permute-done.3.refs_4_), channel_id=1, source_target_pairs={{0,1},{1,0},{2,3},{3,2},{4,5},{5,4},{6,7},{7,6},{8,9},{9,8},{10,11... | collective-permute-start | bytes 393224 | tf_op jit(solution)/shard_map/ppermute | solution.py:289
  19.0 0.0 collective-permute-done.refs_1_
  19.0 1.5 %collective-permute-start.5 = (bf16[8,8192]{1,0:T(8,128)(2,1)S(1)}, bf16[8,8192]{1,0:T(8,128)(2,1)S(1)}, u32[]{:S(2)}, u32[]{:S(2)}) collective-permute-start(bf16[8,8192]{1,0:T(8,128)(2,1)S(1)} %collective-permute-done.1.refs_2_), channel_id=1, source_target_pairs={{0,4},{1,5},{2,6},{3,7},{4,0},{5,1},{6,2},{7,3},{8,12},{9,13},{10,... | collective-permute-start | bytes 393224 | tf_op jit(solution)/shard_map/ppermute | solution.py:289
  20.4 0.8 %collective-permute-done.11.refs_12_ = bf16[8,8192]{1,0:T(8,128)(2,1)S(1)} collective-permute-done((bf16[8,8192]{1,0:T(8,128)(2,1)S(1)}, bf16[8,8192]{1,0:T(8,128)(2,1)S(1)}, u32[]{:S(2)}, u32[]{:S(2)}) %collective-permute-start.11) | collective-permute-done | bytes 131104 | tf_op jit(solution)/shard_map/ppermute | solution.py:289
  21.3 2.3 %collective-permute-start.13 = (bf16[8,8192]{1,0:T(8,128)(2,1)S(1)}, bf16[8,8192]{1,0:T(8,128)(2,1)S(1)}, u32[]{:S(2)}, u32[]{:S(2)}) collective-permute-start(bf16[8,8192]{1,0:T(8,128)(2,1)S(1)} %collective-permute-done.11.refs_12_), channel_id=1, source_target_pairs={{0,2},{1,3},{2,0},{3,1},{4,6},{5,7},{6,4},{7,5},{8,10},{9,11},{10,... | collective-permute-start | bytes 393224 | tf_op jit(solution)/shard_map/ppermute | solution.py:289
  23.6 0.0 collective-permute-done.9.refs_10_
  23.6 0.0 collective-permute-start.2
  23.6 0.0 collective-permute-done.8.refs_9_
  23.6 0.5 %collective-permute-start.12 = (bf16[8,8192]{1,0:T(8,128)(2,1)S(1)}, bf16[8,8192]{1,0:T(8,128)(2,1)S(1)}, u32[]{:S(2)}, u32[]{:S(2)}) collective-permute-start(bf16[8,8192]{1,0:T(8,128)(2,1)S(1)} %collective-permute-done.11.refs_12_), channel_id=1, source_target_pairs={{0,1},{1,0},{2,3},{3,2},{4,5},{5,4},{6,7},{7,6},{8,9},{9,8},{10,11... | collective-permute-start | bytes 393224 | tf_op jit(solution)/shard_map/ppermute | solution.py:289
  24.1 0.0 collective-permute-done.4.refs_5_
  24.1 0.1 collective-permute-start.10
  24.2 0.2 collective-permute-done.5.refs_6_
  24.4 0.2 collective-permute-start.6
  24.6 1.9 %collective-permute-done.13.refs_14_ = bf16[8,8192]{1,0:T(8,128)(2,1)S(1)} collective-permute-done((bf16[8,8192]{1,0:T(8,128)(2,1)S(1)}, bf16[8,8192]{1,0:T(8,128)(2,1)S(1)}, u32[]{:S(2)}, u32[]{:S(2)}) %collective-permute-start.13) | collective-permute-done | bytes 131104 | tf_op jit(solution)/shard_map/ppermute | solution.py:289
  26.5 0.0 collective-permute-start.14
  26.6 1.3 %collective-permute-done.14.refs_15_ = bf16[8,8192]{1,0:T(8,128)(2,1)S(1)} collective-permute-done((bf16[8,8192]{1,0:T(8,128)(2,1)S(1)}, bf16[8,8192]{1,0:T(8,128)(2,1)S(1)}, u32[]{:S(2)}, u32[]{:S(2)}) %collective-permute-start.14) | collective-permute-done | bytes 131104 | tf_op jit(solution)/shard_map/ppermute | solution.py:289
  27.9 2.2 %delta.1 = (bf16[16,16,512]{2,1,0:T(8,128)(2,1)}, bf16[128,8192]{1,0:T(8,128)(2,1)S(1)}) custom-call(bf16[8,8192]{1,0:T(8,128)(2,1)S(1)} %get-tuple-element.13.refs_0_, bf16[8,8192]{1,0:T(8,128)(2,1)S(1)} %collective-permute-done.refs_1_, bf16[8,8192]{1,0:T(8,128)(2,1)S(1)} %collective-permute-done.1.refs_2_, ...), custom_call_target="tpu_custom_call" | custom-call | flops 301989888 | bytes 8650752 | tf_op jit(solution)/shard_map/delta/pallas_call | solution.py:335
  30.1 6.8 %all-to-all-start = ((bf16[16,16,512]{2,1,0:T(8,128)(2,1)}), bf16[16,16,512]{2,1,0:T(8,128)(2,1)S(1)}, u32[]{:S(2)}, u32[]{:S(2)}) async-start(bf16[16,16,512]{2,1,0:T(8,128)(2,1)} %get-tuple-element.20), calls=%async_computation | async-start | bytes 524288 | tf_op jit(solution)/shard_map/all_to_all | solution.py:435
  36.9 0.0 copy-start
  37.0 3.4 %copy-done = bf16[8192,512]{1,0:T(8,128)(2,1)S(1)} copy-done((bf16[8192,512]{1,0:T(8,128)(2,1)S(1)}, bf16[8192,512]{1,0:T(8,128)(2,1)}, u32[]{:S(2)}) %copy-start) | copy-done | bytes 8388632
  40.3 2.4 %base.1.base_ref = f32[128,512]{1,0:T(8,128)S(1)} custom-call(bf16[128,8192]{1,0:T(8,128)(2,1)S(1)} %get-tuple-element.17.a_ref, bf16[8192,512]{1,0:T(8,128)(2,1)S(1)} %copy-done, bf16[128,128]{1,0:T(8,128)(2,1)S(1)} %get-tuple-element.18.order_ref), custom_call_target="tpu_custom_call" | custom-call | flops 1342177280 | bytes 10747904 | tf_op jit(solution)/shard_map/base/pallas_call | solution.py:367
  42.7 4.3 %all-to-all-done.delta_ref = bf16[16,16,512]{2,1,0:T(8,128)(2,1)S(1)} async-done(((bf16[16,16,512]{2,1,0:T(8,128)(2,1)}), bf16[16,16,512]{2,1,0:T(8,128)(2,1)S(1)}, u32[]{:S(2)}, u32[]{:S(2)}) %all-to-all-start) | async-done | bytes 262176 | tf_op jit(solution)/shard_map/all_to_all | solution.py:435
  47.0 0.8 %join.1 = bf16[2,64,512]{2,1,0:T(8,128)(2,1)} custom-call(f32[128,512]{1,0:T(8,128)S(1)} %base.1.base_ref, bf16[128,256]{1,0:T(8,128)(2,1)S(1)} %get-tuple-element.19.place_ref, bf16[16,16,512]{2,1,0:T(8,128)(2,1)S(1)} %all-to-all-done.delta_ref), custom_call_target="tpu_custom_call" | custom-call | tf_op jit(solution)/shard_map/join/pallas_call | solution.py:394
  (6 shorter events, 0.0 us)
Async XLA Ops:
  5.8 10.5 %collective-permute-start.7 = (bf16[8,8192]{1,0:T(8,128)(2,1)S(1)}, bf16[8,8192]{1,0:T(8,128)(2,1)S(1)}, u32[]{:S(2)}, u32[]{:S(2)}) collective-permute-start(bf16[8,8192]{1,0:T(8,128)(2,1)S(1)} %get-tuple-element.13.refs_0_), channel_id=1, source_target_pairs={{0,8},{1,9},{2,10},{3,11},{4,12},{5,13},{6,14},{7,15},{8,0},{9,1},... | collective-permute-start | bytes 393224 | tf_op jit(solution)/shard_map/ppermute | solution.py:289
  9.9 8.5 %collective-permute-start.3 = (bf16[8,8192]{1,0:T(8,128)(2,1)S(1)}, bf16[8,8192]{1,0:T(8,128)(2,1)S(1)}, u32[]{:S(2)}, u32[]{:S(2)}) collective-permute-start(bf16[8,8192]{1,0:T(8,128)(2,1)S(1)} %get-tuple-element.13.refs_0_), channel_id=1, source_target_pairs={{0,4},{1,5},{2,6},{3,7},{4,0},{5,1},{6,2},{7,3},{8,12},{9,13},{10,... | collective-permute-start | bytes 393224 | tf_op jit(solution)/shard_map/ppermute | solution.py:289
  11.5 7.0 %collective-permute-start.1 = (bf16[8,8192]{1,0:T(8,128)(2,1)S(1)}, bf16[8,8192]{1,0:T(8,128)(2,1)S(1)}, u32[]{:S(2)}, u32[]{:S(2)}) collective-permute-start(bf16[8,8192]{1,0:T(8,128)(2,1)S(1)} %get-tuple-element.13.refs_0_), channel_id=1, source_target_pairs={{0,2},{1,3},{2,0},{3,1},{4,6},{5,7},{6,4},{7,5},{8,10},{9,11},{10,... | collective-permute-start | bytes 393224 | tf_op jit(solution)/shard_map/ppermute | solution.py:289
  13.0 6.0 %collective-permute-start = (bf16[8,8192]{1,0:T(8,128)(2,1)S(1)}, bf16[8,8192]{1,0:T(8,128)(2,1)S(1)}, u32[]{:S(2)}, u32[]{:S(2)}) collective-permute-start(bf16[8,8192]{1,0:T(8,128)(2,1)S(1)} %get-tuple-element.13.refs_0_), channel_id=1, source_target_pairs={{0,1},{1,0},{2,3},{3,2},{4,5},{5,4},{6,7},{7,6},{8,9},{9,8},{10,11... | collective-permute-start | bytes 393224 | tf_op jit(solution)/shard_map/ppermute | solution.py:289
  16.3 5.0 %collective-permute-start.11 = (bf16[8,8192]{1,0:T(8,128)(2,1)S(1)}, bf16[8,8192]{1,0:T(8,128)(2,1)S(1)}, u32[]{:S(2)}, u32[]{:S(2)}) collective-permute-start(bf16[8,8192]{1,0:T(8,128)(2,1)S(1)} %collective-permute-done.7.refs_8_), channel_id=1, source_target_pairs={{0,4},{1,5},{2,6},{3,7},{4,0},{5,1},{6,2},{7,3},{8,12},{9,13},{10,... | collective-permute-start | bytes 393224 | tf_op jit(solution)/shard_map/ppermute | solution.py:289
  16.9 6.7 %collective-permute-start.9 = (bf16[8,8192]{1,0:T(8,128)(2,1)S(1)}, bf16[8,8192]{1,0:T(8,128)(2,1)S(1)}, u32[]{:S(2)}, u32[]{:S(2)}) collective-permute-start(bf16[8,8192]{1,0:T(8,128)(2,1)S(1)} %collective-permute-done.7.refs_8_), channel_id=1, source_target_pairs={{0,2},{1,3},{2,0},{3,1},{4,6},{5,7},{6,4},{7,5},{8,10},{9,11},{10,... | collective-permute-start | bytes 393224 | tf_op jit(solution)/shard_map/ppermute | solution.py:289
  18.4 5.2 %collective-permute-start.8 = (bf16[8,8192]{1,0:T(8,128)(2,1)S(1)}, bf16[8,8192]{1,0:T(8,128)(2,1)S(1)}, u32[]{:S(2)}, u32[]{:S(2)}) collective-permute-start(bf16[8,8192]{1,0:T(8,128)(2,1)S(1)} %collective-permute-done.7.refs_8_), channel_id=1, source_target_pairs={{0,1},{1,0},{2,3},{3,2},{4,5},{5,4},{6,7},{7,6},{8,9},{9,8},{10,11... | collective-permute-start | bytes 393224 | tf_op jit(solution)/shard_map/ppermute | solution.py:289
  18.5 5.7 %collective-permute-start.4 = (bf16[8,8192]{1,0:T(8,128)(2,1)S(1)}, bf16[8,8192]{1,0:T(8,128)(2,1)S(1)}, u32[]{:S(2)}, u32[]{:S(2)}) collective-permute-start(bf16[8,8192]{1,0:T(8,128)(2,1)S(1)} %collective-permute-done.3.refs_4_), channel_id=1, source_target_pairs={{0,1},{1,0},{2,3},{3,2},{4,5},{5,4},{6,7},{7,6},{8,9},{9,8},{10,11... | collective-permute-start | bytes 393224 | tf_op jit(solution)/shard_map/ppermute | solution.py:289
  19.0 5.5 %collective-permute-start.5 = (bf16[8,8192]{1,0:T(8,128)(2,1)S(1)}, bf16[8,8192]{1,0:T(8,128)(2,1)S(1)}, u32[]{:S(2)}, u32[]{:S(2)}) collective-permute-start(bf16[8,8192]{1,0:T(8,128)(2,1)S(1)} %collective-permute-done.1.refs_2_), channel_id=1, source_target_pairs={{0,4},{1,5},{2,6},{3,7},{4,0},{5,1},{6,2},{7,3},{8,12},{9,13},{10,... | collective-permute-start | bytes 393224 | tf_op jit(solution)/shard_map/ppermute | solution.py:289
  21.3 5.3 %collective-permute-start.13 = (bf16[8,8192]{1,0:T(8,128)(2,1)S(1)}, bf16[8,8192]{1,0:T(8,128)(2,1)S(1)}, u32[]{:S(2)}, u32[]{:S(2)}) collective-permute-start(bf16[8,8192]{1,0:T(8,128)(2,1)S(1)} %collective-permute-done.11.refs_12_), channel_id=1, source_target_pairs={{0,2},{1,3},{2,0},{3,1},{4,6},{5,7},{6,4},{7,5},{8,10},{9,11},{10,... | collective-permute-start | bytes 393224 | tf_op jit(solution)/shard_map/ppermute | solution.py:289
  23.6 2.9 %collective-permute-start.2 = (bf16[8,8192]{1,0:T(8,128)(2,1)S(1)}, bf16[8,8192]{1,0:T(8,128)(2,1)S(1)}, u32[]{:S(2)}, u32[]{:S(2)}) collective-permute-start(bf16[8,8192]{1,0:T(8,128)(2,1)S(1)} %collective-permute-done.1.refs_2_), channel_id=1, source_target_pairs={{0,1},{1,0},{2,3},{3,2},{4,5},{5,4},{6,7},{7,6},{8,9},{9,8},{10,11... | collective-permute-start | bytes 393224 | tf_op jit(solution)/shard_map/ppermute | solution.py:289
  23.6 2.9 %collective-permute-start.12 = (bf16[8,8192]{1,0:T(8,128)(2,1)S(1)}, bf16[8,8192]{1,0:T(8,128)(2,1)S(1)}, u32[]{:S(2)}, u32[]{:S(2)}) collective-permute-start(bf16[8,8192]{1,0:T(8,128)(2,1)S(1)} %collective-permute-done.11.refs_12_), channel_id=1, source_target_pairs={{0,1},{1,0},{2,3},{3,2},{4,5},{5,4},{6,7},{7,6},{8,9},{9,8},{10,11... | collective-permute-start | bytes 393224 | tf_op jit(solution)/shard_map/ppermute | solution.py:289
  24.1 2.4 %collective-permute-start.10 = (bf16[8,8192]{1,0:T(8,128)(2,1)S(1)}, bf16[8,8192]{1,0:T(8,128)(2,1)S(1)}, u32[]{:S(2)}, u32[]{:S(2)}) collective-permute-start(bf16[8,8192]{1,0:T(8,128)(2,1)S(1)} %collective-permute-done.9.refs_10_), channel_id=1, source_target_pairs={{0,1},{1,0},{2,3},{3,2},{4,5},{5,4},{6,7},{7,6},{8,9},{9,8},{10,11... | collective-permute-start | bytes 393224 | tf_op jit(solution)/shard_map/ppermute | solution.py:289
  24.4 2.1 %collective-permute-start.6 = (bf16[8,8192]{1,0:T(8,128)(2,1)S(1)}, bf16[8,8192]{1,0:T(8,128)(2,1)S(1)}, u32[]{:S(2)}, u32[]{:S(2)}) collective-permute-start(bf16[8,8192]{1,0:T(8,128)(2,1)S(1)} %collective-permute-done.5.refs_6_), channel_id=1, source_target_pairs={{0,1},{1,0},{2,3},{3,2},{4,5},{5,4},{6,7},{7,6},{8,9},{9,8},{10,11... | collective-permute-start | bytes 393224 | tf_op jit(solution)/shard_map/ppermute | solution.py:289
  26.5 1.3 %collective-permute-start.14 = (bf16[8,8192]{1,0:T(8,128)(2,1)S(1)}, bf16[8,8192]{1,0:T(8,128)(2,1)S(1)}, u32[]{:S(2)}, u32[]{:S(2)}) collective-permute-start(bf16[8,8192]{1,0:T(8,128)(2,1)S(1)} %collective-permute-done.13.refs_14_), channel_id=1, source_target_pairs={{0,1},{1,0},{2,3},{3,2},{4,5},{5,4},{6,7},{7,6},{8,9},{9,8},{10,11... | collective-permute-start | bytes 393224 | tf_op jit(solution)/shard_map/ppermute | solution.py:289
  30.1 16.9 %all-to-all-start = ((bf16[16,16,512]{2,1,0:T(8,128)(2,1)}), bf16[16,16,512]{2,1,0:T(8,128)(2,1)S(1)}, u32[]{:S(2)}, u32[]{:S(2)}) async-start(bf16[16,16,512]{2,1,0:T(8,128)(2,1)} %get-tuple-element.20), calls=%async_computation | async-start | bytes 524288 | tf_op jit(solution)/shard_map/all_to_all | solution.py:435
  36.9 3.4 %copy-start = (bf16[8192,512]{1,0:T(8,128)(2,1)S(1)}, bf16[8192,512]{1,0:T(8,128)(2,1)}, u32[]{:S(2)}) copy-start(bf16[8192,512]{1,0:T(8,128)(2,1)} %w_ref.1) | copy-start | bytes 25165828

commit v17 on v13

--- a/solution.py
+++ b/solution.py
@@ -79,7 +79,7 @@
 
     entry = iota((1, parts * slots), 1)
     nth = entry % MOST
-    first, amount = adapter_of(entry // slots)
+    first, amount = adapter_of(parts - 1 - entry // slots)
     goal = jnp.where(nth < amount, (entry % slots) // MOST * requests + first + nth, -1)
     place_ref[...] = one_hot(iota((total, parts * slots), 0) == goal)
 
@@ -322,7 +322,8 @@
         low = low + dot(piece, d_ref[at, :])
     chosen = dot(pick_ref[...], low.astype(BF16)).astype(BF16)
     for p in range(parts):
-        out_ref[p] = dot_nt(chosen, u_ref[p * cols : (p + 1) * cols, :]).astype(BF16)
+        at = (parts - 1 - p) * cols
+        out_ref[p] = dot_nt(chosen, u_ref[at : at + cols, :]).astype(BF16)
 
 
 def deltas(blocks, pick, down, up):
@@ -432,7 +433,8 @@
     )
     blocks = gather(attended, parts)
     send, gathered = deltas(blocks, pick, down, up)
-    delta = lax.all_to_all(send, "tensor", split_axis=0, concat_axis=0, tiled=True)
+    turned = [list(range(parts))[::-1]]
+    delta = lax.all_to_all(send, "tensor", 0, 0, axis_index_groups=turned, tiled=True)
     base = base_part(gathered, out_weight, order)
     return join(base, place, delta, steps)
 

time: 46.5 us -> 45.2 us (0.972)
  waiting for transfers between devices: 14 us -> 10.9 us
  starting transfers between devices: 17.6 us -> 19.4 us
    all_to_all x1, waiting for transfers between devices: 4.26 us -> 1.16 us  [per_device(): lax.all_to_all(send, 'tensor', 0, 0, axis_index_groups=turned, tiled=True)]
    all_to_all x1, starting transfers between devices: 5.01 us -> 6.86 us  [per_device(): lax.all_to_all(send, 'tensor', 0, 0, axis_index_groups=turned, tiled=True)]
where the time goes in v17:
time: 45.2 us; the launch traced here: 45 us
  starting transfers between devices  19.4 us (43%)
  Pallas kernels  11.2 us (25%)
  waiting for transfers between devices  10.9 us (24%)
  local copies, waits for them, and re-layouts  3.38 us (7%)
    ppermute x15, starting transfers between devices, swap(): return lax.ppermute(x, 'tensor', [(i, i ^ bits) for i in range(parts)])  12.5 us
    ppermute x15, waiting for transfers between devices, swap(): return lax.ppermute(x, 'tensor', [(i, i ^ bits) for i in range(parts)])  9.76 us
    all_to_all x1, starting transfers between devices, per_device(): lax.all_to_all(send, 'tensor', 0, 0, axis_index_groups=turned, tiled=True)  6.86 us
    pallas_call x1, Pallas kernels, attend(): pl.pallas_call(attend_kernel, out_shape=[jax.ShapeDtypeStruct(shape, BF16...  5.8 us
    unnamed x2, local copies, waits for them, and re-layouts  3.38 us
    pallas_call x1, Pallas kernels, base_part(): pl.pallas_call(base_kernel, out_shape=jax.ShapeDtypeStruct((total, cols),...  2.4 us
    pallas_call x1, Pallas kernels, deltas(): pl.pallas_call(functools.partial(delta_kernel, at_slot), out_shape=(jax.S...  2.2 us
    all_to_all x1, waiting for transfers between devices, per_device(): lax.all_to_all(send, 'tensor', 0, 0, axis_index_groups=turned, tiled=True)  1.16 us
  transfers between devices with their start and end apart: 16, of which 11 were waited for; matrix products, arithmetic and copies ran while one was open for 0% of the time, Pallas kernels for 5%

profile of v17, /device:TPU:0, one launch (start us, length us, event | category | flops | bytes accessed | tf_op | source)
XLA Modules:
  0.0 45.0 jit_solution(6109755844180146175)
XLA Ops:
  0.0 5.8 %attend.1 = (bf16[8,8192]{1,0:T(8,128)(2,1)S(1)}, bf16[8192,128]{1,0:T(8,128)(2,1)S(1)}, bf16[8192,128]{1,0:T(8,128)(2,1)S(1)}, bf16[16,128]{1,0:T(8,128)(2,1)S(...) custom-call(s32[4]{0:T(128)} %len_hbm.1, bf16[2,4,8192]{2,1,0:T(4,128)(2,1)} %q_hbm.1, ...), custom_call_target="tpu_custom_call" | custom-call | flops 134217728 | bytes 8388608 | tf_op jit(solution)/shard_map/attend/pallas_call | solution.py:244
  5.8 4.1 %collective-permute-start.7 = (bf16[8,8192]{1,0:T(8,128)(2,1)S(1)}, bf16[8,8192]{1,0:T(8,128)(2,1)S(1)}, u32[]{:S(2)}, u32[]{:S(2)}) collective-permute-start(bf16[8,8192]{1,0:T(8,128)(2,1)S(1)} %get-tuple-element.13.refs_0_), channel_id=1, source_target_pairs={{0,8},{1,9},{2,10},{3,11},{4,12},{5,13},{6,14},{7,15},{8,0},{9,1},... | collective-permute-start | bytes 393224 | tf_op jit(solution)/shard_map/ppermute | solution.py:289
  9.9 2.5 %collective-permute-start.5 = (bf16[8,8192]{1,0:T(8,128)(2,1)S(1)}, bf16[8,8192]{1,0:T(8,128)(2,1)S(1)}, u32[]{:S(2)}, u32[]{:S(2)}) collective-permute-start(bf16[8,8192]{1,0:T(8,128)(2,1)S(1)} %get-tuple-element.13.refs_0_), channel_id=1, source_target_pairs={{0,6},{1,7},{2,4},{3,5},{4,2},{5,3},{6,0},{7,1},{8,14},{9,15},{10,... | collective-permute-start | bytes 393224 | tf_op jit(solution)/shard_map/ppermute | solution.py:289
  12.4 0.4 collective-permute-start.3
  12.9 0.5 %collective-permute-start.1 = (bf16[8,8192]{1,0:T(8,128)(2,1)S(1)}, bf16[8,8192]{1,0:T(8,128)(2,1)S(1)}, u32[]{:S(2)}, u32[]{:S(2)}) collective-permute-start(bf16[8,8192]{1,0:T(8,128)(2,1)S(1)} %get-tuple-element.13.refs_0_), channel_id=1, source_target_pairs={{0,2},{1,3},{2,0},{3,1},{4,6},{5,7},{6,4},{7,5},{8,10},{9,11},{10,... | collective-permute-start | bytes 393224 | tf_op jit(solution)/shard_map/ppermute | solution.py:289
  13.4 0.0 collective-permute-start
  13.4 2.9 %collective-permute-done.7.refs_8_ = bf16[8,8192]{1,0:T(8,128)(2,1)S(1)} collective-permute-done((bf16[8,8192]{1,0:T(8,128)(2,1)S(1)}, bf16[8,8192]{1,0:T(8,128)(2,1)S(1)}, u32[]{:S(2)}, u32[]{:S(2)}) %collective-permute-start.7) | collective-permute-done | bytes 131104 | tf_op jit(solution)/shard_map/ppermute | solution.py:289
  16.3 1.6 %collective-permute-start.13 = (bf16[8,8192]{1,0:T(8,128)(2,1)S(1)}, bf16[8,8192]{1,0:T(8,128)(2,1)S(1)}, u32[]{:S(2)}, u32[]{:S(2)}) collective-permute-start(bf16[8,8192]{1,0:T(8,128)(2,1)S(1)} %collective-permute-done.7.refs_8_), channel_id=1, source_target_pairs={{0,6},{1,7},{2,4},{3,5},{4,2},{5,3},{6,0},{7,1},{8,14},{9,15},{10,... | collective-permute-start | bytes 393224 | tf_op jit(solution)/shard_map/ppermute | solution.py:289
  17.9 0.9 %collective-permute-done.5.refs_6_ = bf16[8,8192]{1,0:T(8,128)(2,1)S(1)} collective-permute-done((bf16[8,8192]{1,0:T(8,128)(2,1)S(1)}, bf16[8,8192]{1,0:T(8,128)(2,1)S(1)}, u32[]{:S(2)}, u32[]{:S(2)}) %collective-permute-start.5) | collective-permute-done | bytes 131104 | tf_op jit(solution)/shard_map/ppermute | solution.py:289
  18.9 1.2 %collective-permute-start.11 = (bf16[8,8192]{1,0:T(8,128)(2,1)S(1)}, bf16[8,8192]{1,0:T(8,128)(2,1)S(1)}, u32[]{:S(2)}, u32[]{:S(2)}) collective-permute-start(bf16[8,8192]{1,0:T(8,128)(2,1)S(1)} %collective-permute-done.7.refs_8_), channel_id=1, source_target_pairs={{0,4},{1,5},{2,6},{3,7},{4,0},{5,1},{6,2},{7,3},{8,12},{9,13},{10,... | collective-permute-start | bytes 393224 | tf_op jit(solution)/shard_map/ppermute | solution.py:289
  20.1 1.2 %collective-permute-done.3.refs_4_ = bf16[8,8192]{1,0:T(8,128)(2,1)S(1)} collective-permute-done((bf16[8,8192]{1,0:T(8,128)(2,1)S(1)}, bf16[8,8192]{1,0:T(8,128)(2,1)S(1)}, u32[]{:S(2)}, u32[]{:S(2)}) %collective-permute-start.3) | collective-permute-done | bytes 131104 | tf_op jit(solution)/shard_map/ppermute | solution.py:289
  21.3 0.9 %collective-permute-start.9 = (bf16[8,8192]{1,0:T(8,128)(2,1)S(1)}, bf16[8,8192]{1,0:T(8,128)(2,1)S(1)}, u32[]{:S(2)}, u32[]{:S(2)}) collective-permute-start(bf16[8,8192]{1,0:T(8,128)(2,1)S(1)} %collective-permute-done.7.refs_8_), channel_id=1, source_target_pairs={{0,2},{1,3},{2,0},{3,1},{4,6},{5,7},{6,4},{7,5},{8,10},{9,11},{10,... | collective-permute-start | bytes 393224 | tf_op jit(solution)/shard_map/ppermute | solution.py:289
  22.2 0.0 collective-permute-done.1.refs_2_
  22.2 0.0 collective-permute-start.8
  22.2 0.0 collective-permute-done.refs_1_
  22.2 0.5 %collective-permute-start.6 = (bf16[8,8192]{1,0:T(8,128)(2,1)S(1)}, bf16[8,8192]{1,0:T(8,128)(2,1)S(1)}, u32[]{:S(2)}, u32[]{:S(2)}) collective-permute-start(bf16[8,8192]{1,0:T(8,128)(2,1)S(1)} %collective-permute-done.5.refs_6_), channel_id=1, source_target_pairs={{0,1},{1,0},{2,3},{3,2},{4,5},{5,4},{6,7},{7,6},{8,9},{9,8},{10,11... | collective-permute-start | bytes 393224 | tf_op jit(solution)/shard_map/ppermute | solution.py:289
  22.8 1.7 %collective-permute-done.13.refs_14_ = bf16[8,8192]{1,0:T(8,128)(2,1)S(1)} collective-permute-done((bf16[8,8192]{1,0:T(8,128)(2,1)S(1)}, bf16[8,8192]{1,0:T(8,128)(2,1)S(1)}, u32[]{:S(2)}, u32[]{:S(2)}) %collective-permute-start.13) | collective-permute-done | bytes 131104 | tf_op jit(solution)/shard_map/ppermute | solution.py:289
  24.5 1.4 %collective-permute-done.11.refs_12_ = bf16[8,8192]{1,0:T(8,128)(2,1)S(1)} collective-permute-done((bf16[8,8192]{1,0:T(8,128)(2,1)S(1)}, bf16[8,8192]{1,0:T(8,128)(2,1)S(1)}, u32[]{:S(2)}, u32[]{:S(2)}) %collective-permute-start.11) | collective-permute-done | bytes 131104 | tf_op jit(solution)/shard_map/ppermute | solution.py:289
  25.9 0.4 collective-permute-done.9.refs_10_
  26.3 0.2 collective-permute-start.14
  26.4 0.4 collective-permute-start.12
  26.8 0.2 collective-permute-start.10
  26.9 0.3 collective-permute-done.2.refs_3_
  27.2 0.4 collective-permute-done.14.refs_15_
  27.6 0.2 collective-permute-done.12.refs_13_
  27.8 0.3 collective-permute-done.10.refs_11_
  28.1 2.2 %delta.1 = (bf16[16,16,512]{2,1,0:T(8,128)(2,1)}, bf16[128,8192]{1,0:T(8,128)(2,1)S(1)}) custom-call(bf16[8,8192]{1,0:T(8,128)(2,1)S(1)} %get-tuple-element.13.refs_0_, bf16[8,8192]{1,0:T(8,128)(2,1)S(1)} %collective-permute-done.refs_1_, bf16[8,8192]{1,0:T(8,128)(2,1)S(1)} %collective-permute-done.1.refs_2_, ...), custom_call_target="tpu_custom_call" | custom-call | flops 301989888 | bytes 8650752 | tf_op jit(solution)/shard_map/delta/pallas_call | solution.py:336
  30.3 6.9 %all-to-all-start = ((bf16[16,16,512]{2,1,0:T(8,128)(2,1)}), bf16[16,16,512]{2,1,0:T(8,128)(2,1)S(1)}, u32[]{:S(2)}, u32[]{:S(2)}) async-start(bf16[16,16,512]{2,1,0:T(8,128)(2,1)} %get-tuple-element.20), calls=%async_computation | async-start | bytes 524288 | tf_op jit(solution)/shard_map/all_to_all | solution.py:437
  37.2 3.4 %copy-done = bf16[8192,512]{1,0:T(8,128)(2,1)S(1)} copy-done((bf16[8192,512]{1,0:T(8,128)(2,1)S(1)}, bf16[8192,512]{1,0:T(8,128)(2,1)}, u32[]{:S(2)}) %copy-start) | copy-done | bytes 8388632
  40.6 2.4 %base.1.base_ref = f32[128,512]{1,0:T(8,128)S(1)} custom-call(bf16[128,8192]{1,0:T(8,128)(2,1)S(1)} %get-tuple-element.17.a_ref, bf16[8192,512]{1,0:T(8,128)(2,1)S(1)} %copy-done, bf16[128,128]{1,0:T(8,128)(2,1)S(1)} %get-tuple-element.18.order_ref), custom_call_target="tpu_custom_call" | custom-call | flops 1342177280 | bytes 10747904 | tf_op jit(solution)/shard_map/base/pallas_call | solution.py:368
  43.0 1.2 %all-to-all-done.delta_ref = bf16[16,16,512]{2,1,0:T(8,128)(2,1)S(1)} async-done(((bf16[16,16,512]{2,1,0:T(8,128)(2,1)}), bf16[16,16,512]{2,1,0:T(8,128)(2,1)S(1)}, u32[]{:S(2)}, u32[]{:S(2)}) %all-to-all-start) | async-done | bytes 262176 | tf_op jit(solution)/shard_map/all_to_all | solution.py:437
  44.1 0.8 %join.1 = bf16[2,64,512]{2,1,0:T(8,128)(2,1)} custom-call(f32[128,512]{1,0:T(8,128)S(1)} %base.1.base_ref, bf16[128,256]{1,0:T(8,128)(2,1)S(1)} %get-tuple-element.19.place_ref, bf16[16,16,512]{2,1,0:T(8,128)(2,1)S(1)} %all-to-all-done.delta_ref), custom_call_target="tpu_custom_call" | custom-call | tf_op jit(solution)/shard_map/join/pallas_call | solution.py:395
  (6 shorter events, 0.0 us)
Async XLA Ops:
  5.8 10.5 %collective-permute-start.7 = (bf16[8,8192]{1,0:T(8,128)(2,1)S(1)}, bf16[8,8192]{1,0:T(8,128)(2,1)S(1)}, u32[]{:S(2)}, u32[]{:S(2)}) collective-permute-start(bf16[8,8192]{1,0:T(8,128)(2,1)S(1)} %get-tuple-element.13.refs_0_), channel_id=1, source_target_pairs={{0,8},{1,9},{2,10},{3,11},{4,12},{5,13},{6,14},{7,15},{8,0},{9,1},... | collective-permute-start | bytes 393224 | tf_op jit(solution)/shard_map/ppermute | solution.py:289
  9.9 9.0 %collective-permute-start.5 = (bf16[8,8192]{1,0:T(8,128)(2,1)S(1)}, bf16[8,8192]{1,0:T(8,128)(2,1)S(1)}, u32[]{:S(2)}, u32[]{:S(2)}) collective-permute-start(bf16[8,8192]{1,0:T(8,128)(2,1)S(1)} %get-tuple-element.13.refs_0_), channel_id=1, source_target_pairs={{0,6},{1,7},{2,4},{3,5},{4,2},{5,3},{6,0},{7,1},{8,14},{9,15},{10,... | collective-permute-start | bytes 393224 | tf_op jit(solution)/shard_map/ppermute | solution.py:289
  12.4 8.8 %collective-permute-start.3 = (bf16[8,8192]{1,0:T(8,128)(2,1)S(1)}, bf16[8,8192]{1,0:T(8,128)(2,1)S(1)}, u32[]{:S(2)}, u32[]{:S(2)}) collective-permute-start(bf16[8,8192]{1,0:T(8,128)(2,1)S(1)} %get-tuple-element.13.refs_0_), channel_id=1, source_target_pairs={{0,4},{1,5},{2,6},{3,7},{4,0},{5,1},{6,2},{7,3},{8,12},{9,13},{10,... | collective-permute-start | bytes 393224 | tf_op jit(solution)/shard_map/ppermute | solution.py:289
  12.9 9.3 %collective-permute-start.1 = (bf16[8,8192]{1,0:T(8,128)(2,1)S(1)}, bf16[8,8192]{1,0:T(8,128)(2,1)S(1)}, u32[]{:S(2)}, u32[]{:S(2)}) collective-permute-start(bf16[8,8192]{1,0:T(8,128)(2,1)S(1)} %get-tuple-element.13.refs_0_), channel_id=1, source_target_pairs={{0,2},{1,3},{2,0},{3,1},{4,6},{5,7},{6,4},{7,5},{8,10},{9,11},{10,... | collective-permute-start | bytes 393224 | tf_op jit(solution)/shard_map/ppermute | solution.py:289
  13.4 8.8 %collective-permute-start = (bf16[8,8192]{1,0:T(8,128)(2,1)S(1)}, bf16[8,8192]{1,0:T(8,128)(2,1)S(1)}, u32[]{:S(2)}, u32[]{:S(2)}) collective-permute-start(bf16[8,8192]{1,0:T(8,128)(2,1)S(1)} %get-tuple-element.13.refs_0_), channel_id=1, source_target_pairs={{0,1},{1,0},{2,3},{3,2},{4,5},{5,4},{6,7},{7,6},{8,9},{9,8},{10,11... | collective-permute-start | bytes 393224 | tf_op jit(solution)/shard_map/ppermute | solution.py:289
  16.3 8.2 %collective-permute-start.13 = (bf16[8,8192]{1,0:T(8,128)(2,1)S(1)}, bf16[8,8192]{1,0:T(8,128)(2,1)S(1)}, u32[]{:S(2)}, u32[]{:S(2)}) collective-permute-start(bf16[8,8192]{1,0:T(8,128)(2,1)S(1)} %collective-permute-done.7.refs_8_), channel_id=1, source_target_pairs={{0,6},{1,7},{2,4},{3,5},{4,2},{5,3},{6,0},{7,1},{8,14},{9,15},{10,... | collective-permute-start | bytes 393224 | tf_op jit(solution)/shard_map/ppermute | solution.py:289
  18.9 7.0 %collective-permute-start.11 = (bf16[8,8192]{1,0:T(8,128)(2,1)S(1)}, bf16[8,8192]{1,0:T(8,128)(2,1)S(1)}, u32[]{:S(2)}, u32[]{:S(2)}) collective-permute-start(bf16[8,8192]{1,0:T(8,128)(2,1)S(1)} %collective-permute-done.7.refs_8_), channel_id=1, source_target_pairs={{0,4},{1,5},{2,6},{3,7},{4,0},{5,1},{6,2},{7,3},{8,12},{9,13},{10,... | collective-permute-start | bytes 393224 | tf_op jit(solution)/shard_map/ppermute | solution.py:289
  21.3 5.0 %collective-permute-start.9 = (bf16[8,8192]{1,0:T(8,128)(2,1)S(1)}, bf16[8,8192]{1,0:T(8,128)(2,1)S(1)}, u32[]{:S(2)}, u32[]{:S(2)}) collective-permute-start(bf16[8,8192]{1,0:T(8,128)(2,1)S(1)} %collective-permute-done.7.refs_8_), channel_id=1, source_target_pairs={{0,2},{1,3},{2,0},{3,1},{4,6},{5,7},{6,4},{7,5},{8,10},{9,11},{10,... | collective-permute-start | bytes 393224 | tf_op jit(solution)/shard_map/ppermute | solution.py:289
  22.2 4.2 %collective-permute-start.8 = (bf16[8,8192]{1,0:T(8,128)(2,1)S(1)}, bf16[8,8192]{1,0:T(8,128)(2,1)S(1)}, u32[]{:S(2)}, u32[]{:S(2)}) collective-permute-start(bf16[8,8192]{1,0:T(8,128)(2,1)S(1)} %collective-permute-done.7.refs_8_), channel_id=1, source_target_pairs={{0,1},{1,0},{2,3},{3,2},{4,5},{5,4},{6,7},{7,6},{8,9},{9,8},{10,11... | collective-permute-start | bytes 393224 | tf_op jit(solution)/shard_map/ppermute | solution.py:289
  22.2 4.5 %collective-permute-start.6 = (bf16[8,8192]{1,0:T(8,128)(2,1)S(1)}, bf16[8,8192]{1,0:T(8,128)(2,1)S(1)}, u32[]{:S(2)}, u32[]{:S(2)}) collective-permute-start(bf16[8,8192]{1,0:T(8,128)(2,1)S(1)} %collective-permute-done.5.refs_6_), channel_id=1, source_target_pairs={{0,1},{1,0},{2,3},{3,2},{4,5},{5,4},{6,7},{7,6},{8,9},{9,8},{10,11... | collective-permute-start | bytes 393224 | tf_op jit(solution)/shard_map/ppermute | solution.py:289
  24.5 2.5 %collective-permute-start.4 = (bf16[8,8192]{1,0:T(8,128)(2,1)S(1)}, bf16[8,8192]{1,0:T(8,128)(2,1)S(1)}, u32[]{:S(2)}, u32[]{:S(2)}) collective-permute-start(bf16[8,8192]{1,0:T(8,128)(2,1)S(1)} %collective-permute-done.3.refs_4_), channel_id=1, source_target_pairs={{0,1},{1,0},{2,3},{3,2},{4,5},{5,4},{6,7},{7,6},{8,9},{9,8},{10,11... | collective-permute-start | bytes 393224 | tf_op jit(solution)/shard_map/ppermute | solution.py:289
  25.9 1.3 %collective-permute-start.2 = (bf16[8,8192]{1,0:T(8,128)(2,1)S(1)}, bf16[8,8192]{1,0:T(8,128)(2,1)S(1)}, u32[]{:S(2)}, u32[]{:S(2)}) collective-permute-start(bf16[8,8192]{1,0:T(8,128)(2,1)S(1)} %collective-permute-done.1.refs_2_), channel_id=1, source_target_pairs={{0,1},{1,0},{2,3},{3,2},{4,5},{5,4},{6,7},{7,6},{8,9},{9,8},{10,11... | collective-permute-start | bytes 393224 | tf_op jit(solution)/shard_map/ppermute | solution.py:289
  26.3 1.3 %collective-permute-start.14 = (bf16[8,8192]{1,0:T(8,128)(2,1)S(1)}, bf16[8,8192]{1,0:T(8,128)(2,1)S(1)}, u32[]{:S(2)}, u32[]{:S(2)}) collective-permute-start(bf16[8,8192]{1,0:T(8,128)(2,1)S(1)} %collective-permute-done.13.refs_14_), channel_id=1, source_target_pairs={{0,1},{1,0},{2,3},{3,2},{4,5},{5,4},{6,7},{7,6},{8,9},{9,8},{10,11... | collective-permute-start | bytes 393224 | tf_op jit(solution)/shard_map/ppermute | solution.py:289
  26.4 1.4 %collective-permute-start.12 = (bf16[8,8192]{1,0:T(8,128)(2,1)S(1)}, bf16[8,8192]{1,0:T(8,128)(2,1)S(1)}, u32[]{:S(2)}, u32[]{:S(2)}) collective-permute-start(bf16[8,8192]{1,0:T(8,128)(2,1)S(1)} %collective-permute-done.11.refs_12_), channel_id=1, source_target_pairs={{0,1},{1,0},{2,3},{3,2},{4,5},{5,4},{6,7},{7,6},{8,9},{9,8},{10,11... | collective-permute-start | bytes 393224 | tf_op jit(solution)/shard_map/ppermute | solution.py:289
  26.8 1.3 %collective-permute-start.10 = (bf16[8,8192]{1,0:T(8,128)(2,1)S(1)}, bf16[8,8192]{1,0:T(8,128)(2,1)S(1)}, u32[]{:S(2)}, u32[]{:S(2)}) collective-permute-start(bf16[8,8192]{1,0:T(8,128)(2,1)S(1)} %collective-permute-done.9.refs_10_), channel_id=1, source_target_pairs={{0,1},{1,0},{2,3},{3,2},{4,5},{5,4},{6,7},{7,6},{8,9},{9,8},{10,11... | collective-permute-start | bytes 393224 | tf_op jit(solution)/shard_map/ppermute | solution.py:289
  30.3 13.8 %all-to-all-start = ((bf16[16,16,512]{2,1,0:T(8,128)(2,1)}), bf16[16,16,512]{2,1,0:T(8,128)(2,1)S(1)}, u32[]{:S(2)}, u32[]{:S(2)}) async-start(bf16[16,16,512]{2,1,0:T(8,128)(2,1)} %get-tuple-element.20), calls=%async_computation | async-start | bytes 524288 | tf_op jit(solution)/shard_map/all_to_all | solution.py:437
  37.2 3.4 %copy-start = (bf16[8192,512]{1,0:T(8,128)(2,1)S(1)}, bf16[8192,512]{1,0:T(8,128)(2,1)}, u32[]{:S(2)}) copy-start(bf16[8192,512]{1,0:T(8,128)(2,1)} %w_ref.1) | copy-start | bytes 25165828

commit v18 on v17

--- a/solution.py
+++ b/solution.py
@@ -15,6 +15,7 @@
 MOST = 8
 RING = 16
 ORDER = [0, 1, 2, 3, 4, 5, 6, 7, 8, 9, 10, 11, 12, 13, 14, 15]
+EXCHANGE = [11, 10, 9, 8, 15, 14, 13, 12, 7, 6, 5, 4, 3, 2, 1, 0]
 F32 = jnp.float32
 BF16 = jnp.bfloat16
 NT = (((1,), (1,)), ((), ()))
@@ -42,6 +43,10 @@
 
 def sender(slot, me, parts):
     return me ^ slot if parts == RING else slot
+
+
+def exchange_order(parts):
+    return EXCHANGE if parts == RING else [*range(parts)]
 
 
 def write_plan(rows, count_ref, rank_ref, owner_ref, pick_ref, place_ref, order_ref):
@@ -79,7 +84,10 @@
 
     entry = iota((1, parts * slots), 1)
     nth = entry % MOST
-    first, amount = adapter_of(parts - 1 - entry // slots)
+    source = jnp.zeros_like(entry)
+    for i, device in enumerate(exchange_order(parts)):
+        source = jnp.where(entry // slots == i, device, source)
+    first, amount = adapter_of(source)
     goal = jnp.where(nth < amount, (entry % slots) // MOST * requests + first + nth, -1)
     place_ref[...] = one_hot(iota((total, parts * slots), 0) == goal)
 
@@ -321,8 +329,8 @@
         rows_ref[:, at] = piece
         low = low + dot(piece, d_ref[at, :])
     chosen = dot(pick_ref[...], low.astype(BF16)).astype(BF16)
-    for p in range(parts):
-        at = (parts - 1 - p) * cols
+    for p, device in enumerate(exchange_order(parts)):
+        at = device * cols
         out_ref[p] = dot_nt(chosen, u_ref[at : at + cols, :]).astype(BF16)
 
 
@@ -433,8 +441,8 @@
     )
     blocks = gather(attended, parts)
     send, gathered = deltas(blocks, pick, down, up)
-    turned = [list(range(parts))[::-1]]
-    delta = lax.all_to_all(send, "tensor", 0, 0, axis_index_groups=turned, tiled=True)
+    groups = [exchange_order(parts)]
+    delta = lax.all_to_all(send, "tensor", 0, 0, axis_index_groups=groups, tiled=True)
     base = base_part(gathered, out_weight, order)
     return join(base, place, delta, steps)
 

time: 45.2 us -> 43.5 us (0.962)
  starting transfers between devices: 19.4 us -> 18 us
    all_to_all x1, starting transfers between devices: 6.86 us -> 5.43 us  [per_device(): lax.all_to_all(send, 'tensor', 0, 0, axis_index_groups=groups, tiled=True)]
  transfers between devices with their start and end apart: 16 -> 16, of which waited for: 11 -> 11; matrix products, arithmetic and copies ran while one was open for 0% -> 0% of each run, Pallas kernels for 5% -> 6%
where the time goes in v18:
time: 43.5 us; the launch traced here: 43.2 us
  starting transfers between devices  18 us (41%)
  Pallas kernels  11.3 us (26%)
  waiting for transfers between devices  10.5 us (24%)
  local copies, waits for them, and re-layouts  3.38 us (8%)
    ppermute x15, starting transfers between devices, swap(): return lax.ppermute(x, 'tensor', [(i, i ^ bits) for i in range(parts)])  12.5 us
    ppermute x15, waiting for transfers between devices, swap(): return lax.ppermute(x, 'tensor', [(i, i ^ bits) for i in range(parts)])  9.76 us
    pallas_call x1, Pallas kernels, attend(): pl.pallas_call(attend_kernel, out_shape=[jax.ShapeDtypeStruct(shape, BF16...  5.8 us
    all_to_all x1, starting transfers between devices, per_device(): lax.all_to_all(send, 'tensor', 0, 0, axis_index_groups=groups, tiled=True)  5.43 us
    unnamed x2, local copies, waits for them, and re-layouts  3.38 us
    pallas_call x1, Pallas kernels, base_part(): pl.pallas_call(base_kernel, out_shape=jax.ShapeDtypeStruct((total, cols),...  2.42 us
    pallas_call x1, Pallas kernels, deltas(): pl.pallas_call(functools.partial(delta_kernel, at_slot), out_shape=(jax.S...  2.2 us
  transfers between devices with their start and end apart: 16, of which 11 were waited for; matrix products, arithmetic and copies ran while one was open for 0% of the time, Pallas kernels for 6%

profile of v18, /device:TPU:0, one launch (start us, length us, event | category | flops | bytes accessed | tf_op | source)
XLA Modules:
  0.0 43.2 jit_solution(1063527404875124412)
XLA Ops:
  0.0 5.8 %attend.1 = (bf16[8,8192]{1,0:T(8,128)(2,1)S(1)}, bf16[8192,128]{1,0:T(8,128)(2,1)S(1)}, bf16[8192,128]{1,0:T(8,128)(2,1)S(1)}, bf16[16,128]{1,0:T(8,128)(2,1)S(...) custom-call(s32[4]{0:T(128)} %len_hbm.1, bf16[2,4,8192]{2,1,0:T(4,128)(2,1)} %q_hbm.1, ...), custom_call_target="tpu_custom_call" | custom-call | flops 134217728 | bytes 8388608 | tf_op jit(solution)/shard_map/attend/pallas_call | solution.py:252
  5.8 4.1 %collective-permute-start.7 = (bf16[8,8192]{1,0:T(8,128)(2,1)S(1)}, bf16[8,8192]{1,0:T(8,128)(2,1)S(1)}, u32[]{:S(2)}, u32[]{:S(2)}) collective-permute-start(bf16[8,8192]{1,0:T(8,128)(2,1)S(1)} %get-tuple-element.13.refs_0_), channel_id=1, source_target_pairs={{0,8},{1,9},{2,10},{3,11},{4,12},{5,13},{6,14},{7,15},{8,0},{9,1},... | collective-permute-start | bytes 393224 | tf_op jit(solution)/shard_map/ppermute | solution.py:297
  9.9 2.5 %collective-permute-start.5 = (bf16[8,8192]{1,0:T(8,128)(2,1)S(1)}, bf16[8,8192]{1,0:T(8,128)(2,1)S(1)}, u32[]{:S(2)}, u32[]{:S(2)}) collective-permute-start(bf16[8,8192]{1,0:T(8,128)(2,1)S(1)} %get-tuple-element.13.refs_0_), channel_id=1, source_target_pairs={{0,6},{1,7},{2,4},{3,5},{4,2},{5,3},{6,0},{7,1},{8,14},{9,15},{10,... | collective-permute-start | bytes 393224 | tf_op jit(solution)/shard_map/ppermute | solution.py:297
  12.4 0.4 %collective-permute-start.3 = (bf16[8,8192]{1,0:T(8,128)(2,1)S(1)}, bf16[8,8192]{1,0:T(8,128)(2,1)S(1)}, u32[]{:S(2)}, u32[]{:S(2)}) collective-permute-start(bf16[8,8192]{1,0:T(8,128)(2,1)S(1)} %get-tuple-element.13.refs_0_), channel_id=1, source_target_pairs={{0,4},{1,5},{2,6},{3,7},{4,0},{5,1},{6,2},{7,3},{8,12},{9,13},{10,... | collective-permute-start | bytes 393224 | tf_op jit(solution)/shard_map/ppermute | solution.py:297
  12.9 0.5 %collective-permute-start.1 = (bf16[8,8192]{1,0:T(8,128)(2,1)S(1)}, bf16[8,8192]{1,0:T(8,128)(2,1)S(1)}, u32[]{:S(2)}, u32[]{:S(2)}) collective-permute-start(bf16[8,8192]{1,0:T(8,128)(2,1)S(1)} %get-tuple-element.13.refs_0_), channel_id=1, source_target_pairs={{0,2},{1,3},{2,0},{3,1},{4,6},{5,7},{6,4},{7,5},{8,10},{9,11},{10,... | collective-permute-start | bytes 393224 | tf_op jit(solution)/shard_map/ppermute | solution.py:297
  13.4 0.0 collective-permute-start
  13.4 2.9 %collective-permute-done.7.refs_8_ = bf16[8,8192]{1,0:T(8,128)(2,1)S(1)} collective-permute-done((bf16[8,8192]{1,0:T(8,128)(2,1)S(1)}, bf16[8,8192]{1,0:T(8,128)(2,1)S(1)}, u32[]{:S(2)}, u32[]{:S(2)}) %collective-permute-start.7) | collective-permute-done | bytes 131104 | tf_op jit(solution)/shard_map/ppermute | solution.py:297
  16.3 1.6 %collective-permute-start.13 = (bf16[8,8192]{1,0:T(8,128)(2,1)S(1)}, bf16[8,8192]{1,0:T(8,128)(2,1)S(1)}, u32[]{:S(2)}, u32[]{:S(2)}) collective-permute-start(bf16[8,8192]{1,0:T(8,128)(2,1)S(1)} %collective-permute-done.7.refs_8_), channel_id=1, source_target_pairs={{0,6},{1,7},{2,4},{3,5},{4,2},{5,3},{6,0},{7,1},{8,14},{9,15},{10,... | collective-permute-start | bytes 393224 | tf_op jit(solution)/shard_map/ppermute | solution.py:297
  17.9 0.9 %collective-permute-done.5.refs_6_ = bf16[8,8192]{1,0:T(8,128)(2,1)S(1)} collective-permute-done((bf16[8,8192]{1,0:T(8,128)(2,1)S(1)}, bf16[8,8192]{1,0:T(8,128)(2,1)S(1)}, u32[]{:S(2)}, u32[]{:S(2)}) %collective-permute-start.5) | collective-permute-done | bytes 131104 | tf_op jit(solution)/shard_map/ppermute | solution.py:297
  18.9 1.2 %collective-permute-start.11 = (bf16[8,8192]{1,0:T(8,128)(2,1)S(1)}, bf16[8,8192]{1,0:T(8,128)(2,1)S(1)}, u32[]{:S(2)}, u32[]{:S(2)}) collective-permute-start(bf16[8,8192]{1,0:T(8,128)(2,1)S(1)} %collective-permute-done.7.refs_8_), channel_id=1, source_target_pairs={{0,4},{1,5},{2,6},{3,7},{4,0},{5,1},{6,2},{7,3},{8,12},{9,13},{10,... | collective-permute-start | bytes 393224 | tf_op jit(solution)/shard_map/ppermute | solution.py:297
  20.1 1.2 %collective-permute-done.3.refs_4_ = bf16[8,8192]{1,0:T(8,128)(2,1)S(1)} collective-permute-done((bf16[8,8192]{1,0:T(8,128)(2,1)S(1)}, bf16[8,8192]{1,0:T(8,128)(2,1)S(1)}, u32[]{:S(2)}, u32[]{:S(2)}) %collective-permute-start.3) | collective-permute-done | bytes 131104 | tf_op jit(solution)/shard_map/ppermute | solution.py:297
  21.3 0.9 %collective-permute-start.9 = (bf16[8,8192]{1,0:T(8,128)(2,1)S(1)}, bf16[8,8192]{1,0:T(8,128)(2,1)S(1)}, u32[]{:S(2)}, u32[]{:S(2)}) collective-permute-start(bf16[8,8192]{1,0:T(8,128)(2,1)S(1)} %collective-permute-done.7.refs_8_), channel_id=1, source_target_pairs={{0,2},{1,3},{2,0},{3,1},{4,6},{5,7},{6,4},{7,5},{8,10},{9,11},{10,... | collective-permute-start | bytes 393224 | tf_op jit(solution)/shard_map/ppermute | solution.py:297
  22.2 0.5 %collective-permute-start.6 = (bf16[8,8192]{1,0:T(8,128)(2,1)S(1)}, bf16[8,8192]{1,0:T(8,128)(2,1)S(1)}, u32[]{:S(2)}, u32[]{:S(2)}) collective-permute-start(bf16[8,8192]{1,0:T(8,128)(2,1)S(1)} %collective-permute-done.5.refs_6_), channel_id=1, source_target_pairs={{0,1},{1,0},{2,3},{3,2},{4,5},{5,4},{6,7},{7,6},{8,9},{9,8},{10,11... | collective-permute-start | bytes 393224 | tf_op jit(solution)/shard_map/ppermute | solution.py:297
  22.8 1.7 %collective-permute-done.13.refs_14_ = bf16[8,8192]{1,0:T(8,128)(2,1)S(1)} collective-permute-done((bf16[8,8192]{1,0:T(8,128)(2,1)S(1)}, bf16[8,8192]{1,0:T(8,128)(2,1)S(1)}, u32[]{:S(2)}, u32[]{:S(2)}) %collective-permute-start.13) | collective-permute-done | bytes 131104 | tf_op jit(solution)/shard_map/ppermute | solution.py:297
  24.5 1.4 %collective-permute-done.11.refs_12_ = bf16[8,8192]{1,0:T(8,128)(2,1)S(1)} collective-permute-done((bf16[8,8192]{1,0:T(8,128)(2,1)S(1)}, bf16[8,8192]{1,0:T(8,128)(2,1)S(1)}, u32[]{:S(2)}, u32[]{:S(2)}) %collective-permute-start.11) | collective-permute-done | bytes 131104 | tf_op jit(solution)/shard_map/ppermute | solution.py:297
  25.9 0.0 collective-permute-start.2
  25.9 0.4 collective-permute-done.9.refs_10_
  26.3 0.2 collective-permute-start.14
  26.4 0.0 collective-permute-done.8.refs_9_
  26.4 0.4 collective-permute-start.12
  26.8 0.0 collective-permute-done.6.refs_7_
  26.8 0.2 collective-permute-start.10
  26.9 0.3 collective-permute-done.2.refs_3_
  27.2 0.4 collective-permute-done.14.refs_15_
  27.6 0.2 collective-permute-done.12.refs_13_
  27.8 0.3 collective-permute-done.10.refs_11_
  28.1 2.2 %delta.1 = (bf16[16,16,512]{2,1,0:T(8,128)(2,1)}, bf16[128,8192]{1,0:T(8,128)(2,1)S(1)}) custom-call(bf16[8,8192]{1,0:T(8,128)(2,1)S(1)} %get-tuple-element.13.refs_0_, bf16[8,8192]{1,0:T(8,128)(2,1)S(1)} %collective-permute-done.refs_1_, bf16[8,8192]{1,0:T(8,128)(2,1)S(1)} %collective-permute-done.1.refs_2_, ...), custom_call_target="tpu_custom_call" | custom-call | flops 301989888 | bytes 8650752 | tf_op jit(solution)/shard_map/delta/pallas_call | solution.py:344
  30.3 5.4 %all-to-all-start = ((bf16[16,16,512]{2,1,0:T(8,128)(2,1)}), bf16[16,16,512]{2,1,0:T(8,128)(2,1)S(1)}, u32[]{:S(2)}, u32[]{:S(2)}) async-start(bf16[16,16,512]{2,1,0:T(8,128)(2,1)} %get-tuple-element.20), calls=%async_computation | async-start | bytes 524288 | tf_op jit(solution)/shard_map/all_to_all | solution.py:445
  35.8 3.4 %copy-done = bf16[8192,512]{1,0:T(8,128)(2,1)S(1)} copy-done((bf16[8192,512]{1,0:T(8,128)(2,1)S(1)}, bf16[8192,512]{1,0:T(8,128)(2,1)}, u32[]{:S(2)}) %copy-start) | copy-done | bytes 8388632
  39.1 2.4 %base.1.base_ref = f32[128,512]{1,0:T(8,128)S(1)} custom-call(bf16[128,8192]{1,0:T(8,128)(2,1)S(1)} %get-tuple-element.17.a_ref, bf16[8192,512]{1,0:T(8,128)(2,1)S(1)} %copy-done, bf16[128,128]{1,0:T(8,128)(2,1)S(1)} %get-tuple-element.18.order_ref), custom_call_target="tpu_custom_call" | custom-call | flops 1342177280 | bytes 10747904 | tf_op jit(solution)/shard_map/base/pallas_call | solution.py:376
  41.6 0.8 %all-to-all-done.delta_ref = bf16[16,16,512]{2,1,0:T(8,128)(2,1)S(1)} async-done(((bf16[16,16,512]{2,1,0:T(8,128)(2,1)}), bf16[16,16,512]{2,1,0:T(8,128)(2,1)S(1)}, u32[]{:S(2)}, u32[]{:S(2)}) %all-to-all-start) | async-done | bytes 262176 | tf_op jit(solution)/shard_map/all_to_all | solution.py:445
  42.3 0.8 %join.1 = bf16[2,64,512]{2,1,0:T(8,128)(2,1)} custom-call(f32[128,512]{1,0:T(8,128)S(1)} %base.1.base_ref, bf16[128,256]{1,0:T(8,128)(2,1)S(1)} %get-tuple-element.19.place_ref, bf16[16,16,512]{2,1,0:T(8,128)(2,1)S(1)} %all-to-all-done.delta_ref), custom_call_target="tpu_custom_call" | custom-call | tf_op jit(solution)/shard_map/join/pallas_call | solution.py:403
  (6 shorter events, 0.0 us)
Async XLA Ops:
  5.8 10.5 %collective-permute-start.7 = (bf16[8,8192]{1,0:T(8,128)(2,1)S(1)}, bf16[8,8192]{1,0:T(8,128)(2,1)S(1)}, u32[]{:S(2)}, u32[]{:S(2)}) collective-permute-start(bf16[8,8192]{1,0:T(8,128)(2,1)S(1)} %get-tuple-element.13.refs_0_), channel_id=1, source_target_pairs={{0,8},{1,9},{2,10},{3,11},{4,12},{5,13},{6,14},{7,15},{8,0},{9,1},... | collective-permute-start | bytes 393224 | tf_op jit(solution)/shard_map/ppermute | solution.py:297
  9.9 9.0 %collective-permute-start.5 = (bf16[8,8192]{1,0:T(8,128)(2,1)S(1)}, bf16[8,8192]{1,0:T(8,128)(2,1)S(1)}, u32[]{:S(2)}, u32[]{:S(2)}) collective-permute-start(bf16[8,8192]{1,0:T(8,128)(2,1)S(1)} %get-tuple-element.13.refs_0_), channel_id=1, source_target_pairs={{0,6},{1,7},{2,4},{3,5},{4,2},{5,3},{6,0},{7,1},{8,14},{9,15},{10,... | collective-permute-start | bytes 393224 | tf_op jit(solution)/shard_map/ppermute | solution.py:297
  12.4 8.8 %collective-permute-start.3 = (bf16[8,8192]{1,0:T(8,128)(2,1)S(1)}, bf16[8,8192]{1,0:T(8,128)(2,1)S(1)}, u32[]{:S(2)}, u32[]{:S(2)}) collective-permute-start(bf16[8,8192]{1,0:T(8,128)(2,1)S(1)} %get-tuple-element.13.refs_0_), channel_id=1, source_target_pairs={{0,4},{1,5},{2,6},{3,7},{4,0},{5,1},{6,2},{7,3},{8,12},{9,13},{10,... | collective-permute-start | bytes 393224 | tf_op jit(solution)/shard_map/ppermute | solution.py:297
  12.9 9.3 %collective-permute-start.1 = (bf16[8,8192]{1,0:T(8,128)(2,1)S(1)}, bf16[8,8192]{1,0:T(8,128)(2,1)S(1)}, u32[]{:S(2)}, u32[]{:S(2)}) collective-permute-start(bf16[8,8192]{1,0:T(8,128)(2,1)S(1)} %get-tuple-element.13.refs_0_), channel_id=1, source_target_pairs={{0,2},{1,3},{2,0},{3,1},{4,6},{5,7},{6,4},{7,5},{8,10},{9,11},{10,... | collective-permute-start | bytes 393224 | tf_op jit(solution)/shard_map/ppermute | solution.py:297
  13.4 8.8 %collective-permute-start = (bf16[8,8192]{1,0:T(8,128)(2,1)S(1)}, bf16[8,8192]{1,0:T(8,128)(2,1)S(1)}, u32[]{:S(2)}, u32[]{:S(2)}) collective-permute-start(bf16[8,8192]{1,0:T(8,128)(2,1)S(1)} %get-tuple-element.13.refs_0_), channel_id=1, source_target_pairs={{0,1},{1,0},{2,3},{3,2},{4,5},{5,4},{6,7},{7,6},{8,9},{9,8},{10,11... | collective-permute-start | bytes 393224 | tf_op jit(solution)/shard_map/ppermute | solution.py:297
  16.3 8.2 %collective-permute-start.13 = (bf16[8,8192]{1,0:T(8,128)(2,1)S(1)}, bf16[8,8192]{1,0:T(8,128)(2,1)S(1)}, u32[]{:S(2)}, u32[]{:S(2)}) collective-permute-start(bf16[8,8192]{1,0:T(8,128)(2,1)S(1)} %collective-permute-done.7.refs_8_), channel_id=1, source_target_pairs={{0,6},{1,7},{2,4},{3,5},{4,2},{5,3},{6,0},{7,1},{8,14},{9,15},{10,... | collective-permute-start | bytes 393224 | tf_op jit(solution)/shard_map/ppermute | solution.py:297
  18.9 7.0 %collective-permute-start.11 = (bf16[8,8192]{1,0:T(8,128)(2,1)S(1)}, bf16[8,8192]{1,0:T(8,128)(2,1)S(1)}, u32[]{:S(2)}, u32[]{:S(2)}) collective-permute-start(bf16[8,8192]{1,0:T(8,128)(2,1)S(1)} %collective-permute-done.7.refs_8_), channel_id=1, source_target_pairs={{0,4},{1,5},{2,6},{3,7},{4,0},{5,1},{6,2},{7,3},{8,12},{9,13},{10,... | collective-permute-start | bytes 393224 | tf_op jit(solution)/shard_map/ppermute | solution.py:297
  21.3 5.0 %collective-permute-start.9 = (bf16[8,8192]{1,0:T(8,128)(2,1)S(1)}, bf16[8,8192]{1,0:T(8,128)(2,1)S(1)}, u32[]{:S(2)}, u32[]{:S(2)}) collective-permute-start(bf16[8,8192]{1,0:T(8,128)(2,1)S(1)} %collective-permute-done.7.refs_8_), channel_id=1, source_target_pairs={{0,2},{1,3},{2,0},{3,1},{4,6},{5,7},{6,4},{7,5},{8,10},{9,11},{10,... | collective-permute-start | bytes 393224 | tf_op jit(solution)/shard_map/ppermute | solution.py:297
  22.2 4.2 %collective-permute-start.8 = (bf16[8,8192]{1,0:T(8,128)(2,1)S(1)}, bf16[8,8192]{1,0:T(8,128)(2,1)S(1)}, u32[]{:S(2)}, u32[]{:S(2)}) collective-permute-start(bf16[8,8192]{1,0:T(8,128)(2,1)S(1)} %collective-permute-done.7.refs_8_), channel_id=1, source_target_pairs={{0,1},{1,0},{2,3},{3,2},{4,5},{5,4},{6,7},{7,6},{8,9},{9,8},{10,11... | collective-permute-start | bytes 393224 | tf_op jit(solution)/shard_map/ppermute | solution.py:297
  22.2 4.5 %collective-permute-start.6 = (bf16[8,8192]{1,0:T(8,128)(2,1)S(1)}, bf16[8,8192]{1,0:T(8,128)(2,1)S(1)}, u32[]{:S(2)}, u32[]{:S(2)}) collective-permute-start(bf16[8,8192]{1,0:T(8,128)(2,1)S(1)} %collective-permute-done.5.refs_6_), channel_id=1, source_target_pairs={{0,1},{1,0},{2,3},{3,2},{4,5},{5,4},{6,7},{7,6},{8,9},{9,8},{10,11... | collective-permute-start | bytes 393224 | tf_op jit(solution)/shard_map/ppermute | solution.py:297
  24.5 2.5 %collective-permute-start.4 = (bf16[8,8192]{1,0:T(8,128)(2,1)S(1)}, bf16[8,8192]{1,0:T(8,128)(2,1)S(1)}, u32[]{:S(2)}, u32[]{:S(2)}) collective-permute-start(bf16[8,8192]{1,0:T(8,128)(2,1)S(1)} %collective-permute-done.3.refs_4_), channel_id=1, source_target_pairs={{0,1},{1,0},{2,3},{3,2},{4,5},{5,4},{6,7},{7,6},{8,9},{9,8},{10,11... | collective-permute-start | bytes 393224 | tf_op jit(solution)/shard_map/ppermute | solution.py:297
  25.9 1.3 %collective-permute-start.2 = (bf16[8,8192]{1,0:T(8,128)(2,1)S(1)}, bf16[8,8192]{1,0:T(8,128)(2,1)S(1)}, u32[]{:S(2)}, u32[]{:S(2)}) collective-permute-start(bf16[8,8192]{1,0:T(8,128)(2,1)S(1)} %collective-permute-done.1.refs_2_), channel_id=1, source_target_pairs={{0,1},{1,0},{2,3},{3,2},{4,5},{5,4},{6,7},{7,6},{8,9},{9,8},{10,11... | collective-permute-start | bytes 393224 | tf_op jit(solution)/shard_map/ppermute | solution.py:297
  26.3 1.3 %collective-permute-start.14 = (bf16[8,8192]{1,0:T(8,128)(2,1)S(1)}, bf16[8,8192]{1,0:T(8,128)(2,1)S(1)}, u32[]{:S(2)}, u32[]{:S(2)}) collective-permute-start(bf16[8,8192]{1,0:T(8,128)(2,1)S(1)} %collective-permute-done.13.refs_14_), channel_id=1, source_target_pairs={{0,1},{1,0},{2,3},{3,2},{4,5},{5,4},{6,7},{7,6},{8,9},{9,8},{10,11... | collective-permute-start | bytes 393224 | tf_op jit(solution)/shard_map/ppermute | solution.py:297
  26.4 1.4 %collective-permute-start.12 = (bf16[8,8192]{1,0:T(8,128)(2,1)S(1)}, bf16[8,8192]{1,0:T(8,128)(2,1)S(1)}, u32[]{:S(2)}, u32[]{:S(2)}) collective-permute-start(bf16[8,8192]{1,0:T(8,128)(2,1)S(1)} %collective-permute-done.11.refs_12_), channel_id=1, source_target_pairs={{0,1},{1,0},{2,3},{3,2},{4,5},{5,4},{6,7},{7,6},{8,9},{9,8},{10,11... | collective-permute-start | bytes 393224 | tf_op jit(solution)/shard_map/ppermute | solution.py:297
  26.8 1.3 %collective-permute-start.10 = (bf16[8,8192]{1,0:T(8,128)(2,1)S(1)}, bf16[8,8192]{1,0:T(8,128)(2,1)S(1)}, u32[]{:S(2)}, u32[]{:S(2)}) collective-permute-start(bf16[8,8192]{1,0:T(8,128)(2,1)S(1)} %collective-permute-done.9.refs_10_), channel_id=1, source_target_pairs={{0,1},{1,0},{2,3},{3,2},{4,5},{5,4},{6,7},{7,6},{8,9},{9,8},{10,11... | collective-permute-start | bytes 393224 | tf_op jit(solution)/shard_map/ppermute | solution.py:297
  30.3 12.0 %all-to-all-start = ((bf16[16,16,512]{2,1,0:T(8,128)(2,1)}), bf16[16,16,512]{2,1,0:T(8,128)(2,1)S(1)}, u32[]{:S(2)}, u32[]{:S(2)}) async-start(bf16[16,16,512]{2,1,0:T(8,128)(2,1)} %get-tuple-element.20), calls=%async_computation | async-start | bytes 524288 | tf_op jit(solution)/shard_map/all_to_all | solution.py:445
  35.8 3.4 %copy-start = (bf16[8192,512]{1,0:T(8,128)(2,1)S(1)}, bf16[8192,512]{1,0:T(8,128)(2,1)}, u32[]{:S(2)}) copy-start(bf16[8192,512]{1,0:T(8,128)(2,1)} %w_ref.1) | copy-start | bytes 25165828

commit v19 on v18

--- a/solution.py
+++ b/solution.py
@@ -15,7 +15,7 @@
 MOST = 8
 RING = 16
 ORDER = [0, 1, 2, 3, 4, 5, 6, 7, 8, 9, 10, 11, 12, 13, 14, 15]
-EXCHANGE = [11, 10, 9, 8, 15, 14, 13, 12, 7, 6, 5, 4, 3, 2, 1, 0]
+EXCHANGE = [8, 9, 10, 11, 12, 13, 14, 15, 4, 5, 6, 7, 0, 1, 2, 3]
 F32 = jnp.float32
 BF16 = jnp.bfloat16
 NT = (((1,), (1,)), ((), ()))
@@ -359,13 +359,20 @@
     )(*[blocks[i] for i in at_slot], pick, down, up)
 
 
-def base_kernel(a_ref, w_ref, order_ref, out_ref):
+def base_kernel(a_ref, order_ref, w_hbm, out_ref, w_ref, sems):
     width = a_ref.shape[1]
-    cuts = 8
+    cuts = sems.shape[0]
     deep = width // cuts
+    copies = []
+    for i in range(cuts):
+        at = pl.ds(i * deep, deep)
+        copies.append(pltpu.make_async_copy(w_hbm.at[at], w_ref.at[at], sems.at[i]))
+        copies[-1].start()
     for i in range(cuts):
         at = slice(i * deep, (i + 1) * deep)
-        part = dot(dot(order_ref[...], a_ref[:, at]).astype(BF16), w_ref[at, :])
+        rows = dot(order_ref[...], a_ref[:, at]).astype(BF16)
+        copies[i].wait()
+        part = dot(rows, w_ref[at, :])
         out_ref[...] = part if i == 0 else out_ref[...] + part
 
 
@@ -376,8 +383,9 @@
     return pl.pallas_call(
         base_kernel,
         out_shape=jax.ShapeDtypeStruct((total, cols), F32),
-        in_specs=[vmem] * 3,
+        in_specs=[vmem] * 2 + [pl.BlockSpec(memory_space=pl.ANY)],
         out_specs=vmem,
+        scratch_shapes=[pltpu.VMEM(out_weight.shape, BF16), pltpu.SemaphoreType.DMA((8,))],
         compiler_params=pltpu.CompilerParams(vmem_limit_bytes=24 * 2**20),
         cost_estimate=pl.CostEstimate(
             flops=2 * total * width * (cols + total),
@@ -385,7 +393,7 @@
             transcendentals=0,
         ),
         name="base",
-    )(gathered, out_weight, order)
+    )(gathered, order, *in_hbm(out_weight))
 
 
 def join_kernel(base_ref, place_ref, delta_ref, out_ref):

time: 43.5 us -> 44.4 us (1.021)
  local copies, waits for them, and re-layouts: 3.38 us -> 0 us
  waiting for transfers between devices: 10.5 us -> 12.7 us
  Pallas kernels: 11.3 us -> 13.1 us
    unnamed x2 -> x0, local copies, waits for them, and re-layouts: 3.38 us -> none
    all_to_all x1, waiting for transfers between devices: 0.77 us -> 2.98 us  [per_device(): lax.all_to_all(send, 'tensor', 0, 0, axis_index_groups=groups, tiled=True)]
    pallas_call x1, Pallas kernels: 2.42 us -> 4.25 us  [base_part(): pl.pallas_call(base_kernel, out_shape=jax.ShapeDtypeStruct((total, cols),...]
  transfers between devices with their start and end apart: 16 -> 16, of which waited for: 11 -> 11; matrix products, arithmetic and copies ran while one was open for 0% -> 0% of each run, Pallas kernels for 6% -> 10%
where the time goes in v19:
time: 44.4 us; the launch traced here: 43.9 us
  starting transfers between devices  18 us (41%)
  Pallas kernels  13.1 us (30%)
  waiting for transfers between devices  12.7 us (29%)
    ppermute x15, starting transfers between devices, swap(): return lax.ppermute(x, 'tensor', [(i, i ^ bits) for i in range(parts)])  12.5 us
    ppermute x15, waiting for transfers between devices, swap(): return lax.ppermute(x, 'tensor', [(i, i ^ bits) for i in range(parts)])  9.76 us
    pallas_call x1, Pallas kernels, attend(): pl.pallas_call(attend_kernel, out_shape=[jax.ShapeDtypeStruct(shape, BF16...  5.8 us
    all_to_all x1, starting transfers between devices, per_device(): lax.all_to_all(send, 'tensor', 0, 0, axis_index_groups=groups, tiled=True)  5.48 us
    pallas_call x1, Pallas kernels, base_part(): pl.pallas_call(base_kernel, out_shape=jax.ShapeDtypeStruct((total, cols),...  4.25 us
    all_to_all x1, waiting for transfers between devices, per_device(): lax.all_to_all(send, 'tensor', 0, 0, axis_index_groups=groups, tiled=True)  2.98 us
    pallas_call x1, Pallas kernels, deltas(): pl.pallas_call(functools.partial(delta_kernel, at_slot), out_shape=(jax.S...  2.22 us
  transfers between devices with their start and end apart: 16, of which 11 were waited for; matrix products, arithmetic and copies ran while one was open for 0% of the time, Pallas kernels for 10%

profile of v19, /device:TPU:0, one launch (start us, length us, event | category | flops | bytes accessed | tf_op | source)
XLA Modules:
  0.0 43.9 jit_solution(18010162855019732392)
XLA Ops:
  0.0 5.8 %attend.1 = (bf16[8,8192]{1,0:T(8,128)(2,1)S(1)}, bf16[8192,128]{1,0:T(8,128)(2,1)S(1)}, bf16[8192,128]{1,0:T(8,128)(2,1)S(1)}, bf16[16,128]{1,0:T(8,128)(2,1)S(...) custom-call(s32[4]{0:T(128)} %len_hbm.1, bf16[2,4,8192]{2,1,0:T(4,128)(2,1)} %q_hbm.1, ...), custom_call_target="tpu_custom_call" | custom-call | flops 134217728 | bytes 8388608 | tf_op jit(solution)/shard_map/attend/pallas_call | solution.py:252
  5.8 4.1 %collective-permute-start.7 = (bf16[8,8192]{1,0:T(8,128)(2,1)S(1)}, bf16[8,8192]{1,0:T(8,128)(2,1)S(1)}, u32[]{:S(2)}, u32[]{:S(2)}) collective-permute-start(bf16[8,8192]{1,0:T(8,128)(2,1)S(1)} %get-tuple-element.13.refs_0_), channel_id=1, source_target_pairs={{0,8},{1,9},{2,10},{3,11},{4,12},{5,13},{6,14},{7,15},{8,0},{9,1},... | collective-permute-start | bytes 393224 | tf_op jit(solution)/shard_map/ppermute | solution.py:297
  9.9 2.5 %collective-permute-start.5 = (bf16[8,8192]{1,0:T(8,128)(2,1)S(1)}, bf16[8,8192]{1,0:T(8,128)(2,1)S(1)}, u32[]{:S(2)}, u32[]{:S(2)}) collective-permute-start(bf16[8,8192]{1,0:T(8,128)(2,1)S(1)} %get-tuple-element.13.refs_0_), channel_id=1, source_target_pairs={{0,6},{1,7},{2,4},{3,5},{4,2},{5,3},{6,0},{7,1},{8,14},{9,15},{10,... | collective-permute-start | bytes 393224 | tf_op jit(solution)/shard_map/ppermute | solution.py:297
  12.4 0.4 %collective-permute-start.3 = (bf16[8,8192]{1,0:T(8,128)(2,1)S(1)}, bf16[8,8192]{1,0:T(8,128)(2,1)S(1)}, u32[]{:S(2)}, u32[]{:S(2)}) collective-permute-start(bf16[8,8192]{1,0:T(8,128)(2,1)S(1)} %get-tuple-element.13.refs_0_), channel_id=1, source_target_pairs={{0,4},{1,5},{2,6},{3,7},{4,0},{5,1},{6,2},{7,3},{8,12},{9,13},{10,... | collective-permute-start | bytes 393224 | tf_op jit(solution)/shard_map/ppermute | solution.py:297
  12.9 0.5 %collective-permute-start.1 = (bf16[8,8192]{1,0:T(8,128)(2,1)S(1)}, bf16[8,8192]{1,0:T(8,128)(2,1)S(1)}, u32[]{:S(2)}, u32[]{:S(2)}) collective-permute-start(bf16[8,8192]{1,0:T(8,128)(2,1)S(1)} %get-tuple-element.13.refs_0_), channel_id=1, source_target_pairs={{0,2},{1,3},{2,0},{3,1},{4,6},{5,7},{6,4},{7,5},{8,10},{9,11},{10,... | collective-permute-start | bytes 393224 | tf_op jit(solution)/shard_map/ppermute | solution.py:297
  13.4 2.9 %collective-permute-done.7.refs_8_ = bf16[8,8192]{1,0:T(8,128)(2,1)S(1)} collective-permute-done((bf16[8,8192]{1,0:T(8,128)(2,1)S(1)}, bf16[8,8192]{1,0:T(8,128)(2,1)S(1)}, u32[]{:S(2)}, u32[]{:S(2)}) %collective-permute-start.7) | collective-permute-done | bytes 131104 | tf_op jit(solution)/shard_map/ppermute | solution.py:297
  16.3 1.6 %collective-permute-start.13 = (bf16[8,8192]{1,0:T(8,128)(2,1)S(1)}, bf16[8,8192]{1,0:T(8,128)(2,1)S(1)}, u32[]{:S(2)}, u32[]{:S(2)}) collective-permute-start(bf16[8,8192]{1,0:T(8,128)(2,1)S(1)} %collective-permute-done.7.refs_8_), channel_id=1, source_target_pairs={{0,6},{1,7},{2,4},{3,5},{4,2},{5,3},{6,0},{7,1},{8,14},{9,15},{10,... | collective-permute-start | bytes 393224 | tf_op jit(solution)/shard_map/ppermute | solution.py:297
  17.9 0.9 %collective-permute-done.5.refs_6_ = bf16[8,8192]{1,0:T(8,128)(2,1)S(1)} collective-permute-done((bf16[8,8192]{1,0:T(8,128)(2,1)S(1)}, bf16[8,8192]{1,0:T(8,128)(2,1)S(1)}, u32[]{:S(2)}, u32[]{:S(2)}) %collective-permute-start.5) | collective-permute-done | bytes 131104 | tf_op jit(solution)/shard_map/ppermute | solution.py:297
  18.9 1.2 %collective-permute-start.11 = (bf16[8,8192]{1,0:T(8,128)(2,1)S(1)}, bf16[8,8192]{1,0:T(8,128)(2,1)S(1)}, u32[]{:S(2)}, u32[]{:S(2)}) collective-permute-start(bf16[8,8192]{1,0:T(8,128)(2,1)S(1)} %collective-permute-done.7.refs_8_), channel_id=1, source_target_pairs={{0,4},{1,5},{2,6},{3,7},{4,0},{5,1},{6,2},{7,3},{8,12},{9,13},{10,... | collective-permute-start | bytes 393224 | tf_op jit(solution)/shard_map/ppermute | solution.py:297
  20.1 1.2 %collective-permute-done.3.refs_4_ = bf16[8,8192]{1,0:T(8,128)(2,1)S(1)} collective-permute-done((bf16[8,8192]{1,0:T(8,128)(2,1)S(1)}, bf16[8,8192]{1,0:T(8,128)(2,1)S(1)}, u32[]{:S(2)}, u32[]{:S(2)}) %collective-permute-start.3) | collective-permute-done | bytes 131104 | tf_op jit(solution)/shard_map/ppermute | solution.py:297
  21.3 0.9 %collective-permute-start.9 = (bf16[8,8192]{1,0:T(8,128)(2,1)S(1)}, bf16[8,8192]{1,0:T(8,128)(2,1)S(1)}, u32[]{:S(2)}, u32[]{:S(2)}) collective-permute-start(bf16[8,8192]{1,0:T(8,128)(2,1)S(1)} %collective-permute-done.7.refs_8_), channel_id=1, source_target_pairs={{0,2},{1,3},{2,0},{3,1},{4,6},{5,7},{6,4},{7,5},{8,10},{9,11},{10,... | collective-permute-start | bytes 393224 | tf_op jit(solution)/shard_map/ppermute | solution.py:297
  22.2 0.0 collective-permute-done.1.refs_2_
  22.2 0.0 collective-permute-start.8
  22.2 0.0 collective-permute-done.refs_1_
  22.2 0.5 %collective-permute-start.6 = (bf16[8,8192]{1,0:T(8,128)(2,1)S(1)}, bf16[8,8192]{1,0:T(8,128)(2,1)S(1)}, u32[]{:S(2)}, u32[]{:S(2)}) collective-permute-start(bf16[8,8192]{1,0:T(8,128)(2,1)S(1)} %collective-permute-done.5.refs_6_), channel_id=1, source_target_pairs={{0,1},{1,0},{2,3},{3,2},{4,5},{5,4},{6,7},{7,6},{8,9},{9,8},{10,11... | collective-permute-start | bytes 393224 | tf_op jit(solution)/shard_map/ppermute | solution.py:297
  22.8 1.7 %collective-permute-done.13.refs_14_ = bf16[8,8192]{1,0:T(8,128)(2,1)S(1)} collective-permute-done((bf16[8,8192]{1,0:T(8,128)(2,1)S(1)}, bf16[8,8192]{1,0:T(8,128)(2,1)S(1)}, u32[]{:S(2)}, u32[]{:S(2)}) %collective-permute-start.13) | collective-permute-done | bytes 131104 | tf_op jit(solution)/shard_map/ppermute | solution.py:297
  24.5 0.0 collective-permute-start.4
  24.5 1.4 %collective-permute-done.11.refs_12_ = bf16[8,8192]{1,0:T(8,128)(2,1)S(1)} collective-permute-done((bf16[8,8192]{1,0:T(8,128)(2,1)S(1)}, bf16[8,8192]{1,0:T(8,128)(2,1)S(1)}, u32[]{:S(2)}, u32[]{:S(2)}) %collective-permute-start.11) | collective-permute-done | bytes 131104 | tf_op jit(solution)/shard_map/ppermute | solution.py:297
  25.9 0.0 collective-permute-start.2
  25.9 0.4 collective-permute-done.9.refs_10_
  26.3 0.2 collective-permute-start.14
  26.4 0.4 collective-permute-start.12
  26.8 0.2 collective-permute-start.10
  26.9 0.3 collective-permute-done.2.refs_3_
  27.2 0.4 collective-permute-done.14.refs_15_
  27.6 0.2 collective-permute-done.12.refs_13_
  27.8 0.3 collective-permute-done.10.refs_11_
  28.1 2.2 %delta.1 = (bf16[16,16,512]{2,1,0:T(8,128)(2,1)}, bf16[128,8192]{1,0:T(8,128)(2,1)S(1)}) custom-call(bf16[8,8192]{1,0:T(8,128)(2,1)S(1)} %get-tuple-element.13.refs_0_, bf16[8,8192]{1,0:T(8,128)(2,1)S(1)} %collective-permute-done.refs_1_, bf16[8,8192]{1,0:T(8,128)(2,1)S(1)} %collective-permute-done.1.refs_2_, ...), custom_call_target="tpu_custom_call" | custom-call | flops 301989888 | bytes 8650752 | tf_op jit(solution)/shard_map/delta/pallas_call | solution.py:344
  30.3 5.5 %all-to-all-start = ((bf16[16,16,512]{2,1,0:T(8,128)(2,1)}), bf16[16,16,512]{2,1,0:T(8,128)(2,1)S(1)}, u32[]{:S(2)}, u32[]{:S(2)}) async-start(bf16[16,16,512]{2,1,0:T(8,128)(2,1)} %get-tuple-element.20), calls=%async_computation | async-start | bytes 524288 | tf_op jit(solution)/shard_map/all_to_all | solution.py:453
  35.8 4.3 %base.1.base_ref = f32[128,512]{1,0:T(8,128)S(1)} custom-call(bf16[128,8192]{1,0:T(8,128)(2,1)S(1)} %get-tuple-element.17.a_ref, bf16[128,128]{1,0:T(8,128)(2,1)S(1)} %get-tuple-element.18.order_ref, bf16[8192,512]{1,0:T(8,128)(2,1)} %w_hbm.1), custom_call_target="tpu_custom_call" | custom-call | flops 1342177280 | bytes 10747904 | tf_op jit(solution)/shard_map/base/pallas_call | solution.py:383
  40.1 3.0 %all-to-all-done.delta_ref = bf16[16,16,512]{2,1,0:T(8,128)(2,1)S(1)} async-done(((bf16[16,16,512]{2,1,0:T(8,128)(2,1)}), bf16[16,16,512]{2,1,0:T(8,128)(2,1)S(1)}, u32[]{:S(2)}, u32[]{:S(2)}) %all-to-all-start) | async-done | bytes 262176 | tf_op jit(solution)/shard_map/all_to_all | solution.py:453
  43.1 0.8 %join.1 = bf16[2,64,512]{2,1,0:T(8,128)(2,1)} custom-call(f32[128,512]{1,0:T(8,128)S(1)} %base.1.base_ref, bf16[128,256]{1,0:T(8,128)(2,1)S(1)} %get-tuple-element.19.place_ref, bf16[16,16,512]{2,1,0:T(8,128)(2,1)S(1)} %all-to-all-done.delta_ref), custom_call_target="tpu_custom_call" | custom-call | tf_op jit(solution)/shard_map/join/pallas_call | solution.py:411
  (4 shorter events, 0.0 us)
Async XLA Ops:
  5.8 10.5 %collective-permute-start.7 = (bf16[8,8192]{1,0:T(8,128)(2,1)S(1)}, bf16[8,8192]{1,0:T(8,128)(2,1)S(1)}, u32[]{:S(2)}, u32[]{:S(2)}) collective-permute-start(bf16[8,8192]{1,0:T(8,128)(2,1)S(1)} %get-tuple-element.13.refs_0_), channel_id=1, source_target_pairs={{0,8},{1,9},{2,10},{3,11},{4,12},{5,13},{6,14},{7,15},{8,0},{9,1},... | collective-permute-start | bytes 393224 | tf_op jit(solution)/shard_map/ppermute | solution.py:297
  9.9 9.0 %collective-permute-start.5 = (bf16[8,8192]{1,0:T(8,128)(2,1)S(1)}, bf16[8,8192]{1,0:T(8,128)(2,1)S(1)}, u32[]{:S(2)}, u32[]{:S(2)}) collective-permute-start(bf16[8,8192]{1,0:T(8,128)(2,1)S(1)} %get-tuple-element.13.refs_0_), channel_id=1, source_target_pairs={{0,6},{1,7},{2,4},{3,5},{4,2},{5,3},{6,0},{7,1},{8,14},{9,15},{10,... | collective-permute-start | bytes 393224 | tf_op jit(solution)/shard_map/ppermute | solution.py:297
  12.4 8.8 %collective-permute-start.3 = (bf16[8,8192]{1,0:T(8,128)(2,1)S(1)}, bf16[8,8192]{1,0:T(8,128)(2,1)S(1)}, u32[]{:S(2)}, u32[]{:S(2)}) collective-permute-start(bf16[8,8192]{1,0:T(8,128)(2,1)S(1)} %get-tuple-element.13.refs_0_), channel_id=1, source_target_pairs={{0,4},{1,5},{2,6},{3,7},{4,0},{5,1},{6,2},{7,3},{8,12},{9,13},{10,... | collective-permute-start | bytes 393224 | tf_op jit(solution)/shard_map/ppermute | solution.py:297
  12.9 9.3 %collective-permute-start.1 = (bf16[8,8192]{1,0:T(8,128)(2,1)S(1)}, bf16[8,8192]{1,0:T(8,128)(2,1)S(1)}, u32[]{:S(2)}, u32[]{:S(2)}) collective-permute-start(bf16[8,8192]{1,0:T(8,128)(2,1)S(1)} %get-tuple-element.13.refs_0_), channel_id=1, source_target_pairs={{0,2},{1,3},{2,0},{3,1},{4,6},{5,7},{6,4},{7,5},{8,10},{9,11},{10,... | collective-permute-start | bytes 393224 | tf_op jit(solution)/shard_map/ppermute | solution.py:297
  13.4 8.8 %collective-permute-start = (bf16[8,8192]{1,0:T(8,128)(2,1)S(1)}, bf16[8,8192]{1,0:T(8,128)(2,1)S(1)}, u32[]{:S(2)}, u32[]{:S(2)}) collective-permute-start(bf16[8,8192]{1,0:T(8,128)(2,1)S(1)} %get-tuple-element.13.refs_0_), channel_id=1, source_target_pairs={{0,1},{1,0},{2,3},{3,2},{4,5},{5,4},{6,7},{7,6},{8,9},{9,8},{10,11... | collective-permute-start | bytes 393224 | tf_op jit(solution)/shard_map/ppermute | solution.py:297
  16.3 8.2 %collective-permute-start.13 = (bf16[8,8192]{1,0:T(8,128)(2,1)S(1)}, bf16[8,8192]{1,0:T(8,128)(2,1)S(1)}, u32[]{:S(2)}, u32[]{:S(2)}) collective-permute-start(bf16[8,8192]{1,0:T(8,128)(2,1)S(1)} %collective-permute-done.7.refs_8_), channel_id=1, source_target_pairs={{0,6},{1,7},{2,4},{3,5},{4,2},{5,3},{6,0},{7,1},{8,14},{9,15},{10,... | collective-permute-start | bytes 393224 | tf_op jit(solution)/shard_map/ppermute | solution.py:297
  18.9 7.0 %collective-permute-start.11 = (bf16[8,8192]{1,0:T(8,128)(2,1)S(1)}, bf16[8,8192]{1,0:T(8,128)(2,1)S(1)}, u32[]{:S(2)}, u32[]{:S(2)}) collective-permute-start(bf16[8,8192]{1,0:T(8,128)(2,1)S(1)} %collective-permute-done.7.refs_8_), channel_id=1, source_target_pairs={{0,4},{1,5},{2,6},{3,7},{4,0},{5,1},{6,2},{7,3},{8,12},{9,13},{10,... | collective-permute-start | bytes 393224 | tf_op jit(solution)/shard_map/ppermute | solution.py:297
  21.3 5.0 %collective-permute-start.9 = (bf16[8,8192]{1,0:T(8,128)(2,1)S(1)}, bf16[8,8192]{1,0:T(8,128)(2,1)S(1)}, u32[]{:S(2)}, u32[]{:S(2)}) collective-permute-start(bf16[8,8192]{1,0:T(8,128)(2,1)S(1)} %collective-permute-done.7.refs_8_), channel_id=1, source_target_pairs={{0,2},{1,3},{2,0},{3,1},{4,6},{5,7},{6,4},{7,5},{8,10},{9,11},{10,... | collective-permute-start | bytes 393224 | tf_op jit(solution)/shard_map/ppermute | solution.py:297
  22.2 4.2 %collective-permute-start.8 = (bf16[8,8192]{1,0:T(8,128)(2,1)S(1)}, bf16[8,8192]{1,0:T(8,128)(2,1)S(1)}, u32[]{:S(2)}, u32[]{:S(2)}) collective-permute-start(bf16[8,8192]{1,0:T(8,128)(2,1)S(1)} %collective-permute-done.7.refs_8_), channel_id=1, source_target_pairs={{0,1},{1,0},{2,3},{3,2},{4,5},{5,4},{6,7},{7,6},{8,9},{9,8},{10,11... | collective-permute-start | bytes 393224 | tf_op jit(solution)/shard_map/ppermute | solution.py:297
  22.2 4.5 %collective-permute-start.6 = (bf16[8,8192]{1,0:T(8,128)(2,1)S(1)}, bf16[8,8192]{1,0:T(8,128)(2,1)S(1)}, u32[]{:S(2)}, u32[]{:S(2)}) collective-permute-start(bf16[8,8192]{1,0:T(8,128)(2,1)S(1)} %collective-permute-done.5.refs_6_), channel_id=1, source_target_pairs={{0,1},{1,0},{2,3},{3,2},{4,5},{5,4},{6,7},{7,6},{8,9},{9,8},{10,11... | collective-permute-start | bytes 393224 | tf_op jit(solution)/shard_map/ppermute | solution.py:297
  24.5 2.5 %collective-permute-start.4 = (bf16[8,8192]{1,0:T(8,128)(2,1)S(1)}, bf16[8,8192]{1,0:T(8,128)(2,1)S(1)}, u32[]{:S(2)}, u32[]{:S(2)}) collective-permute-start(bf16[8,8192]{1,0:T(8,128)(2,1)S(1)} %collective-permute-done.3.refs_4_), channel_id=1, source_target_pairs={{0,1},{1,0},{2,3},{3,2},{4,5},{5,4},{6,7},{7,6},{8,9},{9,8},{10,11... | collective-permute-start | bytes 393224 | tf_op jit(solution)/shard_map/ppermute | solution.py:297
  25.9 1.3 %collective-permute-start.2 = (bf16[8,8192]{1,0:T(8,128)(2,1)S(1)}, bf16[8,8192]{1,0:T(8,128)(2,1)S(1)}, u32[]{:S(2)}, u32[]{:S(2)}) collective-permute-start(bf16[8,8192]{1,0:T(8,128)(2,1)S(1)} %collective-permute-done.1.refs_2_), channel_id=1, source_target_pairs={{0,1},{1,0},{2,3},{3,2},{4,5},{5,4},{6,7},{7,6},{8,9},{9,8},{10,11... | collective-permute-start | bytes 393224 | tf_op jit(solution)/shard_map/ppermute | solution.py:297
  26.3 1.3 %collective-permute-start.14 = (bf16[8,8192]{1,0:T(8,128)(2,1)S(1)}, bf16[8,8192]{1,0:T(8,128)(2,1)S(1)}, u32[]{:S(2)}, u32[]{:S(2)}) collective-permute-start(bf16[8,8192]{1,0:T(8,128)(2,1)S(1)} %collective-permute-done.13.refs_14_), channel_id=1, source_target_pairs={{0,1},{1,0},{2,3},{3,2},{4,5},{5,4},{6,7},{7,6},{8,9},{9,8},{10,11... | collective-permute-start | bytes 393224 | tf_op jit(solution)/shard_map/ppermute | solution.py:297
  26.4 1.4 %collective-permute-start.12 = (bf16[8,8192]{1,0:T(8,128)(2,1)S(1)}, bf16[8,8192]{1,0:T(8,128)(2,1)S(1)}, u32[]{:S(2)}, u32[]{:S(2)}) collective-permute-start(bf16[8,8192]{1,0:T(8,128)(2,1)S(1)} %collective-permute-done.11.refs_12_), channel_id=1, source_target_pairs={{0,1},{1,0},{2,3},{3,2},{4,5},{5,4},{6,7},{7,6},{8,9},{9,8},{10,11... | collective-permute-start | bytes 393224 | tf_op jit(solution)/shard_map/ppermute | solution.py:297
  26.8 1.3 %collective-permute-start.10 = (bf16[8,8192]{1,0:T(8,128)(2,1)S(1)}, bf16[8,8192]{1,0:T(8,128)(2,1)S(1)}, u32[]{:S(2)}, u32[]{:S(2)}) collective-permute-start(bf16[8,8192]{1,0:T(8,128)(2,1)S(1)} %collective-permute-done.9.refs_10_), channel_id=1, source_target_pairs={{0,1},{1,0},{2,3},{3,2},{4,5},{5,4},{6,7},{7,6},{8,9},{9,8},{10,11... | collective-permute-start | bytes 393224 | tf_op jit(solution)/shard_map/ppermute | solution.py:297
  30.3 12.7 %all-to-all-start = ((bf16[16,16,512]{2,1,0:T(8,128)(2,1)}), bf16[16,16,512]{2,1,0:T(8,128)(2,1)S(1)}, u32[]{:S(2)}, u32[]{:S(2)}) async-start(bf16[16,16,512]{2,1,0:T(8,128)(2,1)} %get-tuple-element.20), calls=%async_computation | async-start | bytes 524288 | tf_op jit(solution)/shard_map/all_to_all | solution.py:453

commit v20 on v19

--- a/solution.py
+++ b/solution.py
@@ -15,7 +15,7 @@
 MOST = 8
 RING = 16
 ORDER = [0, 1, 2, 3, 4, 5, 6, 7, 8, 9, 10, 11, 12, 13, 14, 15]
-EXCHANGE = [8, 9, 10, 11, 12, 13, 14, 15, 4, 5, 6, 7, 0, 1, 2, 3]
+EXCHANGE = [11, 10, 9, 8, 15, 14, 13, 12, 7, 6, 5, 4, 3, 2, 1, 0]
 F32 = jnp.float32
 BF16 = jnp.bfloat16
 NT = (((1,), (1,)), ((), ()))
@@ -316,7 +316,7 @@
 
 
 def delta_kernel(at_slot, *refs):
-    (*blocks, pick_ref, d_ref, u_ref, out_ref, rows_ref) = refs
+    (*blocks, pick_ref, d_ref, u_ref, out_ref) = refs
     blocks = [blocks[at_slot.index(i)] for i in range(len(blocks))]
     parts, slots, cols = out_ref.shape
     each, width = blocks[0].shape
@@ -326,7 +326,6 @@
     for i in range(cuts):
         at = slice(i * deep, (i + 1) * deep)
         piece = jnp.concatenate([b[:, at] for b in blocks], axis=0)
-        rows_ref[:, at] = piece
         low = low + dot(piece, d_ref[at, :])
     chosen = dot(pick_ref[...], low.astype(BF16)).astype(BF16)
     for p, device in enumerate(exchange_order(parts)):
@@ -343,24 +342,23 @@
     at_slot = ORDER if parts == RING else [*range(parts)]
     return pl.pallas_call(
         functools.partial(delta_kernel, at_slot),
-        out_shape=(
-            jax.ShapeDtypeStruct((parts, slots, width // parts), BF16),
-            jax.ShapeDtypeStruct((parts * each, width), BF16),
-        ),
+        out_shape=jax.ShapeDtypeStruct((parts, slots, width // parts), BF16),
         in_specs=[vmem] * (3 + parts),
-        out_specs=(vmem, vmem),
+        out_specs=vmem,
         compiler_params=pltpu.CompilerParams(vmem_limit_bytes=24 * 2**20),
         cost_estimate=pl.CostEstimate(
             flops=2 * (parts * each + slots) * width * rank_w,
-            bytes_accessed=2 * width * (2 * parts * each + 2 * rank_w + slots),
+            bytes_accessed=2 * width * (parts * each + 2 * rank_w + slots),
             transcendentals=0,
         ),
         name="delta",
     )(*[blocks[i] for i in at_slot], pick, down, up)
 
 
-def base_kernel(a_ref, order_ref, w_hbm, out_ref, w_ref, sems):
-    width = a_ref.shape[1]
+def base_kernel(at_slot, *refs):
+    (*blocks, order_ref, w_hbm, out_ref, w_ref, sems) = refs
+    blocks = [blocks[at_slot.index(i)] for i in range(len(blocks))]
+    width = w_ref.shape[0]
     cuts = sems.shape[0]
     deep = width // cuts
     copies = []
@@ -370,20 +368,23 @@
         copies[-1].start()
     for i in range(cuts):
         at = slice(i * deep, (i + 1) * deep)
-        rows = dot(order_ref[...], a_ref[:, at]).astype(BF16)
+        rows = jnp.concatenate([b[:, at] for b in blocks], axis=0)
+        rows = dot(order_ref[...], rows).astype(BF16)
         copies[i].wait()
         part = dot(rows, w_ref[at, :])
         out_ref[...] = part if i == 0 else out_ref[...] + part
 
 
-def base_part(gathered, out_weight, order):
-    total, width = gathered.shape
-    cols = out_weight.shape[1]
+def base_part(blocks, out_weight, order):
+    parts = len(blocks)
+    total = order.shape[0]
+    width, cols = out_weight.shape
     vmem = pl.BlockSpec(memory_space=pltpu.VMEM)
+    at_slot = ORDER if parts == RING else [*range(parts)]
     return pl.pallas_call(
-        base_kernel,
+        functools.partial(base_kernel, at_slot),
         out_shape=jax.ShapeDtypeStruct((total, cols), F32),
-        in_specs=[vmem] * 2 + [pl.BlockSpec(memory_space=pl.ANY)],
+        in_specs=[vmem] * (1 + parts) + [pl.BlockSpec(memory_space=pl.ANY)],
         out_specs=vmem,
         scratch_shapes=[pltpu.VMEM(out_weight.shape, BF16), pltpu.SemaphoreType.DMA((8,))],
         compiler_params=pltpu.CompilerParams(vmem_limit_bytes=24 * 2**20),
@@ -393,7 +394,7 @@
             transcendentals=0,
         ),
         name="base",
-    )(gathered, order, *in_hbm(out_weight))
+    )(*[blocks[i] for i in at_slot], order, *in_hbm(out_weight))
 
 
 def join_kernel(base_ref, place_ref, delta_ref, out_ref):
@@ -448,10 +449,10 @@
         parts,
     )
     blocks = gather(attended, parts)
-    send, gathered = deltas(blocks, pick, down, up)
+    send = deltas(blocks, pick, down, up)
     groups = [exchange_order(parts)]
     delta = lax.all_to_all(send, "tensor", 0, 0, axis_index_groups=groups, tiled=True)
-    base = base_part(gathered, out_weight, order)
+    base = base_part(blocks, out_weight, order)
     return join(base, place, delta, steps)
 
 

time: 44.4 us -> 43.5 us (0.980)
  waiting for transfers between devices: 12.7 us -> 12.1 us
    all_to_all x1, waiting for transfers between devices: 2.98 us -> 2.31 us  [per_device(): lax.all_to_all(send, 'tensor', 0, 0, axis_index_groups=groups, tiled=True)]
where the time goes in v20:
time: 43.5 us; the launch traced here: 43.1 us
  starting transfers between devices  18 us (41%)
  Pallas kernels  13.1 us (30%)
  waiting for transfers between devices  12.1 us (28%)
    ppermute x15, starting transfers between devices, swap(): return lax.ppermute(x, 'tensor', [(i, i ^ bits) for i in range(parts)])  12.5 us
    ppermute x15, waiting for transfers between devices, swap(): return lax.ppermute(x, 'tensor', [(i, i ^ bits) for i in range(parts)])  9.76 us
    pallas_call x1, Pallas kernels, attend(): pl.pallas_call(attend_kernel, out_shape=[jax.ShapeDtypeStruct(shape, BF16...  5.8 us
    all_to_all x1, starting transfers between devices, per_device(): lax.all_to_all(send, 'tensor', 0, 0, axis_index_groups=groups, tiled=True)  5.42 us
    pallas_call x1, Pallas kernels, base_part(): pl.pallas_call(functools.partial(base_kernel, at_slot), out_shape=jax.Sha...  4.26 us
    all_to_all x1, waiting for transfers between devices, per_device(): lax.all_to_all(send, 'tensor', 0, 0, axis_index_groups=groups, tiled=True)  2.31 us
    pallas_call x1, Pallas kernels, deltas(): pl.pallas_call(functools.partial(delta_kernel, at_slot), out_shape=jax.Sh...  2.16 us
  transfers between devices with their start and end apart: 16, of which 11 were waited for; matrix products, arithmetic and copies ran while one was open for 0% of the time, Pallas kernels for 10%

profile of v20, /device:TPU:0, one launch (start us, length us, event | category | flops | bytes accessed | tf_op | source)
XLA Modules:
  0.0 43.1 jit_solution(8267483632738212930)
XLA Ops:
  0.0 5.8 %attend.1 = (bf16[8,8192]{1,0:T(8,128)(2,1)S(1)}, bf16[8192,128]{1,0:T(8,128)(2,1)S(1)}, bf16[8192,128]{1,0:T(8,128)(2,1)S(1)}, bf16[16,128]{1,0:T(8,128)(2,1)S(...) custom-call(s32[4]{0:T(128)} %len_hbm.1, bf16[2,4,8192]{2,1,0:T(4,128)(2,1)} %q_hbm.1, ...), custom_call_target="tpu_custom_call" | custom-call | flops 134217728 | bytes 8388608 | tf_op jit(solution)/shard_map/attend/pallas_call | solution.py:252
  5.8 4.1 %collective-permute-start.7 = (bf16[8,8192]{1,0:T(8,128)(2,1)S(1)}, bf16[8,8192]{1,0:T(8,128)(2,1)S(1)}, u32[]{:S(2)}, u32[]{:S(2)}) collective-permute-start(bf16[8,8192]{1,0:T(8,128)(2,1)S(1)} %get-tuple-element.11.refs_0_), channel_id=1, source_target_pairs={{0,8},{1,9},{2,10},{3,11},{4,12},{5,13},{6,14},{7,15},{8,0},{9,1},... | collective-permute-start | bytes 393224 | tf_op jit(solution)/shard_map/ppermute | solution.py:297
  9.9 2.5 %collective-permute-start.5 = (bf16[8,8192]{1,0:T(8,128)(2,1)S(1)}, bf16[8,8192]{1,0:T(8,128)(2,1)S(1)}, u32[]{:S(2)}, u32[]{:S(2)}) collective-permute-start(bf16[8,8192]{1,0:T(8,128)(2,1)S(1)} %get-tuple-element.11.refs_0_), channel_id=1, source_target_pairs={{0,6},{1,7},{2,4},{3,5},{4,2},{5,3},{6,0},{7,1},{8,14},{9,15},{10,... | collective-permute-start | bytes 393224 | tf_op jit(solution)/shard_map/ppermute | solution.py:297
  12.4 0.4 %collective-permute-start.3 = (bf16[8,8192]{1,0:T(8,128)(2,1)S(1)}, bf16[8,8192]{1,0:T(8,128)(2,1)S(1)}, u32[]{:S(2)}, u32[]{:S(2)}) collective-permute-start(bf16[8,8192]{1,0:T(8,128)(2,1)S(1)} %get-tuple-element.11.refs_0_), channel_id=1, source_target_pairs={{0,4},{1,5},{2,6},{3,7},{4,0},{5,1},{6,2},{7,3},{8,12},{9,13},{10,... | collective-permute-start | bytes 393224 | tf_op jit(solution)/shard_map/ppermute | solution.py:297
  12.9 0.5 %collective-permute-start.1 = (bf16[8,8192]{1,0:T(8,128)(2,1)S(1)}, bf16[8,8192]{1,0:T(8,128)(2,1)S(1)}, u32[]{:S(2)}, u32[]{:S(2)}) collective-permute-start(bf16[8,8192]{1,0:T(8,128)(2,1)S(1)} %get-tuple-element.11.refs_0_), channel_id=1, source_target_pairs={{0,2},{1,3},{2,0},{3,1},{4,6},{5,7},{6,4},{7,5},{8,10},{9,11},{10,... | collective-permute-start | bytes 393224 | tf_op jit(solution)/shard_map/ppermute | solution.py:297
  13.4 2.9 %collective-permute-done.7.refs_8_ = bf16[8,8192]{1,0:T(8,128)(2,1)S(1)} collective-permute-done((bf16[8,8192]{1,0:T(8,128)(2,1)S(1)}, bf16[8,8192]{1,0:T(8,128)(2,1)S(1)}, u32[]{:S(2)}, u32[]{:S(2)}) %collective-permute-start.7) | collective-permute-done | bytes 131104 | tf_op jit(solution)/shard_map/ppermute | solution.py:297
  16.3 1.6 %collective-permute-start.13 = (bf16[8,8192]{1,0:T(8,128)(2,1)S(1)}, bf16[8,8192]{1,0:T(8,128)(2,1)S(1)}, u32[]{:S(2)}, u32[]{:S(2)}) collective-permute-start(bf16[8,8192]{1,0:T(8,128)(2,1)S(1)} %collective-permute-done.7.refs_8_), channel_id=1, source_target_pairs={{0,6},{1,7},{2,4},{3,5},{4,2},{5,3},{6,0},{7,1},{8,14},{9,15},{10,... | collective-permute-start | bytes 393224 | tf_op jit(solution)/shard_map/ppermute | solution.py:297
  17.9 0.9 %collective-permute-done.5.refs_6_ = bf16[8,8192]{1,0:T(8,128)(2,1)S(1)} collective-permute-done((bf16[8,8192]{1,0:T(8,128)(2,1)S(1)}, bf16[8,8192]{1,0:T(8,128)(2,1)S(1)}, u32[]{:S(2)}, u32[]{:S(2)}) %collective-permute-start.5) | collective-permute-done | bytes 131104 | tf_op jit(solution)/shard_map/ppermute | solution.py:297
  18.9 1.2 %collective-permute-start.11 = (bf16[8,8192]{1,0:T(8,128)(2,1)S(1)}, bf16[8,8192]{1,0:T(8,128)(2,1)S(1)}, u32[]{:S(2)}, u32[]{:S(2)}) collective-permute-start(bf16[8,8192]{1,0:T(8,128)(2,1)S(1)} %collective-permute-done.7.refs_8_), channel_id=1, source_target_pairs={{0,4},{1,5},{2,6},{3,7},{4,0},{5,1},{6,2},{7,3},{8,12},{9,13},{10,... | collective-permute-start | bytes 393224 | tf_op jit(solution)/shard_map/ppermute | solution.py:297
  20.1 1.2 %collective-permute-done.3.refs_4_ = bf16[8,8192]{1,0:T(8,128)(2,1)S(1)} collective-permute-done((bf16[8,8192]{1,0:T(8,128)(2,1)S(1)}, bf16[8,8192]{1,0:T(8,128)(2,1)S(1)}, u32[]{:S(2)}, u32[]{:S(2)}) %collective-permute-start.3) | collective-permute-done | bytes 131104 | tf_op jit(solution)/shard_map/ppermute | solution.py:297
  21.3 0.9 %collective-permute-start.9 = (bf16[8,8192]{1,0:T(8,128)(2,1)S(1)}, bf16[8,8192]{1,0:T(8,128)(2,1)S(1)}, u32[]{:S(2)}, u32[]{:S(2)}) collective-permute-start(bf16[8,8192]{1,0:T(8,128)(2,1)S(1)} %collective-permute-done.7.refs_8_), channel_id=1, source_target_pairs={{0,2},{1,3},{2,0},{3,1},{4,6},{5,7},{6,4},{7,5},{8,10},{9,11},{10,... | collective-permute-start | bytes 393224 | tf_op jit(solution)/shard_map/ppermute | solution.py:297
  22.2 0.0 collective-permute-done.1.refs_2_
  22.2 0.0 collective-permute-start.8
  22.2 0.0 collective-permute-done.refs_1_
  22.2 0.5 %collective-permute-start.6 = (bf16[8,8192]{1,0:T(8,128)(2,1)S(1)}, bf16[8,8192]{1,0:T(8,128)(2,1)S(1)}, u32[]{:S(2)}, u32[]{:S(2)}) collective-permute-start(bf16[8,8192]{1,0:T(8,128)(2,1)S(1)} %collective-permute-done.5.refs_6_), channel_id=1, source_target_pairs={{0,1},{1,0},{2,3},{3,2},{4,5},{5,4},{6,7},{7,6},{8,9},{9,8},{10,11... | collective-permute-start | bytes 393224 | tf_op jit(solution)/shard_map/ppermute | solution.py:297
  22.8 1.7 %collective-permute-done.13.refs_14_ = bf16[8,8192]{1,0:T(8,128)(2,1)S(1)} collective-permute-done((bf16[8,8192]{1,0:T(8,128)(2,1)S(1)}, bf16[8,8192]{1,0:T(8,128)(2,1)S(1)}, u32[]{:S(2)}, u32[]{:S(2)}) %collective-permute-start.13) | collective-permute-done | bytes 131104 | tf_op jit(solution)/shard_map/ppermute | solution.py:297
  24.5 0.0 collective-permute-start.4
  24.5 1.4 %collective-permute-done.11.refs_12_ = bf16[8,8192]{1,0:T(8,128)(2,1)S(1)} collective-permute-done((bf16[8,8192]{1,0:T(8,128)(2,1)S(1)}, bf16[8,8192]{1,0:T(8,128)(2,1)S(1)}, u32[]{:S(2)}, u32[]{:S(2)}) %collective-permute-start.11) | collective-permute-done | bytes 131104 | tf_op jit(solution)/shard_map/ppermute | solution.py:297
  25.9 0.0 collective-permute-start.2
  25.9 0.4 collective-permute-done.9.refs_10_
  26.3 0.2 collective-permute-start.14
  26.4 0.4 collective-permute-start.12
  26.8 0.2 collective-permute-start.10
  26.9 0.3 collective-permute-done.2.refs_3_
  27.2 0.4 collective-permute-done.14.refs_15_
  27.6 0.2 collective-permute-done.12.refs_13_
  27.8 0.3 collective-permute-done.10.refs_11_
  28.1 2.2 %delta.1 = bf16[16,16,512]{2,1,0:T(8,128)(2,1)} custom-call(bf16[8,8192]{1,0:T(8,128)(2,1)S(1)} %get-tuple-element.11.refs_0_, bf16[8,8192]{1,0:T(8,128)(2,1)S(1)} %collective-permute-done.refs_1_, bf16[8,8192]{1,0:T(8,128)(2,1)S(1)} %collective-permute-done.1.refs_2_, bf16[8,8192]{1,0:T(8,128)(2,1)S(1)} %collective-permute-done.2.refs_3_, ...), custom_call_target="tpu_custom_call" | custom-call | flops 301989888 | bytes 6553600 | tf_op jit(solution)/shard_map/delta/pallas_call | solution.py:343
  30.3 5.4 %all-to-all-start = ((bf16[16,16,512]{2,1,0:T(8,128)(2,1)}), bf16[16,16,512]{2,1,0:T(8,128)(2,1)S(1)}, u32[]{:S(2)}, u32[]{:S(2)}) async-start(bf16[16,16,512]{2,1,0:T(8,128)(2,1)} %delta.1), calls=%async_computation | async-start | bytes 524288 | tf_op jit(solution)/shard_map/all_to_all | solution.py:454
  35.7 4.3 %base.1.base_ref = f32[128,512]{1,0:T(8,128)S(1)} custom-call(bf16[8,8192]{1,0:T(8,128)(2,1)S(1)} %get-tuple-element.11.refs_0_, bf16[8,8192]{1,0:T(8,128)(2,1)S(1)} %collective-permute-done.refs_1_, bf16[8,8192]{1,0:T(8,128)(2,1)S(1)} %collective-permute-done.1.refs_2_, bf16[8,8192]{1,0:T(8,128)(2,1)S(1)} %collective-permute-done.2.refs_3_, ...), custom_call_target="tpu_custom_call" | custom-call | flops 1342177280 | bytes 10747904 | tf_op jit(solution)/shard_map/base/pallas_call | solution.py:384
  40.0 2.3 %all-to-all-done.delta_ref = bf16[16,16,512]{2,1,0:T(8,128)(2,1)S(1)} async-done(((bf16[16,16,512]{2,1,0:T(8,128)(2,1)}), bf16[16,16,512]{2,1,0:T(8,128)(2,1)S(1)}, u32[]{:S(2)}, u32[]{:S(2)}) %all-to-all-start) | async-done | bytes 262176 | tf_op jit(solution)/shard_map/all_to_all | solution.py:454
  42.3 0.8 %join.1 = bf16[2,64,512]{2,1,0:T(8,128)(2,1)} custom-call(f32[128,512]{1,0:T(8,128)S(1)} %base.1.base_ref, bf16[128,256]{1,0:T(8,128)(2,1)S(1)} %get-tuple-element.13.place_ref, bf16[16,16,512]{2,1,0:T(8,128)(2,1)S(1)} %all-to-all-done.delta_ref), custom_call_target="tpu_custom_call" | custom-call | tf_op jit(solution)/shard_map/join/pallas_call | solution.py:412
  (4 shorter events, 0.0 us)
Async XLA Ops:
  5.8 10.5 %collective-permute-start.7 = (bf16[8,8192]{1,0:T(8,128)(2,1)S(1)}, bf16[8,8192]{1,0:T(8,128)(2,1)S(1)}, u32[]{:S(2)}, u32[]{:S(2)}) collective-permute-start(bf16[8,8192]{1,0:T(8,128)(2,1)S(1)} %get-tuple-element.11.refs_0_), channel_id=1, source_target_pairs={{0,8},{1,9},{2,10},{3,11},{4,12},{5,13},{6,14},{7,15},{8,0},{9,1},... | collective-permute-start | bytes 393224 | tf_op jit(solution)/shard_map/ppermute | solution.py:297
  9.9 9.0 %collective-permute-start.5 = (bf16[8,8192]{1,0:T(8,128)(2,1)S(1)}, bf16[8,8192]{1,0:T(8,128)(2,1)S(1)}, u32[]{:S(2)}, u32[]{:S(2)}) collective-permute-start(bf16[8,8192]{1,0:T(8,128)(2,1)S(1)} %get-tuple-element.11.refs_0_), channel_id=1, source_target_pairs={{0,6},{1,7},{2,4},{3,5},{4,2},{5,3},{6,0},{7,1},{8,14},{9,15},{10,... | collective-permute-start | bytes 393224 | tf_op jit(solution)/shard_map/ppermute | solution.py:297
  12.4 8.8 %collective-permute-start.3 = (bf16[8,8192]{1,0:T(8,128)(2,1)S(1)}, bf16[8,8192]{1,0:T(8,128)(2,1)S(1)}, u32[]{:S(2)}, u32[]{:S(2)}) collective-permute-start(bf16[8,8192]{1,0:T(8,128)(2,1)S(1)} %get-tuple-element.11.refs_0_), channel_id=1, source_target_pairs={{0,4},{1,5},{2,6},{3,7},{4,0},{5,1},{6,2},{7,3},{8,12},{9,13},{10,... | collective-permute-start | bytes 393224 | tf_op jit(solution)/shard_map/ppermute | solution.py:297
  12.9 9.3 %collective-permute-start.1 = (bf16[8,8192]{1,0:T(8,128)(2,1)S(1)}, bf16[8,8192]{1,0:T(8,128)(2,1)S(1)}, u32[]{:S(2)}, u32[]{:S(2)}) collective-permute-start(bf16[8,8192]{1,0:T(8,128)(2,1)S(1)} %get-tuple-element.11.refs_0_), channel_id=1, source_target_pairs={{0,2},{1,3},{2,0},{3,1},{4,6},{5,7},{6,4},{7,5},{8,10},{9,11},{10,... | collective-permute-start | bytes 393224 | tf_op jit(solution)/shard_map/ppermute | solution.py:297
  13.4 8.8 %collective-permute-start = (bf16[8,8192]{1,0:T(8,128)(2,1)S(1)}, bf16[8,8192]{1,0:T(8,128)(2,1)S(1)}, u32[]{:S(2)}, u32[]{:S(2)}) collective-permute-start(bf16[8,8192]{1,0:T(8,128)(2,1)S(1)} %get-tuple-element.11.refs_0_), channel_id=1, source_target_pairs={{0,1},{1,0},{2,3},{3,2},{4,5},{5,4},{6,7},{7,6},{8,9},{9,8},{10,11... | collective-permute-start | bytes 393224 | tf_op jit(solution)/shard_map/ppermute | solution.py:297
  16.3 8.2 %collective-permute-start.13 = (bf16[8,8192]{1,0:T(8,128)(2,1)S(1)}, bf16[8,8192]{1,0:T(8,128)(2,1)S(1)}, u32[]{:S(2)}, u32[]{:S(2)}) collective-permute-start(bf16[8,8192]{1,0:T(8,128)(2,1)S(1)} %collective-permute-done.7.refs_8_), channel_id=1, source_target_pairs={{0,6},{1,7},{2,4},{3,5},{4,2},{5,3},{6,0},{7,1},{8,14},{9,15},{10,... | collective-permute-start | bytes 393224 | tf_op jit(solution)/shard_map/ppermute | solution.py:297
  18.9 7.0 %collective-permute-start.11 = (bf16[8,8192]{1,0:T(8,128)(2,1)S(1)}, bf16[8,8192]{1,0:T(8,128)(2,1)S(1)}, u32[]{:S(2)}, u32[]{:S(2)}) collective-permute-start(bf16[8,8192]{1,0:T(8,128)(2,1)S(1)} %collective-permute-done.7.refs_8_), channel_id=1, source_target_pairs={{0,4},{1,5},{2,6},{3,7},{4,0},{5,1},{6,2},{7,3},{8,12},{9,13},{10,... | collective-permute-start | bytes 393224 | tf_op jit(solution)/shard_map/ppermute | solution.py:297
  21.3 5.0 %collective-permute-start.9 = (bf16[8,8192]{1,0:T(8,128)(2,1)S(1)}, bf16[8,8192]{1,0:T(8,128)(2,1)S(1)}, u32[]{:S(2)}, u32[]{:S(2)}) collective-permute-start(bf16[8,8192]{1,0:T(8,128)(2,1)S(1)} %collective-permute-done.7.refs_8_), channel_id=1, source_target_pairs={{0,2},{1,3},{2,0},{3,1},{4,6},{5,7},{6,4},{7,5},{8,10},{9,11},{10,... | collective-permute-start | bytes 393224 | tf_op jit(solution)/shard_map/ppermute | solution.py:297
  22.2 4.2 %collective-permute-start.8 = (bf16[8,8192]{1,0:T(8,128)(2,1)S(1)}, bf16[8,8192]{1,0:T(8,128)(2,1)S(1)}, u32[]{:S(2)}, u32[]{:S(2)}) collective-permute-start(bf16[8,8192]{1,0:T(8,128)(2,1)S(1)} %collective-permute-done.7.refs_8_), channel_id=1, source_target_pairs={{0,1},{1,0},{2,3},{3,2},{4,5},{5,4},{6,7},{7,6},{8,9},{9,8},{10,11... | collective-permute-start | bytes 393224 | tf_op jit(solution)/shard_map/ppermute | solution.py:297
  22.2 4.5 %collective-permute-start.6 = (bf16[8,8192]{1,0:T(8,128)(2,1)S(1)}, bf16[8,8192]{1,0:T(8,128)(2,1)S(1)}, u32[]{:S(2)}, u32[]{:S(2)}) collective-permute-start(bf16[8,8192]{1,0:T(8,128)(2,1)S(1)} %collective-permute-done.5.refs_6_), channel_id=1, source_target_pairs={{0,1},{1,0},{2,3},{3,2},{4,5},{5,4},{6,7},{7,6},{8,9},{9,8},{10,11... | collective-permute-start | bytes 393224 | tf_op jit(solution)/shard_map/ppermute | solution.py:297
  24.5 2.5 %collective-permute-start.4 = (bf16[8,8192]{1,0:T(8,128)(2,1)S(1)}, bf16[8,8192]{1,0:T(8,128)(2,1)S(1)}, u32[]{:S(2)}, u32[]{:S(2)}) collective-permute-start(bf16[8,8192]{1,0:T(8,128)(2,1)S(1)} %collective-permute-done.3.refs_4_), channel_id=1, source_target_pairs={{0,1},{1,0},{2,3},{3,2},{4,5},{5,4},{6,7},{7,6},{8,9},{9,8},{10,11... | collective-permute-start | bytes 393224 | tf_op jit(solution)/shard_map/ppermute | solution.py:297
  25.9 1.3 %collective-permute-start.2 = (bf16[8,8192]{1,0:T(8,128)(2,1)S(1)}, bf16[8,8192]{1,0:T(8,128)(2,1)S(1)}, u32[]{:S(2)}, u32[]{:S(2)}) collective-permute-start(bf16[8,8192]{1,0:T(8,128)(2,1)S(1)} %collective-permute-done.1.refs_2_), channel_id=1, source_target_pairs={{0,1},{1,0},{2,3},{3,2},{4,5},{5,4},{6,7},{7,6},{8,9},{9,8},{10,11... | collective-permute-start | bytes 393224 | tf_op jit(solution)/shard_map/ppermute | solution.py:297
  26.3 1.3 %collective-permute-start.14 = (bf16[8,8192]{1,0:T(8,128)(2,1)S(1)}, bf16[8,8192]{1,0:T(8,128)(2,1)S(1)}, u32[]{:S(2)}, u32[]{:S(2)}) collective-permute-start(bf16[8,8192]{1,0:T(8,128)(2,1)S(1)} %collective-permute-done.13.refs_14_), channel_id=1, source_target_pairs={{0,1},{1,0},{2,3},{3,2},{4,5},{5,4},{6,7},{7,6},{8,9},{9,8},{10,11... | collective-permute-start | bytes 393224 | tf_op jit(solution)/shard_map/ppermute | solution.py:297
  26.4 1.4 %collective-permute-start.12 = (bf16[8,8192]{1,0:T(8,128)(2,1)S(1)}, bf16[8,8192]{1,0:T(8,128)(2,1)S(1)}, u32[]{:S(2)}, u32[]{:S(2)}) collective-permute-start(bf16[8,8192]{1,0:T(8,128)(2,1)S(1)} %collective-permute-done.11.refs_12_), channel_id=1, source_target_pairs={{0,1},{1,0},{2,3},{3,2},{4,5},{5,4},{6,7},{7,6},{8,9},{9,8},{10,11... | collective-permute-start | bytes 393224 | tf_op jit(solution)/shard_map/ppermute | solution.py:297
  26.8 1.3 %collective-permute-start.10 = (bf16[8,8192]{1,0:T(8,128)(2,1)S(1)}, bf16[8,8192]{1,0:T(8,128)(2,1)S(1)}, u32[]{:S(2)}, u32[]{:S(2)}) collective-permute-start(bf16[8,8192]{1,0:T(8,128)(2,1)S(1)} %collective-permute-done.9.refs_10_), channel_id=1, source_target_pairs={{0,1},{1,0},{2,3},{3,2},{4,5},{5,4},{6,7},{7,6},{8,9},{9,8},{10,11... | collective-permute-start | bytes 393224 | tf_op jit(solution)/shard_map/ppermute | solution.py:297
  30.3 12.0 %all-to-all-start = ((bf16[16,16,512]{2,1,0:T(8,128)(2,1)}), bf16[16,16,512]{2,1,0:T(8,128)(2,1)S(1)}, u32[]{:S(2)}, u32[]{:S(2)}) async-start(bf16[16,16,512]{2,1,0:T(8,128)(2,1)} %delta.1), calls=%async_computation | async-start | bytes 524288 | tf_op jit(solution)/shard_map/all_to_all | solution.py:454

commit v21 on v20

--- a/solution.py
+++ b/solution.py
@@ -14,8 +14,8 @@
 GROUP = HQ // KVH
 MOST = 8
 RING = 16
-ORDER = [0, 1, 2, 3, 4, 5, 6, 7, 8, 9, 10, 11, 12, 13, 14, 15]
-EXCHANGE = [11, 10, 9, 8, 15, 14, 13, 12, 7, 6, 5, 4, 3, 2, 1, 0]
+ORDER = [0, 1, 2, 3, 4, 5, 6, 7, 8, 9, 14, 15, 12, 13, 10, 11]
+EXCHANGE = [11, 10, 9, 8, 7, 6, 5, 4, 15, 14, 13, 12, 3, 2, 1, 0]
 F32 = jnp.float32
 BF16 = jnp.bfloat16
 NT = (((1,), (1,)), ((), ()))

time: 43.5 us -> 43.8 us (level)
    ppermute x15, waiting for transfers between devices: 9.76 us -> 10.5 us  [swap(): return lax.ppermute(x, 'tensor', [(i, i ^ bits) for i in range(parts)])]
    all_to_all x1, waiting for transfers between devices: 2.31 us -> 1.86 us  [per_device(): lax.all_to_all(send, 'tensor', 0, 0, axis_index_groups=groups, tiled=True)]
  transfers between devices with their start and end apart: 16 -> 16, of which waited for: 11 -> 9; matrix products, arithmetic and copies ran while one was open for 0% -> 0% of each run, Pallas kernels for 10% -> 10%
where the time goes in v21:
time: 43.8 us; the launch traced here: 43.2 us
  starting transfers between devices  17.8 us (41%)
  Pallas kernels  13.1 us (30%)
  waiting for transfers between devices  12.3 us (28%)
    ppermute x15, starting transfers between devices, swap(): return lax.ppermute(x, 'tensor', [(i, i ^ bits) for i in range(parts)])  12.7 us
    ppermute x15, waiting for transfers between devices, swap(): return lax.ppermute(x, 'tensor', [(i, i ^ bits) for i in range(parts)])  10.5 us
    pallas_call x1, Pallas kernels, attend(): pl.pallas_call(attend_kernel, out_shape=[jax.ShapeDtypeStruct(shape, BF16...  5.8 us
    all_to_all x1, starting transfers between devices, per_device(): lax.all_to_all(send, 'tensor', 0, 0, axis_index_groups=groups, tiled=True)  5.06 us
    pallas_call x1, Pallas kernels, base_part(): pl.pallas_call(functools.partial(base_kernel, at_slot), out_shape=jax.Sha...  4.26 us
    pallas_call x1, Pallas kernels, deltas(): pl.pallas_call(functools.partial(delta_kernel, at_slot), out_shape=jax.Sh...  2.16 us
    all_to_all x1, waiting for transfers between devices, per_device(): lax.all_to_all(send, 'tensor', 0, 0, axis_index_groups=groups, tiled=True)  1.86 us
  transfers between devices with their start and end apart: 16, of which 9 were waited for; matrix products, arithmetic and copies ran while one was open for 0% of the time, Pallas kernels for 10%

profile of v21, /device:TPU:0, one launch (start us, length us, event | category | flops | bytes accessed | tf_op | source)
XLA Modules:
  0.0 43.2 jit_solution(8475036052246675138)
XLA Ops:
  0.0 5.8 %attend.1 = (bf16[8,8192]{1,0:T(8,128)(2,1)S(1)}, bf16[8192,128]{1,0:T(8,128)(2,1)S(1)}, bf16[8192,128]{1,0:T(8,128)(2,1)S(1)}, bf16[16,128]{1,0:T(8,128)(2,1)S(...) custom-call(s32[4]{0:T(128)} %len_hbm.1, bf16[2,4,8192]{2,1,0:T(4,128)(2,1)} %q_hbm.1, ...), custom_call_target="tpu_custom_call" | custom-call | flops 134217728 | bytes 8388608 | tf_op jit(solution)/shard_map/attend/pallas_call | solution.py:252
  5.8 4.1 %collective-permute-start.7 = (bf16[8,8192]{1,0:T(8,128)(2,1)S(1)}, bf16[8,8192]{1,0:T(8,128)(2,1)S(1)}, u32[]{:S(2)}, u32[]{:S(2)}) collective-permute-start(bf16[8,8192]{1,0:T(8,128)(2,1)S(1)} %get-tuple-element.11.refs_0_), channel_id=1, source_target_pairs={{0,8},{1,9},{2,10},{3,11},{4,12},{5,13},{6,14},{7,15},{8,0},{9,1},... | collective-permute-start | bytes 393224 | tf_op jit(solution)/shard_map/ppermute | solution.py:297
  9.9 2.5 %collective-permute-start.5 = (bf16[8,8192]{1,0:T(8,128)(2,1)S(1)}, bf16[8,8192]{1,0:T(8,128)(2,1)S(1)}, u32[]{:S(2)}, u32[]{:S(2)}) collective-permute-start(bf16[8,8192]{1,0:T(8,128)(2,1)S(1)} %get-tuple-element.11.refs_0_), channel_id=1, source_target_pairs={{0,6},{1,7},{2,4},{3,5},{4,2},{5,3},{6,0},{7,1},{8,14},{9,15},{10,... | collective-permute-start | bytes 393224 | tf_op jit(solution)/shard_map/ppermute | solution.py:297
  12.4 0.4 %collective-permute-start.3 = (bf16[8,8192]{1,0:T(8,128)(2,1)S(1)}, bf16[8,8192]{1,0:T(8,128)(2,1)S(1)}, u32[]{:S(2)}, u32[]{:S(2)}) collective-permute-start(bf16[8,8192]{1,0:T(8,128)(2,1)S(1)} %get-tuple-element.11.refs_0_), channel_id=1, source_target_pairs={{0,4},{1,5},{2,6},{3,7},{4,0},{5,1},{6,2},{7,3},{8,12},{9,13},{10,... | collective-permute-start | bytes 393224 | tf_op jit(solution)/shard_map/ppermute | solution.py:297
  12.9 0.5 %collective-permute-start.1 = (bf16[8,8192]{1,0:T(8,128)(2,1)S(1)}, bf16[8,8192]{1,0:T(8,128)(2,1)S(1)}, u32[]{:S(2)}, u32[]{:S(2)}) collective-permute-start(bf16[8,8192]{1,0:T(8,128)(2,1)S(1)} %get-tuple-element.11.refs_0_), channel_id=1, source_target_pairs={{0,2},{1,3},{2,0},{3,1},{4,6},{5,7},{6,4},{7,5},{8,10},{9,11},{10,... | collective-permute-start | bytes 393224 | tf_op jit(solution)/shard_map/ppermute | solution.py:297
  13.4 0.0 collective-permute-start
  13.4 2.9 %collective-permute-done.7.refs_8_ = bf16[8,8192]{1,0:T(8,128)(2,1)S(1)} collective-permute-done((bf16[8,8192]{1,0:T(8,128)(2,1)S(1)}, bf16[8,8192]{1,0:T(8,128)(2,1)S(1)}, u32[]{:S(2)}, u32[]{:S(2)}) %collective-permute-start.7) | collective-permute-done | bytes 131104 | tf_op jit(solution)/shard_map/ppermute | solution.py:297
  16.3 1.6 %collective-permute-start.13 = (bf16[8,8192]{1,0:T(8,128)(2,1)S(1)}, bf16[8,8192]{1,0:T(8,128)(2,1)S(1)}, u32[]{:S(2)}, u32[]{:S(2)}) collective-permute-start(bf16[8,8192]{1,0:T(8,128)(2,1)S(1)} %collective-permute-done.7.refs_8_), channel_id=1, source_target_pairs={{0,2},{1,3},{2,0},{3,1},{4,6},{5,7},{6,4},{7,5},{8,10},{9,11},{10,... | collective-permute-start | bytes 393224 | tf_op jit(solution)/shard_map/ppermute | solution.py:297
  17.9 1.1 %collective-permute-done.5.refs_6_ = bf16[8,8192]{1,0:T(8,128)(2,1)S(1)} collective-permute-done((bf16[8,8192]{1,0:T(8,128)(2,1)S(1)}, bf16[8,8192]{1,0:T(8,128)(2,1)S(1)}, u32[]{:S(2)}, u32[]{:S(2)}) %collective-permute-start.5) | collective-permute-done | bytes 131104 | tf_op jit(solution)/shard_map/ppermute | solution.py:297
  19.0 1.1 %collective-permute-start.11 = (bf16[8,8192]{1,0:T(8,128)(2,1)S(1)}, bf16[8,8192]{1,0:T(8,128)(2,1)S(1)}, u32[]{:S(2)}, u32[]{:S(2)}) collective-permute-start(bf16[8,8192]{1,0:T(8,128)(2,1)S(1)} %collective-permute-done.7.refs_8_), channel_id=1, source_target_pairs={{0,4},{1,5},{2,6},{3,7},{4,0},{5,1},{6,2},{7,3},{8,12},{9,13},{10,... | collective-permute-start | bytes 393224 | tf_op jit(solution)/shard_map/ppermute | solution.py:297
  20.1 1.2 %collective-permute-done.3.refs_4_ = bf16[8,8192]{1,0:T(8,128)(2,1)S(1)} collective-permute-done((bf16[8,8192]{1,0:T(8,128)(2,1)S(1)}, bf16[8,8192]{1,0:T(8,128)(2,1)S(1)}, u32[]{:S(2)}, u32[]{:S(2)}) %collective-permute-start.3) | collective-permute-done | bytes 131104 | tf_op jit(solution)/shard_map/ppermute | solution.py:297
  21.3 1.3 %collective-permute-start.9 = (bf16[8,8192]{1,0:T(8,128)(2,1)S(1)}, bf16[8,8192]{1,0:T(8,128)(2,1)S(1)}, u32[]{:S(2)}, u32[]{:S(2)}) collective-permute-start(bf16[8,8192]{1,0:T(8,128)(2,1)S(1)} %collective-permute-done.7.refs_8_), channel_id=1, source_target_pairs={{0,6},{1,7},{2,4},{3,5},{4,2},{5,3},{6,0},{7,1},{8,14},{9,15},{10,... | collective-permute-start | bytes 393224 | tf_op jit(solution)/shard_map/ppermute | solution.py:297
  22.6 0.0 collective-permute-done.1.refs_2_
  22.6 0.5 %collective-permute-start.6 = (bf16[8,8192]{1,0:T(8,128)(2,1)S(1)}, bf16[8,8192]{1,0:T(8,128)(2,1)S(1)}, u32[]{:S(2)}, u32[]{:S(2)}) collective-permute-start(bf16[8,8192]{1,0:T(8,128)(2,1)S(1)} %collective-permute-done.5.refs_6_), channel_id=1, source_target_pairs={{0,1},{1,0},{2,3},{3,2},{4,5},{5,4},{6,7},{7,6},{8,9},{9,8},{10,11... | collective-permute-start | bytes 393224 | tf_op jit(solution)/shard_map/ppermute | solution.py:297
  23.1 0.0 collective-permute-done.13.refs_14_
  23.1 0.1 collective-permute-start.4
  23.2 1.3 %collective-permute-done.11.refs_12_ = bf16[8,8192]{1,0:T(8,128)(2,1)S(1)} collective-permute-done((bf16[8,8192]{1,0:T(8,128)(2,1)S(1)}, bf16[8,8192]{1,0:T(8,128)(2,1)S(1)}, u32[]{:S(2)}, u32[]{:S(2)}) %collective-permute-start.11) | collective-permute-done | bytes 131104 | tf_op jit(solution)/shard_map/ppermute | solution.py:297
  24.5 2.7 %collective-permute-done.9.refs_10_ = bf16[8,8192]{1,0:T(8,128)(2,1)S(1)} collective-permute-done((bf16[8,8192]{1,0:T(8,128)(2,1)S(1)}, bf16[8,8192]{1,0:T(8,128)(2,1)S(1)}, u32[]{:S(2)}, u32[]{:S(2)}) %collective-permute-start.9) | collective-permute-done | bytes 131104 | tf_op jit(solution)/shard_map/ppermute | solution.py:297
  27.2 0.0 collective-permute-start.14
  27.2 0.0 collective-permute-done.8.refs_9_
  27.2 0.5 %collective-permute-start.12 = (bf16[8,8192]{1,0:T(8,128)(2,1)S(1)}, bf16[8,8192]{1,0:T(8,128)(2,1)S(1)}, u32[]{:S(2)}, u32[]{:S(2)}) collective-permute-start(bf16[8,8192]{1,0:T(8,128)(2,1)S(1)} %collective-permute-done.11.refs_12_), channel_id=1, source_target_pairs={{0,1},{1,0},{2,3},{3,2},{4,5},{5,4},{6,7},{7,6},{8,9},{9,8},{10,11... | collective-permute-start | bytes 393224 | tf_op jit(solution)/shard_map/ppermute | solution.py:297
  27.7 0.1 collective-permute-start.10
  27.7 0.0 collective-permute-done.4.refs_5_
  27.7 0.0 collective-permute-done.2.refs_3_
  27.7 0.8 %collective-permute-done.14.refs_15_ = bf16[8,8192]{1,0:T(8,128)(2,1)S(1)} collective-permute-done((bf16[8,8192]{1,0:T(8,128)(2,1)S(1)}, bf16[8,8192]{1,0:T(8,128)(2,1)S(1)}, u32[]{:S(2)}, u32[]{:S(2)}) %collective-permute-start.14) | collective-permute-done | bytes 131104 | tf_op jit(solution)/shard_map/ppermute | solution.py:297
  28.5 0.2 collective-permute-done.12.refs_13_
  28.7 0.3 collective-permute-done.10.refs_11_
  29.0 2.2 %delta.1 = bf16[16,16,512]{2,1,0:T(8,128)(2,1)} custom-call(bf16[8,8192]{1,0:T(8,128)(2,1)S(1)} %get-tuple-element.11.refs_0_, bf16[8,8192]{1,0:T(8,128)(2,1)S(1)} %collective-permute-done.refs_1_, bf16[8,8192]{1,0:T(8,128)(2,1)S(1)} %collective-permute-done.1.refs_2_, bf16[8,8192]{1,0:T(8,128)(2,1)S(1)} %collective-permute-done.2.refs_3_, ...), custom_call_target="tpu_custom_call" | custom-call | flops 301989888 | bytes 6553600 | tf_op jit(solution)/shard_map/delta/pallas_call | solution.py:343
  31.2 5.1 %all-to-all-start = ((bf16[16,16,512]{2,1,0:T(8,128)(2,1)}), bf16[16,16,512]{2,1,0:T(8,128)(2,1)S(1)}, u32[]{:S(2)}, u32[]{:S(2)}) async-start(bf16[16,16,512]{2,1,0:T(8,128)(2,1)} %delta.1), calls=%async_computation | async-start | bytes 524288 | tf_op jit(solution)/shard_map/all_to_all | solution.py:454
  36.2 4.3 %base.1.base_ref = f32[128,512]{1,0:T(8,128)S(1)} custom-call(bf16[8,8192]{1,0:T(8,128)(2,1)S(1)} %get-tuple-element.11.refs_0_, bf16[8,8192]{1,0:T(8,128)(2,1)S(1)} %collective-permute-done.refs_1_, bf16[8,8192]{1,0:T(8,128)(2,1)S(1)} %collective-permute-done.1.refs_2_, bf16[8,8192]{1,0:T(8,128)(2,1)S(1)} %collective-permute-done.2.refs_3_, ...), custom_call_target="tpu_custom_call" | custom-call | flops 1342177280 | bytes 10747904 | tf_op jit(solution)/shard_map/base/pallas_call | solution.py:384
  40.5 1.9 %all-to-all-done.delta_ref = bf16[16,16,512]{2,1,0:T(8,128)(2,1)S(1)} async-done(((bf16[16,16,512]{2,1,0:T(8,128)(2,1)}), bf16[16,16,512]{2,1,0:T(8,128)(2,1)S(1)}, u32[]{:S(2)}, u32[]{:S(2)}) %all-to-all-start) | async-done | bytes 262176 | tf_op jit(solution)/shard_map/all_to_all | solution.py:454
  42.4 0.8 %join.1 = bf16[2,64,512]{2,1,0:T(8,128)(2,1)} custom-call(f32[128,512]{1,0:T(8,128)S(1)} %base.1.base_ref, bf16[128,256]{1,0:T(8,128)(2,1)S(1)} %get-tuple-element.13.place_ref, bf16[16,16,512]{2,1,0:T(8,128)(2,1)S(1)} %all-to-all-done.delta_ref), custom_call_target="tpu_custom_call" | custom-call | tf_op jit(solution)/shard_map/join/pallas_call | solution.py:412
  (4 shorter events, 0.0 us)
Async XLA Ops:
  5.8 10.5 %collective-permute-start.7 = (bf16[8,8192]{1,0:T(8,128)(2,1)S(1)}, bf16[8,8192]{1,0:T(8,128)(2,1)S(1)}, u32[]{:S(2)}, u32[]{:S(2)}) collective-permute-start(bf16[8,8192]{1,0:T(8,128)(2,1)S(1)} %get-tuple-element.11.refs_0_), channel_id=1, source_target_pairs={{0,8},{1,9},{2,10},{3,11},{4,12},{5,13},{6,14},{7,15},{8,0},{9,1},... | collective-permute-start | bytes 393224 | tf_op jit(solution)/shard_map/ppermute | solution.py:297
  9.9 9.1 %collective-permute-start.5 = (bf16[8,8192]{1,0:T(8,128)(2,1)S(1)}, bf16[8,8192]{1,0:T(8,128)(2,1)S(1)}, u32[]{:S(2)}, u32[]{:S(2)}) collective-permute-start(bf16[8,8192]{1,0:T(8,128)(2,1)S(1)} %get-tuple-element.11.refs_0_), channel_id=1, source_target_pairs={{0,6},{1,7},{2,4},{3,5},{4,2},{5,3},{6,0},{7,1},{8,14},{9,15},{10,... | collective-permute-start | bytes 393224 | tf_op jit(solution)/shard_map/ppermute | solution.py:297
  12.4 8.8 %collective-permute-start.3 = (bf16[8,8192]{1,0:T(8,128)(2,1)S(1)}, bf16[8,8192]{1,0:T(8,128)(2,1)S(1)}, u32[]{:S(2)}, u32[]{:S(2)}) collective-permute-start(bf16[8,8192]{1,0:T(8,128)(2,1)S(1)} %get-tuple-element.11.refs_0_), channel_id=1, source_target_pairs={{0,4},{1,5},{2,6},{3,7},{4,0},{5,1},{6,2},{7,3},{8,12},{9,13},{10,... | collective-permute-start | bytes 393224 | tf_op jit(solution)/shard_map/ppermute | solution.py:297
  12.9 9.7 %collective-permute-start.1 = (bf16[8,8192]{1,0:T(8,128)(2,1)S(1)}, bf16[8,8192]{1,0:T(8,128)(2,1)S(1)}, u32[]{:S(2)}, u32[]{:S(2)}) collective-permute-start(bf16[8,8192]{1,0:T(8,128)(2,1)S(1)} %get-tuple-element.11.refs_0_), channel_id=1, source_target_pairs={{0,2},{1,3},{2,0},{3,1},{4,6},{5,7},{6,4},{7,5},{8,10},{9,11},{10,... | collective-permute-start | bytes 393224 | tf_op jit(solution)/shard_map/ppermute | solution.py:297
  13.4 9.2 %collective-permute-start = (bf16[8,8192]{1,0:T(8,128)(2,1)S(1)}, bf16[8,8192]{1,0:T(8,128)(2,1)S(1)}, u32[]{:S(2)}, u32[]{:S(2)}) collective-permute-start(bf16[8,8192]{1,0:T(8,128)(2,1)S(1)} %get-tuple-element.11.refs_0_), channel_id=1, source_target_pairs={{0,1},{1,0},{2,3},{3,2},{4,5},{5,4},{6,7},{7,6},{8,9},{9,8},{10,11... | collective-permute-start | bytes 393224 | tf_op jit(solution)/shard_map/ppermute | solution.py:297
  16.3 6.8 %collective-permute-start.13 = (bf16[8,8192]{1,0:T(8,128)(2,1)S(1)}, bf16[8,8192]{1,0:T(8,128)(2,1)S(1)}, u32[]{:S(2)}, u32[]{:S(2)}) collective-permute-start(bf16[8,8192]{1,0:T(8,128)(2,1)S(1)} %collective-permute-done.7.refs_8_), channel_id=1, source_target_pairs={{0,2},{1,3},{2,0},{3,1},{4,6},{5,7},{6,4},{7,5},{8,10},{9,11},{10,... | collective-permute-start | bytes 393224 | tf_op jit(solution)/shard_map/ppermute | solution.py:297
  19.0 5.5 %collective-permute-start.11 = (bf16[8,8192]{1,0:T(8,128)(2,1)S(1)}, bf16[8,8192]{1,0:T(8,128)(2,1)S(1)}, u32[]{:S(2)}, u32[]{:S(2)}) collective-permute-start(bf16[8,8192]{1,0:T(8,128)(2,1)S(1)} %collective-permute-done.7.refs_8_), channel_id=1, source_target_pairs={{0,4},{1,5},{2,6},{3,7},{4,0},{5,1},{6,2},{7,3},{8,12},{9,13},{10,... | collective-permute-start | bytes 393224 | tf_op jit(solution)/shard_map/ppermute | solution.py:297
  21.3 5.9 %collective-permute-start.9 = (bf16[8,8192]{1,0:T(8,128)(2,1)S(1)}, bf16[8,8192]{1,0:T(8,128)(2,1)S(1)}, u32[]{:S(2)}, u32[]{:S(2)}) collective-permute-start(bf16[8,8192]{1,0:T(8,128)(2,1)S(1)} %collective-permute-done.7.refs_8_), channel_id=1, source_target_pairs={{0,6},{1,7},{2,4},{3,5},{4,2},{5,3},{6,0},{7,1},{8,14},{9,15},{10,... | collective-permute-start | bytes 393224 | tf_op jit(solution)/shard_map/ppermute | solution.py:297
  22.6 4.6 %collective-permute-start.8 = (bf16[8,8192]{1,0:T(8,128)(2,1)S(1)}, bf16[8,8192]{1,0:T(8,128)(2,1)S(1)}, u32[]{:S(2)}, u32[]{:S(2)}) collective-permute-start(bf16[8,8192]{1,0:T(8,128)(2,1)S(1)} %collective-permute-done.7.refs_8_), channel_id=1, source_target_pairs={{0,1},{1,0},{2,3},{3,2},{4,5},{5,4},{6,7},{7,6},{8,9},{9,8},{10,11... | collective-permute-start | bytes 393224 | tf_op jit(solution)/shard_map/ppermute | solution.py:297
  22.6 5.1 %collective-permute-start.6 = (bf16[8,8192]{1,0:T(8,128)(2,1)S(1)}, bf16[8,8192]{1,0:T(8,128)(2,1)S(1)}, u32[]{:S(2)}, u32[]{:S(2)}) collective-permute-start(bf16[8,8192]{1,0:T(8,128)(2,1)S(1)} %collective-permute-done.5.refs_6_), channel_id=1, source_target_pairs={{0,1},{1,0},{2,3},{3,2},{4,5},{5,4},{6,7},{7,6},{8,9},{9,8},{10,11... | collective-permute-start | bytes 393224 | tf_op jit(solution)/shard_map/ppermute | solution.py:297
  23.1 4.6 %collective-permute-start.4 = (bf16[8,8192]{1,0:T(8,128)(2,1)S(1)}, bf16[8,8192]{1,0:T(8,128)(2,1)S(1)}, u32[]{:S(2)}, u32[]{:S(2)}) collective-permute-start(bf16[8,8192]{1,0:T(8,128)(2,1)S(1)} %collective-permute-done.3.refs_4_), channel_id=1, source_target_pairs={{0,1},{1,0},{2,3},{3,2},{4,5},{5,4},{6,7},{7,6},{8,9},{9,8},{10,11... | collective-permute-start | bytes 393224 | tf_op jit(solution)/shard_map/ppermute | solution.py:297
  24.5 3.3 %collective-permute-start.2 = (bf16[8,8192]{1,0:T(8,128)(2,1)S(1)}, bf16[8,8192]{1,0:T(8,128)(2,1)S(1)}, u32[]{:S(2)}, u32[]{:S(2)}) collective-permute-start(bf16[8,8192]{1,0:T(8,128)(2,1)S(1)} %collective-permute-done.1.refs_2_), channel_id=1, source_target_pairs={{0,1},{1,0},{2,3},{3,2},{4,5},{5,4},{6,7},{7,6},{8,9},{9,8},{10,11... | collective-permute-start | bytes 393224 | tf_op jit(solution)/shard_map/ppermute | solution.py:297
  27.2 1.3 %collective-permute-start.14 = (bf16[8,8192]{1,0:T(8,128)(2,1)S(1)}, bf16[8,8192]{1,0:T(8,128)(2,1)S(1)}, u32[]{:S(2)}, u32[]{:S(2)}) collective-permute-start(bf16[8,8192]{1,0:T(8,128)(2,1)S(1)} %collective-permute-done.13.refs_14_), channel_id=1, source_target_pairs={{0,1},{1,0},{2,3},{3,2},{4,5},{5,4},{6,7},{7,6},{8,9},{9,8},{10,11... | collective-permute-start | bytes 393224 | tf_op jit(solution)/shard_map/ppermute | solution.py:297
  27.2 1.5 %collective-permute-start.12 = (bf16[8,8192]{1,0:T(8,128)(2,1)S(1)}, bf16[8,8192]{1,0:T(8,128)(2,1)S(1)}, u32[]{:S(2)}, u32[]{:S(2)}) collective-permute-start(bf16[8,8192]{1,0:T(8,128)(2,1)S(1)} %collective-permute-done.11.refs_12_), channel_id=1, source_target_pairs={{0,1},{1,0},{2,3},{3,2},{4,5},{5,4},{6,7},{7,6},{8,9},{9,8},{10,11... | collective-permute-start | bytes 393224 | tf_op jit(solution)/shard_map/ppermute | solution.py:297
  27.7 1.3 %collective-permute-start.10 = (bf16[8,8192]{1,0:T(8,128)(2,1)S(1)}, bf16[8,8192]{1,0:T(8,128)(2,1)S(1)}, u32[]{:S(2)}, u32[]{:S(2)}) collective-permute-start(bf16[8,8192]{1,0:T(8,128)(2,1)S(1)} %collective-permute-done.9.refs_10_), channel_id=1, source_target_pairs={{0,1},{1,0},{2,3},{3,2},{4,5},{5,4},{6,7},{7,6},{8,9},{9,8},{10,11... | collective-permute-start | bytes 393224 | tf_op jit(solution)/shard_map/ppermute | solution.py:297
  31.2 11.2 %all-to-all-start = ((bf16[16,16,512]{2,1,0:T(8,128)(2,1)}), bf16[16,16,512]{2,1,0:T(8,128)(2,1)S(1)}, u32[]{:S(2)}, u32[]{:S(2)}) async-start(bf16[16,16,512]{2,1,0:T(8,128)(2,1)} %delta.1), calls=%async_computation | async-start | bytes 524288 | tf_op jit(solution)/shard_map/all_to_all | solution.py:454

commit v22 on v20

--- a/solution.py
+++ b/solution.py
@@ -141,13 +141,13 @@
     for r in range(rows):
         queue += [values[r + 1]] if r + 1 < rows else [store]
         queue += [keys[r + 2]] if r + 2 < rows else []
-    for copy in small + queue[0] + queue[1] + queue[2]:
+    for copy in small + queue[0] + queue[1] + queue[2] + queue[3] + queue[4]:
         copy.start()
     for copy in small:
         copy.wait()
-    for copy in queue[3] + queue[4]:
+    for copy in queue[5] + queue[6]:
         copy.start()
-    queue = queue[5:]
+    queue = queue[7:]
 
     flat = jnp.concatenate([q_ref[t].astype(F32) for t in range(steps)], axis=0)
     heads = []

time: 43.5 us -> 44 us (1.011)
    pallas_call x1, Pallas kernels: 5.8 us -> 6.31 us  [attend(): pl.pallas_call(attend_kernel, out_shape=[jax.ShapeDtypeStruct(shape, BF16...]
where the time goes in v22:
time: 44 us; the launch traced here: 43.7 us
  starting transfers between devices  18 us (41%)
  Pallas kernels  13.5 us (31%)
  waiting for transfers between devices  12.1 us (28%)
    ppermute x15, starting transfers between devices, swap(): return lax.ppermute(x, 'tensor', [(i, i ^ bits) for i in range(parts)])  12.5 us
    ppermute x15, waiting for transfers between devices, swap(): return lax.ppermute(x, 'tensor', [(i, i ^ bits) for i in range(parts)])  9.76 us
    pallas_call x1, Pallas kernels, attend(): pl.pallas_call(attend_kernel, out_shape=[jax.ShapeDtypeStruct(shape, BF16...  6.31 us
    all_to_all x1, starting transfers between devices, per_device(): lax.all_to_all(send, 'tensor', 0, 0, axis_index_groups=groups, tiled=True)  5.43 us
    pallas_call x1, Pallas kernels, base_part(): pl.pallas_call(functools.partial(base_kernel, at_slot), out_shape=jax.Sha...  4.23 us
    all_to_all x1, waiting for transfers between devices, per_device(): lax.all_to_all(send, 'tensor', 0, 0, axis_index_groups=groups, tiled=True)  2.34 us
    pallas_call x1, Pallas kernels, deltas(): pl.pallas_call(functools.partial(delta_kernel, at_slot), out_shape=jax.Sh...  2.16 us
  transfers between devices with their start and end apart: 16, of which 11 were waited for; matrix products, arithmetic and copies ran while one was open for 0% of the time, Pallas kernels for 10%

profile of v22, /device:TPU:0, one launch (start us, length us, event | category | flops | bytes accessed | tf_op | source)
XLA Modules:
  0.0 43.7 jit_solution(845361114466334982)
XLA Ops:
  0.0 6.3 %attend.1 = (bf16[8,8192]{1,0:T(8,128)(2,1)S(1)}, bf16[8192,128]{1,0:T(8,128)(2,1)S(1)}, bf16[8192,128]{1,0:T(8,128)(2,1)S(1)}, bf16[16,128]{1,0:T(8,128)(2,1)S(...) custom-call(s32[4]{0:T(128)} %len_hbm.1, bf16[2,4,8192]{2,1,0:T(4,128)(2,1)} %q_hbm.1, ...), custom_call_target="tpu_custom_call" | custom-call | flops 134217728 | bytes 8388608 | tf_op jit(solution)/shard_map/attend/pallas_call | solution.py:252
  6.3 4.1 %collective-permute-start.7 = (bf16[8,8192]{1,0:T(8,128)(2,1)S(1)}, bf16[8,8192]{1,0:T(8,128)(2,1)S(1)}, u32[]{:S(2)}, u32[]{:S(2)}) collective-permute-start(bf16[8,8192]{1,0:T(8,128)(2,1)S(1)} %get-tuple-element.11.refs_0_), channel_id=1, source_target_pairs={{0,8},{1,9},{2,10},{3,11},{4,12},{5,13},{6,14},{7,15},{8,0},{9,1},... | collective-permute-start | bytes 393224 | tf_op jit(solution)/shard_map/ppermute | solution.py:297
  10.4 2.5 %collective-permute-start.5 = (bf16[8,8192]{1,0:T(8,128)(2,1)S(1)}, bf16[8,8192]{1,0:T(8,128)(2,1)S(1)}, u32[]{:S(2)}, u32[]{:S(2)}) collective-permute-start(bf16[8,8192]{1,0:T(8,128)(2,1)S(1)} %get-tuple-element.11.refs_0_), channel_id=1, source_target_pairs={{0,6},{1,7},{2,4},{3,5},{4,2},{5,3},{6,0},{7,1},{8,14},{9,15},{10,... | collective-permute-start | bytes 393224 | tf_op jit(solution)/shard_map/ppermute | solution.py:297
  13.0 0.4 %collective-permute-start.3 = (bf16[8,8192]{1,0:T(8,128)(2,1)S(1)}, bf16[8,8192]{1,0:T(8,128)(2,1)S(1)}, u32[]{:S(2)}, u32[]{:S(2)}) collective-permute-start(bf16[8,8192]{1,0:T(8,128)(2,1)S(1)} %get-tuple-element.11.refs_0_), channel_id=1, source_target_pairs={{0,4},{1,5},{2,6},{3,7},{4,0},{5,1},{6,2},{7,3},{8,12},{9,13},{10,... | collective-permute-start | bytes 393224 | tf_op jit(solution)/shard_map/ppermute | solution.py:297
  13.4 0.5 %collective-permute-start.1 = (bf16[8,8192]{1,0:T(8,128)(2,1)S(1)}, bf16[8,8192]{1,0:T(8,128)(2,1)S(1)}, u32[]{:S(2)}, u32[]{:S(2)}) collective-permute-start(bf16[8,8192]{1,0:T(8,128)(2,1)S(1)} %get-tuple-element.11.refs_0_), channel_id=1, source_target_pairs={{0,2},{1,3},{2,0},{3,1},{4,6},{5,7},{6,4},{7,5},{8,10},{9,11},{10,... | collective-permute-start | bytes 393224 | tf_op jit(solution)/shard_map/ppermute | solution.py:297
  13.9 0.0 collective-permute-start
  13.9 2.9 %collective-permute-done.7.refs_8_ = bf16[8,8192]{1,0:T(8,128)(2,1)S(1)} collective-permute-done((bf16[8,8192]{1,0:T(8,128)(2,1)S(1)}, bf16[8,8192]{1,0:T(8,128)(2,1)S(1)}, u32[]{:S(2)}, u32[]{:S(2)}) %collective-permute-start.7) | collective-permute-done | bytes 131104 | tf_op jit(solution)/shard_map/ppermute | solution.py:297
  16.8 1.6 %collective-permute-start.13 = (bf16[8,8192]{1,0:T(8,128)(2,1)S(1)}, bf16[8,8192]{1,0:T(8,128)(2,1)S(1)}, u32[]{:S(2)}, u32[]{:S(2)}) collective-permute-start(bf16[8,8192]{1,0:T(8,128)(2,1)S(1)} %collective-permute-done.7.refs_8_), channel_id=1, source_target_pairs={{0,6},{1,7},{2,4},{3,5},{4,2},{5,3},{6,0},{7,1},{8,14},{9,15},{10,... | collective-permute-start | bytes 393224 | tf_op jit(solution)/shard_map/ppermute | solution.py:297
  18.5 0.9 %collective-permute-done.5.refs_6_ = bf16[8,8192]{1,0:T(8,128)(2,1)S(1)} collective-permute-done((bf16[8,8192]{1,0:T(8,128)(2,1)S(1)}, bf16[8,8192]{1,0:T(8,128)(2,1)S(1)}, u32[]{:S(2)}, u32[]{:S(2)}) %collective-permute-start.5) | collective-permute-done | bytes 131104 | tf_op jit(solution)/shard_map/ppermute | solution.py:297
  19.4 1.2 %collective-permute-start.11 = (bf16[8,8192]{1,0:T(8,128)(2,1)S(1)}, bf16[8,8192]{1,0:T(8,128)(2,1)S(1)}, u32[]{:S(2)}, u32[]{:S(2)}) collective-permute-start(bf16[8,8192]{1,0:T(8,128)(2,1)S(1)} %collective-permute-done.7.refs_8_), channel_id=1, source_target_pairs={{0,4},{1,5},{2,6},{3,7},{4,0},{5,1},{6,2},{7,3},{8,12},{9,13},{10,... | collective-permute-start | bytes 393224 | tf_op jit(solution)/shard_map/ppermute | solution.py:297
  20.6 1.2 %collective-permute-done.3.refs_4_ = bf16[8,8192]{1,0:T(8,128)(2,1)S(1)} collective-permute-done((bf16[8,8192]{1,0:T(8,128)(2,1)S(1)}, bf16[8,8192]{1,0:T(8,128)(2,1)S(1)}, u32[]{:S(2)}, u32[]{:S(2)}) %collective-permute-start.3) | collective-permute-done | bytes 131104 | tf_op jit(solution)/shard_map/ppermute | solution.py:297
  21.8 0.9 %collective-permute-start.9 = (bf16[8,8192]{1,0:T(8,128)(2,1)S(1)}, bf16[8,8192]{1,0:T(8,128)(2,1)S(1)}, u32[]{:S(2)}, u32[]{:S(2)}) collective-permute-start(bf16[8,8192]{1,0:T(8,128)(2,1)S(1)} %collective-permute-done.7.refs_8_), channel_id=1, source_target_pairs={{0,2},{1,3},{2,0},{3,1},{4,6},{5,7},{6,4},{7,5},{8,10},{9,11},{10,... | collective-permute-start | bytes 393224 | tf_op jit(solution)/shard_map/ppermute | solution.py:297
  22.8 0.0 collective-permute-start.8
  22.8 0.0 collective-permute-done.refs_1_
  22.8 0.5 %collective-permute-start.6 = (bf16[8,8192]{1,0:T(8,128)(2,1)S(1)}, bf16[8,8192]{1,0:T(8,128)(2,1)S(1)}, u32[]{:S(2)}, u32[]{:S(2)}) collective-permute-start(bf16[8,8192]{1,0:T(8,128)(2,1)S(1)} %collective-permute-done.5.refs_6_), channel_id=1, source_target_pairs={{0,1},{1,0},{2,3},{3,2},{4,5},{5,4},{6,7},{7,6},{8,9},{9,8},{10,11... | collective-permute-start | bytes 393224 | tf_op jit(solution)/shard_map/ppermute | solution.py:297
  23.3 1.7 %collective-permute-done.13.refs_14_ = bf16[8,8192]{1,0:T(8,128)(2,1)S(1)} collective-permute-done((bf16[8,8192]{1,0:T(8,128)(2,1)S(1)}, bf16[8,8192]{1,0:T(8,128)(2,1)S(1)}, u32[]{:S(2)}, u32[]{:S(2)}) %collective-permute-start.13) | collective-permute-done | bytes 131104 | tf_op jit(solution)/shard_map/ppermute | solution.py:297
  25.0 0.0 collective-permute-start.4
  25.0 1.4 %collective-permute-done.11.refs_12_ = bf16[8,8192]{1,0:T(8,128)(2,1)S(1)} collective-permute-done((bf16[8,8192]{1,0:T(8,128)(2,1)S(1)}, bf16[8,8192]{1,0:T(8,128)(2,1)S(1)}, u32[]{:S(2)}, u32[]{:S(2)}) %collective-permute-start.11) | collective-permute-done | bytes 131104 | tf_op jit(solution)/shard_map/ppermute | solution.py:297
  26.4 0.0 collective-permute-start.2
  26.4 0.4 collective-permute-done.9.refs_10_
  26.8 0.2 collective-permute-start.14
  26.9 0.4 collective-permute-start.12
  27.3 0.2 collective-permute-start.10
  27.5 0.3 collective-permute-done.2.refs_3_
  27.8 0.4 collective-permute-done.14.refs_15_
  28.1 0.2 collective-permute-done.12.refs_13_
  28.3 0.3 collective-permute-done.10.refs_11_
  28.6 2.2 %delta.1 = bf16[16,16,512]{2,1,0:T(8,128)(2,1)} custom-call(bf16[8,8192]{1,0:T(8,128)(2,1)S(1)} %get-tuple-element.11.refs_0_, bf16[8,8192]{1,0:T(8,128)(2,1)S(1)} %collective-permute-done.refs_1_, bf16[8,8192]{1,0:T(8,128)(2,1)S(1)} %collective-permute-done.1.refs_2_, bf16[8,8192]{1,0:T(8,128)(2,1)S(1)} %collective-permute-done.2.refs_3_, ...), custom_call_target="tpu_custom_call" | custom-call | flops 301989888 | bytes 6553600 | tf_op jit(solution)/shard_map/delta/pallas_call | solution.py:343
  30.8 5.4 %all-to-all-start = ((bf16[16,16,512]{2,1,0:T(8,128)(2,1)}), bf16[16,16,512]{2,1,0:T(8,128)(2,1)S(1)}, u32[]{:S(2)}, u32[]{:S(2)}) async-start(bf16[16,16,512]{2,1,0:T(8,128)(2,1)} %delta.1), calls=%async_computation | async-start | bytes 524288 | tf_op jit(solution)/shard_map/all_to_all | solution.py:454
  36.2 4.2 %base.1.base_ref = f32[128,512]{1,0:T(8,128)S(1)} custom-call(bf16[8,8192]{1,0:T(8,128)(2,1)S(1)} %get-tuple-element.11.refs_0_, bf16[8,8192]{1,0:T(8,128)(2,1)S(1)} %collective-permute-done.refs_1_, bf16[8,8192]{1,0:T(8,128)(2,1)S(1)} %collective-permute-done.1.refs_2_, bf16[8,8192]{1,0:T(8,128)(2,1)S(1)} %collective-permute-done.2.refs_3_, ...), custom_call_target="tpu_custom_call" | custom-call | flops 1342177280 | bytes 10747904 | tf_op jit(solution)/shard_map/base/pallas_call | solution.py:384
  40.5 2.3 %all-to-all-done.delta_ref = bf16[16,16,512]{2,1,0:T(8,128)(2,1)S(1)} async-done(((bf16[16,16,512]{2,1,0:T(8,128)(2,1)}), bf16[16,16,512]{2,1,0:T(8,128)(2,1)S(1)}, u32[]{:S(2)}, u32[]{:S(2)}) %all-to-all-start) | async-done | bytes 262176 | tf_op jit(solution)/shard_map/all_to_all | solution.py:454
  42.8 0.8 %join.1 = bf16[2,64,512]{2,1,0:T(8,128)(2,1)} custom-call(f32[128,512]{1,0:T(8,128)S(1)} %base.1.base_ref, bf16[128,256]{1,0:T(8,128)(2,1)S(1)} %get-tuple-element.13.place_ref, bf16[16,16,512]{2,1,0:T(8,128)(2,1)S(1)} %all-to-all-done.delta_ref), custom_call_target="tpu_custom_call" | custom-call | tf_op jit(solution)/shard_map/join/pallas_call | solution.py:412
  (4 shorter events, 0.0 us)
Async XLA Ops:
  6.3 10.5 %collective-permute-start.7 = (bf16[8,8192]{1,0:T(8,128)(2,1)S(1)}, bf16[8,8192]{1,0:T(8,128)(2,1)S(1)}, u32[]{:S(2)}, u32[]{:S(2)}) collective-permute-start(bf16[8,8192]{1,0:T(8,128)(2,1)S(1)} %get-tuple-element.11.refs_0_), channel_id=1, source_target_pairs={{0,8},{1,9},{2,10},{3,11},{4,12},{5,13},{6,14},{7,15},{8,0},{9,1},... | collective-permute-start | bytes 393224 | tf_op jit(solution)/shard_map/ppermute | solution.py:297
  10.4 9.0 %collective-permute-start.5 = (bf16[8,8192]{1,0:T(8,128)(2,1)S(1)}, bf16[8,8192]{1,0:T(8,128)(2,1)S(1)}, u32[]{:S(2)}, u32[]{:S(2)}) collective-permute-start(bf16[8,8192]{1,0:T(8,128)(2,1)S(1)} %get-tuple-element.11.refs_0_), channel_id=1, source_target_pairs={{0,6},{1,7},{2,4},{3,5},{4,2},{5,3},{6,0},{7,1},{8,14},{9,15},{10,... | collective-permute-start | bytes 393224 | tf_op jit(solution)/shard_map/ppermute | solution.py:297
  13.0 8.8 %collective-permute-start.3 = (bf16[8,8192]{1,0:T(8,128)(2,1)S(1)}, bf16[8,8192]{1,0:T(8,128)(2,1)S(1)}, u32[]{:S(2)}, u32[]{:S(2)}) collective-permute-start(bf16[8,8192]{1,0:T(8,128)(2,1)S(1)} %get-tuple-element.11.refs_0_), channel_id=1, source_target_pairs={{0,4},{1,5},{2,6},{3,7},{4,0},{5,1},{6,2},{7,3},{8,12},{9,13},{10,... | collective-permute-start | bytes 393224 | tf_op jit(solution)/shard_map/ppermute | solution.py:297
  13.4 9.3 %collective-permute-start.1 = (bf16[8,8192]{1,0:T(8,128)(2,1)S(1)}, bf16[8,8192]{1,0:T(8,128)(2,1)S(1)}, u32[]{:S(2)}, u32[]{:S(2)}) collective-permute-start(bf16[8,8192]{1,0:T(8,128)(2,1)S(1)} %get-tuple-element.11.refs_0_), channel_id=1, source_target_pairs={{0,2},{1,3},{2,0},{3,1},{4,6},{5,7},{6,4},{7,5},{8,10},{9,11},{10,... | collective-permute-start | bytes 393224 | tf_op jit(solution)/shard_map/ppermute | solution.py:297
  13.9 8.8 %collective-permute-start = (bf16[8,8192]{1,0:T(8,128)(2,1)S(1)}, bf16[8,8192]{1,0:T(8,128)(2,1)S(1)}, u32[]{:S(2)}, u32[]{:S(2)}) collective-permute-start(bf16[8,8192]{1,0:T(8,128)(2,1)S(1)} %get-tuple-element.11.refs_0_), channel_id=1, source_target_pairs={{0,1},{1,0},{2,3},{3,2},{4,5},{5,4},{6,7},{7,6},{8,9},{9,8},{10,11... | collective-permute-start | bytes 393224 | tf_op jit(solution)/shard_map/ppermute | solution.py:297
  16.8 8.2 %collective-permute-start.13 = (bf16[8,8192]{1,0:T(8,128)(2,1)S(1)}, bf16[8,8192]{1,0:T(8,128)(2,1)S(1)}, u32[]{:S(2)}, u32[]{:S(2)}) collective-permute-start(bf16[8,8192]{1,0:T(8,128)(2,1)S(1)} %collective-permute-done.7.refs_8_), channel_id=1, source_target_pairs={{0,6},{1,7},{2,4},{3,5},{4,2},{5,3},{6,0},{7,1},{8,14},{9,15},{10,... | collective-permute-start | bytes 393224 | tf_op jit(solution)/shard_map/ppermute | solution.py:297
  19.4 7.0 %collective-permute-start.11 = (bf16[8,8192]{1,0:T(8,128)(2,1)S(1)}, bf16[8,8192]{1,0:T(8,128)(2,1)S(1)}, u32[]{:S(2)}, u32[]{:S(2)}) collective-permute-start(bf16[8,8192]{1,0:T(8,128)(2,1)S(1)} %collective-permute-done.7.refs_8_), channel_id=1, source_target_pairs={{0,4},{1,5},{2,6},{3,7},{4,0},{5,1},{6,2},{7,3},{8,12},{9,13},{10,... | collective-permute-start | bytes 393224 | tf_op jit(solution)/shard_map/ppermute | solution.py:297
  21.8 5.0 %collective-permute-start.9 = (bf16[8,8192]{1,0:T(8,128)(2,1)S(1)}, bf16[8,8192]{1,0:T(8,128)(2,1)S(1)}, u32[]{:S(2)}, u32[]{:S(2)}) collective-permute-start(bf16[8,8192]{1,0:T(8,128)(2,1)S(1)} %collective-permute-done.7.refs_8_), channel_id=1, source_target_pairs={{0,2},{1,3},{2,0},{3,1},{4,6},{5,7},{6,4},{7,5},{8,10},{9,11},{10,... | collective-permute-start | bytes 393224 | tf_op jit(solution)/shard_map/ppermute | solution.py:297
  22.8 4.2 %collective-permute-start.8 = (bf16[8,8192]{1,0:T(8,128)(2,1)S(1)}, bf16[8,8192]{1,0:T(8,128)(2,1)S(1)}, u32[]{:S(2)}, u32[]{:S(2)}) collective-permute-start(bf16[8,8192]{1,0:T(8,128)(2,1)S(1)} %collective-permute-done.7.refs_8_), channel_id=1, source_target_pairs={{0,1},{1,0},{2,3},{3,2},{4,5},{5,4},{6,7},{7,6},{8,9},{9,8},{10,11... | collective-permute-start | bytes 393224 | tf_op jit(solution)/shard_map/ppermute | solution.py:297
  22.8 4.5 %collective-permute-start.6 = (bf16[8,8192]{1,0:T(8,128)(2,1)S(1)}, bf16[8,8192]{1,0:T(8,128)(2,1)S(1)}, u32[]{:S(2)}, u32[]{:S(2)}) collective-permute-start(bf16[8,8192]{1,0:T(8,128)(2,1)S(1)} %collective-permute-done.5.refs_6_), channel_id=1, source_target_pairs={{0,1},{1,0},{2,3},{3,2},{4,5},{5,4},{6,7},{7,6},{8,9},{9,8},{10,11... | collective-permute-start | bytes 393224 | tf_op jit(solution)/shard_map/ppermute | solution.py:297
  25.0 2.5 %collective-permute-start.4 = (bf16[8,8192]{1,0:T(8,128)(2,1)S(1)}, bf16[8,8192]{1,0:T(8,128)(2,1)S(1)}, u32[]{:S(2)}, u32[]{:S(2)}) collective-permute-start(bf16[8,8192]{1,0:T(8,128)(2,1)S(1)} %collective-permute-done.3.refs_4_), channel_id=1, source_target_pairs={{0,1},{1,0},{2,3},{3,2},{4,5},{5,4},{6,7},{7,6},{8,9},{9,8},{10,11... | collective-permute-start | bytes 393224 | tf_op jit(solution)/shard_map/ppermute | solution.py:297
  26.4 1.3 %collective-permute-start.2 = (bf16[8,8192]{1,0:T(8,128)(2,1)S(1)}, bf16[8,8192]{1,0:T(8,128)(2,1)S(1)}, u32[]{:S(2)}, u32[]{:S(2)}) collective-permute-start(bf16[8,8192]{1,0:T(8,128)(2,1)S(1)} %collective-permute-done.1.refs_2_), channel_id=1, source_target_pairs={{0,1},{1,0},{2,3},{3,2},{4,5},{5,4},{6,7},{7,6},{8,9},{9,8},{10,11... | collective-permute-start | bytes 393224 | tf_op jit(solution)/shard_map/ppermute | solution.py:297
  26.8 1.3 %collective-permute-start.14 = (bf16[8,8192]{1,0:T(8,128)(2,1)S(1)}, bf16[8,8192]{1,0:T(8,128)(2,1)S(1)}, u32[]{:S(2)}, u32[]{:S(2)}) collective-permute-start(bf16[8,8192]{1,0:T(8,128)(2,1)S(1)} %collective-permute-done.13.refs_14_), channel_id=1, source_target_pairs={{0,1},{1,0},{2,3},{3,2},{4,5},{5,4},{6,7},{7,6},{8,9},{9,8},{10,11... | collective-permute-start | bytes 393224 | tf_op jit(solution)/shard_map/ppermute | solution.py:297
  26.9 1.4 %collective-permute-start.12 = (bf16[8,8192]{1,0:T(8,128)(2,1)S(1)}, bf16[8,8192]{1,0:T(8,128)(2,1)S(1)}, u32[]{:S(2)}, u32[]{:S(2)}) collective-permute-start(bf16[8,8192]{1,0:T(8,128)(2,1)S(1)} %collective-permute-done.11.refs_12_), channel_id=1, source_target_pairs={{0,1},{1,0},{2,3},{3,2},{4,5},{5,4},{6,7},{7,6},{8,9},{9,8},{10,11... | collective-permute-start | bytes 393224 | tf_op jit(solution)/shard_map/ppermute | solution.py:297
  27.3 1.3 %collective-permute-start.10 = (bf16[8,8192]{1,0:T(8,128)(2,1)S(1)}, bf16[8,8192]{1,0:T(8,128)(2,1)S(1)}, u32[]{:S(2)}, u32[]{:S(2)}) collective-permute-start(bf16[8,8192]{1,0:T(8,128)(2,1)S(1)} %collective-permute-done.9.refs_10_), channel_id=1, source_target_pairs={{0,1},{1,0},{2,3},{3,2},{4,5},{5,4},{6,7},{7,6},{8,9},{9,8},{10,11... | collective-permute-start | bytes 393224 | tf_op jit(solution)/shard_map/ppermute | solution.py:297
  30.8 12.0 %all-to-all-start = ((bf16[16,16,512]{2,1,0:T(8,128)(2,1)}), bf16[16,16,512]{2,1,0:T(8,128)(2,1)S(1)}, u32[]{:S(2)}, u32[]{:S(2)}) async-start(bf16[16,16,512]{2,1,0:T(8,128)(2,1)} %delta.1), calls=%async_computation | async-start | bytes 524288 | tf_op jit(solution)/shard_map/all_to_all | solution.py:454

commit v23 on v20

--- a/solution.py
+++ b/solution.py
@@ -141,11 +141,11 @@
     for r in range(rows):
         queue += [values[r + 1]] if r + 1 < rows else [store]
         queue += [keys[r + 2]] if r + 2 < rows else []
-    for copy in small + queue[0] + queue[1] + queue[2]:
+    for copy in small + queue[0] + queue[1]:
         copy.start()
     for copy in small:
         copy.wait()
-    for copy in queue[3] + queue[4]:
+    for copy in queue[2] + queue[3] + queue[4]:
         copy.start()
     queue = queue[5:]
 

time: 43.5 us -> 43.9 us (level)
  no operation moved by 1% of the time
where the time goes in v23:
time: 43.9 us; the launch traced here: 43.5 us
  starting transfers between devices  18 us (41%)
  Pallas kernels  13.4 us (31%)
  waiting for transfers between devices  12.1 us (28%)
    ppermute x15, starting transfers between devices, swap(): return lax.ppermute(x, 'tensor', [(i, i ^ bits) for i in range(parts)])  12.5 us
    ppermute x15, waiting for transfers between devices, swap(): return lax.ppermute(x, 'tensor', [(i, i ^ bits) for i in range(parts)])  9.76 us
    pallas_call x1, Pallas kernels, attend(): pl.pallas_call(attend_kernel, out_shape=[jax.ShapeDtypeStruct(shape, BF16...  6.17 us
    all_to_all x1, starting transfers between devices, per_device(): lax.all_to_all(send, 'tensor', 0, 0, axis_index_groups=groups, tiled=True)  5.43 us
    pallas_call x1, Pallas kernels, base_part(): pl.pallas_call(functools.partial(base_kernel, at_slot), out_shape=jax.Sha...  4.23 us
    all_to_all x1, waiting for transfers between devices, per_device(): lax.all_to_all(send, 'tensor', 0, 0, axis_index_groups=groups, tiled=True)  2.34 us
    pallas_call x1, Pallas kernels, deltas(): pl.pallas_call(functools.partial(delta_kernel, at_slot), out_shape=jax.Sh...  2.16 us
  transfers between devices with their start and end apart: 16, of which 11 were waited for; matrix products, arithmetic and copies ran while one was open for 0% of the time, Pallas kernels for 10%

profile of v23, /device:TPU:0, one launch (start us, length us, event | category | flops | bytes accessed | tf_op | source)
XLA Modules:
  0.0 43.5 jit_solution(13039127630386880988)
XLA Ops:
  0.0 6.2 %attend.1 = (bf16[8,8192]{1,0:T(8,128)(2,1)S(1)}, bf16[8192,128]{1,0:T(8,128)(2,1)S(1)}, bf16[8192,128]{1,0:T(8,128)(2,1)S(1)}, bf16[16,128]{1,0:T(8,128)(2,1)S(...) custom-call(s32[4]{0:T(128)} %len_hbm.1, bf16[2,4,8192]{2,1,0:T(4,128)(2,1)} %q_hbm.1, ...), custom_call_target="tpu_custom_call" | custom-call | flops 134217728 | bytes 8388608 | tf_op jit(solution)/shard_map/attend/pallas_call | solution.py:252
  6.2 4.1 %collective-permute-start.7 = (bf16[8,8192]{1,0:T(8,128)(2,1)S(1)}, bf16[8,8192]{1,0:T(8,128)(2,1)S(1)}, u32[]{:S(2)}, u32[]{:S(2)}) collective-permute-start(bf16[8,8192]{1,0:T(8,128)(2,1)S(1)} %get-tuple-element.11.refs_0_), channel_id=1, source_target_pairs={{0,8},{1,9},{2,10},{3,11},{4,12},{5,13},{6,14},{7,15},{8,0},{9,1},... | collective-permute-start | bytes 393224 | tf_op jit(solution)/shard_map/ppermute | solution.py:297
  10.3 2.5 %collective-permute-start.5 = (bf16[8,8192]{1,0:T(8,128)(2,1)S(1)}, bf16[8,8192]{1,0:T(8,128)(2,1)S(1)}, u32[]{:S(2)}, u32[]{:S(2)}) collective-permute-start(bf16[8,8192]{1,0:T(8,128)(2,1)S(1)} %get-tuple-element.11.refs_0_), channel_id=1, source_target_pairs={{0,6},{1,7},{2,4},{3,5},{4,2},{5,3},{6,0},{7,1},{8,14},{9,15},{10,... | collective-permute-start | bytes 393224 | tf_op jit(solution)/shard_map/ppermute | solution.py:297
  12.8 0.4 %collective-permute-start.3 = (bf16[8,8192]{1,0:T(8,128)(2,1)S(1)}, bf16[8,8192]{1,0:T(8,128)(2,1)S(1)}, u32[]{:S(2)}, u32[]{:S(2)}) collective-permute-start(bf16[8,8192]{1,0:T(8,128)(2,1)S(1)} %get-tuple-element.11.refs_0_), channel_id=1, source_target_pairs={{0,4},{1,5},{2,6},{3,7},{4,0},{5,1},{6,2},{7,3},{8,12},{9,13},{10,... | collective-permute-start | bytes 393224 | tf_op jit(solution)/shard_map/ppermute | solution.py:297
  13.3 0.5 %collective-permute-start.1 = (bf16[8,8192]{1,0:T(8,128)(2,1)S(1)}, bf16[8,8192]{1,0:T(8,128)(2,1)S(1)}, u32[]{:S(2)}, u32[]{:S(2)}) collective-permute-start(bf16[8,8192]{1,0:T(8,128)(2,1)S(1)} %get-tuple-element.11.refs_0_), channel_id=1, source_target_pairs={{0,2},{1,3},{2,0},{3,1},{4,6},{5,7},{6,4},{7,5},{8,10},{9,11},{10,... | collective-permute-start | bytes 393224 | tf_op jit(solution)/shard_map/ppermute | solution.py:297
  13.8 0.0 collective-permute-start
  13.8 2.9 %collective-permute-done.7.refs_8_ = bf16[8,8192]{1,0:T(8,128)(2,1)S(1)} collective-permute-done((bf16[8,8192]{1,0:T(8,128)(2,1)S(1)}, bf16[8,8192]{1,0:T(8,128)(2,1)S(1)}, u32[]{:S(2)}, u32[]{:S(2)}) %collective-permute-start.7) | collective-permute-done | bytes 131104 | tf_op jit(solution)/shard_map/ppermute | solution.py:297
  16.7 1.6 %collective-permute-start.13 = (bf16[8,8192]{1,0:T(8,128)(2,1)S(1)}, bf16[8,8192]{1,0:T(8,128)(2,1)S(1)}, u32[]{:S(2)}, u32[]{:S(2)}) collective-permute-start(bf16[8,8192]{1,0:T(8,128)(2,1)S(1)} %collective-permute-done.7.refs_8_), channel_id=1, source_target_pairs={{0,6},{1,7},{2,4},{3,5},{4,2},{5,3},{6,0},{7,1},{8,14},{9,15},{10,... | collective-permute-start | bytes 393224 | tf_op jit(solution)/shard_map/ppermute | solution.py:297
  18.3 0.9 %collective-permute-done.5.refs_6_ = bf16[8,8192]{1,0:T(8,128)(2,1)S(1)} collective-permute-done((bf16[8,8192]{1,0:T(8,128)(2,1)S(1)}, bf16[8,8192]{1,0:T(8,128)(2,1)S(1)}, u32[]{:S(2)}, u32[]{:S(2)}) %collective-permute-start.5) | collective-permute-done | bytes 131104 | tf_op jit(solution)/shard_map/ppermute | solution.py:297
  19.2 1.2 %collective-permute-start.11 = (bf16[8,8192]{1,0:T(8,128)(2,1)S(1)}, bf16[8,8192]{1,0:T(8,128)(2,1)S(1)}, u32[]{:S(2)}, u32[]{:S(2)}) collective-permute-start(bf16[8,8192]{1,0:T(8,128)(2,1)S(1)} %collective-permute-done.7.refs_8_), channel_id=1, source_target_pairs={{0,4},{1,5},{2,6},{3,7},{4,0},{5,1},{6,2},{7,3},{8,12},{9,13},{10,... | collective-permute-start | bytes 393224 | tf_op jit(solution)/shard_map/ppermute | solution.py:297
  20.4 1.2 %collective-permute-done.3.refs_4_ = bf16[8,8192]{1,0:T(8,128)(2,1)S(1)} collective-permute-done((bf16[8,8192]{1,0:T(8,128)(2,1)S(1)}, bf16[8,8192]{1,0:T(8,128)(2,1)S(1)}, u32[]{:S(2)}, u32[]{:S(2)}) %collective-permute-start.3) | collective-permute-done | bytes 131104 | tf_op jit(solution)/shard_map/ppermute | solution.py:297
  21.7 0.9 %collective-permute-start.9 = (bf16[8,8192]{1,0:T(8,128)(2,1)S(1)}, bf16[8,8192]{1,0:T(8,128)(2,1)S(1)}, u32[]{:S(2)}, u32[]{:S(2)}) collective-permute-start(bf16[8,8192]{1,0:T(8,128)(2,1)S(1)} %collective-permute-done.7.refs_8_), channel_id=1, source_target_pairs={{0,2},{1,3},{2,0},{3,1},{4,6},{5,7},{6,4},{7,5},{8,10},{9,11},{10,... | collective-permute-start | bytes 393224 | tf_op jit(solution)/shard_map/ppermute | solution.py:297
  22.6 0.0 collective-permute-done.1.refs_2_
  22.6 0.0 collective-permute-start.8
  22.6 0.5 %collective-permute-start.6 = (bf16[8,8192]{1,0:T(8,128)(2,1)S(1)}, bf16[8,8192]{1,0:T(8,128)(2,1)S(1)}, u32[]{:S(2)}, u32[]{:S(2)}) collective-permute-start(bf16[8,8192]{1,0:T(8,128)(2,1)S(1)} %collective-permute-done.5.refs_6_), channel_id=1, source_target_pairs={{0,1},{1,0},{2,3},{3,2},{4,5},{5,4},{6,7},{7,6},{8,9},{9,8},{10,11... | collective-permute-start | bytes 393224 | tf_op jit(solution)/shard_map/ppermute | solution.py:297
  23.1 1.7 %collective-permute-done.13.refs_14_ = bf16[8,8192]{1,0:T(8,128)(2,1)S(1)} collective-permute-done((bf16[8,8192]{1,0:T(8,128)(2,1)S(1)}, bf16[8,8192]{1,0:T(8,128)(2,1)S(1)}, u32[]{:S(2)}, u32[]{:S(2)}) %collective-permute-start.13) | collective-permute-done | bytes 131104 | tf_op jit(solution)/shard_map/ppermute | solution.py:297
  24.9 1.4 %collective-permute-done.11.refs_12_ = bf16[8,8192]{1,0:T(8,128)(2,1)S(1)} collective-permute-done((bf16[8,8192]{1,0:T(8,128)(2,1)S(1)}, bf16[8,8192]{1,0:T(8,128)(2,1)S(1)}, u32[]{:S(2)}, u32[]{:S(2)}) %collective-permute-start.11) | collective-permute-done | bytes 131104 | tf_op jit(solution)/shard_map/ppermute | solution.py:297
  26.3 0.0 collective-permute-start.2
  26.3 0.4 collective-permute-done.9.refs_10_
  26.6 0.2 collective-permute-start.14
  26.8 0.0 collective-permute-done.8.refs_9_
  26.8 0.4 collective-permute-start.12
  27.1 0.2 collective-permute-start.10
  27.3 0.3 collective-permute-done.2.refs_3_
  27.6 0.4 collective-permute-done.14.refs_15_
  28.0 0.2 collective-permute-done.12.refs_13_
  28.2 0.3 collective-permute-done.10.refs_11_
  28.5 2.2 %delta.1 = bf16[16,16,512]{2,1,0:T(8,128)(2,1)} custom-call(bf16[8,8192]{1,0:T(8,128)(2,1)S(1)} %get-tuple-element.11.refs_0_, bf16[8,8192]{1,0:T(8,128)(2,1)S(1)} %collective-permute-done.refs_1_, bf16[8,8192]{1,0:T(8,128)(2,1)S(1)} %collective-permute-done.1.refs_2_, bf16[8,8192]{1,0:T(8,128)(2,1)S(1)} %collective-permute-done.2.refs_3_, ...), custom_call_target="tpu_custom_call" | custom-call | flops 301989888 | bytes 6553600 | tf_op jit(solution)/shard_map/delta/pallas_call | solution.py:343
  30.7 5.4 %all-to-all-start = ((bf16[16,16,512]{2,1,0:T(8,128)(2,1)}), bf16[16,16,512]{2,1,0:T(8,128)(2,1)S(1)}, u32[]{:S(2)}, u32[]{:S(2)}) async-start(bf16[16,16,512]{2,1,0:T(8,128)(2,1)} %delta.1), calls=%async_computation | async-start | bytes 524288 | tf_op jit(solution)/shard_map/all_to_all | solution.py:454
  36.1 4.2 %base.1.base_ref = f32[128,512]{1,0:T(8,128)S(1)} custom-call(bf16[8,8192]{1,0:T(8,128)(2,1)S(1)} %get-tuple-element.11.refs_0_, bf16[8,8192]{1,0:T(8,128)(2,1)S(1)} %collective-permute-done.refs_1_, bf16[8,8192]{1,0:T(8,128)(2,1)S(1)} %collective-permute-done.1.refs_2_, bf16[8,8192]{1,0:T(8,128)(2,1)S(1)} %collective-permute-done.2.refs_3_, ...), custom_call_target="tpu_custom_call" | custom-call | flops 1342177280 | bytes 10747904 | tf_op jit(solution)/shard_map/base/pallas_call | solution.py:384
  40.3 2.3 %all-to-all-done.delta_ref = bf16[16,16,512]{2,1,0:T(8,128)(2,1)S(1)} async-done(((bf16[16,16,512]{2,1,0:T(8,128)(2,1)}), bf16[16,16,512]{2,1,0:T(8,128)(2,1)S(1)}, u32[]{:S(2)}, u32[]{:S(2)}) %all-to-all-start) | async-done | bytes 262176 | tf_op jit(solution)/shard_map/all_to_all | solution.py:454
  42.7 0.8 %join.1 = bf16[2,64,512]{2,1,0:T(8,128)(2,1)} custom-call(f32[128,512]{1,0:T(8,128)S(1)} %base.1.base_ref, bf16[128,256]{1,0:T(8,128)(2,1)S(1)} %get-tuple-element.13.place_ref, bf16[16,16,512]{2,1,0:T(8,128)(2,1)S(1)} %all-to-all-done.delta_ref), custom_call_target="tpu_custom_call" | custom-call | tf_op jit(solution)/shard_map/join/pallas_call | solution.py:412
  (4 shorter events, 0.0 us)
Async XLA Ops:
  6.2 10.5 %collective-permute-start.7 = (bf16[8,8192]{1,0:T(8,128)(2,1)S(1)}, bf16[8,8192]{1,0:T(8,128)(2,1)S(1)}, u32[]{:S(2)}, u32[]{:S(2)}) collective-permute-start(bf16[8,8192]{1,0:T(8,128)(2,1)S(1)} %get-tuple-element.11.refs_0_), channel_id=1, source_target_pairs={{0,8},{1,9},{2,10},{3,11},{4,12},{5,13},{6,14},{7,15},{8,0},{9,1},... | collective-permute-start | bytes 393224 | tf_op jit(solution)/shard_map/ppermute | solution.py:297
  10.3 9.0 %collective-permute-start.5 = (bf16[8,8192]{1,0:T(8,128)(2,1)S(1)}, bf16[8,8192]{1,0:T(8,128)(2,1)S(1)}, u32[]{:S(2)}, u32[]{:S(2)}) collective-permute-start(bf16[8,8192]{1,0:T(8,128)(2,1)S(1)} %get-tuple-element.11.refs_0_), channel_id=1, source_target_pairs={{0,6},{1,7},{2,4},{3,5},{4,2},{5,3},{6,0},{7,1},{8,14},{9,15},{10,... | collective-permute-start | bytes 393224 | tf_op jit(solution)/shard_map/ppermute | solution.py:297
  12.8 8.8 %collective-permute-start.3 = (bf16[8,8192]{1,0:T(8,128)(2,1)S(1)}, bf16[8,8192]{1,0:T(8,128)(2,1)S(1)}, u32[]{:S(2)}, u32[]{:S(2)}) collective-permute-start(bf16[8,8192]{1,0:T(8,128)(2,1)S(1)} %get-tuple-element.11.refs_0_), channel_id=1, source_target_pairs={{0,4},{1,5},{2,6},{3,7},{4,0},{5,1},{6,2},{7,3},{8,12},{9,13},{10,... | collective-permute-start | bytes 393224 | tf_op jit(solution)/shard_map/ppermute | solution.py:297
  13.3 9.3 %collective-permute-start.1 = (bf16[8,8192]{1,0:T(8,128)(2,1)S(1)}, bf16[8,8192]{1,0:T(8,128)(2,1)S(1)}, u32[]{:S(2)}, u32[]{:S(2)}) collective-permute-start(bf16[8,8192]{1,0:T(8,128)(2,1)S(1)} %get-tuple-element.11.refs_0_), channel_id=1, source_target_pairs={{0,2},{1,3},{2,0},{3,1},{4,6},{5,7},{6,4},{7,5},{8,10},{9,11},{10,... | collective-permute-start | bytes 393224 | tf_op jit(solution)/shard_map/ppermute | solution.py:297
  13.8 8.8 %collective-permute-start = (bf16[8,8192]{1,0:T(8,128)(2,1)S(1)}, bf16[8,8192]{1,0:T(8,128)(2,1)S(1)}, u32[]{:S(2)}, u32[]{:S(2)}) collective-permute-start(bf16[8,8192]{1,0:T(8,128)(2,1)S(1)} %get-tuple-element.11.refs_0_), channel_id=1, source_target_pairs={{0,1},{1,0},{2,3},{3,2},{4,5},{5,4},{6,7},{7,6},{8,9},{9,8},{10,11... | collective-permute-start | bytes 393224 | tf_op jit(solution)/shard_map/ppermute | solution.py:297
  16.7 8.2 %collective-permute-start.13 = (bf16[8,8192]{1,0:T(8,128)(2,1)S(1)}, bf16[8,8192]{1,0:T(8,128)(2,1)S(1)}, u32[]{:S(2)}, u32[]{:S(2)}) collective-permute-start(bf16[8,8192]{1,0:T(8,128)(2,1)S(1)} %collective-permute-done.7.refs_8_), channel_id=1, source_target_pairs={{0,6},{1,7},{2,4},{3,5},{4,2},{5,3},{6,0},{7,1},{8,14},{9,15},{10,... | collective-permute-start | bytes 393224 | tf_op jit(solution)/shard_map/ppermute | solution.py:297
  19.2 7.0 %collective-permute-start.11 = (bf16[8,8192]{1,0:T(8,128)(2,1)S(1)}, bf16[8,8192]{1,0:T(8,128)(2,1)S(1)}, u32[]{:S(2)}, u32[]{:S(2)}) collective-permute-start(bf16[8,8192]{1,0:T(8,128)(2,1)S(1)} %collective-permute-done.7.refs_8_), channel_id=1, source_target_pairs={{0,4},{1,5},{2,6},{3,7},{4,0},{5,1},{6,2},{7,3},{8,12},{9,13},{10,... | collective-permute-start | bytes 393224 | tf_op jit(solution)/shard_map/ppermute | solution.py:297
  21.7 5.0 %collective-permute-start.9 = (bf16[8,8192]{1,0:T(8,128)(2,1)S(1)}, bf16[8,8192]{1,0:T(8,128)(2,1)S(1)}, u32[]{:S(2)}, u32[]{:S(2)}) collective-permute-start(bf16[8,8192]{1,0:T(8,128)(2,1)S(1)} %collective-permute-done.7.refs_8_), channel_id=1, source_target_pairs={{0,2},{1,3},{2,0},{3,1},{4,6},{5,7},{6,4},{7,5},{8,10},{9,11},{10,... | collective-permute-start | bytes 393224 | tf_op jit(solution)/shard_map/ppermute | solution.py:297
  22.6 4.2 %collective-permute-start.8 = (bf16[8,8192]{1,0:T(8,128)(2,1)S(1)}, bf16[8,8192]{1,0:T(8,128)(2,1)S(1)}, u32[]{:S(2)}, u32[]{:S(2)}) collective-permute-start(bf16[8,8192]{1,0:T(8,128)(2,1)S(1)} %collective-permute-done.7.refs_8_), channel_id=1, source_target_pairs={{0,1},{1,0},{2,3},{3,2},{4,5},{5,4},{6,7},{7,6},{8,9},{9,8},{10,11... | collective-permute-start | bytes 393224 | tf_op jit(solution)/shard_map/ppermute | solution.py:297
  22.6 4.5 %collective-permute-start.6 = (bf16[8,8192]{1,0:T(8,128)(2,1)S(1)}, bf16[8,8192]{1,0:T(8,128)(2,1)S(1)}, u32[]{:S(2)}, u32[]{:S(2)}) collective-permute-start(bf16[8,8192]{1,0:T(8,128)(2,1)S(1)} %collective-permute-done.5.refs_6_), channel_id=1, source_target_pairs={{0,1},{1,0},{2,3},{3,2},{4,5},{5,4},{6,7},{7,6},{8,9},{9,8},{10,11... | collective-permute-start | bytes 393224 | tf_op jit(solution)/shard_map/ppermute | solution.py:297
  24.8 2.5 %collective-permute-start.4 = (bf16[8,8192]{1,0:T(8,128)(2,1)S(1)}, bf16[8,8192]{1,0:T(8,128)(2,1)S(1)}, u32[]{:S(2)}, u32[]{:S(2)}) collective-permute-start(bf16[8,8192]{1,0:T(8,128)(2,1)S(1)} %collective-permute-done.3.refs_4_), channel_id=1, source_target_pairs={{0,1},{1,0},{2,3},{3,2},{4,5},{5,4},{6,7},{7,6},{8,9},{9,8},{10,11... | collective-permute-start | bytes 393224 | tf_op jit(solution)/shard_map/ppermute | solution.py:297
  26.3 1.3 %collective-permute-start.2 = (bf16[8,8192]{1,0:T(8,128)(2,1)S(1)}, bf16[8,8192]{1,0:T(8,128)(2,1)S(1)}, u32[]{:S(2)}, u32[]{:S(2)}) collective-permute-start(bf16[8,8192]{1,0:T(8,128)(2,1)S(1)} %collective-permute-done.1.refs_2_), channel_id=1, source_target_pairs={{0,1},{1,0},{2,3},{3,2},{4,5},{5,4},{6,7},{7,6},{8,9},{9,8},{10,11... | collective-permute-start | bytes 393224 | tf_op jit(solution)/shard_map/ppermute | solution.py:297
  26.6 1.3 %collective-permute-start.14 = (bf16[8,8192]{1,0:T(8,128)(2,1)S(1)}, bf16[8,8192]{1,0:T(8,128)(2,1)S(1)}, u32[]{:S(2)}, u32[]{:S(2)}) collective-permute-start(bf16[8,8192]{1,0:T(8,128)(2,1)S(1)} %collective-permute-done.13.refs_14_), channel_id=1, source_target_pairs={{0,1},{1,0},{2,3},{3,2},{4,5},{5,4},{6,7},{7,6},{8,9},{9,8},{10,11... | collective-permute-start | bytes 393224 | tf_op jit(solution)/shard_map/ppermute | solution.py:297
  26.8 1.4 %collective-permute-start.12 = (bf16[8,8192]{1,0:T(8,128)(2,1)S(1)}, bf16[8,8192]{1,0:T(8,128)(2,1)S(1)}, u32[]{:S(2)}, u32[]{:S(2)}) collective-permute-start(bf16[8,8192]{1,0:T(8,128)(2,1)S(1)} %collective-permute-done.11.refs_12_), channel_id=1, source_target_pairs={{0,1},{1,0},{2,3},{3,2},{4,5},{5,4},{6,7},{7,6},{8,9},{9,8},{10,11... | collective-permute-start | bytes 393224 | tf_op jit(solution)/shard_map/ppermute | solution.py:297
  27.1 1.3 %collective-permute-start.10 = (bf16[8,8192]{1,0:T(8,128)(2,1)S(1)}, bf16[8,8192]{1,0:T(8,128)(2,1)S(1)}, u32[]{:S(2)}, u32[]{:S(2)}) collective-permute-start(bf16[8,8192]{1,0:T(8,128)(2,1)S(1)} %collective-permute-done.9.refs_10_), channel_id=1, source_target_pairs={{0,1},{1,0},{2,3},{3,2},{4,5},{5,4},{6,7},{7,6},{8,9},{9,8},{10,11... | collective-permute-start | bytes 393224 | tf_op jit(solution)/shard_map/ppermute | solution.py:297
  30.7 12.0 %all-to-all-start = ((bf16[16,16,512]{2,1,0:T(8,128)(2,1)}), bf16[16,16,512]{2,1,0:T(8,128)(2,1)S(1)}, u32[]{:S(2)}, u32[]{:S(2)}) async-start(bf16[16,16,512]{2,1,0:T(8,128)(2,1)} %delta.1), calls=%async_computation | async-start | bytes 524288 | tf_op jit(solution)/shard_map/all_to_all | solution.py:454

commit v24 on v20

--- a/solution.py
+++ b/solution.py
@@ -15,7 +15,7 @@
 MOST = 8
 RING = 16
 ORDER = [0, 1, 2, 3, 4, 5, 6, 7, 8, 9, 10, 11, 12, 13, 14, 15]
-EXCHANGE = [11, 10, 9, 8, 15, 14, 13, 12, 7, 6, 5, 4, 3, 2, 1, 0]
+EXCHANGE = [7, 6, 5, 4, 11, 10, 9, 8, 15, 14, 13, 12, 3, 2, 1, 0]
 F32 = jnp.float32
 BF16 = jnp.bfloat16
 NT = (((1,), (1,)), ((), ()))

time: 43.5 us -> 44 us (1.011)
  the two profiles are of different devices: /device:TPU:0 before, /device:TPU:1 now
where the time goes in v24:
time: 44 us; the launch traced here: 43.8 us
  starting transfers between devices  23.3 us (53%)
  Pallas kernels  13.1 us (30%)
  waiting for transfers between devices  7.42 us (17%)
    ppermute x15, starting transfers between devices, swap(): return lax.ppermute(x, 'tensor', [(i, i ^ bits) for i in range(parts)])  17.9 us
    pallas_call x1, Pallas kernels, attend(): pl.pallas_call(attend_kernel, out_shape=[jax.ShapeDtypeStruct(shape, BF16...  5.8 us
    all_to_all x1, starting transfers between devices, per_device(): lax.all_to_all(send, 'tensor', 0, 0, axis_index_groups=groups, tiled=True)  5.32 us
    pallas_call x1, Pallas kernels, base_part(): pl.pallas_call(functools.partial(base_kernel, at_slot), out_shape=jax.Sha...  4.25 us
    ppermute x15, waiting for transfers between devices, swap(): return lax.ppermute(x, 'tensor', [(i, i ^ bits) for i in range(parts)])  4.08 us
    all_to_all x1, waiting for transfers between devices, per_device(): lax.all_to_all(send, 'tensor', 0, 0, axis_index_groups=groups, tiled=True)  3.34 us
    pallas_call x1, Pallas kernels, deltas(): pl.pallas_call(functools.partial(delta_kernel, at_slot), out_shape=jax.Sh...  2.16 us
  transfers between devices with their start and end apart: 16, of which 7 were waited for; matrix products, arithmetic and copies ran while one was open for 0% of the time, Pallas kernels for 10%

profile of v24, /device:TPU:1, one launch (start us, length us, event | category | flops | bytes accessed | tf_op | source)
XLA Modules:
  0.0 43.8 jit_solution(2751341469749154172)
XLA Ops:
  0.0 5.8 %attend.1 = (bf16[8,8192]{1,0:T(8,128)(2,1)S(1)}, bf16[8192,128]{1,0:T(8,128)(2,1)S(1)}, bf16[8192,128]{1,0:T(8,128)(2,1)S(1)}, bf16[16,128]{1,0:T(8,128)(2,1)S(...) custom-call(s32[4]{0:T(128)} %len_hbm.1, bf16[2,4,8192]{2,1,0:T(4,128)(2,1)} %q_hbm.1, ...), custom_call_target="tpu_custom_call" | custom-call | flops 134217728 | bytes 8388608 | tf_op jit(solution)/shard_map/attend/pallas_call | solution.py:252
  5.8 3.2 %collective-permute-start.7 = (bf16[8,8192]{1,0:T(8,128)(2,1)S(1)}, bf16[8,8192]{1,0:T(8,128)(2,1)S(1)}, u32[]{:S(2)}, u32[]{:S(2)}) collective-permute-start(bf16[8,8192]{1,0:T(8,128)(2,1)S(1)} %get-tuple-element.11.refs_0_), channel_id=1, source_target_pairs={{0,8},{1,9},{2,10},{3,11},{4,12},{5,13},{6,14},{7,15},{8,0},{9,1},... | collective-permute-start | bytes 393224 | tf_op jit(solution)/shard_map/ppermute | solution.py:297
  9.0 2.3 %collective-permute-start.5 = (bf16[8,8192]{1,0:T(8,128)(2,1)S(1)}, bf16[8,8192]{1,0:T(8,128)(2,1)S(1)}, u32[]{:S(2)}, u32[]{:S(2)}) collective-permute-start(bf16[8,8192]{1,0:T(8,128)(2,1)S(1)} %get-tuple-element.11.refs_0_), channel_id=1, source_target_pairs={{0,6},{1,7},{2,4},{3,5},{4,2},{5,3},{6,0},{7,1},{8,14},{9,15},{10,... | collective-permute-start | bytes 393224 | tf_op jit(solution)/shard_map/ppermute | solution.py:297
  11.3 0.2 collective-permute-start.3
  11.4 0.2 collective-permute-start.1
  11.7 1.8 %collective-permute-start = (bf16[8,8192]{1,0:T(8,128)(2,1)S(1)}, bf16[8,8192]{1,0:T(8,128)(2,1)S(1)}, u32[]{:S(2)}, u32[]{:S(2)}) collective-permute-start(bf16[8,8192]{1,0:T(8,128)(2,1)S(1)} %get-tuple-element.11.refs_0_), channel_id=1, source_target_pairs={{0,1},{1,0},{2,3},{3,2},{4,5},{5,4},{6,7},{7,6},{8,9},{9,8},{10,11... | collective-permute-start | bytes 393224 | tf_op jit(solution)/shard_map/ppermute | solution.py:297
  13.5 1.3 %collective-permute-done.7.refs_8_ = bf16[8,8192]{1,0:T(8,128)(2,1)S(1)} collective-permute-done((bf16[8,8192]{1,0:T(8,128)(2,1)S(1)}, bf16[8,8192]{1,0:T(8,128)(2,1)S(1)}, u32[]{:S(2)}, u32[]{:S(2)}) %collective-permute-start.7) | collective-permute-done | bytes 131104 | tf_op jit(solution)/shard_map/ppermute | solution.py:297
  14.8 2.4 %collective-permute-start.13 = (bf16[8,8192]{1,0:T(8,128)(2,1)S(1)}, bf16[8,8192]{1,0:T(8,128)(2,1)S(1)}, u32[]{:S(2)}, u32[]{:S(2)}) collective-permute-start(bf16[8,8192]{1,0:T(8,128)(2,1)S(1)} %collective-permute-done.7.refs_8_), channel_id=1, source_target_pairs={{0,6},{1,7},{2,4},{3,5},{4,2},{5,3},{6,0},{7,1},{8,14},{9,15},{10,... | collective-permute-start | bytes 393224 | tf_op jit(solution)/shard_map/ppermute | solution.py:297
  17.2 0.0 collective-permute-start.11
  17.2 1.7 %collective-permute-done.3.refs_4_ = bf16[8,8192]{1,0:T(8,128)(2,1)S(1)} collective-permute-done((bf16[8,8192]{1,0:T(8,128)(2,1)S(1)}, bf16[8,8192]{1,0:T(8,128)(2,1)S(1)}, u32[]{:S(2)}, u32[]{:S(2)}) %collective-permute-start.3) | collective-permute-done | bytes 131104 | tf_op jit(solution)/shard_map/ppermute | solution.py:297
  18.9 0.0 collective-permute-start.9
  18.9 0.0 collective-permute-done.1.refs_2_
  18.9 3.4 %collective-permute-start.8 = (bf16[8,8192]{1,0:T(8,128)(2,1)S(1)}, bf16[8,8192]{1,0:T(8,128)(2,1)S(1)}, u32[]{:S(2)}, u32[]{:S(2)}) collective-permute-start(bf16[8,8192]{1,0:T(8,128)(2,1)S(1)} %collective-permute-done.7.refs_8_), channel_id=1, source_target_pairs={{0,1},{1,0},{2,3},{3,2},{4,5},{5,4},{6,7},{7,6},{8,9},{9,8},{10,11... | collective-permute-start | bytes 393224 | tf_op jit(solution)/shard_map/ppermute | solution.py:297
  22.3 0.0 collective-permute-done.refs_1_
  22.3 0.1 collective-permute-start.6
  22.4 2.2 %collective-permute-start.4 = (bf16[8,8192]{1,0:T(8,128)(2,1)S(1)}, bf16[8,8192]{1,0:T(8,128)(2,1)S(1)}, u32[]{:S(2)}, u32[]{:S(2)}) collective-permute-start(bf16[8,8192]{1,0:T(8,128)(2,1)S(1)} %collective-permute-done.3.refs_4_), channel_id=1, source_target_pairs={{0,1},{1,0},{2,3},{3,2},{4,5},{5,4},{6,7},{7,6},{8,9},{9,8},{10,11... | collective-permute-start | bytes 393224 | tf_op jit(solution)/shard_map/ppermute | solution.py:297
  24.5 0.0 collective-permute-done.11.refs_12_
  24.5 1.4 %collective-permute-start.2 = (bf16[8,8192]{1,0:T(8,128)(2,1)S(1)}, bf16[8,8192]{1,0:T(8,128)(2,1)S(1)}, u32[]{:S(2)}, u32[]{:S(2)}) collective-permute-start(bf16[8,8192]{1,0:T(8,128)(2,1)S(1)} %collective-permute-done.1.refs_2_), channel_id=1, source_target_pairs={{0,1},{1,0},{2,3},{3,2},{4,5},{5,4},{6,7},{7,6},{8,9},{9,8},{10,11... | collective-permute-start | bytes 393224 | tf_op jit(solution)/shard_map/ppermute | solution.py:297
  26.0 0.4 collective-permute-start.14
  26.3 0.2 collective-permute-start.12
  26.5 0.0 collective-permute-done.6.refs_7_
  26.5 0.4 collective-permute-start.10
  26.8 0.0 collective-permute-done.4.refs_5_
  26.8 0.1 collective-permute-done.2.refs_3_
  26.9 0.4 collective-permute-done.14.refs_15_
  27.3 0.4 collective-permute-done.12.refs_13_
  27.7 0.2 collective-permute-done.10.refs_11_
  27.9 2.2 %delta.1 = bf16[16,16,512]{2,1,0:T(8,128)(2,1)} custom-call(bf16[8,8192]{1,0:T(8,128)(2,1)S(1)} %get-tuple-element.11.refs_0_, bf16[8,8192]{1,0:T(8,128)(2,1)S(1)} %collective-permute-done.refs_1_, bf16[8,8192]{1,0:T(8,128)(2,1)S(1)} %collective-permute-done.1.refs_2_, bf16[8,8192]{1,0:T(8,128)(2,1)S(1)} %collective-permute-done.2.refs_3_, ...), custom_call_target="tpu_custom_call" | custom-call | flops 301989888 | bytes 6553600 | tf_op jit(solution)/shard_map/delta/pallas_call | solution.py:343
  30.0 5.3 %all-to-all-start = ((bf16[16,16,512]{2,1,0:T(8,128)(2,1)}), bf16[16,16,512]{2,1,0:T(8,128)(2,1)S(1)}, u32[]{:S(2)}, u32[]{:S(2)}) async-start(bf16[16,16,512]{2,1,0:T(8,128)(2,1)} %delta.1), calls=%async_computation | async-start | bytes 524288 | tf_op jit(solution)/shard_map/all_to_all | solution.py:454
  35.3 4.3 %base.1.base_ref = f32[128,512]{1,0:T(8,128)S(1)} custom-call(bf16[8,8192]{1,0:T(8,128)(2,1)S(1)} %get-tuple-element.11.refs_0_, bf16[8,8192]{1,0:T(8,128)(2,1)S(1)} %collective-permute-done.refs_1_, bf16[8,8192]{1,0:T(8,128)(2,1)S(1)} %collective-permute-done.1.refs_2_, bf16[8,8192]{1,0:T(8,128)(2,1)S(1)} %collective-permute-done.2.refs_3_, ...), custom_call_target="tpu_custom_call" | custom-call | flops 1342177280 | bytes 10747904 | tf_op jit(solution)/shard_map/base/pallas_call | solution.py:384
  39.6 3.3 %all-to-all-done.delta_ref = bf16[16,16,512]{2,1,0:T(8,128)(2,1)S(1)} async-done(((bf16[16,16,512]{2,1,0:T(8,128)(2,1)}), bf16[16,16,512]{2,1,0:T(8,128)(2,1)S(1)}, u32[]{:S(2)}, u32[]{:S(2)}) %all-to-all-start) | async-done | bytes 262176 | tf_op jit(solution)/shard_map/all_to_all | solution.py:454
  42.9 0.8 %join.1 = bf16[2,64,512]{2,1,0:T(8,128)(2,1)} custom-call(f32[128,512]{1,0:T(8,128)S(1)} %base.1.base_ref, bf16[128,256]{1,0:T(8,128)(2,1)S(1)} %get-tuple-element.13.place_ref, bf16[16,16,512]{2,1,0:T(8,128)(2,1)S(1)} %all-to-all-done.delta_ref), custom_call_target="tpu_custom_call" | custom-call | tf_op jit(solution)/shard_map/join/pallas_call | solution.py:412
  (4 shorter events, 0.0 us)
Async XLA Ops:
  5.8 9.0 %collective-permute-start.7 = (bf16[8,8192]{1,0:T(8,128)(2,1)S(1)}, bf16[8,8192]{1,0:T(8,128)(2,1)S(1)}, u32[]{:S(2)}, u32[]{:S(2)}) collective-permute-start(bf16[8,8192]{1,0:T(8,128)(2,1)S(1)} %get-tuple-element.11.refs_0_), channel_id=1, source_target_pairs={{0,8},{1,9},{2,10},{3,11},{4,12},{5,13},{6,14},{7,15},{8,0},{9,1},... | collective-permute-start | bytes 393224 | tf_op jit(solution)/shard_map/ppermute | solution.py:297
  9.0 8.2 %collective-permute-start.5 = (bf16[8,8192]{1,0:T(8,128)(2,1)S(1)}, bf16[8,8192]{1,0:T(8,128)(2,1)S(1)}, u32[]{:S(2)}, u32[]{:S(2)}) collective-permute-start(bf16[8,8192]{1,0:T(8,128)(2,1)S(1)} %get-tuple-element.11.refs_0_), channel_id=1, source_target_pairs={{0,6},{1,7},{2,4},{3,5},{4,2},{5,3},{6,0},{7,1},{8,14},{9,15},{10,... | collective-permute-start | bytes 393224 | tf_op jit(solution)/shard_map/ppermute | solution.py:297
  11.3 7.7 %collective-permute-start.3 = (bf16[8,8192]{1,0:T(8,128)(2,1)S(1)}, bf16[8,8192]{1,0:T(8,128)(2,1)S(1)}, u32[]{:S(2)}, u32[]{:S(2)}) collective-permute-start(bf16[8,8192]{1,0:T(8,128)(2,1)S(1)} %get-tuple-element.11.refs_0_), channel_id=1, source_target_pairs={{0,4},{1,5},{2,6},{3,7},{4,0},{5,1},{6,2},{7,3},{8,12},{9,13},{10,... | collective-permute-start | bytes 393224 | tf_op jit(solution)/shard_map/ppermute | solution.py:297
  11.4 7.5 %collective-permute-start.1 = (bf16[8,8192]{1,0:T(8,128)(2,1)S(1)}, bf16[8,8192]{1,0:T(8,128)(2,1)S(1)}, u32[]{:S(2)}, u32[]{:S(2)}) collective-permute-start(bf16[8,8192]{1,0:T(8,128)(2,1)S(1)} %get-tuple-element.11.refs_0_), channel_id=1, source_target_pairs={{0,2},{1,3},{2,0},{3,1},{4,6},{5,7},{6,4},{7,5},{8,10},{9,11},{10,... | collective-permute-start | bytes 393224 | tf_op jit(solution)/shard_map/ppermute | solution.py:297
  11.7 10.6 %collective-permute-start = (bf16[8,8192]{1,0:T(8,128)(2,1)S(1)}, bf16[8,8192]{1,0:T(8,128)(2,1)S(1)}, u32[]{:S(2)}, u32[]{:S(2)}) collective-permute-start(bf16[8,8192]{1,0:T(8,128)(2,1)S(1)} %get-tuple-element.11.refs_0_), channel_id=1, source_target_pairs={{0,1},{1,0},{2,3},{3,2},{4,5},{5,4},{6,7},{7,6},{8,9},{9,8},{10,11... | collective-permute-start | bytes 393224 | tf_op jit(solution)/shard_map/ppermute | solution.py:297
  14.8 7.6 %collective-permute-start.13 = (bf16[8,8192]{1,0:T(8,128)(2,1)S(1)}, bf16[8,8192]{1,0:T(8,128)(2,1)S(1)}, u32[]{:S(2)}, u32[]{:S(2)}) collective-permute-start(bf16[8,8192]{1,0:T(8,128)(2,1)S(1)} %collective-permute-done.7.refs_8_), channel_id=1, source_target_pairs={{0,6},{1,7},{2,4},{3,5},{4,2},{5,3},{6,0},{7,1},{8,14},{9,15},{10,... | collective-permute-start | bytes 393224 | tf_op jit(solution)/shard_map/ppermute | solution.py:297
  17.2 7.3 %collective-permute-start.11 = (bf16[8,8192]{1,0:T(8,128)(2,1)S(1)}, bf16[8,8192]{1,0:T(8,128)(2,1)S(1)}, u32[]{:S(2)}, u32[]{:S(2)}) collective-permute-start(bf16[8,8192]{1,0:T(8,128)(2,1)S(1)} %collective-permute-done.7.refs_8_), channel_id=1, source_target_pairs={{0,4},{1,5},{2,6},{3,7},{4,0},{5,1},{6,2},{7,3},{8,12},{9,13},{10,... | collective-permute-start | bytes 393224 | tf_op jit(solution)/shard_map/ppermute | solution.py:297
  18.9 7.0 %collective-permute-start.9 = (bf16[8,8192]{1,0:T(8,128)(2,1)S(1)}, bf16[8,8192]{1,0:T(8,128)(2,1)S(1)}, u32[]{:S(2)}, u32[]{:S(2)}) collective-permute-start(bf16[8,8192]{1,0:T(8,128)(2,1)S(1)} %collective-permute-done.7.refs_8_), channel_id=1, source_target_pairs={{0,2},{1,3},{2,0},{3,1},{4,6},{5,7},{6,4},{7,5},{8,10},{9,11},{10,... | collective-permute-start | bytes 393224 | tf_op jit(solution)/shard_map/ppermute | solution.py:297
  18.9 7.4 %collective-permute-start.8 = (bf16[8,8192]{1,0:T(8,128)(2,1)S(1)}, bf16[8,8192]{1,0:T(8,128)(2,1)S(1)}, u32[]{:S(2)}, u32[]{:S(2)}) collective-permute-start(bf16[8,8192]{1,0:T(8,128)(2,1)S(1)} %collective-permute-done.7.refs_8_), channel_id=1, source_target_pairs={{0,1},{1,0},{2,3},{3,2},{4,5},{5,4},{6,7},{7,6},{8,9},{9,8},{10,11... | collective-permute-start | bytes 393224 | tf_op jit(solution)/shard_map/ppermute | solution.py:297
  22.3 4.2 %collective-permute-start.6 = (bf16[8,8192]{1,0:T(8,128)(2,1)S(1)}, bf16[8,8192]{1,0:T(8,128)(2,1)S(1)}, u32[]{:S(2)}, u32[]{:S(2)}) collective-permute-start(bf16[8,8192]{1,0:T(8,128)(2,1)S(1)} %collective-permute-done.5.refs_6_), channel_id=1, source_target_pairs={{0,1},{1,0},{2,3},{3,2},{4,5},{5,4},{6,7},{7,6},{8,9},{9,8},{10,11... | collective-permute-start | bytes 393224 | tf_op jit(solution)/shard_map/ppermute | solution.py:297
  22.4 4.5 %collective-permute-start.4 = (bf16[8,8192]{1,0:T(8,128)(2,1)S(1)}, bf16[8,8192]{1,0:T(8,128)(2,1)S(1)}, u32[]{:S(2)}, u32[]{:S(2)}) collective-permute-start(bf16[8,8192]{1,0:T(8,128)(2,1)S(1)} %collective-permute-done.3.refs_4_), channel_id=1, source_target_pairs={{0,1},{1,0},{2,3},{3,2},{4,5},{5,4},{6,7},{7,6},{8,9},{9,8},{10,11... | collective-permute-start | bytes 393224 | tf_op jit(solution)/shard_map/ppermute | solution.py:297
  24.5 2.4 %collective-permute-start.2 = (bf16[8,8192]{1,0:T(8,128)(2,1)S(1)}, bf16[8,8192]{1,0:T(8,128)(2,1)S(1)}, u32[]{:S(2)}, u32[]{:S(2)}) collective-permute-start(bf16[8,8192]{1,0:T(8,128)(2,1)S(1)} %collective-permute-done.1.refs_2_), channel_id=1, source_target_pairs={{0,1},{1,0},{2,3},{3,2},{4,5},{5,4},{6,7},{7,6},{8,9},{9,8},{10,11... | collective-permute-start | bytes 393224 | tf_op jit(solution)/shard_map/ppermute | solution.py:297
  26.0 1.3 %collective-permute-start.14 = (bf16[8,8192]{1,0:T(8,128)(2,1)S(1)}, bf16[8,8192]{1,0:T(8,128)(2,1)S(1)}, u32[]{:S(2)}, u32[]{:S(2)}) collective-permute-start(bf16[8,8192]{1,0:T(8,128)(2,1)S(1)} %collective-permute-done.13.refs_14_), channel_id=1, source_target_pairs={{0,1},{1,0},{2,3},{3,2},{4,5},{5,4},{6,7},{7,6},{8,9},{9,8},{10,11... | collective-permute-start | bytes 393224 | tf_op jit(solution)/shard_map/ppermute | solution.py:297
  26.3 1.3 %collective-permute-start.12 = (bf16[8,8192]{1,0:T(8,128)(2,1)S(1)}, bf16[8,8192]{1,0:T(8,128)(2,1)S(1)}, u32[]{:S(2)}, u32[]{:S(2)}) collective-permute-start(bf16[8,8192]{1,0:T(8,128)(2,1)S(1)} %collective-permute-done.11.refs_12_), channel_id=1, source_target_pairs={{0,1},{1,0},{2,3},{3,2},{4,5},{5,4},{6,7},{7,6},{8,9},{9,8},{10,11... | collective-permute-start | bytes 393224 | tf_op jit(solution)/shard_map/ppermute | solution.py:297
  26.5 1.4 %collective-permute-start.10 = (bf16[8,8192]{1,0:T(8,128)(2,1)S(1)}, bf16[8,8192]{1,0:T(8,128)(2,1)S(1)}, u32[]{:S(2)}, u32[]{:S(2)}) collective-permute-start(bf16[8,8192]{1,0:T(8,128)(2,1)S(1)} %collective-permute-done.9.refs_10_), channel_id=1, source_target_pairs={{0,1},{1,0},{2,3},{3,2},{4,5},{5,4},{6,7},{7,6},{8,9},{9,8},{10,11... | collective-permute-start | bytes 393224 | tf_op jit(solution)/shard_map/ppermute | solution.py:297
  30.0 12.9 %all-to-all-start = ((bf16[16,16,512]{2,1,0:T(8,128)(2,1)}), bf16[16,16,512]{2,1,0:T(8,128)(2,1)S(1)}, u32[]{:S(2)}, u32[]{:S(2)}) async-start(bf16[16,16,512]{2,1,0:T(8,128)(2,1)} %delta.1), calls=%async_computation | async-start | bytes 524288 | tf_op jit(solution)/shard_map/all_to_all | solution.py:454

commit v25 on v21

--- a/solution.py
+++ b/solution.py
@@ -15,7 +15,7 @@
 MOST = 8
 RING = 16
 ORDER = [0, 1, 2, 3, 4, 5, 6, 7, 8, 9, 14, 15, 12, 13, 10, 11]
-EXCHANGE = [11, 10, 9, 8, 7, 6, 5, 4, 15, 14, 13, 12, 3, 2, 1, 0]
+EXCHANGE = [11, 10, 9, 8, 15, 14, 13, 12, 7, 6, 5, 4, 3, 2, 1, 0]
 F32 = jnp.float32
 BF16 = jnp.bfloat16
 NT = (((1,), (1,)), ((), ()))

time: 43.8 us -> 44 us (level)
  waiting for transfers between devices: 12.3 us -> 12.8 us
where the time goes in v25:
time: 44 us; the launch traced here: 43.6 us
  starting transfers between devices  17.8 us (40%)
  Pallas kernels  13.1 us (30%)
  waiting for transfers between devices  12.8 us (29%)
    ppermute x15, starting transfers between devices, swap(): return lax.ppermute(x, 'tensor', [(i, i ^ bits) for i in range(parts)])  12.7 us
    ppermute x15, waiting for transfers between devices, swap(): return lax.ppermute(x, 'tensor', [(i, i ^ bits) for i in range(parts)])  10.5 us
    pallas_call x1, Pallas kernels, attend(): pl.pallas_call(attend_kernel, out_shape=[jax.ShapeDtypeStruct(shape, BF16...  5.8 us
    all_to_all x1, starting transfers between devices, per_device(): lax.all_to_all(send, 'tensor', 0, 0, axis_index_groups=groups, tiled=True)  5.06 us
    pallas_call x1, Pallas kernels, base_part(): pl.pallas_call(functools.partial(base_kernel, at_slot), out_shape=jax.Sha...  4.26 us
    all_to_all x1, waiting for transfers between devices, per_device(): lax.all_to_all(send, 'tensor', 0, 0, axis_index_groups=groups, tiled=True)  2.29 us
    pallas_call x1, Pallas kernels, deltas(): pl.pallas_call(functools.partial(delta_kernel, at_slot), out_shape=jax.Sh...  2.16 us
  transfers between devices with their start and end apart: 16, of which 9 were waited for; matrix products, arithmetic and copies ran while one was open for 0% of the time, Pallas kernels for 10%

profile of v25, /device:TPU:0, one launch (start us, length us, event | category | flops | bytes accessed | tf_op | source)
XLA Modules:
  0.0 43.6 jit_solution(4578099575180270442)
XLA Ops:
  0.0 5.8 %attend.1 = (bf16[8,8192]{1,0:T(8,128)(2,1)S(1)}, bf16[8192,128]{1,0:T(8,128)(2,1)S(1)}, bf16[8192,128]{1,0:T(8,128)(2,1)S(1)}, bf16[16,128]{1,0:T(8,128)(2,1)S(...) custom-call(s32[4]{0:T(128)} %len_hbm.1, bf16[2,4,8192]{2,1,0:T(4,128)(2,1)} %q_hbm.1, ...), custom_call_target="tpu_custom_call" | custom-call | flops 134217728 | bytes 8388608 | tf_op jit(solution)/shard_map/attend/pallas_call | solution.py:252
  5.8 4.1 %collective-permute-start.7 = (bf16[8,8192]{1,0:T(8,128)(2,1)S(1)}, bf16[8,8192]{1,0:T(8,128)(2,1)S(1)}, u32[]{:S(2)}, u32[]{:S(2)}) collective-permute-start(bf16[8,8192]{1,0:T(8,128)(2,1)S(1)} %get-tuple-element.11.refs_0_), channel_id=1, source_target_pairs={{0,8},{1,9},{2,10},{3,11},{4,12},{5,13},{6,14},{7,15},{8,0},{9,1},... | collective-permute-start | bytes 393224 | tf_op jit(solution)/shard_map/ppermute | solution.py:297
  9.9 2.5 %collective-permute-start.5 = (bf16[8,8192]{1,0:T(8,128)(2,1)S(1)}, bf16[8,8192]{1,0:T(8,128)(2,1)S(1)}, u32[]{:S(2)}, u32[]{:S(2)}) collective-permute-start(bf16[8,8192]{1,0:T(8,128)(2,1)S(1)} %get-tuple-element.11.refs_0_), channel_id=1, source_target_pairs={{0,6},{1,7},{2,4},{3,5},{4,2},{5,3},{6,0},{7,1},{8,14},{9,15},{10,... | collective-permute-start | bytes 393224 | tf_op jit(solution)/shard_map/ppermute | solution.py:297
  12.4 0.4 %collective-permute-start.3 = (bf16[8,8192]{1,0:T(8,128)(2,1)S(1)}, bf16[8,8192]{1,0:T(8,128)(2,1)S(1)}, u32[]{:S(2)}, u32[]{:S(2)}) collective-permute-start(bf16[8,8192]{1,0:T(8,128)(2,1)S(1)} %get-tuple-element.11.refs_0_), channel_id=1, source_target_pairs={{0,4},{1,5},{2,6},{3,7},{4,0},{5,1},{6,2},{7,3},{8,12},{9,13},{10,... | collective-permute-start | bytes 393224 | tf_op jit(solution)/shard_map/ppermute | solution.py:297
  12.9 0.5 %collective-permute-start.1 = (bf16[8,8192]{1,0:T(8,128)(2,1)S(1)}, bf16[8,8192]{1,0:T(8,128)(2,1)S(1)}, u32[]{:S(2)}, u32[]{:S(2)}) collective-permute-start(bf16[8,8192]{1,0:T(8,128)(2,1)S(1)} %get-tuple-element.11.refs_0_), channel_id=1, source_target_pairs={{0,2},{1,3},{2,0},{3,1},{4,6},{5,7},{6,4},{7,5},{8,10},{9,11},{10,... | collective-permute-start | bytes 393224 | tf_op jit(solution)/shard_map/ppermute | solution.py:297
  13.4 0.0 collective-permute-start
  13.4 2.9 %collective-permute-done.7.refs_8_ = bf16[8,8192]{1,0:T(8,128)(2,1)S(1)} collective-permute-done((bf16[8,8192]{1,0:T(8,128)(2,1)S(1)}, bf16[8,8192]{1,0:T(8,128)(2,1)S(1)}, u32[]{:S(2)}, u32[]{:S(2)}) %collective-permute-start.7) | collective-permute-done | bytes 131104 | tf_op jit(solution)/shard_map/ppermute | solution.py:297
  16.3 1.6 %collective-permute-start.13 = (bf16[8,8192]{1,0:T(8,128)(2,1)S(1)}, bf16[8,8192]{1,0:T(8,128)(2,1)S(1)}, u32[]{:S(2)}, u32[]{:S(2)}) collective-permute-start(bf16[8,8192]{1,0:T(8,128)(2,1)S(1)} %collective-permute-done.7.refs_8_), channel_id=1, source_target_pairs={{0,2},{1,3},{2,0},{3,1},{4,6},{5,7},{6,4},{7,5},{8,10},{9,11},{10,... | collective-permute-start | bytes 393224 | tf_op jit(solution)/shard_map/ppermute | solution.py:297
  17.9 1.1 %collective-permute-done.5.refs_6_ = bf16[8,8192]{1,0:T(8,128)(2,1)S(1)} collective-permute-done((bf16[8,8192]{1,0:T(8,128)(2,1)S(1)}, bf16[8,8192]{1,0:T(8,128)(2,1)S(1)}, u32[]{:S(2)}, u32[]{:S(2)}) %collective-permute-start.5) | collective-permute-done | bytes 131104 | tf_op jit(solution)/shard_map/ppermute | solution.py:297
  19.0 1.1 %collective-permute-start.11 = (bf16[8,8192]{1,0:T(8,128)(2,1)S(1)}, bf16[8,8192]{1,0:T(8,128)(2,1)S(1)}, u32[]{:S(2)}, u32[]{:S(2)}) collective-permute-start(bf16[8,8192]{1,0:T(8,128)(2,1)S(1)} %collective-permute-done.7.refs_8_), channel_id=1, source_target_pairs={{0,4},{1,5},{2,6},{3,7},{4,0},{5,1},{6,2},{7,3},{8,12},{9,13},{10,... | collective-permute-start | bytes 393224 | tf_op jit(solution)/shard_map/ppermute | solution.py:297
  20.1 1.2 %collective-permute-done.3.refs_4_ = bf16[8,8192]{1,0:T(8,128)(2,1)S(1)} collective-permute-done((bf16[8,8192]{1,0:T(8,128)(2,1)S(1)}, bf16[8,8192]{1,0:T(8,128)(2,1)S(1)}, u32[]{:S(2)}, u32[]{:S(2)}) %collective-permute-start.3) | collective-permute-done | bytes 131104 | tf_op jit(solution)/shard_map/ppermute | solution.py:297
  21.3 1.3 %collective-permute-start.9 = (bf16[8,8192]{1,0:T(8,128)(2,1)S(1)}, bf16[8,8192]{1,0:T(8,128)(2,1)S(1)}, u32[]{:S(2)}, u32[]{:S(2)}) collective-permute-start(bf16[8,8192]{1,0:T(8,128)(2,1)S(1)} %collective-permute-done.7.refs_8_), channel_id=1, source_target_pairs={{0,6},{1,7},{2,4},{3,5},{4,2},{5,3},{6,0},{7,1},{8,14},{9,15},{10,... | collective-permute-start | bytes 393224 | tf_op jit(solution)/shard_map/ppermute | solution.py:297
  22.6 0.0 collective-permute-done.1.refs_2_
  22.6 0.0 collective-permute-start.8
  22.6 0.0 collective-permute-done.refs_1_
  22.6 0.5 %collective-permute-start.6 = (bf16[8,8192]{1,0:T(8,128)(2,1)S(1)}, bf16[8,8192]{1,0:T(8,128)(2,1)S(1)}, u32[]{:S(2)}, u32[]{:S(2)}) collective-permute-start(bf16[8,8192]{1,0:T(8,128)(2,1)S(1)} %collective-permute-done.5.refs_6_), channel_id=1, source_target_pairs={{0,1},{1,0},{2,3},{3,2},{4,5},{5,4},{6,7},{7,6},{8,9},{9,8},{10,11... | collective-permute-start | bytes 393224 | tf_op jit(solution)/shard_map/ppermute | solution.py:297
  23.1 0.0 collective-permute-done.13.refs_14_
  23.1 0.1 collective-permute-start.4
  23.2 1.3 %collective-permute-done.11.refs_12_ = bf16[8,8192]{1,0:T(8,128)(2,1)S(1)} collective-permute-done((bf16[8,8192]{1,0:T(8,128)(2,1)S(1)}, bf16[8,8192]{1,0:T(8,128)(2,1)S(1)}, u32[]{:S(2)}, u32[]{:S(2)}) %collective-permute-start.11) | collective-permute-done | bytes 131104 | tf_op jit(solution)/shard_map/ppermute | solution.py:297
  24.5 0.0 collective-permute-start.2
  24.5 2.7 %collective-permute-done.9.refs_10_ = bf16[8,8192]{1,0:T(8,128)(2,1)S(1)} collective-permute-done((bf16[8,8192]{1,0:T(8,128)(2,1)S(1)}, bf16[8,8192]{1,0:T(8,128)(2,1)S(1)}, u32[]{:S(2)}, u32[]{:S(2)}) %collective-permute-start.9) | collective-permute-done | bytes 131104 | tf_op jit(solution)/shard_map/ppermute | solution.py:297
  27.2 0.0 collective-permute-start.14
  27.2 0.5 %collective-permute-start.12 = (bf16[8,8192]{1,0:T(8,128)(2,1)S(1)}, bf16[8,8192]{1,0:T(8,128)(2,1)S(1)}, u32[]{:S(2)}, u32[]{:S(2)}) collective-permute-start(bf16[8,8192]{1,0:T(8,128)(2,1)S(1)} %collective-permute-done.11.refs_12_), channel_id=1, source_target_pairs={{0,1},{1,0},{2,3},{3,2},{4,5},{5,4},{6,7},{7,6},{8,9},{9,8},{10,11... | collective-permute-start | bytes 393224 | tf_op jit(solution)/shard_map/ppermute | solution.py:297
  27.7 0.1 collective-permute-start.10
  27.7 0.8 %collective-permute-done.14.refs_15_ = bf16[8,8192]{1,0:T(8,128)(2,1)S(1)} collective-permute-done((bf16[8,8192]{1,0:T(8,128)(2,1)S(1)}, bf16[8,8192]{1,0:T(8,128)(2,1)S(1)}, u32[]{:S(2)}, u32[]{:S(2)}) %collective-permute-start.14) | collective-permute-done | bytes 131104 | tf_op jit(solution)/shard_map/ppermute | solution.py:297
  28.5 0.2 collective-permute-done.12.refs_13_
  28.7 0.3 collective-permute-done.10.refs_11_
  29.0 2.2 %delta.1 = bf16[16,16,512]{2,1,0:T(8,128)(2,1)} custom-call(bf16[8,8192]{1,0:T(8,128)(2,1)S(1)} %get-tuple-element.11.refs_0_, bf16[8,8192]{1,0:T(8,128)(2,1)S(1)} %collective-permute-done.refs_1_, bf16[8,8192]{1,0:T(8,128)(2,1)S(1)} %collective-permute-done.1.refs_2_, bf16[8,8192]{1,0:T(8,128)(2,1)S(1)} %collective-permute-done.2.refs_3_, ...), custom_call_target="tpu_custom_call" | custom-call | flops 301989888 | bytes 6553600 | tf_op jit(solution)/shard_map/delta/pallas_call | solution.py:343
  31.2 5.1 %all-to-all-start = ((bf16[16,16,512]{2,1,0:T(8,128)(2,1)}), bf16[16,16,512]{2,1,0:T(8,128)(2,1)S(1)}, u32[]{:S(2)}, u32[]{:S(2)}) async-start(bf16[16,16,512]{2,1,0:T(8,128)(2,1)} %delta.1), calls=%async_computation | async-start | bytes 524288 | tf_op jit(solution)/shard_map/all_to_all | solution.py:454
  36.2 4.3 %base.1.base_ref = f32[128,512]{1,0:T(8,128)S(1)} custom-call(bf16[8,8192]{1,0:T(8,128)(2,1)S(1)} %get-tuple-element.11.refs_0_, bf16[8,8192]{1,0:T(8,128)(2,1)S(1)} %collective-permute-done.refs_1_, bf16[8,8192]{1,0:T(8,128)(2,1)S(1)} %collective-permute-done.1.refs_2_, bf16[8,8192]{1,0:T(8,128)(2,1)S(1)} %collective-permute-done.2.refs_3_, ...), custom_call_target="tpu_custom_call" | custom-call | flops 1342177280 | bytes 10747904 | tf_op jit(solution)/shard_map/base/pallas_call | solution.py:384
  40.5 2.3 %all-to-all-done.delta_ref = bf16[16,16,512]{2,1,0:T(8,128)(2,1)S(1)} async-done(((bf16[16,16,512]{2,1,0:T(8,128)(2,1)}), bf16[16,16,512]{2,1,0:T(8,128)(2,1)S(1)}, u32[]{:S(2)}, u32[]{:S(2)}) %all-to-all-start) | async-done | bytes 262176 | tf_op jit(solution)/shard_map/all_to_all | solution.py:454
  42.8 0.8 %join.1 = bf16[2,64,512]{2,1,0:T(8,128)(2,1)} custom-call(f32[128,512]{1,0:T(8,128)S(1)} %base.1.base_ref, bf16[128,256]{1,0:T(8,128)(2,1)S(1)} %get-tuple-element.13.place_ref, bf16[16,16,512]{2,1,0:T(8,128)(2,1)S(1)} %all-to-all-done.delta_ref), custom_call_target="tpu_custom_call" | custom-call | tf_op jit(solution)/shard_map/join/pallas_call | solution.py:412
  (4 shorter events, 0.0 us)
Async XLA Ops:
  5.8 10.5 %collective-permute-start.7 = (bf16[8,8192]{1,0:T(8,128)(2,1)S(1)}, bf16[8,8192]{1,0:T(8,128)(2,1)S(1)}, u32[]{:S(2)}, u32[]{:S(2)}) collective-permute-start(bf16[8,8192]{1,0:T(8,128)(2,1)S(1)} %get-tuple-element.11.refs_0_), channel_id=1, source_target_pairs={{0,8},{1,9},{2,10},{3,11},{4,12},{5,13},{6,14},{7,15},{8,0},{9,1},... | collective-permute-start | bytes 393224 | tf_op jit(solution)/shard_map/ppermute | solution.py:297
  9.9 9.1 %collective-permute-start.5 = (bf16[8,8192]{1,0:T(8,128)(2,1)S(1)}, bf16[8,8192]{1,0:T(8,128)(2,1)S(1)}, u32[]{:S(2)}, u32[]{:S(2)}) collective-permute-start(bf16[8,8192]{1,0:T(8,128)(2,1)S(1)} %get-tuple-element.11.refs_0_), channel_id=1, source_target_pairs={{0,6},{1,7},{2,4},{3,5},{4,2},{5,3},{6,0},{7,1},{8,14},{9,15},{10,... | collective-permute-start | bytes 393224 | tf_op jit(solution)/shard_map/ppermute | solution.py:297
  12.4 8.8 %collective-permute-start.3 = (bf16[8,8192]{1,0:T(8,128)(2,1)S(1)}, bf16[8,8192]{1,0:T(8,128)(2,1)S(1)}, u32[]{:S(2)}, u32[]{:S(2)}) collective-permute-start(bf16[8,8192]{1,0:T(8,128)(2,1)S(1)} %get-tuple-element.11.refs_0_), channel_id=1, source_target_pairs={{0,4},{1,5},{2,6},{3,7},{4,0},{5,1},{6,2},{7,3},{8,12},{9,13},{10,... | collective-permute-start | bytes 393224 | tf_op jit(solution)/shard_map/ppermute | solution.py:297
  12.9 9.7 %collective-permute-start.1 = (bf16[8,8192]{1,0:T(8,128)(2,1)S(1)}, bf16[8,8192]{1,0:T(8,128)(2,1)S(1)}, u32[]{:S(2)}, u32[]{:S(2)}) collective-permute-start(bf16[8,8192]{1,0:T(8,128)(2,1)S(1)} %get-tuple-element.11.refs_0_), channel_id=1, source_target_pairs={{0,2},{1,3},{2,0},{3,1},{4,6},{5,7},{6,4},{7,5},{8,10},{9,11},{10,... | collective-permute-start | bytes 393224 | tf_op jit(solution)/shard_map/ppermute | solution.py:297
  13.4 9.2 %collective-permute-start = (bf16[8,8192]{1,0:T(8,128)(2,1)S(1)}, bf16[8,8192]{1,0:T(8,128)(2,1)S(1)}, u32[]{:S(2)}, u32[]{:S(2)}) collective-permute-start(bf16[8,8192]{1,0:T(8,128)(2,1)S(1)} %get-tuple-element.11.refs_0_), channel_id=1, source_target_pairs={{0,1},{1,0},{2,3},{3,2},{4,5},{5,4},{6,7},{7,6},{8,9},{9,8},{10,11... | collective-permute-start | bytes 393224 | tf_op jit(solution)/shard_map/ppermute | solution.py:297
  16.3 6.8 %collective-permute-start.13 = (bf16[8,8192]{1,0:T(8,128)(2,1)S(1)}, bf16[8,8192]{1,0:T(8,128)(2,1)S(1)}, u32[]{:S(2)}, u32[]{:S(2)}) collective-permute-start(bf16[8,8192]{1,0:T(8,128)(2,1)S(1)} %collective-permute-done.7.refs_8_), channel_id=1, source_target_pairs={{0,2},{1,3},{2,0},{3,1},{4,6},{5,7},{6,4},{7,5},{8,10},{9,11},{10,... | collective-permute-start | bytes 393224 | tf_op jit(solution)/shard_map/ppermute | solution.py:297
  19.0 5.5 %collective-permute-start.11 = (bf16[8,8192]{1,0:T(8,128)(2,1)S(1)}, bf16[8,8192]{1,0:T(8,128)(2,1)S(1)}, u32[]{:S(2)}, u32[]{:S(2)}) collective-permute-start(bf16[8,8192]{1,0:T(8,128)(2,1)S(1)} %collective-permute-done.7.refs_8_), channel_id=1, source_target_pairs={{0,4},{1,5},{2,6},{3,7},{4,0},{5,1},{6,2},{7,3},{8,12},{9,13},{10,... | collective-permute-start | bytes 393224 | tf_op jit(solution)/shard_map/ppermute | solution.py:297
  21.3 5.9 %collective-permute-start.9 = (bf16[8,8192]{1,0:T(8,128)(2,1)S(1)}, bf16[8,8192]{1,0:T(8,128)(2,1)S(1)}, u32[]{:S(2)}, u32[]{:S(2)}) collective-permute-start(bf16[8,8192]{1,0:T(8,128)(2,1)S(1)} %collective-permute-done.7.refs_8_), channel_id=1, source_target_pairs={{0,6},{1,7},{2,4},{3,5},{4,2},{5,3},{6,0},{7,1},{8,14},{9,15},{10,... | collective-permute-start | bytes 393224 | tf_op jit(solution)/shard_map/ppermute | solution.py:297
  22.6 4.6 %collective-permute-start.8 = (bf16[8,8192]{1,0:T(8,128)(2,1)S(1)}, bf16[8,8192]{1,0:T(8,128)(2,1)S(1)}, u32[]{:S(2)}, u32[]{:S(2)}) collective-permute-start(bf16[8,8192]{1,0:T(8,128)(2,1)S(1)} %collective-permute-done.7.refs_8_), channel_id=1, source_target_pairs={{0,1},{1,0},{2,3},{3,2},{4,5},{5,4},{6,7},{7,6},{8,9},{9,8},{10,11... | collective-permute-start | bytes 393224 | tf_op jit(solution)/shard_map/ppermute | solution.py:297
  22.6 5.1 %collective-permute-start.6 = (bf16[8,8192]{1,0:T(8,128)(2,1)S(1)}, bf16[8,8192]{1,0:T(8,128)(2,1)S(1)}, u32[]{:S(2)}, u32[]{:S(2)}) collective-permute-start(bf16[8,8192]{1,0:T(8,128)(2,1)S(1)} %collective-permute-done.5.refs_6_), channel_id=1, source_target_pairs={{0,1},{1,0},{2,3},{3,2},{4,5},{5,4},{6,7},{7,6},{8,9},{9,8},{10,11... | collective-permute-start | bytes 393224 | tf_op jit(solution)/shard_map/ppermute | solution.py:297
  23.1 4.6 %collective-permute-start.4 = (bf16[8,8192]{1,0:T(8,128)(2,1)S(1)}, bf16[8,8192]{1,0:T(8,128)(2,1)S(1)}, u32[]{:S(2)}, u32[]{:S(2)}) collective-permute-start(bf16[8,8192]{1,0:T(8,128)(2,1)S(1)} %collective-permute-done.3.refs_4_), channel_id=1, source_target_pairs={{0,1},{1,0},{2,3},{3,2},{4,5},{5,4},{6,7},{7,6},{8,9},{9,8},{10,11... | collective-permute-start | bytes 393224 | tf_op jit(solution)/shard_map/ppermute | solution.py:297
  24.5 3.3 %collective-permute-start.2 = (bf16[8,8192]{1,0:T(8,128)(2,1)S(1)}, bf16[8,8192]{1,0:T(8,128)(2,1)S(1)}, u32[]{:S(2)}, u32[]{:S(2)}) collective-permute-start(bf16[8,8192]{1,0:T(8,128)(2,1)S(1)} %collective-permute-done.1.refs_2_), channel_id=1, source_target_pairs={{0,1},{1,0},{2,3},{3,2},{4,5},{5,4},{6,7},{7,6},{8,9},{9,8},{10,11... | collective-permute-start | bytes 393224 | tf_op jit(solution)/shard_map/ppermute | solution.py:297
  27.2 1.3 %collective-permute-start.14 = (bf16[8,8192]{1,0:T(8,128)(2,1)S(1)}, bf16[8,8192]{1,0:T(8,128)(2,1)S(1)}, u32[]{:S(2)}, u32[]{:S(2)}) collective-permute-start(bf16[8,8192]{1,0:T(8,128)(2,1)S(1)} %collective-permute-done.13.refs_14_), channel_id=1, source_target_pairs={{0,1},{1,0},{2,3},{3,2},{4,5},{5,4},{6,7},{7,6},{8,9},{9,8},{10,11... | collective-permute-start | bytes 393224 | tf_op jit(solution)/shard_map/ppermute | solution.py:297
  27.2 1.5 %collective-permute-start.12 = (bf16[8,8192]{1,0:T(8,128)(2,1)S(1)}, bf16[8,8192]{1,0:T(8,128)(2,1)S(1)}, u32[]{:S(2)}, u32[]{:S(2)}) collective-permute-start(bf16[8,8192]{1,0:T(8,128)(2,1)S(1)} %collective-permute-done.11.refs_12_), channel_id=1, source_target_pairs={{0,1},{1,0},{2,3},{3,2},{4,5},{5,4},{6,7},{7,6},{8,9},{9,8},{10,11... | collective-permute-start | bytes 393224 | tf_op jit(solution)/shard_map/ppermute | solution.py:297
  27.7 1.3 %collective-permute-start.10 = (bf16[8,8192]{1,0:T(8,128)(2,1)S(1)}, bf16[8,8192]{1,0:T(8,128)(2,1)S(1)}, u32[]{:S(2)}, u32[]{:S(2)}) collective-permute-start(bf16[8,8192]{1,0:T(8,128)(2,1)S(1)} %collective-permute-done.9.refs_10_), channel_id=1, source_target_pairs={{0,1},{1,0},{2,3},{3,2},{4,5},{5,4},{6,7},{7,6},{8,9},{9,8},{10,11... | collective-permute-start | bytes 393224 | tf_op jit(solution)/shard_map/ppermute | solution.py:297
  31.2 11.6 %all-to-all-start = ((bf16[16,16,512]{2,1,0:T(8,128)(2,1)}), bf16[16,16,512]{2,1,0:T(8,128)(2,1)S(1)}, u32[]{:S(2)}, u32[]{:S(2)}) async-start(bf16[16,16,512]{2,1,0:T(8,128)(2,1)} %delta.1), calls=%async_computation | async-start | bytes 524288 | tf_op jit(solution)/shard_map/all_to_all | solution.py:454

commit v26 on v24

--- a/solution.py
+++ b/solution.py
@@ -15,7 +15,7 @@
 MOST = 8
 RING = 16
 ORDER = [0, 1, 2, 3, 4, 5, 6, 7, 8, 9, 10, 11, 12, 13, 14, 15]
-EXCHANGE = [7, 6, 5, 4, 11, 10, 9, 8, 15, 14, 13, 12, 3, 2, 1, 0]
+EXCHANGE = [10, 11, 8, 9, 14, 15, 12, 13, 6, 7, 4, 5, 2, 3, 0, 1]
 F32 = jnp.float32
 BF16 = jnp.bfloat16
 NT = (((1,), (1,)), ((), ()))

time: 44 us -> 44 us (level)
  the two profiles are of different devices: /device:TPU:1 before, /device:TPU:0 now
where the time goes in v26:
time: 44 us; the launch traced here: 43.8 us
  starting transfers between devices  18.2 us (41%)
  Pallas kernels  13 us (30%)
  waiting for transfers between devices  12.5 us (28%)
    ppermute x15, starting transfers between devices, swap(): return lax.ppermute(x, 'tensor', [(i, i ^ bits) for i in range(parts)])  12.5 us
    ppermute x15, waiting for transfers between devices, swap(): return lax.ppermute(x, 'tensor', [(i, i ^ bits) for i in range(parts)])  9.76 us
    pallas_call x1, Pallas kernels, attend(): pl.pallas_call(attend_kernel, out_shape=[jax.ShapeDtypeStruct(shape, BF16...  5.8 us
    all_to_all x1, starting transfers between devices, per_device(): lax.all_to_all(send, 'tensor', 0, 0, axis_index_groups=groups, tiled=True)  5.67 us
    pallas_call x1, Pallas kernels, base_part(): pl.pallas_call(functools.partial(base_kernel, at_slot), out_shape=jax.Sha...  4.24 us
    all_to_all x1, waiting for transfers between devices, per_device(): lax.all_to_all(send, 'tensor', 0, 0, axis_index_groups=groups, tiled=True)  2.73 us
    pallas_call x1, Pallas kernels, deltas(): pl.pallas_call(functools.partial(delta_kernel, at_slot), out_shape=jax.Sh...  2.16 us
  transfers between devices with their start and end apart: 16, of which 11 were waited for; matrix products, arithmetic and copies ran while one was open for 0% of the time, Pallas kernels for 10%

profile of v26, /device:TPU:0, one launch (start us, length us, event | category | flops | bytes accessed | tf_op | source)
XLA Modules:
  0.0 43.8 jit_solution(74977714921518734)
XLA Ops:
  0.0 5.8 %attend.1 = (bf16[8,8192]{1,0:T(8,128)(2,1)S(1)}, bf16[8192,128]{1,0:T(8,128)(2,1)S(1)}, bf16[8192,128]{1,0:T(8,128)(2,1)S(1)}, bf16[16,128]{1,0:T(8,128)(2,1)S(...) custom-call(s32[4]{0:T(128)} %len_hbm.1, bf16[2,4,8192]{2,1,0:T(4,128)(2,1)} %q_hbm.1, ...), custom_call_target="tpu_custom_call" | custom-call | flops 134217728 | bytes 8388608 | tf_op jit(solution)/shard_map/attend/pallas_call | solution.py:252
  5.8 4.1 %collective-permute-start.7 = (bf16[8,8192]{1,0:T(8,128)(2,1)S(1)}, bf16[8,8192]{1,0:T(8,128)(2,1)S(1)}, u32[]{:S(2)}, u32[]{:S(2)}) collective-permute-start(bf16[8,8192]{1,0:T(8,128)(2,1)S(1)} %get-tuple-element.11.refs_0_), channel_id=1, source_target_pairs={{0,8},{1,9},{2,10},{3,11},{4,12},{5,13},{6,14},{7,15},{8,0},{9,1},... | collective-permute-start | bytes 393224 | tf_op jit(solution)/shard_map/ppermute | solution.py:297
  9.9 2.5 %collective-permute-start.5 = (bf16[8,8192]{1,0:T(8,128)(2,1)S(1)}, bf16[8,8192]{1,0:T(8,128)(2,1)S(1)}, u32[]{:S(2)}, u32[]{:S(2)}) collective-permute-start(bf16[8,8192]{1,0:T(8,128)(2,1)S(1)} %get-tuple-element.11.refs_0_), channel_id=1, source_target_pairs={{0,6},{1,7},{2,4},{3,5},{4,2},{5,3},{6,0},{7,1},{8,14},{9,15},{10,... | collective-permute-start | bytes 393224 | tf_op jit(solution)/shard_map/ppermute | solution.py:297
  12.4 0.4 %collective-permute-start.3 = (bf16[8,8192]{1,0:T(8,128)(2,1)S(1)}, bf16[8,8192]{1,0:T(8,128)(2,1)S(1)}, u32[]{:S(2)}, u32[]{:S(2)}) collective-permute-start(bf16[8,8192]{1,0:T(8,128)(2,1)S(1)} %get-tuple-element.11.refs_0_), channel_id=1, source_target_pairs={{0,4},{1,5},{2,6},{3,7},{4,0},{5,1},{6,2},{7,3},{8,12},{9,13},{10,... | collective-permute-start | bytes 393224 | tf_op jit(solution)/shard_map/ppermute | solution.py:297
  12.9 0.5 %collective-permute-start.1 = (bf16[8,8192]{1,0:T(8,128)(2,1)S(1)}, bf16[8,8192]{1,0:T(8,128)(2,1)S(1)}, u32[]{:S(2)}, u32[]{:S(2)}) collective-permute-start(bf16[8,8192]{1,0:T(8,128)(2,1)S(1)} %get-tuple-element.11.refs_0_), channel_id=1, source_target_pairs={{0,2},{1,3},{2,0},{3,1},{4,6},{5,7},{6,4},{7,5},{8,10},{9,11},{10,... | collective-permute-start | bytes 393224 | tf_op jit(solution)/shard_map/ppermute | solution.py:297
  13.4 0.0 collective-permute-start
  13.4 2.9 %collective-permute-done.7.refs_8_ = bf16[8,8192]{1,0:T(8,128)(2,1)S(1)} collective-permute-done((bf16[8,8192]{1,0:T(8,128)(2,1)S(1)}, bf16[8,8192]{1,0:T(8,128)(2,1)S(1)}, u32[]{:S(2)}, u32[]{:S(2)}) %collective-permute-start.7) | collective-permute-done | bytes 131104 | tf_op jit(solution)/shard_map/ppermute | solution.py:297
  16.3 1.6 %collective-permute-start.13 = (bf16[8,8192]{1,0:T(8,128)(2,1)S(1)}, bf16[8,8192]{1,0:T(8,128)(2,1)S(1)}, u32[]{:S(2)}, u32[]{:S(2)}) collective-permute-start(bf16[8,8192]{1,0:T(8,128)(2,1)S(1)} %collective-permute-done.7.refs_8_), channel_id=1, source_target_pairs={{0,6},{1,7},{2,4},{3,5},{4,2},{5,3},{6,0},{7,1},{8,14},{9,15},{10,... | collective-permute-start | bytes 393224 | tf_op jit(solution)/shard_map/ppermute | solution.py:297
  17.9 0.9 %collective-permute-done.5.refs_6_ = bf16[8,8192]{1,0:T(8,128)(2,1)S(1)} collective-permute-done((bf16[8,8192]{1,0:T(8,128)(2,1)S(1)}, bf16[8,8192]{1,0:T(8,128)(2,1)S(1)}, u32[]{:S(2)}, u32[]{:S(2)}) %collective-permute-start.5) | collective-permute-done | bytes 131104 | tf_op jit(solution)/shard_map/ppermute | solution.py:297
  18.9 1.2 %collective-permute-start.11 = (bf16[8,8192]{1,0:T(8,128)(2,1)S(1)}, bf16[8,8192]{1,0:T(8,128)(2,1)S(1)}, u32[]{:S(2)}, u32[]{:S(2)}) collective-permute-start(bf16[8,8192]{1,0:T(8,128)(2,1)S(1)} %collective-permute-done.7.refs_8_), channel_id=1, source_target_pairs={{0,4},{1,5},{2,6},{3,7},{4,0},{5,1},{6,2},{7,3},{8,12},{9,13},{10,... | collective-permute-start | bytes 393224 | tf_op jit(solution)/shard_map/ppermute | solution.py:297
  20.1 1.2 %collective-permute-done.3.refs_4_ = bf16[8,8192]{1,0:T(8,128)(2,1)S(1)} collective-permute-done((bf16[8,8192]{1,0:T(8,128)(2,1)S(1)}, bf16[8,8192]{1,0:T(8,128)(2,1)S(1)}, u32[]{:S(2)}, u32[]{:S(2)}) %collective-permute-start.3) | collective-permute-done | bytes 131104 | tf_op jit(solution)/shard_map/ppermute | solution.py:297
  21.3 0.9 %collective-permute-start.9 = (bf16[8,8192]{1,0:T(8,128)(2,1)S(1)}, bf16[8,8192]{1,0:T(8,128)(2,1)S(1)}, u32[]{:S(2)}, u32[]{:S(2)}) collective-permute-start(bf16[8,8192]{1,0:T(8,128)(2,1)S(1)} %collective-permute-done.7.refs_8_), channel_id=1, source_target_pairs={{0,2},{1,3},{2,0},{3,1},{4,6},{5,7},{6,4},{7,5},{8,10},{9,11},{10,... | collective-permute-start | bytes 393224 | tf_op jit(solution)/shard_map/ppermute | solution.py:297
  22.2 0.0 collective-permute-start.8
  22.2 0.0 collective-permute-done.refs_1_
  22.2 0.5 %collective-permute-start.6 = (bf16[8,8192]{1,0:T(8,128)(2,1)S(1)}, bf16[8,8192]{1,0:T(8,128)(2,1)S(1)}, u32[]{:S(2)}, u32[]{:S(2)}) collective-permute-start(bf16[8,8192]{1,0:T(8,128)(2,1)S(1)} %collective-permute-done.5.refs_6_), channel_id=1, source_target_pairs={{0,1},{1,0},{2,3},{3,2},{4,5},{5,4},{6,7},{7,6},{8,9},{9,8},{10,11... | collective-permute-start | bytes 393224 | tf_op jit(solution)/shard_map/ppermute | solution.py:297
  22.8 1.7 %collective-permute-done.13.refs_14_ = bf16[8,8192]{1,0:T(8,128)(2,1)S(1)} collective-permute-done((bf16[8,8192]{1,0:T(8,128)(2,1)S(1)}, bf16[8,8192]{1,0:T(8,128)(2,1)S(1)}, u32[]{:S(2)}, u32[]{:S(2)}) %collective-permute-start.13) | collective-permute-done | bytes 131104 | tf_op jit(solution)/shard_map/ppermute | solution.py:297
  24.5 0.0 collective-permute-start.4
  24.5 1.4 %collective-permute-done.11.refs_12_ = bf16[8,8192]{1,0:T(8,128)(2,1)S(1)} collective-permute-done((bf16[8,8192]{1,0:T(8,128)(2,1)S(1)}, bf16[8,8192]{1,0:T(8,128)(2,1)S(1)}, u32[]{:S(2)}, u32[]{:S(2)}) %collective-permute-start.11) | collective-permute-done | bytes 131104 | tf_op jit(solution)/shard_map/ppermute | solution.py:297
  25.9 0.0 collective-permute-start.2
  25.9 0.4 collective-permute-done.9.refs_10_
  26.3 0.2 collective-permute-start.14
  26.4 0.4 collective-permute-start.12
  26.8 0.2 collective-permute-start.10
  26.9 0.3 collective-permute-done.2.refs_3_
  27.2 0.4 collective-permute-done.14.refs_15_
  27.6 0.2 collective-permute-done.12.refs_13_
  27.8 0.3 collective-permute-done.10.refs_11_
  28.1 2.2 %delta.1 = bf16[16,16,512]{2,1,0:T(8,128)(2,1)} custom-call(bf16[8,8192]{1,0:T(8,128)(2,1)S(1)} %get-tuple-element.11.refs_0_, bf16[8,8192]{1,0:T(8,128)(2,1)S(1)} %collective-permute-done.refs_1_, bf16[8,8192]{1,0:T(8,128)(2,1)S(1)} %collective-permute-done.1.refs_2_, bf16[8,8192]{1,0:T(8,128)(2,1)S(1)} %collective-permute-done.2.refs_3_, ...), custom_call_target="tpu_custom_call" | custom-call | flops 301989888 | bytes 6553600 | tf_op jit(solution)/shard_map/delta/pallas_call | solution.py:343
  30.3 5.7 %all-to-all-start = ((bf16[16,16,512]{2,1,0:T(8,128)(2,1)}), bf16[16,16,512]{2,1,0:T(8,128)(2,1)S(1)}, u32[]{:S(2)}, u32[]{:S(2)}) async-start(bf16[16,16,512]{2,1,0:T(8,128)(2,1)} %delta.1), calls=%async_computation | async-start | bytes 524288 | tf_op jit(solution)/shard_map/all_to_all | solution.py:454
  35.9 4.2 %base.1.base_ref = f32[128,512]{1,0:T(8,128)S(1)} custom-call(bf16[8,8192]{1,0:T(8,128)(2,1)S(1)} %get-tuple-element.11.refs_0_, bf16[8,8192]{1,0:T(8,128)(2,1)S(1)} %collective-permute-done.refs_1_, bf16[8,8192]{1,0:T(8,128)(2,1)S(1)} %collective-permute-done.1.refs_2_, bf16[8,8192]{1,0:T(8,128)(2,1)S(1)} %collective-permute-done.2.refs_3_, ...), custom_call_target="tpu_custom_call" | custom-call | flops 1342177280 | bytes 10747904 | tf_op jit(solution)/shard_map/base/pallas_call | solution.py:384
  40.2 2.7 %all-to-all-done.delta_ref = bf16[16,16,512]{2,1,0:T(8,128)(2,1)S(1)} async-done(((bf16[16,16,512]{2,1,0:T(8,128)(2,1)}), bf16[16,16,512]{2,1,0:T(8,128)(2,1)S(1)}, u32[]{:S(2)}, u32[]{:S(2)}) %all-to-all-start) | async-done | bytes 262176 | tf_op jit(solution)/shard_map/all_to_all | solution.py:454
  42.9 0.8 %join.1 = bf16[2,64,512]{2,1,0:T(8,128)(2,1)} custom-call(f32[128,512]{1,0:T(8,128)S(1)} %base.1.base_ref, bf16[128,256]{1,0:T(8,128)(2,1)S(1)} %get-tuple-element.13.place_ref, bf16[16,16,512]{2,1,0:T(8,128)(2,1)S(1)} %all-to-all-done.delta_ref), custom_call_target="tpu_custom_call" | custom-call | tf_op jit(solution)/shard_map/join/pallas_call | solution.py:412
  (4 shorter events, 0.0 us)
Async XLA Ops:
  5.8 10.5 %collective-permute-start.7 = (bf16[8,8192]{1,0:T(8,128)(2,1)S(1)}, bf16[8,8192]{1,0:T(8,128)(2,1)S(1)}, u32[]{:S(2)}, u32[]{:S(2)}) collective-permute-start(bf16[8,8192]{1,0:T(8,128)(2,1)S(1)} %get-tuple-element.11.refs_0_), channel_id=1, source_target_pairs={{0,8},{1,9},{2,10},{3,11},{4,12},{5,13},{6,14},{7,15},{8,0},{9,1},... | collective-permute-start | bytes 393224 | tf_op jit(solution)/shard_map/ppermute | solution.py:297
  9.9 9.0 %collective-permute-start.5 = (bf16[8,8192]{1,0:T(8,128)(2,1)S(1)}, bf16[8,8192]{1,0:T(8,128)(2,1)S(1)}, u32[]{:S(2)}, u32[]{:S(2)}) collective-permute-start(bf16[8,8192]{1,0:T(8,128)(2,1)S(1)} %get-tuple-element.11.refs_0_), channel_id=1, source_target_pairs={{0,6},{1,7},{2,4},{3,5},{4,2},{5,3},{6,0},{7,1},{8,14},{9,15},{10,... | collective-permute-start | bytes 393224 | tf_op jit(solution)/shard_map/ppermute | solution.py:297
  12.4 8.8 %collective-permute-start.3 = (bf16[8,8192]{1,0:T(8,128)(2,1)S(1)}, bf16[8,8192]{1,0:T(8,128)(2,1)S(1)}, u32[]{:S(2)}, u32[]{:S(2)}) collective-permute-start(bf16[8,8192]{1,0:T(8,128)(2,1)S(1)} %get-tuple-element.11.refs_0_), channel_id=1, source_target_pairs={{0,4},{1,5},{2,6},{3,7},{4,0},{5,1},{6,2},{7,3},{8,12},{9,13},{10,... | collective-permute-start | bytes 393224 | tf_op jit(solution)/shard_map/ppermute | solution.py:297
  12.9 9.3 %collective-permute-start.1 = (bf16[8,8192]{1,0:T(8,128)(2,1)S(1)}, bf16[8,8192]{1,0:T(8,128)(2,1)S(1)}, u32[]{:S(2)}, u32[]{:S(2)}) collective-permute-start(bf16[8,8192]{1,0:T(8,128)(2,1)S(1)} %get-tuple-element.11.refs_0_), channel_id=1, source_target_pairs={{0,2},{1,3},{2,0},{3,1},{4,6},{5,7},{6,4},{7,5},{8,10},{9,11},{10,... | collective-permute-start | bytes 393224 | tf_op jit(solution)/shard_map/ppermute | solution.py:297
  13.4 8.8 %collective-permute-start = (bf16[8,8192]{1,0:T(8,128)(2,1)S(1)}, bf16[8,8192]{1,0:T(8,128)(2,1)S(1)}, u32[]{:S(2)}, u32[]{:S(2)}) collective-permute-start(bf16[8,8192]{1,0:T(8,128)(2,1)S(1)} %get-tuple-element.11.refs_0_), channel_id=1, source_target_pairs={{0,1},{1,0},{2,3},{3,2},{4,5},{5,4},{6,7},{7,6},{8,9},{9,8},{10,11... | collective-permute-start | bytes 393224 | tf_op jit(solution)/shard_map/ppermute | solution.py:297
  16.3 8.2 %collective-permute-start.13 = (bf16[8,8192]{1,0:T(8,128)(2,1)S(1)}, bf16[8,8192]{1,0:T(8,128)(2,1)S(1)}, u32[]{:S(2)}, u32[]{:S(2)}) collective-permute-start(bf16[8,8192]{1,0:T(8,128)(2,1)S(1)} %collective-permute-done.7.refs_8_), channel_id=1, source_target_pairs={{0,6},{1,7},{2,4},{3,5},{4,2},{5,3},{6,0},{7,1},{8,14},{9,15},{10,... | collective-permute-start | bytes 393224 | tf_op jit(solution)/shard_map/ppermute | solution.py:297
  18.9 7.0 %collective-permute-start.11 = (bf16[8,8192]{1,0:T(8,128)(2,1)S(1)}, bf16[8,8192]{1,0:T(8,128)(2,1)S(1)}, u32[]{:S(2)}, u32[]{:S(2)}) collective-permute-start(bf16[8,8192]{1,0:T(8,128)(2,1)S(1)} %collective-permute-done.7.refs_8_), channel_id=1, source_target_pairs={{0,4},{1,5},{2,6},{3,7},{4,0},{5,1},{6,2},{7,3},{8,12},{9,13},{10,... | collective-permute-start | bytes 393224 | tf_op jit(solution)/shard_map/ppermute | solution.py:297
  21.3 5.0 %collective-permute-start.9 = (bf16[8,8192]{1,0:T(8,128)(2,1)S(1)}, bf16[8,8192]{1,0:T(8,128)(2,1)S(1)}, u32[]{:S(2)}, u32[]{:S(2)}) collective-permute-start(bf16[8,8192]{1,0:T(8,128)(2,1)S(1)} %collective-permute-done.7.refs_8_), channel_id=1, source_target_pairs={{0,2},{1,3},{2,0},{3,1},{4,6},{5,7},{6,4},{7,5},{8,10},{9,11},{10,... | collective-permute-start | bytes 393224 | tf_op jit(solution)/shard_map/ppermute | solution.py:297
  22.2 4.2 %collective-permute-start.8 = (bf16[8,8192]{1,0:T(8,128)(2,1)S(1)}, bf16[8,8192]{1,0:T(8,128)(2,1)S(1)}, u32[]{:S(2)}, u32[]{:S(2)}) collective-permute-start(bf16[8,8192]{1,0:T(8,128)(2,1)S(1)} %collective-permute-done.7.refs_8_), channel_id=1, source_target_pairs={{0,1},{1,0},{2,3},{3,2},{4,5},{5,4},{6,7},{7,6},{8,9},{9,8},{10,11... | collective-permute-start | bytes 393224 | tf_op jit(solution)/shard_map/ppermute | solution.py:297
  22.2 4.5 %collective-permute-start.6 = (bf16[8,8192]{1,0:T(8,128)(2,1)S(1)}, bf16[8,8192]{1,0:T(8,128)(2,1)S(1)}, u32[]{:S(2)}, u32[]{:S(2)}) collective-permute-start(bf16[8,8192]{1,0:T(8,128)(2,1)S(1)} %collective-permute-done.5.refs_6_), channel_id=1, source_target_pairs={{0,1},{1,0},{2,3},{3,2},{4,5},{5,4},{6,7},{7,6},{8,9},{9,8},{10,11... | collective-permute-start | bytes 393224 | tf_op jit(solution)/shard_map/ppermute | solution.py:297
  24.5 2.5 %collective-permute-start.4 = (bf16[8,8192]{1,0:T(8,128)(2,1)S(1)}, bf16[8,8192]{1,0:T(8,128)(2,1)S(1)}, u32[]{:S(2)}, u32[]{:S(2)}) collective-permute-start(bf16[8,8192]{1,0:T(8,128)(2,1)S(1)} %collective-permute-done.3.refs_4_), channel_id=1, source_target_pairs={{0,1},{1,0},{2,3},{3,2},{4,5},{5,4},{6,7},{7,6},{8,9},{9,8},{10,11... | collective-permute-start | bytes 393224 | tf_op jit(solution)/shard_map/ppermute | solution.py:297
  25.9 1.3 %collective-permute-start.2 = (bf16[8,8192]{1,0:T(8,128)(2,1)S(1)}, bf16[8,8192]{1,0:T(8,128)(2,1)S(1)}, u32[]{:S(2)}, u32[]{:S(2)}) collective-permute-start(bf16[8,8192]{1,0:T(8,128)(2,1)S(1)} %collective-permute-done.1.refs_2_), channel_id=1, source_target_pairs={{0,1},{1,0},{2,3},{3,2},{4,5},{5,4},{6,7},{7,6},{8,9},{9,8},{10,11... | collective-permute-start | bytes 393224 | tf_op jit(solution)/shard_map/ppermute | solution.py:297
  26.3 1.3 %collective-permute-start.14 = (bf16[8,8192]{1,0:T(8,128)(2,1)S(1)}, bf16[8,8192]{1,0:T(8,128)(2,1)S(1)}, u32[]{:S(2)}, u32[]{:S(2)}) collective-permute-start(bf16[8,8192]{1,0:T(8,128)(2,1)S(1)} %collective-permute-done.13.refs_14_), channel_id=1, source_target_pairs={{0,1},{1,0},{2,3},{3,2},{4,5},{5,4},{6,7},{7,6},{8,9},{9,8},{10,11... | collective-permute-start | bytes 393224 | tf_op jit(solution)/shard_map/ppermute | solution.py:297
  26.4 1.4 %collective-permute-start.12 = (bf16[8,8192]{1,0:T(8,128)(2,1)S(1)}, bf16[8,8192]{1,0:T(8,128)(2,1)S(1)}, u32[]{:S(2)}, u32[]{:S(2)}) collective-permute-start(bf16[8,8192]{1,0:T(8,128)(2,1)S(1)} %collective-permute-done.11.refs_12_), channel_id=1, source_target_pairs={{0,1},{1,0},{2,3},{3,2},{4,5},{5,4},{6,7},{7,6},{8,9},{9,8},{10,11... | collective-permute-start | bytes 393224 | tf_op jit(solution)/shard_map/ppermute | solution.py:297
  26.8 1.3 %collective-permute-start.10 = (bf16[8,8192]{1,0:T(8,128)(2,1)S(1)}, bf16[8,8192]{1,0:T(8,128)(2,1)S(1)}, u32[]{:S(2)}, u32[]{:S(2)}) collective-permute-start(bf16[8,8192]{1,0:T(8,128)(2,1)S(1)} %collective-permute-done.9.refs_10_), channel_id=1, source_target_pairs={{0,1},{1,0},{2,3},{3,2},{4,5},{5,4},{6,7},{7,6},{8,9},{9,8},{10,11... | collective-permute-start | bytes 393224 | tf_op jit(solution)/shard_map/ppermute | solution.py:297
  30.3 12.7 %all-to-all-start = ((bf16[16,16,512]{2,1,0:T(8,128)(2,1)}), bf16[16,16,512]{2,1,0:T(8,128)(2,1)S(1)}, u32[]{:S(2)}, u32[]{:S(2)}) async-start(bf16[16,16,512]{2,1,0:T(8,128)(2,1)} %delta.1), calls=%async_computation | async-start | bytes 524288 | tf_op jit(solution)/shard_map/all_to_all | solution.py:454
